TPU v7x, 32 devices: a whole 2x2x4 slice. The times are simulated.
32 devices in a mesh: groups: 2 (over y), batch: 8 (over z, x), tensor: 2 (over core).
Axes of the slice: x: 2, y: 2, z: 4, core: 2. Of those that a mesh axis runs over, the one named last changes fastest.
Arguments:
- hidden: bfloat16 [4096, 8192], P(('groups', 'batch'), 'tensor'), parts along dimension 0, may hold values from -6 to 6
- demand: int32 [16, 4], P(('groups', 'batch')), parts along dimension 0, may hold values from 0 to 7, as said below
- lengths: int32 [16, 4], P(('groups', 'batch')), parts along dimension 0, may hold values from 62 to 66, as said below
- holder_slot: int32 [8], replicated, may hold values from 0 to 7, each once
- value_weight: bfloat16 [8192, 1024], P('tensor'), may hold values from -0.0625 to 0.0625
- factor_in: bfloat16 [8, 8192, 64], P('batch', 'tensor'), may hold values from -0.0625 to 0.0625
- factor_out: bfloat16 [8, 64, 1024], P('batch', None, 'tensor'), may hold values from -0.75 to 0.75
Outputs:
- values: bfloat16 [4096, 1024], P(('groups', 'batch'), 'tensor'), parts along dimension 0
There are 2 independent parts, one for each index of `groups`. A program takes and returns all parts, laid end to end along the dimension named above; an argument that names none is the same for every part. Nothing has to cross between parts.
Inputs may be any that keep to these rules, and one draw needn't show every extreme that they name: `demand`: each row lists 4 different adapters in rising order; one adapter is listed in every row. `lengths`: each row sums to 256; the adapter listed in every row of demand has exactly 66 rows in each block. `holder_slot`: A permutation.
All inputs are finite; a program needn't handle non-finite values.
Results may differ from a plain program's by a relative error of at most 0.005.
Values may be sent and summed in bfloat16 or wider, within the bound.
No kernel may reach another device: no remote copies, remote signals or barrier semaphores. Data moves between devices by JAX's collectives and lax.ppermute only.
A program may use at most 128 MiB of HBM per device.

v0:
```python
import jax
import jax.numpy as jnp
from jax import lax
from jax.sharding import PartitionSpec as P


def per_device(hidden, demand, lengths, holder_slot, value_weight, factor_in, factor_out):
    row_count, feature_half = hidden.shape
    wanted_count = demand.shape[1]
    capacity = row_count // wanted_count + 2
    owners = lax.axis_size("batch")
    wanted = demand[0]
    seg_lengths = lengths[0]
    seg_ends = jnp.cumsum(seg_lengths)
    seg_starts = seg_ends - seg_lengths
    row_index = jnp.arange(row_count, dtype=jnp.int32)
    row_segment = jnp.sum((row_index[:, None] >= seg_ends[None, :]).astype(jnp.int32), axis=1)
    row_onehot = (
        row_segment[:, None] == jnp.arange(wanted_count, dtype=jnp.int32)[None, :]
    ).astype(jnp.int32)
    within = row_index - jnp.sum(row_onehot * seg_starts[None, :], axis=1)
    adapter_index = jnp.arange(holder_slot.shape[0], dtype=jnp.int32)
    seg_owner = jnp.sum(
        (wanted[:, None] == adapter_index[None, :]).astype(jnp.int32) * holder_slot[None, :], axis=1
    )
    row_owner = jnp.sum(row_onehot * seg_owner[None, :], axis=1)
    row_slot = row_owner * capacity + within
    base_part = jnp.dot(hidden, value_weight, preferred_element_type=jnp.float32)
    projected = lax.psum_scatter(base_part, "tensor", scatter_dimension=1, tiled=True)
    owner_hits = (seg_owner[None, :] == jnp.arange(owners, dtype=jnp.int32)[:, None]).astype(
        jnp.int32
    )
    owner_start = jnp.sum(owner_hits * seg_starts[None, :], axis=1)
    owner_length = jnp.sum(owner_hits * seg_lengths[None, :], axis=1)
    slot_index = jnp.arange(capacity, dtype=jnp.int32)
    source_row = jnp.clip(owner_start[:, None] + slot_index[None, :], 0, row_count - 1)
    filled = slot_index[None, :] < owner_length[:, None]
    outgoing = hidden[source_row.reshape(-1)].reshape(owners, capacity, feature_half)
    outgoing = jnp.where(filled[:, :, None], outgoing, jnp.zeros_like(outgoing))
    incoming = lax.all_to_all(outgoing, "batch", split_axis=0, concat_axis=0, tiled=True)
    rank_part = jnp.dot(
        incoming.reshape(owners * capacity, feature_half),
        factor_in[0],
        preferred_element_type=jnp.float32,
    )
    rank_full = lax.psum(rank_part, "tensor")
    rank_bf = rank_full.astype(jnp.bfloat16)
    adapted = jnp.dot(rank_bf, factor_out[0], preferred_element_type=jnp.float32).astype(
        jnp.bfloat16
    )
    returned = lax.all_to_all(
        adapted.reshape(owners, capacity, adapted.shape[1]),
        "batch",
        split_axis=0,
        concat_axis=0,
        tiled=True,
    )
    low_rank = returned.reshape(owners * capacity, adapted.shape[1])[row_slot]
    return (projected + low_rank.astype(jnp.float32)).astype(jnp.bfloat16)


def solution(mesh):
    return jax.shard_map(
        per_device,
        mesh=mesh,
        in_specs=(
            P(("groups", "batch"), "tensor"),
            P(("groups", "batch"), None),
            P(("groups", "batch"), None),
            P(),
            P("tensor", None),
            P("batch", "tensor", None),
            P("batch", None, "tensor"),
        ),
        out_specs=P(("groups", "batch"), "tensor"),
        check_vma=False,
    )
```

profile of v0, /device:TPU:0, one launch (start us, length us, event | category | flops | bytes accessed | tf_op | source)
XLA Modules:
  0.0 179.5 jit_solution(18317285190056779691)
XLA Ops:
  6.5 0.0 copy-start
  6.5 1.0 reduce-window.4
  7.5 0.7 fusion.5
  8.2 0.9 select_reduce_fusion.4
  9.0 0.7 select_reduce_fusion.3
  9.8 0.1 add_clamp_fusion
  9.8 0.1 min.12
  10.0 0.0 copy-done
  10.0 5.0 %gather_fusion = bf16[528,4096]{1,0:T(8,128)(2,1)} fusion(bf16[256,4096]{1,0:T(8,128)(2,1)S(1)} %copy-done, s32[1024]{0:T(1024)S(1)} %pad_clamp_fusion.1), kind=kCustom, calls=%fused_computation | custom fusion | bytes 8652864 | tf_op jit(solution)/shard_map/gather | solution.py:38
  15.0 4.4 %reshape.118 = bf16[8,66,4096]{2,1,0:T(8,128)(2,1)} reshape(bf16[528,4096]{1,0:T(8,128)(2,1)} %gather_fusion) | data formatting | bytes 8650752 | tf_op jit(solution)/shard_map/reshape | solution.py:38
  19.4 0.1 iota_compare_fusion.2
  19.5 4.9 %broadcast_select_fusion = bf16[8,66,4096]{2,1,0:T(8,128)(2,1)} fusion(bf16[8,66,4096]{2,1,0:T(8,128)(2,1)} %reshape.118, pred[8,66]{1,0:T(8,128)(4,1)S(1)} %iota_compare_fusion.2), kind=kLoop, calls=%fused_computation.2 | loop fusion | flops 2162688 | bytes 8651280 | tf_op jit(solution)/shard_map/jit(_where)/select_n | solution.py:39
  24.3 7.3 %all-to-all-start = ((bf16[8,66,4096]{2,1,0:T(8,128)(2,1)}), bf16[8,66,4096]{2,1,0:T(8,128)(2,1)}, u32[]{:S(2)}, u32[]{:S(2)}) async-start(bf16[8,66,4096]{2,1,0:T(8,128)(2,1)} %broadcast_select_fusion), calls=%async_computation.1 | async-start | bytes 9437184 | tf_op jit(solution)/shard_map/all_to_all | solution.py:40
  31.6 0.0 reduce-scatter.2.cloned.1.call-start
  31.6 6.7 %fusion.6 = f32[256,1024]{1,0:T(8,128)} fusion(bf16[256,4096]{1,0:T(8,128)(2,1)S(1)} %copy-done, bf16[4096,1024]{1,0:T(8,128)(2,1)} %param.11), kind=kOutput, calls=%fused_computation.29 | convolution fusion | flops 2147483648 | bytes 11534336 | tf_op jit(solution)/shard_map/dot_general | solution.py:28
  38.3 0.0 reduce-scatter.2.cloned.1.call-update
  38.3 0.0 copy-start.1
  38.4 97.8 %all-to-all-done = bf16[8,66,4096]{2,1,0:T(8,128)(2,1)} async-done(((bf16[8,66,4096]{2,1,0:T(8,128)(2,1)}), bf16[8,66,4096]{2,1,0:T(8,128)(2,1)}, u32[]{:S(2)}, u32[]{:S(2)}) %all-to-all-start) | async-done | bytes 4325408 | tf_op jit(solution)/shard_map/all_to_all | solution.py:40
  136.1 4.4 %reshape.119 = bf16[528,4096]{1,0:T(8,128)(2,1)} reshape(bf16[8,66,4096]{2,1,0:T(8,128)(2,1)} %all-to-all-done) | data formatting | bytes 8650752 | tf_op jit(solution)/shard_map/reshape | solution.py:42
  140.5 0.0 copy-done.1
  140.5 0.0 copy-start.2
  140.5 3.8 %fusion = f32[528,64]{0,1:T(8,128)S(1)} fusion(bf16[528,4096]{1,0:T(8,128)(2,1)} %reshape.119, bf16[1,4096,64]{1,2,0:T(8,128)(2,1)S(1)} %copy-done.1), kind=kOutput, calls=%fused_computation.4 | convolution fusion | flops 276824064 | bytes 4984832 | tf_op jit(solution)/shard_map/dot_general | solution.py:41
  144.3 3.8 %all-reduce.1 = bf16[528,64]{0,1:T(8,128)(2,1)S(1)} all-reduce(f32[528,64]{0,1:T(8,128)S(1)} %fusion), channel_id=1, replica_groups=mesh['groups'=2,'batch'=8,'tensor'=2] {'tensor'}, use_global_device_ids=true, to_apply=%region_5.6 | all-reduce | flops 33792 | bytes 202752 | tf_op jit(solution)/shard_map/psum | solution.py:46
  148.1 0.0 copy-done.2
  148.1 0.3 convolution_convert_fusion
  148.4 1.0 reshape.120
  149.4 3.6 %all-to-all-start.1 = ((bf16[8,66,512]{2,1,0:T(8,128)(2,1)}), bf16[8,66,512]{2,1,0:T(8,128)(2,1)S(1)}, u32[]{:S(2)}, u32[]{:S(2)}) async-start(bf16[8,66,512]{2,1,0:T(8,128)(2,1)} %reshape.120), calls=%async_computation.2 | async-start | bytes 1179648 | tf_op jit(solution)/shard_map/all_to_all | solution.py:51
  153.0 0.1 convert_reduce_fusion
  153.1 0.1 select_reduce_fusion
  153.2 16.3 %all-to-all-done.1 = bf16[8,66,512]{2,1,0:T(8,128)(2,1)S(1)} async-done(((bf16[8,66,512]{2,1,0:T(8,128)(2,1)}), bf16[8,66,512]{2,1,0:T(8,128)(2,1)S(1)}, u32[]{:S(2)}, u32[]{:S(2)}) %all-to-all-start.1) | async-done | bytes 540704 | tf_op jit(solution)/shard_map/all_to_all | solution.py:51
  169.5 0.1 reshape.121
  169.7 1.2 gather_fusion.1
  170.9 0.0 reduce-scatter.2.cloned.1.call-done
  170.9 1.8 %add_convert_fusion = bf16[256,512]{1,0:T(8,128)(2,1)} fusion(f32[256,512]{1,0:T(8,128)} %reduce-scatter.2.cloned.1.call-done, bf16[256,512]{1,0:T(8,128)(2,1)S(1)} %gather_fusion.1), kind=kLoop, calls=%fused_computation.6 | loop fusion | flops 393216 | bytes 1048576 | tf_op jit(solution)/shard_map/convert_element_type | solution.py:59
  (5 shorter events, 0.0 us)
Async XLA Ops:
  6.5 3.4 %copy-start = (bf16[256,4096]{1,0:T(8,128)(2,1)S(1)}, bf16[256,4096]{1,0:T(8,128)(2,1)}, u32[]{:S(2)}) copy-start(bf16[256,4096]{1,0:T(8,128)(2,1)} %param.7) | copy-start | bytes 6291460
  24.3 111.8 %all-to-all-start = ((bf16[8,66,4096]{2,1,0:T(8,128)(2,1)}), bf16[8,66,4096]{2,1,0:T(8,128)(2,1)}, u32[]{:S(2)}, u32[]{:S(2)}) async-start(bf16[8,66,4096]{2,1,0:T(8,128)(2,1)} %broadcast_select_fusion), calls=%async_computation.1 | async-start | bytes 9437184 | tf_op jit(solution)/shard_map/all_to_all | solution.py:40
  31.6 139.3 %reduce-scatter.2.cloned.1.call-start = ((), (), s32[]{:S(2)}) async-start(), calls=%async_computation.3 | async-start | bytes 1572864 | tf_op jit(solution)/shard_map/reduce_scatter | solution.py:29
  38.3 102.2 %copy-start.1 = (bf16[1,4096,64]{1,2,0:T(8,128)(2,1)S(1)}, bf16[1,4096,64]{1,2,0:T(8,128)(2,1)}, u32[]{:S(2)}) copy-start(bf16[1,4096,64]{1,2,0:T(8,128)(2,1)} %param.12) | copy-start | bytes 1572868
  140.5 7.6 %copy-start.2 = (bf16[1,64,512]{2,1,0:T(8,128)(2,1)S(1)}, bf16[1,64,512]{2,1,0:T(8,128)(2,1)}, u32[]{:S(2)}) copy-start(bf16[1,64,512]{2,1,0:T(8,128)(2,1)} %param.13) | copy-start | bytes 196612
  149.4 20.1 %all-to-all-start.1 = ((bf16[8,66,512]{2,1,0:T(8,128)(2,1)}), bf16[8,66,512]{2,1,0:T(8,128)(2,1)S(1)}, u32[]{:S(2)}, u32[]{:S(2)}) async-start(bf16[8,66,512]{2,1,0:T(8,128)(2,1)} %reshape.120), calls=%async_computation.2 | async-start | bytes 1179648 | tf_op jit(solution)/shard_map/all_to_all | solution.py:51
Sparse Core Ops, SparseCore 0:
  38.5 9.9 reduce-scatter.1
where the time goes:
time: 180 us
  waiting for transfers between devices  114 us (63%)
  local copies, waits for them, and re-layouts  16.1 us (9%)
  between operations  13.5 us (8%)
  starting transfers between devices  10.9 us (6%)
  matrix products  10.8 us (6%)
  other arithmetic  10.3 us (6%)
  blocking collectives  3.83 us (2%)
    all_to_all x1, waiting for transfers between devices, per_device(): lax.all_to_all(outgoing, 'batch', split_axis=0, concat_axis=0, tiled=True)  97.8 us
    all_to_all x1, waiting for transfers between devices, per_device(): lax.all_to_all(adapted.reshape(owners, capacity, adapted.shape[1]), 'batc...  16.3 us
    all_to_all x1, starting transfers between devices, per_device(): lax.all_to_all(outgoing, 'batch', split_axis=0, concat_axis=0, tiled=True)  7.25 us
    dot_general x1, matrix products, per_device(): jnp.dot(hidden, value_weight, preferred_element_type=jnp.float32)  6.69 us
    gather x1, local copies, waits for them, and re-layouts, per_device(): hidden[source_row.reshape(-1)].reshape(owners, capacity, feature_half)  5.04 us
    select_n x1, other arithmetic, per_device(): outgoing = jnp.where(filled[:, :, None], outgoing, jnp.zeros_like(outgoing))  4.88 us
    reshape x1, local copies, waits for them, and re-layouts, per_device(): incoming.reshape(owners * capacity, feature_half)  4.4 us
    reshape x1, local copies, waits for them, and re-layouts, per_device(): hidden[source_row.reshape(-1)].reshape(owners, capacity, feature_half)  4.37 us
  transfers between devices with their start and end apart: 3, of which 2 were waited for; matrix products, arithmetic and copies ran while one was open for 10% of the time, Pallas kernels for 0%

commit v1 on v0

v1 whole, which is shorter than its diff:
```python
import functools

import jax
import jax.numpy as jnp
from jax import lax
from jax.experimental import pallas as pl
from jax.experimental.pallas import tpu as pltpu
from jax.sharding import PartitionSpec as P

F32, BF16 = jnp.float32, jnp.bfloat16
VMEM_LIMIT = 40 * 1024 * 1024


def ring_order(size):
    if size % 4:
        return list(range(size))
    columns = size // 4
    order = [0]
    for row in range(4):
        across = range(1, columns) if row % 2 == 0 else range(columns - 1, 0, -1)
        order += [row * columns + column for column in across]
    return order + [row * columns for row in (3, 2, 1)]


def contract(left, right):
    return lax.dot_general(left, right, (((1,), (1,)), ((), ())), preferred_element_type=F32)


def base_kernel(side_ref, rows_ref, weight_ref, out_ref):
    part = jnp.dot(rows_ref[...], weight_ref[...], preferred_element_type=F32)

    @pl.when(pl.program_id(0) == 0)
    def first():
        out_ref[...] = part

    @pl.when(pl.program_id(0) > 0)
    def later():
        out_ref[...] += part


def base_half(side, hidden, weight):
    rows, depth = hidden.shape
    width = weight.shape[1] // 2
    step = min(depth, 1024)
    return pl.pallas_call(
        base_kernel,
        out_shape=jax.ShapeDtypeStruct((rows, width), F32),
        grid_spec=pltpu.PrefetchScalarGridSpec(
            num_scalar_prefetch=1,
            grid=(depth // step,),
            in_specs=[
                pl.BlockSpec((rows, step), lambda k, side: (0, k)),
                pl.BlockSpec((step, width), lambda k, side: (k, side[0])),
            ],
            out_specs=pl.BlockSpec((rows, width), lambda k, side: (0, 0)),
        ),
        compiler_params=pltpu.CompilerParams(vmem_limit_bytes=VMEM_LIMIT),
        cost_estimate=pl.CostEstimate(
            flops=2 * rows * depth * width,
            bytes_accessed=2 * depth * (rows + width) + 4 * rows * width,
            transcendentals=0,
        ),
    )(side, hidden, weight)


def row_mask(bounds_ref, side, chunk, shape):
    row = lax.broadcasted_iota(jnp.int32, shape, 0)
    return (row >= bounds_ref[side, 0, chunk]) & (row < bounds_ref[side, 1, chunk])


def pack(part):
    half = part.shape[0] // 2
    return jnp.concatenate([part[:half], part[half:]], axis=1)


def unpack(packed):
    half = packed.shape[1] // 2
    return jnp.concatenate([packed[:, :half], packed[:, half:]], axis=0)


def rank_kernel(chunks, depth, has_start, pieces, bounds_ref, group_ref, *refs):
    refs = list(refs)
    own_ref, other_ref = refs[0], refs[1]
    factors = refs[2 : 2 + pieces]
    rest = refs[2 + pieces :]
    start_ref = rest.pop(0) if has_start else None
    out_ref = rest[0]
    offset = pl.multiple_of(group_ref[0] * depth, 128)
    own = own_ref[:, pl.ds(offset, depth)]
    other = other_ref[...]
    rank = out_ref.shape[-1] if not has_start else start_ref.shape[-1]
    for side, rows in ((0, own), (1, other)):
        total = start_ref[side] if has_start else jnp.zeros((rows.shape[0], rank), F32)
        for chunk, spans in chunks:
            part = None
            for piece, begin, size in spans:
                product = contract(rows[:, begin : begin + size], factors[piece][:, :size])
                part = product if part is None else part + product
            total = total + jnp.where(row_mask(bounds_ref, side, chunk, part.shape), part, 0.0)
        out_ref[side] = pack(total) if has_start else total


def rank_call(chunks, depth, bounds, group, own, other, factors, start, rank):
    rows = own.shape[0]
    vmem, smem = pl.BlockSpec(memory_space=pltpu.VMEM), pl.BlockSpec(memory_space=pltpu.SMEM)
    operands = [bounds, group, own, other, *factors]
    if start is None:
        shape = (2, rows, rank)
    else:
        operands.append(start)
        shape = (2, rows // 2, 2 * rank)
    return pl.pallas_call(
        functools.partial(rank_kernel, chunks, depth, start is not None, len(factors)),
        out_shape=jax.ShapeDtypeStruct(shape, F32),
        in_specs=[smem, smem] + [vmem] * (len(operands) - 2),
        out_specs=vmem,
        compiler_params=pltpu.CompilerParams(vmem_limit_bytes=VMEM_LIMIT),
        cost_estimate=pl.CostEstimate(
            flops=4 * rows * depth * rank * len(chunks),
            bytes_accessed=2 * depth * (2 * rows + rank * len(chunks)),
            transcendentals=0,
        ),
    )(*operands)


def final_kernel(count, bounds_ref, mine_ref, one_ref, two_ref, three_ref, base_ref, far_ref, *refs):
    outs, out_ref = refs[:count], refs[count]
    rank = unpack((mine_ref[0] + one_ref[...]) + (two_ref[...] + three_ref[...])).astype(BF16)
    total = jnp.zeros(out_ref.shape, F32)
    for chunk in range(count):
        chosen = jnp.where(row_mask(bounds_ref, 0, chunk, rank.shape), rank, jnp.zeros_like(rank))
        total = total + jnp.dot(chosen, outs[chunk][...], preferred_element_type=F32)
    adapted = total.astype(BF16).astype(F32)
    out_ref[...] = ((base_ref[...] + far_ref[...]) + adapted).astype(BF16)


def per_device(hidden, demand, lengths, holder_slot, value_weight, factor_in, factor_out):
    rows, features = hidden.shape
    owners = lax.axis_size("batch")
    rank, width = factor_out.shape[1:]
    depth = features // 2
    group, core = lax.axis_index("groups"), lax.axis_index("tensor")
    order = ring_order(owners)
    forward = [(order[i], order[(i + 1) % owners]) for i in range(owners)]
    backward = [(b, a) for a, b in forward]
    swap = [(0, 1), (1, 0)]

    to_other = lax.dynamic_slice(hidden, (0, (1 - group) * depth), (rows, depth))
    factor = lax.dynamic_slice(factor_in[0].T, (0, group * depth), (rank, depth))
    own = jnp.concatenate([factor, factor_out[0]], axis=1)
    other = lax.ppermute(to_other, "groups", swap)

    full = (owners - 1) // 2
    ahead = behind = own
    chunks = [(0, [(own, 0, depth)], own[:, depth:])]
    for step in range(1, full + 1):
        ahead = lax.ppermute(ahead, "batch", forward)
        behind = lax.ppermute(behind, "batch", backward)
        chunks.append((step, [(ahead, 0, depth)], ahead[:, depth:]))
        chunks.append((-step, [(behind, 0, depth)], behind[:, depth:]))
    if owners % 2 == 0:
        cut = (depth + width) // 2
        first = lax.ppermute(ahead[:, :cut], "batch", forward)
        second = lax.ppermute(behind[:, cut:], "batch", backward)
        chunks.append(
            (owners // 2, [(first, 0, cut), (second, cut, depth - cut)], second[:, depth - cut :])
        )

    position = jnp.asarray([order.index(i) for i in range(owners)], jnp.int32)
    place = position[lax.axis_index("batch")]
    distance = jnp.asarray([c[0] for c in chunks], jnp.int32)
    slots = jnp.asarray(order, jnp.int32)[(place - distance + owners) % owners]
    wanted = demand[0]
    adapter = jnp.arange(holder_slot.shape[0], dtype=jnp.int32)
    holder = jnp.sum(jnp.where(wanted[:, None] == adapter[None, :], holder_slot[None, :], 0), axis=1)
    hits = slots[:, None] == holder[None, :]
    item = jnp.arange(wanted.shape[0])
    before = item[:, None] > item[None, :]
    starts = jnp.sum(jnp.where(before, lengths[0][None, :], 0), axis=1)
    low = jnp.sum(jnp.where(hits, starts[None, :], 0), axis=1)
    high = low + jnp.sum(jnp.where(hits, lengths[0][None, :], 0), axis=1)
    bounds = jnp.stack([low, high]).astype(jnp.int32)
    bounds = jnp.stack([bounds, lax.ppermute(bounds, "groups", swap)])

    far = base_half((1 - core).reshape(1), hidden, value_weight)
    far = lax.ppermute(far, "tensor", swap)
    near = base_half(core.reshape(1), hidden, value_weight)

    def listing(items, first):
        arrays, spans = [], []
        for i, (_, pieces, _) in enumerate(items):
            span = []
            for array, begin, size in pieces:
                span.append((len(arrays), begin, size))
                arrays.append(array)
            spans.append((first + i, span))
        return spans, arrays

    early = len(chunks) - 1
    group_index = group.reshape(1)
    spans, arrays = listing(chunks[:early], 0)
    started = rank_call(spans, depth, bounds, group_index, hidden, other, arrays, None, rank)
    spans, arrays = listing(chunks[early:], early)
    mine = rank_call(spans, depth, bounds, group_index, hidden, other, arrays, started, rank)

    one = lax.ppermute(mine[0], "tensor", swap)
    two = lax.ppermute(mine[1], "groups", swap)
    three = lax.ppermute(mine[1], ("groups", "tensor"), [(0, 3), (1, 2), (2, 1), (3, 0)])

    vmem, smem = pl.BlockSpec(memory_space=pltpu.VMEM), pl.BlockSpec(memory_space=pltpu.SMEM)
    outs = [c[2] for c in chunks]
    return pl.pallas_call(
        functools.partial(final_kernel, len(outs)),
        out_shape=jax.ShapeDtypeStruct((rows, width), BF16),
        in_specs=[smem] + [vmem] * (6 + len(outs)),
        out_specs=vmem,
        compiler_params=pltpu.CompilerParams(vmem_limit_bytes=VMEM_LIMIT),
    )(bounds, mine, one, two, three, near, far, *outs)


def solution(mesh):
    return jax.shard_map(
        per_device,
        mesh=mesh,
        in_specs=(
            P(("groups", "batch"), "tensor"),
            P(("groups", "batch"), None),
            P(("groups", "batch"), None),
            P(),
            P("tensor", None),
            P("batch", "tensor", None),
            P("batch", None, "tensor"),
        ),
        out_specs=P(("groups", "batch"), "tensor"),
        check_vma=False,
    )
```

time: 180 us -> 53.3 us (0.30)
  waiting for transfers between devices: 114 us -> 8.15 us
  Pallas kernels: 0 us -> 14.5 us
  between operations: 13.5 us -> 0.25 us
  matrix products: 10.8 us -> 0 us
  other arithmetic: 10.3 us -> 1.93 us
  starting transfers between devices: 10.9 us -> 14.9 us
  blocking collectives: 3.83 us -> 0 us
  local copies, waits for them, and re-layouts: 16.1 us -> 13 us
    all_to_all x2 -> x0, waiting for transfers between devices: 114 us -> none  [the longest x1 97.8 us: per_device(): lax.all_to_all(outgoing, 'batch', split_axis=0, concat_axis=0, tiled=True)]
    ppermute x0 -> x14, starting transfers between devices: none -> 14.9 us  [the longest x3 5.98 us: per_device(): ahead = lax.ppermute(ahead, 'batch', forward)]
    pallas_call x0 -> x5, Pallas kernels: none -> 14.5 us  [the longest x2 7.69 us: rank_call(): pl.pallas_call(functools.partial(rank_kernel, chunks, depth, start is not...]
    all_to_all x2 -> x0, starting transfers between devices: 10.9 us -> none  [the longest x1 7.25 us: per_device(): lax.all_to_all(outgoing, 'batch', split_axis=0, concat_axis=0, tiled=True)]
    dot_general x3 -> x0, matrix products: 10.8 us -> none  [the longest x1 6.69 us: per_device(): jnp.dot(hidden, value_weight, preferred_element_type=jnp.float32)]
    reshape x4 -> x0, local copies, waits for them, and re-layouts: 9.86 us -> none  [the longest x1 4.4 us: per_device(): incoming.reshape(owners * capacity, feature_half)]
    ppermute x0 -> x14, waiting for transfers between devices: none -> 8.15 us  [the longest x3 7.45 us: per_device(): ahead = lax.ppermute(ahead, 'batch', forward)]
    gather x2 -> x1, local copies, waits for them, and re-layouts: 6.19 us -> 0.64 us  [per_device(): slots = jnp.asarray(order, jnp.int32)[(place - distance + owners) % owners]]
  transfers between devices with their start and end apart: 3 -> 14, of which waited for: 2 -> 3; matrix products, arithmetic and copies ran while one was open for 10% -> 17% of each run, Pallas kernels for 0% -> 24%
where the time goes in v1:
time: 53.3 us; the launch traced here: 52.8 us
  starting transfers between devices  14.9 us (28%)
  Pallas kernels  14.5 us (27%)
  local copies, waits for them, and re-layouts  13 us (24%)
  waiting for transfers between devices  8.15 us (15%)
  other arithmetic  1.93 us (4%)
    pallas_call x2, Pallas kernels, rank_call(): pl.pallas_call(functools.partial(rank_kernel, chunks, depth, start is not...  7.69 us
    ppermute x3, waiting for transfers between devices, per_device(): ahead = lax.ppermute(ahead, 'batch', forward)  7.45 us
    ppermute x3, starting transfers between devices, per_device(): ahead = lax.ppermute(ahead, 'batch', forward)  5.98 us
    unnamed x26, local copies, waits for them, and re-layouts  5.13 us
    pallas_call x2, Pallas kernels, base_half(): pl.pallas_call(base_kernel, out_shape=jax.ShapeDtypeStruct((rows, width),...  4.81 us
    slice x3, local copies, waits for them, and re-layouts, per_device(): chunks.append((-step, [(behind, 0, depth)], behind[:, depth:]))  2.54 us
    dynamic_slice x1, local copies, waits for them, and re-layouts, per_device(): lax.dynamic_slice(hidden, (0, (1 - group) * depth), (rows, depth))  2.33 us
    pallas_call x1, Pallas kernels, per_device(): pl.pallas_call(functools.partial(final_kernel, len(outs)), out_shape=jax....  1.99 us
  transfers between devices with their start and end apart: 14, of which 3 were waited for; matrix products, arithmetic and copies ran while one was open for 17% of the time, Pallas kernels for 24%

profile of v1, /device:TPU:0, one launch (start us, length us, event | category | flops | bytes accessed | tf_op | source)
XLA Modules:
  0.0 52.8 jit_solution(10870444063085176294)
XLA Ops:
  0.0 0.0 copy-start.1
  0.1 1.0 %copy-done = bf16[1,4096,64]{1,2,0:T(8,128)(2,1)S(1)} copy-done((bf16[1,4096,64]{1,2,0:T(8,128)(2,1)S(1)}, bf16[1,4096,64]{1,2,0:T(8,128)(2,1)}, u32[]{:S(2)}) %copy-start) | copy-done | bytes 524312
  1.1 0.9 %pad_maximum_fusion.refs_2_ = bf16[64,2560]{1,0:T(8,128)(2,1)S(1)} fusion(bf16[64,512]{1,0:T(8,128)(2,1)} %bitcast.22, bf16[64,2048]{1,0:T(8,128)(2,1)S(1)} %dynamic-slice_bitcast_fusion), kind=kLoop, calls=%fused_computation.1 | loop fusion | flops 655360 | bytes 655360 | tf_op jit(solution)/shard_map/concatenate | solution.py:150
  1.9 3.0 %collective-permute-start.2 = (bf16[64,2560]{1,0:T(8,128)(2,1)S(1)}, bf16[64,2560]{1,0:T(8,128)(2,1)S(1)}, u32[]{:S(2)}, u32[]{:S(2)}) collective-permute-start(bf16[64,2560]{1,0:T(8,128)(2,1)S(1)} %pad_maximum_fusion.refs_2_), channel_id=1, source_target_pairs={{0,2},{2,6},{6,10},{10,14},{14,12},{12,8},{8,4},{4,0},{1,3},{3,7},... | collective-permute-start | bytes 983048 | tf_op jit(solution)/shard_map/ppermute | solution.py:157
  4.9 0.2 collective-permute-start.6
  5.1 2.3 %constant_dynamic-slice_fusion = bf16[256,2048]{1,0:T(8,128)(2,1)} fusion(bf16[256,4096]{1,0:T(8,128)(2,1)} %rows_ref.3, s32[]{:T(128)S(6)} %select_n.41), kind=kLoop, calls=%fused_computation.23 | loop fusion | bytes 2097156 | tf_op jit(solution)/shard_map/dynamic_slice | solution.py:148
  7.4 1.9 %collective-permute-start.1 = (bf16[256,2048]{1,0:T(8,128)(2,1)}, bf16[256,2048]{1,0:T(8,128)(2,1)}, u32[]{:S(2)}, u32[]{:S(2)}) collective-permute-start(bf16[256,2048]{1,0:T(8,128)(2,1)} %constant_dynamic-slice_fusion), channel_id=1, source_target_pairs={{0,16},{16,0},{1,17},{17,1},{2,18},{18,2},{3,19},{19,3},{4,20},{20... | collective-permute-start | bytes 3145736 | tf_op jit(solution)/shard_map/ppermute | solution.py:151
  9.3 0.6 %dynamic_slice.9 = s32[1]{0:T(128)} dynamic-slice(s32[8]{0:T(128)S(1)} %copy-done.12, s32[]{:T(128)S(6)} %select_n.34), dynamic_slice_sizes={1} | dynamic-slice | bytes 12 | tf_op jit(solution)/shard_map/dynamic_slice | solution.py:170
  9.9 0.7 %compare_select_fusion = s32[8]{0:T(128)S(1)} fusion(s32[8]{0:T(128)S(1)} %copy-done.11, s32[]{:T(128)} %bitcast), kind=kLoop, calls=%fused_computation.6 | loop fusion | flops 128 | bytes 68 | tf_op jit(solution)/shard_map/select_n | solution.py:172
  10.6 0.6 %gather_fusion = s32[8]{0:T(128)S(1)} fusion(s32[8]{0:T(128)S(1)} %copy-done.7, s32[1024]{0:T(1024)S(1)} %pad_clamp_fusion), kind=kCustom, calls=%fused_computation | custom fusion | bytes 96 | tf_op jit(solution)/shard_map/gather | solution.py:172
  11.2 1.5 %collective-permute-done.2.refs_3_ = bf16[64,2560]{1,0:T(8,128)(2,1)S(1)} collective-permute-done((bf16[64,2560]{1,0:T(8,128)(2,1)S(1)}, bf16[64,2560]{1,0:T(8,128)(2,1)S(1)}, u32[]{:S(2)}, u32[]{:S(2)}) %collective-permute-start.2) | collective-permute-done | bytes 327712 | tf_op jit(solution)/shard_map/ppermute | solution.py:157
  12.7 1.7 %collective-permute-start.3 = (bf16[64,2560]{1,0:T(8,128)(2,1)S(1)}, bf16[64,2560]{1,0:T(8,128)(2,1)}, u32[]{:S(2)}, u32[]{:S(2)}) collective-permute-start(bf16[64,2560]{1,0:T(8,128)(2,1)S(1)} %collective-permute-done.2.refs_3_), channel_id=1, source_target_pairs={{0,2},{2,6},{6,10},{10,14},{14,12},{12,8},{8,4},{4,0},{1,3},{3,7},... | collective-permute-start | bytes 983048 | tf_op jit(solution)/shard_map/ppermute | solution.py:157
  14.4 0.7 %copy-done.4 = bf16[64,2560]{1,0:T(8,128)(2,1)} copy-done((bf16[64,2560]{1,0:T(8,128)(2,1)}, bf16[64,2560]{1,0:T(8,128)(2,1)S(1)}, u32[]{:S(2)}) %copy-start.4) | copy-done | bytes 327704
  15.1 0.0 collective-permute-done.6.refs_4_
  15.1 0.4 collective-permute-start.7
  15.5 0.1 select_reduce_fusion
  15.6 0.2 select_reduce_fusion.1
  15.8 0.1 fusion
  15.9 6.0 %collective-permute-done.3.refs_5_ = bf16[64,2560]{1,0:T(8,128)(2,1)} collective-permute-done((bf16[64,2560]{1,0:T(8,128)(2,1)S(1)}, bf16[64,2560]{1,0:T(8,128)(2,1)}, u32[]{:S(2)}, u32[]{:S(2)}) %collective-permute-start.3) | collective-permute-done | bytes 327712 | tf_op jit(solution)/shard_map/ppermute | solution.py:157
  21.8 1.3 %collective-permute-start.4 = (bf16[64,2560]{1,0:T(8,128)(2,1)}, bf16[64,2560]{1,0:T(8,128)(2,1)S(1)}, u32[]{:S(2)}, u32[]{:S(2)}) collective-permute-start(bf16[64,2560]{1,0:T(8,128)(2,1)} %collective-permute-done.3.refs_5_), channel_id=1, source_target_pairs={{0,2},{2,6},{6,10},{10,14},{14,12},{12,8},{8,4},{4,0},{1,3},{3,7},... | collective-permute-start | bytes 983048 | tf_op jit(solution)/shard_map/ppermute | solution.py:157
  23.2 0.7 %collective-permute-done.7.refs_6_ = bf16[64,2560]{1,0:T(8,128)(2,1)} collective-permute-done((bf16[64,2560]{1,0:T(8,128)(2,1)}, bf16[64,2560]{1,0:T(8,128)(2,1)}, u32[]{:S(2)}, u32[]{:S(2)}) %collective-permute-start.7) | collective-permute-done | bytes 327712 | tf_op jit(solution)/shard_map/ppermute | solution.py:158
  23.8 0.7 %collective-permute-start.8 = (bf16[64,2560]{1,0:T(8,128)(2,1)}, bf16[64,2560]{1,0:T(8,128)(2,1)}, u32[]{:S(2)}, u32[]{:S(2)}) collective-permute-start(bf16[64,2560]{1,0:T(8,128)(2,1)} %collective-permute-done.7.refs_6_), channel_id=1, source_target_pairs={{2,0},{6,2},{10,6},{14,10},{12,14},{8,12},{4,8},{0,4},{3,1},{7,3},... | collective-permute-start | bytes 983048 | tf_op jit(solution)/shard_map/ppermute | solution.py:158
  24.5 1.4 %collective-permute-start = (s32[2,8]{1,0:T(2,128)S(1)}, s32[2,8]{1,0:T(2,128)S(1)}, u32[]{:S(2)}, u32[]{:S(2)}) collective-permute-start(s32[2,8]{1,0:T(2,128)S(1)} %get-tuple-element.10), channel_id=1, source_target_pairs={{0,16},{16,0},{1,17},{17,1},{2,18},{18,2},{3,19},{19,3},{4,20},{20... | collective-permute-start | bytes 200 | tf_op jit(solution)/shard_map/ppermute | solution.py:183
  26.0 3.4 %copy-done.2 = bf16[4096,1024]{1,0:T(8,128)(2,1)S(1)} copy-done((bf16[4096,1024]{1,0:T(8,128)(2,1)S(1)}, bf16[4096,1024]{1,0:T(8,128)(2,1)}, u32[]{:S(2)}) %copy-start.2) | copy-done | bytes 8388632
  29.3 2.4 %shard_map.103 = f32[256,512]{1,0:T(8,128)S(1)} custom-call(s32[1]{0:T(128)} %bitcast.14.side_ref, bf16[256,4096]{1,0:T(8,128)(2,1)S(1)} %copy-done.1, bf16[4096,1024]{1,0:T(8,128)(2,1)S(1)} %copy-done.2), custom_call_target="tpu_custom_call" | custom-call | flops 1073741824 | bytes 6815744 | tf_op jit(solution)/shard_map/pallas_call | solution.py:45
  31.8 0.1 collective-permute-start.13
  31.8 0.0 collective-permute-done.4.refs_7_
  31.9 1.5 %collective-permute-start.5 = (bf16[64,1280]{1,0:T(8,128)(2,1)S(1)}, bf16[64,1280]{1,0:T(8,128)(2,1)S(1)}, u32[]{:S(2)}, u32[]{:S(2)}) collective-permute-start(bf16[64,1280]{1,0:T(8,128)(2,1)S(1)} %slice.47), channel_id=1, source_target_pairs={{0,2},{2,6},{6,10},{10,14},{14,12},{12,8},{8,4},{4,0},{1,3},{3,7},... | collective-permute-start | bytes 491528 | tf_op jit(solution)/shard_map/ppermute | solution.py:163
  33.4 0.0 collective-permute-done.8.refs_8_
  33.4 0.9 %slice.48 = bf16[64,1280]{1,0:T(8,128)(2,1)S(1)} slice(bf16[64,2560]{1,0:T(8,128)(2,1)} %collective-permute-done.8.refs_8_), slice={[0:64], [1280:2560]} | slice | bytes 327680 | tf_op jit(solution)/shard_map/slice | solution.py:164
  34.3 0.6 %collective-permute-start.9 = (bf16[64,1280]{1,0:T(8,128)(2,1)S(1)}, bf16[64,1280]{1,0:T(8,128)(2,1)S(1)}, u32[]{:S(2)}, u32[]{:S(2)}) collective-permute-start(bf16[64,1280]{1,0:T(8,128)(2,1)S(1)} %slice.48), channel_id=1, source_target_pairs={{2,0},{6,2},{10,6},{14,10},{12,14},{8,12},{4,8},{0,4},{3,1},{7,3},... | collective-permute-start | bytes 491528 | tf_op jit(solution)/shard_map/ppermute | solution.py:164
  34.9 0.0 collective-permute-done
  34.9 0.0 collective-permute-done.1.refs_1_
  35.0 0.0 copy-start.3
  35.0 5.7 %shard_map.100.refs_4_ = f32[2,256,64]{2,1,0:T(8,128)S(1)} custom-call(s32[2,2,8]{2,1,0:T(2,128)S(1)} %pad_add_fusion.bounds_ref, s32[1]{0:T(128)} %bitcast.7.group_ref, bf16[256,4096]{1,0:T(8,128)(2,1)S(1)} %copy-done.1, bf16[256,2048]{1,0:T(8,128)(2,1)} %collective-permute-done.1.refs_1_, bf16[64,2560]{1,0:T(8,128)(2,1)S(1)} %pad_maximum_fusion.refs_2_, ...), custom_call_target="tpu_custom_call" | custom-call | flops 939524096 | bytes 3932160 | tf_op jit(solution)/shard_map/pallas_call | solution.py:112
  40.7 0.0 collective-permute-done.5.refs_2_
  40.7 0.0 collective-permute-done.9.refs_3_
  40.7 2.0 %shard_map.101.mine_ref = f32[2,128,128]{2,1,0:T(8,128)S(1)} custom-call(s32[2,2,8]{2,1,0:T(2,128)S(1)} %pad_add_fusion.bounds_ref, s32[1]{0:T(128)} %bitcast.7.group_ref, bf16[256,4096]{1,0:T(8,128)(2,1)S(1)} %copy-done.1, bf16[256,2048]{1,0:T(8,128)(2,1)} %collective-permute-done.1.refs_1_, bf16[64,1280]{1,0:T(8,128)(2,1)S(1)} %collective-permute-done.5.refs_2_, ...), custom_call_target="tpu_custom_call" | custom-call | flops 134217728 | bytes 2359296 | tf_op jit(solution)/shard_map/pallas_call | solution.py:112
  42.7 0.7 %collective-permute-start.11 = (f32[128,128]{1,0:T(8,128)S(1)}, f32[128,128]{1,0:T(8,128)S(1)}, u32[]{:S(2)}, u32[]{:S(2)}) collective-permute-start(f32[128,128]{1,0:T(8,128)S(1)} %get-tuple-element.7), channel_id=1, source_target_pairs={{0,16},{16,0},{1,17},{17,1},{2,18},{18,2},{3,19},{19,3},{4,20},{20... | collective-permute-start | bytes 196616 | tf_op jit(solution)/shard_map/ppermute | solution.py:207
  43.4 0.6 %collective-permute-start.12 = (f32[128,128]{1,0:T(8,128)S(1)}, f32[128,128]{1,0:T(8,128)S(1)}, u32[]{:S(2)}, u32[]{:S(2)}) collective-permute-start(f32[128,128]{1,0:T(8,128)S(1)} %get-tuple-element.7), channel_id=1, source_target_pairs={{0,17},{1,16},{16,1},{17,0},{2,19},{3,18},{18,3},{19,2},{4,21},{5,... | collective-permute-start | bytes 196616 | tf_op jit(solution)/shard_map/ppermute | solution.py:208
  44.0 0.9 %collective-permute-start.10 = (f32[128,128]{1,0:T(8,128)S(1)}, f32[128,128]{1,0:T(8,128)S(1)}, u32[]{:S(2)}, u32[]{:S(2)}) collective-permute-start(f32[128,128]{1,0:T(8,128)S(1)} %get-tuple-element.8), channel_id=1, source_target_pairs={{0,1},{1,0},{2,3},{3,2},{4,5},{5,4},{6,7},{7,6},{8,9},{9,8},{10,11... | collective-permute-start | bytes 196616 | tf_op jit(solution)/shard_map/ppermute | solution.py:206
  44.9 2.4 %shard_map.102.base_ref = f32[256,512]{1,0:T(8,128)S(1)} custom-call(s32[1]{0:T(128)} %bitcast.13.side_ref, bf16[256,4096]{1,0:T(8,128)(2,1)S(1)} %copy-done.1, bf16[4096,1024]{1,0:T(8,128)(2,1)S(1)} %copy-done.3), custom_call_target="tpu_custom_call" | custom-call | flops 1073741824 | bytes 6815744 | tf_op jit(solution)/shard_map/pallas_call | solution.py:45
  47.4 0.8 %slice.52.refs_2_ = bf16[64,512]{1,0:T(8,128)(2,1)S(1)} slice(bf16[64,2560]{1,0:T(8,128)(2,1)} %collective-permute-done.6.refs_4_), slice={[0:64], [2048:2560]} | slice | bytes 131072 | tf_op jit(solution)/shard_map/slice | solution.py:160
  48.2 0.8 %slice.53.refs_3_ = bf16[64,512]{1,0:T(8,128)(2,1)S(1)} slice(bf16[64,2560]{1,0:T(8,128)(2,1)} %collective-permute-done.3.refs_5_), slice={[0:64], [2048:2560]} | slice | bytes 131072 | tf_op jit(solution)/shard_map/slice | solution.py:159
  49.1 0.8 %slice.54.refs_4_ = bf16[64,512]{1,0:T(8,128)(2,1)S(1)} slice(bf16[64,2560]{1,0:T(8,128)(2,1)} %collective-permute-done.7.refs_6_), slice={[0:64], [2048:2560]} | slice | bytes 131072 | tf_op jit(solution)/shard_map/slice | solution.py:160
  49.9 0.8 %slice.56.refs_6_ = bf16[64,512]{1,0:T(8,128)(2,1)S(1)} slice(bf16[64,2560]{1,0:T(8,128)(2,1)} %collective-permute-done.8.refs_8_), slice={[0:64], [2048:2560]} | slice | bytes 131072 | tf_op jit(solution)/shard_map/slice | solution.py:160
  50.8 0.0 collective-permute-done.11.two_ref
  50.8 2.0 %shard_map.104 = bf16[256,512]{1,0:T(8,128)(2,1)} custom-call(s32[2,2,8]{2,1,0:T(2,128)S(1)} %pad_add_fusion.bounds_ref, f32[2,128,128]{2,1,0:T(8,128)S(1)} %shard_map.101.mine_ref, f32[128,128]{1,0:T(8,128)S(1)} %collective-permute-done.10.one_ref, f32[128,128]{1,0:T(8,128)S(1)} %collective-permute-done.11.two_ref, ...), custom_call_target="tpu_custom_call" | custom-call | tf_op jit(solution)/shard_map/pallas_call | solution.py:212
  (34 shorter events, 0.1 us)
Async XLA Ops:
  0.0 1.0 %copy-start = (bf16[1,4096,64]{1,2,0:T(8,128)(2,1)S(1)}, bf16[1,4096,64]{1,2,0:T(8,128)(2,1)}, u32[]{:S(2)}) copy-start(bf16[1,4096,64]{1,2,0:T(8,128)(2,1)} %param.15) | copy-start | bytes 1572868
  0.0 9.3 %copy-start.12 = (s32[8]{0:T(128)S(1)}, s32[8]{0:T(128)}, u32[]{:S(2)}) copy-start(s32[8]{0:T(128)} %constant.43.clone) | copy-start | bytes 100
  0.0 9.9 %copy-start.11 = (s32[8]{0:T(128)S(1)}, s32[8]{0:T(128)}, u32[]{:S(2)}) copy-start(s32[8]{0:T(128)} %constant.50) | copy-start | bytes 100
  0.0 10.6 %copy-start.7 = (s32[8]{0:T(128)S(1)}, s32[8]{0:T(128)}, u32[]{:S(2)}) copy-start(s32[8]{0:T(128)} %constant.45.clone) | copy-start | bytes 100
  0.0 25.9 %copy-start.1 = (bf16[256,4096]{1,0:T(8,128)(2,1)S(1)}, bf16[256,4096]{1,0:T(8,128)(2,1)}, u32[]{:S(2)}) copy-start(bf16[256,4096]{1,0:T(8,128)(2,1)} %rows_ref.3) | copy-start | bytes 6291460
  0.0 15.4 %copy-start.8 = (s32[1,4]{1,0:T(1,128)S(1)}, s32[1,4]{1,0:T(1,128)}, u32[]{:S(2)}) copy-start(s32[1,4]{1,0:T(1,128)} %param.12) | copy-start | bytes 52
  0.0 15.6 %copy-start.9 = (s32[8]{0:T(128)S(1)}, s32[8]{0:T(128)}, u32[]{:S(2)}) copy-start(s32[8]{0:T(128)} %param.13) | copy-start | bytes 100
  0.0 15.5 %copy-start.10 = (s32[1,4]{1,0:T(1,128)S(1)}, s32[1,4]{1,0:T(1,128)}, u32[]{:S(2)}) copy-start(s32[1,4]{1,0:T(1,128)} %param.11) | copy-start | bytes 52
  1.9 10.8 %collective-permute-start.2 = (bf16[64,2560]{1,0:T(8,128)(2,1)S(1)}, bf16[64,2560]{1,0:T(8,128)(2,1)S(1)}, u32[]{:S(2)}, u32[]{:S(2)}) collective-permute-start(bf16[64,2560]{1,0:T(8,128)(2,1)S(1)} %pad_maximum_fusion.refs_2_), channel_id=1, source_target_pairs={{0,2},{2,6},{6,10},{10,14},{14,12},{12,8},{8,4},{4,0},{1,3},{3,7},... | collective-permute-start | bytes 983048 | tf_op jit(solution)/shard_map/ppermute | solution.py:157
  4.9 10.2 %collective-permute-start.6 = (bf16[64,2560]{1,0:T(8,128)(2,1)S(1)}, bf16[64,2560]{1,0:T(8,128)(2,1)}, u32[]{:S(2)}, u32[]{:S(2)}) collective-permute-start(bf16[64,2560]{1,0:T(8,128)(2,1)S(1)} %pad_maximum_fusion.refs_2_), channel_id=1, source_target_pairs={{2,0},{6,2},{10,6},{14,10},{12,14},{8,12},{4,8},{0,4},{3,1},{7,3},... | collective-permute-start | bytes 983048 | tf_op jit(solution)/shard_map/ppermute | solution.py:158
  7.4 27.5 %collective-permute-start.1 = (bf16[256,2048]{1,0:T(8,128)(2,1)}, bf16[256,2048]{1,0:T(8,128)(2,1)}, u32[]{:S(2)}, u32[]{:S(2)}) collective-permute-start(bf16[256,2048]{1,0:T(8,128)(2,1)} %constant_dynamic-slice_fusion), channel_id=1, source_target_pairs={{0,16},{16,0},{1,17},{17,1},{2,18},{18,2},{3,19},{19,3},{4,20},{20... | collective-permute-start | bytes 3145736 | tf_op jit(solution)/shard_map/ppermute | solution.py:151
  12.7 9.1 %collective-permute-start.3 = (bf16[64,2560]{1,0:T(8,128)(2,1)S(1)}, bf16[64,2560]{1,0:T(8,128)(2,1)}, u32[]{:S(2)}, u32[]{:S(2)}) collective-permute-start(bf16[64,2560]{1,0:T(8,128)(2,1)S(1)} %collective-permute-done.2.refs_3_), channel_id=1, source_target_pairs={{0,2},{2,6},{6,10},{10,14},{14,12},{12,8},{8,4},{4,0},{1,3},{3,7},... | collective-permute-start | bytes 983048 | tf_op jit(solution)/shard_map/ppermute | solution.py:157
  14.4 0.7 %copy-start.4 = (bf16[64,2560]{1,0:T(8,128)(2,1)}, bf16[64,2560]{1,0:T(8,128)(2,1)S(1)}, u32[]{:S(2)}) copy-start(bf16[64,2560]{1,0:T(8,128)(2,1)S(1)} %collective-permute-done.2.refs_3_) | copy-start | bytes 983044
  15.1 8.7 %collective-permute-start.7 = (bf16[64,2560]{1,0:T(8,128)(2,1)}, bf16[64,2560]{1,0:T(8,128)(2,1)}, u32[]{:S(2)}, u32[]{:S(2)}) collective-permute-start(bf16[64,2560]{1,0:T(8,128)(2,1)} %collective-permute-done.6.refs_4_), channel_id=1, source_target_pairs={{2,0},{6,2},{10,6},{14,10},{12,14},{8,12},{4,8},{0,4},{3,1},{7,3},... | collective-permute-start | bytes 983048 | tf_op jit(solution)/shard_map/ppermute | solution.py:158
  21.8 10.0 %collective-permute-start.4 = (bf16[64,2560]{1,0:T(8,128)(2,1)}, bf16[64,2560]{1,0:T(8,128)(2,1)S(1)}, u32[]{:S(2)}, u32[]{:S(2)}) collective-permute-start(bf16[64,2560]{1,0:T(8,128)(2,1)} %collective-permute-done.3.refs_5_), channel_id=1, source_target_pairs={{0,2},{2,6},{6,10},{10,14},{14,12},{12,8},{8,4},{4,0},{1,3},{3,7},... | collective-permute-start | bytes 983048 | tf_op jit(solution)/shard_map/ppermute | solution.py:157
  23.8 9.6 %collective-permute-start.8 = (bf16[64,2560]{1,0:T(8,128)(2,1)}, bf16[64,2560]{1,0:T(8,128)(2,1)}, u32[]{:S(2)}, u32[]{:S(2)}) collective-permute-start(bf16[64,2560]{1,0:T(8,128)(2,1)} %collective-permute-done.7.refs_6_), channel_id=1, source_target_pairs={{2,0},{6,2},{10,6},{14,10},{12,14},{8,12},{4,8},{0,4},{3,1},{7,3},... | collective-permute-start | bytes 983048 | tf_op jit(solution)/shard_map/ppermute | solution.py:158
  24.5 10.4 %collective-permute-start = (s32[2,8]{1,0:T(2,128)S(1)}, s32[2,8]{1,0:T(2,128)S(1)}, u32[]{:S(2)}, u32[]{:S(2)}) collective-permute-start(s32[2,8]{1,0:T(2,128)S(1)} %get-tuple-element.10), channel_id=1, source_target_pairs={{0,16},{16,0},{1,17},{17,1},{2,18},{18,2},{3,19},{19,3},{4,20},{20... | collective-permute-start | bytes 200 | tf_op jit(solution)/shard_map/ppermute | solution.py:183
  26.0 3.4 %copy-start.2 = (bf16[4096,1024]{1,0:T(8,128)(2,1)S(1)}, bf16[4096,1024]{1,0:T(8,128)(2,1)}, u32[]{:S(2)}) copy-start(bf16[4096,1024]{1,0:T(8,128)(2,1)} %weight_ref.3) | copy-start | bytes 25165828
  29.3 5.6 %copy-start.5 = (bf16[64,2560]{1,0:T(8,128)(2,1)S(1)}, bf16[64,2560]{1,0:T(8,128)(2,1)}, u32[]{:S(2)}) copy-start(bf16[64,2560]{1,0:T(8,128)(2,1)} %copy-done.4) | copy-start | bytes 983044
  31.8 19.0 %collective-permute-start.13 = (f32[256,512]{1,0:T(8,128)S(1)}, f32[256,512]{1,0:T(8,128)S(1)}, u32[]{:S(2)}, u32[]{:S(2)}) collective-permute-start(f32[256,512]{1,0:T(8,128)S(1)} %shard_map.103), channel_id=1, source_target_pairs={{0,1},{1,0},{2,3},{3,2},{4,5},{5,4},{6,7},{7,6},{8,9},{9,8},{10,11... | collective-permute-start | bytes 1572872 | tf_op jit(solution)/shard_map/ppermute | solution.py:186
  31.9 8.8 %collective-permute-start.5 = (bf16[64,1280]{1,0:T(8,128)(2,1)S(1)}, bf16[64,1280]{1,0:T(8,128)(2,1)S(1)}, u32[]{:S(2)}, u32[]{:S(2)}) collective-permute-start(bf16[64,1280]{1,0:T(8,128)(2,1)S(1)} %slice.47), channel_id=1, source_target_pairs={{0,2},{2,6},{6,10},{10,14},{14,12},{12,8},{8,4},{4,0},{1,3},{3,7},... | collective-permute-start | bytes 491528 | tf_op jit(solution)/shard_map/ppermute | solution.py:163
  34.3 6.4 %collective-permute-start.9 = (bf16[64,1280]{1,0:T(8,128)(2,1)S(1)}, bf16[64,1280]{1,0:T(8,128)(2,1)S(1)}, u32[]{:S(2)}, u32[]{:S(2)}) collective-permute-start(bf16[64,1280]{1,0:T(8,128)(2,1)S(1)} %slice.48), channel_id=1, source_target_pairs={{2,0},{6,2},{10,6},{14,10},{12,14},{8,12},{4,8},{0,4},{3,1},{7,3},... | collective-permute-start | bytes 491528 | tf_op jit(solution)/shard_map/ppermute | solution.py:164
  35.0 10.0 %copy-start.3 = (bf16[4096,1024]{1,0:T(8,128)(2,1)S(1)}, bf16[4096,1024]{1,0:T(8,128)(2,1)}, u32[]{:S(2)}) copy-start(bf16[4096,1024]{1,0:T(8,128)(2,1)} %weight_ref.3) | copy-start | bytes 25165828
  42.7 8.1 %collective-permute-start.11 = (f32[128,128]{1,0:T(8,128)S(1)}, f32[128,128]{1,0:T(8,128)S(1)}, u32[]{:S(2)}, u32[]{:S(2)}) collective-permute-start(f32[128,128]{1,0:T(8,128)S(1)} %get-tuple-element.7), channel_id=1, source_target_pairs={{0,16},{16,0},{1,17},{17,1},{2,18},{18,2},{3,19},{19,3},{4,20},{20... | collective-permute-start | bytes 196616 | tf_op jit(solution)/shard_map/ppermute | solution.py:207
  43.4 7.4 %collective-permute-start.12 = (f32[128,128]{1,0:T(8,128)S(1)}, f32[128,128]{1,0:T(8,128)S(1)}, u32[]{:S(2)}, u32[]{:S(2)}) collective-permute-start(f32[128,128]{1,0:T(8,128)S(1)} %get-tuple-element.7), channel_id=1, source_target_pairs={{0,17},{1,16},{16,1},{17,0},{2,19},{3,18},{18,3},{19,2},{4,21},{5,... | collective-permute-start | bytes 196616 | tf_op jit(solution)/shard_map/ppermute | solution.py:208
  44.0 6.7 %collective-permute-start.10 = (f32[128,128]{1,0:T(8,128)S(1)}, f32[128,128]{1,0:T(8,128)S(1)}, u32[]{:S(2)}, u32[]{:S(2)}) collective-permute-start(f32[128,128]{1,0:T(8,128)S(1)} %get-tuple-element.8), channel_id=1, source_target_pairs={{0,1},{1,0},{2,3},{3,2},{4,5},{5,4},{6,7},{7,6},{8,9},{9,8},{10,11... | collective-permute-start | bytes 196616 | tf_op jit(solution)/shard_map/ppermute | solution.py:206
  44.9 5.9 %copy-start.6 = (bf16[1,64,512]{2,1,0:T(8,128)(2,1)S(1)}, bf16[1,64,512]{2,1,0:T(8,128)(2,1)}, u32[]{:S(2)}) copy-start(bf16[1,64,512]{2,1,0:T(8,128)(2,1)} %param.16) | copy-start | bytes 196612

commit v2 on v0

v2 whole, which is shorter than its diff:
```python
import functools

import jax
import jax.numpy as jnp
from jax import lax
from jax.experimental import pallas as pl
from jax.experimental.pallas import tpu as pltpu
from jax.sharding import PartitionSpec as P

F32, BF16, I32 = jnp.float32, jnp.bfloat16, jnp.int32
VMEM_LIMIT = 40 * 1024 * 1024
GROUP = 4
VMEM = pl.BlockSpec(memory_space=pltpu.VMEM)
HBM = pl.BlockSpec(memory_space=pltpu.HBM)


def in_hbm(array):
    return pltpu.with_memory_space_constraint(array, pltpu.HBM)


def params():
    return pltpu.CompilerParams(vmem_limit_bytes=VMEM_LIMIT)


def ring_order(size):
    if size % 4:
        return list(range(size))
    columns = size // 4
    order = [0]
    for row in range(4):
        across = range(1, columns) if row % 2 == 0 else range(columns - 1, 0, -1)
        order += [row * columns + column for column in across]
    return order + [row * columns for row in (3, 2, 1)]


def contract(left, right):
    return lax.dot_general(left, right, (((1,), (1,)), ((), ())), preferred_element_type=F32)


def prologue_kernel(
    depth,
    rank,
    hidden_ref,
    factor_ref,
    factor_out_ref,
    demand_ref,
    lengths_ref,
    holder_ref,
    slots_ref,
    to_other_ref,
    first_ref,
    second_ref,
    bounds_ref,
    demand,
    lengths,
    holder,
    slots,
    sems,
):
    group, place = lax.axis_index("groups"), lax.axis_index("batch")
    cut = first_ref.shape[1]
    here = pl.multiple_of(group * depth, 128)
    there = pl.multiple_of((1 - group) * depth, 128)
    after = pl.multiple_of(group * depth + cut, 128)
    small = [
        pltpu.make_async_copy(demand_ref, demand, sems.at[0]),
        pltpu.make_async_copy(lengths_ref, lengths, sems.at[1]),
        pltpu.make_async_copy(holder_ref, holder, sems.at[2]),
        pltpu.make_async_copy(slots_ref.at[pl.ds(place, 1)], slots, sems.at[3]),
    ]
    large = [
        pltpu.make_async_copy(factor_ref.at[:, pl.ds(here, cut)], first_ref, sems.at[4]),
        pltpu.make_async_copy(
            factor_ref.at[:, pl.ds(after, depth - cut)], second_ref.at[:, : depth - cut], sems.at[5]
        ),
        pltpu.make_async_copy(factor_out_ref, second_ref.at[:, depth - cut :], sems.at[6]),
        pltpu.make_async_copy(hidden_ref.at[:, pl.ds(there, depth)], to_other_ref, sems.at[7]),
    ]
    for copy in small + large:
        copy.start()
    for copy in small:
        copy.wait()
    count = slots.shape[2]
    column = lax.broadcasted_iota(I32, (1, count * rank), 1)

    def chunk_bounds(chunk, carry):
        low, high = carry
        slot = slots[0, 0, chunk]

        def item_bounds(item, state):
            start, begin, end = state
            length = lengths[0, item]
            hit = holder[demand[0, item]] == slot
            begin = jnp.where(hit, start, begin)
            end = jnp.where(hit, start + length, end)
            return start + length, begin, end

        zero = jnp.int32(0)
        state = (zero, zero, zero)
        if demand.shape[1] <= 4:
            for item in range(demand.shape[1]):
                state = item_bounds(item, state)
        else:
            state = lax.fori_loop(0, demand.shape[1], item_bounds, state)
        inside = (column >= chunk * rank) & (column < (chunk + 1) * rank)
        return jnp.where(inside, state[1], low), jnp.where(inside, state[2], high)

    none = jnp.zeros((1, count * rank), I32)
    carry = (none, none)
    if count <= 8:
        for chunk in range(count):
            carry = chunk_bounds(chunk, carry)
    else:
        carry = lax.fori_loop(0, count, chunk_bounds, carry)
    bounds_ref[0:1, :] = carry[0]
    bounds_ref[1:2, :] = carry[1]
    bounds_ref[2:8, :] = jnp.zeros((6, count * rank), I32)
    for copy in large:
        copy.wait()


def prologue(hidden, factor, factor_out, demand, lengths, holder_slot, slots):
    rows, features = hidden.shape
    rank, width = factor_out.shape
    depth = features // 2
    cut = (depth + width) // 2
    count = slots.shape[2]
    return pl.pallas_call(
        functools.partial(prologue_kernel, depth, rank),
        out_shape=(
            jax.ShapeDtypeStruct((rows, depth), hidden.dtype),
            jax.ShapeDtypeStruct((rank, cut), factor.dtype),
            jax.ShapeDtypeStruct((rank, cut), factor.dtype),
            jax.ShapeDtypeStruct((8, count * rank), I32),
        ),
        in_specs=[HBM] * 7,
        out_specs=(VMEM,) * 4,
        scratch_shapes=[
            pltpu.SMEM(demand.shape, I32),
            pltpu.SMEM(lengths.shape, I32),
            pltpu.SMEM(holder_slot.shape, I32),
            pltpu.SMEM((1, 1, count), I32),
            pltpu.SemaphoreType.DMA((8,)),
        ],
        compiler_params=params(),
    )(*map(in_hbm, (hidden, factor, factor_out, demand, lengths, holder_slot, slots)))


def base_kernel(rows_ref, weight_ref, near_ref, far_ref, buffer, sems):
    width = near_ref.shape[1]
    core = lax.axis_index("tensor")
    here = pl.multiple_of(core * width, 128)
    there = pl.multiple_of((1 - core) * width, 128)
    step = buffer.shape[1]
    steps = weight_ref.shape[0] // step

    def fetch(k):
        return pltpu.make_async_copy(
            weight_ref.at[pl.ds(k * step, step)], buffer.at[k % 3], sems.at[k % 3]
        )

    fetch(0).start()
    if steps > 1:
        fetch(1).start()
    for k in range(steps):
        if k + 2 < steps:
            fetch(k + 2).start()
        fetch(k).wait()
        rows = rows_ref[:, k * step : (k + 1) * step]
        weight = buffer.at[k % 3]
        for out_ref, offset in ((far_ref, there), (near_ref, here)):
            part = jnp.dot(rows, weight[:, pl.ds(offset, width)], preferred_element_type=F32)
            if k == 0:
                out_ref[...] = part
            else:
                out_ref[...] += part


def base_call(hidden, weight):
    rows, depth = hidden.shape
    width = weight.shape[1] // 2
    step = 1024
    out = jax.ShapeDtypeStruct((rows, width), F32)
    return pl.pallas_call(
        base_kernel,
        out_shape=(out, out),
        in_specs=[VMEM, HBM],
        out_specs=(VMEM, VMEM),
        scratch_shapes=[
            pltpu.VMEM((3, step, 2 * width), weight.dtype),
            pltpu.SemaphoreType.DMA((3,)),
        ],
        compiler_params=params(),
        cost_estimate=pl.CostEstimate(
            flops=4 * rows * depth * width,
            bytes_accessed=2 * depth * (rows + 2 * width) + 8 * rows * width,
            transcendentals=0,
        ),
    )(hidden, in_hbm(weight))


def group_mask(bounds_ref, group, size, shape):
    row = lax.broadcasted_iota(I32, shape, 0)
    columns = pl.ds(group * size, shape[1])
    return (row >= bounds_ref[0:1, columns]) & (row < bounds_ref[1:2, columns])


def fold(masked):
    total = masked[:, :128]
    for begin in range(128, masked.shape[1], 128):
        total = total + masked[:, begin : begin + 128]
    return total


def rank_kernel(groups, depth, last, *refs):
    refs = list(refs)
    own_ref, other_ref, own_bounds, other_bounds = refs[:4]
    pieces = refs[4:]
    pieces, rest = pieces[: 2 * GROUP * len(groups)], pieces[2 * GROUP * len(groups) :]
    starts, outs = (rest[:2], rest[2:]) if last else ((None, None), rest)
    cut = pieces[0].shape[1]
    offset = pl.multiple_of(lax.axis_index("groups") * depth, 128)
    own = own_ref[:, pl.ds(offset, depth)]
    other = other_ref[...]
    rank = pieces[0].shape[0]
    size = GROUP * rank
    sides = ((own, own_bounds, starts[0], outs[0]), (other, other_bounds, starts[1], outs[1]))
    totals = [start_ref[...] if last else None for _, _, start_ref, _ in sides]
    for i, group in enumerate(groups):
        held = pieces[2 * GROUP * i : 2 * GROUP * (i + 1)]
        first = jnp.concatenate([ref[...] for ref in held[:GROUP]], axis=0)
        second = jnp.concatenate([ref[:, : depth - cut] for ref in held[GROUP:]], axis=0)
        for s, (rows, bounds, _, _) in enumerate(sides):
            part = contract(rows[:, :cut], first) + contract(rows[:, cut:], second)
            kept = fold(jnp.where(group_mask(bounds, group, size, part.shape), part, 0.0))
            totals[s] = kept if totals[s] is None else totals[s] + kept
    for total, (_, _, _, out_ref) in zip(totals, sides):
        if last:
            total = total + pltpu.roll(total, rank, 1)
            half = total.shape[0] // 2
            lane = lax.broadcasted_iota(I32, (half, 2 * rank), 1)
            total = jnp.where(lane < rank, total[:half], total[half:])
        out_ref[...] = total


def rank_call(groups, depth, own, other, own_bounds, other_bounds, pieces, starts):
    rows = own.shape[0]
    rank = pieces[0].shape[0]
    last = starts is not None
    shape = (rows // 2, 2 * rank) if last else (rows, 2 * rank)
    out = jax.ShapeDtypeStruct(shape, F32)
    operands = [own, other, own_bounds, other_bounds, *pieces, *(starts or ())]
    return pl.pallas_call(
        functools.partial(rank_kernel, groups, depth, last),
        out_shape=(out, out),
        in_specs=[VMEM] * len(operands),
        out_specs=(VMEM, VMEM),
        compiler_params=params(),
        cost_estimate=pl.CostEstimate(
            flops=4 * rows * depth * rank * GROUP * len(groups),
            bytes_accessed=2 * depth * (2 * rows + rank * GROUP * len(groups)),
            transcendentals=0,
        ),
    )(*operands)


def final_kernel(bounds_ref, mine, one, two, three, near_ref, far_ref, *refs):
    factors, out_ref = refs[:-1], refs[-1]
    rank, width = factors[0].shape[0], out_ref.shape[1]
    begin = factors[0].shape[1] - width
    packed = (mine[...] + one[...]) + (two[...] + three[...])
    turned = pltpu.roll(packed, rank, 1)
    lane = lax.broadcasted_iota(I32, packed.shape, 1)
    values = jnp.concatenate(
        [jnp.where(lane < rank, packed, turned), jnp.where(lane < rank, turned, packed)], axis=0
    )
    wide = jnp.concatenate([values] * (GROUP // 2), axis=1)
    total = None
    for group in range(len(factors) // GROUP):
        mask = group_mask(bounds_ref, group, GROUP * rank, wide.shape)
        chosen = jnp.where(mask, wide, 0.0).astype(BF16)
        factor = jnp.concatenate(
            [ref[:, begin:] for ref in factors[group * GROUP : (group + 1) * GROUP]], axis=0
        )
        part = jnp.dot(chosen, factor, preferred_element_type=F32)
        total = part if total is None else total + part
    adapted = total.astype(BF16).astype(F32)
    out_ref[...] = ((near_ref[...] + far_ref[...]) + adapted).astype(BF16)


def per_device(hidden, demand, lengths, holder_slot, value_weight, factor_in, factor_out):
    rows, features = hidden.shape
    owners = lax.axis_size("batch")
    rank, width = factor_out.shape[1:]
    depth = features // 2
    order = ring_order(owners)
    forward = [(order[i], order[(i + 1) % owners]) for i in range(owners)]
    backward = [(b, a) for a, b in forward]
    swap = [(0, 1), (1, 0)]

    full = (owners - 1) // 2
    distances = [0]
    for step in range(1, full + 1):
        distances += [step, -step]
    distances.append(owners // 2)
    table = [
        [[order[(order.index(me) - distance) % owners] for distance in distances]]
        for me in range(owners)
    ]
    to_other, first, second, bounds = prologue(
        hidden,
        factor_in[0].T,
        factor_out[0],
        demand,
        lengths,
        holder_slot,
        jnp.asarray(table, I32),
    )

    firsts, seconds = [first], [second]
    ahead, behind = (first, second), (first, second)
    for step in range(1, full + 1):
        a = lax.ppermute(ahead[0], "batch", forward)
        b = lax.ppermute(behind[1], "batch", backward)
        ahead = (a, lax.ppermute(ahead[1], "batch", forward))
        behind = (lax.ppermute(behind[0], "batch", backward), b)
        firsts += [ahead[0], behind[0]]
        seconds += [ahead[1], behind[1]]
    firsts.append(lax.ppermute(ahead[0], "batch", forward))
    seconds.append(lax.ppermute(behind[1], "batch", backward))
    other = lax.ppermute(to_other, "groups", swap)
    other_bounds = lax.ppermute(bounds, "groups", swap)

    near, far = base_call(hidden, value_weight)
    far = lax.ppermute(far, "tensor", swap)

    count = owners // GROUP
    early = range(count - 1)
    pieces = []
    for group in early:
        pieces += firsts[group * GROUP : (group + 1) * GROUP]
        pieces += seconds[group * GROUP : (group + 1) * GROUP]
    sides = (hidden, other, bounds, other_bounds)
    starts = rank_call(tuple(early), depth, *sides, pieces, None)
    pieces = firsts[-GROUP:] + seconds[-GROUP:]
    mine, theirs = rank_call((count - 1,), depth, *sides, pieces, starts)

    two = lax.ppermute(theirs, "groups", swap)
    three = lax.ppermute(theirs, ("groups", "tensor"), [(0, 3), (1, 2), (2, 1), (3, 0)])
    one = lax.ppermute(mine, "tensor", swap)

    operands = [bounds, mine, one, two, three, near, far, *seconds]
    return pl.pallas_call(
        final_kernel,
        out_shape=jax.ShapeDtypeStruct((rows, width), BF16),
        in_specs=[VMEM] * len(operands),
        out_specs=VMEM,
        compiler_params=params(),
    )(*operands)


def solution(mesh):
    return jax.shard_map(
        per_device,
        mesh=mesh,
        in_specs=(
            P(("groups", "batch"), "tensor"),
            P(("groups", "batch"), None),
            P(("groups", "batch"), None),
            P(),
            P("tensor", None),
            P("batch", "tensor", None),
            P("batch", None, "tensor"),
        ),
        out_specs=P(("groups", "batch"), "tensor"),
        check_vma=False,
    )
```

time: 180 us -> 65.9 us (0.37)
  waiting for transfers between devices: 114 us -> 32.6 us
  local copies, waits for them, and re-layouts: 16.1 us -> 1.59 us
  between operations: 13.5 us -> 0.09 us
  starting transfers between devices: 10.9 us -> 22.5 us
  matrix products: 10.8 us -> 0 us
  other arithmetic: 10.3 us -> 0 us
  Pallas kernels: 0 us -> 8.82 us
  blocking collectives: 3.83 us -> 0 us
    all_to_all x2 -> x0, waiting for transfers between devices: 114 us -> none  [the longest x1 97.8 us: per_device(): lax.all_to_all(outgoing, 'batch', split_axis=0, concat_axis=0, tiled=True)]
    ppermute x0 -> x20, waiting for transfers between devices: none -> 32.6 us  [the longest x1 19.5 us: per_device(): other_bounds = lax.ppermute(bounds, 'groups', swap)]
    ppermute x0 -> x20, starting transfers between devices: none -> 22.5 us  [the longest x3 5.44 us: per_device(): behind = (lax.ppermute(behind[0], 'batch', backward), b)]
    all_to_all x2 -> x0, starting transfers between devices: 10.9 us -> none  [the longest x1 7.25 us: per_device(): lax.all_to_all(outgoing, 'batch', split_axis=0, concat_axis=0, tiled=True)]
    dot_general x3 -> x0, matrix products: 10.8 us -> none  [the longest x1 6.69 us: per_device(): jnp.dot(hidden, value_weight, preferred_element_type=jnp.float32)]
    reshape x4 -> x0, local copies, waits for them, and re-layouts: 9.86 us -> none  [the longest x1 4.4 us: per_device(): incoming.reshape(owners * capacity, feature_half)]
    pallas_call x0 -> x5, Pallas kernels: none -> 8.82 us  [the longest x1 4.58 us: base_call(): pl.pallas_call(base_kernel, out_shape=(out, out), in_specs=[VMEM, HBM], o...]
    gather x2 -> x0, local copies, waits for them, and re-layouts: 6.19 us -> none  [the longest x1 5.04 us: per_device(): hidden[source_row.reshape(-1)].reshape(owners, capacity, feature_half)]
  transfers between devices with their start and end apart: 3 -> 20, of which waited for: 2 -> 7; matrix products, arithmetic and copies ran while one was open for 10% -> 0% of each run, Pallas kernels for 0% -> 9%
where the time goes in v2:
time: 65.9 us; the launch traced here: 65.7 us
  waiting for transfers between devices  32.6 us (49%)
  starting transfers between devices  22.5 us (34%)
  Pallas kernels  8.82 us (13%)
  local copies, waits for them, and re-layouts  1.59 us (2%)
    ppermute x1, waiting for transfers between devices, per_device(): other_bounds = lax.ppermute(bounds, 'groups', swap)  19.5 us
    ppermute x3, waiting for transfers between devices, per_device(): behind = (lax.ppermute(behind[0], 'batch', backward), b)  5.65 us
    ppermute x3, starting transfers between devices, per_device(): behind = (lax.ppermute(behind[0], 'batch', backward), b)  5.44 us
    pallas_call x1, Pallas kernels, base_call(): pl.pallas_call(base_kernel, out_shape=(out, out), in_specs=[VMEM, HBM], o...  4.58 us
    ppermute x3, starting transfers between devices, per_device(): a = lax.ppermute(ahead[0], 'batch', forward)  3.74 us
    ppermute x3, starting transfers between devices, per_device(): ahead = (a, lax.ppermute(ahead[1], 'batch', forward))  3.43 us
    ppermute x1, starting transfers between devices, per_device(): other = lax.ppermute(to_other, 'groups', swap)  3.03 us
    ppermute x1, waiting for transfers between devices, per_device(): two = lax.ppermute(theirs, 'groups', swap)  2.63 us
  transfers between devices with their start and end apart: 20, of which 7 were waited for; matrix products, arithmetic and copies ran while one was open for 0% of the time, Pallas kernels for 9%

profile of v2, /device:TPU:0, one launch (start us, length us, event | category | flops | bytes accessed | tf_op | source)
XLA Modules:
  0.0 65.7 jit_solution(5430621431309120467)
XLA Ops:
  0.0 1.5 %shard_map.82 = (bf16[256,2048]{1,0:T(8,128)(2,1)S(1)}, bf16[64,1280]{1,0:T(8,128)(2,1)S(1)}, bf16[64,1280]{1,0:T(8,128)(2,1)S(1)}, s32[8,512]{1,0:T(8,128)S(1)}) custom-call(bf16[256,4096]{1,0:T(8,128)(2,1)} %rows_ref.1, bf16[64,4096]{1,0:T(8,128)(2,1)} %bitcast.4, bf16[64,512]{1,0:T(8,128)(2,1)} %bitcast.5, s32[1,4]{1,0:T(1,128)} %demand_ref.1, ...), custom_call_target="tpu_custom_call" | custom-call | tf_op jit(solution)/shard_map/pallas_call | solution.py:128
  1.5 3.0 %collective-permute-start = (bf16[256,2048]{1,0:T(8,128)(2,1)S(1)}, bf16[256,2048]{1,0:T(8,128)(2,1)S(1)}, u32[]{:S(2)}, u32[]{:S(2)}) collective-permute-start(bf16[256,2048]{1,0:T(8,128)(2,1)S(1)} %get-tuple-element.16), channel_id=1, source_target_pairs={{0,16},{16,0},{1,17},{17,1},{2,18},{18,2},{3,19},{19,3},{4,20},{20... | collective-permute-start | bytes 3145736 | tf_op jit(solution)/shard_map/ppermute | solution.py:331
  4.5 1.5 %collective-permute-start.11 = (bf16[64,1280]{1,0:T(8,128)(2,1)S(1)}, bf16[64,1280]{1,0:T(8,128)(2,1)S(1)}, u32[]{:S(2)}, u32[]{:S(2)}) collective-permute-start(bf16[64,1280]{1,0:T(8,128)(2,1)S(1)} %get-tuple-element.18.refs_8_.refs_0_), channel_id=1, source_target_pairs={{0,2},{2,6},{6,10},{10,14},{14,12},{12,8},{8,4},{4,0},{1,3},{3,7},... | collective-permute-start | bytes 491528 | tf_op jit(solution)/shard_map/ppermute | solution.py:325
  6.0 1.6 %collective-permute-start.4 = (bf16[64,1280]{1,0:T(8,128)(2,1)S(1)}, bf16[64,1280]{1,0:T(8,128)(2,1)S(1)}, u32[]{:S(2)}, u32[]{:S(2)}) collective-permute-start(bf16[64,1280]{1,0:T(8,128)(2,1)S(1)} %get-tuple-element.17.refs_4_), channel_id=1, source_target_pairs={{0,2},{2,6},{6,10},{10,14},{14,12},{12,8},{8,4},{4,0},{1,3},{3,7},... | collective-permute-start | bytes 491528 | tf_op jit(solution)/shard_map/ppermute | solution.py:323
  7.6 0.4 collective-permute-start.9
  8.0 0.5 collective-permute-start.1
  8.5 19.5 %collective-permute-done.1.refs_3_ = s32[8,512]{1,0:T(8,128)S(1)} collective-permute-done((s32[8,512]{1,0:T(8,128)S(1)}, s32[8,512]{1,0:T(8,128)S(1)}, u32[]{:S(2)}, u32[]{:S(2)}) %collective-permute-start.1) | collective-permute-done | bytes 16416 | tf_op jit(solution)/shard_map/ppermute | solution.py:332
  28.0 1.8 %collective-permute-start.2 = (bf16[64,1280]{1,0:T(8,128)(2,1)S(1)}, bf16[64,1280]{1,0:T(8,128)(2,1)S(1)}, u32[]{:S(2)}, u32[]{:S(2)}) collective-permute-start(bf16[64,1280]{1,0:T(8,128)(2,1)S(1)} %get-tuple-element.17.refs_4_), channel_id=1, source_target_pairs={{2,0},{6,2},{10,6},{14,10},{12,14},{8,12},{4,8},{0,4},{3,1},{7,3},... | collective-permute-start | bytes 491528 | tf_op jit(solution)/shard_map/ppermute | solution.py:326
  29.8 0.0 collective-permute-done.11.refs_9_.refs_1_
  29.8 0.2 collective-permute-start.12
  30.1 0.0 collective-permute-done.4.refs_5_
  30.1 1.7 %collective-permute-start.5 = (bf16[64,1280]{1,0:T(8,128)(2,1)S(1)}, bf16[64,1280]{1,0:T(8,128)(2,1)S(1)}, u32[]{:S(2)}, u32[]{:S(2)}) collective-permute-start(bf16[64,1280]{1,0:T(8,128)(2,1)S(1)} %collective-permute-done.4.refs_5_), channel_id=1, source_target_pairs={{0,2},{2,6},{6,10},{10,14},{14,12},{12,8},{8,4},{4,0},{1,3},{3,7},... | collective-permute-start | bytes 491528 | tf_op jit(solution)/shard_map/ppermute | solution.py:323
  31.8 0.0 collective-permute-done.9.refs_10_.refs_2_
  31.8 0.3 collective-permute-start.10
  32.1 0.0 copy-start
  32.1 1.6 %copy-done = bf16[256,4096]{1,0:T(8,128)(2,1)S(1)} copy-done((bf16[256,4096]{1,0:T(8,128)(2,1)S(1)}, bf16[256,4096]{1,0:T(8,128)(2,1)}, u32[]{:S(2)}) %copy-start) | copy-done | bytes 2097176
  33.7 4.6 %shard_map.85 = (f32[256,512]{1,0:T(8,128)S(1)}, f32[256,512]{1,0:T(8,128)S(1)}) custom-call(bf16[256,4096]{1,0:T(8,128)(2,1)S(1)} %copy-done, bf16[4096,1024]{1,0:T(8,128)(2,1)} %weight_ref.1), custom_call_target="tpu_custom_call" | custom-call | flops 2147483648 | bytes 11534336 | tf_op jit(solution)/shard_map/pallas_call | solution.py:184
  38.3 0.0 collective-permute-done.2.refs_6_
  38.3 0.1 collective-permute-start.19
  38.4 0.0 collective-permute-done.12.refs_11_.refs_3_
  38.4 1.8 %collective-permute-start.3 = (bf16[64,1280]{1,0:T(8,128)(2,1)S(1)}, bf16[64,1280]{1,0:T(8,128)(2,1)S(1)}, u32[]{:S(2)}, u32[]{:S(2)}) collective-permute-start(bf16[64,1280]{1,0:T(8,128)(2,1)S(1)} %collective-permute-done.2.refs_6_), channel_id=1, source_target_pairs={{2,0},{6,2},{10,6},{14,10},{12,14},{8,12},{4,8},{0,4},{3,1},{7,3},... | collective-permute-start | bytes 491528 | tf_op jit(solution)/shard_map/ppermute | solution.py:326
  40.2 0.0 collective-permute-done.10.refs_8_.refs_4_
  40.2 1.6 %collective-permute-start.14 = (bf16[64,1280]{1,0:T(8,128)(2,1)S(1)}, bf16[64,1280]{1,0:T(8,128)(2,1)S(1)}, u32[]{:S(2)}, u32[]{:S(2)}) collective-permute-start(bf16[64,1280]{1,0:T(8,128)(2,1)S(1)} %collective-permute-done.10.refs_8_.refs_4_), channel_id=1, source_target_pairs={{2,0},{6,2},{10,6},{14,10},{12,14},{8,12},{4,8},{0,4},{3,1},{7,3},... | collective-permute-start | bytes 491528 | tf_op jit(solution)/shard_map/ppermute | solution.py:324
  41.8 0.0 collective-permute-done.5.refs_7_
  41.8 0.4 collective-permute-start.6
  42.3 3.2 %collective-permute-done.3.refs_4_ = bf16[64,1280]{1,0:T(8,128)(2,1)S(1)} collective-permute-done((bf16[64,1280]{1,0:T(8,128)(2,1)S(1)}, bf16[64,1280]{1,0:T(8,128)(2,1)S(1)}, u32[]{:S(2)}, u32[]{:S(2)}) %collective-permute-start.3) | collective-permute-done | bytes 163872 | tf_op jit(solution)/shard_map/ppermute | solution.py:326
  45.4 1.7 %collective-permute-start.13 = (bf16[64,1280]{1,0:T(8,128)(2,1)S(1)}, bf16[64,1280]{1,0:T(8,128)(2,1)S(1)}, u32[]{:S(2)}, u32[]{:S(2)}) collective-permute-start(bf16[64,1280]{1,0:T(8,128)(2,1)S(1)} %collective-permute-done.12.refs_11_.refs_3_), channel_id=1, source_target_pairs={{0,2},{2,6},{6,10},{10,14},{14,12},{12,8},{8,4},{4,0},{1,3},{3,7},... | collective-permute-start | bytes 491528 | tf_op jit(solution)/shard_map/ppermute | solution.py:325
  47.1 1.3 %collective-permute-done.14.refs_10_.refs_6_ = bf16[64,1280]{1,0:T(8,128)(2,1)S(1)} collective-permute-done((bf16[64,1280]{1,0:T(8,128)(2,1)S(1)}, bf16[64,1280]{1,0:T(8,128)(2,1)S(1)}, u32[]{:S(2)}, u32[]{:S(2)}) %collective-permute-start.14) | collective-permute-done | bytes 163872 | tf_op jit(solution)/shard_map/ppermute | solution.py:324
  48.5 1.8 %collective-permute-start.7 = (bf16[64,1280]{1,0:T(8,128)(2,1)S(1)}, bf16[64,1280]{1,0:T(8,128)(2,1)S(1)}, u32[]{:S(2)}, u32[]{:S(2)}) collective-permute-start(bf16[64,1280]{1,0:T(8,128)(2,1)S(1)} %collective-permute-done.3.refs_4_), channel_id=1, source_target_pairs={{2,0},{6,2},{10,6},{14,10},{12,14},{8,12},{4,8},{0,4},{3,1},{7,3},... | collective-permute-start | bytes 491528 | tf_op jit(solution)/shard_map/ppermute | solution.py:326
  50.3 0.0 collective-permute-done.6.refs_5_
  50.3 1.6 %collective-permute-start.15 = (bf16[64,1280]{1,0:T(8,128)(2,1)S(1)}, bf16[64,1280]{1,0:T(8,128)(2,1)S(1)}, u32[]{:S(2)}, u32[]{:S(2)}) collective-permute-start(bf16[64,1280]{1,0:T(8,128)(2,1)S(1)} %collective-permute-done.14.refs_10_.refs_6_), channel_id=1, source_target_pairs={{2,0},{6,2},{10,6},{14,10},{12,14},{8,12},{4,8},{0,4},{3,1},{7,3},... | collective-permute-start | bytes 491528 | tf_op jit(solution)/shard_map/ppermute | solution.py:330
  51.9 0.0 collective-permute-done.refs_1_
  51.9 0.5 collective-permute-start.8
  52.3 0.8 %shard_map.83 = (f32[256,128]{1,0:T(8,128)S(1)}, f32[256,128]{1,0:T(8,128)S(1)}) custom-call(bf16[256,4096]{1,0:T(8,128)(2,1)S(1)} %copy-done, bf16[256,2048]{1,0:T(8,128)(2,1)S(1)} %collective-permute-done.refs_1_, s32[8,512]{1,0:T(8,128)S(1)} %get-tuple-element.15.refs_2_.bounds_ref, s32[8,512]{1,0:T(8,128)S(1)} %collective-permute-done.1.refs_3_, ...), custom_call_target="tpu_custom_call" | custom-call | flops 536870912 | bytes 3145728 | tf_op jit(solution)/shard_map/pallas_call | solution.py:253
  53.1 0.0 collective-permute-done.13.refs_9_.refs_5_
  53.1 2.5 %collective-permute-done.7.refs_6_ = bf16[64,1280]{1,0:T(8,128)(2,1)S(1)} collective-permute-done((bf16[64,1280]{1,0:T(8,128)(2,1)S(1)}, bf16[64,1280]{1,0:T(8,128)(2,1)S(1)}, u32[]{:S(2)}, u32[]{:S(2)}) %collective-permute-start.7) | collective-permute-done | bytes 163872 | tf_op jit(solution)/shard_map/ppermute | solution.py:326
  55.6 2.1 %collective-permute-done.15.refs_11_.refs_7_ = bf16[64,1280]{1,0:T(8,128)(2,1)S(1)} collective-permute-done((bf16[64,1280]{1,0:T(8,128)(2,1)S(1)}, bf16[64,1280]{1,0:T(8,128)(2,1)S(1)}, u32[]{:S(2)}, u32[]{:S(2)}) %collective-permute-start.15) | collective-permute-done | bytes 163872 | tf_op jit(solution)/shard_map/ppermute | solution.py:330
  57.7 0.0 collective-permute-done.8.refs_7_
  57.7 0.9 %shard_map.84 = (f32[128,128]{1,0:T(8,128)S(1)}, f32[128,128]{1,0:T(8,128)S(1)}) custom-call(bf16[256,4096]{1,0:T(8,128)(2,1)S(1)} %copy-done, bf16[256,2048]{1,0:T(8,128)(2,1)S(1)} %collective-permute-done.refs_1_, s32[8,512]{1,0:T(8,128)S(1)} %get-tuple-element.15.refs_2_.bounds_ref, s32[8,512]{1,0:T(8,128)S(1)} %collective-permute-done.1.refs_3_, ...), custom_call_target="tpu_custom_call" | custom-call | flops 536870912 | bytes 3145728 | tf_op jit(solution)/shard_map/pallas_call | solution.py:253
  58.6 0.1 collective-permute-start.16
  58.7 1.8 %collective-permute-start.17 = (f32[128,128]{1,0:T(8,128)S(1)}, f32[128,128]{1,0:T(8,128)S(1)}, u32[]{:S(2)}, u32[]{:S(2)}) collective-permute-start(f32[128,128]{1,0:T(8,128)S(1)} %get-tuple-element.22), channel_id=1, source_target_pairs={{0,16},{16,0},{1,17},{17,1},{2,18},{18,2},{3,19},{19,3},{4,20},{20... | collective-permute-start | bytes 196616 | tf_op jit(solution)/shard_map/ppermute | solution.py:348
  60.5 0.1 collective-permute-start.18
  60.6 0.0 collective-permute-done.19.far_ref
  60.6 0.0 collective-permute-done.16.one
  60.6 2.6 %collective-permute-done.17.two = f32[128,128]{1,0:T(8,128)S(1)} collective-permute-done((f32[128,128]{1,0:T(8,128)S(1)}, f32[128,128]{1,0:T(8,128)S(1)}, u32[]{:S(2)}, u32[]{:S(2)}) %collective-permute-start.17) | collective-permute-done | bytes 65568 | tf_op jit(solution)/shard_map/ppermute | solution.py:348
  63.2 1.3 %collective-permute-done.18.three = f32[128,128]{1,0:T(8,128)S(1)} collective-permute-done((f32[128,128]{1,0:T(8,128)S(1)}, f32[128,128]{1,0:T(8,128)S(1)}, u32[]{:S(2)}, u32[]{:S(2)}) %collective-permute-start.18) | collective-permute-done | bytes 65568 | tf_op jit(solution)/shard_map/ppermute | solution.py:349
  64.6 1.1 %shard_map.86 = bf16[256,512]{1,0:T(8,128)(2,1)} custom-call(s32[8,512]{1,0:T(8,128)S(1)} %get-tuple-element.15.refs_2_.bounds_ref, f32[128,128]{1,0:T(8,128)S(1)} %get-tuple-element.21.mine, f32[128,128]{1,0:T(8,128)S(1)} %collective-permute-done.16.one, f32[128,128]{1,0:T(8,128)S(1)} %collective-permute-done.17.two, ...), custom_call_target="tpu_custom_call" | custom-call | tf_op jit(solution)/shard_map/pallas_call | solution.py:353
Async XLA Ops:
  1.5 50.4 %collective-permute-start = (bf16[256,2048]{1,0:T(8,128)(2,1)S(1)}, bf16[256,2048]{1,0:T(8,128)(2,1)S(1)}, u32[]{:S(2)}, u32[]{:S(2)}) collective-permute-start(bf16[256,2048]{1,0:T(8,128)(2,1)S(1)} %get-tuple-element.16), channel_id=1, source_target_pairs={{0,16},{16,0},{1,17},{17,1},{2,18},{18,2},{3,19},{19,3},{4,20},{20... | collective-permute-start | bytes 3145736 | tf_op jit(solution)/shard_map/ppermute | solution.py:331
  4.5 25.3 %collective-permute-start.11 = (bf16[64,1280]{1,0:T(8,128)(2,1)S(1)}, bf16[64,1280]{1,0:T(8,128)(2,1)S(1)}, u32[]{:S(2)}, u32[]{:S(2)}) collective-permute-start(bf16[64,1280]{1,0:T(8,128)(2,1)S(1)} %get-tuple-element.18.refs_8_.refs_0_), channel_id=1, source_target_pairs={{0,2},{2,6},{6,10},{10,14},{14,12},{12,8},{8,4},{4,0},{1,3},{3,7},... | collective-permute-start | bytes 491528 | tf_op jit(solution)/shard_map/ppermute | solution.py:325
  6.0 24.1 %collective-permute-start.4 = (bf16[64,1280]{1,0:T(8,128)(2,1)S(1)}, bf16[64,1280]{1,0:T(8,128)(2,1)S(1)}, u32[]{:S(2)}, u32[]{:S(2)}) collective-permute-start(bf16[64,1280]{1,0:T(8,128)(2,1)S(1)} %get-tuple-element.17.refs_4_), channel_id=1, source_target_pairs={{0,2},{2,6},{6,10},{10,14},{14,12},{12,8},{8,4},{4,0},{1,3},{3,7},... | collective-permute-start | bytes 491528 | tf_op jit(solution)/shard_map/ppermute | solution.py:323
  7.6 24.2 %collective-permute-start.9 = (bf16[64,1280]{1,0:T(8,128)(2,1)S(1)}, bf16[64,1280]{1,0:T(8,128)(2,1)S(1)}, u32[]{:S(2)}, u32[]{:S(2)}) collective-permute-start(bf16[64,1280]{1,0:T(8,128)(2,1)S(1)} %get-tuple-element.18.refs_8_.refs_0_), channel_id=1, source_target_pairs={{2,0},{6,2},{10,6},{14,10},{12,14},{8,12},{4,8},{0,4},{3,1},{7,3},... | collective-permute-start | bytes 491528 | tf_op jit(solution)/shard_map/ppermute | solution.py:324
  8.0 20.0 %collective-permute-start.1 = (s32[8,512]{1,0:T(8,128)S(1)}, s32[8,512]{1,0:T(8,128)S(1)}, u32[]{:S(2)}, u32[]{:S(2)}) collective-permute-start(s32[8,512]{1,0:T(8,128)S(1)} %get-tuple-element.15.refs_2_.bounds_ref), channel_id=1, source_target_pairs={{0,16},{16,0},{1,17},{17,1},{2,18},{18,2},{3,19},{19,3},{4,20},{20... | collective-permute-start | bytes 49160 | tf_op jit(solution)/shard_map/ppermute | solution.py:332
  28.0 10.2 %collective-permute-start.2 = (bf16[64,1280]{1,0:T(8,128)(2,1)S(1)}, bf16[64,1280]{1,0:T(8,128)(2,1)S(1)}, u32[]{:S(2)}, u32[]{:S(2)}) collective-permute-start(bf16[64,1280]{1,0:T(8,128)(2,1)S(1)} %get-tuple-element.17.refs_4_), channel_id=1, source_target_pairs={{2,0},{6,2},{10,6},{14,10},{12,14},{8,12},{4,8},{0,4},{3,1},{7,3},... | collective-permute-start | bytes 491528 | tf_op jit(solution)/shard_map/ppermute | solution.py:326
  29.8 8.5 %collective-permute-start.12 = (bf16[64,1280]{1,0:T(8,128)(2,1)S(1)}, bf16[64,1280]{1,0:T(8,128)(2,1)S(1)}, u32[]{:S(2)}, u32[]{:S(2)}) collective-permute-start(bf16[64,1280]{1,0:T(8,128)(2,1)S(1)} %collective-permute-done.11.refs_9_.refs_1_), channel_id=1, source_target_pairs={{0,2},{2,6},{6,10},{10,14},{14,12},{12,8},{8,4},{4,0},{1,3},{3,7},... | collective-permute-start | bytes 491528 | tf_op jit(solution)/shard_map/ppermute | solution.py:325
  30.1 11.7 %collective-permute-start.5 = (bf16[64,1280]{1,0:T(8,128)(2,1)S(1)}, bf16[64,1280]{1,0:T(8,128)(2,1)S(1)}, u32[]{:S(2)}, u32[]{:S(2)}) collective-permute-start(bf16[64,1280]{1,0:T(8,128)(2,1)S(1)} %collective-permute-done.4.refs_5_), channel_id=1, source_target_pairs={{0,2},{2,6},{6,10},{10,14},{14,12},{12,8},{8,4},{4,0},{1,3},{3,7},... | collective-permute-start | bytes 491528 | tf_op jit(solution)/shard_map/ppermute | solution.py:323
  31.8 8.4 %collective-permute-start.10 = (bf16[64,1280]{1,0:T(8,128)(2,1)S(1)}, bf16[64,1280]{1,0:T(8,128)(2,1)S(1)}, u32[]{:S(2)}, u32[]{:S(2)}) collective-permute-start(bf16[64,1280]{1,0:T(8,128)(2,1)S(1)} %collective-permute-done.9.refs_10_.refs_2_), channel_id=1, source_target_pairs={{2,0},{6,2},{10,6},{14,10},{12,14},{8,12},{4,8},{0,4},{3,1},{7,3},... | collective-permute-start | bytes 491528 | tf_op jit(solution)/shard_map/ppermute | solution.py:324
  32.1 1.6 %copy-start = (bf16[256,4096]{1,0:T(8,128)(2,1)S(1)}, bf16[256,4096]{1,0:T(8,128)(2,1)}, u32[]{:S(2)}) copy-start(bf16[256,4096]{1,0:T(8,128)(2,1)} %rows_ref.1) | copy-start | bytes 6291460
  38.3 22.3 %collective-permute-start.19 = (f32[256,512]{1,0:T(8,128)S(1)}, f32[256,512]{1,0:T(8,128)S(1)}, u32[]{:S(2)}, u32[]{:S(2)}) collective-permute-start(f32[256,512]{1,0:T(8,128)S(1)} %get-tuple-element.24), channel_id=1, source_target_pairs={{0,1},{1,0},{2,3},{3,2},{4,5},{5,4},{6,7},{7,6},{8,9},{9,8},{10,11... | collective-permute-start | bytes 1572872 | tf_op jit(solution)/shard_map/ppermute | solution.py:335
  38.4 7.1 %collective-permute-start.3 = (bf16[64,1280]{1,0:T(8,128)(2,1)S(1)}, bf16[64,1280]{1,0:T(8,128)(2,1)S(1)}, u32[]{:S(2)}, u32[]{:S(2)}) collective-permute-start(bf16[64,1280]{1,0:T(8,128)(2,1)S(1)} %collective-permute-done.2.refs_6_), channel_id=1, source_target_pairs={{2,0},{6,2},{10,6},{14,10},{12,14},{8,12},{4,8},{0,4},{3,1},{7,3},... | collective-permute-start | bytes 491528 | tf_op jit(solution)/shard_map/ppermute | solution.py:326
  40.2 8.3 %collective-permute-start.14 = (bf16[64,1280]{1,0:T(8,128)(2,1)S(1)}, bf16[64,1280]{1,0:T(8,128)(2,1)S(1)}, u32[]{:S(2)}, u32[]{:S(2)}) collective-permute-start(bf16[64,1280]{1,0:T(8,128)(2,1)S(1)} %collective-permute-done.10.refs_8_.refs_4_), channel_id=1, source_target_pairs={{2,0},{6,2},{10,6},{14,10},{12,14},{8,12},{4,8},{0,4},{3,1},{7,3},... | collective-permute-start | bytes 491528 | tf_op jit(solution)/shard_map/ppermute | solution.py:324
  41.8 8.5 %collective-permute-start.6 = (bf16[64,1280]{1,0:T(8,128)(2,1)S(1)}, bf16[64,1280]{1,0:T(8,128)(2,1)S(1)}, u32[]{:S(2)}, u32[]{:S(2)}) collective-permute-start(bf16[64,1280]{1,0:T(8,128)(2,1)S(1)} %collective-permute-done.5.refs_7_), channel_id=1, source_target_pairs={{0,2},{2,6},{6,10},{10,14},{14,12},{12,8},{8,4},{4,0},{1,3},{3,7},... | collective-permute-start | bytes 491528 | tf_op jit(solution)/shard_map/ppermute | solution.py:323
  45.4 7.7 %collective-permute-start.13 = (bf16[64,1280]{1,0:T(8,128)(2,1)S(1)}, bf16[64,1280]{1,0:T(8,128)(2,1)S(1)}, u32[]{:S(2)}, u32[]{:S(2)}) collective-permute-start(bf16[64,1280]{1,0:T(8,128)(2,1)S(1)} %collective-permute-done.12.refs_11_.refs_3_), channel_id=1, source_target_pairs={{0,2},{2,6},{6,10},{10,14},{14,12},{12,8},{8,4},{4,0},{1,3},{3,7},... | collective-permute-start | bytes 491528 | tf_op jit(solution)/shard_map/ppermute | solution.py:325
  48.5 7.1 %collective-permute-start.7 = (bf16[64,1280]{1,0:T(8,128)(2,1)S(1)}, bf16[64,1280]{1,0:T(8,128)(2,1)S(1)}, u32[]{:S(2)}, u32[]{:S(2)}) collective-permute-start(bf16[64,1280]{1,0:T(8,128)(2,1)S(1)} %collective-permute-done.3.refs_4_), channel_id=1, source_target_pairs={{2,0},{6,2},{10,6},{14,10},{12,14},{8,12},{4,8},{0,4},{3,1},{7,3},... | collective-permute-start | bytes 491528 | tf_op jit(solution)/shard_map/ppermute | solution.py:326
  50.3 7.5 %collective-permute-start.15 = (bf16[64,1280]{1,0:T(8,128)(2,1)S(1)}, bf16[64,1280]{1,0:T(8,128)(2,1)S(1)}, u32[]{:S(2)}, u32[]{:S(2)}) collective-permute-start(bf16[64,1280]{1,0:T(8,128)(2,1)S(1)} %collective-permute-done.14.refs_10_.refs_6_), channel_id=1, source_target_pairs={{2,0},{6,2},{10,6},{14,10},{12,14},{8,12},{4,8},{0,4},{3,1},{7,3},... | collective-permute-start | bytes 491528 | tf_op jit(solution)/shard_map/ppermute | solution.py:330
  51.9 5.9 %collective-permute-start.8 = (bf16[64,1280]{1,0:T(8,128)(2,1)S(1)}, bf16[64,1280]{1,0:T(8,128)(2,1)S(1)}, u32[]{:S(2)}, u32[]{:S(2)}) collective-permute-start(bf16[64,1280]{1,0:T(8,128)(2,1)S(1)} %collective-permute-done.6.refs_5_), channel_id=1, source_target_pairs={{0,2},{2,6},{6,10},{10,14},{14,12},{12,8},{8,4},{4,0},{1,3},{3,7},... | collective-permute-start | bytes 491528 | tf_op jit(solution)/shard_map/ppermute | solution.py:329
  58.6 2.0 %collective-permute-start.16 = (f32[128,128]{1,0:T(8,128)S(1)}, f32[128,128]{1,0:T(8,128)S(1)}, u32[]{:S(2)}, u32[]{:S(2)}) collective-permute-start(f32[128,128]{1,0:T(8,128)S(1)} %get-tuple-element.21.mine), channel_id=1, source_target_pairs={{0,1},{1,0},{2,3},{3,2},{4,5},{5,4},{6,7},{7,6},{8,9},{9,8},{10,11... | collective-permute-start | bytes 196616 | tf_op jit(solution)/shard_map/ppermute | solution.py:350
  58.7 4.5 %collective-permute-start.17 = (f32[128,128]{1,0:T(8,128)S(1)}, f32[128,128]{1,0:T(8,128)S(1)}, u32[]{:S(2)}, u32[]{:S(2)}) collective-permute-start(f32[128,128]{1,0:T(8,128)S(1)} %get-tuple-element.22), channel_id=1, source_target_pairs={{0,16},{16,0},{1,17},{17,1},{2,18},{18,2},{3,19},{19,3},{4,20},{20... | collective-permute-start | bytes 196616 | tf_op jit(solution)/shard_map/ppermute | solution.py:348
  60.5 4.0 %collective-permute-start.18 = (f32[128,128]{1,0:T(8,128)S(1)}, f32[128,128]{1,0:T(8,128)S(1)}, u32[]{:S(2)}, u32[]{:S(2)}) collective-permute-start(f32[128,128]{1,0:T(8,128)S(1)} %get-tuple-element.22), channel_id=1, source_target_pairs={{0,17},{1,16},{16,1},{17,0},{2,19},{3,18},{18,3},{19,2},{4,21},{5,... | collective-permute-start | bytes 196616 | tf_op jit(solution)/shard_map/ppermute | solution.py:349

commit v3 on v2

--- a/solution.py
+++ b/solution.py
@@ -74,7 +74,7 @@
             factor_ref.at[:, pl.ds(after, depth - cut)], second_ref.at[:, : depth - cut], sems.at[5]
         ),
         pltpu.make_async_copy(factor_out_ref, second_ref.at[:, depth - cut :], sems.at[6]),
-        pltpu.make_async_copy(hidden_ref.at[:, pl.ds(there, depth)], to_other_ref, sems.at[7]),
+        pltpu.make_async_copy(hidden_ref.at[:, pl.ds(there, depth)], to_other_ref.at[:-16], sems.at[7]),
     ]
     for copy in small + large:
         copy.start()
@@ -115,6 +115,13 @@
     bounds_ref[0:1, :] = carry[0]
     bounds_ref[1:2, :] = carry[1]
     bounds_ref[2:8, :] = jnp.zeros((6, count * rank), I32)
+    span = min(depth, count * rank)
+    line = lax.broadcasted_iota(I32, (16, span), 0)
+    extra = jnp.zeros((16, span), I32)
+    for i in range(count * rank // span):
+        for first_line, ends in ((0, carry[0]), (8, carry[1])):
+            extra = jnp.where(line == first_line + i, ends[:, i * span : (i + 1) * span], extra)
+    to_other_ref[-16:, :span] = extra.astype(F32).astype(BF16)
     for copy in large:
         copy.wait()
 
@@ -128,7 +135,7 @@
     return pl.pallas_call(
         functools.partial(prologue_kernel, depth, rank),
         out_shape=(
-            jax.ShapeDtypeStruct((rows, depth), hidden.dtype),
+            jax.ShapeDtypeStruct((rows + 16, depth), hidden.dtype),
             jax.ShapeDtypeStruct((rank, cut), factor.dtype),
             jax.ShapeDtypeStruct((rank, cut), factor.dtype),
             jax.ShapeDtypeStruct((8, count * rank), I32),
@@ -146,30 +153,30 @@
     )(*map(in_hbm, (hidden, factor, factor_out, demand, lengths, holder_slot, slots)))
 
 
-def base_kernel(rows_ref, weight_ref, near_ref, far_ref, buffer, sems):
+def base_kernel(hidden_ref, weight_ref, near_ref, far_ref, rows_ref, buffer, sems):
     width = near_ref.shape[1]
     core = lax.axis_index("tensor")
     here = pl.multiple_of(core * width, 128)
     there = pl.multiple_of((1 - core) * width, 128)
-    step = buffer.shape[1]
-    steps = weight_ref.shape[0] // step
-
-    def fetch(k):
-        return pltpu.make_async_copy(
-            weight_ref.at[pl.ds(k * step, step)], buffer.at[k % 3], sems.at[k % 3]
+    steps, step = buffer.shape[:2]
+    copies = []
+    for k in range(steps):
+        span = pl.ds(k * step, step)
+        copies.append(
+            (
+                pltpu.make_async_copy(hidden_ref.at[:, span], rows_ref.at[:, span], sems.at[0, k]),
+                pltpu.make_async_copy(weight_ref.at[span], buffer.at[k], sems.at[1, k]),
+            )
         )
-
-    fetch(0).start()
-    if steps > 1:
-        fetch(1).start()
-    for k in range(steps):
-        if k + 2 < steps:
-            fetch(k + 2).start()
-        fetch(k).wait()
+    for pair in copies:
+        for copy in pair:
+            copy.start()
+    for k, pair in enumerate(copies):
+        for copy in pair:
+            copy.wait()
         rows = rows_ref[:, k * step : (k + 1) * step]
-        weight = buffer.at[k % 3]
         for out_ref, offset in ((far_ref, there), (near_ref, here)):
-            part = jnp.dot(rows, weight[:, pl.ds(offset, width)], preferred_element_type=F32)
+            part = jnp.dot(rows, buffer[k, :, pl.ds(offset, width)], preferred_element_type=F32)
             if k == 0:
                 out_ref[...] = part
             else:
@@ -179,16 +186,16 @@
 def base_call(hidden, weight):
     rows, depth = hidden.shape
     width = weight.shape[1] // 2
-    step = 1024
+    steps = 8
     out = jax.ShapeDtypeStruct((rows, width), F32)
     return pl.pallas_call(
         base_kernel,
-        out_shape=(out, out),
-        in_specs=[VMEM, HBM],
-        out_specs=(VMEM, VMEM),
+        out_shape=(out, out, jax.ShapeDtypeStruct(hidden.shape, hidden.dtype)),
+        in_specs=[HBM, HBM],
+        out_specs=(VMEM,) * 3,
         scratch_shapes=[
-            pltpu.VMEM((3, step, 2 * width), weight.dtype),
-            pltpu.SemaphoreType.DMA((3,)),
+            pltpu.VMEM((steps, depth // steps, 2 * width), weight.dtype),
+            pltpu.SemaphoreType.DMA((2, steps)),
         ],
         compiler_params=params(),
         cost_estimate=pl.CostEstimate(
@@ -196,13 +203,23 @@
             bytes_accessed=2 * depth * (rows + 2 * width) + 8 * rows * width,
             transcendentals=0,
         ),
-    )(hidden, in_hbm(weight))
-
-
-def group_mask(bounds_ref, group, size, shape):
+    )(in_hbm(hidden), in_hbm(weight))
+
+
+def group_mask(low, high, shape):
     row = lax.broadcasted_iota(I32, shape, 0)
-    columns = pl.ds(group * size, shape[1])
-    return (row >= bounds_ref[0:1, columns]) & (row < bounds_ref[1:2, columns])
+    return (row >= low) & (row < high)
+
+
+def own_ends(bounds_ref, group, size):
+    columns = slice(group * size, (group + 1) * size)
+    return bounds_ref[0:1, columns], bounds_ref[1:2, columns]
+
+
+def other_ends(other_ref, group, size):
+    line, column = divmod(group * size, other_ref.shape[1])
+    ends = other_ref[-16:, column : column + size].astype(F32).astype(I32)
+    return ends[line : line + 1], ends[8 + line : 9 + line]
 
 
 def fold(masked):
@@ -214,27 +231,27 @@
 
 def rank_kernel(groups, depth, last, *refs):
     refs = list(refs)
-    own_ref, other_ref, own_bounds, other_bounds = refs[:4]
-    pieces = refs[4:]
+    own_ref, other_ref, bounds_ref = refs[:3]
+    pieces = refs[3:]
     pieces, rest = pieces[: 2 * GROUP * len(groups)], pieces[2 * GROUP * len(groups) :]
     starts, outs = (rest[:2], rest[2:]) if last else ((None, None), rest)
     cut = pieces[0].shape[1]
     offset = pl.multiple_of(lax.axis_index("groups") * depth, 128)
     own = own_ref[:, pl.ds(offset, depth)]
-    other = other_ref[...]
+    other = other_ref[:-16]
     rank = pieces[0].shape[0]
     size = GROUP * rank
-    sides = ((own, own_bounds, starts[0], outs[0]), (other, other_bounds, starts[1], outs[1]))
-    totals = [start_ref[...] if last else None for _, _, start_ref, _ in sides]
+    totals = [start_ref[...] if last else None for start_ref in starts]
     for i, group in enumerate(groups):
         held = pieces[2 * GROUP * i : 2 * GROUP * (i + 1)]
         first = jnp.concatenate([ref[...] for ref in held[:GROUP]], axis=0)
         second = jnp.concatenate([ref[:, : depth - cut] for ref in held[GROUP:]], axis=0)
-        for s, (rows, bounds, _, _) in enumerate(sides):
+        ends = (own_ends(bounds_ref, group, size), other_ends(other_ref, group, size))
+        for s, rows in enumerate((own, other)):
             part = contract(rows[:, :cut], first) + contract(rows[:, cut:], second)
-            kept = fold(jnp.where(group_mask(bounds, group, size, part.shape), part, 0.0))
+            kept = fold(jnp.where(group_mask(*ends[s], part.shape), part, 0.0))
             totals[s] = kept if totals[s] is None else totals[s] + kept
-    for total, (_, _, _, out_ref) in zip(totals, sides):
+    for total, out_ref in zip(totals, outs):
         if last:
             total = total + pltpu.roll(total, rank, 1)
             half = total.shape[0] // 2
@@ -243,13 +260,13 @@
         out_ref[...] = total
 
 
-def rank_call(groups, depth, own, other, own_bounds, other_bounds, pieces, starts):
+def rank_call(groups, depth, own, other, bounds, pieces, starts):
     rows = own.shape[0]
     rank = pieces[0].shape[0]
     last = starts is not None
     shape = (rows // 2, 2 * rank) if last else (rows, 2 * rank)
     out = jax.ShapeDtypeStruct(shape, F32)
-    operands = [own, other, own_bounds, other_bounds, *pieces, *(starts or ())]
+    operands = [own, other, bounds, *pieces, *(starts or ())]
     return pl.pallas_call(
         functools.partial(rank_kernel, groups, depth, last),
         out_shape=(out, out),
@@ -277,7 +294,7 @@
     wide = jnp.concatenate([values] * (GROUP // 2), axis=1)
     total = None
     for group in range(len(factors) // GROUP):
-        mask = group_mask(bounds_ref, group, GROUP * rank, wide.shape)
+        mask = group_mask(*own_ends(bounds_ref, group, GROUP * rank), wide.shape)
         chosen = jnp.where(mask, wide, 0.0).astype(BF16)
         factor = jnp.concatenate(
             [ref[:, begin:] for ref in factors[group * GROUP : (group + 1) * GROUP]], axis=0
@@ -329,9 +346,8 @@
     firsts.append(lax.ppermute(ahead[0], "batch", forward))
     seconds.append(lax.ppermute(behind[1], "batch", backward))
     other = lax.ppermute(to_other, "groups", swap)
-    other_bounds = lax.ppermute(bounds, "groups", swap)
-
-    near, far = base_call(hidden, value_weight)
+
+    near, far, held = base_call(hidden, value_weight)
     far = lax.ppermute(far, "tensor", swap)
 
     count = owners // GROUP
@@ -340,14 +356,14 @@
     for group in early:
         pieces += firsts[group * GROUP : (group + 1) * GROUP]
         pieces += seconds[group * GROUP : (group + 1) * GROUP]
-    sides = (hidden, other, bounds, other_bounds)
+    sides = (held, other, bounds)
     starts = rank_call(tuple(early), depth, *sides, pieces, None)
     pieces = firsts[-GROUP:] + seconds[-GROUP:]
     mine, theirs = rank_call((count - 1,), depth, *sides, pieces, starts)
 
     two = lax.ppermute(theirs, "groups", swap)
-    three = lax.ppermute(theirs, ("groups", "tensor"), [(0, 3), (1, 2), (2, 1), (3, 0)])
     one = lax.ppermute(mine, "tensor", swap)
+    three = lax.ppermute(two, "tensor", swap)
 
     operands = [bounds, mine, one, two, three, near, far, *seconds]
     return pl.pallas_call(

time: 65.9 us -> 49 us (0.74)
  waiting for transfers between devices: 32.6 us -> 20 us
  starting transfers between devices: 22.5 us -> 19.9 us
  local copies, waits for them, and re-layouts: 1.59 us -> 0 us
    ppermute x2 -> x1, waiting for transfers between devices: 20.8 us -> 1.24 us  [per_device(): three = lax.ppermute(two, 'tensor', swap)]
    ppermute x3, waiting for transfers between devices: 0.01 us -> 3.08 us  [per_device(): ahead = (a, lax.ppermute(ahead[1], 'batch', forward))]
    ppermute x3, waiting for transfers between devices: 0.01 us -> 2.02 us  [per_device(): a = lax.ppermute(ahead[0], 'batch', forward)]
    ppermute x3, starting transfers between devices: 5.44 us -> 3.74 us  [per_device(): behind = (lax.ppermute(behind[0], 'batch', backward), b)]
    unnamed x2 -> x0, local copies, waits for them, and re-layouts: 1.59 us -> none
    ppermute x1, starting transfers between devices: 1.81 us -> 0.45 us  [per_device(): two = lax.ppermute(theirs, 'groups', swap)]
    ppermute x1, waiting for transfers between devices: 2.63 us -> 3.87 us  [per_device(): two = lax.ppermute(theirs, 'groups', swap)]
    ppermute x3, starting transfers between devices: 3.43 us -> 4.47 us  [per_device(): ahead = (a, lax.ppermute(ahead[1], 'batch', forward))]
  transfers between devices with their start and end apart: 20 -> 19, of which waited for: 7 -> 8; matrix products, arithmetic and copies ran while one was open for 0% -> 0% of each run, Pallas kernels for 9% -> 13%
where the time goes in v3:
time: 49 us; the launch traced here: 48.8 us
  waiting for transfers between devices  20 us (41%)
  starting transfers between devices  19.9 us (41%)
  Pallas kernels  8.84 us (18%)
    ppermute x3, waiting for transfers between devices, per_device(): behind = (lax.ppermute(behind[0], 'batch', backward), b)  6.1 us
    pallas_call x1, Pallas kernels, base_call(): pl.pallas_call(base_kernel, out_shape=(out, out, jax.ShapeDtypeStruct(hid...  4.61 us
    ppermute x3, starting transfers between devices, per_device(): ahead = (a, lax.ppermute(ahead[1], 'batch', forward))  4.47 us
    ppermute x1, waiting for transfers between devices, per_device(): two = lax.ppermute(theirs, 'groups', swap)  3.87 us
    ppermute x3, starting transfers between devices, per_device(): behind = (lax.ppermute(behind[0], 'batch', backward), b)  3.74 us
    ppermute x3, starting transfers between devices, per_device(): a = lax.ppermute(ahead[0], 'batch', forward)  3.52 us
    ppermute x3, waiting for transfers between devices, per_device(): ahead = (a, lax.ppermute(ahead[1], 'batch', forward))  3.08 us
    ppermute x1, starting transfers between devices, per_device(): other = lax.ppermute(to_other, 'groups', swap)  3.03 us
  transfers between devices with their start and end apart: 19, of which 8 were waited for; matrix products, arithmetic and copies ran while one was open for 0% of the time, Pallas kernels for 13%

profile of v3, /device:TPU:0, one launch (start us, length us, event | category | flops | bytes accessed | tf_op | source)
XLA Modules:
  0.0 48.8 jit_solution(516912501914223616)
XLA Ops:
  0.0 1.5 %shard_map.82 = (bf16[272,2048]{1,0:T(8,128)(2,1)S(1)}, bf16[64,1280]{1,0:T(8,128)(2,1)S(1)}, bf16[64,1280]{1,0:T(8,128)(2,1)S(1)}, s32[8,512]{1,0:T(8,128)S(1)}) custom-call(bf16[256,4096]{1,0:T(8,128)(2,1)} %hidden_ref.3, bf16[64,4096]{1,0:T(8,128)(2,1)} %bitcast.4, bf16[64,512]{1,0:T(8,128)(2,1)} %bitcast.5, s32[1,4]{1,0:T(1,128)} %demand_ref.1, ...), custom_call_target="tpu_custom_call" | custom-call | tf_op jit(solution)/shard_map/pallas_call | solution.py:135
  1.5 3.0 %collective-permute-start = (bf16[272,2048]{1,0:T(8,128)(2,1)S(1)}, bf16[272,2048]{1,0:T(8,128)(2,1)S(1)}, u32[]{:S(2)}, u32[]{:S(2)}) collective-permute-start(bf16[272,2048]{1,0:T(8,128)(2,1)S(1)} %get-tuple-element.18), channel_id=1, source_target_pairs={{0,16},{16,0},{1,17},{17,1},{2,18},{18,2},{3,19},{19,3},{4,20},{20... | collective-permute-start | bytes 3342344 | tf_op jit(solution)/shard_map/ppermute | solution.py:348
  4.5 1.5 %collective-permute-start.10 = (bf16[64,1280]{1,0:T(8,128)(2,1)S(1)}, bf16[64,1280]{1,0:T(8,128)(2,1)S(1)}, u32[]{:S(2)}, u32[]{:S(2)}) collective-permute-start(bf16[64,1280]{1,0:T(8,128)(2,1)S(1)} %get-tuple-element.20.refs_7_.refs_0_), channel_id=1, source_target_pairs={{0,2},{2,6},{6,10},{10,14},{14,12},{12,8},{8,4},{4,0},{1,3},{3,7},... | collective-permute-start | bytes 491528 | tf_op jit(solution)/shard_map/ppermute | solution.py:342
  6.0 1.6 %collective-permute-start.3 = (bf16[64,1280]{1,0:T(8,128)(2,1)S(1)}, bf16[64,1280]{1,0:T(8,128)(2,1)S(1)}, u32[]{:S(2)}, u32[]{:S(2)}) collective-permute-start(bf16[64,1280]{1,0:T(8,128)(2,1)S(1)} %get-tuple-element.19.refs_3_), channel_id=1, source_target_pairs={{0,2},{2,6},{6,10},{10,14},{14,12},{12,8},{8,4},{4,0},{1,3},{3,7},... | collective-permute-start | bytes 491528 | tf_op jit(solution)/shard_map/ppermute | solution.py:340
  7.6 0.4 collective-permute-start.8
  8.0 0.5 %collective-permute-start.1 = (bf16[64,1280]{1,0:T(8,128)(2,1)S(1)}, bf16[64,1280]{1,0:T(8,128)(2,1)S(1)}, u32[]{:S(2)}, u32[]{:S(2)}) collective-permute-start(bf16[64,1280]{1,0:T(8,128)(2,1)S(1)} %get-tuple-element.19.refs_3_), channel_id=1, source_target_pairs={{2,0},{6,2},{10,6},{14,10},{12,14},{8,12},{4,8},{0,4},{3,1},{7,3},... | collective-permute-start | bytes 491528 | tf_op jit(solution)/shard_map/ppermute | solution.py:343
  8.6 3.1 %collective-permute-done.10.refs_8_.refs_1_ = bf16[64,1280]{1,0:T(8,128)(2,1)S(1)} collective-permute-done((bf16[64,1280]{1,0:T(8,128)(2,1)S(1)}, bf16[64,1280]{1,0:T(8,128)(2,1)S(1)}, u32[]{:S(2)}, u32[]{:S(2)}) %collective-permute-start.10) | collective-permute-done | bytes 163872 | tf_op jit(solution)/shard_map/ppermute | solution.py:342
  11.6 1.5 %collective-permute-start.11 = (bf16[64,1280]{1,0:T(8,128)(2,1)S(1)}, bf16[64,1280]{1,0:T(8,128)(2,1)S(1)}, u32[]{:S(2)}, u32[]{:S(2)}) collective-permute-start(bf16[64,1280]{1,0:T(8,128)(2,1)S(1)} %collective-permute-done.10.refs_8_.refs_1_), channel_id=1, source_target_pairs={{0,2},{2,6},{6,10},{10,14},{14,12},{12,8},{8,4},{4,0},{1,3},{3,7},... | collective-permute-start | bytes 491528 | tf_op jit(solution)/shard_map/ppermute | solution.py:342
  13.1 2.0 %collective-permute-done.3.refs_4_ = bf16[64,1280]{1,0:T(8,128)(2,1)S(1)} collective-permute-done((bf16[64,1280]{1,0:T(8,128)(2,1)S(1)}, bf16[64,1280]{1,0:T(8,128)(2,1)S(1)}, u32[]{:S(2)}, u32[]{:S(2)}) %collective-permute-start.3) | collective-permute-done | bytes 163872 | tf_op jit(solution)/shard_map/ppermute | solution.py:340
  15.1 1.5 %collective-permute-start.4 = (bf16[64,1280]{1,0:T(8,128)(2,1)S(1)}, bf16[64,1280]{1,0:T(8,128)(2,1)S(1)}, u32[]{:S(2)}, u32[]{:S(2)}) collective-permute-start(bf16[64,1280]{1,0:T(8,128)(2,1)S(1)} %collective-permute-done.3.refs_4_), channel_id=1, source_target_pairs={{0,2},{2,6},{6,10},{10,14},{14,12},{12,8},{8,4},{4,0},{1,3},{3,7},... | collective-permute-start | bytes 491528 | tf_op jit(solution)/shard_map/ppermute | solution.py:340
  16.6 0.0 collective-permute-done.8.refs_9_.refs_2_
  16.6 0.5 %collective-permute-start.9 = (bf16[64,1280]{1,0:T(8,128)(2,1)S(1)}, bf16[64,1280]{1,0:T(8,128)(2,1)S(1)}, u32[]{:S(2)}, u32[]{:S(2)}) collective-permute-start(bf16[64,1280]{1,0:T(8,128)(2,1)S(1)} %collective-permute-done.8.refs_9_.refs_2_), channel_id=1, source_target_pairs={{2,0},{6,2},{10,6},{14,10},{12,14},{8,12},{4,8},{0,4},{3,1},{7,3},... | collective-permute-start | bytes 491528 | tf_op jit(solution)/shard_map/ppermute | solution.py:341
  17.2 4.6 %shard_map.83 = (f32[256,512]{1,0:T(8,128)S(1)}, f32[256,512]{1,0:T(8,128)S(1)}, bf16[256,4096]{1,0:T(8,128)(2,1)S(1)}) custom-call(bf16[256,4096]{1,0:T(8,128)(2,1)} %hidden_ref.3, bf16[4096,1024]{1,0:T(8,128)(2,1)} %weight_ref.1), custom_call_target="tpu_custom_call" | custom-call | flops 2147483648 | bytes 11534336 | tf_op jit(solution)/shard_map/pallas_call | solution.py:191
  21.8 0.0 collective-permute-done.1.refs_5_
  21.8 0.1 collective-permute-start.18
  21.9 0.0 collective-permute-done.11.refs_10_.refs_3_
  21.9 1.6 %collective-permute-start.2 = (bf16[64,1280]{1,0:T(8,128)(2,1)S(1)}, bf16[64,1280]{1,0:T(8,128)(2,1)S(1)}, u32[]{:S(2)}, u32[]{:S(2)}) collective-permute-start(bf16[64,1280]{1,0:T(8,128)(2,1)S(1)} %collective-permute-done.1.refs_5_), channel_id=1, source_target_pairs={{2,0},{6,2},{10,6},{14,10},{12,14},{8,12},{4,8},{0,4},{3,1},{7,3},... | collective-permute-start | bytes 491528 | tf_op jit(solution)/shard_map/ppermute | solution.py:343
  23.5 0.0 collective-permute-done.9.refs_7_.refs_4_
  23.5 1.6 %collective-permute-start.13 = (bf16[64,1280]{1,0:T(8,128)(2,1)S(1)}, bf16[64,1280]{1,0:T(8,128)(2,1)S(1)}, u32[]{:S(2)}, u32[]{:S(2)}) collective-permute-start(bf16[64,1280]{1,0:T(8,128)(2,1)S(1)} %collective-permute-done.9.refs_7_.refs_4_), channel_id=1, source_target_pairs={{2,0},{6,2},{10,6},{14,10},{12,14},{8,12},{4,8},{0,4},{3,1},{7,3},... | collective-permute-start | bytes 491528 | tf_op jit(solution)/shard_map/ppermute | solution.py:341
  25.1 0.0 collective-permute-done.4.refs_6_
  25.1 0.5 collective-permute-start.5
  25.6 3.4 %collective-permute-done.2.refs_3_ = bf16[64,1280]{1,0:T(8,128)(2,1)S(1)} collective-permute-done((bf16[64,1280]{1,0:T(8,128)(2,1)S(1)}, bf16[64,1280]{1,0:T(8,128)(2,1)S(1)}, u32[]{:S(2)}, u32[]{:S(2)}) %collective-permute-start.2) | collective-permute-done | bytes 163872 | tf_op jit(solution)/shard_map/ppermute | solution.py:343
  28.9 1.5 %collective-permute-start.12 = (bf16[64,1280]{1,0:T(8,128)(2,1)S(1)}, bf16[64,1280]{1,0:T(8,128)(2,1)S(1)}, u32[]{:S(2)}, u32[]{:S(2)}) collective-permute-start(bf16[64,1280]{1,0:T(8,128)(2,1)S(1)} %collective-permute-done.11.refs_10_.refs_3_), channel_id=1, source_target_pairs={{0,2},{2,6},{6,10},{10,14},{14,12},{12,8},{8,4},{4,0},{1,3},{3,7},... | collective-permute-start | bytes 491528 | tf_op jit(solution)/shard_map/ppermute | solution.py:342
  30.4 1.6 %collective-permute-done.13.refs_9_.refs_6_ = bf16[64,1280]{1,0:T(8,128)(2,1)S(1)} collective-permute-done((bf16[64,1280]{1,0:T(8,128)(2,1)S(1)}, bf16[64,1280]{1,0:T(8,128)(2,1)S(1)}, u32[]{:S(2)}, u32[]{:S(2)}) %collective-permute-start.13) | collective-permute-done | bytes 163872 | tf_op jit(solution)/shard_map/ppermute | solution.py:341
  32.0 1.6 %collective-permute-start.6 = (bf16[64,1280]{1,0:T(8,128)(2,1)S(1)}, bf16[64,1280]{1,0:T(8,128)(2,1)S(1)}, u32[]{:S(2)}, u32[]{:S(2)}) collective-permute-start(bf16[64,1280]{1,0:T(8,128)(2,1)S(1)} %collective-permute-done.2.refs_3_), channel_id=1, source_target_pairs={{2,0},{6,2},{10,6},{14,10},{12,14},{8,12},{4,8},{0,4},{3,1},{7,3},... | collective-permute-start | bytes 491528 | tf_op jit(solution)/shard_map/ppermute | solution.py:343
  33.6 0.0 collective-permute-done.5.refs_4_
  33.6 1.6 %collective-permute-start.14 = (bf16[64,1280]{1,0:T(8,128)(2,1)S(1)}, bf16[64,1280]{1,0:T(8,128)(2,1)S(1)}, u32[]{:S(2)}, u32[]{:S(2)}) collective-permute-start(bf16[64,1280]{1,0:T(8,128)(2,1)S(1)} %collective-permute-done.13.refs_9_.refs_6_), channel_id=1, source_target_pairs={{2,0},{6,2},{10,6},{14,10},{12,14},{8,12},{4,8},{0,4},{3,1},{7,3},... | collective-permute-start | bytes 491528 | tf_op jit(solution)/shard_map/ppermute | solution.py:347
  35.2 0.0 collective-permute-done.refs_1_
  35.2 0.5 collective-permute-start.7
  35.6 0.8 %shard_map.84 = (f32[256,128]{1,0:T(8,128)S(1)}, f32[256,128]{1,0:T(8,128)S(1)}) custom-call(bf16[256,4096]{1,0:T(8,128)(2,1)S(1)} %get-tuple-element.17.refs_0_, bf16[272,2048]{1,0:T(8,128)(2,1)S(1)} %collective-permute-done.refs_1_, s32[8,512]{1,0:T(8,128)S(1)} %get-tuple-element.16.refs_2_.bounds_ref, bf16[64,1280]{1,0:T(8,128)(2,1)S(1)} %get-tuple-element.19.refs_3_, ...), custom_call_target="tpu_custom_call" | custom-call | flops 536870912 | bytes 3145728 | tf_op jit(solution)/shard_map/pallas_call | solution.py:270
  36.4 0.0 collective-permute-done.12.refs_8_.refs_5_
  36.4 2.7 %collective-permute-done.6.refs_5_ = bf16[64,1280]{1,0:T(8,128)(2,1)S(1)} collective-permute-done((bf16[64,1280]{1,0:T(8,128)(2,1)S(1)}, bf16[64,1280]{1,0:T(8,128)(2,1)S(1)}, u32[]{:S(2)}, u32[]{:S(2)}) %collective-permute-start.6) | collective-permute-done | bytes 163872 | tf_op jit(solution)/shard_map/ppermute | solution.py:343
  39.1 2.1 %collective-permute-done.14.refs_10_.refs_7_ = bf16[64,1280]{1,0:T(8,128)(2,1)S(1)} collective-permute-done((bf16[64,1280]{1,0:T(8,128)(2,1)S(1)}, bf16[64,1280]{1,0:T(8,128)(2,1)S(1)}, u32[]{:S(2)}, u32[]{:S(2)}) %collective-permute-start.14) | collective-permute-done | bytes 163872 | tf_op jit(solution)/shard_map/ppermute | solution.py:347
  41.3 0.0 collective-permute-done.7.refs_6_
  41.3 0.9 %shard_map.85 = (f32[128,128]{1,0:T(8,128)S(1)}, f32[128,128]{1,0:T(8,128)S(1)}) custom-call(bf16[256,4096]{1,0:T(8,128)(2,1)S(1)} %get-tuple-element.17.refs_0_, bf16[272,2048]{1,0:T(8,128)(2,1)S(1)} %collective-permute-done.refs_1_, s32[8,512]{1,0:T(8,128)S(1)} %get-tuple-element.16.refs_2_.bounds_ref, ...), custom_call_target="tpu_custom_call" | custom-call | flops 536870912 | bytes 3145728 | tf_op jit(solution)/shard_map/pallas_call | solution.py:270
  42.1 0.5 collective-permute-start.16
  42.6 0.0 collective-permute-start.15
  42.6 3.9 %collective-permute-done.16.two = f32[128,128]{1,0:T(8,128)S(1)} collective-permute-done((f32[128,128]{1,0:T(8,128)S(1)}, f32[128,128]{1,0:T(8,128)S(1)}, u32[]{:S(2)}, u32[]{:S(2)}) %collective-permute-start.16) | collective-permute-done | bytes 65568 | tf_op jit(solution)/shard_map/ppermute | solution.py:364
  46.5 0.0 collective-permute-start.17
  46.5 0.0 collective-permute-done.18.far_ref
  46.5 0.0 collective-permute-done.15.one
  46.5 1.2 %collective-permute-done.17.three = f32[128,128]{1,0:T(8,128)S(1)} collective-permute-done((f32[128,128]{1,0:T(8,128)S(1)}, f32[128,128]{1,0:T(8,128)S(1)}, u32[]{:S(2)}, u32[]{:S(2)}) %collective-permute-start.17) | collective-permute-done | bytes 65568 | tf_op jit(solution)/shard_map/ppermute | solution.py:366
  47.7 1.1 %shard_map.86 = bf16[256,512]{1,0:T(8,128)(2,1)} custom-call(s32[8,512]{1,0:T(8,128)S(1)} %get-tuple-element.16.refs_2_.bounds_ref, f32[128,128]{1,0:T(8,128)S(1)} %get-tuple-element.23.mine, f32[128,128]{1,0:T(8,128)S(1)} %collective-permute-done.15.one, f32[128,128]{1,0:T(8,128)S(1)} %collective-permute-done.16.two, ...), custom_call_target="tpu_custom_call" | custom-call | tf_op jit(solution)/shard_map/pallas_call | solution.py:369
Async XLA Ops:
  1.5 33.7 %collective-permute-start = (bf16[272,2048]{1,0:T(8,128)(2,1)S(1)}, bf16[272,2048]{1,0:T(8,128)(2,1)S(1)}, u32[]{:S(2)}, u32[]{:S(2)}) collective-permute-start(bf16[272,2048]{1,0:T(8,128)(2,1)S(1)} %get-tuple-element.18), channel_id=1, source_target_pairs={{0,16},{16,0},{1,17},{17,1},{2,18},{18,2},{3,19},{19,3},{4,20},{20... | collective-permute-start | bytes 3342344 | tf_op jit(solution)/shard_map/ppermute | solution.py:348
  4.5 7.1 %collective-permute-start.10 = (bf16[64,1280]{1,0:T(8,128)(2,1)S(1)}, bf16[64,1280]{1,0:T(8,128)(2,1)S(1)}, u32[]{:S(2)}, u32[]{:S(2)}) collective-permute-start(bf16[64,1280]{1,0:T(8,128)(2,1)S(1)} %get-tuple-element.20.refs_7_.refs_0_), channel_id=1, source_target_pairs={{0,2},{2,6},{6,10},{10,14},{14,12},{12,8},{8,4},{4,0},{1,3},{3,7},... | collective-permute-start | bytes 491528 | tf_op jit(solution)/shard_map/ppermute | solution.py:342
  6.0 9.1 %collective-permute-start.3 = (bf16[64,1280]{1,0:T(8,128)(2,1)S(1)}, bf16[64,1280]{1,0:T(8,128)(2,1)S(1)}, u32[]{:S(2)}, u32[]{:S(2)}) collective-permute-start(bf16[64,1280]{1,0:T(8,128)(2,1)S(1)} %get-tuple-element.19.refs_3_), channel_id=1, source_target_pairs={{0,2},{2,6},{6,10},{10,14},{14,12},{12,8},{8,4},{4,0},{1,3},{3,7},... | collective-permute-start | bytes 491528 | tf_op jit(solution)/shard_map/ppermute | solution.py:340
  7.6 9.1 %collective-permute-start.8 = (bf16[64,1280]{1,0:T(8,128)(2,1)S(1)}, bf16[64,1280]{1,0:T(8,128)(2,1)S(1)}, u32[]{:S(2)}, u32[]{:S(2)}) collective-permute-start(bf16[64,1280]{1,0:T(8,128)(2,1)S(1)} %get-tuple-element.20.refs_7_.refs_0_), channel_id=1, source_target_pairs={{2,0},{6,2},{10,6},{14,10},{12,14},{8,12},{4,8},{0,4},{3,1},{7,3},... | collective-permute-start | bytes 491528 | tf_op jit(solution)/shard_map/ppermute | solution.py:341
  8.0 13.8 %collective-permute-start.1 = (bf16[64,1280]{1,0:T(8,128)(2,1)S(1)}, bf16[64,1280]{1,0:T(8,128)(2,1)S(1)}, u32[]{:S(2)}, u32[]{:S(2)}) collective-permute-start(bf16[64,1280]{1,0:T(8,128)(2,1)S(1)} %get-tuple-element.19.refs_3_), channel_id=1, source_target_pairs={{2,0},{6,2},{10,6},{14,10},{12,14},{8,12},{4,8},{0,4},{3,1},{7,3},... | collective-permute-start | bytes 491528 | tf_op jit(solution)/shard_map/ppermute | solution.py:343
  11.6 10.2 %collective-permute-start.11 = (bf16[64,1280]{1,0:T(8,128)(2,1)S(1)}, bf16[64,1280]{1,0:T(8,128)(2,1)S(1)}, u32[]{:S(2)}, u32[]{:S(2)}) collective-permute-start(bf16[64,1280]{1,0:T(8,128)(2,1)S(1)} %collective-permute-done.10.refs_8_.refs_1_), channel_id=1, source_target_pairs={{0,2},{2,6},{6,10},{10,14},{14,12},{12,8},{8,4},{4,0},{1,3},{3,7},... | collective-permute-start | bytes 491528 | tf_op jit(solution)/shard_map/ppermute | solution.py:342
  15.1 10.0 %collective-permute-start.4 = (bf16[64,1280]{1,0:T(8,128)(2,1)S(1)}, bf16[64,1280]{1,0:T(8,128)(2,1)S(1)}, u32[]{:S(2)}, u32[]{:S(2)}) collective-permute-start(bf16[64,1280]{1,0:T(8,128)(2,1)S(1)} %collective-permute-done.3.refs_4_), channel_id=1, source_target_pairs={{0,2},{2,6},{6,10},{10,14},{14,12},{12,8},{8,4},{4,0},{1,3},{3,7},... | collective-permute-start | bytes 491528 | tf_op jit(solution)/shard_map/ppermute | solution.py:340
  16.6 6.9 %collective-permute-start.9 = (bf16[64,1280]{1,0:T(8,128)(2,1)S(1)}, bf16[64,1280]{1,0:T(8,128)(2,1)S(1)}, u32[]{:S(2)}, u32[]{:S(2)}) collective-permute-start(bf16[64,1280]{1,0:T(8,128)(2,1)S(1)} %collective-permute-done.8.refs_9_.refs_2_), channel_id=1, source_target_pairs={{2,0},{6,2},{10,6},{14,10},{12,14},{8,12},{4,8},{0,4},{3,1},{7,3},... | collective-permute-start | bytes 491528 | tf_op jit(solution)/shard_map/ppermute | solution.py:341
  21.8 24.7 %collective-permute-start.18 = (f32[256,512]{1,0:T(8,128)S(1)}, f32[256,512]{1,0:T(8,128)S(1)}, u32[]{:S(2)}, u32[]{:S(2)}) collective-permute-start(f32[256,512]{1,0:T(8,128)S(1)} %get-tuple-element.26), channel_id=1, source_target_pairs={{0,1},{1,0},{2,3},{3,2},{4,5},{5,4},{6,7},{7,6},{8,9},{9,8},{10,11... | collective-permute-start | bytes 1572872 | tf_op jit(solution)/shard_map/ppermute | solution.py:351
  21.9 7.1 %collective-permute-start.2 = (bf16[64,1280]{1,0:T(8,128)(2,1)S(1)}, bf16[64,1280]{1,0:T(8,128)(2,1)S(1)}, u32[]{:S(2)}, u32[]{:S(2)}) collective-permute-start(bf16[64,1280]{1,0:T(8,128)(2,1)S(1)} %collective-permute-done.1.refs_5_), channel_id=1, source_target_pairs={{2,0},{6,2},{10,6},{14,10},{12,14},{8,12},{4,8},{0,4},{3,1},{7,3},... | collective-permute-start | bytes 491528 | tf_op jit(solution)/shard_map/ppermute | solution.py:343
  23.5 8.5 %collective-permute-start.13 = (bf16[64,1280]{1,0:T(8,128)(2,1)S(1)}, bf16[64,1280]{1,0:T(8,128)(2,1)S(1)}, u32[]{:S(2)}, u32[]{:S(2)}) collective-permute-start(bf16[64,1280]{1,0:T(8,128)(2,1)S(1)} %collective-permute-done.9.refs_7_.refs_4_), channel_id=1, source_target_pairs={{2,0},{6,2},{10,6},{14,10},{12,14},{8,12},{4,8},{0,4},{3,1},{7,3},... | collective-permute-start | bytes 491528 | tf_op jit(solution)/shard_map/ppermute | solution.py:341
  25.1 8.5 %collective-permute-start.5 = (bf16[64,1280]{1,0:T(8,128)(2,1)S(1)}, bf16[64,1280]{1,0:T(8,128)(2,1)S(1)}, u32[]{:S(2)}, u32[]{:S(2)}) collective-permute-start(bf16[64,1280]{1,0:T(8,128)(2,1)S(1)} %collective-permute-done.4.refs_6_), channel_id=1, source_target_pairs={{0,2},{2,6},{6,10},{10,14},{14,12},{12,8},{8,4},{4,0},{1,3},{3,7},... | collective-permute-start | bytes 491528 | tf_op jit(solution)/shard_map/ppermute | solution.py:340
  28.9 7.5 %collective-permute-start.12 = (bf16[64,1280]{1,0:T(8,128)(2,1)S(1)}, bf16[64,1280]{1,0:T(8,128)(2,1)S(1)}, u32[]{:S(2)}, u32[]{:S(2)}) collective-permute-start(bf16[64,1280]{1,0:T(8,128)(2,1)S(1)} %collective-permute-done.11.refs_10_.refs_3_), channel_id=1, source_target_pairs={{0,2},{2,6},{6,10},{10,14},{14,12},{12,8},{8,4},{4,0},{1,3},{3,7},... | collective-permute-start | bytes 491528 | tf_op jit(solution)/shard_map/ppermute | solution.py:342
  32.0 7.1 %collective-permute-start.6 = (bf16[64,1280]{1,0:T(8,128)(2,1)S(1)}, bf16[64,1280]{1,0:T(8,128)(2,1)S(1)}, u32[]{:S(2)}, u32[]{:S(2)}) collective-permute-start(bf16[64,1280]{1,0:T(8,128)(2,1)S(1)} %collective-permute-done.2.refs_3_), channel_id=1, source_target_pairs={{2,0},{6,2},{10,6},{14,10},{12,14},{8,12},{4,8},{0,4},{3,1},{7,3},... | collective-permute-start | bytes 491528 | tf_op jit(solution)/shard_map/ppermute | solution.py:343
  33.6 7.7 %collective-permute-start.14 = (bf16[64,1280]{1,0:T(8,128)(2,1)S(1)}, bf16[64,1280]{1,0:T(8,128)(2,1)S(1)}, u32[]{:S(2)}, u32[]{:S(2)}) collective-permute-start(bf16[64,1280]{1,0:T(8,128)(2,1)S(1)} %collective-permute-done.13.refs_9_.refs_6_), channel_id=1, source_target_pairs={{2,0},{6,2},{10,6},{14,10},{12,14},{8,12},{4,8},{0,4},{3,1},{7,3},... | collective-permute-start | bytes 491528 | tf_op jit(solution)/shard_map/ppermute | solution.py:347
  35.2 6.1 %collective-permute-start.7 = (bf16[64,1280]{1,0:T(8,128)(2,1)S(1)}, bf16[64,1280]{1,0:T(8,128)(2,1)S(1)}, u32[]{:S(2)}, u32[]{:S(2)}) collective-permute-start(bf16[64,1280]{1,0:T(8,128)(2,1)S(1)} %collective-permute-done.5.refs_4_), channel_id=1, source_target_pairs={{0,2},{2,6},{6,10},{10,14},{14,12},{12,8},{8,4},{4,0},{1,3},{3,7},... | collective-permute-start | bytes 491528 | tf_op jit(solution)/shard_map/ppermute | solution.py:346
  42.1 4.3 %collective-permute-start.16 = (f32[128,128]{1,0:T(8,128)S(1)}, f32[128,128]{1,0:T(8,128)S(1)}, u32[]{:S(2)}, u32[]{:S(2)}) collective-permute-start(f32[128,128]{1,0:T(8,128)S(1)} %get-tuple-element.24), channel_id=1, source_target_pairs={{0,16},{16,0},{1,17},{17,1},{2,18},{18,2},{3,19},{19,3},{4,20},{20... | collective-permute-start | bytes 196616 | tf_op jit(solution)/shard_map/ppermute | solution.py:364
  42.6 3.9 %collective-permute-start.15 = (f32[128,128]{1,0:T(8,128)S(1)}, f32[128,128]{1,0:T(8,128)S(1)}, u32[]{:S(2)}, u32[]{:S(2)}) collective-permute-start(f32[128,128]{1,0:T(8,128)S(1)} %get-tuple-element.23.mine), channel_id=1, source_target_pairs={{0,1},{1,0},{2,3},{3,2},{4,5},{5,4},{6,7},{7,6},{8,9},{9,8},{10,11... | collective-permute-start | bytes 196616 | tf_op jit(solution)/shard_map/ppermute | solution.py:365
  46.5 1.3 %collective-permute-start.17 = (f32[128,128]{1,0:T(8,128)S(1)}, f32[128,128]{1,0:T(8,128)S(1)}, u32[]{:S(2)}, u32[]{:S(2)}) collective-permute-start(f32[128,128]{1,0:T(8,128)S(1)} %collective-permute-done.16.two), channel_id=1, source_target_pairs={{0,1},{1,0},{2,3},{3,2},{4,5},{5,4},{6,7},{7,6},{8,9},{9,8},{10,11... | collective-permute-start | bytes 196616 | tf_op jit(solution)/shard_map/ppermute | solution.py:366

commit v4 on v3

--- a/solution.py
+++ b/solution.py
@@ -9,6 +9,8 @@
 
 F32, BF16, I32 = jnp.float32, jnp.bfloat16, jnp.int32
 VMEM_LIMIT = 40 * 1024 * 1024
+HALF = pl.CostEstimate(flops=0, bytes_accessed=1 << 22, transcendentals=0)
+LONG = pl.CostEstimate(flops=1 << 33, bytes_accessed=1 << 24, transcendentals=0)
 GROUP = 4
 VMEM = pl.BlockSpec(memory_space=pltpu.VMEM)
 HBM = pl.BlockSpec(memory_space=pltpu.HBM)
@@ -153,57 +155,61 @@
     )(*map(in_hbm, (hidden, factor, factor_out, demand, lengths, holder_slot, slots)))
 
 
-def base_kernel(hidden_ref, weight_ref, near_ref, far_ref, rows_ref, buffer, sems):
-    width = near_ref.shape[1]
+def base_kernel(side, fetch_rows, rows_in_ref, weight_ref, out_ref, *rest):
+    rows_ref = rest[0] if fetch_rows else rows_in_ref
+    buffer, sems = rest[-2:]
+    width = out_ref.shape[1]
     core = lax.axis_index("tensor")
-    here = pl.multiple_of(core * width, 128)
-    there = pl.multiple_of((1 - core) * width, 128)
+    offset = pl.multiple_of((core if side == 0 else 1 - core) * width, 128)
     steps, step = buffer.shape[:2]
     copies = []
     for k in range(steps):
         span = pl.ds(k * step, step)
-        copies.append(
-            (
-                pltpu.make_async_copy(hidden_ref.at[:, span], rows_ref.at[:, span], sems.at[0, k]),
-                pltpu.make_async_copy(weight_ref.at[span], buffer.at[k], sems.at[1, k]),
+        need = [
+            pltpu.make_async_copy(
+                weight_ref.at[span, pl.ds(offset, width)], buffer.at[k], sems.at[0, k]
             )
-        )
-    for pair in copies:
-        for copy in pair:
+        ]
+        if fetch_rows:
+            need.append(
+                pltpu.make_async_copy(
+                    rows_in_ref.at[:, span], rows_ref.at[:, span], sems.at[1, k]
+                )
+            )
+        copies.append(need)
+    for need in copies:
+        for copy in need:
             copy.start()
-    for k, pair in enumerate(copies):
-        for copy in pair:
+    for k, need in enumerate(copies):
+        for copy in need:
             copy.wait()
         rows = rows_ref[:, k * step : (k + 1) * step]
-        for out_ref, offset in ((far_ref, there), (near_ref, here)):
-            part = jnp.dot(rows, buffer[k, :, pl.ds(offset, width)], preferred_element_type=F32)
-            if k == 0:
-                out_ref[...] = part
-            else:
-                out_ref[...] += part
-
-
-def base_call(hidden, weight):
-    rows, depth = hidden.shape
+        part = jnp.dot(rows, buffer[k], preferred_element_type=F32)
+        if k == 0:
+            out_ref[...] = part
+        else:
+            out_ref[...] += part
+
+
+def base_call(side, fetch_rows, rows, weight):
+    count, depth = rows.shape
     width = weight.shape[1] // 2
-    steps = 8
-    out = jax.ShapeDtypeStruct((rows, width), F32)
+    steps = 4
+    out = (jax.ShapeDtypeStruct((count, width), F32),)
+    if fetch_rows:
+        out += (jax.ShapeDtypeStruct(rows.shape, rows.dtype),)
     return pl.pallas_call(
-        base_kernel,
-        out_shape=(out, out, jax.ShapeDtypeStruct(hidden.shape, hidden.dtype)),
-        in_specs=[HBM, HBM],
-        out_specs=(VMEM,) * 3,
+        functools.partial(base_kernel, side, fetch_rows),
+        out_shape=out,
+        in_specs=[HBM if fetch_rows else VMEM, HBM],
+        out_specs=(VMEM,) * len(out),
         scratch_shapes=[
-            pltpu.VMEM((steps, depth // steps, 2 * width), weight.dtype),
+            pltpu.VMEM((steps, depth // steps, width), weight.dtype),
             pltpu.SemaphoreType.DMA((2, steps)),
         ],
         compiler_params=params(),
-        cost_estimate=pl.CostEstimate(
-            flops=4 * rows * depth * width,
-            bytes_accessed=2 * depth * (rows + 2 * width) + 8 * rows * width,
-            transcendentals=0,
-        ),
-    )(in_hbm(hidden), in_hbm(weight))
+        cost_estimate=HALF,
+    )(in_hbm(rows) if fetch_rows else rows, in_hbm(weight))
 
 
 def group_mask(low, high, shape):
@@ -273,11 +279,7 @@
         in_specs=[VMEM] * len(operands),
         out_specs=(VMEM, VMEM),
         compiler_params=params(),
-        cost_estimate=pl.CostEstimate(
-            flops=4 * rows * depth * rank * GROUP * len(groups),
-            bytes_accessed=2 * depth * (2 * rows + rank * GROUP * len(groups)),
-            transcendentals=0,
-        ),
+        cost_estimate=LONG,
     )(*operands)
 
 
@@ -334,21 +336,24 @@
         jnp.asarray(table, I32),
     )
 
+    far, held = base_call(1, True, hidden, value_weight)
     firsts, seconds = [first], [second]
     ahead, behind = (first, second), (first, second)
     for step in range(1, full + 1):
         a = lax.ppermute(ahead[0], "batch", forward)
-        b = lax.ppermute(behind[1], "batch", backward)
-        ahead = (a, lax.ppermute(ahead[1], "batch", forward))
-        behind = (lax.ppermute(behind[0], "batch", backward), b)
-        firsts += [ahead[0], behind[0]]
-        seconds += [ahead[1], behind[1]]
+        d = lax.ppermute(behind[1], "batch", backward)
+        b = lax.ppermute(ahead[1], "batch", forward)
+        c = lax.ppermute(behind[0], "batch", backward)
+        if step == 1:
+            a, far = lax.optimization_barrier((a, far))
+        ahead, behind = (a, b), (c, d)
+        firsts += [a, c]
+        seconds += [b, d]
     firsts.append(lax.ppermute(ahead[0], "batch", forward))
     seconds.append(lax.ppermute(behind[1], "batch", backward))
     other = lax.ppermute(to_other, "groups", swap)
-
-    near, far, held = base_call(hidden, value_weight)
-    far = lax.ppermute(far, "tensor", swap)
+    (near,) = base_call(0, False, held, value_weight)
+    held, near = lax.optimization_barrier((held, near))
 
     count = owners // GROUP
     early = range(count - 1)
@@ -358,6 +363,8 @@
         pieces += seconds[group * GROUP : (group + 1) * GROUP]
     sides = (held, other, bounds)
     starts = rank_call(tuple(early), depth, *sides, pieces, None)
+    *starts, far = lax.optimization_barrier((*starts, far))
+    far = lax.ppermute(far, "tensor", swap)
     pieces = firsts[-GROUP:] + seconds[-GROUP:]
     mine, theirs = rank_call((count - 1,), depth, *sides, pieces, starts)
 

time: 49 us -> 41.5 us (0.85)
  waiting for transfers between devices: 20 us -> 12.9 us
  starting transfers between devices: 19.9 us -> 18.1 us
  Pallas kernels: 8.84 us -> 10.2 us
    ppermute x9, waiting for transfers between devices: 10.7 us -> 6.13 us  [the longest x3 4.36 us: per_device(): d = lax.ppermute(behind[1], 'batch', backward)]
    ppermute x9, starting transfers between devices: 10.8 us -> 7.72 us  [the longest x3 4.7 us: per_device(): b = lax.ppermute(ahead[1], 'batch', forward)]
    ppermute x3, waiting for transfers between devices: 2.02 us -> 0.01 us  [per_device(): a = lax.ppermute(ahead[0], 'batch', forward)]
    pallas_call x1 -> x2, Pallas kernels: 4.61 us -> 5.97 us  [base_call(): pl.pallas_call(functools.partial(base_kernel, side, fetch_rows), out_shap...]
    ppermute x1, starting transfers between devices: 0.45 us -> 1.7 us  [per_device(): firsts.append(lax.ppermute(ahead[0], 'batch', forward))]
    ppermute x1, starting transfers between devices: 1.58 us -> 0.53 us  [per_device(): seconds.append(lax.ppermute(behind[1], 'batch', backward))]
    ppermute x3, starting transfers between devices: 3.52 us -> 4.48 us  [per_device(): a = lax.ppermute(ahead[0], 'batch', forward)]
  transfers between devices with their start and end apart: 19 -> 19, of which waited for: 8 -> 7; matrix products, arithmetic and copies ran while one was open for 0% -> 0% of each run, Pallas kernels for 13% -> 18%
where the time goes in v4:
time: 41.5 us; the launch traced here: 41.3 us
  starting transfers between devices  18.1 us (44%)
  waiting for transfers between devices  12.9 us (31%)
  Pallas kernels  10.2 us (25%)
    pallas_call x2, Pallas kernels, base_call(): pl.pallas_call(functools.partial(base_kernel, side, fetch_rows), out_shap...  5.97 us
    ppermute x3, starting transfers between devices, per_device(): b = lax.ppermute(ahead[1], 'batch', forward)  4.7 us
    ppermute x3, starting transfers between devices, per_device(): a = lax.ppermute(ahead[0], 'batch', forward)  4.48 us
    ppermute x3, waiting for transfers between devices, per_device(): d = lax.ppermute(behind[1], 'batch', backward)  4.36 us
    ppermute x1, waiting for transfers between devices, per_device(): two = lax.ppermute(theirs, 'groups', swap)  3.76 us
    ppermute x1, starting transfers between devices, per_device(): other = lax.ppermute(to_other, 'groups', swap)  3.03 us
    ppermute x1, waiting for transfers between devices, per_device(): seconds.append(lax.ppermute(behind[1], 'batch', backward))  1.76 us
    ppermute x1, starting transfers between devices, per_device(): firsts.append(lax.ppermute(ahead[0], 'batch', forward))  1.7 us
  transfers between devices with their start and end apart: 19, of which 7 were waited for; matrix products, arithmetic and copies ran while one was open for 0% of the time, Pallas kernels for 18%

profile of v4, /device:TPU:0, one launch (start us, length us, event | category | flops | bytes accessed | tf_op | source)
XLA Modules:
  0.0 41.3 jit_solution(18087541004507596183)
XLA Ops:
  0.0 1.5 %shard_map.82 = (bf16[272,2048]{1,0:T(8,128)(2,1)S(1)}, bf16[64,1280]{1,0:T(8,128)(2,1)S(1)}, bf16[64,1280]{1,0:T(8,128)(2,1)S(1)}, s32[8,512]{1,0:T(8,128)S(1)}) custom-call(bf16[256,4096]{1,0:T(8,128)(2,1)} %rows_in_ref.1, bf16[64,4096]{1,0:T(8,128)(2,1)} %bitcast.4, bf16[64,512]{1,0:T(8,128)(2,1)} %bitcast.5, s32[1,4]{1,0:T(1,128)} %demand_ref.1, ...), custom_call_target="tpu_custom_call" | custom-call | tf_op jit(solution)/shard_map/pallas_call | solution.py:137
  1.5 3.0 %collective-permute-start = (bf16[272,2048]{1,0:T(8,128)(2,1)S(1)}, bf16[272,2048]{1,0:T(8,128)(2,1)S(1)}, u32[]{:S(2)}, u32[]{:S(2)}) collective-permute-start(bf16[272,2048]{1,0:T(8,128)(2,1)S(1)} %get-tuple-element.25), channel_id=1, source_target_pairs={{0,16},{16,0},{1,17},{17,1},{2,18},{18,2},{3,19},{19,3},{4,20},{20... | collective-permute-start | bytes 3342344 | tf_op jit(solution)/shard_map/ppermute | solution.py:354
  4.5 1.5 %collective-permute-start.3 = (bf16[64,1280]{1,0:T(8,128)(2,1)S(1)}, bf16[64,1280]{1,0:T(8,128)(2,1)S(1)}, u32[]{:S(2)}, u32[]{:S(2)}) collective-permute-start(bf16[64,1280]{1,0:T(8,128)(2,1)S(1)} %get-tuple-element.26.refs_3_), channel_id=1, source_target_pairs={{0,2},{2,6},{6,10},{10,14},{14,12},{12,8},{8,4},{4,0},{1,3},{3,7},... | collective-permute-start | bytes 491528 | tf_op jit(solution)/shard_map/ppermute | solution.py:343
  6.0 0.5 %collective-permute-start.8 = (bf16[64,1280]{1,0:T(8,128)(2,1)S(1)}, bf16[64,1280]{1,0:T(8,128)(2,1)S(1)}, u32[]{:S(2)}, u32[]{:S(2)}) collective-permute-start(bf16[64,1280]{1,0:T(8,128)(2,1)S(1)} %get-tuple-element.29.refs_7_.refs_0_), channel_id=1, source_target_pairs={{2,0},{6,2},{10,6},{14,10},{12,14},{8,12},{4,8},{0,4},{3,1},{7,3},... | collective-permute-start | bytes 491528 | tf_op jit(solution)/shard_map/ppermute | solution.py:344
  6.5 1.5 %collective-permute-start.10 = (bf16[64,1280]{1,0:T(8,128)(2,1)S(1)}, bf16[64,1280]{1,0:T(8,128)(2,1)S(1)}, u32[]{:S(2)}, u32[]{:S(2)}) collective-permute-start(bf16[64,1280]{1,0:T(8,128)(2,1)S(1)} %get-tuple-element.29.refs_7_.refs_0_), channel_id=1, source_target_pairs={{0,2},{2,6},{6,10},{10,14},{14,12},{12,8},{8,4},{4,0},{1,3},{3,7},... | collective-permute-start | bytes 491528 | tf_op jit(solution)/shard_map/ppermute | solution.py:345
  8.0 0.5 %collective-permute-start.1 = (bf16[64,1280]{1,0:T(8,128)(2,1)S(1)}, bf16[64,1280]{1,0:T(8,128)(2,1)S(1)}, u32[]{:S(2)}, u32[]{:S(2)}) collective-permute-start(bf16[64,1280]{1,0:T(8,128)(2,1)S(1)} %get-tuple-element.26.refs_3_), channel_id=1, source_target_pairs={{2,0},{6,2},{10,6},{14,10},{12,14},{8,12},{4,8},{0,4},{3,1},{7,3},... | collective-permute-start | bytes 491528 | tf_op jit(solution)/shard_map/ppermute | solution.py:346
  8.6 3.3 %shard_map.83 = (f32[256,512]{1,0:T(8,128)S(1)}, bf16[256,4096]{1,0:T(8,128)(2,1)S(1)}) custom-call(bf16[256,4096]{1,0:T(8,128)(2,1)} %rows_in_ref.1, bf16[4096,1024]{1,0:T(8,128)(2,1)} %weight_ref.3), custom_call_target="tpu_custom_call" | custom-call | bytes 4194304 | tf_op jit(solution)/shard_map/pallas_call | solution.py:201
  11.9 0.0 collective-permute-done.3.refs_4_
  11.9 1.3 %collective-permute-done.8.refs_9_.refs_2_ = bf16[64,1280]{1,0:T(8,128)(2,1)S(1)} collective-permute-done((bf16[64,1280]{1,0:T(8,128)(2,1)S(1)}, bf16[64,1280]{1,0:T(8,128)(2,1)S(1)}, u32[]{:S(2)}, u32[]{:S(2)}) %collective-permute-start.8) | collective-permute-done | bytes 163872 | tf_op jit(solution)/shard_map/ppermute | solution.py:344
  13.1 0.5 %collective-permute-start.9 = (bf16[64,1280]{1,0:T(8,128)(2,1)S(1)}, bf16[64,1280]{1,0:T(8,128)(2,1)S(1)}, u32[]{:S(2)}, u32[]{:S(2)}) collective-permute-start(bf16[64,1280]{1,0:T(8,128)(2,1)S(1)} %collective-permute-done.8.refs_9_.refs_2_), channel_id=1, source_target_pairs={{2,0},{6,2},{10,6},{14,10},{12,14},{8,12},{4,8},{0,4},{3,1},{7,3},... | collective-permute-start | bytes 491528 | tf_op jit(solution)/shard_map/ppermute | solution.py:344
  13.7 1.5 %collective-permute-start.4 = (bf16[64,1280]{1,0:T(8,128)(2,1)S(1)}, bf16[64,1280]{1,0:T(8,128)(2,1)S(1)}, u32[]{:S(2)}, u32[]{:S(2)}) collective-permute-start(bf16[64,1280]{1,0:T(8,128)(2,1)S(1)} %collective-permute-done.3.refs_4_), channel_id=1, source_target_pairs={{0,2},{2,6},{6,10},{10,14},{14,12},{12,8},{8,4},{4,0},{1,3},{3,7},... | collective-permute-start | bytes 491528 | tf_op jit(solution)/shard_map/ppermute | solution.py:343
  15.2 0.0 collective-permute-done.10.refs_8_.refs_1_
  15.2 1.6 %collective-permute-start.11 = (bf16[64,1280]{1,0:T(8,128)(2,1)S(1)}, bf16[64,1280]{1,0:T(8,128)(2,1)S(1)}, u32[]{:S(2)}, u32[]{:S(2)}) collective-permute-start(bf16[64,1280]{1,0:T(8,128)(2,1)S(1)} %collective-permute-done.10.refs_8_.refs_1_), channel_id=1, source_target_pairs={{0,2},{2,6},{6,10},{10,14},{14,12},{12,8},{8,4},{4,0},{1,3},{3,7},... | collective-permute-start | bytes 491528 | tf_op jit(solution)/shard_map/ppermute | solution.py:345
  16.8 0.0 collective-permute-done.1.refs_5_
  16.8 0.5 %collective-permute-start.2 = (bf16[64,1280]{1,0:T(8,128)(2,1)S(1)}, bf16[64,1280]{1,0:T(8,128)(2,1)S(1)}, u32[]{:S(2)}, u32[]{:S(2)}) collective-permute-start(bf16[64,1280]{1,0:T(8,128)(2,1)S(1)} %collective-permute-done.1.refs_5_), channel_id=1, source_target_pairs={{2,0},{6,2},{10,6},{14,10},{12,14},{8,12},{4,8},{0,4},{3,1},{7,3},... | collective-permute-start | bytes 491528 | tf_op jit(solution)/shard_map/ppermute | solution.py:346
  17.2 3.1 %collective-permute-done.9.refs_7_.refs_4_ = bf16[64,1280]{1,0:T(8,128)(2,1)S(1)} collective-permute-done((bf16[64,1280]{1,0:T(8,128)(2,1)S(1)}, bf16[64,1280]{1,0:T(8,128)(2,1)S(1)}, u32[]{:S(2)}, u32[]{:S(2)}) %collective-permute-start.9) | collective-permute-done | bytes 163872 | tf_op jit(solution)/shard_map/ppermute | solution.py:344
  20.3 0.5 %collective-permute-start.13 = (bf16[64,1280]{1,0:T(8,128)(2,1)S(1)}, bf16[64,1280]{1,0:T(8,128)(2,1)S(1)}, u32[]{:S(2)}, u32[]{:S(2)}) collective-permute-start(bf16[64,1280]{1,0:T(8,128)(2,1)S(1)} %collective-permute-done.9.refs_7_.refs_4_), channel_id=1, source_target_pairs={{2,0},{6,2},{10,6},{14,10},{12,14},{8,12},{4,8},{0,4},{3,1},{7,3},... | collective-permute-start | bytes 491528 | tf_op jit(solution)/shard_map/ppermute | solution.py:344
  20.8 0.0 collective-permute-done.4.refs_6_
  20.8 1.5 %collective-permute-start.5 = (bf16[64,1280]{1,0:T(8,128)(2,1)S(1)}, bf16[64,1280]{1,0:T(8,128)(2,1)S(1)}, u32[]{:S(2)}, u32[]{:S(2)}) collective-permute-start(bf16[64,1280]{1,0:T(8,128)(2,1)S(1)} %collective-permute-done.4.refs_6_), channel_id=1, source_target_pairs={{0,2},{2,6},{6,10},{10,14},{14,12},{12,8},{8,4},{4,0},{1,3},{3,7},... | collective-permute-start | bytes 491528 | tf_op jit(solution)/shard_map/ppermute | solution.py:343
  22.3 2.7 %shard_map.84.near_ref = f32[256,512]{1,0:T(8,128)S(1)} custom-call(bf16[256,4096]{1,0:T(8,128)(2,1)S(1)} %get-tuple-element.24.rows_in_ref.refs_0_, bf16[4096,1024]{1,0:T(8,128)(2,1)} %weight_ref.3), custom_call_target="tpu_custom_call" | custom-call | bytes 4194304 | tf_op jit(solution)/shard_map/pallas_call | solution.py:201
  25.0 0.0 collective-permute-done.11.refs_10_.refs_3_
  25.0 1.6 %collective-permute-start.12 = (bf16[64,1280]{1,0:T(8,128)(2,1)S(1)}, bf16[64,1280]{1,0:T(8,128)(2,1)S(1)}, u32[]{:S(2)}, u32[]{:S(2)}) collective-permute-start(bf16[64,1280]{1,0:T(8,128)(2,1)S(1)} %collective-permute-done.11.refs_10_.refs_3_), channel_id=1, source_target_pairs={{0,2},{2,6},{6,10},{10,14},{14,12},{12,8},{8,4},{4,0},{1,3},{3,7},... | collective-permute-start | bytes 491528 | tf_op jit(solution)/shard_map/ppermute | solution.py:345
  26.7 0.0 collective-permute-done.2.refs_3_
  26.7 0.5 %collective-permute-start.6 = (bf16[64,1280]{1,0:T(8,128)(2,1)S(1)}, bf16[64,1280]{1,0:T(8,128)(2,1)S(1)}, u32[]{:S(2)}, u32[]{:S(2)}) collective-permute-start(bf16[64,1280]{1,0:T(8,128)(2,1)S(1)} %collective-permute-done.2.refs_3_), channel_id=1, source_target_pairs={{2,0},{6,2},{10,6},{14,10},{12,14},{8,12},{4,8},{0,4},{3,1},{7,3},... | collective-permute-start | bytes 491528 | tf_op jit(solution)/shard_map/ppermute | solution.py:346
  27.1 0.0 collective-permute-done.13.refs_9_.refs_6_
  27.1 0.5 %collective-permute-start.14 = (bf16[64,1280]{1,0:T(8,128)(2,1)S(1)}, bf16[64,1280]{1,0:T(8,128)(2,1)S(1)}, u32[]{:S(2)}, u32[]{:S(2)}) collective-permute-start(bf16[64,1280]{1,0:T(8,128)(2,1)S(1)} %collective-permute-done.13.refs_9_.refs_6_), channel_id=1, source_target_pairs={{2,0},{6,2},{10,6},{14,10},{12,14},{8,12},{4,8},{0,4},{3,1},{7,3},... | collective-permute-start | bytes 491528 | tf_op jit(solution)/shard_map/ppermute | solution.py:353
  27.6 0.0 collective-permute-done.5.refs_4_
  27.6 1.7 %collective-permute-start.7 = (bf16[64,1280]{1,0:T(8,128)(2,1)S(1)}, bf16[64,1280]{1,0:T(8,128)(2,1)S(1)}, u32[]{:S(2)}, u32[]{:S(2)}) collective-permute-start(bf16[64,1280]{1,0:T(8,128)(2,1)S(1)} %collective-permute-done.5.refs_4_), channel_id=1, source_target_pairs={{0,2},{2,6},{6,10},{10,14},{14,12},{12,8},{8,4},{4,0},{1,3},{3,7},... | collective-permute-start | bytes 491528 | tf_op jit(solution)/shard_map/ppermute | solution.py:352
  29.3 0.0 collective-permute-done.refs_1_
  29.3 0.8 %shard_map.85 = (f32[256,128]{1,0:T(8,128)S(1)}, f32[256,128]{1,0:T(8,128)S(1)}) custom-call(bf16[256,4096]{1,0:T(8,128)(2,1)S(1)} %get-tuple-element.24.rows_in_ref.refs_0_, bf16[272,2048]{1,0:T(8,128)(2,1)S(1)} %collective-permute-done.refs_1_, s32[8,512]{1,0:T(8,128)S(1)} %get-tuple-element.22.refs_2_.bounds_ref, ...), custom_call_target="tpu_custom_call" | custom-call | flops 8589934592 | bytes 16777216 | tf_op jit(solution)/shard_map/pallas_call | solution.py:276
  30.1 0.1 collective-permute-start.18
  30.2 0.4 collective-permute-done.12.refs_8_.refs_5_
  30.6 1.4 %collective-permute-done.6.refs_5_ = bf16[64,1280]{1,0:T(8,128)(2,1)S(1)} collective-permute-done((bf16[64,1280]{1,0:T(8,128)(2,1)S(1)}, bf16[64,1280]{1,0:T(8,128)(2,1)S(1)}, u32[]{:S(2)}, u32[]{:S(2)}) %collective-permute-start.6) | collective-permute-done | bytes 163872 | tf_op jit(solution)/shard_map/ppermute | solution.py:346
  32.0 1.8 %collective-permute-done.14.refs_10_.refs_7_ = bf16[64,1280]{1,0:T(8,128)(2,1)S(1)} collective-permute-done((bf16[64,1280]{1,0:T(8,128)(2,1)S(1)}, bf16[64,1280]{1,0:T(8,128)(2,1)S(1)}, u32[]{:S(2)}, u32[]{:S(2)}) %collective-permute-start.14) | collective-permute-done | bytes 163872 | tf_op jit(solution)/shard_map/ppermute | solution.py:353
  33.7 0.0 collective-permute-done.7.refs_6_
  33.7 0.9 %shard_map.86 = (f32[128,128]{1,0:T(8,128)S(1)}, f32[128,128]{1,0:T(8,128)S(1)}) custom-call(bf16[256,4096]{1,0:T(8,128)(2,1)S(1)} %get-tuple-element.24.rows_in_ref.refs_0_, bf16[272,2048]{1,0:T(8,128)(2,1)S(1)} %collective-permute-done.refs_1_, s32[8,512]{1,0:T(8,128)S(1)} %get-tuple-element.22.refs_2_.bounds_ref, ...), custom_call_target="tpu_custom_call" | custom-call | flops 8589934592 | bytes 16777216 | tf_op jit(solution)/shard_map/pallas_call | solution.py:276
  34.6 0.6 %collective-permute-start.16 = (f32[128,128]{1,0:T(8,128)S(1)}, f32[128,128]{1,0:T(8,128)S(1)}, u32[]{:S(2)}, u32[]{:S(2)}) collective-permute-start(f32[128,128]{1,0:T(8,128)S(1)} %get-tuple-element.36), channel_id=1, source_target_pairs={{0,16},{16,0},{1,17},{17,1},{2,18},{18,2},{3,19},{19,3},{4,20},{20... | collective-permute-start | bytes 196616 | tf_op jit(solution)/shard_map/ppermute | solution.py:371
  35.2 0.0 collective-permute-start.15
  35.2 3.8 %collective-permute-done.16.two = f32[128,128]{1,0:T(8,128)S(1)} collective-permute-done((f32[128,128]{1,0:T(8,128)S(1)}, f32[128,128]{1,0:T(8,128)S(1)}, u32[]{:S(2)}, u32[]{:S(2)}) %collective-permute-start.16) | collective-permute-done | bytes 65568 | tf_op jit(solution)/shard_map/ppermute | solution.py:371
  39.0 0.0 collective-permute-start.17
  39.0 0.0 collective-permute-done.15.one
  39.0 1.2 %collective-permute-done.17.three = f32[128,128]{1,0:T(8,128)S(1)} collective-permute-done((f32[128,128]{1,0:T(8,128)S(1)}, f32[128,128]{1,0:T(8,128)S(1)}, u32[]{:S(2)}, u32[]{:S(2)}) %collective-permute-start.17) | collective-permute-done | bytes 65568 | tf_op jit(solution)/shard_map/ppermute | solution.py:373
  40.2 0.0 collective-permute-done.18.far_ref
  40.2 1.1 %shard_map.87 = bf16[256,512]{1,0:T(8,128)(2,1)} custom-call(s32[8,512]{1,0:T(8,128)S(1)} %get-tuple-element.22.refs_2_.bounds_ref, f32[128,128]{1,0:T(8,128)S(1)} %get-tuple-element.35.mine, f32[128,128]{1,0:T(8,128)S(1)} %collective-permute-done.15.one, f32[128,128]{1,0:T(8,128)S(1)} %collective-permute-done.16.two, ...), custom_call_target="tpu_custom_call" | custom-call | tf_op jit(solution)/shard_map/pallas_call | solution.py:376
Async XLA Ops:
  1.5 27.9 %collective-permute-start = (bf16[272,2048]{1,0:T(8,128)(2,1)S(1)}, bf16[272,2048]{1,0:T(8,128)(2,1)S(1)}, u32[]{:S(2)}, u32[]{:S(2)}) collective-permute-start(bf16[272,2048]{1,0:T(8,128)(2,1)S(1)} %get-tuple-element.25), channel_id=1, source_target_pairs={{0,16},{16,0},{1,17},{17,1},{2,18},{18,2},{3,19},{19,3},{4,20},{20... | collective-permute-start | bytes 3342344 | tf_op jit(solution)/shard_map/ppermute | solution.py:354
  4.5 7.3 %collective-permute-start.3 = (bf16[64,1280]{1,0:T(8,128)(2,1)S(1)}, bf16[64,1280]{1,0:T(8,128)(2,1)S(1)}, u32[]{:S(2)}, u32[]{:S(2)}) collective-permute-start(bf16[64,1280]{1,0:T(8,128)(2,1)S(1)} %get-tuple-element.26.refs_3_), channel_id=1, source_target_pairs={{0,2},{2,6},{6,10},{10,14},{14,12},{12,8},{8,4},{4,0},{1,3},{3,7},... | collective-permute-start | bytes 491528 | tf_op jit(solution)/shard_map/ppermute | solution.py:343
  6.0 7.1 %collective-permute-start.8 = (bf16[64,1280]{1,0:T(8,128)(2,1)S(1)}, bf16[64,1280]{1,0:T(8,128)(2,1)S(1)}, u32[]{:S(2)}, u32[]{:S(2)}) collective-permute-start(bf16[64,1280]{1,0:T(8,128)(2,1)S(1)} %get-tuple-element.29.refs_7_.refs_0_), channel_id=1, source_target_pairs={{2,0},{6,2},{10,6},{14,10},{12,14},{8,12},{4,8},{0,4},{3,1},{7,3},... | collective-permute-start | bytes 491528 | tf_op jit(solution)/shard_map/ppermute | solution.py:344
  6.5 8.6 %collective-permute-start.10 = (bf16[64,1280]{1,0:T(8,128)(2,1)S(1)}, bf16[64,1280]{1,0:T(8,128)(2,1)S(1)}, u32[]{:S(2)}, u32[]{:S(2)}) collective-permute-start(bf16[64,1280]{1,0:T(8,128)(2,1)S(1)} %get-tuple-element.29.refs_7_.refs_0_), channel_id=1, source_target_pairs={{0,2},{2,6},{6,10},{10,14},{14,12},{12,8},{8,4},{4,0},{1,3},{3,7},... | collective-permute-start | bytes 491528 | tf_op jit(solution)/shard_map/ppermute | solution.py:345
  8.0 8.7 %collective-permute-start.1 = (bf16[64,1280]{1,0:T(8,128)(2,1)S(1)}, bf16[64,1280]{1,0:T(8,128)(2,1)S(1)}, u32[]{:S(2)}, u32[]{:S(2)}) collective-permute-start(bf16[64,1280]{1,0:T(8,128)(2,1)S(1)} %get-tuple-element.26.refs_3_), channel_id=1, source_target_pairs={{2,0},{6,2},{10,6},{14,10},{12,14},{8,12},{4,8},{0,4},{3,1},{7,3},... | collective-permute-start | bytes 491528 | tf_op jit(solution)/shard_map/ppermute | solution.py:346
  13.1 7.1 %collective-permute-start.9 = (bf16[64,1280]{1,0:T(8,128)(2,1)S(1)}, bf16[64,1280]{1,0:T(8,128)(2,1)S(1)}, u32[]{:S(2)}, u32[]{:S(2)}) collective-permute-start(bf16[64,1280]{1,0:T(8,128)(2,1)S(1)} %collective-permute-done.8.refs_9_.refs_2_), channel_id=1, source_target_pairs={{2,0},{6,2},{10,6},{14,10},{12,14},{8,12},{4,8},{0,4},{3,1},{7,3},... | collective-permute-start | bytes 491528 | tf_op jit(solution)/shard_map/ppermute | solution.py:344
  13.7 7.1 %collective-permute-start.4 = (bf16[64,1280]{1,0:T(8,128)(2,1)S(1)}, bf16[64,1280]{1,0:T(8,128)(2,1)S(1)}, u32[]{:S(2)}, u32[]{:S(2)}) collective-permute-start(bf16[64,1280]{1,0:T(8,128)(2,1)S(1)} %collective-permute-done.3.refs_4_), channel_id=1, source_target_pairs={{0,2},{2,6},{6,10},{10,14},{14,12},{12,8},{8,4},{4,0},{1,3},{3,7},... | collective-permute-start | bytes 491528 | tf_op jit(solution)/shard_map/ppermute | solution.py:343
  15.2 9.8 %collective-permute-start.11 = (bf16[64,1280]{1,0:T(8,128)(2,1)S(1)}, bf16[64,1280]{1,0:T(8,128)(2,1)S(1)}, u32[]{:S(2)}, u32[]{:S(2)}) collective-permute-start(bf16[64,1280]{1,0:T(8,128)(2,1)S(1)} %collective-permute-done.10.refs_8_.refs_1_), channel_id=1, source_target_pairs={{0,2},{2,6},{6,10},{10,14},{14,12},{12,8},{8,4},{4,0},{1,3},{3,7},... | collective-permute-start | bytes 491528 | tf_op jit(solution)/shard_map/ppermute | solution.py:345
  16.8 9.9 %collective-permute-start.2 = (bf16[64,1280]{1,0:T(8,128)(2,1)S(1)}, bf16[64,1280]{1,0:T(8,128)(2,1)S(1)}, u32[]{:S(2)}, u32[]{:S(2)}) collective-permute-start(bf16[64,1280]{1,0:T(8,128)(2,1)S(1)} %collective-permute-done.1.refs_5_), channel_id=1, source_target_pairs={{2,0},{6,2},{10,6},{14,10},{12,14},{8,12},{4,8},{0,4},{3,1},{7,3},... | collective-permute-start | bytes 491528 | tf_op jit(solution)/shard_map/ppermute | solution.py:346
  20.3 6.8 %collective-permute-start.13 = (bf16[64,1280]{1,0:T(8,128)(2,1)S(1)}, bf16[64,1280]{1,0:T(8,128)(2,1)S(1)}, u32[]{:S(2)}, u32[]{:S(2)}) collective-permute-start(bf16[64,1280]{1,0:T(8,128)(2,1)S(1)} %collective-permute-done.9.refs_7_.refs_4_), channel_id=1, source_target_pairs={{2,0},{6,2},{10,6},{14,10},{12,14},{8,12},{4,8},{0,4},{3,1},{7,3},... | collective-permute-start | bytes 491528 | tf_op jit(solution)/shard_map/ppermute | solution.py:344
  20.8 6.8 %collective-permute-start.5 = (bf16[64,1280]{1,0:T(8,128)(2,1)S(1)}, bf16[64,1280]{1,0:T(8,128)(2,1)S(1)}, u32[]{:S(2)}, u32[]{:S(2)}) collective-permute-start(bf16[64,1280]{1,0:T(8,128)(2,1)S(1)} %collective-permute-done.4.refs_6_), channel_id=1, source_target_pairs={{0,2},{2,6},{6,10},{10,14},{14,12},{12,8},{8,4},{4,0},{1,3},{3,7},... | collective-permute-start | bytes 491528 | tf_op jit(solution)/shard_map/ppermute | solution.py:343
  25.0 5.6 %collective-permute-start.12 = (bf16[64,1280]{1,0:T(8,128)(2,1)S(1)}, bf16[64,1280]{1,0:T(8,128)(2,1)S(1)}, u32[]{:S(2)}, u32[]{:S(2)}) collective-permute-start(bf16[64,1280]{1,0:T(8,128)(2,1)S(1)} %collective-permute-done.11.refs_10_.refs_3_), channel_id=1, source_target_pairs={{0,2},{2,6},{6,10},{10,14},{14,12},{12,8},{8,4},{4,0},{1,3},{3,7},... | collective-permute-start | bytes 491528 | tf_op jit(solution)/shard_map/ppermute | solution.py:345
  26.7 5.3 %collective-permute-start.6 = (bf16[64,1280]{1,0:T(8,128)(2,1)S(1)}, bf16[64,1280]{1,0:T(8,128)(2,1)S(1)}, u32[]{:S(2)}, u32[]{:S(2)}) collective-permute-start(bf16[64,1280]{1,0:T(8,128)(2,1)S(1)} %collective-permute-done.2.refs_3_), channel_id=1, source_target_pairs={{2,0},{6,2},{10,6},{14,10},{12,14},{8,12},{4,8},{0,4},{3,1},{7,3},... | collective-permute-start | bytes 491528 | tf_op jit(solution)/shard_map/ppermute | solution.py:346
  27.1 6.6 %collective-permute-start.14 = (bf16[64,1280]{1,0:T(8,128)(2,1)S(1)}, bf16[64,1280]{1,0:T(8,128)(2,1)S(1)}, u32[]{:S(2)}, u32[]{:S(2)}) collective-permute-start(bf16[64,1280]{1,0:T(8,128)(2,1)S(1)} %collective-permute-done.13.refs_9_.refs_6_), channel_id=1, source_target_pairs={{2,0},{6,2},{10,6},{14,10},{12,14},{8,12},{4,8},{0,4},{3,1},{7,3},... | collective-permute-start | bytes 491528 | tf_op jit(solution)/shard_map/ppermute | solution.py:353
  27.6 6.1 %collective-permute-start.7 = (bf16[64,1280]{1,0:T(8,128)(2,1)S(1)}, bf16[64,1280]{1,0:T(8,128)(2,1)S(1)}, u32[]{:S(2)}, u32[]{:S(2)}) collective-permute-start(bf16[64,1280]{1,0:T(8,128)(2,1)S(1)} %collective-permute-done.5.refs_4_), channel_id=1, source_target_pairs={{0,2},{2,6},{6,10},{10,14},{14,12},{12,8},{8,4},{4,0},{1,3},{3,7},... | collective-permute-start | bytes 491528 | tf_op jit(solution)/shard_map/ppermute | solution.py:352
  30.1 10.1 %collective-permute-start.18 = (f32[256,512]{1,0:T(8,128)S(1)}, f32[256,512]{1,0:T(8,128)S(1)}, u32[]{:S(2)}, u32[]{:S(2)}) collective-permute-start(f32[256,512]{1,0:T(8,128)S(1)} %get-tuple-element.38), channel_id=1, source_target_pairs={{0,1},{1,0},{2,3},{3,2},{4,5},{5,4},{6,7},{7,6},{8,9},{9,8},{10,11... | collective-permute-start | bytes 1572872 | tf_op jit(solution)/shard_map/ppermute | solution.py:367
  34.6 4.3 %collective-permute-start.16 = (f32[128,128]{1,0:T(8,128)S(1)}, f32[128,128]{1,0:T(8,128)S(1)}, u32[]{:S(2)}, u32[]{:S(2)}) collective-permute-start(f32[128,128]{1,0:T(8,128)S(1)} %get-tuple-element.36), channel_id=1, source_target_pairs={{0,16},{16,0},{1,17},{17,1},{2,18},{18,2},{3,19},{19,3},{4,20},{20... | collective-permute-start | bytes 196616 | tf_op jit(solution)/shard_map/ppermute | solution.py:371
  35.2 3.8 %collective-permute-start.15 = (f32[128,128]{1,0:T(8,128)S(1)}, f32[128,128]{1,0:T(8,128)S(1)}, u32[]{:S(2)}, u32[]{:S(2)}) collective-permute-start(f32[128,128]{1,0:T(8,128)S(1)} %get-tuple-element.35.mine), channel_id=1, source_target_pairs={{0,1},{1,0},{2,3},{3,2},{4,5},{5,4},{6,7},{7,6},{8,9},{9,8},{10,11... | collective-permute-start | bytes 196616 | tf_op jit(solution)/shard_map/ppermute | solution.py:372
  39.0 1.3 %collective-permute-start.17 = (f32[128,128]{1,0:T(8,128)S(1)}, f32[128,128]{1,0:T(8,128)S(1)}, u32[]{:S(2)}, u32[]{:S(2)}) collective-permute-start(f32[128,128]{1,0:T(8,128)S(1)} %collective-permute-done.16.two), channel_id=1, source_target_pairs={{0,1},{1,0},{2,3},{3,2},{4,5},{5,4},{6,7},{7,6},{8,9},{9,8},{10,11... | collective-permute-start | bytes 196616 | tf_op jit(solution)/shard_map/ppermute | solution.py:373

commit v5 on v4

--- a/solution.py
+++ b/solution.py
@@ -37,6 +37,10 @@
 
 def contract(left, right):
     return lax.dot_general(left, right, (((1,), (1,)), ((), ())), preferred_element_type=F32)
+
+
+def extra_rows(columns):
+    return 2 * -(-columns // 1024) * 8
 
 
 def prologue_kernel(
@@ -58,9 +62,11 @@
     holder,
     slots,
     sems,
+    hidden_sem,
 ):
     group, place = lax.axis_index("groups"), lax.axis_index("batch")
     cut = first_ref.shape[1]
+    rows = hidden_ref.shape[0]
     here = pl.multiple_of(group * depth, 128)
     there = pl.multiple_of((1 - group) * depth, 128)
     after = pl.multiple_of(group * depth + cut, 128)
@@ -76,54 +82,71 @@
             factor_ref.at[:, pl.ds(after, depth - cut)], second_ref.at[:, : depth - cut], sems.at[5]
         ),
         pltpu.make_async_copy(factor_out_ref, second_ref.at[:, depth - cut :], sems.at[6]),
-        pltpu.make_async_copy(hidden_ref.at[:, pl.ds(there, depth)], to_other_ref.at[:-16], sems.at[7]),
     ]
+    for i in range(depth // 128):
+        large.append(
+            pltpu.make_async_copy(
+                hidden_ref.at[:, pl.ds(there + i * 128, 128)],
+                to_other_ref.at[i * rows : (i + 1) * rows],
+                hidden_sem.at[i],
+            )
+        )
     for copy in small + large:
         copy.start()
     for copy in small:
         copy.wait()
     count = slots.shape[2]
+    items = demand.shape[1]
     column = lax.broadcasted_iota(I32, (1, count * rank), 1)
-
-    def chunk_bounds(chunk, carry):
-        low, high = carry
-        slot = slots[0, 0, chunk]
-
-        def item_bounds(item, state):
-            start, begin, end = state
-            length = lengths[0, item]
-            hit = holder[demand[0, item]] == slot
-            begin = jnp.where(hit, start, begin)
-            end = jnp.where(hit, start + length, end)
-            return start + length, begin, end
-
-        zero = jnp.int32(0)
-        state = (zero, zero, zero)
-        if demand.shape[1] <= 4:
-            for item in range(demand.shape[1]):
-                state = item_bounds(item, state)
-        else:
-            state = lax.fori_loop(0, demand.shape[1], item_bounds, state)
-        inside = (column >= chunk * rank) & (column < (chunk + 1) * rank)
-        return jnp.where(inside, state[1], low), jnp.where(inside, state[2], high)
-
-    none = jnp.zeros((1, count * rank), I32)
-    carry = (none, none)
-    if count <= 8:
+    zero = jnp.int32(0)
+
+    def chunk_mask(chunk):
+        return (column >= chunk * rank) & (column < (chunk + 1) * rank)
+
+    low = high = jnp.zeros((1, count * rank), I32)
+    if items * count <= 64:
+        start = zero
+        spans = []
+        for item in range(items):
+            end = start + lengths[0, item]
+            spans.append((holder[demand[0, item]], start, end))
+            start = end
         for chunk in range(count):
-            carry = chunk_bounds(chunk, carry)
+            slot = slots[0, 0, chunk]
+            begin = end = zero
+            for owner, first, last in spans:
+                begin = jnp.where(owner == slot, first, begin)
+                end = jnp.where(owner == slot, last, end)
+            low = jnp.where(chunk_mask(chunk), begin, low)
+            high = jnp.where(chunk_mask(chunk), end, high)
     else:
-        carry = lax.fori_loop(0, count, chunk_bounds, carry)
-    bounds_ref[0:1, :] = carry[0]
-    bounds_ref[1:2, :] = carry[1]
+
+        def chunk_ends(chunk, carry):
+            low, high = carry
+            slot = slots[0, 0, chunk]
+
+            def item_ends(item, state):
+                start, begin, end = state
+                last = start + lengths[0, item]
+                hit = holder[demand[0, item]] == slot
+                return last, jnp.where(hit, start, begin), jnp.where(hit, last, end)
+
+            _, begin, end = lax.fori_loop(0, items, item_ends, (zero, zero, zero))
+            mask = chunk_mask(chunk)
+            return jnp.where(mask, begin, low), jnp.where(mask, end, high)
+
+        low, high = lax.fori_loop(0, count, chunk_ends, (low, high))
+    bounds_ref[0:1, :] = low
+    bounds_ref[1:2, :] = high
     bounds_ref[2:8, :] = jnp.zeros((6, count * rank), I32)
-    span = min(depth, count * rank)
-    line = lax.broadcasted_iota(I32, (16, span), 0)
-    extra = jnp.zeros((16, span), I32)
-    for i in range(count * rank // span):
-        for first_line, ends in ((0, carry[0]), (8, carry[1])):
-            extra = jnp.where(line == first_line + i, ends[:, i * span : (i + 1) * span], extra)
-    to_other_ref[-16:, :span] = extra.astype(F32).astype(BF16)
+    extra = extra_rows(count * rank)
+    line = lax.broadcasted_iota(I32, (extra, 128), 0)
+    ends = jnp.zeros((extra, 128), I32)
+    for i in range(count * rank // 128):
+        columns = slice(i * 128, (i + 1) * 128)
+        ends = jnp.where(line == i, low[:, columns], ends)
+        ends = jnp.where(line == extra // 2 + i, high[:, columns], ends)
+    to_other_ref[-extra:, :] = ends.astype(F32).astype(BF16)
     for copy in large:
         copy.wait()
 
@@ -134,10 +157,11 @@
     depth = features // 2
     cut = (depth + width) // 2
     count = slots.shape[2]
+    tall = depth // 128 * rows + extra_rows(count * rank)
     return pl.pallas_call(
         functools.partial(prologue_kernel, depth, rank),
         out_shape=(
-            jax.ShapeDtypeStruct((rows + 16, depth), hidden.dtype),
+            jax.ShapeDtypeStruct((tall, 128), hidden.dtype),
             jax.ShapeDtypeStruct((rank, cut), factor.dtype),
             jax.ShapeDtypeStruct((rank, cut), factor.dtype),
             jax.ShapeDtypeStruct((8, count * rank), I32),
@@ -149,7 +173,8 @@
             pltpu.SMEM(lengths.shape, I32),
             pltpu.SMEM(holder_slot.shape, I32),
             pltpu.SMEM((1, 1, count), I32),
-            pltpu.SemaphoreType.DMA((8,)),
+            pltpu.SemaphoreType.DMA((7,)),
+            pltpu.SemaphoreType.DMA((depth // 128,)),
         ],
         compiler_params=params(),
     )(*map(in_hbm, (hidden, factor, factor_out, demand, lengths, holder_slot, slots)))
@@ -222,10 +247,12 @@
     return bounds_ref[0:1, columns], bounds_ref[1:2, columns]
 
 
-def other_ends(other_ref, group, size):
-    line, column = divmod(group * size, other_ref.shape[1])
-    ends = other_ref[-16:, column : column + size].astype(F32).astype(I32)
-    return ends[line : line + 1], ends[8 + line : 9 + line]
+def other_ends(other_ref, extra, group, size):
+    ends = other_ref[-extra:, :].astype(F32).astype(I32)
+    lines = range(group * size // 128, (group + 1) * size // 128)
+    low = jnp.concatenate([ends[i : i + 1] for i in lines], axis=1)
+    high = jnp.concatenate([ends[extra // 2 + i : extra // 2 + i + 1] for i in lines], axis=1)
+    return low, high
 
 
 def fold(masked):
@@ -244,15 +271,19 @@
     cut = pieces[0].shape[1]
     offset = pl.multiple_of(lax.axis_index("groups") * depth, 128)
     own = own_ref[:, pl.ds(offset, depth)]
-    other = other_ref[:-16]
+    count = own.shape[0]
+    other = jnp.concatenate(
+        [other_ref[i * count : (i + 1) * count, :] for i in range(depth // 128)], axis=1
+    )
     rank = pieces[0].shape[0]
     size = GROUP * rank
+    extra = extra_rows(bounds_ref.shape[1])
     totals = [start_ref[...] if last else None for start_ref in starts]
     for i, group in enumerate(groups):
         held = pieces[2 * GROUP * i : 2 * GROUP * (i + 1)]
         first = jnp.concatenate([ref[...] for ref in held[:GROUP]], axis=0)
         second = jnp.concatenate([ref[:, : depth - cut] for ref in held[GROUP:]], axis=0)
-        ends = (own_ends(bounds_ref, group, size), other_ends(other_ref, group, size))
+        ends = (own_ends(bounds_ref, group, size), other_ends(other_ref, extra, group, size))
         for s, rows in enumerate((own, other)):
             part = contract(rows[:, :cut], first) + contract(rows[:, cut:], second)
             kept = fold(jnp.where(group_mask(*ends[s], part.shape), part, 0.0))
@@ -336,7 +367,7 @@
         jnp.asarray(table, I32),
     )
 
-    far, held = base_call(1, True, hidden, value_weight)
+    near, held = base_call(0, True, hidden, value_weight)
     firsts, seconds = [first], [second]
     ahead, behind = (first, second), (first, second)
     for step in range(1, full + 1):
@@ -344,15 +375,14 @@
         d = lax.ppermute(behind[1], "batch", backward)
         b = lax.ppermute(ahead[1], "batch", forward)
         c = lax.ppermute(behind[0], "batch", backward)
-        if step == 1:
-            a, far = lax.optimization_barrier((a, far))
         ahead, behind = (a, b), (c, d)
         firsts += [a, c]
         seconds += [b, d]
-    firsts.append(lax.ppermute(ahead[0], "batch", forward))
-    seconds.append(lax.ppermute(behind[1], "batch", backward))
+    rows_far, a, d = lax.optimization_barrier((held, ahead[0], behind[1]))
+    firsts.append(lax.ppermute(a, "batch", forward))
+    seconds.append(lax.ppermute(d, "batch", backward))
     other = lax.ppermute(to_other, "groups", swap)
-    (near,) = base_call(0, False, held, value_weight)
+    (far,) = base_call(1, False, rows_far, value_weight)
     held, near = lax.optimization_barrier((held, near))
 
     count = owners // GROUP

time: 41.5 us -> 41.9 us (level)
  starting transfers between devices: 18.1 us -> 18.8 us
    ppermute x3, waiting for transfers between devices: 4.36 us -> 1.01 us  [per_device(): d = lax.ppermute(behind[1], 'batch', backward)]
    ppermute x3, waiting for transfers between devices: 0.01 us -> 2.31 us  [per_device(): a = lax.ppermute(ahead[0], 'batch', forward)]
    ppermute x3, starting transfers between devices: 4.7 us -> 2.4 us  [per_device(): b = lax.ppermute(ahead[1], 'batch', forward)]
    ppermute x3, starting transfers between devices: 1.44 us -> 3.73 us  [per_device(): c = lax.ppermute(behind[0], 'batch', backward)]
    ppermute x3, waiting for transfers between devices: 1.37 us -> 2.98 us  [per_device(): c = lax.ppermute(behind[0], 'batch', backward)]
    ppermute x3, starting transfers between devices: 4.48 us -> 5.32 us  [per_device(): a = lax.ppermute(ahead[0], 'batch', forward)]
    ppermute x2, waiting for transfers between devices: 1.76 us -> 1.24 us  [the longest x1 1.24 us: per_device(): seconds.append(lax.ppermute(d, 'batch', backward))]
  transfers between devices with their start and end apart: 19 -> 19, of which waited for: 7 -> 6; matrix products, arithmetic and copies ran while one was open for 0% -> 0% of each run, Pallas kernels for 18% -> 18%
where the time goes in v5:
time: 41.9 us; the launch traced here: 41.8 us
  starting transfers between devices  18.8 us (45%)
  waiting for transfers between devices  12.6 us (30%)
  Pallas kernels  10.4 us (25%)
    pallas_call x2, Pallas kernels, base_call(): pl.pallas_call(functools.partial(base_kernel, side, fetch_rows), out_shap...  5.99 us
    ppermute x3, starting transfers between devices, per_device(): a = lax.ppermute(ahead[0], 'batch', forward)  5.32 us
    ppermute x1, waiting for transfers between devices, per_device(): two = lax.ppermute(theirs, 'groups', swap)  3.75 us
    ppermute x3, starting transfers between devices, per_device(): c = lax.ppermute(behind[0], 'batch', backward)  3.73 us
    ppermute x1, starting transfers between devices, per_device(): other = lax.ppermute(to_other, 'groups', swap)  3.03 us
    ppermute x3, waiting for transfers between devices, per_device(): c = lax.ppermute(behind[0], 'batch', backward)  2.98 us
    ppermute x3, starting transfers between devices, per_device(): b = lax.ppermute(ahead[1], 'batch', forward)  2.4 us
    ppermute x3, waiting for transfers between devices, per_device(): a = lax.ppermute(ahead[0], 'batch', forward)  2.31 us
  transfers between devices with their start and end apart: 19, of which 6 were waited for; matrix products, arithmetic and copies ran while one was open for 0% of the time, Pallas kernels for 18%

profile of v5, /device:TPU:0, one launch (start us, length us, event | category | flops | bytes accessed | tf_op | source)
XLA Modules:
  0.0 41.8 jit_solution(17300752713440718037)
XLA Ops:
  0.0 1.6 %shard_map.82 = (bf16[4112,128]{1,0:T(8,128)(2,1)S(1)}, bf16[64,1280]{1,0:T(8,128)(2,1)S(1)}, bf16[64,1280]{1,0:T(8,128)(2,1)S(1)}, s32[8,512]{1,0:T(8,128)S(1)}) custom-call(bf16[256,4096]{1,0:T(8,128)(2,1)} %rows_in_ref.1, bf16[64,4096]{1,0:T(8,128)(2,1)} %bitcast.4, bf16[64,512]{1,0:T(8,128)(2,1)} %bitcast.5, s32[1,4]{1,0:T(1,128)} %demand_ref.1, ...), custom_call_target="tpu_custom_call" | custom-call | tf_op jit(solution)/shard_map/pallas_call | solution.py:161
  1.6 3.0 %collective-permute-start = (bf16[4112,128]{1,0:T(8,128)(2,1)S(1)}, bf16[4112,128]{1,0:T(8,128)(2,1)S(1)}, u32[]{:S(2)}, u32[]{:S(2)}) collective-permute-start(bf16[4112,128]{1,0:T(8,128)(2,1)S(1)} %get-tuple-element.27), channel_id=1, source_target_pairs={{0,16},{16,0},{1,17},{17,1},{2,18},{18,2},{3,19},{19,3},{4,20},{20... | collective-permute-start | bytes 3158024 | tf_op jit(solution)/shard_map/ppermute | solution.py:384
  4.6 1.5 %collective-permute-start.3 = (bf16[64,1280]{1,0:T(8,128)(2,1)S(1)}, bf16[64,1280]{1,0:T(8,128)(2,1)S(1)}, u32[]{:S(2)}, u32[]{:S(2)}) collective-permute-start(bf16[64,1280]{1,0:T(8,128)(2,1)S(1)} %get-tuple-element.28.refs_3_), channel_id=1, source_target_pairs={{0,2},{2,6},{6,10},{10,14},{14,12},{12,8},{8,4},{4,0},{1,3},{3,7},... | collective-permute-start | bytes 491528 | tf_op jit(solution)/shard_map/ppermute | solution.py:374
  6.1 0.5 %collective-permute-start.7 = (bf16[64,1280]{1,0:T(8,128)(2,1)S(1)}, bf16[64,1280]{1,0:T(8,128)(2,1)S(1)}, u32[]{:S(2)}, u32[]{:S(2)}) collective-permute-start(bf16[64,1280]{1,0:T(8,128)(2,1)S(1)} %get-tuple-element.29.refs_7_.refs_0_), channel_id=1, source_target_pairs={{2,0},{6,2},{10,6},{14,10},{12,14},{8,12},{4,8},{0,4},{3,1},{7,3},... | collective-permute-start | bytes 491528 | tf_op jit(solution)/shard_map/ppermute | solution.py:375
  6.7 1.6 %collective-permute-start.1 = (bf16[64,1280]{1,0:T(8,128)(2,1)S(1)}, bf16[64,1280]{1,0:T(8,128)(2,1)S(1)}, u32[]{:S(2)}, u32[]{:S(2)}) collective-permute-start(bf16[64,1280]{1,0:T(8,128)(2,1)S(1)} %get-tuple-element.28.refs_3_), channel_id=1, source_target_pairs={{2,0},{6,2},{10,6},{14,10},{12,14},{8,12},{4,8},{0,4},{3,1},{7,3},... | collective-permute-start | bytes 491528 | tf_op jit(solution)/shard_map/ppermute | solution.py:377
  8.2 0.4 %collective-permute-start.11 = (bf16[64,1280]{1,0:T(8,128)(2,1)S(1)}, bf16[64,1280]{1,0:T(8,128)(2,1)S(1)}, u32[]{:S(2)}, u32[]{:S(2)}) collective-permute-start(bf16[64,1280]{1,0:T(8,128)(2,1)S(1)} %get-tuple-element.29.refs_7_.refs_0_), channel_id=1, source_target_pairs={{0,2},{2,6},{6,10},{10,14},{14,12},{12,8},{8,4},{4,0},{1,3},{3,7},... | collective-permute-start | bytes 491528 | tf_op jit(solution)/shard_map/ppermute | solution.py:376
  8.7 2.3 %collective-permute-done.3.refs_4_ = bf16[64,1280]{1,0:T(8,128)(2,1)S(1)} collective-permute-done((bf16[64,1280]{1,0:T(8,128)(2,1)S(1)}, bf16[64,1280]{1,0:T(8,128)(2,1)S(1)}, u32[]{:S(2)}, u32[]{:S(2)}) %collective-permute-start.3) | collective-permute-done | bytes 163872 | tf_op jit(solution)/shard_map/ppermute | solution.py:374
  11.0 2.3 %collective-permute-start.4 = (bf16[64,1280]{1,0:T(8,128)(2,1)S(1)}, bf16[64,1280]{1,0:T(8,128)(2,1)S(1)}, u32[]{:S(2)}, u32[]{:S(2)}) collective-permute-start(bf16[64,1280]{1,0:T(8,128)(2,1)S(1)} %collective-permute-done.3.refs_4_), channel_id=1, source_target_pairs={{0,2},{2,6},{6,10},{10,14},{14,12},{12,8},{8,4},{4,0},{1,3},{3,7},... | collective-permute-start | bytes 491528 | tf_op jit(solution)/shard_map/ppermute | solution.py:374
  13.3 0.0 collective-permute-done.7.refs_9_.refs_2_
  13.3 0.5 %collective-permute-start.8 = (bf16[64,1280]{1,0:T(8,128)(2,1)S(1)}, bf16[64,1280]{1,0:T(8,128)(2,1)S(1)}, u32[]{:S(2)}, u32[]{:S(2)}) collective-permute-start(bf16[64,1280]{1,0:T(8,128)(2,1)S(1)} %collective-permute-done.7.refs_9_.refs_2_), channel_id=1, source_target_pairs={{2,0},{6,2},{10,6},{14,10},{12,14},{8,12},{4,8},{0,4},{3,1},{7,3},... | collective-permute-start | bytes 491528 | tf_op jit(solution)/shard_map/ppermute | solution.py:375
  13.8 3.0 %collective-permute-done.1.refs_5_ = bf16[64,1280]{1,0:T(8,128)(2,1)S(1)} collective-permute-done((bf16[64,1280]{1,0:T(8,128)(2,1)S(1)}, bf16[64,1280]{1,0:T(8,128)(2,1)S(1)}, u32[]{:S(2)}, u32[]{:S(2)}) %collective-permute-start.1) | collective-permute-done | bytes 163872 | tf_op jit(solution)/shard_map/ppermute | solution.py:377
  16.8 0.5 %collective-permute-start.2 = (bf16[64,1280]{1,0:T(8,128)(2,1)S(1)}, bf16[64,1280]{1,0:T(8,128)(2,1)S(1)}, u32[]{:S(2)}, u32[]{:S(2)}) collective-permute-start(bf16[64,1280]{1,0:T(8,128)(2,1)S(1)} %collective-permute-done.1.refs_5_), channel_id=1, source_target_pairs={{2,0},{6,2},{10,6},{14,10},{12,14},{8,12},{4,8},{0,4},{3,1},{7,3},... | collective-permute-start | bytes 491528 | tf_op jit(solution)/shard_map/ppermute | solution.py:377
  17.3 0.0 collective-permute-done.11.refs_8_.refs_1_
  17.3 1.5 %collective-permute-start.12 = (bf16[64,1280]{1,0:T(8,128)(2,1)S(1)}, bf16[64,1280]{1,0:T(8,128)(2,1)S(1)}, u32[]{:S(2)}, u32[]{:S(2)}) collective-permute-start(bf16[64,1280]{1,0:T(8,128)(2,1)S(1)} %collective-permute-done.11.refs_8_.refs_1_), channel_id=1, source_target_pairs={{0,2},{2,6},{6,10},{10,14},{14,12},{12,8},{8,4},{4,0},{1,3},{3,7},... | collective-permute-start | bytes 491528 | tf_op jit(solution)/shard_map/ppermute | solution.py:376
  18.8 0.0 collective-permute-done.4.refs_6_
  18.8 1.6 %collective-permute-start.5 = (bf16[64,1280]{1,0:T(8,128)(2,1)S(1)}, bf16[64,1280]{1,0:T(8,128)(2,1)S(1)}, u32[]{:S(2)}, u32[]{:S(2)}) collective-permute-start(bf16[64,1280]{1,0:T(8,128)(2,1)S(1)} %collective-permute-done.4.refs_6_), channel_id=1, source_target_pairs={{0,2},{2,6},{6,10},{10,14},{14,12},{12,8},{8,4},{4,0},{1,3},{3,7},... | collective-permute-start | bytes 491528 | tf_op jit(solution)/shard_map/ppermute | solution.py:374
  20.4 0.0 collective-permute-done.8.refs_7_.refs_4_
  20.4 0.5 %collective-permute-start.9 = (bf16[64,1280]{1,0:T(8,128)(2,1)S(1)}, bf16[64,1280]{1,0:T(8,128)(2,1)S(1)}, u32[]{:S(2)}, u32[]{:S(2)}) collective-permute-start(bf16[64,1280]{1,0:T(8,128)(2,1)S(1)} %collective-permute-done.8.refs_7_.refs_4_), channel_id=1, source_target_pairs={{2,0},{6,2},{10,6},{14,10},{12,14},{8,12},{4,8},{0,4},{3,1},{7,3},... | collective-permute-start | bytes 491528 | tf_op jit(solution)/shard_map/ppermute | solution.py:375
  20.9 3.3 %shard_map.83 = (f32[256,512]{1,0:T(8,128)S(1)}, bf16[256,4096]{1,0:T(8,128)(2,1)S(1)}) custom-call(bf16[256,4096]{1,0:T(8,128)(2,1)} %rows_in_ref.1, bf16[4096,1024]{1,0:T(8,128)(2,1)} %weight_ref.3), custom_call_target="tpu_custom_call" | custom-call | bytes 4194304 | tf_op jit(solution)/shard_map/pallas_call | solution.py:226
  24.2 0.0 collective-permute-done.2.refs_3_
  24.2 1.6 %collective-permute-start.6 = (bf16[64,1280]{1,0:T(8,128)(2,1)S(1)}, bf16[64,1280]{1,0:T(8,128)(2,1)S(1)}, u32[]{:S(2)}, u32[]{:S(2)}) collective-permute-start(bf16[64,1280]{1,0:T(8,128)(2,1)S(1)} %collective-permute-done.2.refs_3_), channel_id=1, source_target_pairs={{2,0},{6,2},{10,6},{14,10},{12,14},{8,12},{4,8},{0,4},{3,1},{7,3},... | collective-permute-start | bytes 491528 | tf_op jit(solution)/shard_map/ppermute | solution.py:377
  25.9 0.0 collective-permute-done.12.refs_10_.refs_3_
  25.9 0.5 %collective-permute-start.13 = (bf16[64,1280]{1,0:T(8,128)(2,1)S(1)}, bf16[64,1280]{1,0:T(8,128)(2,1)S(1)}, u32[]{:S(2)}, u32[]{:S(2)}) collective-permute-start(bf16[64,1280]{1,0:T(8,128)(2,1)S(1)} %collective-permute-done.12.refs_10_.refs_3_), channel_id=1, source_target_pairs={{0,2},{2,6},{6,10},{10,14},{14,12},{12,8},{8,4},{4,0},{1,3},{3,7},... | collective-permute-start | bytes 491528 | tf_op jit(solution)/shard_map/ppermute | solution.py:376
  26.3 0.0 collective-permute-done.5.refs_4_
  26.3 1.0 %collective-permute-done.9.refs_9_.refs_6_ = bf16[64,1280]{1,0:T(8,128)(2,1)S(1)} collective-permute-done((bf16[64,1280]{1,0:T(8,128)(2,1)S(1)}, bf16[64,1280]{1,0:T(8,128)(2,1)S(1)}, u32[]{:S(2)}, u32[]{:S(2)}) %collective-permute-start.9) | collective-permute-done | bytes 163872 | tf_op jit(solution)/shard_map/ppermute | solution.py:375
  27.3 1.6 %collective-permute-start.10 = (bf16[64,1280]{1,0:T(8,128)(2,1)S(1)}, bf16[64,1280]{1,0:T(8,128)(2,1)S(1)}, u32[]{:S(2)}, u32[]{:S(2)}) collective-permute-start(bf16[64,1280]{1,0:T(8,128)(2,1)S(1)} %collective-permute-done.5.refs_4_), channel_id=1, source_target_pairs={{0,2},{2,6},{6,10},{10,14},{14,12},{12,8},{8,4},{4,0},{1,3},{3,7},... | collective-permute-start | bytes 491528 | tf_op jit(solution)/shard_map/ppermute | solution.py:382
  28.9 0.4 %collective-permute-start.14 = (bf16[64,1280]{1,0:T(8,128)(2,1)S(1)}, bf16[64,1280]{1,0:T(8,128)(2,1)S(1)}, u32[]{:S(2)}, u32[]{:S(2)}) collective-permute-start(bf16[64,1280]{1,0:T(8,128)(2,1)S(1)} %collective-permute-done.9.refs_9_.refs_6_), channel_id=1, source_target_pairs={{2,0},{6,2},{10,6},{14,10},{12,14},{8,12},{4,8},{0,4},{3,1},{7,3},... | collective-permute-start | bytes 491528 | tf_op jit(solution)/shard_map/ppermute | solution.py:383
  29.3 2.7 %shard_map.85 = f32[256,512]{1,0:T(8,128)S(1)} custom-call(bf16[256,4096]{1,0:T(8,128)(2,1)S(1)} %get-tuple-element.34.refs_0_.rows_in_ref, bf16[4096,1024]{1,0:T(8,128)(2,1)} %weight_ref.3), custom_call_target="tpu_custom_call" | custom-call | bytes 4194304 | tf_op jit(solution)/shard_map/pallas_call | solution.py:226
  32.0 0.0 collective-permute-done.refs_1_
  32.1 0.8 %shard_map.84 = (f32[256,128]{1,0:T(8,128)S(1)}, f32[256,128]{1,0:T(8,128)S(1)}) custom-call(bf16[256,4096]{1,0:T(8,128)(2,1)S(1)} %get-tuple-element.34.refs_0_.rows_in_ref, bf16[4112,128]{1,0:T(8,128)(2,1)S(1)} %collective-permute-done.refs_1_, s32[8,512]{1,0:T(8,128)S(1)} %get-tuple-element.23.refs_2_.bounds_ref, ...), custom_call_target="tpu_custom_call" | custom-call | flops 8589934592 | bytes 16777216 | tf_op jit(solution)/shard_map/pallas_call | solution.py:307
  32.9 0.1 collective-permute-start.18
  32.9 0.0 collective-permute-done.6.refs_5_
  32.9 0.0 collective-permute-done.13.refs_8_.refs_5_
  33.0 0.0 collective-permute-done.10.refs_6_
  33.0 1.2 %collective-permute-done.14.refs_10_.refs_7_ = bf16[64,1280]{1,0:T(8,128)(2,1)S(1)} collective-permute-done((bf16[64,1280]{1,0:T(8,128)(2,1)S(1)}, bf16[64,1280]{1,0:T(8,128)(2,1)S(1)}, u32[]{:S(2)}, u32[]{:S(2)}) %collective-permute-start.14) | collective-permute-done | bytes 163872 | tf_op jit(solution)/shard_map/ppermute | solution.py:383
  34.2 0.9 %shard_map.86 = (f32[128,128]{1,0:T(8,128)S(1)}, f32[128,128]{1,0:T(8,128)S(1)}) custom-call(bf16[256,4096]{1,0:T(8,128)(2,1)S(1)} %get-tuple-element.34.refs_0_.rows_in_ref, bf16[4112,128]{1,0:T(8,128)(2,1)S(1)} %collective-permute-done.refs_1_, s32[8,512]{1,0:T(8,128)S(1)} %get-tuple-element.23.refs_2_.bounds_ref, ...), custom_call_target="tpu_custom_call" | custom-call | flops 8589934592 | bytes 16777216 | tf_op jit(solution)/shard_map/pallas_call | solution.py:307
  35.1 0.6 %collective-permute-start.16 = (f32[128,128]{1,0:T(8,128)S(1)}, f32[128,128]{1,0:T(8,128)S(1)}, u32[]{:S(2)}, u32[]{:S(2)}) collective-permute-start(f32[128,128]{1,0:T(8,128)S(1)} %get-tuple-element.38), channel_id=1, source_target_pairs={{0,16},{16,0},{1,17},{17,1},{2,18},{18,2},{3,19},{19,3},{4,20},{20... | collective-permute-start | bytes 196616 | tf_op jit(solution)/shard_map/ppermute | solution.py:401
  35.6 0.0 collective-permute-start.15
  35.7 3.8 %collective-permute-done.16.two = f32[128,128]{1,0:T(8,128)S(1)} collective-permute-done((f32[128,128]{1,0:T(8,128)S(1)}, f32[128,128]{1,0:T(8,128)S(1)}, u32[]{:S(2)}, u32[]{:S(2)}) %collective-permute-start.16) | collective-permute-done | bytes 65568 | tf_op jit(solution)/shard_map/ppermute | solution.py:401
  39.4 0.0 collective-permute-start.17
  39.4 0.0 collective-permute-done.15.one
  39.4 1.2 %collective-permute-done.17.three = f32[128,128]{1,0:T(8,128)S(1)} collective-permute-done((f32[128,128]{1,0:T(8,128)S(1)}, f32[128,128]{1,0:T(8,128)S(1)}, u32[]{:S(2)}, u32[]{:S(2)}) %collective-permute-start.17) | collective-permute-done | bytes 65568 | tf_op jit(solution)/shard_map/ppermute | solution.py:403
  40.7 0.0 collective-permute-done.18.far_ref
  40.7 1.1 %shard_map.87 = bf16[256,512]{1,0:T(8,128)(2,1)} custom-call(s32[8,512]{1,0:T(8,128)S(1)} %get-tuple-element.23.refs_2_.bounds_ref, f32[128,128]{1,0:T(8,128)S(1)} %get-tuple-element.37.mine, f32[128,128]{1,0:T(8,128)S(1)} %collective-permute-done.15.one, f32[128,128]{1,0:T(8,128)S(1)} %collective-permute-done.16.two, ...), custom_call_target="tpu_custom_call" | custom-call | tf_op jit(solution)/shard_map/pallas_call | solution.py:406
Async XLA Ops:
  1.6 30.4 %collective-permute-start = (bf16[4112,128]{1,0:T(8,128)(2,1)S(1)}, bf16[4112,128]{1,0:T(8,128)(2,1)S(1)}, u32[]{:S(2)}, u32[]{:S(2)}) collective-permute-start(bf16[4112,128]{1,0:T(8,128)(2,1)S(1)} %get-tuple-element.27), channel_id=1, source_target_pairs={{0,16},{16,0},{1,17},{17,1},{2,18},{18,2},{3,19},{19,3},{4,20},{20... | collective-permute-start | bytes 3158024 | tf_op jit(solution)/shard_map/ppermute | solution.py:384
  4.6 6.4 %collective-permute-start.3 = (bf16[64,1280]{1,0:T(8,128)(2,1)S(1)}, bf16[64,1280]{1,0:T(8,128)(2,1)S(1)}, u32[]{:S(2)}, u32[]{:S(2)}) collective-permute-start(bf16[64,1280]{1,0:T(8,128)(2,1)S(1)} %get-tuple-element.28.refs_3_), channel_id=1, source_target_pairs={{0,2},{2,6},{6,10},{10,14},{14,12},{12,8},{8,4},{4,0},{1,3},{3,7},... | collective-permute-start | bytes 491528 | tf_op jit(solution)/shard_map/ppermute | solution.py:374
  6.1 7.1 %collective-permute-start.7 = (bf16[64,1280]{1,0:T(8,128)(2,1)S(1)}, bf16[64,1280]{1,0:T(8,128)(2,1)S(1)}, u32[]{:S(2)}, u32[]{:S(2)}) collective-permute-start(bf16[64,1280]{1,0:T(8,128)(2,1)S(1)} %get-tuple-element.29.refs_7_.refs_0_), channel_id=1, source_target_pairs={{2,0},{6,2},{10,6},{14,10},{12,14},{8,12},{4,8},{0,4},{3,1},{7,3},... | collective-permute-start | bytes 491528 | tf_op jit(solution)/shard_map/ppermute | solution.py:375
  6.7 10.1 %collective-permute-start.1 = (bf16[64,1280]{1,0:T(8,128)(2,1)S(1)}, bf16[64,1280]{1,0:T(8,128)(2,1)S(1)}, u32[]{:S(2)}, u32[]{:S(2)}) collective-permute-start(bf16[64,1280]{1,0:T(8,128)(2,1)S(1)} %get-tuple-element.28.refs_3_), channel_id=1, source_target_pairs={{2,0},{6,2},{10,6},{14,10},{12,14},{8,12},{4,8},{0,4},{3,1},{7,3},... | collective-permute-start | bytes 491528 | tf_op jit(solution)/shard_map/ppermute | solution.py:377
  8.2 9.1 %collective-permute-start.11 = (bf16[64,1280]{1,0:T(8,128)(2,1)S(1)}, bf16[64,1280]{1,0:T(8,128)(2,1)S(1)}, u32[]{:S(2)}, u32[]{:S(2)}) collective-permute-start(bf16[64,1280]{1,0:T(8,128)(2,1)S(1)} %get-tuple-element.29.refs_7_.refs_0_), channel_id=1, source_target_pairs={{0,2},{2,6},{6,10},{10,14},{14,12},{12,8},{8,4},{4,0},{1,3},{3,7},... | collective-permute-start | bytes 491528 | tf_op jit(solution)/shard_map/ppermute | solution.py:376
  11.0 7.8 %collective-permute-start.4 = (bf16[64,1280]{1,0:T(8,128)(2,1)S(1)}, bf16[64,1280]{1,0:T(8,128)(2,1)S(1)}, u32[]{:S(2)}, u32[]{:S(2)}) collective-permute-start(bf16[64,1280]{1,0:T(8,128)(2,1)S(1)} %collective-permute-done.3.refs_4_), channel_id=1, source_target_pairs={{0,2},{2,6},{6,10},{10,14},{14,12},{12,8},{8,4},{4,0},{1,3},{3,7},... | collective-permute-start | bytes 491528 | tf_op jit(solution)/shard_map/ppermute | solution.py:374
  13.3 7.1 %collective-permute-start.8 = (bf16[64,1280]{1,0:T(8,128)(2,1)S(1)}, bf16[64,1280]{1,0:T(8,128)(2,1)S(1)}, u32[]{:S(2)}, u32[]{:S(2)}) collective-permute-start(bf16[64,1280]{1,0:T(8,128)(2,1)S(1)} %collective-permute-done.7.refs_9_.refs_2_), channel_id=1, source_target_pairs={{2,0},{6,2},{10,6},{14,10},{12,14},{8,12},{4,8},{0,4},{3,1},{7,3},... | collective-permute-start | bytes 491528 | tf_op jit(solution)/shard_map/ppermute | solution.py:375
  16.8 7.5 %collective-permute-start.2 = (bf16[64,1280]{1,0:T(8,128)(2,1)S(1)}, bf16[64,1280]{1,0:T(8,128)(2,1)S(1)}, u32[]{:S(2)}, u32[]{:S(2)}) collective-permute-start(bf16[64,1280]{1,0:T(8,128)(2,1)S(1)} %collective-permute-done.1.refs_5_), channel_id=1, source_target_pairs={{2,0},{6,2},{10,6},{14,10},{12,14},{8,12},{4,8},{0,4},{3,1},{7,3},... | collective-permute-start | bytes 491528 | tf_op jit(solution)/shard_map/ppermute | solution.py:377
  17.3 8.6 %collective-permute-start.12 = (bf16[64,1280]{1,0:T(8,128)(2,1)S(1)}, bf16[64,1280]{1,0:T(8,128)(2,1)S(1)}, u32[]{:S(2)}, u32[]{:S(2)}) collective-permute-start(bf16[64,1280]{1,0:T(8,128)(2,1)S(1)} %collective-permute-done.11.refs_8_.refs_1_), channel_id=1, source_target_pairs={{0,2},{2,6},{6,10},{10,14},{14,12},{12,8},{8,4},{4,0},{1,3},{3,7},... | collective-permute-start | bytes 491528 | tf_op jit(solution)/shard_map/ppermute | solution.py:376
  18.8 7.5 %collective-permute-start.5 = (bf16[64,1280]{1,0:T(8,128)(2,1)S(1)}, bf16[64,1280]{1,0:T(8,128)(2,1)S(1)}, u32[]{:S(2)}, u32[]{:S(2)}) collective-permute-start(bf16[64,1280]{1,0:T(8,128)(2,1)S(1)} %collective-permute-done.4.refs_6_), channel_id=1, source_target_pairs={{0,2},{2,6},{6,10},{10,14},{14,12},{12,8},{8,4},{4,0},{1,3},{3,7},... | collective-permute-start | bytes 491528 | tf_op jit(solution)/shard_map/ppermute | solution.py:374
  20.4 6.9 %collective-permute-start.9 = (bf16[64,1280]{1,0:T(8,128)(2,1)S(1)}, bf16[64,1280]{1,0:T(8,128)(2,1)S(1)}, u32[]{:S(2)}, u32[]{:S(2)}) collective-permute-start(bf16[64,1280]{1,0:T(8,128)(2,1)S(1)} %collective-permute-done.8.refs_7_.refs_4_), channel_id=1, source_target_pairs={{2,0},{6,2},{10,6},{14,10},{12,14},{8,12},{4,8},{0,4},{3,1},{7,3},... | collective-permute-start | bytes 491528 | tf_op jit(solution)/shard_map/ppermute | solution.py:375
  24.2 8.7 %collective-permute-start.6 = (bf16[64,1280]{1,0:T(8,128)(2,1)S(1)}, bf16[64,1280]{1,0:T(8,128)(2,1)S(1)}, u32[]{:S(2)}, u32[]{:S(2)}) collective-permute-start(bf16[64,1280]{1,0:T(8,128)(2,1)S(1)} %collective-permute-done.2.refs_3_), channel_id=1, source_target_pairs={{2,0},{6,2},{10,6},{14,10},{12,14},{8,12},{4,8},{0,4},{3,1},{7,3},... | collective-permute-start | bytes 491528 | tf_op jit(solution)/shard_map/ppermute | solution.py:377
  25.9 7.1 %collective-permute-start.13 = (bf16[64,1280]{1,0:T(8,128)(2,1)S(1)}, bf16[64,1280]{1,0:T(8,128)(2,1)S(1)}, u32[]{:S(2)}, u32[]{:S(2)}) collective-permute-start(bf16[64,1280]{1,0:T(8,128)(2,1)S(1)} %collective-permute-done.12.refs_10_.refs_3_), channel_id=1, source_target_pairs={{0,2},{2,6},{6,10},{10,14},{14,12},{12,8},{8,4},{4,0},{1,3},{3,7},... | collective-permute-start | bytes 491528 | tf_op jit(solution)/shard_map/ppermute | solution.py:376
  27.3 5.6 %collective-permute-start.10 = (bf16[64,1280]{1,0:T(8,128)(2,1)S(1)}, bf16[64,1280]{1,0:T(8,128)(2,1)S(1)}, u32[]{:S(2)}, u32[]{:S(2)}) collective-permute-start(bf16[64,1280]{1,0:T(8,128)(2,1)S(1)} %collective-permute-done.5.refs_4_), channel_id=1, source_target_pairs={{0,2},{2,6},{6,10},{10,14},{14,12},{12,8},{8,4},{4,0},{1,3},{3,7},... | collective-permute-start | bytes 491528 | tf_op jit(solution)/shard_map/ppermute | solution.py:382
  28.9 5.3 %collective-permute-start.14 = (bf16[64,1280]{1,0:T(8,128)(2,1)S(1)}, bf16[64,1280]{1,0:T(8,128)(2,1)S(1)}, u32[]{:S(2)}, u32[]{:S(2)}) collective-permute-start(bf16[64,1280]{1,0:T(8,128)(2,1)S(1)} %collective-permute-done.9.refs_9_.refs_6_), channel_id=1, source_target_pairs={{2,0},{6,2},{10,6},{14,10},{12,14},{8,12},{4,8},{0,4},{3,1},{7,3},... | collective-permute-start | bytes 491528 | tf_op jit(solution)/shard_map/ppermute | solution.py:383
  32.9 7.8 %collective-permute-start.18 = (f32[256,512]{1,0:T(8,128)S(1)}, f32[256,512]{1,0:T(8,128)S(1)}, u32[]{:S(2)}, u32[]{:S(2)}) collective-permute-start(f32[256,512]{1,0:T(8,128)S(1)} %shard_map.85), channel_id=1, source_target_pairs={{0,1},{1,0},{2,3},{3,2},{4,5},{5,4},{6,7},{7,6},{8,9},{9,8},{10,11... | collective-permute-start | bytes 1572872 | tf_op jit(solution)/shard_map/ppermute | solution.py:397
  35.1 4.3 %collective-permute-start.16 = (f32[128,128]{1,0:T(8,128)S(1)}, f32[128,128]{1,0:T(8,128)S(1)}, u32[]{:S(2)}, u32[]{:S(2)}) collective-permute-start(f32[128,128]{1,0:T(8,128)S(1)} %get-tuple-element.38), channel_id=1, source_target_pairs={{0,16},{16,0},{1,17},{17,1},{2,18},{18,2},{3,19},{19,3},{4,20},{20... | collective-permute-start | bytes 196616 | tf_op jit(solution)/shard_map/ppermute | solution.py:401
  35.6 3.8 %collective-permute-start.15 = (f32[128,128]{1,0:T(8,128)S(1)}, f32[128,128]{1,0:T(8,128)S(1)}, u32[]{:S(2)}, u32[]{:S(2)}) collective-permute-start(f32[128,128]{1,0:T(8,128)S(1)} %get-tuple-element.37.mine), channel_id=1, source_target_pairs={{0,1},{1,0},{2,3},{3,2},{4,5},{5,4},{6,7},{7,6},{8,9},{9,8},{10,11... | collective-permute-start | bytes 196616 | tf_op jit(solution)/shard_map/ppermute | solution.py:402
  39.4 1.3 %collective-permute-start.17 = (f32[128,128]{1,0:T(8,128)S(1)}, f32[128,128]{1,0:T(8,128)S(1)}, u32[]{:S(2)}, u32[]{:S(2)}) collective-permute-start(f32[128,128]{1,0:T(8,128)S(1)} %collective-permute-done.16.two), channel_id=1, source_target_pairs={{0,1},{1,0},{2,3},{3,2},{4,5},{5,4},{6,7},{7,6},{8,9},{9,8},{10,11... | collective-permute-start | bytes 196616 | tf_op jit(solution)/shard_map/ppermute | solution.py:403

commit v6 on v5

--- a/solution.py
+++ b/solution.py
@@ -367,7 +367,7 @@
         jnp.asarray(table, I32),
     )
 
-    near, held = base_call(0, True, hidden, value_weight)
+    far, held = base_call(1, True, hidden, value_weight)
     firsts, seconds = [first], [second]
     ahead, behind = (first, second), (first, second)
     for step in range(1, full + 1):
@@ -375,15 +375,16 @@
         d = lax.ppermute(behind[1], "batch", backward)
         b = lax.ppermute(ahead[1], "batch", forward)
         c = lax.ppermute(behind[0], "batch", backward)
+        if step == 1:
+            a, far = lax.optimization_barrier((a, far))
         ahead, behind = (a, b), (c, d)
         firsts += [a, c]
         seconds += [b, d]
-    rows_far, a, d = lax.optimization_barrier((held, ahead[0], behind[1]))
+    rows_near, a, d = lax.optimization_barrier((held, ahead[0], behind[1]))
     firsts.append(lax.ppermute(a, "batch", forward))
     seconds.append(lax.ppermute(d, "batch", backward))
     other = lax.ppermute(to_other, "groups", swap)
-    (far,) = base_call(1, False, rows_far, value_weight)
-    held, near = lax.optimization_barrier((held, near))
+    (near,) = base_call(0, False, rows_near, value_weight)
 
     count = owners // GROUP
     early = range(count - 1)
@@ -393,7 +394,7 @@
         pieces += seconds[group * GROUP : (group + 1) * GROUP]
     sides = (held, other, bounds)
     starts = rank_call(tuple(early), depth, *sides, pieces, None)
-    *starts, far = lax.optimization_barrier((*starts, far))
+    *starts, far, near = lax.optimization_barrier((*starts, far, near))
     far = lax.ppermute(far, "tensor", swap)
     pieces = firsts[-GROUP:] + seconds[-GROUP:]
     mine, theirs = rank_call((count - 1,), depth, *sides, pieces, starts)

time: 41.9 us -> 42 us (level)
  starting transfers between devices: 18.8 us -> 17.9 us
  waiting for transfers between devices: 12.6 us -> 13.5 us
    ppermute x3, waiting for transfers between devices: 1.01 us -> 4.24 us  [per_device(): d = lax.ppermute(behind[1], 'batch', backward)]
    ppermute x3, waiting for transfers between devices: 2.31 us -> 0.01 us  [per_device(): a = lax.ppermute(ahead[0], 'batch', forward)]
    ppermute x3, starting transfers between devices: 3.73 us -> 2.11 us  [per_device(): c = lax.ppermute(behind[0], 'batch', backward)]
    ppermute x3, starting transfers between devices: 2.4 us -> 3.97 us  [per_device(): b = lax.ppermute(ahead[1], 'batch', forward)]
    ppermute x3, starting transfers between devices: 5.32 us -> 4.48 us  [per_device(): a = lax.ppermute(ahead[0], 'batch', forward)]
  transfers between devices with their start and end apart: 19 -> 19, of which waited for: 6 -> 8; matrix products, arithmetic and copies ran while one was open for 0% -> 0% of each run, Pallas kernels for 18% -> 18%
where the time goes in v6:
time: 42 us; the launch traced here: 41.8 us
  starting transfers between devices  17.9 us (43%)
  waiting for transfers between devices  13.5 us (32%)
  Pallas kernels  10.4 us (25%)
    pallas_call x2, Pallas kernels, base_call(): pl.pallas_call(functools.partial(base_kernel, side, fetch_rows), out_shap...  5.98 us
    ppermute x3, starting transfers between devices, per_device(): a = lax.ppermute(ahead[0], 'batch', forward)  4.48 us
    ppermute x3, waiting for transfers between devices, per_device(): d = lax.ppermute(behind[1], 'batch', backward)  4.24 us
    ppermute x3, starting transfers between devices, per_device(): b = lax.ppermute(ahead[1], 'batch', forward)  3.97 us
    ppermute x1, waiting for transfers between devices, per_device(): two = lax.ppermute(theirs, 'groups', swap)  3.75 us
    ppermute x1, starting transfers between devices, per_device(): other = lax.ppermute(to_other, 'groups', swap)  3.03 us
    ppermute x3, waiting for transfers between devices, per_device(): c = lax.ppermute(behind[0], 'batch', backward)  2.97 us
    ppermute x3, starting transfers between devices, per_device(): c = lax.ppermute(behind[0], 'batch', backward)  2.11 us
  transfers between devices with their start and end apart: 19, of which 8 were waited for; matrix products, arithmetic and copies ran while one was open for 0% of the time, Pallas kernels for 18%

profile of v6, /device:TPU:0, one launch (start us, length us, event | category | flops | bytes accessed | tf_op | source)
XLA Modules:
  0.0 41.8 jit_solution(11462815106233458698)
XLA Ops:
  0.0 1.6 %shard_map.82 = (bf16[4112,128]{1,0:T(8,128)(2,1)S(1)}, bf16[64,1280]{1,0:T(8,128)(2,1)S(1)}, bf16[64,1280]{1,0:T(8,128)(2,1)S(1)}, s32[8,512]{1,0:T(8,128)S(1)}) custom-call(bf16[256,4096]{1,0:T(8,128)(2,1)} %rows_in_ref.1, bf16[64,4096]{1,0:T(8,128)(2,1)} %bitcast.4, bf16[64,512]{1,0:T(8,128)(2,1)} %bitcast.5, s32[1,4]{1,0:T(1,128)} %demand_ref.1, ...), custom_call_target="tpu_custom_call" | custom-call | tf_op jit(solution)/shard_map/pallas_call | solution.py:161
  1.6 3.0 %collective-permute-start = (bf16[4112,128]{1,0:T(8,128)(2,1)S(1)}, bf16[4112,128]{1,0:T(8,128)(2,1)S(1)}, u32[]{:S(2)}, u32[]{:S(2)}) collective-permute-start(bf16[4112,128]{1,0:T(8,128)(2,1)S(1)} %get-tuple-element.26), channel_id=1, source_target_pairs={{0,16},{16,0},{1,17},{17,1},{2,18},{18,2},{3,19},{19,3},{4,20},{20... | collective-permute-start | bytes 3158024 | tf_op jit(solution)/shard_map/ppermute | solution.py:386
  4.6 1.5 %collective-permute-start.3 = (bf16[64,1280]{1,0:T(8,128)(2,1)S(1)}, bf16[64,1280]{1,0:T(8,128)(2,1)S(1)}, u32[]{:S(2)}, u32[]{:S(2)}) collective-permute-start(bf16[64,1280]{1,0:T(8,128)(2,1)S(1)} %get-tuple-element.27.refs_3_), channel_id=1, source_target_pairs={{0,2},{2,6},{6,10},{10,14},{14,12},{12,8},{8,4},{4,0},{1,3},{3,7},... | collective-permute-start | bytes 491528 | tf_op jit(solution)/shard_map/ppermute | solution.py:374
  6.1 0.5 %collective-permute-start.7 = (bf16[64,1280]{1,0:T(8,128)(2,1)S(1)}, bf16[64,1280]{1,0:T(8,128)(2,1)S(1)}, u32[]{:S(2)}, u32[]{:S(2)}) collective-permute-start(bf16[64,1280]{1,0:T(8,128)(2,1)S(1)} %get-tuple-element.30.refs_7_.refs_0_), channel_id=1, source_target_pairs={{2,0},{6,2},{10,6},{14,10},{12,14},{8,12},{4,8},{0,4},{3,1},{7,3},... | collective-permute-start | bytes 491528 | tf_op jit(solution)/shard_map/ppermute | solution.py:375
  6.7 1.6 %collective-permute-start.1 = (bf16[64,1280]{1,0:T(8,128)(2,1)S(1)}, bf16[64,1280]{1,0:T(8,128)(2,1)S(1)}, u32[]{:S(2)}, u32[]{:S(2)}) collective-permute-start(bf16[64,1280]{1,0:T(8,128)(2,1)S(1)} %get-tuple-element.27.refs_3_), channel_id=1, source_target_pairs={{2,0},{6,2},{10,6},{14,10},{12,14},{8,12},{4,8},{0,4},{3,1},{7,3},... | collective-permute-start | bytes 491528 | tf_op jit(solution)/shard_map/ppermute | solution.py:377
  8.2 0.4 %collective-permute-start.11 = (bf16[64,1280]{1,0:T(8,128)(2,1)S(1)}, bf16[64,1280]{1,0:T(8,128)(2,1)S(1)}, u32[]{:S(2)}, u32[]{:S(2)}) collective-permute-start(bf16[64,1280]{1,0:T(8,128)(2,1)S(1)} %get-tuple-element.30.refs_7_.refs_0_), channel_id=1, source_target_pairs={{0,2},{2,6},{6,10},{10,14},{14,12},{12,8},{8,4},{4,0},{1,3},{3,7},... | collective-permute-start | bytes 491528 | tf_op jit(solution)/shard_map/ppermute | solution.py:376
  8.7 3.3 %shard_map.83 = (f32[256,512]{1,0:T(8,128)S(1)}, bf16[256,4096]{1,0:T(8,128)(2,1)S(1)}) custom-call(bf16[256,4096]{1,0:T(8,128)(2,1)} %rows_in_ref.1, bf16[4096,1024]{1,0:T(8,128)(2,1)} %weight_ref.3), custom_call_target="tpu_custom_call" | custom-call | bytes 4194304 | tf_op jit(solution)/shard_map/pallas_call | solution.py:226
  12.0 0.0 collective-permute-done.3.refs_4_
  12.0 1.3 %collective-permute-done.7.refs_9_.refs_2_ = bf16[64,1280]{1,0:T(8,128)(2,1)S(1)} collective-permute-done((bf16[64,1280]{1,0:T(8,128)(2,1)S(1)}, bf16[64,1280]{1,0:T(8,128)(2,1)S(1)}, u32[]{:S(2)}, u32[]{:S(2)}) %collective-permute-start.7) | collective-permute-done | bytes 163872 | tf_op jit(solution)/shard_map/ppermute | solution.py:375
  13.3 0.5 %collective-permute-start.8 = (bf16[64,1280]{1,0:T(8,128)(2,1)S(1)}, bf16[64,1280]{1,0:T(8,128)(2,1)S(1)}, u32[]{:S(2)}, u32[]{:S(2)}) collective-permute-start(bf16[64,1280]{1,0:T(8,128)(2,1)S(1)} %collective-permute-done.7.refs_9_.refs_2_), channel_id=1, source_target_pairs={{2,0},{6,2},{10,6},{14,10},{12,14},{8,12},{4,8},{0,4},{3,1},{7,3},... | collective-permute-start | bytes 491528 | tf_op jit(solution)/shard_map/ppermute | solution.py:375
  13.8 1.5 %collective-permute-start.4 = (bf16[64,1280]{1,0:T(8,128)(2,1)S(1)}, bf16[64,1280]{1,0:T(8,128)(2,1)S(1)}, u32[]{:S(2)}, u32[]{:S(2)}) collective-permute-start(bf16[64,1280]{1,0:T(8,128)(2,1)S(1)} %collective-permute-done.3.refs_4_), channel_id=1, source_target_pairs={{0,2},{2,6},{6,10},{10,14},{14,12},{12,8},{8,4},{4,0},{1,3},{3,7},... | collective-permute-start | bytes 491528 | tf_op jit(solution)/shard_map/ppermute | solution.py:374
  15.3 1.5 %collective-permute-done.1.refs_5_ = bf16[64,1280]{1,0:T(8,128)(2,1)S(1)} collective-permute-done((bf16[64,1280]{1,0:T(8,128)(2,1)S(1)}, bf16[64,1280]{1,0:T(8,128)(2,1)S(1)}, u32[]{:S(2)}, u32[]{:S(2)}) %collective-permute-start.1) | collective-permute-done | bytes 163872 | tf_op jit(solution)/shard_map/ppermute | solution.py:377
  16.8 0.0 collective-permute-start.2
  16.8 0.0 collective-permute-done.11.refs_8_.refs_1_
  16.8 2.0 %collective-permute-start.12 = (bf16[64,1280]{1,0:T(8,128)(2,1)S(1)}, bf16[64,1280]{1,0:T(8,128)(2,1)S(1)}, u32[]{:S(2)}, u32[]{:S(2)}) collective-permute-start(bf16[64,1280]{1,0:T(8,128)(2,1)S(1)} %collective-permute-done.11.refs_8_.refs_1_), channel_id=1, source_target_pairs={{0,2},{2,6},{6,10},{10,14},{14,12},{12,8},{8,4},{4,0},{1,3},{3,7},... | collective-permute-start | bytes 491528 | tf_op jit(solution)/shard_map/ppermute | solution.py:376
  18.8 1.6 %collective-permute-done.8.refs_7_.refs_4_ = bf16[64,1280]{1,0:T(8,128)(2,1)S(1)} collective-permute-done((bf16[64,1280]{1,0:T(8,128)(2,1)S(1)}, bf16[64,1280]{1,0:T(8,128)(2,1)S(1)}, u32[]{:S(2)}, u32[]{:S(2)}) %collective-permute-start.8) | collective-permute-done | bytes 163872 | tf_op jit(solution)/shard_map/ppermute | solution.py:375
  20.4 0.5 %collective-permute-start.9 = (bf16[64,1280]{1,0:T(8,128)(2,1)S(1)}, bf16[64,1280]{1,0:T(8,128)(2,1)S(1)}, u32[]{:S(2)}, u32[]{:S(2)}) collective-permute-start(bf16[64,1280]{1,0:T(8,128)(2,1)S(1)} %collective-permute-done.8.refs_7_.refs_4_), channel_id=1, source_target_pairs={{2,0},{6,2},{10,6},{14,10},{12,14},{8,12},{4,8},{0,4},{3,1},{7,3},... | collective-permute-start | bytes 491528 | tf_op jit(solution)/shard_map/ppermute | solution.py:375
  20.9 0.0 collective-permute-done.4.refs_6_
  20.9 1.5 %collective-permute-start.5 = (bf16[64,1280]{1,0:T(8,128)(2,1)S(1)}, bf16[64,1280]{1,0:T(8,128)(2,1)S(1)}, u32[]{:S(2)}, u32[]{:S(2)}) collective-permute-start(bf16[64,1280]{1,0:T(8,128)(2,1)S(1)} %collective-permute-done.4.refs_6_), channel_id=1, source_target_pairs={{0,2},{2,6},{6,10},{10,14},{14,12},{12,8},{8,4},{4,0},{1,3},{3,7},... | collective-permute-start | bytes 491528 | tf_op jit(solution)/shard_map/ppermute | solution.py:374
  22.4 1.5 %collective-permute-done.2.refs_3_ = bf16[64,1280]{1,0:T(8,128)(2,1)S(1)} collective-permute-done((bf16[64,1280]{1,0:T(8,128)(2,1)S(1)}, bf16[64,1280]{1,0:T(8,128)(2,1)S(1)}, u32[]{:S(2)}, u32[]{:S(2)}) %collective-permute-start.2) | collective-permute-done | bytes 163872 | tf_op jit(solution)/shard_map/ppermute | solution.py:377
  23.9 0.5 %collective-permute-start.6 = (bf16[64,1280]{1,0:T(8,128)(2,1)S(1)}, bf16[64,1280]{1,0:T(8,128)(2,1)S(1)}, u32[]{:S(2)}, u32[]{:S(2)}) collective-permute-start(bf16[64,1280]{1,0:T(8,128)(2,1)S(1)} %collective-permute-done.2.refs_3_), channel_id=1, source_target_pairs={{2,0},{6,2},{10,6},{14,10},{12,14},{8,12},{4,8},{0,4},{3,1},{7,3},... | collective-permute-start | bytes 491528 | tf_op jit(solution)/shard_map/ppermute | solution.py:377
  24.4 0.0 collective-permute-done.12.refs_10_.refs_3_
  24.5 1.5 %collective-permute-start.13 = (bf16[64,1280]{1,0:T(8,128)(2,1)S(1)}, bf16[64,1280]{1,0:T(8,128)(2,1)S(1)}, u32[]{:S(2)}, u32[]{:S(2)}) collective-permute-start(bf16[64,1280]{1,0:T(8,128)(2,1)S(1)} %collective-permute-done.12.refs_10_.refs_3_), channel_id=1, source_target_pairs={{0,2},{2,6},{6,10},{10,14},{14,12},{12,8},{8,4},{4,0},{1,3},{3,7},... | collective-permute-start | bytes 491528 | tf_op jit(solution)/shard_map/ppermute | solution.py:376
  25.9 1.4 %collective-permute-done.9.refs_9_.refs_6_ = bf16[64,1280]{1,0:T(8,128)(2,1)S(1)} collective-permute-done((bf16[64,1280]{1,0:T(8,128)(2,1)S(1)}, bf16[64,1280]{1,0:T(8,128)(2,1)S(1)}, u32[]{:S(2)}, u32[]{:S(2)}) %collective-permute-start.9) | collective-permute-done | bytes 163872 | tf_op jit(solution)/shard_map/ppermute | solution.py:375
  27.3 0.0 collective-permute-done.5.refs_4_
  27.3 1.6 %collective-permute-start.10 = (bf16[64,1280]{1,0:T(8,128)(2,1)S(1)}, bf16[64,1280]{1,0:T(8,128)(2,1)S(1)}, u32[]{:S(2)}, u32[]{:S(2)}) collective-permute-start(bf16[64,1280]{1,0:T(8,128)(2,1)S(1)} %collective-permute-done.5.refs_4_), channel_id=1, source_target_pairs={{0,2},{2,6},{6,10},{10,14},{14,12},{12,8},{8,4},{4,0},{1,3},{3,7},... | collective-permute-start | bytes 491528 | tf_op jit(solution)/shard_map/ppermute | solution.py:384
  28.9 0.4 %collective-permute-start.14 = (bf16[64,1280]{1,0:T(8,128)(2,1)S(1)}, bf16[64,1280]{1,0:T(8,128)(2,1)S(1)}, u32[]{:S(2)}, u32[]{:S(2)}) collective-permute-start(bf16[64,1280]{1,0:T(8,128)(2,1)S(1)} %collective-permute-done.9.refs_9_.refs_6_), channel_id=1, source_target_pairs={{2,0},{6,2},{10,6},{14,10},{12,14},{8,12},{4,8},{0,4},{3,1},{7,3},... | collective-permute-start | bytes 491528 | tf_op jit(solution)/shard_map/ppermute | solution.py:385
  29.3 2.7 %shard_map.85.near_ref = f32[256,512]{1,0:T(8,128)S(1)} custom-call(bf16[256,4096]{1,0:T(8,128)(2,1)S(1)} %get-tuple-element.36.refs_0_.rows_in_ref, bf16[4096,1024]{1,0:T(8,128)(2,1)} %weight_ref.3), custom_call_target="tpu_custom_call" | custom-call | bytes 4194304 | tf_op jit(solution)/shard_map/pallas_call | solution.py:226
  32.1 0.0 collective-permute-done.refs_1_
  32.1 0.8 %shard_map.84 = (f32[256,128]{1,0:T(8,128)S(1)}, f32[256,128]{1,0:T(8,128)S(1)}) custom-call(bf16[256,4096]{1,0:T(8,128)(2,1)S(1)} %get-tuple-element.36.refs_0_.rows_in_ref, bf16[4112,128]{1,0:T(8,128)(2,1)S(1)} %collective-permute-done.refs_1_, s32[8,512]{1,0:T(8,128)S(1)} %get-tuple-element.24.refs_2_.bounds_ref, ...), custom_call_target="tpu_custom_call" | custom-call | flops 8589934592 | bytes 16777216 | tf_op jit(solution)/shard_map/pallas_call | solution.py:307
  32.9 0.1 collective-permute-start.18
  32.9 0.0 collective-permute-done.6.refs_5_
  32.9 0.0 collective-permute-done.13.refs_8_.refs_5_
  33.0 0.0 collective-permute-done.10.refs_6_
  33.0 1.2 %collective-permute-done.14.refs_10_.refs_7_ = bf16[64,1280]{1,0:T(8,128)(2,1)S(1)} collective-permute-done((bf16[64,1280]{1,0:T(8,128)(2,1)S(1)}, bf16[64,1280]{1,0:T(8,128)(2,1)S(1)}, u32[]{:S(2)}, u32[]{:S(2)}) %collective-permute-start.14) | collective-permute-done | bytes 163872 | tf_op jit(solution)/shard_map/ppermute | solution.py:385
  34.2 0.9 %shard_map.86 = (f32[128,128]{1,0:T(8,128)S(1)}, f32[128,128]{1,0:T(8,128)S(1)}) custom-call(bf16[256,4096]{1,0:T(8,128)(2,1)S(1)} %get-tuple-element.36.refs_0_.rows_in_ref, bf16[4112,128]{1,0:T(8,128)(2,1)S(1)} %collective-permute-done.refs_1_, s32[8,512]{1,0:T(8,128)S(1)} %get-tuple-element.24.refs_2_.bounds_ref, ...), custom_call_target="tpu_custom_call" | custom-call | flops 8589934592 | bytes 16777216 | tf_op jit(solution)/shard_map/pallas_call | solution.py:307
  35.1 0.6 %collective-permute-start.16 = (f32[128,128]{1,0:T(8,128)S(1)}, f32[128,128]{1,0:T(8,128)S(1)}, u32[]{:S(2)}, u32[]{:S(2)}) collective-permute-start(f32[128,128]{1,0:T(8,128)S(1)} %get-tuple-element.40), channel_id=1, source_target_pairs={{0,16},{16,0},{1,17},{17,1},{2,18},{18,2},{3,19},{19,3},{4,20},{20... | collective-permute-start | bytes 196616 | tf_op jit(solution)/shard_map/ppermute | solution.py:402
  35.7 0.0 collective-permute-start.15
  35.7 3.8 %collective-permute-done.16.two = f32[128,128]{1,0:T(8,128)S(1)} collective-permute-done((f32[128,128]{1,0:T(8,128)S(1)}, f32[128,128]{1,0:T(8,128)S(1)}, u32[]{:S(2)}, u32[]{:S(2)}) %collective-permute-start.16) | collective-permute-done | bytes 65568 | tf_op jit(solution)/shard_map/ppermute | solution.py:402
  39.4 0.0 collective-permute-start.17
  39.4 0.0 collective-permute-done.15.one
  39.4 1.2 %collective-permute-done.17.three = f32[128,128]{1,0:T(8,128)S(1)} collective-permute-done((f32[128,128]{1,0:T(8,128)S(1)}, f32[128,128]{1,0:T(8,128)S(1)}, u32[]{:S(2)}, u32[]{:S(2)}) %collective-permute-start.17) | collective-permute-done | bytes 65568 | tf_op jit(solution)/shard_map/ppermute | solution.py:404
  40.7 0.0 collective-permute-done.18.far_ref
  40.7 1.1 %shard_map.87 = bf16[256,512]{1,0:T(8,128)(2,1)} custom-call(s32[8,512]{1,0:T(8,128)S(1)} %get-tuple-element.24.refs_2_.bounds_ref, f32[128,128]{1,0:T(8,128)S(1)} %get-tuple-element.39.mine, f32[128,128]{1,0:T(8,128)S(1)} %collective-permute-done.15.one, f32[128,128]{1,0:T(8,128)S(1)} %collective-permute-done.16.two, ...), custom_call_target="tpu_custom_call" | custom-call | tf_op jit(solution)/shard_map/pallas_call | solution.py:407
Async XLA Ops:
  1.6 30.5 %collective-permute-start = (bf16[4112,128]{1,0:T(8,128)(2,1)S(1)}, bf16[4112,128]{1,0:T(8,128)(2,1)S(1)}, u32[]{:S(2)}, u32[]{:S(2)}) collective-permute-start(bf16[4112,128]{1,0:T(8,128)(2,1)S(1)} %get-tuple-element.26), channel_id=1, source_target_pairs={{0,16},{16,0},{1,17},{17,1},{2,18},{18,2},{3,19},{19,3},{4,20},{20... | collective-permute-start | bytes 3158024 | tf_op jit(solution)/shard_map/ppermute | solution.py:386
  4.6 7.3 %collective-permute-start.3 = (bf16[64,1280]{1,0:T(8,128)(2,1)S(1)}, bf16[64,1280]{1,0:T(8,128)(2,1)S(1)}, u32[]{:S(2)}, u32[]{:S(2)}) collective-permute-start(bf16[64,1280]{1,0:T(8,128)(2,1)S(1)} %get-tuple-element.27.refs_3_), channel_id=1, source_target_pairs={{0,2},{2,6},{6,10},{10,14},{14,12},{12,8},{8,4},{4,0},{1,3},{3,7},... | collective-permute-start | bytes 491528 | tf_op jit(solution)/shard_map/ppermute | solution.py:374
  6.1 7.1 %collective-permute-start.7 = (bf16[64,1280]{1,0:T(8,128)(2,1)S(1)}, bf16[64,1280]{1,0:T(8,128)(2,1)S(1)}, u32[]{:S(2)}, u32[]{:S(2)}) collective-permute-start(bf16[64,1280]{1,0:T(8,128)(2,1)S(1)} %get-tuple-element.30.refs_7_.refs_0_), channel_id=1, source_target_pairs={{2,0},{6,2},{10,6},{14,10},{12,14},{8,12},{4,8},{0,4},{3,1},{7,3},... | collective-permute-start | bytes 491528 | tf_op jit(solution)/shard_map/ppermute | solution.py:375
  6.7 10.1 %collective-permute-start.1 = (bf16[64,1280]{1,0:T(8,128)(2,1)S(1)}, bf16[64,1280]{1,0:T(8,128)(2,1)S(1)}, u32[]{:S(2)}, u32[]{:S(2)}) collective-permute-start(bf16[64,1280]{1,0:T(8,128)(2,1)S(1)} %get-tuple-element.27.refs_3_), channel_id=1, source_target_pairs={{2,0},{6,2},{10,6},{14,10},{12,14},{8,12},{4,8},{0,4},{3,1},{7,3},... | collective-permute-start | bytes 491528 | tf_op jit(solution)/shard_map/ppermute | solution.py:377
  8.2 8.5 %collective-permute-start.11 = (bf16[64,1280]{1,0:T(8,128)(2,1)S(1)}, bf16[64,1280]{1,0:T(8,128)(2,1)S(1)}, u32[]{:S(2)}, u32[]{:S(2)}) collective-permute-start(bf16[64,1280]{1,0:T(8,128)(2,1)S(1)} %get-tuple-element.30.refs_7_.refs_0_), channel_id=1, source_target_pairs={{0,2},{2,6},{6,10},{10,14},{14,12},{12,8},{8,4},{4,0},{1,3},{3,7},... | collective-permute-start | bytes 491528 | tf_op jit(solution)/shard_map/ppermute | solution.py:376
  13.3 7.1 %collective-permute-start.8 = (bf16[64,1280]{1,0:T(8,128)(2,1)S(1)}, bf16[64,1280]{1,0:T(8,128)(2,1)S(1)}, u32[]{:S(2)}, u32[]{:S(2)}) collective-permute-start(bf16[64,1280]{1,0:T(8,128)(2,1)S(1)} %collective-permute-done.7.refs_9_.refs_2_), channel_id=1, source_target_pairs={{2,0},{6,2},{10,6},{14,10},{12,14},{8,12},{4,8},{0,4},{3,1},{7,3},... | collective-permute-start | bytes 491528 | tf_op jit(solution)/shard_map/ppermute | solution.py:375
  13.8 7.1 %collective-permute-start.4 = (bf16[64,1280]{1,0:T(8,128)(2,1)S(1)}, bf16[64,1280]{1,0:T(8,128)(2,1)S(1)}, u32[]{:S(2)}, u32[]{:S(2)}) collective-permute-start(bf16[64,1280]{1,0:T(8,128)(2,1)S(1)} %collective-permute-done.3.refs_4_), channel_id=1, source_target_pairs={{0,2},{2,6},{6,10},{10,14},{14,12},{12,8},{8,4},{4,0},{1,3},{3,7},... | collective-permute-start | bytes 491528 | tf_op jit(solution)/shard_map/ppermute | solution.py:374
  16.8 7.1 %collective-permute-start.2 = (bf16[64,1280]{1,0:T(8,128)(2,1)S(1)}, bf16[64,1280]{1,0:T(8,128)(2,1)S(1)}, u32[]{:S(2)}, u32[]{:S(2)}) collective-permute-start(bf16[64,1280]{1,0:T(8,128)(2,1)S(1)} %collective-permute-done.1.refs_5_), channel_id=1, source_target_pairs={{2,0},{6,2},{10,6},{14,10},{12,14},{8,12},{4,8},{0,4},{3,1},{7,3},... | collective-permute-start | bytes 491528 | tf_op jit(solution)/shard_map/ppermute | solution.py:377
  16.8 7.7 %collective-permute-start.12 = (bf16[64,1280]{1,0:T(8,128)(2,1)S(1)}, bf16[64,1280]{1,0:T(8,128)(2,1)S(1)}, u32[]{:S(2)}, u32[]{:S(2)}) collective-permute-start(bf16[64,1280]{1,0:T(8,128)(2,1)S(1)} %collective-permute-done.11.refs_8_.refs_1_), channel_id=1, source_target_pairs={{0,2},{2,6},{6,10},{10,14},{14,12},{12,8},{8,4},{4,0},{1,3},{3,7},... | collective-permute-start | bytes 491528 | tf_op jit(solution)/shard_map/ppermute | solution.py:376
  20.4 6.9 %collective-permute-start.9 = (bf16[64,1280]{1,0:T(8,128)(2,1)S(1)}, bf16[64,1280]{1,0:T(8,128)(2,1)S(1)}, u32[]{:S(2)}, u32[]{:S(2)}) collective-permute-start(bf16[64,1280]{1,0:T(8,128)(2,1)S(1)} %collective-permute-done.8.refs_7_.refs_4_), channel_id=1, source_target_pairs={{2,0},{6,2},{10,6},{14,10},{12,14},{8,12},{4,8},{0,4},{3,1},{7,3},... | collective-permute-start | bytes 491528 | tf_op jit(solution)/shard_map/ppermute | solution.py:375
  20.9 6.4 %collective-permute-start.5 = (bf16[64,1280]{1,0:T(8,128)(2,1)S(1)}, bf16[64,1280]{1,0:T(8,128)(2,1)S(1)}, u32[]{:S(2)}, u32[]{:S(2)}) collective-permute-start(bf16[64,1280]{1,0:T(8,128)(2,1)S(1)} %collective-permute-done.4.refs_6_), channel_id=1, source_target_pairs={{0,2},{2,6},{6,10},{10,14},{14,12},{12,8},{8,4},{4,0},{1,3},{3,7},... | collective-permute-start | bytes 491528 | tf_op jit(solution)/shard_map/ppermute | solution.py:374
  23.9 9.0 %collective-permute-start.6 = (bf16[64,1280]{1,0:T(8,128)(2,1)S(1)}, bf16[64,1280]{1,0:T(8,128)(2,1)S(1)}, u32[]{:S(2)}, u32[]{:S(2)}) collective-permute-start(bf16[64,1280]{1,0:T(8,128)(2,1)S(1)} %collective-permute-done.2.refs_3_), channel_id=1, source_target_pairs={{2,0},{6,2},{10,6},{14,10},{12,14},{8,12},{4,8},{0,4},{3,1},{7,3},... | collective-permute-start | bytes 491528 | tf_op jit(solution)/shard_map/ppermute | solution.py:377
  24.5 8.5 %collective-permute-start.13 = (bf16[64,1280]{1,0:T(8,128)(2,1)S(1)}, bf16[64,1280]{1,0:T(8,128)(2,1)S(1)}, u32[]{:S(2)}, u32[]{:S(2)}) collective-permute-start(bf16[64,1280]{1,0:T(8,128)(2,1)S(1)} %collective-permute-done.12.refs_10_.refs_3_), channel_id=1, source_target_pairs={{0,2},{2,6},{6,10},{10,14},{14,12},{12,8},{8,4},{4,0},{1,3},{3,7},... | collective-permute-start | bytes 491528 | tf_op jit(solution)/shard_map/ppermute | solution.py:376
  27.3 5.6 %collective-permute-start.10 = (bf16[64,1280]{1,0:T(8,128)(2,1)S(1)}, bf16[64,1280]{1,0:T(8,128)(2,1)S(1)}, u32[]{:S(2)}, u32[]{:S(2)}) collective-permute-start(bf16[64,1280]{1,0:T(8,128)(2,1)S(1)} %collective-permute-done.5.refs_4_), channel_id=1, source_target_pairs={{0,2},{2,6},{6,10},{10,14},{14,12},{12,8},{8,4},{4,0},{1,3},{3,7},... | collective-permute-start | bytes 491528 | tf_op jit(solution)/shard_map/ppermute | solution.py:384
  28.9 5.3 %collective-permute-start.14 = (bf16[64,1280]{1,0:T(8,128)(2,1)S(1)}, bf16[64,1280]{1,0:T(8,128)(2,1)S(1)}, u32[]{:S(2)}, u32[]{:S(2)}) collective-permute-start(bf16[64,1280]{1,0:T(8,128)(2,1)S(1)} %collective-permute-done.9.refs_9_.refs_6_), channel_id=1, source_target_pairs={{2,0},{6,2},{10,6},{14,10},{12,14},{8,12},{4,8},{0,4},{3,1},{7,3},... | collective-permute-start | bytes 491528 | tf_op jit(solution)/shard_map/ppermute | solution.py:385
  32.9 7.8 %collective-permute-start.18 = (f32[256,512]{1,0:T(8,128)S(1)}, f32[256,512]{1,0:T(8,128)S(1)}, u32[]{:S(2)}, u32[]{:S(2)}) collective-permute-start(f32[256,512]{1,0:T(8,128)S(1)} %get-tuple-element.42), channel_id=1, source_target_pairs={{0,1},{1,0},{2,3},{3,2},{4,5},{5,4},{6,7},{7,6},{8,9},{9,8},{10,11... | collective-permute-start | bytes 1572872 | tf_op jit(solution)/shard_map/ppermute | solution.py:398
  35.1 4.3 %collective-permute-start.16 = (f32[128,128]{1,0:T(8,128)S(1)}, f32[128,128]{1,0:T(8,128)S(1)}, u32[]{:S(2)}, u32[]{:S(2)}) collective-permute-start(f32[128,128]{1,0:T(8,128)S(1)} %get-tuple-element.40), channel_id=1, source_target_pairs={{0,16},{16,0},{1,17},{17,1},{2,18},{18,2},{3,19},{19,3},{4,20},{20... | collective-permute-start | bytes 196616 | tf_op jit(solution)/shard_map/ppermute | solution.py:402
  35.7 3.8 %collective-permute-start.15 = (f32[128,128]{1,0:T(8,128)S(1)}, f32[128,128]{1,0:T(8,128)S(1)}, u32[]{:S(2)}, u32[]{:S(2)}) collective-permute-start(f32[128,128]{1,0:T(8,128)S(1)} %get-tuple-element.39.mine), channel_id=1, source_target_pairs={{0,1},{1,0},{2,3},{3,2},{4,5},{5,4},{6,7},{7,6},{8,9},{9,8},{10,11... | collective-permute-start | bytes 196616 | tf_op jit(solution)/shard_map/ppermute | solution.py:403
  39.4 1.3 %collective-permute-start.17 = (f32[128,128]{1,0:T(8,128)S(1)}, f32[128,128]{1,0:T(8,128)S(1)}, u32[]{:S(2)}, u32[]{:S(2)}) collective-permute-start(f32[128,128]{1,0:T(8,128)S(1)} %collective-permute-done.16.two), channel_id=1, source_target_pairs={{0,1},{1,0},{2,3},{3,2},{4,5},{5,4},{6,7},{7,6},{8,9},{9,8},{10,11... | collective-permute-start | bytes 196616 | tf_op jit(solution)/shard_map/ppermute | solution.py:404

commit v7 on v6

--- a/solution.py
+++ b/solution.py
@@ -54,8 +54,7 @@
     holder_ref,
     slots_ref,
     to_other_ref,
-    first_ref,
-    second_ref,
+    shard_ref,
     bounds_ref,
     demand,
     lengths,
@@ -65,23 +64,21 @@
     hidden_sem,
 ):
     group, place = lax.axis_index("groups"), lax.axis_index("batch")
-    cut = first_ref.shape[1]
+    core = lax.axis_index("tensor")
     rows = hidden_ref.shape[0]
     here = pl.multiple_of(group * depth, 128)
     there = pl.multiple_of((1 - group) * depth, 128)
-    after = pl.multiple_of(group * depth + cut, 128)
     small = [
         pltpu.make_async_copy(demand_ref, demand, sems.at[0]),
         pltpu.make_async_copy(lengths_ref, lengths, sems.at[1]),
         pltpu.make_async_copy(holder_ref, holder, sems.at[2]),
-        pltpu.make_async_copy(slots_ref.at[pl.ds(place, 1)], slots, sems.at[3]),
+        pltpu.make_async_copy(slots_ref.at[pl.ds(place * 2 + core, 1)], slots, sems.at[3]),
     ]
     large = [
-        pltpu.make_async_copy(factor_ref.at[:, pl.ds(here, cut)], first_ref, sems.at[4]),
         pltpu.make_async_copy(
-            factor_ref.at[:, pl.ds(after, depth - cut)], second_ref.at[:, : depth - cut], sems.at[5]
+            factor_ref.at[:, pl.ds(here, depth)], shard_ref.at[:, :depth], sems.at[4]
         ),
-        pltpu.make_async_copy(factor_out_ref, second_ref.at[:, depth - cut :], sems.at[6]),
+        pltpu.make_async_copy(factor_out_ref, shard_ref.at[:, depth:], sems.at[5]),
     ]
     for i in range(depth // 128):
         large.append(
@@ -155,25 +152,23 @@
     rows, features = hidden.shape
     rank, width = factor_out.shape
     depth = features // 2
-    cut = (depth + width) // 2
     count = slots.shape[2]
     tall = depth // 128 * rows + extra_rows(count * rank)
     return pl.pallas_call(
         functools.partial(prologue_kernel, depth, rank),
         out_shape=(
             jax.ShapeDtypeStruct((tall, 128), hidden.dtype),
-            jax.ShapeDtypeStruct((rank, cut), factor.dtype),
-            jax.ShapeDtypeStruct((rank, cut), factor.dtype),
+            jax.ShapeDtypeStruct((rank, depth + width), factor.dtype),
             jax.ShapeDtypeStruct((8, count * rank), I32),
         ),
         in_specs=[HBM] * 7,
-        out_specs=(VMEM,) * 4,
+        out_specs=(VMEM,) * 3,
         scratch_shapes=[
             pltpu.SMEM(demand.shape, I32),
             pltpu.SMEM(lengths.shape, I32),
             pltpu.SMEM(holder_slot.shape, I32),
             pltpu.SMEM((1, 1, count), I32),
-            pltpu.SemaphoreType.DMA((7,)),
+            pltpu.SemaphoreType.DMA((6,)),
             pltpu.SemaphoreType.DMA((depth // 128,)),
         ],
         compiler_params=params(),
@@ -265,27 +260,24 @@
 def rank_kernel(groups, depth, last, *refs):
     refs = list(refs)
     own_ref, other_ref, bounds_ref = refs[:3]
-    pieces = refs[3:]
-    pieces, rest = pieces[: 2 * GROUP * len(groups)], pieces[2 * GROUP * len(groups) :]
+    shards, rest = refs[3 : 3 + GROUP * len(groups)], refs[3 + GROUP * len(groups) :]
     starts, outs = (rest[:2], rest[2:]) if last else ((None, None), rest)
-    cut = pieces[0].shape[1]
     offset = pl.multiple_of(lax.axis_index("groups") * depth, 128)
     own = own_ref[:, pl.ds(offset, depth)]
     count = own.shape[0]
     other = jnp.concatenate(
         [other_ref[i * count : (i + 1) * count, :] for i in range(depth // 128)], axis=1
     )
-    rank = pieces[0].shape[0]
+    rank = shards[0].shape[0]
     size = GROUP * rank
     extra = extra_rows(bounds_ref.shape[1])
     totals = [start_ref[...] if last else None for start_ref in starts]
     for i, group in enumerate(groups):
-        held = pieces[2 * GROUP * i : 2 * GROUP * (i + 1)]
-        first = jnp.concatenate([ref[...] for ref in held[:GROUP]], axis=0)
-        second = jnp.concatenate([ref[:, : depth - cut] for ref in held[GROUP:]], axis=0)
+        held = shards[GROUP * i : GROUP * (i + 1)]
+        factor = jnp.concatenate([ref[:, :depth] for ref in held], axis=0)
         ends = (own_ends(bounds_ref, group, size), other_ends(other_ref, extra, group, size))
         for s, rows in enumerate((own, other)):
-            part = contract(rows[:, :cut], first) + contract(rows[:, cut:], second)
+            part = contract(rows, factor)
             kept = fold(jnp.where(group_mask(*ends[s], part.shape), part, 0.0))
             totals[s] = kept if totals[s] is None else totals[s] + kept
     for total, out_ref in zip(totals, outs):
@@ -297,13 +289,13 @@
         out_ref[...] = total
 
 
-def rank_call(groups, depth, own, other, bounds, pieces, starts):
+def rank_call(groups, depth, own, other, bounds, shards, starts):
     rows = own.shape[0]
-    rank = pieces[0].shape[0]
+    rank = shards[0].shape[0]
     last = starts is not None
     shape = (rows // 2, 2 * rank) if last else (rows, 2 * rank)
     out = jax.ShapeDtypeStruct(shape, F32)
-    operands = [own, other, bounds, *pieces, *(starts or ())]
+    operands = [own, other, bounds, *shards, *(starts or ())]
     return pl.pallas_call(
         functools.partial(rank_kernel, groups, depth, last),
         out_shape=(out, out),
@@ -344,9 +336,16 @@
     rank, width = factor_out.shape[1:]
     depth = features // 2
     order = ring_order(owners)
-    forward = [(order[i], order[(i + 1) % owners]) for i in range(owners)]
-    backward = [(b, a) for a, b in forward]
+    ring = [(order[i], order[(i + 1) % owners]) for i in range(owners)]
+    chain = [
+        [(2 * a + core, 2 * b + core) if core == side else (2 * b + core, 2 * a + core)
+         for a, b in ring for core in (0, 1)]
+        for side in (0, 1)
+    ]
     swap = [(0, 1), (1, 0)]
+
+    def hop(side, shard):
+        return lax.ppermute(shard, ("batch", "tensor"), chain[side])
 
     full = (owners - 1) // 2
     distances = [0]
@@ -354,10 +353,11 @@
         distances += [step, -step]
     distances.append(owners // 2)
     table = [
-        [[order[(order.index(me) - distance) % owners] for distance in distances]]
+        [[order[(order.index(me) - sign * distance) % owners] for distance in distances]]
         for me in range(owners)
+        for sign in (1, -1)
     ]
-    to_other, first, second, bounds = prologue(
+    to_other, shard, bounds = prologue(
         hidden,
         factor_in[0].T,
         factor_out[0],
@@ -368,42 +368,31 @@
     )
 
     far, held = base_call(1, True, hidden, value_weight)
-    firsts, seconds = [first], [second]
-    ahead, behind = (first, second), (first, second)
+    shards = [shard]
+    x = y = shard
     for step in range(1, full + 1):
-        a = lax.ppermute(ahead[0], "batch", forward)
-        d = lax.ppermute(behind[1], "batch", backward)
-        b = lax.ppermute(ahead[1], "batch", forward)
-        c = lax.ppermute(behind[0], "batch", backward)
+        x, y = hop(0, x), hop(1, y)
         if step == 1:
-            a, far = lax.optimization_barrier((a, far))
-        ahead, behind = (a, b), (c, d)
-        firsts += [a, c]
-        seconds += [b, d]
-    rows_near, a, d = lax.optimization_barrier((held, ahead[0], behind[1]))
-    firsts.append(lax.ppermute(a, "batch", forward))
-    seconds.append(lax.ppermute(d, "batch", backward))
+            x, far = lax.optimization_barrier((x, far))
+            (near,) = base_call(0, False, held, value_weight)
+            y, near = lax.optimization_barrier((y, near))
+        shards += [x, y]
+    shards.append(hop(0, x))
     other = lax.ppermute(to_other, "groups", swap)
-    (near,) = base_call(0, False, rows_near, value_weight)
 
     count = owners // GROUP
     early = range(count - 1)
-    pieces = []
-    for group in early:
-        pieces += firsts[group * GROUP : (group + 1) * GROUP]
-        pieces += seconds[group * GROUP : (group + 1) * GROUP]
     sides = (held, other, bounds)
-    starts = rank_call(tuple(early), depth, *sides, pieces, None)
-    *starts, far, near = lax.optimization_barrier((*starts, far, near))
+    starts = rank_call(tuple(early), depth, *sides, shards[:-GROUP], None)
+    *starts, far = lax.optimization_barrier((*starts, far))
     far = lax.ppermute(far, "tensor", swap)
-    pieces = firsts[-GROUP:] + seconds[-GROUP:]
-    mine, theirs = rank_call((count - 1,), depth, *sides, pieces, starts)
+    mine, theirs = rank_call((count - 1,), depth, *sides, shards[-GROUP:], starts)
 
     two = lax.ppermute(theirs, "groups", swap)
     one = lax.ppermute(mine, "tensor", swap)
     three = lax.ppermute(two, "tensor", swap)
 
-    operands = [bounds, mine, one, two, three, near, far, *seconds]
+    operands = [bounds, mine, one, two, three, near, far, *shards]
     return pl.pallas_call(
         final_kernel,
         out_shape=jax.ShapeDtypeStruct((rows, width), BF16),

time: 42 us -> 50.2 us (1.20)
  waiting for transfers between devices: 13.5 us -> 29.1 us
  starting transfers between devices: 17.9 us -> 10.5 us
    ppermute x14 -> x7, waiting for transfers between devices: 8.46 us -> 23.9 us  [hop(): return lax.ppermute(shard, ('batch', 'tensor'), chain[side])]
    ppermute x14 -> x7, starting transfers between devices: 14.2 us -> 7.01 us  [hop(): return lax.ppermute(shard, ('batch', 'tensor'), chain[side])]
  transfers between devices with their start and end apart: 19 -> 12, of which waited for: 8 -> 7; matrix products, arithmetic and copies ran while one was open for 0% -> 0% of each run, Pallas kernels for 18% -> 15%
where the time goes in v7:
time: 50.2 us; the launch traced here: 50 us
  waiting for transfers between devices  29.1 us (58%)
  starting transfers between devices  10.5 us (21%)
  Pallas kernels  10.3 us (21%)
    ppermute x7, waiting for transfers between devices, hop(): return lax.ppermute(shard, ('batch', 'tensor'), chain[side])  23.9 us
    ppermute x7, starting transfers between devices, hop(): return lax.ppermute(shard, ('batch', 'tensor'), chain[side])  7.01 us
    pallas_call x2, Pallas kernels, base_call(): pl.pallas_call(functools.partial(base_kernel, side, fetch_rows), out_shap...  5.99 us
    ppermute x1, waiting for transfers between devices, per_device(): two = lax.ppermute(theirs, 'groups', swap)  3.93 us
    ppermute x1, starting transfers between devices, per_device(): other = lax.ppermute(to_other, 'groups', swap)  3.03 us
    pallas_call x2, Pallas kernels, rank_call(): pl.pallas_call(functools.partial(rank_kernel, groups, depth, last), out_s...  1.65 us
    pallas_call x1, Pallas kernels, prologue(): pl.pallas_call(functools.partial(prologue_kernel, depth, rank), out_shape...  1.59 us
    ppermute x1, waiting for transfers between devices, per_device(): three = lax.ppermute(two, 'tensor', swap)  1.25 us
  transfers between devices with their start and end apart: 12, of which 7 were waited for; matrix products, arithmetic and copies ran while one was open for 0% of the time, Pallas kernels for 15%

profile of v7, /device:TPU:0, one launch (start us, length us, event | category | flops | bytes accessed | tf_op | source)
XLA Modules:
  0.0 50.0 jit_solution(7482868443743003303)
XLA Ops:
  0.0 1.6 %shard_map.82 = (bf16[4112,128]{1,0:T(8,128)(2,1)S(1)}, bf16[64,2560]{1,0:T(8,128)(2,1)S(1)}, s32[8,512]{1,0:T(8,128)S(1)}) custom-call(bf16[256,4096]{1,0:T(8,128)(2,1)} %rows_in_ref.1, bf16[64,4096]{1,0:T(8,128)(2,1)} %bitcast.4, bf16[64,512]{1,0:T(8,128)(2,1)} %bitcast.5, s32[1,4]{1,0:T(1,128)} %demand_ref.1, s32[1,4]{1,0:T(1,128)} %lengths_ref.1, ...), custom_call_target="tpu_custom_call" | custom-call | tf_op jit(solution)/shard_map/pallas_call | solution.py:157
  1.6 3.0 %collective-permute-start = (bf16[4112,128]{1,0:T(8,128)(2,1)S(1)}, bf16[4112,128]{1,0:T(8,128)(2,1)S(1)}, u32[]{:S(2)}, u32[]{:S(2)}) collective-permute-start(bf16[4112,128]{1,0:T(8,128)(2,1)S(1)} %get-tuple-element.23), channel_id=1, source_target_pairs={{0,16},{16,0},{1,17},{17,1},{2,18},{18,2},{3,19},{19,3},{4,20},{20... | collective-permute-start | bytes 3158024 | tf_op jit(solution)/shard_map/ppermute | solution.py:381
  4.6 1.5 %collective-permute-start.3 = (bf16[64,2560]{1,0:T(8,128)(2,1)S(1)}, bf16[64,2560]{1,0:T(8,128)(2,1)S(1)}, u32[]{:S(2)}, u32[]{:S(2)}) collective-permute-start(bf16[64,2560]{1,0:T(8,128)(2,1)S(1)} %get-tuple-element.24.refs_3_.refs_0_), channel_id=1, source_target_pairs={{0,2},{3,1},{2,6},{7,3},{6,10},{11,7},{10,14},{15,11},{14,12},{13,... | collective-permute-start | bytes 983048 | tf_op jit(solution)/shard_map/ppermute | solution.py:348
  6.1 0.5 %collective-permute-start.1 = (bf16[64,2560]{1,0:T(8,128)(2,1)S(1)}, bf16[64,2560]{1,0:T(8,128)(2,1)S(1)}, u32[]{:S(2)}, u32[]{:S(2)}) collective-permute-start(bf16[64,2560]{1,0:T(8,128)(2,1)S(1)} %get-tuple-element.24.refs_3_.refs_0_), channel_id=1, source_target_pairs={{2,0},{1,3},{6,2},{3,7},{10,6},{7,11},{14,10},{11,15},{12,14},{15,... | collective-permute-start | bytes 983048 | tf_op jit(solution)/shard_map/ppermute | solution.py:348
  6.7 3.3 %shard_map.83 = (f32[256,512]{1,0:T(8,128)S(1)}, bf16[256,4096]{1,0:T(8,128)(2,1)S(1)}) custom-call(bf16[256,4096]{1,0:T(8,128)(2,1)} %rows_in_ref.1, bf16[4096,1024]{1,0:T(8,128)(2,1)} %weight_ref.3), custom_call_target="tpu_custom_call" | custom-call | bytes 4194304 | tf_op jit(solution)/shard_map/pallas_call | solution.py:221
  9.9 5.2 %collective-permute-done.3.refs_4_.refs_1_ = bf16[64,2560]{1,0:T(8,128)(2,1)S(1)} collective-permute-done((bf16[64,2560]{1,0:T(8,128)(2,1)S(1)}, bf16[64,2560]{1,0:T(8,128)(2,1)S(1)}, u32[]{:S(2)}, u32[]{:S(2)}) %collective-permute-start.3) | collective-permute-done | bytes 327712 | tf_op jit(solution)/shard_map/ppermute | solution.py:348
  15.1 0.4 collective-permute-start.4
  15.5 2.7 %shard_map.84.near_ref = f32[256,512]{1,0:T(8,128)S(1)} custom-call(bf16[256,4096]{1,0:T(8,128)(2,1)S(1)} %get-tuple-element.22.rows_in_ref.refs_0_, bf16[4096,1024]{1,0:T(8,128)(2,1)} %weight_ref.3), custom_call_target="tpu_custom_call" | custom-call | bytes 4194304 | tf_op jit(solution)/shard_map/pallas_call | solution.py:221
  18.3 0.0 collective-permute-done.1.refs_5_.refs_2_
  18.3 1.6 %collective-permute-start.2 = (bf16[64,2560]{1,0:T(8,128)(2,1)S(1)}, bf16[64,2560]{1,0:T(8,128)(2,1)S(1)}, u32[]{:S(2)}, u32[]{:S(2)}) collective-permute-start(bf16[64,2560]{1,0:T(8,128)(2,1)S(1)} %collective-permute-done.1.refs_5_.refs_2_), channel_id=1, source_target_pairs={{2,0},{1,3},{6,2},{3,7},{10,6},{7,11},{14,10},{11,15},{12,14},{15,... | collective-permute-start | bytes 983048 | tf_op jit(solution)/shard_map/ppermute | solution.py:348
  19.9 5.8 %collective-permute-done.4.refs_6_.refs_3_ = bf16[64,2560]{1,0:T(8,128)(2,1)S(1)} collective-permute-done((bf16[64,2560]{1,0:T(8,128)(2,1)S(1)}, bf16[64,2560]{1,0:T(8,128)(2,1)S(1)}, u32[]{:S(2)}, u32[]{:S(2)}) %collective-permute-start.4) | collective-permute-done | bytes 327712 | tf_op jit(solution)/shard_map/ppermute | solution.py:348
  25.7 0.3 collective-permute-start.5
  26.0 1.1 %collective-permute-done.2.refs_3_.refs_4_ = bf16[64,2560]{1,0:T(8,128)(2,1)S(1)} collective-permute-done((bf16[64,2560]{1,0:T(8,128)(2,1)S(1)}, bf16[64,2560]{1,0:T(8,128)(2,1)S(1)}, u32[]{:S(2)}, u32[]{:S(2)}) %collective-permute-start.2) | collective-permute-done | bytes 327712 | tf_op jit(solution)/shard_map/ppermute | solution.py:348
  27.0 2.3 %collective-permute-start.6 = (bf16[64,2560]{1,0:T(8,128)(2,1)S(1)}, bf16[64,2560]{1,0:T(8,128)(2,1)S(1)}, u32[]{:S(2)}, u32[]{:S(2)}) collective-permute-start(bf16[64,2560]{1,0:T(8,128)(2,1)S(1)} %collective-permute-done.2.refs_3_.refs_4_), channel_id=1, source_target_pairs={{2,0},{1,3},{6,2},{3,7},{10,6},{7,11},{14,10},{11,15},{12,14},{15,... | collective-permute-start | bytes 983048 | tf_op jit(solution)/shard_map/ppermute | solution.py:348
  29.4 6.0 %collective-permute-done.5.refs_4_.refs_5_ = bf16[64,2560]{1,0:T(8,128)(2,1)S(1)} collective-permute-done((bf16[64,2560]{1,0:T(8,128)(2,1)S(1)}, bf16[64,2560]{1,0:T(8,128)(2,1)S(1)}, u32[]{:S(2)}, u32[]{:S(2)}) %collective-permute-start.5) | collective-permute-done | bytes 327712 | tf_op jit(solution)/shard_map/ppermute | solution.py:348
  35.4 0.3 collective-permute-start.7
  35.7 0.0 collective-permute-done.refs_1_
  35.7 0.8 %shard_map.85 = (f32[256,128]{1,0:T(8,128)S(1)}, f32[256,128]{1,0:T(8,128)S(1)}) custom-call(bf16[256,4096]{1,0:T(8,128)(2,1)S(1)} %get-tuple-element.22.rows_in_ref.refs_0_, bf16[4112,128]{1,0:T(8,128)(2,1)S(1)} %collective-permute-done.refs_1_, s32[8,512]{1,0:T(8,128)S(1)} %get-tuple-element.21.refs_2_.bounds_ref, ...), custom_call_target="tpu_custom_call" | custom-call | flops 8589934592 | bytes 16777216 | tf_op jit(solution)/shard_map/pallas_call | solution.py:299
  36.5 0.1 collective-permute-start.11
  36.5 0.0 collective-permute-done.6.refs_5_.refs_6_
  36.6 5.9 %collective-permute-done.7.refs_6_.refs_7_ = bf16[64,2560]{1,0:T(8,128)(2,1)S(1)} collective-permute-done((bf16[64,2560]{1,0:T(8,128)(2,1)S(1)}, bf16[64,2560]{1,0:T(8,128)(2,1)S(1)}, u32[]{:S(2)}, u32[]{:S(2)}) %collective-permute-start.7) | collective-permute-done | bytes 327712 | tf_op jit(solution)/shard_map/ppermute | solution.py:348
  42.5 0.9 %shard_map.86 = (f32[128,128]{1,0:T(8,128)S(1)}, f32[128,128]{1,0:T(8,128)S(1)}) custom-call(bf16[256,4096]{1,0:T(8,128)(2,1)S(1)} %get-tuple-element.22.rows_in_ref.refs_0_, bf16[4112,128]{1,0:T(8,128)(2,1)S(1)} %collective-permute-done.refs_1_, s32[8,512]{1,0:T(8,128)S(1)} %get-tuple-element.21.refs_2_.bounds_ref, ...), custom_call_target="tpu_custom_call" | custom-call | flops 8589934592 | bytes 16777216 | tf_op jit(solution)/shard_map/pallas_call | solution.py:299
  43.3 0.4 collective-permute-start.9
  43.7 0.0 collective-permute-start.8
  43.7 3.9 %collective-permute-done.9.two = f32[128,128]{1,0:T(8,128)S(1)} collective-permute-done((f32[128,128]{1,0:T(8,128)S(1)}, f32[128,128]{1,0:T(8,128)S(1)}, u32[]{:S(2)}, u32[]{:S(2)}) %collective-permute-start.9) | collective-permute-done | bytes 65568 | tf_op jit(solution)/shard_map/ppermute | solution.py:391
  47.7 0.0 collective-permute-start.10
  47.7 0.0 collective-permute-done.8.one
  47.7 1.2 %collective-permute-done.10.three = f32[128,128]{1,0:T(8,128)S(1)} collective-permute-done((f32[128,128]{1,0:T(8,128)S(1)}, f32[128,128]{1,0:T(8,128)S(1)}, u32[]{:S(2)}, u32[]{:S(2)}) %collective-permute-start.10) | collective-permute-done | bytes 65568 | tf_op jit(solution)/shard_map/ppermute | solution.py:393
  48.9 0.0 collective-permute-done.11.far_ref
  48.9 1.1 %shard_map.87 = bf16[256,512]{1,0:T(8,128)(2,1)} custom-call(s32[8,512]{1,0:T(8,128)S(1)} %get-tuple-element.21.refs_2_.bounds_ref, f32[128,128]{1,0:T(8,128)S(1)} %get-tuple-element.33.mine, f32[128,128]{1,0:T(8,128)S(1)} %collective-permute-done.8.one, f32[128,128]{1,0:T(8,128)S(1)} %collective-permute-done.9.two, ...), custom_call_target="tpu_custom_call" | custom-call | tf_op jit(solution)/shard_map/pallas_call | solution.py:396
Async XLA Ops:
  1.6 34.1 %collective-permute-start = (bf16[4112,128]{1,0:T(8,128)(2,1)S(1)}, bf16[4112,128]{1,0:T(8,128)(2,1)S(1)}, u32[]{:S(2)}, u32[]{:S(2)}) collective-permute-start(bf16[4112,128]{1,0:T(8,128)(2,1)S(1)} %get-tuple-element.23), channel_id=1, source_target_pairs={{0,16},{16,0},{1,17},{17,1},{2,18},{18,2},{3,19},{19,3},{4,20},{20... | collective-permute-start | bytes 3158024 | tf_op jit(solution)/shard_map/ppermute | solution.py:381
  4.6 10.5 %collective-permute-start.3 = (bf16[64,2560]{1,0:T(8,128)(2,1)S(1)}, bf16[64,2560]{1,0:T(8,128)(2,1)S(1)}, u32[]{:S(2)}, u32[]{:S(2)}) collective-permute-start(bf16[64,2560]{1,0:T(8,128)(2,1)S(1)} %get-tuple-element.24.refs_3_.refs_0_), channel_id=1, source_target_pairs={{0,2},{3,1},{2,6},{7,3},{6,10},{11,7},{10,14},{15,11},{14,12},{13,... | collective-permute-start | bytes 983048 | tf_op jit(solution)/shard_map/ppermute | solution.py:348
  6.1 12.1 %collective-permute-start.1 = (bf16[64,2560]{1,0:T(8,128)(2,1)S(1)}, bf16[64,2560]{1,0:T(8,128)(2,1)S(1)}, u32[]{:S(2)}, u32[]{:S(2)}) collective-permute-start(bf16[64,2560]{1,0:T(8,128)(2,1)S(1)} %get-tuple-element.24.refs_3_.refs_0_), channel_id=1, source_target_pairs={{2,0},{1,3},{6,2},{3,7},{10,6},{7,11},{14,10},{11,15},{12,14},{15,... | collective-permute-start | bytes 983048 | tf_op jit(solution)/shard_map/ppermute | solution.py:348
  15.1 10.6 %collective-permute-start.4 = (bf16[64,2560]{1,0:T(8,128)(2,1)S(1)}, bf16[64,2560]{1,0:T(8,128)(2,1)S(1)}, u32[]{:S(2)}, u32[]{:S(2)}) collective-permute-start(bf16[64,2560]{1,0:T(8,128)(2,1)S(1)} %collective-permute-done.3.refs_4_.refs_1_), channel_id=1, source_target_pairs={{0,2},{3,1},{2,6},{7,3},{6,10},{11,7},{10,14},{15,11},{14,12},{13,... | collective-permute-start | bytes 983048 | tf_op jit(solution)/shard_map/ppermute | solution.py:348
  18.3 8.8 %collective-permute-start.2 = (bf16[64,2560]{1,0:T(8,128)(2,1)S(1)}, bf16[64,2560]{1,0:T(8,128)(2,1)S(1)}, u32[]{:S(2)}, u32[]{:S(2)}) collective-permute-start(bf16[64,2560]{1,0:T(8,128)(2,1)S(1)} %collective-permute-done.1.refs_5_.refs_2_), channel_id=1, source_target_pairs={{2,0},{1,3},{6,2},{3,7},{10,6},{7,11},{14,10},{11,15},{12,14},{15,... | collective-permute-start | bytes 983048 | tf_op jit(solution)/shard_map/ppermute | solution.py:348
  25.7 9.7 %collective-permute-start.5 = (bf16[64,2560]{1,0:T(8,128)(2,1)S(1)}, bf16[64,2560]{1,0:T(8,128)(2,1)S(1)}, u32[]{:S(2)}, u32[]{:S(2)}) collective-permute-start(bf16[64,2560]{1,0:T(8,128)(2,1)S(1)} %collective-permute-done.4.refs_6_.refs_3_), channel_id=1, source_target_pairs={{0,2},{3,1},{2,6},{7,3},{6,10},{11,7},{10,14},{15,11},{14,12},{13,... | collective-permute-start | bytes 983048 | tf_op jit(solution)/shard_map/ppermute | solution.py:348
  27.0 9.5 %collective-permute-start.6 = (bf16[64,2560]{1,0:T(8,128)(2,1)S(1)}, bf16[64,2560]{1,0:T(8,128)(2,1)S(1)}, u32[]{:S(2)}, u32[]{:S(2)}) collective-permute-start(bf16[64,2560]{1,0:T(8,128)(2,1)S(1)} %collective-permute-done.2.refs_3_.refs_4_), channel_id=1, source_target_pairs={{2,0},{1,3},{6,2},{3,7},{10,6},{7,11},{14,10},{11,15},{12,14},{15,... | collective-permute-start | bytes 983048 | tf_op jit(solution)/shard_map/ppermute | solution.py:348
  35.4 7.1 %collective-permute-start.7 = (bf16[64,2560]{1,0:T(8,128)(2,1)S(1)}, bf16[64,2560]{1,0:T(8,128)(2,1)S(1)}, u32[]{:S(2)}, u32[]{:S(2)}) collective-permute-start(bf16[64,2560]{1,0:T(8,128)(2,1)S(1)} %collective-permute-done.5.refs_4_.refs_5_), channel_id=1, source_target_pairs={{0,2},{3,1},{2,6},{7,3},{6,10},{11,7},{10,14},{15,11},{14,12},{13,... | collective-permute-start | bytes 983048 | tf_op jit(solution)/shard_map/ppermute | solution.py:348
  36.5 12.5 %collective-permute-start.11 = (f32[256,512]{1,0:T(8,128)S(1)}, f32[256,512]{1,0:T(8,128)S(1)}, u32[]{:S(2)}, u32[]{:S(2)}) collective-permute-start(f32[256,512]{1,0:T(8,128)S(1)} %get-tuple-element.36), channel_id=1, source_target_pairs={{0,1},{1,0},{2,3},{3,2},{4,5},{5,4},{6,7},{7,6},{8,9},{9,8},{10,11... | collective-permute-start | bytes 1572872 | tf_op jit(solution)/shard_map/ppermute | solution.py:388
  43.3 4.3 %collective-permute-start.9 = (f32[128,128]{1,0:T(8,128)S(1)}, f32[128,128]{1,0:T(8,128)S(1)}, u32[]{:S(2)}, u32[]{:S(2)}) collective-permute-start(f32[128,128]{1,0:T(8,128)S(1)} %get-tuple-element.34), channel_id=1, source_target_pairs={{0,16},{16,0},{1,17},{17,1},{2,18},{18,2},{3,19},{19,3},{4,20},{20... | collective-permute-start | bytes 196616 | tf_op jit(solution)/shard_map/ppermute | solution.py:391
  43.7 3.9 %collective-permute-start.8 = (f32[128,128]{1,0:T(8,128)S(1)}, f32[128,128]{1,0:T(8,128)S(1)}, u32[]{:S(2)}, u32[]{:S(2)}) collective-permute-start(f32[128,128]{1,0:T(8,128)S(1)} %get-tuple-element.33.mine), channel_id=1, source_target_pairs={{0,1},{1,0},{2,3},{3,2},{4,5},{5,4},{6,7},{7,6},{8,9},{9,8},{10,11... | collective-permute-start | bytes 196616 | tf_op jit(solution)/shard_map/ppermute | solution.py:392
  47.7 1.3 %collective-permute-start.10 = (f32[128,128]{1,0:T(8,128)S(1)}, f32[128,128]{1,0:T(8,128)S(1)}, u32[]{:S(2)}, u32[]{:S(2)}) collective-permute-start(f32[128,128]{1,0:T(8,128)S(1)} %collective-permute-done.9.two), channel_id=1, source_target_pairs={{0,1},{1,0},{2,3},{3,2},{4,5},{5,4},{6,7},{7,6},{8,9},{9,8},{10,11... | collective-permute-start | bytes 196616 | tf_op jit(solution)/shard_map/ppermute | solution.py:393

commit v8 on v6

--- a/solution.py
+++ b/solution.py
@@ -180,61 +180,40 @@
     )(*map(in_hbm, (hidden, factor, factor_out, demand, lengths, holder_slot, slots)))
 
 
-def base_kernel(side, fetch_rows, rows_in_ref, weight_ref, out_ref, *rest):
-    rows_ref = rest[0] if fetch_rows else rows_in_ref
-    buffer, sems = rest[-2:]
-    width = out_ref.shape[1]
+def mark_kernel(bounds_ref, out_ref):
+    out_ref[...] = bounds_ref[...]
+
+
+def mark(bounds):
+    return pl.pallas_call(
+        mark_kernel,
+        out_shape=jax.ShapeDtypeStruct(bounds.shape, bounds.dtype),
+        in_specs=[VMEM],
+        out_specs=VMEM,
+        cost_estimate=LONG,
+    )(bounds)
+
+
+def base_kernel(rows_ref, weight_ref, near_ref, far_ref):
+    width = near_ref.shape[1]
     core = lax.axis_index("tensor")
-    offset = pl.multiple_of((core if side == 0 else 1 - core) * width, 128)
-    steps, step = buffer.shape[:2]
-    copies = []
-    for k in range(steps):
-        span = pl.ds(k * step, step)
-        need = [
-            pltpu.make_async_copy(
-                weight_ref.at[span, pl.ds(offset, width)], buffer.at[k], sems.at[0, k]
-            )
-        ]
-        if fetch_rows:
-            need.append(
-                pltpu.make_async_copy(
-                    rows_in_ref.at[:, span], rows_ref.at[:, span], sems.at[1, k]
-                )
-            )
-        copies.append(need)
-    for need in copies:
-        for copy in need:
-            copy.start()
-    for k, need in enumerate(copies):
-        for copy in need:
-            copy.wait()
-        rows = rows_ref[:, k * step : (k + 1) * step]
-        part = jnp.dot(rows, buffer[k], preferred_element_type=F32)
-        if k == 0:
-            out_ref[...] = part
-        else:
-            out_ref[...] += part
-
-
-def base_call(side, fetch_rows, rows, weight):
-    count, depth = rows.shape
-    width = weight.shape[1] // 2
-    steps = 4
-    out = (jax.ShapeDtypeStruct((count, width), F32),)
-    if fetch_rows:
-        out += (jax.ShapeDtypeStruct(rows.shape, rows.dtype),)
+    for out_ref, side in ((near_ref, core), (far_ref, 1 - core)):
+        columns = pl.ds(pl.multiple_of(side * width, 128), width)
+        out_ref[...] = jnp.dot(
+            rows_ref[...], weight_ref[:, columns], preferred_element_type=F32
+        )
+
+
+def base_call(rows, weight):
+    out = jax.ShapeDtypeStruct((rows.shape[0], weight.shape[1] // 2), F32)
     return pl.pallas_call(
-        functools.partial(base_kernel, side, fetch_rows),
-        out_shape=out,
-        in_specs=[HBM if fetch_rows else VMEM, HBM],
-        out_specs=(VMEM,) * len(out),
-        scratch_shapes=[
-            pltpu.VMEM((steps, depth // steps, width), weight.dtype),
-            pltpu.SemaphoreType.DMA((2, steps)),
-        ],
+        base_kernel,
+        out_shape=(out, out),
+        in_specs=[VMEM] * 2,
+        out_specs=(VMEM,) * 2,
         compiler_params=params(),
         cost_estimate=HALF,
-    )(in_hbm(rows) if fetch_rows else rows, in_hbm(weight))
+    )(rows, weight)
 
 
 def group_mask(low, high, shape):
@@ -367,7 +346,9 @@
         jnp.asarray(table, I32),
     )
 
-    far, held = base_call(1, True, hidden, value_weight)
+    bounds, first, second = lax.optimization_barrier((mark(bounds), first, second))
+
+    near, far = base_call(hidden, value_weight)
     firsts, seconds = [first], [second]
     ahead, behind = (first, second), (first, second)
     for step in range(1, full + 1):
@@ -380,11 +361,9 @@
         ahead, behind = (a, b), (c, d)
         firsts += [a, c]
         seconds += [b, d]
-    rows_near, a, d = lax.optimization_barrier((held, ahead[0], behind[1]))
-    firsts.append(lax.ppermute(a, "batch", forward))
-    seconds.append(lax.ppermute(d, "batch", backward))
+    firsts.append(lax.ppermute(ahead[0], "batch", forward))
+    seconds.append(lax.ppermute(behind[1], "batch", backward))
     other = lax.ppermute(to_other, "groups", swap)
-    (near,) = base_call(0, False, rows_near, value_weight)
 
     count = owners // GROUP
     early = range(count - 1)
@@ -392,9 +371,9 @@
     for group in early:
         pieces += firsts[group * GROUP : (group + 1) * GROUP]
         pieces += seconds[group * GROUP : (group + 1) * GROUP]
-    sides = (held, other, bounds)
+    sides = (hidden, other, bounds)
     starts = rank_call(tuple(early), depth, *sides, pieces, None)
-    *starts, far, near = lax.optimization_barrier((*starts, far, near))
+    *starts, far = lax.optimization_barrier((*starts, far))
     far = lax.ppermute(far, "tensor", swap)
     pieces = firsts[-GROUP:] + seconds[-GROUP:]
     mine, theirs = rank_call((count - 1,), depth, *sides, pieces, starts)

time: 42 us -> 46.4 us (1.10)
  local copies, waits for them, and re-layouts: 0 us -> 3.99 us
  waiting for transfers between devices: 13.5 us -> 15.1 us
  Pallas kernels: 10.4 us -> 9.21 us
    unnamed x0 -> x8, local copies, waits for them, and re-layouts: none -> 3.99 us
    ppermute x3, waiting for transfers between devices: 0.01 us -> 3.9 us  [per_device(): b = lax.ppermute(ahead[1], 'batch', forward)]
    ppermute x3, waiting for transfers between devices: 2.97 us -> 0.01 us  [per_device(): c = lax.ppermute(behind[0], 'batch', backward)]
    ppermute x3, starting transfers between devices: 1.59 us -> 3.82 us  [per_device(): d = lax.ppermute(behind[1], 'batch', backward)]
    pallas_call x2, Pallas kernels: 5.98 us -> 3.81 us  [the longest x1 2.35 us: base_call(): pl.pallas_call(base_kernel, out_shape=(out, out), in_specs=[VMEM] * 2, ou...]
    ppermute x3, starting transfers between devices: 4.48 us -> 2.31 us  [per_device(): a = lax.ppermute(ahead[0], 'batch', forward)]
    ppermute x2, waiting for transfers between devices: 1.25 us -> 2.92 us  [the longest x1 1.55 us: per_device(): firsts.append(lax.ppermute(ahead[0], 'batch', forward))]
    ppermute x3, waiting for transfers between devices: 4.24 us -> 3.2 us  [per_device(): d = lax.ppermute(behind[1], 'batch', backward)]
  transfers between devices with their start and end apart: 19 -> 19, of which waited for: 8 -> 8; matrix products, arithmetic and copies ran while one was open for 0% -> 0% of each run, Pallas kernels for 18% -> 12%
where the time goes in v8:
time: 46.4 us; the launch traced here: 46.2 us
  starting transfers between devices  17.8 us (38%)
  waiting for transfers between devices  15.1 us (33%)
  Pallas kernels  9.21 us (20%)
  local copies, waits for them, and re-layouts  3.99 us (9%)
    unnamed x8, local copies, waits for them, and re-layouts  3.99 us
    ppermute x3, waiting for transfers between devices, per_device(): b = lax.ppermute(ahead[1], 'batch', forward)  3.9 us
    ppermute x3, starting transfers between devices, per_device(): d = lax.ppermute(behind[1], 'batch', backward)  3.82 us
    ppermute x1, waiting for transfers between devices, per_device(): two = lax.ppermute(theirs, 'groups', swap)  3.73 us
    ppermute x3, starting transfers between devices, per_device(): b = lax.ppermute(ahead[1], 'batch', forward)  3.45 us
    ppermute x3, waiting for transfers between devices, per_device(): d = lax.ppermute(behind[1], 'batch', backward)  3.2 us
    ppermute x1, starting transfers between devices, per_device(): other = lax.ppermute(to_other, 'groups', swap)  2.97 us
    ppermute x3, starting transfers between devices, per_device(): c = lax.ppermute(behind[0], 'batch', backward)  2.63 us
  transfers between devices with their start and end apart: 19, of which 8 were waited for; matrix products, arithmetic and copies ran while one was open for 0% of the time, Pallas kernels for 12%

profile of v8, /device:TPU:0, one launch (start us, length us, event | category | flops | bytes accessed | tf_op | source)
XLA Modules:
  0.0 46.2 jit_solution(3637179845191963817)
XLA Ops:
  0.0 2.6 %shard_map.82 = (bf16[4112,128]{1,0:T(8,128)(2,1)}, bf16[64,1280]{1,0:T(8,128)(2,1)S(1)}, bf16[64,1280]{1,0:T(8,128)(2,1)S(1)}, s32[8,512]{1,0:T(8,128)S(1)}) custom-call(bf16[256,4096]{1,0:T(8,128)(2,1)} %refs_0_.3, bf16[64,4096]{1,0:T(8,128)(2,1)} %bitcast.4, bf16[64,512]{1,0:T(8,128)(2,1)} %bitcast.5, s32[1,4]{1,0:T(1,128)} %demand_ref.1, ...), custom_call_target="tpu_custom_call" | custom-call | tf_op jit(solution)/shard_map/pallas_call | solution.py:161
  2.6 0.0 copy-start.3
  2.6 0.6 %copy-done.3 = s32[8,512]{1,0:T(8,128)} copy-done((s32[8,512]{1,0:T(8,128)}, s32[8,512]{1,0:T(8,128)S(1)}, u32[]{:S(2)}) %copy-start.3) | copy-done | bytes 16408
  3.2 3.0 %collective-permute-start = (bf16[4112,128]{1,0:T(8,128)(2,1)}, bf16[4112,128]{1,0:T(8,128)(2,1)S(1)}, u32[]{:S(2)}, u32[]{:S(2)}) collective-permute-start(bf16[4112,128]{1,0:T(8,128)(2,1)} %get-tuple-element.27), channel_id=1, source_target_pairs={{0,16},{16,0},{1,17},{17,1},{2,18},{18,2},{3,19},{19,3},{4,20},{20... | collective-permute-start | bytes 3158024 | tf_op jit(solution)/shard_map/ppermute | solution.py:366
  6.2 1.5 %shard_map.83.refs_2_.bounds_ref = s32[8,512]{1,0:T(8,128)} custom-call(s32[8,512]{1,0:T(8,128)} %copy-done.3), custom_call_target="tpu_custom_call" | custom-call | flops 8589934592 | bytes 16777216 | tf_op jit(solution)/shard_map/pallas_call | solution.py:188
  7.7 1.5 %collective-permute-start.3 = (bf16[64,1280]{1,0:T(8,128)(2,1)S(1)}, bf16[64,1280]{1,0:T(8,128)(2,1)S(1)}, u32[]{:S(2)}, u32[]{:S(2)}) collective-permute-start(bf16[64,1280]{1,0:T(8,128)(2,1)S(1)} %get-tuple-element.28.refs_3_), channel_id=1, source_target_pairs={{0,2},{2,6},{6,10},{10,14},{14,12},{12,8},{8,4},{4,0},{1,3},{3,7},... | collective-permute-start | bytes 491528 | tf_op jit(solution)/shard_map/ppermute | solution.py:355
  9.2 0.5 %collective-permute-start.8 = (bf16[64,1280]{1,0:T(8,128)(2,1)S(1)}, bf16[64,1280]{1,0:T(8,128)(2,1)S(1)}, u32[]{:S(2)}, u32[]{:S(2)}) collective-permute-start(bf16[64,1280]{1,0:T(8,128)(2,1)S(1)} %get-tuple-element.31.refs_7_.refs_0_), channel_id=1, source_target_pairs={{2,0},{6,2},{10,6},{14,10},{12,14},{8,12},{4,8},{0,4},{3,1},{7,3},... | collective-permute-start | bytes 491528 | tf_op jit(solution)/shard_map/ppermute | solution.py:356
  9.7 1.5 %collective-permute-start.10 = (bf16[64,1280]{1,0:T(8,128)(2,1)S(1)}, bf16[64,1280]{1,0:T(8,128)(2,1)S(1)}, u32[]{:S(2)}, u32[]{:S(2)}) collective-permute-start(bf16[64,1280]{1,0:T(8,128)(2,1)S(1)} %get-tuple-element.31.refs_7_.refs_0_), channel_id=1, source_target_pairs={{0,2},{2,6},{6,10},{10,14},{14,12},{12,8},{8,4},{4,0},{1,3},{3,7},... | collective-permute-start | bytes 491528 | tf_op jit(solution)/shard_map/ppermute | solution.py:357
  11.2 0.5 %collective-permute-start.1 = (bf16[64,1280]{1,0:T(8,128)(2,1)S(1)}, bf16[64,1280]{1,0:T(8,128)(2,1)S(1)}, u32[]{:S(2)}, u32[]{:S(2)}) collective-permute-start(bf16[64,1280]{1,0:T(8,128)(2,1)S(1)} %get-tuple-element.28.refs_3_), channel_id=1, source_target_pairs={{2,0},{6,2},{10,6},{14,10},{12,14},{8,12},{4,8},{0,4},{3,1},{7,3},... | collective-permute-start | bytes 491528 | tf_op jit(solution)/shard_map/ppermute | solution.py:358
  11.7 0.0 copy-done.1
  11.7 3.4 %copy-done = bf16[4096,1024]{1,0:T(8,128)(2,1)S(1)} copy-done((bf16[4096,1024]{1,0:T(8,128)(2,1)S(1)}, bf16[4096,1024]{1,0:T(8,128)(2,1)}, u32[]{:S(2)}) %copy-start) | copy-done | bytes 8388632
  15.1 2.3 %shard_map.84 = (f32[256,512]{1,0:T(8,128)S(1)}, f32[256,512]{1,0:T(8,128)S(1)}) custom-call(bf16[256,4096]{1,0:T(8,128)(2,1)S(1)} %copy-done.1, bf16[4096,1024]{1,0:T(8,128)(2,1)S(1)} %copy-done), custom_call_target="tpu_custom_call" | custom-call | bytes 4194304 | tf_op jit(solution)/shard_map/pallas_call | solution.py:209
  17.5 0.0 collective-permute-done.3.refs_4_
  17.5 0.0 collective-permute-done.8.refs_9_.refs_2_
  17.5 1.6 %collective-permute-start.9 = (bf16[64,1280]{1,0:T(8,128)(2,1)S(1)}, bf16[64,1280]{1,0:T(8,128)(2,1)S(1)}, u32[]{:S(2)}, u32[]{:S(2)}) collective-permute-start(bf16[64,1280]{1,0:T(8,128)(2,1)S(1)} %collective-permute-done.8.refs_9_.refs_2_), channel_id=1, source_target_pairs={{2,0},{6,2},{10,6},{14,10},{12,14},{8,12},{4,8},{0,4},{3,1},{7,3},... | collective-permute-start | bytes 491528 | tf_op jit(solution)/shard_map/ppermute | solution.py:356
  19.1 0.4 collective-permute-start.4
  19.6 0.0 collective-permute-done.10.refs_8_.refs_1_
  19.6 1.5 %collective-permute-start.11 = (bf16[64,1280]{1,0:T(8,128)(2,1)S(1)}, bf16[64,1280]{1,0:T(8,128)(2,1)S(1)}, u32[]{:S(2)}, u32[]{:S(2)}) collective-permute-start(bf16[64,1280]{1,0:T(8,128)(2,1)S(1)} %collective-permute-done.10.refs_8_.refs_1_), channel_id=1, source_target_pairs={{0,2},{2,6},{6,10},{10,14},{14,12},{12,8},{8,4},{4,0},{1,3},{3,7},... | collective-permute-start | bytes 491528 | tf_op jit(solution)/shard_map/ppermute | solution.py:357
  21.1 0.0 collective-permute-done.1.refs_5_
  21.1 0.5 %collective-permute-start.2 = (bf16[64,1280]{1,0:T(8,128)(2,1)S(1)}, bf16[64,1280]{1,0:T(8,128)(2,1)S(1)}, u32[]{:S(2)}, u32[]{:S(2)}) collective-permute-start(bf16[64,1280]{1,0:T(8,128)(2,1)S(1)} %collective-permute-done.1.refs_5_), channel_id=1, source_target_pairs={{2,0},{6,2},{10,6},{14,10},{12,14},{8,12},{4,8},{0,4},{3,1},{7,3},... | collective-permute-start | bytes 491528 | tf_op jit(solution)/shard_map/ppermute | solution.py:358
  21.6 2.9 %collective-permute-done.9.refs_7_.refs_4_ = bf16[64,1280]{1,0:T(8,128)(2,1)S(1)} collective-permute-done((bf16[64,1280]{1,0:T(8,128)(2,1)S(1)}, bf16[64,1280]{1,0:T(8,128)(2,1)S(1)}, u32[]{:S(2)}, u32[]{:S(2)}) %collective-permute-start.9) | collective-permute-done | bytes 163872 | tf_op jit(solution)/shard_map/ppermute | solution.py:356
  24.5 1.7 %collective-permute-start.13 = (bf16[64,1280]{1,0:T(8,128)(2,1)S(1)}, bf16[64,1280]{1,0:T(8,128)(2,1)S(1)}, u32[]{:S(2)}, u32[]{:S(2)}) collective-permute-start(bf16[64,1280]{1,0:T(8,128)(2,1)S(1)} %collective-permute-done.9.refs_7_.refs_4_), channel_id=1, source_target_pairs={{2,0},{6,2},{10,6},{14,10},{12,14},{8,12},{4,8},{0,4},{3,1},{7,3},... | collective-permute-start | bytes 491528 | tf_op jit(solution)/shard_map/ppermute | solution.py:356
  26.1 0.0 collective-permute-done.4.refs_6_
  26.1 0.4 collective-permute-start.5
  26.5 2.9 %collective-permute-done.11.refs_10_.refs_3_ = bf16[64,1280]{1,0:T(8,128)(2,1)S(1)} collective-permute-done((bf16[64,1280]{1,0:T(8,128)(2,1)S(1)}, bf16[64,1280]{1,0:T(8,128)(2,1)S(1)}, u32[]{:S(2)}, u32[]{:S(2)}) %collective-permute-start.11) | collective-permute-done | bytes 163872 | tf_op jit(solution)/shard_map/ppermute | solution.py:357
  29.3 0.5 %collective-permute-start.12 = (bf16[64,1280]{1,0:T(8,128)(2,1)S(1)}, bf16[64,1280]{1,0:T(8,128)(2,1)S(1)}, u32[]{:S(2)}, u32[]{:S(2)}) collective-permute-start(bf16[64,1280]{1,0:T(8,128)(2,1)S(1)} %collective-permute-done.11.refs_10_.refs_3_), channel_id=1, source_target_pairs={{0,2},{2,6},{6,10},{10,14},{14,12},{12,8},{8,4},{4,0},{1,3},{3,7},... | collective-permute-start | bytes 491528 | tf_op jit(solution)/shard_map/ppermute | solution.py:357
  29.8 0.0 collective-permute-done.2.refs_3_
  29.8 1.6 %collective-permute-start.6 = (bf16[64,1280]{1,0:T(8,128)(2,1)S(1)}, bf16[64,1280]{1,0:T(8,128)(2,1)S(1)}, u32[]{:S(2)}, u32[]{:S(2)}) collective-permute-start(bf16[64,1280]{1,0:T(8,128)(2,1)S(1)} %collective-permute-done.2.refs_3_), channel_id=1, source_target_pairs={{2,0},{6,2},{10,6},{14,10},{12,14},{8,12},{4,8},{0,4},{3,1},{7,3},... | collective-permute-start | bytes 491528 | tf_op jit(solution)/shard_map/ppermute | solution.py:358
  31.4 0.3 collective-permute-done.13.refs_9_.refs_6_
  31.7 1.5 %collective-permute-start.14 = (bf16[64,1280]{1,0:T(8,128)(2,1)S(1)}, bf16[64,1280]{1,0:T(8,128)(2,1)S(1)}, u32[]{:S(2)}, u32[]{:S(2)}) collective-permute-start(bf16[64,1280]{1,0:T(8,128)(2,1)S(1)} %collective-permute-done.13.refs_9_.refs_6_), channel_id=1, source_target_pairs={{2,0},{6,2},{10,6},{14,10},{12,14},{8,12},{4,8},{0,4},{3,1},{7,3},... | collective-permute-start | bytes 491528 | tf_op jit(solution)/shard_map/ppermute | solution.py:365
  33.2 0.0 collective-permute-done.5.refs_4_
  33.3 0.5 %collective-permute-start.7 = (bf16[64,1280]{1,0:T(8,128)(2,1)S(1)}, bf16[64,1280]{1,0:T(8,128)(2,1)S(1)}, u32[]{:S(2)}, u32[]{:S(2)}) collective-permute-start(bf16[64,1280]{1,0:T(8,128)(2,1)S(1)} %collective-permute-done.5.refs_4_), channel_id=1, source_target_pairs={{0,2},{2,6},{6,10},{10,14},{14,12},{12,8},{8,4},{4,0},{1,3},{3,7},... | collective-permute-start | bytes 491528 | tf_op jit(solution)/shard_map/ppermute | solution.py:364
  33.7 0.0 collective-permute-done.refs_1_
  33.7 0.8 %shard_map.85 = (f32[256,128]{1,0:T(8,128)S(1)}, f32[256,128]{1,0:T(8,128)S(1)}) custom-call(bf16[256,4096]{1,0:T(8,128)(2,1)S(1)} %copy-done.1, bf16[4112,128]{1,0:T(8,128)(2,1)S(1)} %collective-permute-done.refs_1_, s32[8,512]{1,0:T(8,128)S(1)} %copy-done.2, bf16[64,1280]{1,0:T(8,128)(2,1)S(1)} %get-tuple-element.28.refs_3_, ...), custom_call_target="tpu_custom_call" | custom-call | flops 8589934592 | bytes 16777216 | tf_op jit(solution)/shard_map/pallas_call | solution.py:286
  34.5 0.1 collective-permute-start.18
  34.6 1.0 %collective-permute-done.12.refs_8_.refs_5_ = bf16[64,1280]{1,0:T(8,128)(2,1)S(1)} collective-permute-done((bf16[64,1280]{1,0:T(8,128)(2,1)S(1)}, bf16[64,1280]{1,0:T(8,128)(2,1)S(1)}, u32[]{:S(2)}, u32[]{:S(2)}) %collective-permute-start.12) | collective-permute-done | bytes 163872 | tf_op jit(solution)/shard_map/ppermute | solution.py:357
  35.7 0.0 collective-permute-done.6.refs_5_
  35.7 1.4 %collective-permute-done.14.refs_10_.refs_7_ = bf16[64,1280]{1,0:T(8,128)(2,1)S(1)} collective-permute-done((bf16[64,1280]{1,0:T(8,128)(2,1)S(1)}, bf16[64,1280]{1,0:T(8,128)(2,1)S(1)}, u32[]{:S(2)}, u32[]{:S(2)}) %collective-permute-start.14) | collective-permute-done | bytes 163872 | tf_op jit(solution)/shard_map/ppermute | solution.py:365
  37.0 1.5 %collective-permute-done.7.refs_6_ = bf16[64,1280]{1,0:T(8,128)(2,1)S(1)} collective-permute-done((bf16[64,1280]{1,0:T(8,128)(2,1)S(1)}, bf16[64,1280]{1,0:T(8,128)(2,1)S(1)}, u32[]{:S(2)}, u32[]{:S(2)}) %collective-permute-start.7) | collective-permute-done | bytes 163872 | tf_op jit(solution)/shard_map/ppermute | solution.py:364
  38.6 0.9 %shard_map.86 = (f32[128,128]{1,0:T(8,128)S(1)}, f32[128,128]{1,0:T(8,128)S(1)}) custom-call(bf16[256,4096]{1,0:T(8,128)(2,1)S(1)} %copy-done.1, bf16[4112,128]{1,0:T(8,128)(2,1)S(1)} %collective-permute-done.refs_1_, s32[8,512]{1,0:T(8,128)S(1)} %copy-done.2, bf16[64,1280]{1,0:T(8,128)(2,1)S(1)} %collective-permute-done.2.refs_3_, ...), custom_call_target="tpu_custom_call" | custom-call | flops 8589934592 | bytes 16777216 | tf_op jit(solution)/shard_map/pallas_call | solution.py:286
  39.4 0.6 %collective-permute-start.16 = (f32[128,128]{1,0:T(8,128)S(1)}, f32[128,128]{1,0:T(8,128)S(1)}, u32[]{:S(2)}, u32[]{:S(2)}) collective-permute-start(f32[128,128]{1,0:T(8,128)S(1)} %get-tuple-element.38), channel_id=1, source_target_pairs={{0,16},{16,0},{1,17},{17,1},{2,18},{18,2},{3,19},{19,3},{4,20},{20... | collective-permute-start | bytes 196616 | tf_op jit(solution)/shard_map/ppermute | solution.py:381
  40.0 0.0 collective-permute-start.15
  40.0 3.7 %collective-permute-done.16.two = f32[128,128]{1,0:T(8,128)S(1)} collective-permute-done((f32[128,128]{1,0:T(8,128)S(1)}, f32[128,128]{1,0:T(8,128)S(1)}, u32[]{:S(2)}, u32[]{:S(2)}) %collective-permute-start.16) | collective-permute-done | bytes 65568 | tf_op jit(solution)/shard_map/ppermute | solution.py:381
  43.8 0.0 collective-permute-start.17
  43.8 0.0 collective-permute-done.15.one
  43.8 1.2 %collective-permute-done.17.three = f32[128,128]{1,0:T(8,128)S(1)} collective-permute-done((f32[128,128]{1,0:T(8,128)S(1)}, f32[128,128]{1,0:T(8,128)S(1)}, u32[]{:S(2)}, u32[]{:S(2)}) %collective-permute-start.17) | collective-permute-done | bytes 65568 | tf_op jit(solution)/shard_map/ppermute | solution.py:383
  45.0 0.0 collective-permute-done.18.far_ref
  45.0 1.1 %shard_map.87 = bf16[256,512]{1,0:T(8,128)(2,1)} custom-call(s32[8,512]{1,0:T(8,128)S(1)} %copy-done.2, f32[128,128]{1,0:T(8,128)S(1)} %get-tuple-element.37.mine, f32[128,128]{1,0:T(8,128)S(1)} %collective-permute-done.15.one, f32[128,128]{1,0:T(8,128)S(1)} %collective-permute-done.16.two, f32[128,128]{1,0:T(8,128)S(1)} %collective-permute-done.17.three, ...), custom_call_target="tpu_custom_call" | custom-call | tf_op jit(solution)/shard_map/pallas_call | solution.py:386
  (4 shorter events, 0.0 us)
Async XLA Ops:
  2.6 0.6 %copy-start.3 = (s32[8,512]{1,0:T(8,128)}, s32[8,512]{1,0:T(8,128)S(1)}, u32[]{:S(2)}) copy-start(s32[8,512]{1,0:T(8,128)S(1)} %get-tuple-element.23.bounds_ref) | copy-start | bytes 49156
  3.2 30.5 %collective-permute-start = (bf16[4112,128]{1,0:T(8,128)(2,1)}, bf16[4112,128]{1,0:T(8,128)(2,1)S(1)}, u32[]{:S(2)}, u32[]{:S(2)}) collective-permute-start(bf16[4112,128]{1,0:T(8,128)(2,1)} %get-tuple-element.27), channel_id=1, source_target_pairs={{0,16},{16,0},{1,17},{17,1},{2,18},{18,2},{3,19},{19,3},{4,20},{20... | collective-permute-start | bytes 3158024 | tf_op jit(solution)/shard_map/ppermute | solution.py:366
  6.2 5.5 %copy-start.1 = (bf16[256,4096]{1,0:T(8,128)(2,1)S(1)}, bf16[256,4096]{1,0:T(8,128)(2,1)}, u32[]{:S(2)}) copy-start(bf16[256,4096]{1,0:T(8,128)(2,1)} %refs_0_.3) | copy-start | bytes 6291460
  7.7 9.8 %collective-permute-start.3 = (bf16[64,1280]{1,0:T(8,128)(2,1)S(1)}, bf16[64,1280]{1,0:T(8,128)(2,1)S(1)}, u32[]{:S(2)}, u32[]{:S(2)}) collective-permute-start(bf16[64,1280]{1,0:T(8,128)(2,1)S(1)} %get-tuple-element.28.refs_3_), channel_id=1, source_target_pairs={{0,2},{2,6},{6,10},{10,14},{14,12},{12,8},{8,4},{4,0},{1,3},{3,7},... | collective-permute-start | bytes 491528 | tf_op jit(solution)/shard_map/ppermute | solution.py:355
  9.2 8.3 %collective-permute-start.8 = (bf16[64,1280]{1,0:T(8,128)(2,1)S(1)}, bf16[64,1280]{1,0:T(8,128)(2,1)S(1)}, u32[]{:S(2)}, u32[]{:S(2)}) collective-permute-start(bf16[64,1280]{1,0:T(8,128)(2,1)S(1)} %get-tuple-element.31.refs_7_.refs_0_), channel_id=1, source_target_pairs={{2,0},{6,2},{10,6},{14,10},{12,14},{8,12},{4,8},{0,4},{3,1},{7,3},... | collective-permute-start | bytes 491528 | tf_op jit(solution)/shard_map/ppermute | solution.py:356
  9.7 9.9 %collective-permute-start.10 = (bf16[64,1280]{1,0:T(8,128)(2,1)S(1)}, bf16[64,1280]{1,0:T(8,128)(2,1)S(1)}, u32[]{:S(2)}, u32[]{:S(2)}) collective-permute-start(bf16[64,1280]{1,0:T(8,128)(2,1)S(1)} %get-tuple-element.31.refs_7_.refs_0_), channel_id=1, source_target_pairs={{0,2},{2,6},{6,10},{10,14},{14,12},{12,8},{8,4},{4,0},{1,3},{3,7},... | collective-permute-start | bytes 491528 | tf_op jit(solution)/shard_map/ppermute | solution.py:357
  11.2 9.9 %collective-permute-start.1 = (bf16[64,1280]{1,0:T(8,128)(2,1)S(1)}, bf16[64,1280]{1,0:T(8,128)(2,1)S(1)}, u32[]{:S(2)}, u32[]{:S(2)}) collective-permute-start(bf16[64,1280]{1,0:T(8,128)(2,1)S(1)} %get-tuple-element.28.refs_3_), channel_id=1, source_target_pairs={{2,0},{6,2},{10,6},{14,10},{12,14},{8,12},{4,8},{0,4},{3,1},{7,3},... | collective-permute-start | bytes 491528 | tf_op jit(solution)/shard_map/ppermute | solution.py:358
  11.7 3.4 %copy-start = (bf16[4096,1024]{1,0:T(8,128)(2,1)S(1)}, bf16[4096,1024]{1,0:T(8,128)(2,1)}, u32[]{:S(2)}) copy-start(bf16[4096,1024]{1,0:T(8,128)(2,1)} %weight_ref.1) | copy-start | bytes 25165828
  15.1 18.6 %copy-start.2 = (s32[8,512]{1,0:T(8,128)S(1)}, s32[8,512]{1,0:T(8,128)}, u32[]{:S(2)}) copy-start(s32[8,512]{1,0:T(8,128)} %shard_map.83.refs_2_.bounds_ref) | copy-start | bytes 49156
  17.5 7.0 %collective-permute-start.9 = (bf16[64,1280]{1,0:T(8,128)(2,1)S(1)}, bf16[64,1280]{1,0:T(8,128)(2,1)S(1)}, u32[]{:S(2)}, u32[]{:S(2)}) collective-permute-start(bf16[64,1280]{1,0:T(8,128)(2,1)S(1)} %collective-permute-done.8.refs_9_.refs_2_), channel_id=1, source_target_pairs={{2,0},{6,2},{10,6},{14,10},{12,14},{8,12},{4,8},{0,4},{3,1},{7,3},... | collective-permute-start | bytes 491528 | tf_op jit(solution)/shard_map/ppermute | solution.py:356
  19.1 7.0 %collective-permute-start.4 = (bf16[64,1280]{1,0:T(8,128)(2,1)S(1)}, bf16[64,1280]{1,0:T(8,128)(2,1)S(1)}, u32[]{:S(2)}, u32[]{:S(2)}) collective-permute-start(bf16[64,1280]{1,0:T(8,128)(2,1)S(1)} %collective-permute-done.3.refs_4_), channel_id=1, source_target_pairs={{0,2},{2,6},{6,10},{10,14},{14,12},{12,8},{8,4},{4,0},{1,3},{3,7},... | collective-permute-start | bytes 491528 | tf_op jit(solution)/shard_map/ppermute | solution.py:355
  19.6 9.8 %collective-permute-start.11 = (bf16[64,1280]{1,0:T(8,128)(2,1)S(1)}, bf16[64,1280]{1,0:T(8,128)(2,1)S(1)}, u32[]{:S(2)}, u32[]{:S(2)}) collective-permute-start(bf16[64,1280]{1,0:T(8,128)(2,1)S(1)} %collective-permute-done.10.refs_8_.refs_1_), channel_id=1, source_target_pairs={{0,2},{2,6},{6,10},{10,14},{14,12},{12,8},{8,4},{4,0},{1,3},{3,7},... | collective-permute-start | bytes 491528 | tf_op jit(solution)/shard_map/ppermute | solution.py:357
  21.1 8.8 %collective-permute-start.2 = (bf16[64,1280]{1,0:T(8,128)(2,1)S(1)}, bf16[64,1280]{1,0:T(8,128)(2,1)S(1)}, u32[]{:S(2)}, u32[]{:S(2)}) collective-permute-start(bf16[64,1280]{1,0:T(8,128)(2,1)S(1)} %collective-permute-done.1.refs_5_), channel_id=1, source_target_pairs={{2,0},{6,2},{10,6},{14,10},{12,14},{8,12},{4,8},{0,4},{3,1},{7,3},... | collective-permute-start | bytes 491528 | tf_op jit(solution)/shard_map/ppermute | solution.py:358
  24.5 7.2 %collective-permute-start.13 = (bf16[64,1280]{1,0:T(8,128)(2,1)S(1)}, bf16[64,1280]{1,0:T(8,128)(2,1)S(1)}, u32[]{:S(2)}, u32[]{:S(2)}) collective-permute-start(bf16[64,1280]{1,0:T(8,128)(2,1)S(1)} %collective-permute-done.9.refs_7_.refs_4_), channel_id=1, source_target_pairs={{2,0},{6,2},{10,6},{14,10},{12,14},{8,12},{4,8},{0,4},{3,1},{7,3},... | collective-permute-start | bytes 491528 | tf_op jit(solution)/shard_map/ppermute | solution.py:356
  26.1 7.1 %collective-permute-start.5 = (bf16[64,1280]{1,0:T(8,128)(2,1)S(1)}, bf16[64,1280]{1,0:T(8,128)(2,1)S(1)}, u32[]{:S(2)}, u32[]{:S(2)}) collective-permute-start(bf16[64,1280]{1,0:T(8,128)(2,1)S(1)} %collective-permute-done.4.refs_6_), channel_id=1, source_target_pairs={{0,2},{2,6},{6,10},{10,14},{14,12},{12,8},{8,4},{4,0},{1,3},{3,7},... | collective-permute-start | bytes 491528 | tf_op jit(solution)/shard_map/ppermute | solution.py:355
  29.3 6.3 %collective-permute-start.12 = (bf16[64,1280]{1,0:T(8,128)(2,1)S(1)}, bf16[64,1280]{1,0:T(8,128)(2,1)S(1)}, u32[]{:S(2)}, u32[]{:S(2)}) collective-permute-start(bf16[64,1280]{1,0:T(8,128)(2,1)S(1)} %collective-permute-done.11.refs_10_.refs_3_), channel_id=1, source_target_pairs={{0,2},{2,6},{6,10},{10,14},{14,12},{12,8},{8,4},{4,0},{1,3},{3,7},... | collective-permute-start | bytes 491528 | tf_op jit(solution)/shard_map/ppermute | solution.py:357
  29.8 5.8 %collective-permute-start.6 = (bf16[64,1280]{1,0:T(8,128)(2,1)S(1)}, bf16[64,1280]{1,0:T(8,128)(2,1)S(1)}, u32[]{:S(2)}, u32[]{:S(2)}) collective-permute-start(bf16[64,1280]{1,0:T(8,128)(2,1)S(1)} %collective-permute-done.2.refs_3_), channel_id=1, source_target_pairs={{2,0},{6,2},{10,6},{14,10},{12,14},{8,12},{4,8},{0,4},{3,1},{7,3},... | collective-permute-start | bytes 491528 | tf_op jit(solution)/shard_map/ppermute | solution.py:358
  31.7 5.3 %collective-permute-start.14 = (bf16[64,1280]{1,0:T(8,128)(2,1)S(1)}, bf16[64,1280]{1,0:T(8,128)(2,1)S(1)}, u32[]{:S(2)}, u32[]{:S(2)}) collective-permute-start(bf16[64,1280]{1,0:T(8,128)(2,1)S(1)} %collective-permute-done.13.refs_9_.refs_6_), channel_id=1, source_target_pairs={{2,0},{6,2},{10,6},{14,10},{12,14},{8,12},{4,8},{0,4},{3,1},{7,3},... | collective-permute-start | bytes 491528 | tf_op jit(solution)/shard_map/ppermute | solution.py:365
  33.3 5.3 %collective-permute-start.7 = (bf16[64,1280]{1,0:T(8,128)(2,1)S(1)}, bf16[64,1280]{1,0:T(8,128)(2,1)S(1)}, u32[]{:S(2)}, u32[]{:S(2)}) collective-permute-start(bf16[64,1280]{1,0:T(8,128)(2,1)S(1)} %collective-permute-done.5.refs_4_), channel_id=1, source_target_pairs={{0,2},{2,6},{6,10},{10,14},{14,12},{12,8},{8,4},{4,0},{1,3},{3,7},... | collective-permute-start | bytes 491528 | tf_op jit(solution)/shard_map/ppermute | solution.py:364
  34.5 10.5 %collective-permute-start.18 = (f32[256,512]{1,0:T(8,128)S(1)}, f32[256,512]{1,0:T(8,128)S(1)}, u32[]{:S(2)}, u32[]{:S(2)}) collective-permute-start(f32[256,512]{1,0:T(8,128)S(1)} %get-tuple-element.40), channel_id=1, source_target_pairs={{0,1},{1,0},{2,3},{3,2},{4,5},{5,4},{6,7},{7,6},{8,9},{9,8},{10,11... | collective-permute-start | bytes 1572872 | tf_op jit(solution)/shard_map/ppermute | solution.py:377
  39.4 4.3 %collective-permute-start.16 = (f32[128,128]{1,0:T(8,128)S(1)}, f32[128,128]{1,0:T(8,128)S(1)}, u32[]{:S(2)}, u32[]{:S(2)}) collective-permute-start(f32[128,128]{1,0:T(8,128)S(1)} %get-tuple-element.38), channel_id=1, source_target_pairs={{0,16},{16,0},{1,17},{17,1},{2,18},{18,2},{3,19},{19,3},{4,20},{20... | collective-permute-start | bytes 196616 | tf_op jit(solution)/shard_map/ppermute | solution.py:381
  40.0 3.7 %collective-permute-start.15 = (f32[128,128]{1,0:T(8,128)S(1)}, f32[128,128]{1,0:T(8,128)S(1)}, u32[]{:S(2)}, u32[]{:S(2)}) collective-permute-start(f32[128,128]{1,0:T(8,128)S(1)} %get-tuple-element.37.mine), channel_id=1, source_target_pairs={{0,1},{1,0},{2,3},{3,2},{4,5},{5,4},{6,7},{7,6},{8,9},{9,8},{10,11... | collective-permute-start | bytes 196616 | tf_op jit(solution)/shard_map/ppermute | solution.py:382
  43.8 1.3 %collective-permute-start.17 = (f32[128,128]{1,0:T(8,128)S(1)}, f32[128,128]{1,0:T(8,128)S(1)}, u32[]{:S(2)}, u32[]{:S(2)}) collective-permute-start(f32[128,128]{1,0:T(8,128)S(1)} %collective-permute-done.16.two), channel_id=1, source_target_pairs={{0,1},{1,0},{2,3},{3,2},{4,5},{5,4},{6,7},{7,6},{8,9},{9,8},{10,11... | collective-permute-start | bytes 196616 | tf_op jit(solution)/shard_map/ppermute | solution.py:383

commit v9 on v8

--- a/solution.py
+++ b/solution.py
@@ -8,7 +8,7 @@
 from jax.sharding import PartitionSpec as P
 
 F32, BF16, I32 = jnp.float32, jnp.bfloat16, jnp.int32
-VMEM_LIMIT = 40 * 1024 * 1024
+VMEM_LIMIT = 24 * 1024 * 1024
 HALF = pl.CostEstimate(flops=0, bytes_accessed=1 << 22, transcendentals=0)
 LONG = pl.CostEstimate(flops=1 << 33, bytes_accessed=1 << 24, transcendentals=0)
 GROUP = 4
@@ -190,6 +190,7 @@
         out_shape=jax.ShapeDtypeStruct(bounds.shape, bounds.dtype),
         in_specs=[VMEM],
         out_specs=VMEM,
+        compiler_params=params(),
         cost_estimate=LONG,
     )(bounds)
 

time: 46.4 us -> 41.2 us (0.89)
  local copies, waits for them, and re-layouts: 3.99 us -> 0.01 us
  Pallas kernels: 9.21 us -> 6.74 us
  waiting for transfers between devices: 15.1 us -> 16.4 us
    unnamed x8 -> x6, local copies, waits for them, and re-layouts: 3.99 us -> 0.01 us
    ppermute x3, waiting for transfers between devices: 3.2 us -> 6.83 us  [per_device(): d = lax.ppermute(behind[1], 'batch', backward)]
    ppermute x3, waiting for transfers between devices: 3.9 us -> 0.81 us  [per_device(): b = lax.ppermute(ahead[1], 'batch', forward)]
    ppermute x3, starting transfers between devices: 2.31 us -> 4.54 us  [per_device(): a = lax.ppermute(ahead[0], 'batch', forward)]
    ppermute x3, starting transfers between devices: 3.82 us -> 1.59 us  [per_device(): d = lax.ppermute(behind[1], 'batch', backward)]
    pallas_call x1, Pallas kernels: 1.47 us -> 0.01 us  [mark(): pl.pallas_call(mark_kernel, out_shape=jax.ShapeDtypeStruct(bounds.shape,...]
    pallas_call x1, Pallas kernels: 2.61 us -> 1.59 us  [prologue(): pl.pallas_call(functools.partial(prologue_kernel, depth, rank), out_shape...]
    ppermute x1, starting transfers between devices: 0.48 us -> 1.48 us  [per_device(): firsts.append(lax.ppermute(ahead[0], 'batch', forward))]
  transfers between devices with their start and end apart: 19 -> 19, of which waited for: 8 -> 10; matrix products, arithmetic and copies ran while one was open for 0% -> 0% of each run, Pallas kernels for 12% -> 10%
where the time goes in v9:
time: 41.2 us; the launch traced here: 41.1 us
  starting transfers between devices  17.8 us (43%)
  waiting for transfers between devices  16.4 us (40%)
  Pallas kernels  6.74 us (16%)
    ppermute x3, waiting for transfers between devices, per_device(): d = lax.ppermute(behind[1], 'batch', backward)  6.83 us
    ppermute x3, starting transfers between devices, per_device(): a = lax.ppermute(ahead[0], 'batch', forward)  4.54 us
    ppermute x3, starting transfers between devices, per_device(): b = lax.ppermute(ahead[1], 'batch', forward)  3.84 us
    ppermute x1, waiting for transfers between devices, per_device(): two = lax.ppermute(theirs, 'groups', swap)  3.84 us
    ppermute x1, starting transfers between devices, per_device(): other = lax.ppermute(to_other, 'groups', swap)  3.03 us
    pallas_call x1, Pallas kernels, base_call(): pl.pallas_call(base_kernel, out_shape=(out, out), in_specs=[VMEM] * 2, ou...  2.35 us
    ppermute x3, starting transfers between devices, per_device(): c = lax.ppermute(behind[0], 'batch', backward)  2.24 us
    ppermute x1, waiting for transfers between devices, per_device(): seconds.append(lax.ppermute(behind[1], 'batch', backward))  2.03 us
  transfers between devices with their start and end apart: 19, of which 10 were waited for; matrix products, arithmetic and copies ran while one was open for 0% of the time, Pallas kernels for 10%

profile of v9, /device:TPU:0, one launch (start us, length us, event | category | flops | bytes accessed | tf_op | source)
XLA Modules:
  0.0 41.1 jit_solution(14863335714396615438)
XLA Ops:
  0.0 1.6 %shard_map.82 = (bf16[4112,128]{1,0:T(8,128)(2,1)S(1)}, bf16[64,1280]{1,0:T(8,128)(2,1)S(1)}, bf16[64,1280]{1,0:T(8,128)(2,1)S(1)}, s32[8,512]{1,0:T(8,128)S(1)}) custom-call(bf16[256,4096]{1,0:T(8,128)(2,1)} %refs_0_.3, bf16[64,4096]{1,0:T(8,128)(2,1)} %bitcast.6, bf16[64,512]{1,0:T(8,128)(2,1)} %bitcast.7, s32[1,4]{1,0:T(1,128)} %demand_ref.1, ...), custom_call_target="tpu_custom_call" | custom-call | tf_op jit(solution)/shard_map/pallas_call | solution.py:161
  1.6 3.0 %collective-permute-start = (bf16[4112,128]{1,0:T(8,128)(2,1)S(1)}, bf16[4112,128]{1,0:T(8,128)(2,1)S(1)}, u32[]{:S(2)}, u32[]{:S(2)}) collective-permute-start(bf16[4112,128]{1,0:T(8,128)(2,1)S(1)} %get-tuple-element.27), channel_id=1, source_target_pairs={{0,16},{16,0},{1,17},{17,1},{2,18},{18,2},{3,19},{19,3},{4,20},{20... | collective-permute-start | bytes 3158024 | tf_op jit(solution)/shard_map/ppermute | solution.py:367
  4.6 0.0 slice-start
  4.6 0.0 slice-start.1
  4.6 1.5 %collective-permute-start.3 = (bf16[64,1280]{1,0:T(8,128)(2,1)S(1)}, bf16[64,1280]{1,0:T(8,128)(2,1)S(1)}, u32[]{:S(2)}, u32[]{:S(2)}) collective-permute-start(bf16[64,1280]{1,0:T(8,128)(2,1)S(1)} %get-tuple-element.28.refs_3_), channel_id=1, source_target_pairs={{0,2},{2,6},{6,10},{10,14},{14,12},{12,8},{8,4},{4,0},{1,3},{3,7},... | collective-permute-start | bytes 491528 | tf_op jit(solution)/shard_map/ppermute | solution.py:356
  6.2 0.5 %collective-permute-start.8 = (bf16[64,1280]{1,0:T(8,128)(2,1)S(1)}, bf16[64,1280]{1,0:T(8,128)(2,1)S(1)}, u32[]{:S(2)}, u32[]{:S(2)}) collective-permute-start(bf16[64,1280]{1,0:T(8,128)(2,1)S(1)} %get-tuple-element.31.refs_7_.refs_0_), channel_id=1, source_target_pairs={{2,0},{6,2},{10,6},{14,10},{12,14},{8,12},{4,8},{0,4},{3,1},{7,3},... | collective-permute-start | bytes 491528 | tf_op jit(solution)/shard_map/ppermute | solution.py:357
  6.7 1.5 %collective-permute-start.10 = (bf16[64,1280]{1,0:T(8,128)(2,1)S(1)}, bf16[64,1280]{1,0:T(8,128)(2,1)S(1)}, u32[]{:S(2)}, u32[]{:S(2)}) collective-permute-start(bf16[64,1280]{1,0:T(8,128)(2,1)S(1)} %get-tuple-element.31.refs_7_.refs_0_), channel_id=1, source_target_pairs={{0,2},{2,6},{6,10},{10,14},{14,12},{12,8},{8,4},{4,0},{1,3},{3,7},... | collective-permute-start | bytes 491528 | tf_op jit(solution)/shard_map/ppermute | solution.py:358
  8.2 0.5 %collective-permute-start.1 = (bf16[64,1280]{1,0:T(8,128)(2,1)S(1)}, bf16[64,1280]{1,0:T(8,128)(2,1)S(1)}, u32[]{:S(2)}, u32[]{:S(2)}) collective-permute-start(bf16[64,1280]{1,0:T(8,128)(2,1)S(1)} %get-tuple-element.28.refs_3_), channel_id=1, source_target_pairs={{2,0},{6,2},{10,6},{14,10},{12,14},{8,12},{4,8},{0,4},{3,1},{7,3},... | collective-permute-start | bytes 491528 | tf_op jit(solution)/shard_map/ppermute | solution.py:359
  8.8 0.0 slice-done
  8.8 0.0 slice-done.1
  8.8 0.0 copy-done
  8.8 2.4 %shard_map.84 = (f32[256,512]{1,0:T(8,128)S(1)}, f32[256,512]{1,0:T(8,128)S(1)}) custom-call(bf16[256,4096]{1,0:T(8,128)(2,1)S(1)} %copy-done, bf16[4096,1024]{1,0:T(8,128)(2,1)S(1)} %bitcast.5), custom_call_target="tpu_custom_call" | custom-call | bytes 4194304 | tf_op jit(solution)/shard_map/pallas_call | solution.py:210
  11.1 0.7 %collective-permute-done.3.refs_4_ = bf16[64,1280]{1,0:T(8,128)(2,1)S(1)} collective-permute-done((bf16[64,1280]{1,0:T(8,128)(2,1)S(1)}, bf16[64,1280]{1,0:T(8,128)(2,1)S(1)}, u32[]{:S(2)}, u32[]{:S(2)}) %collective-permute-start.3) | collective-permute-done | bytes 163872 | tf_op jit(solution)/shard_map/ppermute | solution.py:356
  11.8 1.5 %collective-permute-done.8.refs_9_.refs_2_ = bf16[64,1280]{1,0:T(8,128)(2,1)S(1)} collective-permute-done((bf16[64,1280]{1,0:T(8,128)(2,1)S(1)}, bf16[64,1280]{1,0:T(8,128)(2,1)S(1)}, u32[]{:S(2)}, u32[]{:S(2)}) %collective-permute-start.8) | collective-permute-done | bytes 163872 | tf_op jit(solution)/shard_map/ppermute | solution.py:357
  13.3 0.5 %collective-permute-start.9 = (bf16[64,1280]{1,0:T(8,128)(2,1)S(1)}, bf16[64,1280]{1,0:T(8,128)(2,1)S(1)}, u32[]{:S(2)}, u32[]{:S(2)}) collective-permute-start(bf16[64,1280]{1,0:T(8,128)(2,1)S(1)} %collective-permute-done.8.refs_9_.refs_2_), channel_id=1, source_target_pairs={{2,0},{6,2},{10,6},{14,10},{12,14},{8,12},{4,8},{0,4},{3,1},{7,3},... | collective-permute-start | bytes 491528 | tf_op jit(solution)/shard_map/ppermute | solution.py:357
  13.9 1.5 %collective-permute-start.4 = (bf16[64,1280]{1,0:T(8,128)(2,1)S(1)}, bf16[64,1280]{1,0:T(8,128)(2,1)S(1)}, u32[]{:S(2)}, u32[]{:S(2)}) collective-permute-start(bf16[64,1280]{1,0:T(8,128)(2,1)S(1)} %collective-permute-done.3.refs_4_), channel_id=1, source_target_pairs={{0,2},{2,6},{6,10},{10,14},{14,12},{12,8},{8,4},{4,0},{1,3},{3,7},... | collective-permute-start | bytes 491528 | tf_op jit(solution)/shard_map/ppermute | solution.py:356
  15.4 0.0 collective-permute-done.10.refs_8_.refs_1_
  15.4 1.6 %collective-permute-start.11 = (bf16[64,1280]{1,0:T(8,128)(2,1)S(1)}, bf16[64,1280]{1,0:T(8,128)(2,1)S(1)}, u32[]{:S(2)}, u32[]{:S(2)}) collective-permute-start(bf16[64,1280]{1,0:T(8,128)(2,1)S(1)} %collective-permute-done.10.refs_8_.refs_1_), channel_id=1, source_target_pairs={{0,2},{2,6},{6,10},{10,14},{14,12},{12,8},{8,4},{4,0},{1,3},{3,7},... | collective-permute-start | bytes 491528 | tf_op jit(solution)/shard_map/ppermute | solution.py:358
  16.9 0.0 collective-permute-done.1.refs_5_
  16.9 0.5 %collective-permute-start.2 = (bf16[64,1280]{1,0:T(8,128)(2,1)S(1)}, bf16[64,1280]{1,0:T(8,128)(2,1)S(1)}, u32[]{:S(2)}, u32[]{:S(2)}) collective-permute-start(bf16[64,1280]{1,0:T(8,128)(2,1)S(1)} %collective-permute-done.1.refs_5_), channel_id=1, source_target_pairs={{2,0},{6,2},{10,6},{14,10},{12,14},{8,12},{4,8},{0,4},{3,1},{7,3},... | collective-permute-start | bytes 491528 | tf_op jit(solution)/shard_map/ppermute | solution.py:359
  17.4 3.1 %collective-permute-done.9.refs_7_.refs_4_ = bf16[64,1280]{1,0:T(8,128)(2,1)S(1)} collective-permute-done((bf16[64,1280]{1,0:T(8,128)(2,1)S(1)}, bf16[64,1280]{1,0:T(8,128)(2,1)S(1)}, u32[]{:S(2)}, u32[]{:S(2)}) %collective-permute-start.9) | collective-permute-done | bytes 163872 | tf_op jit(solution)/shard_map/ppermute | solution.py:357
  20.5 0.5 %collective-permute-start.13 = (bf16[64,1280]{1,0:T(8,128)(2,1)S(1)}, bf16[64,1280]{1,0:T(8,128)(2,1)S(1)}, u32[]{:S(2)}, u32[]{:S(2)}) collective-permute-start(bf16[64,1280]{1,0:T(8,128)(2,1)S(1)} %collective-permute-done.9.refs_7_.refs_4_), channel_id=1, source_target_pairs={{2,0},{6,2},{10,6},{14,10},{12,14},{8,12},{4,8},{0,4},{3,1},{7,3},... | collective-permute-start | bytes 491528 | tf_op jit(solution)/shard_map/ppermute | solution.py:357
  21.0 0.0 collective-permute-done.4.refs_6_
  21.0 1.5 %collective-permute-start.5 = (bf16[64,1280]{1,0:T(8,128)(2,1)S(1)}, bf16[64,1280]{1,0:T(8,128)(2,1)S(1)}, u32[]{:S(2)}, u32[]{:S(2)}) collective-permute-start(bf16[64,1280]{1,0:T(8,128)(2,1)S(1)} %collective-permute-done.4.refs_6_), channel_id=1, source_target_pairs={{0,2},{2,6},{6,10},{10,14},{14,12},{12,8},{8,4},{4,0},{1,3},{3,7},... | collective-permute-start | bytes 491528 | tf_op jit(solution)/shard_map/ppermute | solution.py:356
  22.5 0.8 %collective-permute-done.11.refs_10_.refs_3_ = bf16[64,1280]{1,0:T(8,128)(2,1)S(1)} collective-permute-done((bf16[64,1280]{1,0:T(8,128)(2,1)S(1)}, bf16[64,1280]{1,0:T(8,128)(2,1)S(1)}, u32[]{:S(2)}, u32[]{:S(2)}) %collective-permute-start.11) | collective-permute-done | bytes 163872 | tf_op jit(solution)/shard_map/ppermute | solution.py:358
  23.3 0.8 %collective-permute-start.12 = (bf16[64,1280]{1,0:T(8,128)(2,1)S(1)}, bf16[64,1280]{1,0:T(8,128)(2,1)S(1)}, u32[]{:S(2)}, u32[]{:S(2)}) collective-permute-start(bf16[64,1280]{1,0:T(8,128)(2,1)S(1)} %collective-permute-done.11.refs_10_.refs_3_), channel_id=1, source_target_pairs={{0,2},{2,6},{6,10},{10,14},{14,12},{12,8},{8,4},{4,0},{1,3},{3,7},... | collective-permute-start | bytes 491528 | tf_op jit(solution)/shard_map/ppermute | solution.py:358
  24.1 0.0 collective-permute-done.2.refs_3_
  24.1 1.3 %collective-permute-start.6 = (bf16[64,1280]{1,0:T(8,128)(2,1)S(1)}, bf16[64,1280]{1,0:T(8,128)(2,1)S(1)}, u32[]{:S(2)}, u32[]{:S(2)}) collective-permute-start(bf16[64,1280]{1,0:T(8,128)(2,1)S(1)} %collective-permute-done.2.refs_3_), channel_id=1, source_target_pairs={{2,0},{6,2},{10,6},{14,10},{12,14},{8,12},{4,8},{0,4},{3,1},{7,3},... | collective-permute-start | bytes 491528 | tf_op jit(solution)/shard_map/ppermute | solution.py:359
  25.3 2.3 %collective-permute-done.13.refs_9_.refs_6_ = bf16[64,1280]{1,0:T(8,128)(2,1)S(1)} collective-permute-done((bf16[64,1280]{1,0:T(8,128)(2,1)S(1)}, bf16[64,1280]{1,0:T(8,128)(2,1)S(1)}, u32[]{:S(2)}, u32[]{:S(2)}) %collective-permute-start.13) | collective-permute-done | bytes 163872 | tf_op jit(solution)/shard_map/ppermute | solution.py:357
  27.6 0.5 %collective-permute-start.14 = (bf16[64,1280]{1,0:T(8,128)(2,1)S(1)}, bf16[64,1280]{1,0:T(8,128)(2,1)S(1)}, u32[]{:S(2)}, u32[]{:S(2)}) collective-permute-start(bf16[64,1280]{1,0:T(8,128)(2,1)S(1)} %collective-permute-done.13.refs_9_.refs_6_), channel_id=1, source_target_pairs={{2,0},{6,2},{10,6},{14,10},{12,14},{8,12},{4,8},{0,4},{3,1},{7,3},... | collective-permute-start | bytes 491528 | tf_op jit(solution)/shard_map/ppermute | solution.py:366
  28.1 0.0 collective-permute-done.5.refs_4_
  28.1 1.5 %collective-permute-start.7 = (bf16[64,1280]{1,0:T(8,128)(2,1)S(1)}, bf16[64,1280]{1,0:T(8,128)(2,1)S(1)}, u32[]{:S(2)}, u32[]{:S(2)}) collective-permute-start(bf16[64,1280]{1,0:T(8,128)(2,1)S(1)} %collective-permute-done.5.refs_4_), channel_id=1, source_target_pairs={{0,2},{2,6},{6,10},{10,14},{14,12},{12,8},{8,4},{4,0},{1,3},{3,7},... | collective-permute-start | bytes 491528 | tf_op jit(solution)/shard_map/ppermute | solution.py:365
  29.6 0.0 collective-permute-done.refs_1_
  29.6 0.8 %shard_map.85 = (f32[256,128]{1,0:T(8,128)S(1)}, f32[256,128]{1,0:T(8,128)S(1)}) custom-call(bf16[256,4096]{1,0:T(8,128)(2,1)S(1)} %copy-done, bf16[4112,128]{1,0:T(8,128)(2,1)S(1)} %collective-permute-done.refs_1_, s32[8,512]{1,0:T(8,128)S(1)} %shard_map.83.refs_2_.bounds_ref, bf16[64,1280]{1,0:T(8,128)(2,1)S(1)} %get-tuple-element.28.refs_3_, ...), custom_call_target="tpu_custom_call" | custom-call | flops 8589934592 | bytes 16777216 | tf_op jit(solution)/shard_map/pallas_call | solution.py:287
  30.4 0.1 collective-permute-start.18
  30.5 0.0 collective-permute-done.12.refs_8_.refs_5_
  30.5 0.4 collective-permute-done.6.refs_5_
  30.9 2.0 %collective-permute-done.14.refs_10_.refs_7_ = bf16[64,1280]{1,0:T(8,128)(2,1)S(1)} collective-permute-done((bf16[64,1280]{1,0:T(8,128)(2,1)S(1)}, bf16[64,1280]{1,0:T(8,128)(2,1)S(1)}, u32[]{:S(2)}, u32[]{:S(2)}) %collective-permute-start.14) | collective-permute-done | bytes 163872 | tf_op jit(solution)/shard_map/ppermute | solution.py:366
  32.9 0.5 %collective-permute-done.7.refs_6_ = bf16[64,1280]{1,0:T(8,128)(2,1)S(1)} collective-permute-done((bf16[64,1280]{1,0:T(8,128)(2,1)S(1)}, bf16[64,1280]{1,0:T(8,128)(2,1)S(1)}, u32[]{:S(2)}, u32[]{:S(2)}) %collective-permute-start.7) | collective-permute-done | bytes 163872 | tf_op jit(solution)/shard_map/ppermute | solution.py:365
  33.5 0.9 %shard_map.86 = (f32[128,128]{1,0:T(8,128)S(1)}, f32[128,128]{1,0:T(8,128)S(1)}) custom-call(bf16[256,4096]{1,0:T(8,128)(2,1)S(1)} %copy-done, bf16[4112,128]{1,0:T(8,128)(2,1)S(1)} %collective-permute-done.refs_1_, s32[8,512]{1,0:T(8,128)S(1)} %shard_map.83.refs_2_.bounds_ref, bf16[64,1280]{1,0:T(8,128)(2,1)S(1)} %collective-permute-done.2.refs_3_, ...), custom_call_target="tpu_custom_call" | custom-call | flops 8589934592 | bytes 16777216 | tf_op jit(solution)/shard_map/pallas_call | solution.py:287
  34.3 0.5 %collective-permute-start.16 = (f32[128,128]{1,0:T(8,128)S(1)}, f32[128,128]{1,0:T(8,128)S(1)}, u32[]{:S(2)}, u32[]{:S(2)}) collective-permute-start(f32[128,128]{1,0:T(8,128)S(1)} %get-tuple-element.38), channel_id=1, source_target_pairs={{0,16},{16,0},{1,17},{17,1},{2,18},{18,2},{3,19},{19,3},{4,20},{20... | collective-permute-start | bytes 196616 | tf_op jit(solution)/shard_map/ppermute | solution.py:382
  34.8 0.0 collective-permute-start.15
  34.8 3.8 %collective-permute-done.16.two = f32[128,128]{1,0:T(8,128)S(1)} collective-permute-done((f32[128,128]{1,0:T(8,128)S(1)}, f32[128,128]{1,0:T(8,128)S(1)}, u32[]{:S(2)}, u32[]{:S(2)}) %collective-permute-start.16) | collective-permute-done | bytes 65568 | tf_op jit(solution)/shard_map/ppermute | solution.py:382
  38.7 0.0 collective-permute-start.17
  38.7 0.0 collective-permute-done.15.one
  38.7 1.2 %collective-permute-done.17.three = f32[128,128]{1,0:T(8,128)S(1)} collective-permute-done((f32[128,128]{1,0:T(8,128)S(1)}, f32[128,128]{1,0:T(8,128)S(1)}, u32[]{:S(2)}, u32[]{:S(2)}) %collective-permute-start.17) | collective-permute-done | bytes 65568 | tf_op jit(solution)/shard_map/ppermute | solution.py:384
  39.9 0.0 collective-permute-done.18.far_ref
  39.9 1.1 %shard_map.87 = bf16[256,512]{1,0:T(8,128)(2,1)} custom-call(s32[8,512]{1,0:T(8,128)S(1)} %shard_map.83.refs_2_.bounds_ref, f32[128,128]{1,0:T(8,128)S(1)} %get-tuple-element.37.mine, f32[128,128]{1,0:T(8,128)S(1)} %collective-permute-done.15.one, f32[128,128]{1,0:T(8,128)S(1)} %collective-permute-done.16.two, f32[128,128]{1,0:T(8,128)S(1)} %collective-permute-done.17.three, ...), custom_call_target="tpu_custom_call" | custom-call | tf_op jit(solution)/shard_map/pallas_call | solution.py:387
  (3 shorter events, 0.0 us)
Async XLA Ops:
  1.6 28.0 %collective-permute-start = (bf16[4112,128]{1,0:T(8,128)(2,1)S(1)}, bf16[4112,128]{1,0:T(8,128)(2,1)S(1)}, u32[]{:S(2)}, u32[]{:S(2)}) collective-permute-start(bf16[4112,128]{1,0:T(8,128)(2,1)S(1)} %get-tuple-element.27), channel_id=1, source_target_pairs={{0,16},{16,0},{1,17},{17,1},{2,18},{18,2},{3,19},{19,3},{4,20},{20... | collective-permute-start | bytes 3158024 | tf_op jit(solution)/shard_map/ppermute | solution.py:367
  4.6 4.1 %slice-start = ((s8[8388608]{0:T(1024)(128)(4,1)}), s8[4194304]{0:T(1024)(128)(4,1)S(1)}, s32[]{:S(2)}) async-start(s8[8388608]{0:T(1024)(128)(4,1)} %bitcast.4), calls=%async_computation | async-start | bytes 8388608
  4.6 4.1 %slice-start.1 = ((s8[8388608]{0:T(1024)(128)(4,1)}), s8[4194304]{0:T(1024)(128)(4,1)S(1)}, s32[]{:S(2)}) async-start(s8[8388608]{0:T(1024)(128)(4,1)} %bitcast.4), calls=%async_computation.1 | async-start | bytes 8388608
  4.6 4.1 %copy-start = (bf16[256,4096]{1,0:T(8,128)(2,1)S(1)}, bf16[256,4096]{1,0:T(8,128)(2,1)}, u32[]{:S(2)}) copy-start(bf16[256,4096]{1,0:T(8,128)(2,1)} %refs_0_.3) | copy-start | bytes 6291460
  4.6 7.2 %collective-permute-start.3 = (bf16[64,1280]{1,0:T(8,128)(2,1)S(1)}, bf16[64,1280]{1,0:T(8,128)(2,1)S(1)}, u32[]{:S(2)}, u32[]{:S(2)}) collective-permute-start(bf16[64,1280]{1,0:T(8,128)(2,1)S(1)} %get-tuple-element.28.refs_3_), channel_id=1, source_target_pairs={{0,2},{2,6},{6,10},{10,14},{14,12},{12,8},{8,4},{4,0},{1,3},{3,7},... | collective-permute-start | bytes 491528 | tf_op jit(solution)/shard_map/ppermute | solution.py:356
  6.2 7.1 %collective-permute-start.8 = (bf16[64,1280]{1,0:T(8,128)(2,1)S(1)}, bf16[64,1280]{1,0:T(8,128)(2,1)S(1)}, u32[]{:S(2)}, u32[]{:S(2)}) collective-permute-start(bf16[64,1280]{1,0:T(8,128)(2,1)S(1)} %get-tuple-element.31.refs_7_.refs_0_), channel_id=1, source_target_pairs={{2,0},{6,2},{10,6},{14,10},{12,14},{8,12},{4,8},{0,4},{3,1},{7,3},... | collective-permute-start | bytes 491528 | tf_op jit(solution)/shard_map/ppermute | solution.py:357
  6.7 8.6 %collective-permute-start.10 = (bf16[64,1280]{1,0:T(8,128)(2,1)S(1)}, bf16[64,1280]{1,0:T(8,128)(2,1)S(1)}, u32[]{:S(2)}, u32[]{:S(2)}) collective-permute-start(bf16[64,1280]{1,0:T(8,128)(2,1)S(1)} %get-tuple-element.31.refs_7_.refs_0_), channel_id=1, source_target_pairs={{0,2},{2,6},{6,10},{10,14},{14,12},{12,8},{8,4},{4,0},{1,3},{3,7},... | collective-permute-start | bytes 491528 | tf_op jit(solution)/shard_map/ppermute | solution.py:358
  8.2 8.7 %collective-permute-start.1 = (bf16[64,1280]{1,0:T(8,128)(2,1)S(1)}, bf16[64,1280]{1,0:T(8,128)(2,1)S(1)}, u32[]{:S(2)}, u32[]{:S(2)}) collective-permute-start(bf16[64,1280]{1,0:T(8,128)(2,1)S(1)} %get-tuple-element.28.refs_3_), channel_id=1, source_target_pairs={{2,0},{6,2},{10,6},{14,10},{12,14},{8,12},{4,8},{0,4},{3,1},{7,3},... | collective-permute-start | bytes 491528 | tf_op jit(solution)/shard_map/ppermute | solution.py:359
  13.3 7.1 %collective-permute-start.9 = (bf16[64,1280]{1,0:T(8,128)(2,1)S(1)}, bf16[64,1280]{1,0:T(8,128)(2,1)S(1)}, u32[]{:S(2)}, u32[]{:S(2)}) collective-permute-start(bf16[64,1280]{1,0:T(8,128)(2,1)S(1)} %collective-permute-done.8.refs_9_.refs_2_), channel_id=1, source_target_pairs={{2,0},{6,2},{10,6},{14,10},{12,14},{8,12},{4,8},{0,4},{3,1},{7,3},... | collective-permute-start | bytes 491528 | tf_op jit(solution)/shard_map/ppermute | solution.py:357
  13.9 7.1 %collective-permute-start.4 = (bf16[64,1280]{1,0:T(8,128)(2,1)S(1)}, bf16[64,1280]{1,0:T(8,128)(2,1)S(1)}, u32[]{:S(2)}, u32[]{:S(2)}) collective-permute-start(bf16[64,1280]{1,0:T(8,128)(2,1)S(1)} %collective-permute-done.3.refs_4_), channel_id=1, source_target_pairs={{0,2},{2,6},{6,10},{10,14},{14,12},{12,8},{8,4},{4,0},{1,3},{3,7},... | collective-permute-start | bytes 491528 | tf_op jit(solution)/shard_map/ppermute | solution.py:356
  15.4 7.9 %collective-permute-start.11 = (bf16[64,1280]{1,0:T(8,128)(2,1)S(1)}, bf16[64,1280]{1,0:T(8,128)(2,1)S(1)}, u32[]{:S(2)}, u32[]{:S(2)}) collective-permute-start(bf16[64,1280]{1,0:T(8,128)(2,1)S(1)} %collective-permute-done.10.refs_8_.refs_1_), channel_id=1, source_target_pairs={{0,2},{2,6},{6,10},{10,14},{14,12},{12,8},{8,4},{4,0},{1,3},{3,7},... | collective-permute-start | bytes 491528 | tf_op jit(solution)/shard_map/ppermute | solution.py:358
  16.9 7.1 %collective-permute-start.2 = (bf16[64,1280]{1,0:T(8,128)(2,1)S(1)}, bf16[64,1280]{1,0:T(8,128)(2,1)S(1)}, u32[]{:S(2)}, u32[]{:S(2)}) collective-permute-start(bf16[64,1280]{1,0:T(8,128)(2,1)S(1)} %collective-permute-done.1.refs_5_), channel_id=1, source_target_pairs={{2,0},{6,2},{10,6},{14,10},{12,14},{8,12},{4,8},{0,4},{3,1},{7,3},... | collective-permute-start | bytes 491528 | tf_op jit(solution)/shard_map/ppermute | solution.py:359
  20.5 7.1 %collective-permute-start.13 = (bf16[64,1280]{1,0:T(8,128)(2,1)S(1)}, bf16[64,1280]{1,0:T(8,128)(2,1)S(1)}, u32[]{:S(2)}, u32[]{:S(2)}) collective-permute-start(bf16[64,1280]{1,0:T(8,128)(2,1)S(1)} %collective-permute-done.9.refs_7_.refs_4_), channel_id=1, source_target_pairs={{2,0},{6,2},{10,6},{14,10},{12,14},{8,12},{4,8},{0,4},{3,1},{7,3},... | collective-permute-start | bytes 491528 | tf_op jit(solution)/shard_map/ppermute | solution.py:357
  21.0 7.1 %collective-permute-start.5 = (bf16[64,1280]{1,0:T(8,128)(2,1)S(1)}, bf16[64,1280]{1,0:T(8,128)(2,1)S(1)}, u32[]{:S(2)}, u32[]{:S(2)}) collective-permute-start(bf16[64,1280]{1,0:T(8,128)(2,1)S(1)} %collective-permute-done.4.refs_6_), channel_id=1, source_target_pairs={{0,2},{2,6},{6,10},{10,14},{14,12},{12,8},{8,4},{4,0},{1,3},{3,7},... | collective-permute-start | bytes 491528 | tf_op jit(solution)/shard_map/ppermute | solution.py:356
  23.3 7.2 %collective-permute-start.12 = (bf16[64,1280]{1,0:T(8,128)(2,1)S(1)}, bf16[64,1280]{1,0:T(8,128)(2,1)S(1)}, u32[]{:S(2)}, u32[]{:S(2)}) collective-permute-start(bf16[64,1280]{1,0:T(8,128)(2,1)S(1)} %collective-permute-done.11.refs_10_.refs_3_), channel_id=1, source_target_pairs={{0,2},{2,6},{6,10},{10,14},{14,12},{12,8},{8,4},{4,0},{1,3},{3,7},... | collective-permute-start | bytes 491528 | tf_op jit(solution)/shard_map/ppermute | solution.py:358
  24.1 6.8 %collective-permute-start.6 = (bf16[64,1280]{1,0:T(8,128)(2,1)S(1)}, bf16[64,1280]{1,0:T(8,128)(2,1)S(1)}, u32[]{:S(2)}, u32[]{:S(2)}) collective-permute-start(bf16[64,1280]{1,0:T(8,128)(2,1)S(1)} %collective-permute-done.2.refs_3_), channel_id=1, source_target_pairs={{2,0},{6,2},{10,6},{14,10},{12,14},{8,12},{4,8},{0,4},{3,1},{7,3},... | collective-permute-start | bytes 491528 | tf_op jit(solution)/shard_map/ppermute | solution.py:359
  27.6 5.3 %collective-permute-start.14 = (bf16[64,1280]{1,0:T(8,128)(2,1)S(1)}, bf16[64,1280]{1,0:T(8,128)(2,1)S(1)}, u32[]{:S(2)}, u32[]{:S(2)}) collective-permute-start(bf16[64,1280]{1,0:T(8,128)(2,1)S(1)} %collective-permute-done.13.refs_9_.refs_6_), channel_id=1, source_target_pairs={{2,0},{6,2},{10,6},{14,10},{12,14},{8,12},{4,8},{0,4},{3,1},{7,3},... | collective-permute-start | bytes 491528 | tf_op jit(solution)/shard_map/ppermute | solution.py:366
  28.1 5.3 %collective-permute-start.7 = (bf16[64,1280]{1,0:T(8,128)(2,1)S(1)}, bf16[64,1280]{1,0:T(8,128)(2,1)S(1)}, u32[]{:S(2)}, u32[]{:S(2)}) collective-permute-start(bf16[64,1280]{1,0:T(8,128)(2,1)S(1)} %collective-permute-done.5.refs_4_), channel_id=1, source_target_pairs={{0,2},{2,6},{6,10},{10,14},{14,12},{12,8},{8,4},{4,0},{1,3},{3,7},... | collective-permute-start | bytes 491528 | tf_op jit(solution)/shard_map/ppermute | solution.py:365
  30.4 9.5 %collective-permute-start.18 = (f32[256,512]{1,0:T(8,128)S(1)}, f32[256,512]{1,0:T(8,128)S(1)}, u32[]{:S(2)}, u32[]{:S(2)}) collective-permute-start(f32[256,512]{1,0:T(8,128)S(1)} %get-tuple-element.40), channel_id=1, source_target_pairs={{0,1},{1,0},{2,3},{3,2},{4,5},{5,4},{6,7},{7,6},{8,9},{9,8},{10,11... | collective-permute-start | bytes 1572872 | tf_op jit(solution)/shard_map/ppermute | solution.py:378
  34.3 4.3 %collective-permute-start.16 = (f32[128,128]{1,0:T(8,128)S(1)}, f32[128,128]{1,0:T(8,128)S(1)}, u32[]{:S(2)}, u32[]{:S(2)}) collective-permute-start(f32[128,128]{1,0:T(8,128)S(1)} %get-tuple-element.38), channel_id=1, source_target_pairs={{0,16},{16,0},{1,17},{17,1},{2,18},{18,2},{3,19},{19,3},{4,20},{20... | collective-permute-start | bytes 196616 | tf_op jit(solution)/shard_map/ppermute | solution.py:382
  34.8 3.9 %collective-permute-start.15 = (f32[128,128]{1,0:T(8,128)S(1)}, f32[128,128]{1,0:T(8,128)S(1)}, u32[]{:S(2)}, u32[]{:S(2)}) collective-permute-start(f32[128,128]{1,0:T(8,128)S(1)} %get-tuple-element.37.mine), channel_id=1, source_target_pairs={{0,1},{1,0},{2,3},{3,2},{4,5},{5,4},{6,7},{7,6},{8,9},{9,8},{10,11... | collective-permute-start | bytes 196616 | tf_op jit(solution)/shard_map/ppermute | solution.py:383
  38.7 1.3 %collective-permute-start.17 = (f32[128,128]{1,0:T(8,128)S(1)}, f32[128,128]{1,0:T(8,128)S(1)}, u32[]{:S(2)}, u32[]{:S(2)}) collective-permute-start(f32[128,128]{1,0:T(8,128)S(1)} %collective-permute-done.16.two), channel_id=1, source_target_pairs={{0,1},{1,0},{2,3},{3,2},{4,5},{5,4},{6,7},{7,6},{8,9},{9,8},{10,11... | collective-permute-start | bytes 196616 | tf_op jit(solution)/shard_map/ppermute | solution.py:384

commit v10 on v9

--- a/solution.py
+++ b/solution.py
@@ -347,23 +347,22 @@
         jnp.asarray(table, I32),
     )
 
-    bounds, first, second = lax.optimization_barrier((mark(bounds), first, second))
-
-    near, far = base_call(hidden, value_weight)
+    bounds, first_later, second_later = lax.optimization_barrier((mark(bounds), first, second))
+
     firsts, seconds = [first], [second]
-    ahead, behind = (first, second), (first, second)
+    ahead, behind = (first, second_later), (first_later, second)
     for step in range(1, full + 1):
         a = lax.ppermute(ahead[0], "batch", forward)
         d = lax.ppermute(behind[1], "batch", backward)
         b = lax.ppermute(ahead[1], "batch", forward)
         c = lax.ppermute(behind[0], "batch", backward)
-        if step == 1:
-            a, far = lax.optimization_barrier((a, far))
         ahead, behind = (a, b), (c, d)
         firsts += [a, c]
         seconds += [b, d]
-    firsts.append(lax.ppermute(ahead[0], "batch", forward))
-    seconds.append(lax.ppermute(behind[1], "batch", backward))
+    rows_base, a, d = lax.optimization_barrier((hidden, ahead[0], behind[1]))
+    firsts.append(lax.ppermute(a, "batch", forward))
+    seconds.append(lax.ppermute(d, "batch", backward))
+    near, far = base_call(rows_base, value_weight)
     other = lax.ppermute(to_other, "groups", swap)
 
     count = owners // GROUP
@@ -374,7 +373,7 @@
         pieces += seconds[group * GROUP : (group + 1) * GROUP]
     sides = (hidden, other, bounds)
     starts = rank_call(tuple(early), depth, *sides, pieces, None)
-    *starts, far = lax.optimization_barrier((*starts, far))
+    *starts, far, near = lax.optimization_barrier((*starts, far, near))
     far = lax.ppermute(far, "tensor", swap)
     pieces = firsts[-GROUP:] + seconds[-GROUP:]
     mine, theirs = rank_call((count - 1,), depth, *sides, pieces, starts)

time: 41.2 us -> 40.7 us (0.988)
  waiting for transfers between devices: 16.4 us -> 14.5 us
  starting transfers between devices: 17.8 us -> 19.2 us
    ppermute x3, waiting for transfers between devices: 6.83 us -> 0.64 us  [per_device(): d = lax.ppermute(behind[1], 'batch', backward)]
    ppermute x3, waiting for transfers between devices: 0.81 us -> 6.28 us  [per_device(): b = lax.ppermute(ahead[1], 'batch', forward)]
    ppermute x3, starting transfers between devices: 1.59 us -> 6.68 us  [per_device(): d = lax.ppermute(behind[1], 'batch', backward)]
    ppermute x3, starting transfers between devices: 4.54 us -> 0.74 us  [per_device(): a = lax.ppermute(ahead[0], 'batch', forward)]
    ppermute x3, starting transfers between devices: 2.24 us -> 4.56 us  [per_device(): c = lax.ppermute(behind[0], 'batch', backward)]
    ppermute x3, starting transfers between devices: 3.84 us -> 1.57 us  [per_device(): b = lax.ppermute(ahead[1], 'batch', forward)]
    ppermute x3, waiting for transfers between devices: 0.7 us -> 2.01 us  [per_device(): a = lax.ppermute(ahead[0], 'batch', forward)]
    ppermute x1, starting transfers between devices: 0.49 us -> 1.59 us  [per_device(): two = lax.ppermute(theirs, 'groups', swap)]
where the time goes in v10:
time: 40.7 us; the launch traced here: 40.6 us
  starting transfers between devices  19.2 us (47%)
  waiting for transfers between devices  14.5 us (36%)
  Pallas kernels  6.74 us (17%)
    ppermute x3, starting transfers between devices, per_device(): d = lax.ppermute(behind[1], 'batch', backward)  6.68 us
    ppermute x3, waiting for transfers between devices, per_device(): b = lax.ppermute(ahead[1], 'batch', forward)  6.28 us
    ppermute x3, starting transfers between devices, per_device(): c = lax.ppermute(behind[0], 'batch', backward)  4.56 us
    ppermute x1, waiting for transfers between devices, per_device(): two = lax.ppermute(theirs, 'groups', swap)  2.74 us
    pallas_call x1, Pallas kernels, base_call(): pl.pallas_call(base_kernel, out_shape=(out, out), in_specs=[VMEM] * 2, ou...  2.35 us
    ppermute x3, waiting for transfers between devices, per_device(): a = lax.ppermute(ahead[0], 'batch', forward)  2.01 us
    ppermute x1, starting transfers between devices, per_device(): other = lax.ppermute(to_other, 'groups', swap)  1.97 us
    pallas_call x2, Pallas kernels, rank_call(): pl.pallas_call(functools.partial(rank_kernel, groups, depth, last), out_s...  1.65 us
  transfers between devices with their start and end apart: 19, of which 10 were waited for; matrix products, arithmetic and copies ran while one was open for 0% of the time, Pallas kernels for 10%

profile of v10, /device:TPU:0, one launch (start us, length us, event | category | flops | bytes accessed | tf_op | source)
XLA Modules:
  0.0 40.6 jit_solution(15532886254899954338)
XLA Ops:
  0.0 1.6 %shard_map.82 = (bf16[4112,128]{1,0:T(8,128)(2,1)S(1)}, bf16[64,1280]{1,0:T(8,128)(2,1)S(1)}, bf16[64,1280]{1,0:T(8,128)(2,1)S(1)}, s32[8,512]{1,0:T(8,128)S(1)}) custom-call(bf16[256,4096]{1,0:T(8,128)(2,1)} %refs_0_.3, bf16[64,4096]{1,0:T(8,128)(2,1)} %bitcast.6, bf16[64,512]{1,0:T(8,128)(2,1)} %bitcast.7, s32[1,4]{1,0:T(1,128)} %demand_ref.1, ...), custom_call_target="tpu_custom_call" | custom-call | tf_op jit(solution)/shard_map/pallas_call | solution.py:161
  1.6 3.1 %collective-permute-start.7 = (bf16[64,1280]{1,0:T(8,128)(2,1)S(1)}, bf16[64,1280]{1,0:T(8,128)(2,1)S(1)}, u32[]{:S(2)}, u32[]{:S(2)}) collective-permute-start(bf16[64,1280]{1,0:T(8,128)(2,1)S(1)} %get-tuple-element.32.refs_7_.refs_0_), channel_id=1, source_target_pairs={{2,0},{6,2},{10,6},{14,10},{12,14},{8,12},{4,8},{0,4},{3,1},{7,3},... | collective-permute-start | bytes 491528 | tf_op jit(solution)/shard_map/ppermute | solution.py:356
  4.7 0.0 collective-permute-start.3
  4.7 2.0 %collective-permute-start = (bf16[4112,128]{1,0:T(8,128)(2,1)S(1)}, bf16[4112,128]{1,0:T(8,128)(2,1)S(1)}, u32[]{:S(2)}, u32[]{:S(2)}) collective-permute-start(bf16[4112,128]{1,0:T(8,128)(2,1)S(1)} %get-tuple-element.29), channel_id=1, source_target_pairs={{0,16},{16,0},{1,17},{17,1},{2,18},{18,2},{3,19},{19,3},{4,20},{20... | collective-permute-start | bytes 3158024 | tf_op jit(solution)/shard_map/ppermute | solution.py:366
  6.7 0.0 slice-start
  6.7 0.0 slice-start.1
  6.7 1.5 %collective-permute-start.11 = (bf16[64,1280]{1,0:T(8,128)(2,1)S(1)}, bf16[64,1280]{1,0:T(8,128)(2,1)S(1)}, u32[]{:S(2)}, u32[]{:S(2)}) collective-permute-start(bf16[64,1280]{1,0:T(8,128)(2,1)S(1)} %get-tuple-element.32.refs_7_.refs_0_), channel_id=1, source_target_pairs={{0,2},{2,6},{6,10},{10,14},{14,12},{12,8},{8,4},{4,0},{1,3},{3,7},... | collective-permute-start | bytes 491528 | tf_op jit(solution)/shard_map/ppermute | solution.py:357
  8.2 0.5 %collective-permute-start.1 = (bf16[64,1280]{1,0:T(8,128)(2,1)S(1)}, bf16[64,1280]{1,0:T(8,128)(2,1)S(1)}, u32[]{:S(2)}, u32[]{:S(2)}) collective-permute-start(bf16[64,1280]{1,0:T(8,128)(2,1)S(1)} %get-tuple-element.30.refs_3_), channel_id=1, source_target_pairs={{2,0},{6,2},{10,6},{14,10},{12,14},{8,12},{4,8},{0,4},{3,1},{7,3},... | collective-permute-start | bytes 491528 | tf_op jit(solution)/shard_map/ppermute | solution.py:358
  8.7 0.1 collective-permute-done.7.refs_9_.refs_2_
  8.8 2.3 %collective-permute-start.8 = (bf16[64,1280]{1,0:T(8,128)(2,1)S(1)}, bf16[64,1280]{1,0:T(8,128)(2,1)S(1)}, u32[]{:S(2)}, u32[]{:S(2)}) collective-permute-start(bf16[64,1280]{1,0:T(8,128)(2,1)S(1)} %collective-permute-done.7.refs_9_.refs_2_), channel_id=1, source_target_pairs={{2,0},{6,2},{10,6},{14,10},{12,14},{8,12},{4,8},{0,4},{3,1},{7,3},... | collective-permute-start | bytes 491528 | tf_op jit(solution)/shard_map/ppermute | solution.py:356
  11.1 0.7 %collective-permute-done.3.refs_4_ = bf16[64,1280]{1,0:T(8,128)(2,1)S(1)} collective-permute-done((bf16[64,1280]{1,0:T(8,128)(2,1)S(1)}, bf16[64,1280]{1,0:T(8,128)(2,1)S(1)}, u32[]{:S(2)}, u32[]{:S(2)}) %collective-permute-start.3) | collective-permute-done | bytes 163872 | tf_op jit(solution)/shard_map/ppermute | solution.py:355
  11.8 0.0 collective-permute-start.4
  11.8 3.5 %collective-permute-done.11.refs_8_.refs_1_ = bf16[64,1280]{1,0:T(8,128)(2,1)S(1)} collective-permute-done((bf16[64,1280]{1,0:T(8,128)(2,1)S(1)}, bf16[64,1280]{1,0:T(8,128)(2,1)S(1)}, u32[]{:S(2)}, u32[]{:S(2)}) %collective-permute-start.11) | collective-permute-done | bytes 163872 | tf_op jit(solution)/shard_map/ppermute | solution.py:357
  15.3 0.0 collective-permute-start.12
  15.3 0.0 collective-permute-done.1.refs_5_
  15.3 2.0 %collective-permute-start.2 = (bf16[64,1280]{1,0:T(8,128)(2,1)S(1)}, bf16[64,1280]{1,0:T(8,128)(2,1)S(1)}, u32[]{:S(2)}, u32[]{:S(2)}) collective-permute-start(bf16[64,1280]{1,0:T(8,128)(2,1)S(1)} %collective-permute-done.1.refs_5_), channel_id=1, source_target_pairs={{2,0},{6,2},{10,6},{14,10},{12,14},{8,12},{4,8},{0,4},{3,1},{7,3},... | collective-permute-start | bytes 491528 | tf_op jit(solution)/shard_map/ppermute | solution.py:358
  17.3 0.3 collective-permute-done.8.refs_7_.refs_4_
  17.6 1.3 %collective-permute-start.9 = (bf16[64,1280]{1,0:T(8,128)(2,1)S(1)}, bf16[64,1280]{1,0:T(8,128)(2,1)S(1)}, u32[]{:S(2)}, u32[]{:S(2)}) collective-permute-start(bf16[64,1280]{1,0:T(8,128)(2,1)S(1)} %collective-permute-done.8.refs_7_.refs_4_), channel_id=1, source_target_pairs={{2,0},{6,2},{10,6},{14,10},{12,14},{8,12},{4,8},{0,4},{3,1},{7,3},... | collective-permute-start | bytes 491528 | tf_op jit(solution)/shard_map/ppermute | solution.py:356
  18.9 0.0 collective-permute-done.4.refs_6_
  18.9 0.7 %collective-permute-start.5 = (bf16[64,1280]{1,0:T(8,128)(2,1)S(1)}, bf16[64,1280]{1,0:T(8,128)(2,1)S(1)}, u32[]{:S(2)}, u32[]{:S(2)}) collective-permute-start(bf16[64,1280]{1,0:T(8,128)(2,1)S(1)} %collective-permute-done.4.refs_6_), channel_id=1, source_target_pairs={{0,2},{2,6},{6,10},{10,14},{14,12},{12,8},{8,4},{4,0},{1,3},{3,7},... | collective-permute-start | bytes 491528 | tf_op jit(solution)/shard_map/ppermute | solution.py:355
  19.7 2.8 %collective-permute-done.12.refs_10_.refs_3_ = bf16[64,1280]{1,0:T(8,128)(2,1)S(1)} collective-permute-done((bf16[64,1280]{1,0:T(8,128)(2,1)S(1)}, bf16[64,1280]{1,0:T(8,128)(2,1)S(1)}, u32[]{:S(2)}, u32[]{:S(2)}) %collective-permute-start.12) | collective-permute-done | bytes 163872 | tf_op jit(solution)/shard_map/ppermute | solution.py:357
  22.5 0.0 collective-permute-start.13
  22.5 0.0 collective-permute-done.2.refs_3_
  22.5 2.0 %collective-permute-start.6 = (bf16[64,1280]{1,0:T(8,128)(2,1)S(1)}, bf16[64,1280]{1,0:T(8,128)(2,1)S(1)}, u32[]{:S(2)}, u32[]{:S(2)}) collective-permute-start(bf16[64,1280]{1,0:T(8,128)(2,1)S(1)} %collective-permute-done.2.refs_3_), channel_id=1, source_target_pairs={{2,0},{6,2},{10,6},{14,10},{12,14},{8,12},{4,8},{0,4},{3,1},{7,3},... | collective-permute-start | bytes 491528 | tf_op jit(solution)/shard_map/ppermute | solution.py:358
  24.5 0.3 collective-permute-done.9.refs_9_.refs_6_
  24.8 1.3 %collective-permute-done.5.refs_4_ = bf16[64,1280]{1,0:T(8,128)(2,1)S(1)} collective-permute-done((bf16[64,1280]{1,0:T(8,128)(2,1)S(1)}, bf16[64,1280]{1,0:T(8,128)(2,1)S(1)}, u32[]{:S(2)}, u32[]{:S(2)}) %collective-permute-start.5) | collective-permute-done | bytes 163872 | tf_op jit(solution)/shard_map/ppermute | solution.py:355
  26.1 1.6 %collective-permute-start.14 = (bf16[64,1280]{1,0:T(8,128)(2,1)S(1)}, bf16[64,1280]{1,0:T(8,128)(2,1)S(1)}, u32[]{:S(2)}, u32[]{:S(2)}) collective-permute-start(bf16[64,1280]{1,0:T(8,128)(2,1)S(1)} %collective-permute-done.9.refs_9_.refs_6_), channel_id=1, source_target_pairs={{2,0},{6,2},{10,6},{14,10},{12,14},{8,12},{4,8},{0,4},{3,1},{7,3},... | collective-permute-start | bytes 491528 | tf_op jit(solution)/shard_map/ppermute | solution.py:364
  27.7 0.4 %collective-permute-start.10 = (bf16[64,1280]{1,0:T(8,128)(2,1)S(1)}, bf16[64,1280]{1,0:T(8,128)(2,1)S(1)}, u32[]{:S(2)}, u32[]{:S(2)}) collective-permute-start(bf16[64,1280]{1,0:T(8,128)(2,1)S(1)} %collective-permute-done.5.refs_4_), channel_id=1, source_target_pairs={{0,2},{2,6},{6,10},{10,14},{14,12},{12,8},{8,4},{4,0},{1,3},{3,7},... | collective-permute-start | bytes 491528 | tf_op jit(solution)/shard_map/ppermute | solution.py:363
  28.1 0.0 slice-done
  28.1 0.0 slice-done.1
  28.1 0.0 copy-done
  28.1 2.4 %shard_map.85 = (f32[256,512]{1,0:T(8,128)S(1)}, f32[256,512]{1,0:T(8,128)S(1)}) custom-call(bf16[256,4096]{1,0:T(8,128)(2,1)S(1)} %copy-done, bf16[4096,1024]{1,0:T(8,128)(2,1)S(1)} %bitcast.5), custom_call_target="tpu_custom_call" | custom-call | bytes 4194304 | tf_op jit(solution)/shard_map/pallas_call | solution.py:210
  30.5 0.0 collective-permute-done.refs_1_
  30.5 0.8 %shard_map.84 = (f32[256,128]{1,0:T(8,128)S(1)}, f32[256,128]{1,0:T(8,128)S(1)}) custom-call(bf16[256,4096]{1,0:T(8,128)(2,1)S(1)} %copy-done, bf16[4112,128]{1,0:T(8,128)(2,1)S(1)} %collective-permute-done.refs_1_, s32[8,512]{1,0:T(8,128)S(1)} %shard_map.83.refs_2_.bounds_ref, bf16[64,1280]{1,0:T(8,128)(2,1)S(1)} %get-tuple-element.30.refs_3_, ...), custom_call_target="tpu_custom_call" | custom-call | flops 8589934592 | bytes 16777216 | tf_op jit(solution)/shard_map/pallas_call | solution.py:287
  31.3 0.1 collective-permute-start.18
  31.4 0.0 collective-permute-done.13.refs_8_.refs_5_
  31.4 0.0 collective-permute-done.6.refs_5_
  31.4 0.0 collective-permute-done.14.refs_10_.refs_7_
  31.4 1.6 %collective-permute-done.10.refs_6_ = bf16[64,1280]{1,0:T(8,128)(2,1)S(1)} collective-permute-done((bf16[64,1280]{1,0:T(8,128)(2,1)S(1)}, bf16[64,1280]{1,0:T(8,128)(2,1)S(1)}, u32[]{:S(2)}, u32[]{:S(2)}) %collective-permute-start.10) | collective-permute-done | bytes 163872 | tf_op jit(solution)/shard_map/ppermute | solution.py:363
  33.0 0.9 %shard_map.86 = (f32[128,128]{1,0:T(8,128)S(1)}, f32[128,128]{1,0:T(8,128)S(1)}) custom-call(bf16[256,4096]{1,0:T(8,128)(2,1)S(1)} %copy-done, bf16[4112,128]{1,0:T(8,128)(2,1)S(1)} %collective-permute-done.refs_1_, s32[8,512]{1,0:T(8,128)S(1)} %shard_map.83.refs_2_.bounds_ref, bf16[64,1280]{1,0:T(8,128)(2,1)S(1)} %collective-permute-done.2.refs_3_, ...), custom_call_target="tpu_custom_call" | custom-call | flops 8589934592 | bytes 16777216 | tf_op jit(solution)/shard_map/pallas_call | solution.py:287
  33.8 1.6 %collective-permute-start.16 = (f32[128,128]{1,0:T(8,128)S(1)}, f32[128,128]{1,0:T(8,128)S(1)}, u32[]{:S(2)}, u32[]{:S(2)}) collective-permute-start(f32[128,128]{1,0:T(8,128)S(1)} %get-tuple-element.42), channel_id=1, source_target_pairs={{0,16},{16,0},{1,17},{17,1},{2,18},{18,2},{3,19},{19,3},{4,20},{20... | collective-permute-start | bytes 196616 | tf_op jit(solution)/shard_map/ppermute | solution.py:381
  35.4 0.0 collective-permute-start.15
  35.4 2.7 %collective-permute-done.16.two = f32[128,128]{1,0:T(8,128)S(1)} collective-permute-done((f32[128,128]{1,0:T(8,128)S(1)}, f32[128,128]{1,0:T(8,128)S(1)}, u32[]{:S(2)}, u32[]{:S(2)}) %collective-permute-start.16) | collective-permute-done | bytes 65568 | tf_op jit(solution)/shard_map/ppermute | solution.py:381
  38.2 0.0 collective-permute-start.17
  38.2 0.0 collective-permute-done.15.one
  38.2 1.2 %collective-permute-done.17.three = f32[128,128]{1,0:T(8,128)S(1)} collective-permute-done((f32[128,128]{1,0:T(8,128)S(1)}, f32[128,128]{1,0:T(8,128)S(1)}, u32[]{:S(2)}, u32[]{:S(2)}) %collective-permute-start.17) | collective-permute-done | bytes 65568 | tf_op jit(solution)/shard_map/ppermute | solution.py:383
  39.4 0.0 collective-permute-done.18.far_ref
  39.4 1.1 %shard_map.87 = bf16[256,512]{1,0:T(8,128)(2,1)} custom-call(s32[8,512]{1,0:T(8,128)S(1)} %shard_map.83.refs_2_.bounds_ref, f32[128,128]{1,0:T(8,128)S(1)} %get-tuple-element.41.mine, f32[128,128]{1,0:T(8,128)S(1)} %collective-permute-done.15.one, f32[128,128]{1,0:T(8,128)S(1)} %collective-permute-done.16.two, f32[128,128]{1,0:T(8,128)S(1)} %collective-permute-done.17.three, ...), custom_call_target="tpu_custom_call" | custom-call | tf_op jit(solution)/shard_map/pallas_call | solution.py:386
  (3 shorter events, 0.0 us)
Async XLA Ops:
  1.6 7.2 %collective-permute-start.7 = (bf16[64,1280]{1,0:T(8,128)(2,1)S(1)}, bf16[64,1280]{1,0:T(8,128)(2,1)S(1)}, u32[]{:S(2)}, u32[]{:S(2)}) collective-permute-start(bf16[64,1280]{1,0:T(8,128)(2,1)S(1)} %get-tuple-element.32.refs_7_.refs_0_), channel_id=1, source_target_pairs={{2,0},{6,2},{10,6},{14,10},{12,14},{8,12},{4,8},{0,4},{3,1},{7,3},... | collective-permute-start | bytes 491528 | tf_op jit(solution)/shard_map/ppermute | solution.py:356
  4.7 7.1 %collective-permute-start.3 = (bf16[64,1280]{1,0:T(8,128)(2,1)S(1)}, bf16[64,1280]{1,0:T(8,128)(2,1)S(1)}, u32[]{:S(2)}, u32[]{:S(2)}) collective-permute-start(bf16[64,1280]{1,0:T(8,128)(2,1)S(1)} %get-tuple-element.30.refs_3_), channel_id=1, source_target_pairs={{0,2},{2,6},{6,10},{10,14},{14,12},{12,8},{8,4},{4,0},{1,3},{3,7},... | collective-permute-start | bytes 491528 | tf_op jit(solution)/shard_map/ppermute | solution.py:355
  4.7 25.8 %collective-permute-start = (bf16[4112,128]{1,0:T(8,128)(2,1)S(1)}, bf16[4112,128]{1,0:T(8,128)(2,1)S(1)}, u32[]{:S(2)}, u32[]{:S(2)}) collective-permute-start(bf16[4112,128]{1,0:T(8,128)(2,1)S(1)} %get-tuple-element.29), channel_id=1, source_target_pairs={{0,16},{16,0},{1,17},{17,1},{2,18},{18,2},{3,19},{19,3},{4,20},{20... | collective-permute-start | bytes 3158024 | tf_op jit(solution)/shard_map/ppermute | solution.py:366
  6.7 21.5 %slice-start = ((s8[8388608]{0:T(1024)(128)(4,1)}), s8[4194304]{0:T(1024)(128)(4,1)S(1)}, s32[]{:S(2)}) async-start(s8[8388608]{0:T(1024)(128)(4,1)} %bitcast.4), calls=%async_computation | async-start | bytes 8388608
  6.7 21.5 %slice-start.1 = ((s8[8388608]{0:T(1024)(128)(4,1)}), s8[4194304]{0:T(1024)(128)(4,1)S(1)}, s32[]{:S(2)}) async-start(s8[8388608]{0:T(1024)(128)(4,1)} %bitcast.4), calls=%async_computation.1 | async-start | bytes 8388608
  6.7 21.5 %copy-start = (bf16[256,4096]{1,0:T(8,128)(2,1)S(1)}, bf16[256,4096]{1,0:T(8,128)(2,1)}, u32[]{:S(2)}) copy-start(bf16[256,4096]{1,0:T(8,128)(2,1)} %refs_0_.3) | copy-start | bytes 6291460
  6.7 8.7 %collective-permute-start.11 = (bf16[64,1280]{1,0:T(8,128)(2,1)S(1)}, bf16[64,1280]{1,0:T(8,128)(2,1)S(1)}, u32[]{:S(2)}, u32[]{:S(2)}) collective-permute-start(bf16[64,1280]{1,0:T(8,128)(2,1)S(1)} %get-tuple-element.32.refs_7_.refs_0_), channel_id=1, source_target_pairs={{0,2},{2,6},{6,10},{10,14},{14,12},{12,8},{8,4},{4,0},{1,3},{3,7},... | collective-permute-start | bytes 491528 | tf_op jit(solution)/shard_map/ppermute | solution.py:357
  8.2 7.1 %collective-permute-start.1 = (bf16[64,1280]{1,0:T(8,128)(2,1)S(1)}, bf16[64,1280]{1,0:T(8,128)(2,1)S(1)}, u32[]{:S(2)}, u32[]{:S(2)}) collective-permute-start(bf16[64,1280]{1,0:T(8,128)(2,1)S(1)} %get-tuple-element.30.refs_3_), channel_id=1, source_target_pairs={{2,0},{6,2},{10,6},{14,10},{12,14},{8,12},{4,8},{0,4},{3,1},{7,3},... | collective-permute-start | bytes 491528 | tf_op jit(solution)/shard_map/ppermute | solution.py:358
  8.8 8.9 %collective-permute-start.8 = (bf16[64,1280]{1,0:T(8,128)(2,1)S(1)}, bf16[64,1280]{1,0:T(8,128)(2,1)S(1)}, u32[]{:S(2)}, u32[]{:S(2)}) collective-permute-start(bf16[64,1280]{1,0:T(8,128)(2,1)S(1)} %collective-permute-done.7.refs_9_.refs_2_), channel_id=1, source_target_pairs={{2,0},{6,2},{10,6},{14,10},{12,14},{8,12},{4,8},{0,4},{3,1},{7,3},... | collective-permute-start | bytes 491528 | tf_op jit(solution)/shard_map/ppermute | solution.py:356
  11.8 7.1 %collective-permute-start.4 = (bf16[64,1280]{1,0:T(8,128)(2,1)S(1)}, bf16[64,1280]{1,0:T(8,128)(2,1)S(1)}, u32[]{:S(2)}, u32[]{:S(2)}) collective-permute-start(bf16[64,1280]{1,0:T(8,128)(2,1)S(1)} %collective-permute-done.3.refs_4_), channel_id=1, source_target_pairs={{0,2},{2,6},{6,10},{10,14},{14,12},{12,8},{8,4},{4,0},{1,3},{3,7},... | collective-permute-start | bytes 491528 | tf_op jit(solution)/shard_map/ppermute | solution.py:355
  15.3 7.1 %collective-permute-start.12 = (bf16[64,1280]{1,0:T(8,128)(2,1)S(1)}, bf16[64,1280]{1,0:T(8,128)(2,1)S(1)}, u32[]{:S(2)}, u32[]{:S(2)}) collective-permute-start(bf16[64,1280]{1,0:T(8,128)(2,1)S(1)} %collective-permute-done.11.refs_8_.refs_1_), channel_id=1, source_target_pairs={{0,2},{2,6},{6,10},{10,14},{14,12},{12,8},{8,4},{4,0},{1,3},{3,7},... | collective-permute-start | bytes 491528 | tf_op jit(solution)/shard_map/ppermute | solution.py:357
  15.3 7.1 %collective-permute-start.2 = (bf16[64,1280]{1,0:T(8,128)(2,1)S(1)}, bf16[64,1280]{1,0:T(8,128)(2,1)S(1)}, u32[]{:S(2)}, u32[]{:S(2)}) collective-permute-start(bf16[64,1280]{1,0:T(8,128)(2,1)S(1)} %collective-permute-done.1.refs_5_), channel_id=1, source_target_pairs={{2,0},{6,2},{10,6},{14,10},{12,14},{8,12},{4,8},{0,4},{3,1},{7,3},... | collective-permute-start | bytes 491528 | tf_op jit(solution)/shard_map/ppermute | solution.py:358
  17.6 7.1 %collective-permute-start.9 = (bf16[64,1280]{1,0:T(8,128)(2,1)S(1)}, bf16[64,1280]{1,0:T(8,128)(2,1)S(1)}, u32[]{:S(2)}, u32[]{:S(2)}) collective-permute-start(bf16[64,1280]{1,0:T(8,128)(2,1)S(1)} %collective-permute-done.8.refs_7_.refs_4_), channel_id=1, source_target_pairs={{2,0},{6,2},{10,6},{14,10},{12,14},{8,12},{4,8},{0,4},{3,1},{7,3},... | collective-permute-start | bytes 491528 | tf_op jit(solution)/shard_map/ppermute | solution.py:356
  18.9 7.1 %collective-permute-start.5 = (bf16[64,1280]{1,0:T(8,128)(2,1)S(1)}, bf16[64,1280]{1,0:T(8,128)(2,1)S(1)}, u32[]{:S(2)}, u32[]{:S(2)}) collective-permute-start(bf16[64,1280]{1,0:T(8,128)(2,1)S(1)} %collective-permute-done.4.refs_6_), channel_id=1, source_target_pairs={{0,2},{2,6},{6,10},{10,14},{14,12},{12,8},{8,4},{4,0},{1,3},{3,7},... | collective-permute-start | bytes 491528 | tf_op jit(solution)/shard_map/ppermute | solution.py:355
  22.5 8.9 %collective-permute-start.13 = (bf16[64,1280]{1,0:T(8,128)(2,1)S(1)}, bf16[64,1280]{1,0:T(8,128)(2,1)S(1)}, u32[]{:S(2)}, u32[]{:S(2)}) collective-permute-start(bf16[64,1280]{1,0:T(8,128)(2,1)S(1)} %collective-permute-done.12.refs_10_.refs_3_), channel_id=1, source_target_pairs={{0,2},{2,6},{6,10},{10,14},{14,12},{12,8},{8,4},{4,0},{1,3},{3,7},... | collective-permute-start | bytes 491528 | tf_op jit(solution)/shard_map/ppermute | solution.py:357
  22.5 8.9 %collective-permute-start.6 = (bf16[64,1280]{1,0:T(8,128)(2,1)S(1)}, bf16[64,1280]{1,0:T(8,128)(2,1)S(1)}, u32[]{:S(2)}, u32[]{:S(2)}) collective-permute-start(bf16[64,1280]{1,0:T(8,128)(2,1)S(1)} %collective-permute-done.2.refs_3_), channel_id=1, source_target_pairs={{2,0},{6,2},{10,6},{14,10},{12,14},{8,12},{4,8},{0,4},{3,1},{7,3},... | collective-permute-start | bytes 491528 | tf_op jit(solution)/shard_map/ppermute | solution.py:358
  26.1 5.3 %collective-permute-start.14 = (bf16[64,1280]{1,0:T(8,128)(2,1)S(1)}, bf16[64,1280]{1,0:T(8,128)(2,1)S(1)}, u32[]{:S(2)}, u32[]{:S(2)}) collective-permute-start(bf16[64,1280]{1,0:T(8,128)(2,1)S(1)} %collective-permute-done.9.refs_9_.refs_6_), channel_id=1, source_target_pairs={{2,0},{6,2},{10,6},{14,10},{12,14},{8,12},{4,8},{0,4},{3,1},{7,3},... | collective-permute-start | bytes 491528 | tf_op jit(solution)/shard_map/ppermute | solution.py:364
  27.7 5.3 %collective-permute-start.10 = (bf16[64,1280]{1,0:T(8,128)(2,1)S(1)}, bf16[64,1280]{1,0:T(8,128)(2,1)S(1)}, u32[]{:S(2)}, u32[]{:S(2)}) collective-permute-start(bf16[64,1280]{1,0:T(8,128)(2,1)S(1)} %collective-permute-done.5.refs_4_), channel_id=1, source_target_pairs={{0,2},{2,6},{6,10},{10,14},{14,12},{12,8},{8,4},{4,0},{1,3},{3,7},... | collective-permute-start | bytes 491528 | tf_op jit(solution)/shard_map/ppermute | solution.py:363
  31.3 8.2 %collective-permute-start.18 = (f32[256,512]{1,0:T(8,128)S(1)}, f32[256,512]{1,0:T(8,128)S(1)}, u32[]{:S(2)}, u32[]{:S(2)}) collective-permute-start(f32[256,512]{1,0:T(8,128)S(1)} %get-tuple-element.44), channel_id=1, source_target_pairs={{0,1},{1,0},{2,3},{3,2},{4,5},{5,4},{6,7},{7,6},{8,9},{9,8},{10,11... | collective-permute-start | bytes 1572872 | tf_op jit(solution)/shard_map/ppermute | solution.py:377
  33.8 4.3 %collective-permute-start.16 = (f32[128,128]{1,0:T(8,128)S(1)}, f32[128,128]{1,0:T(8,128)S(1)}, u32[]{:S(2)}, u32[]{:S(2)}) collective-permute-start(f32[128,128]{1,0:T(8,128)S(1)} %get-tuple-element.42), channel_id=1, source_target_pairs={{0,16},{16,0},{1,17},{17,1},{2,18},{18,2},{3,19},{19,3},{4,20},{20... | collective-permute-start | bytes 196616 | tf_op jit(solution)/shard_map/ppermute | solution.py:381
  35.4 2.7 %collective-permute-start.15 = (f32[128,128]{1,0:T(8,128)S(1)}, f32[128,128]{1,0:T(8,128)S(1)}, u32[]{:S(2)}, u32[]{:S(2)}) collective-permute-start(f32[128,128]{1,0:T(8,128)S(1)} %get-tuple-element.41.mine), channel_id=1, source_target_pairs={{0,1},{1,0},{2,3},{3,2},{4,5},{5,4},{6,7},{7,6},{8,9},{9,8},{10,11... | collective-permute-start | bytes 196616 | tf_op jit(solution)/shard_map/ppermute | solution.py:382
  38.2 1.3 %collective-permute-start.17 = (f32[128,128]{1,0:T(8,128)S(1)}, f32[128,128]{1,0:T(8,128)S(1)}, u32[]{:S(2)}, u32[]{:S(2)}) collective-permute-start(f32[128,128]{1,0:T(8,128)S(1)} %collective-permute-done.16.two), channel_id=1, source_target_pairs={{0,1},{1,0},{2,3},{3,2},{4,5},{5,4},{6,7},{7,6},{8,9},{9,8},{10,11... | collective-permute-start | bytes 196616 | tf_op jit(solution)/shard_map/ppermute | solution.py:383

commit v11 on v9

--- a/solution.py
+++ b/solution.py
@@ -347,23 +347,22 @@
         jnp.asarray(table, I32),
     )
 
-    bounds, first, second = lax.optimization_barrier((mark(bounds), first, second))
-
-    near, far = base_call(hidden, value_weight)
+    bounds, first_later, second_later = lax.optimization_barrier((mark(bounds), first, second))
+
     firsts, seconds = [first], [second]
-    ahead, behind = (first, second), (first, second)
+    ahead, behind = (first, second_later), (first_later, second)
     for step in range(1, full + 1):
         a = lax.ppermute(ahead[0], "batch", forward)
         d = lax.ppermute(behind[1], "batch", backward)
         b = lax.ppermute(ahead[1], "batch", forward)
         c = lax.ppermute(behind[0], "batch", backward)
-        if step == 1:
-            a, far = lax.optimization_barrier((a, far))
         ahead, behind = (a, b), (c, d)
         firsts += [a, c]
         seconds += [b, d]
     firsts.append(lax.ppermute(ahead[0], "batch", forward))
     seconds.append(lax.ppermute(behind[1], "batch", backward))
+    near, far = base_call(hidden, value_weight)
+    hidden, near, far = lax.optimization_barrier((hidden, near, far))
     other = lax.ppermute(to_other, "groups", swap)
 
     count = owners // GROUP

time: 41.2 us -> 39.2 us (0.951)
  waiting for transfers between devices: 16.4 us -> 12.7 us
  starting transfers between devices: 17.8 us -> 19.4 us
    ppermute x3, waiting for transfers between devices: 6.83 us -> 0.36 us  [per_device(): d = lax.ppermute(behind[1], 'batch', backward)]
    ppermute x3, starting transfers between devices: 1.59 us -> 6.68 us  [per_device(): d = lax.ppermute(behind[1], 'batch', backward)]
    ppermute x3, starting transfers between devices: 4.54 us -> 0.74 us  [per_device(): a = lax.ppermute(ahead[0], 'batch', forward)]
    ppermute x3, waiting for transfers between devices: 0.81 us -> 3.91 us  [per_device(): b = lax.ppermute(ahead[1], 'batch', forward)]
    ppermute x1, waiting for transfers between devices: 0.01 us -> 2.64 us  [per_device(): other = lax.ppermute(to_other, 'groups', swap)]
    ppermute x1, waiting for transfers between devices: 2.03 us -> 0.32 us  [per_device(): seconds.append(lax.ppermute(behind[1], 'batch', backward))]
    ppermute x3, starting transfers between devices: 2.24 us -> 3.48 us  [per_device(): c = lax.ppermute(behind[0], 'batch', backward)]
    ppermute x3, starting transfers between devices: 3.84 us -> 2.65 us  [per_device(): b = lax.ppermute(ahead[1], 'batch', forward)]
where the time goes in v11:
time: 39.2 us; the launch traced here: 39 us
  starting transfers between devices  19.4 us (49%)
  waiting for transfers between devices  12.7 us (32%)
  Pallas kernels  6.75 us (17%)
    ppermute x3, starting transfers between devices, per_device(): d = lax.ppermute(behind[1], 'batch', backward)  6.68 us
    ppermute x3, waiting for transfers between devices, per_device(): b = lax.ppermute(ahead[1], 'batch', forward)  3.91 us
    ppermute x3, starting transfers between devices, per_device(): c = lax.ppermute(behind[0], 'batch', backward)  3.48 us
    ppermute x1, waiting for transfers between devices, per_device(): two = lax.ppermute(theirs, 'groups', swap)  2.74 us
    ppermute x3, starting transfers between devices, per_device(): b = lax.ppermute(ahead[1], 'batch', forward)  2.65 us
    ppermute x1, waiting for transfers between devices, per_device(): other = lax.ppermute(to_other, 'groups', swap)  2.64 us
    pallas_call x1, Pallas kernels, base_call(): pl.pallas_call(base_kernel, out_shape=(out, out), in_specs=[VMEM] * 2, ou...  2.35 us
    ppermute x1, starting transfers between devices, per_device(): other = lax.ppermute(to_other, 'groups', swap)  1.97 us
  transfers between devices with their start and end apart: 19, of which 10 were waited for; matrix products, arithmetic and copies ran while one was open for 0% of the time, Pallas kernels for 10%

profile of v11, /device:TPU:0, one launch (start us, length us, event | category | flops | bytes accessed | tf_op | source)
XLA Modules:
  0.0 39.0 jit_solution(10708874669106320550)
XLA Ops:
  0.0 1.6 %shard_map.82 = (bf16[4112,128]{1,0:T(8,128)(2,1)S(1)}, bf16[64,1280]{1,0:T(8,128)(2,1)S(1)}, bf16[64,1280]{1,0:T(8,128)(2,1)S(1)}, s32[8,512]{1,0:T(8,128)S(1)}) custom-call(bf16[256,4096]{1,0:T(8,128)(2,1)} %refs_0_.1, bf16[64,4096]{1,0:T(8,128)(2,1)} %bitcast.6, bf16[64,512]{1,0:T(8,128)(2,1)} %bitcast.7, s32[1,4]{1,0:T(1,128)} %demand_ref.1, ...), custom_call_target="tpu_custom_call" | custom-call | tf_op jit(solution)/shard_map/pallas_call | solution.py:161
  1.6 3.1 %collective-permute-start.8 = (bf16[64,1280]{1,0:T(8,128)(2,1)S(1)}, bf16[64,1280]{1,0:T(8,128)(2,1)S(1)}, u32[]{:S(2)}, u32[]{:S(2)}) collective-permute-start(bf16[64,1280]{1,0:T(8,128)(2,1)S(1)} %get-tuple-element.33.refs_7_.refs_0_), channel_id=1, source_target_pairs={{2,0},{6,2},{10,6},{14,10},{12,14},{8,12},{4,8},{0,4},{3,1},{7,3},... | collective-permute-start | bytes 491528 | tf_op jit(solution)/shard_map/ppermute | solution.py:356
  4.7 0.0 collective-permute-start.3
  4.7 2.0 %collective-permute-start = (bf16[4112,128]{1,0:T(8,128)(2,1)S(1)}, bf16[4112,128]{1,0:T(8,128)(2,1)S(1)}, u32[]{:S(2)}, u32[]{:S(2)}) collective-permute-start(bf16[4112,128]{1,0:T(8,128)(2,1)S(1)} %get-tuple-element.31), channel_id=1, source_target_pairs={{0,16},{16,0},{1,17},{17,1},{2,18},{18,2},{3,19},{19,3},{4,20},{20... | collective-permute-start | bytes 3158024 | tf_op jit(solution)/shard_map/ppermute | solution.py:366
  6.7 0.0 slice-start
  6.7 0.0 slice-start.1
  6.7 1.5 %collective-permute-start.10 = (bf16[64,1280]{1,0:T(8,128)(2,1)S(1)}, bf16[64,1280]{1,0:T(8,128)(2,1)S(1)}, u32[]{:S(2)}, u32[]{:S(2)}) collective-permute-start(bf16[64,1280]{1,0:T(8,128)(2,1)S(1)} %get-tuple-element.33.refs_7_.refs_0_), channel_id=1, source_target_pairs={{0,2},{2,6},{6,10},{10,14},{14,12},{12,8},{8,4},{4,0},{1,3},{3,7},... | collective-permute-start | bytes 491528 | tf_op jit(solution)/shard_map/ppermute | solution.py:357
  8.2 0.5 %collective-permute-start.1 = (bf16[64,1280]{1,0:T(8,128)(2,1)S(1)}, bf16[64,1280]{1,0:T(8,128)(2,1)S(1)}, u32[]{:S(2)}, u32[]{:S(2)}) collective-permute-start(bf16[64,1280]{1,0:T(8,128)(2,1)S(1)} %get-tuple-element.32.refs_3_), channel_id=1, source_target_pairs={{2,0},{6,2},{10,6},{14,10},{12,14},{8,12},{4,8},{0,4},{3,1},{7,3},... | collective-permute-start | bytes 491528 | tf_op jit(solution)/shard_map/ppermute | solution.py:358
  8.7 0.1 collective-permute-done.8.refs_9_.refs_2_
  8.8 2.3 %collective-permute-start.9 = (bf16[64,1280]{1,0:T(8,128)(2,1)S(1)}, bf16[64,1280]{1,0:T(8,128)(2,1)S(1)}, u32[]{:S(2)}, u32[]{:S(2)}) collective-permute-start(bf16[64,1280]{1,0:T(8,128)(2,1)S(1)} %collective-permute-done.8.refs_9_.refs_2_), channel_id=1, source_target_pairs={{2,0},{6,2},{10,6},{14,10},{12,14},{8,12},{4,8},{0,4},{3,1},{7,3},... | collective-permute-start | bytes 491528 | tf_op jit(solution)/shard_map/ppermute | solution.py:356
  11.1 0.7 %collective-permute-done.3.refs_4_ = bf16[64,1280]{1,0:T(8,128)(2,1)S(1)} collective-permute-done((bf16[64,1280]{1,0:T(8,128)(2,1)S(1)}, bf16[64,1280]{1,0:T(8,128)(2,1)S(1)}, u32[]{:S(2)}, u32[]{:S(2)}) %collective-permute-start.3) | collective-permute-done | bytes 163872 | tf_op jit(solution)/shard_map/ppermute | solution.py:355
  11.8 0.0 collective-permute-start.4
  11.8 3.5 %collective-permute-done.10.refs_8_.refs_1_ = bf16[64,1280]{1,0:T(8,128)(2,1)S(1)} collective-permute-done((bf16[64,1280]{1,0:T(8,128)(2,1)S(1)}, bf16[64,1280]{1,0:T(8,128)(2,1)S(1)}, u32[]{:S(2)}, u32[]{:S(2)}) %collective-permute-start.10) | collective-permute-done | bytes 163872 | tf_op jit(solution)/shard_map/ppermute | solution.py:357
  15.3 0.0 collective-permute-start.11
  15.3 0.0 collective-permute-done.1.refs_5_
  15.3 2.0 %collective-permute-start.2 = (bf16[64,1280]{1,0:T(8,128)(2,1)S(1)}, bf16[64,1280]{1,0:T(8,128)(2,1)S(1)}, u32[]{:S(2)}, u32[]{:S(2)}) collective-permute-start(bf16[64,1280]{1,0:T(8,128)(2,1)S(1)} %collective-permute-done.1.refs_5_), channel_id=1, source_target_pairs={{2,0},{6,2},{10,6},{14,10},{12,14},{8,12},{4,8},{0,4},{3,1},{7,3},... | collective-permute-start | bytes 491528 | tf_op jit(solution)/shard_map/ppermute | solution.py:358
  17.3 0.3 collective-permute-done.9.refs_7_.refs_4_
  17.6 1.3 %collective-permute-start.13 = (bf16[64,1280]{1,0:T(8,128)(2,1)S(1)}, bf16[64,1280]{1,0:T(8,128)(2,1)S(1)}, u32[]{:S(2)}, u32[]{:S(2)}) collective-permute-start(bf16[64,1280]{1,0:T(8,128)(2,1)S(1)} %collective-permute-done.9.refs_7_.refs_4_), channel_id=1, source_target_pairs={{2,0},{6,2},{10,6},{14,10},{12,14},{8,12},{4,8},{0,4},{3,1},{7,3},... | collective-permute-start | bytes 491528 | tf_op jit(solution)/shard_map/ppermute | solution.py:356
  18.9 0.0 collective-permute-done.4.refs_6_
  18.9 0.7 %collective-permute-start.5 = (bf16[64,1280]{1,0:T(8,128)(2,1)S(1)}, bf16[64,1280]{1,0:T(8,128)(2,1)S(1)}, u32[]{:S(2)}, u32[]{:S(2)}) collective-permute-start(bf16[64,1280]{1,0:T(8,128)(2,1)S(1)} %collective-permute-done.4.refs_6_), channel_id=1, source_target_pairs={{0,2},{2,6},{6,10},{10,14},{14,12},{12,8},{8,4},{4,0},{1,3},{3,7},... | collective-permute-start | bytes 491528 | tf_op jit(solution)/shard_map/ppermute | solution.py:355
  19.7 0.0 slice-done
  19.7 0.0 slice-done.1
  19.7 0.0 copy-done
  19.7 2.4 %shard_map.84 = (f32[256,512]{1,0:T(8,128)S(1)}, f32[256,512]{1,0:T(8,128)S(1)}) custom-call(bf16[256,4096]{1,0:T(8,128)(2,1)S(1)} %copy-done, bf16[4096,1024]{1,0:T(8,128)(2,1)S(1)} %bitcast.5), custom_call_target="tpu_custom_call" | custom-call | bytes 4194304 | tf_op jit(solution)/shard_map/pallas_call | solution.py:210
  22.1 0.4 %collective-permute-done.11.refs_10_.refs_3_ = bf16[64,1280]{1,0:T(8,128)(2,1)S(1)} collective-permute-done((bf16[64,1280]{1,0:T(8,128)(2,1)S(1)}, bf16[64,1280]{1,0:T(8,128)(2,1)S(1)}, u32[]{:S(2)}, u32[]{:S(2)}) %collective-permute-start.11) | collective-permute-done | bytes 163872 | tf_op jit(solution)/shard_map/ppermute | solution.py:357
  22.5 1.1 %collective-permute-start.12 = (bf16[64,1280]{1,0:T(8,128)(2,1)S(1)}, bf16[64,1280]{1,0:T(8,128)(2,1)S(1)}, u32[]{:S(2)}, u32[]{:S(2)}) collective-permute-start(bf16[64,1280]{1,0:T(8,128)(2,1)S(1)} %collective-permute-done.11.refs_10_.refs_3_), channel_id=1, source_target_pairs={{0,2},{2,6},{6,10},{10,14},{14,12},{12,8},{8,4},{4,0},{1,3},{3,7},... | collective-permute-start | bytes 491528 | tf_op jit(solution)/shard_map/ppermute | solution.py:357
  23.5 0.0 collective-permute-done.2.refs_3_
  23.5 0.9 %collective-permute-start.6 = (bf16[64,1280]{1,0:T(8,128)(2,1)S(1)}, bf16[64,1280]{1,0:T(8,128)(2,1)S(1)}, u32[]{:S(2)}, u32[]{:S(2)}) collective-permute-start(bf16[64,1280]{1,0:T(8,128)(2,1)S(1)} %collective-permute-done.2.refs_3_), channel_id=1, source_target_pairs={{2,0},{6,2},{10,6},{14,10},{12,14},{8,12},{4,8},{0,4},{3,1},{7,3},... | collective-permute-start | bytes 491528 | tf_op jit(solution)/shard_map/ppermute | solution.py:358
  24.5 0.0 collective-permute-done.13.refs_9_.refs_6_
  24.5 1.6 %collective-permute-start.14 = (bf16[64,1280]{1,0:T(8,128)(2,1)S(1)}, bf16[64,1280]{1,0:T(8,128)(2,1)S(1)}, u32[]{:S(2)}, u32[]{:S(2)}) collective-permute-start(bf16[64,1280]{1,0:T(8,128)(2,1)S(1)} %collective-permute-done.13.refs_9_.refs_6_), channel_id=1, source_target_pairs={{2,0},{6,2},{10,6},{14,10},{12,14},{8,12},{4,8},{0,4},{3,1},{7,3},... | collective-permute-start | bytes 491528 | tf_op jit(solution)/shard_map/ppermute | solution.py:363
  26.1 0.0 collective-permute-done.5.refs_4_
  26.1 0.7 %collective-permute-start.7 = (bf16[64,1280]{1,0:T(8,128)(2,1)S(1)}, bf16[64,1280]{1,0:T(8,128)(2,1)S(1)}, u32[]{:S(2)}, u32[]{:S(2)}) collective-permute-start(bf16[64,1280]{1,0:T(8,128)(2,1)S(1)} %collective-permute-done.5.refs_4_), channel_id=1, source_target_pairs={{0,2},{2,6},{6,10},{10,14},{14,12},{12,8},{8,4},{4,0},{1,3},{3,7},... | collective-permute-start | bytes 491528 | tf_op jit(solution)/shard_map/ppermute | solution.py:362
  26.8 2.6 %collective-permute-done.refs_1_ = bf16[4112,128]{1,0:T(8,128)(2,1)S(1)} collective-permute-done((bf16[4112,128]{1,0:T(8,128)(2,1)S(1)}, bf16[4112,128]{1,0:T(8,128)(2,1)S(1)}, u32[]{:S(2)}, u32[]{:S(2)}) %collective-permute-start) | collective-permute-done | bytes 1052704 | tf_op jit(solution)/shard_map/ppermute | solution.py:366
  29.4 0.8 %shard_map.85 = (f32[256,128]{1,0:T(8,128)S(1)}, f32[256,128]{1,0:T(8,128)S(1)}) custom-call(bf16[256,4096]{1,0:T(8,128)(2,1)S(1)} %copy-done, bf16[4112,128]{1,0:T(8,128)(2,1)S(1)} %collective-permute-done.refs_1_, s32[8,512]{1,0:T(8,128)S(1)} %shard_map.83.refs_2_.bounds_ref, bf16[64,1280]{1,0:T(8,128)(2,1)S(1)} %get-tuple-element.32.refs_3_, ...), custom_call_target="tpu_custom_call" | custom-call | flops 8589934592 | bytes 16777216 | tf_op jit(solution)/shard_map/pallas_call | solution.py:287
  30.2 0.1 collective-permute-start.18
  30.3 0.0 collective-permute-done.12.refs_8_.refs_5_
  30.3 0.0 collective-permute-done.6.refs_5_
  30.3 0.3 collective-permute-done.14.refs_10_.refs_7_
  30.6 0.8 %collective-permute-done.7.refs_6_ = bf16[64,1280]{1,0:T(8,128)(2,1)S(1)} collective-permute-done((bf16[64,1280]{1,0:T(8,128)(2,1)S(1)}, bf16[64,1280]{1,0:T(8,128)(2,1)S(1)}, u32[]{:S(2)}, u32[]{:S(2)}) %collective-permute-start.7) | collective-permute-done | bytes 163872 | tf_op jit(solution)/shard_map/ppermute | solution.py:362
  31.4 0.9 %shard_map.86 = (f32[128,128]{1,0:T(8,128)S(1)}, f32[128,128]{1,0:T(8,128)S(1)}) custom-call(bf16[256,4096]{1,0:T(8,128)(2,1)S(1)} %copy-done, bf16[4112,128]{1,0:T(8,128)(2,1)S(1)} %collective-permute-done.refs_1_, s32[8,512]{1,0:T(8,128)S(1)} %shard_map.83.refs_2_.bounds_ref, bf16[64,1280]{1,0:T(8,128)(2,1)S(1)} %collective-permute-done.2.refs_3_, ...), custom_call_target="tpu_custom_call" | custom-call | flops 8589934592 | bytes 16777216 | tf_op jit(solution)/shard_map/pallas_call | solution.py:287
  32.3 1.6 %collective-permute-start.16 = (f32[128,128]{1,0:T(8,128)S(1)}, f32[128,128]{1,0:T(8,128)S(1)}, u32[]{:S(2)}, u32[]{:S(2)}) collective-permute-start(f32[128,128]{1,0:T(8,128)S(1)} %get-tuple-element.40), channel_id=1, source_target_pairs={{0,16},{16,0},{1,17},{17,1},{2,18},{18,2},{3,19},{19,3},{4,20},{20... | collective-permute-start | bytes 196616 | tf_op jit(solution)/shard_map/ppermute | solution.py:381
  33.9 0.0 collective-permute-start.15
  33.9 2.7 %collective-permute-done.16.two = f32[128,128]{1,0:T(8,128)S(1)} collective-permute-done((f32[128,128]{1,0:T(8,128)S(1)}, f32[128,128]{1,0:T(8,128)S(1)}, u32[]{:S(2)}, u32[]{:S(2)}) %collective-permute-start.16) | collective-permute-done | bytes 65568 | tf_op jit(solution)/shard_map/ppermute | solution.py:381
  36.6 0.0 collective-permute-start.17
  36.6 0.0 collective-permute-done.15.one
  36.6 1.2 %collective-permute-done.17.three = f32[128,128]{1,0:T(8,128)S(1)} collective-permute-done((f32[128,128]{1,0:T(8,128)S(1)}, f32[128,128]{1,0:T(8,128)S(1)}, u32[]{:S(2)}, u32[]{:S(2)}) %collective-permute-start.17) | collective-permute-done | bytes 65568 | tf_op jit(solution)/shard_map/ppermute | solution.py:383
  37.9 0.0 collective-permute-done.18.far_ref
  37.9 1.1 %shard_map.87 = bf16[256,512]{1,0:T(8,128)(2,1)} custom-call(s32[8,512]{1,0:T(8,128)S(1)} %shard_map.83.refs_2_.bounds_ref, f32[128,128]{1,0:T(8,128)S(1)} %get-tuple-element.39.mine, f32[128,128]{1,0:T(8,128)S(1)} %collective-permute-done.15.one, f32[128,128]{1,0:T(8,128)S(1)} %collective-permute-done.16.two, f32[128,128]{1,0:T(8,128)S(1)} %collective-permute-done.17.three, ...), custom_call_target="tpu_custom_call" | custom-call | tf_op jit(solution)/shard_map/pallas_call | solution.py:386
  (3 shorter events, 0.0 us)
Async XLA Ops:
  1.6 7.2 %collective-permute-start.8 = (bf16[64,1280]{1,0:T(8,128)(2,1)S(1)}, bf16[64,1280]{1,0:T(8,128)(2,1)S(1)}, u32[]{:S(2)}, u32[]{:S(2)}) collective-permute-start(bf16[64,1280]{1,0:T(8,128)(2,1)S(1)} %get-tuple-element.33.refs_7_.refs_0_), channel_id=1, source_target_pairs={{2,0},{6,2},{10,6},{14,10},{12,14},{8,12},{4,8},{0,4},{3,1},{7,3},... | collective-permute-start | bytes 491528 | tf_op jit(solution)/shard_map/ppermute | solution.py:356
  4.7 7.1 %collective-permute-start.3 = (bf16[64,1280]{1,0:T(8,128)(2,1)S(1)}, bf16[64,1280]{1,0:T(8,128)(2,1)S(1)}, u32[]{:S(2)}, u32[]{:S(2)}) collective-permute-start(bf16[64,1280]{1,0:T(8,128)(2,1)S(1)} %get-tuple-element.32.refs_3_), channel_id=1, source_target_pairs={{0,2},{2,6},{6,10},{10,14},{14,12},{12,8},{8,4},{4,0},{1,3},{3,7},... | collective-permute-start | bytes 491528 | tf_op jit(solution)/shard_map/ppermute | solution.py:355
  4.7 24.7 %collective-permute-start = (bf16[4112,128]{1,0:T(8,128)(2,1)S(1)}, bf16[4112,128]{1,0:T(8,128)(2,1)S(1)}, u32[]{:S(2)}, u32[]{:S(2)}) collective-permute-start(bf16[4112,128]{1,0:T(8,128)(2,1)S(1)} %get-tuple-element.31), channel_id=1, source_target_pairs={{0,16},{16,0},{1,17},{17,1},{2,18},{18,2},{3,19},{19,3},{4,20},{20... | collective-permute-start | bytes 3158024 | tf_op jit(solution)/shard_map/ppermute | solution.py:366
  6.7 13.0 %slice-start = ((s8[8388608]{0:T(1024)(128)(4,1)}), s8[4194304]{0:T(1024)(128)(4,1)S(1)}, s32[]{:S(2)}) async-start(s8[8388608]{0:T(1024)(128)(4,1)} %bitcast.4), calls=%async_computation | async-start | bytes 8388608
  6.7 13.0 %slice-start.1 = ((s8[8388608]{0:T(1024)(128)(4,1)}), s8[4194304]{0:T(1024)(128)(4,1)S(1)}, s32[]{:S(2)}) async-start(s8[8388608]{0:T(1024)(128)(4,1)} %bitcast.4), calls=%async_computation.1 | async-start | bytes 8388608
  6.7 13.0 %copy-start = (bf16[256,4096]{1,0:T(8,128)(2,1)S(1)}, bf16[256,4096]{1,0:T(8,128)(2,1)}, u32[]{:S(2)}) copy-start(bf16[256,4096]{1,0:T(8,128)(2,1)} %refs_0_.1) | copy-start | bytes 6291460
  6.7 8.7 %collective-permute-start.10 = (bf16[64,1280]{1,0:T(8,128)(2,1)S(1)}, bf16[64,1280]{1,0:T(8,128)(2,1)S(1)}, u32[]{:S(2)}, u32[]{:S(2)}) collective-permute-start(bf16[64,1280]{1,0:T(8,128)(2,1)S(1)} %get-tuple-element.33.refs_7_.refs_0_), channel_id=1, source_target_pairs={{0,2},{2,6},{6,10},{10,14},{14,12},{12,8},{8,4},{4,0},{1,3},{3,7},... | collective-permute-start | bytes 491528 | tf_op jit(solution)/shard_map/ppermute | solution.py:357
  8.2 7.1 %collective-permute-start.1 = (bf16[64,1280]{1,0:T(8,128)(2,1)S(1)}, bf16[64,1280]{1,0:T(8,128)(2,1)S(1)}, u32[]{:S(2)}, u32[]{:S(2)}) collective-permute-start(bf16[64,1280]{1,0:T(8,128)(2,1)S(1)} %get-tuple-element.32.refs_3_), channel_id=1, source_target_pairs={{2,0},{6,2},{10,6},{14,10},{12,14},{8,12},{4,8},{0,4},{3,1},{7,3},... | collective-permute-start | bytes 491528 | tf_op jit(solution)/shard_map/ppermute | solution.py:358
  8.8 8.9 %collective-permute-start.9 = (bf16[64,1280]{1,0:T(8,128)(2,1)S(1)}, bf16[64,1280]{1,0:T(8,128)(2,1)S(1)}, u32[]{:S(2)}, u32[]{:S(2)}) collective-permute-start(bf16[64,1280]{1,0:T(8,128)(2,1)S(1)} %collective-permute-done.8.refs_9_.refs_2_), channel_id=1, source_target_pairs={{2,0},{6,2},{10,6},{14,10},{12,14},{8,12},{4,8},{0,4},{3,1},{7,3},... | collective-permute-start | bytes 491528 | tf_op jit(solution)/shard_map/ppermute | solution.py:356
  11.8 7.1 %collective-permute-start.4 = (bf16[64,1280]{1,0:T(8,128)(2,1)S(1)}, bf16[64,1280]{1,0:T(8,128)(2,1)S(1)}, u32[]{:S(2)}, u32[]{:S(2)}) collective-permute-start(bf16[64,1280]{1,0:T(8,128)(2,1)S(1)} %collective-permute-done.3.refs_4_), channel_id=1, source_target_pairs={{0,2},{2,6},{6,10},{10,14},{14,12},{12,8},{8,4},{4,0},{1,3},{3,7},... | collective-permute-start | bytes 491528 | tf_op jit(solution)/shard_map/ppermute | solution.py:355
  15.3 7.1 %collective-permute-start.11 = (bf16[64,1280]{1,0:T(8,128)(2,1)S(1)}, bf16[64,1280]{1,0:T(8,128)(2,1)S(1)}, u32[]{:S(2)}, u32[]{:S(2)}) collective-permute-start(bf16[64,1280]{1,0:T(8,128)(2,1)S(1)} %collective-permute-done.10.refs_8_.refs_1_), channel_id=1, source_target_pairs={{0,2},{2,6},{6,10},{10,14},{14,12},{12,8},{8,4},{4,0},{1,3},{3,7},... | collective-permute-start | bytes 491528 | tf_op jit(solution)/shard_map/ppermute | solution.py:357
  15.3 8.2 %collective-permute-start.2 = (bf16[64,1280]{1,0:T(8,128)(2,1)S(1)}, bf16[64,1280]{1,0:T(8,128)(2,1)S(1)}, u32[]{:S(2)}, u32[]{:S(2)}) collective-permute-start(bf16[64,1280]{1,0:T(8,128)(2,1)S(1)} %collective-permute-done.1.refs_5_), channel_id=1, source_target_pairs={{2,0},{6,2},{10,6},{14,10},{12,14},{8,12},{4,8},{0,4},{3,1},{7,3},... | collective-permute-start | bytes 491528 | tf_op jit(solution)/shard_map/ppermute | solution.py:358
  17.6 6.8 %collective-permute-start.13 = (bf16[64,1280]{1,0:T(8,128)(2,1)S(1)}, bf16[64,1280]{1,0:T(8,128)(2,1)S(1)}, u32[]{:S(2)}, u32[]{:S(2)}) collective-permute-start(bf16[64,1280]{1,0:T(8,128)(2,1)S(1)} %collective-permute-done.9.refs_7_.refs_4_), channel_id=1, source_target_pairs={{2,0},{6,2},{10,6},{14,10},{12,14},{8,12},{4,8},{0,4},{3,1},{7,3},... | collective-permute-start | bytes 491528 | tf_op jit(solution)/shard_map/ppermute | solution.py:356
  18.9 7.1 %collective-permute-start.5 = (bf16[64,1280]{1,0:T(8,128)(2,1)S(1)}, bf16[64,1280]{1,0:T(8,128)(2,1)S(1)}, u32[]{:S(2)}, u32[]{:S(2)}) collective-permute-start(bf16[64,1280]{1,0:T(8,128)(2,1)S(1)} %collective-permute-done.4.refs_6_), channel_id=1, source_target_pairs={{0,2},{2,6},{6,10},{10,14},{14,12},{12,8},{8,4},{4,0},{1,3},{3,7},... | collective-permute-start | bytes 491528 | tf_op jit(solution)/shard_map/ppermute | solution.py:355
  22.5 7.8 %collective-permute-start.12 = (bf16[64,1280]{1,0:T(8,128)(2,1)S(1)}, bf16[64,1280]{1,0:T(8,128)(2,1)S(1)}, u32[]{:S(2)}, u32[]{:S(2)}) collective-permute-start(bf16[64,1280]{1,0:T(8,128)(2,1)S(1)} %collective-permute-done.11.refs_10_.refs_3_), channel_id=1, source_target_pairs={{0,2},{2,6},{6,10},{10,14},{14,12},{12,8},{8,4},{4,0},{1,3},{3,7},... | collective-permute-start | bytes 491528 | tf_op jit(solution)/shard_map/ppermute | solution.py:357
  23.5 6.7 %collective-permute-start.6 = (bf16[64,1280]{1,0:T(8,128)(2,1)S(1)}, bf16[64,1280]{1,0:T(8,128)(2,1)S(1)}, u32[]{:S(2)}, u32[]{:S(2)}) collective-permute-start(bf16[64,1280]{1,0:T(8,128)(2,1)S(1)} %collective-permute-done.2.refs_3_), channel_id=1, source_target_pairs={{2,0},{6,2},{10,6},{14,10},{12,14},{8,12},{4,8},{0,4},{3,1},{7,3},... | collective-permute-start | bytes 491528 | tf_op jit(solution)/shard_map/ppermute | solution.py:358
  24.5 6.1 %collective-permute-start.14 = (bf16[64,1280]{1,0:T(8,128)(2,1)S(1)}, bf16[64,1280]{1,0:T(8,128)(2,1)S(1)}, u32[]{:S(2)}, u32[]{:S(2)}) collective-permute-start(bf16[64,1280]{1,0:T(8,128)(2,1)S(1)} %collective-permute-done.13.refs_9_.refs_6_), channel_id=1, source_target_pairs={{2,0},{6,2},{10,6},{14,10},{12,14},{8,12},{4,8},{0,4},{3,1},{7,3},... | collective-permute-start | bytes 491528 | tf_op jit(solution)/shard_map/ppermute | solution.py:363
  26.1 5.3 %collective-permute-start.7 = (bf16[64,1280]{1,0:T(8,128)(2,1)S(1)}, bf16[64,1280]{1,0:T(8,128)(2,1)S(1)}, u32[]{:S(2)}, u32[]{:S(2)}) collective-permute-start(bf16[64,1280]{1,0:T(8,128)(2,1)S(1)} %collective-permute-done.5.refs_4_), channel_id=1, source_target_pairs={{0,2},{2,6},{6,10},{10,14},{14,12},{12,8},{8,4},{4,0},{1,3},{3,7},... | collective-permute-start | bytes 491528 | tf_op jit(solution)/shard_map/ppermute | solution.py:362
  30.2 7.7 %collective-permute-start.18 = (f32[256,512]{1,0:T(8,128)S(1)}, f32[256,512]{1,0:T(8,128)S(1)}, u32[]{:S(2)}, u32[]{:S(2)}) collective-permute-start(f32[256,512]{1,0:T(8,128)S(1)} %get-tuple-element.42), channel_id=1, source_target_pairs={{0,1},{1,0},{2,3},{3,2},{4,5},{5,4},{6,7},{7,6},{8,9},{9,8},{10,11... | collective-permute-start | bytes 1572872 | tf_op jit(solution)/shard_map/ppermute | solution.py:377
  32.3 4.3 %collective-permute-start.16 = (f32[128,128]{1,0:T(8,128)S(1)}, f32[128,128]{1,0:T(8,128)S(1)}, u32[]{:S(2)}, u32[]{:S(2)}) collective-permute-start(f32[128,128]{1,0:T(8,128)S(1)} %get-tuple-element.40), channel_id=1, source_target_pairs={{0,16},{16,0},{1,17},{17,1},{2,18},{18,2},{3,19},{19,3},{4,20},{20... | collective-permute-start | bytes 196616 | tf_op jit(solution)/shard_map/ppermute | solution.py:381
  33.9 2.8 %collective-permute-start.15 = (f32[128,128]{1,0:T(8,128)S(1)}, f32[128,128]{1,0:T(8,128)S(1)}, u32[]{:S(2)}, u32[]{:S(2)}) collective-permute-start(f32[128,128]{1,0:T(8,128)S(1)} %get-tuple-element.39.mine), channel_id=1, source_target_pairs={{0,1},{1,0},{2,3},{3,2},{4,5},{5,4},{6,7},{7,6},{8,9},{9,8},{10,11... | collective-permute-start | bytes 196616 | tf_op jit(solution)/shard_map/ppermute | solution.py:382
  36.6 1.3 %collective-permute-start.17 = (f32[128,128]{1,0:T(8,128)S(1)}, f32[128,128]{1,0:T(8,128)S(1)}, u32[]{:S(2)}, u32[]{:S(2)}) collective-permute-start(f32[128,128]{1,0:T(8,128)S(1)} %collective-permute-done.16.two), channel_id=1, source_target_pairs={{0,1},{1,0},{2,3},{3,2},{4,5},{5,4},{6,7},{7,6},{8,9},{9,8},{10,11... | collective-permute-start | bytes 196616 | tf_op jit(solution)/shard_map/ppermute | solution.py:383

commit v12 on v11

--- a/solution.py
+++ b/solution.py
@@ -43,19 +43,46 @@
     return 2 * -(-columns // 1024) * 8
 
 
-def prologue_kernel(
+def shard_kernel(depth, factor_ref, factor_out_ref, first_ref, second_ref, sems):
+    cut = first_ref.shape[1]
+    here = pl.multiple_of(lax.axis_index("groups") * depth, 128)
+    after = pl.multiple_of(lax.axis_index("groups") * depth + cut, 128)
+    rest = depth - cut
+    copies = (
+        pltpu.make_async_copy(factor_ref.at[:, pl.ds(here, cut)], first_ref, sems.at[0]),
+        pltpu.make_async_copy(
+            factor_ref.at[:, pl.ds(after, rest)], second_ref.at[:, :rest], sems.at[1]
+        ),
+        pltpu.make_async_copy(factor_out_ref, second_ref.at[:, rest:], sems.at[2]),
+    )
+    for copy in copies:
+        copy.start()
+    for copy in copies:
+        copy.wait()
+
+
+def shard_call(factor, factor_out, depth):
+    rank, width = factor_out.shape
+    out = jax.ShapeDtypeStruct((rank, (depth + width) // 2), factor.dtype)
+    return pl.pallas_call(
+        functools.partial(shard_kernel, depth),
+        out_shape=(out, out),
+        in_specs=[HBM] * 2,
+        out_specs=(VMEM,) * 2,
+        scratch_shapes=[pltpu.SemaphoreType.DMA((3,))],
+        compiler_params=params(),
+    )(in_hbm(factor), in_hbm(factor_out))
+
+
+def rows_kernel(
     depth,
     rank,
     hidden_ref,
-    factor_ref,
-    factor_out_ref,
     demand_ref,
     lengths_ref,
     holder_ref,
     slots_ref,
     to_other_ref,
-    first_ref,
-    second_ref,
     bounds_ref,
     demand,
     lengths,
@@ -65,11 +92,8 @@
     hidden_sem,
 ):
     group, place = lax.axis_index("groups"), lax.axis_index("batch")
-    cut = first_ref.shape[1]
     rows = hidden_ref.shape[0]
-    here = pl.multiple_of(group * depth, 128)
     there = pl.multiple_of((1 - group) * depth, 128)
-    after = pl.multiple_of(group * depth + cut, 128)
     small = [
         pltpu.make_async_copy(demand_ref, demand, sems.at[0]),
         pltpu.make_async_copy(lengths_ref, lengths, sems.at[1]),
@@ -77,20 +101,13 @@
         pltpu.make_async_copy(slots_ref.at[pl.ds(place, 1)], slots, sems.at[3]),
     ]
     large = [
-        pltpu.make_async_copy(factor_ref.at[:, pl.ds(here, cut)], first_ref, sems.at[4]),
         pltpu.make_async_copy(
-            factor_ref.at[:, pl.ds(after, depth - cut)], second_ref.at[:, : depth - cut], sems.at[5]
-        ),
-        pltpu.make_async_copy(factor_out_ref, second_ref.at[:, depth - cut :], sems.at[6]),
+            hidden_ref.at[:, pl.ds(there + i * 128, 128)],
+            to_other_ref.at[i * rows : (i + 1) * rows],
+            hidden_sem.at[i],
+        )
+        for i in range(depth // 128)
     ]
-    for i in range(depth // 128):
-        large.append(
-            pltpu.make_async_copy(
-                hidden_ref.at[:, pl.ds(there + i * 128, 128)],
-                to_other_ref.at[i * rows : (i + 1) * rows],
-                hidden_sem.at[i],
-            )
-        )
     for copy in small + large:
         copy.start()
     for copy in small:
@@ -151,33 +168,30 @@
         copy.wait()
 
 
-def prologue(hidden, factor, factor_out, demand, lengths, holder_slot, slots):
+def rows_call(hidden, demand, lengths, holder_slot, slots, rank):
     rows, features = hidden.shape
-    rank, width = factor_out.shape
     depth = features // 2
-    cut = (depth + width) // 2
     count = slots.shape[2]
     tall = depth // 128 * rows + extra_rows(count * rank)
     return pl.pallas_call(
-        functools.partial(prologue_kernel, depth, rank),
+        functools.partial(rows_kernel, depth, rank),
         out_shape=(
             jax.ShapeDtypeStruct((tall, 128), hidden.dtype),
-            jax.ShapeDtypeStruct((rank, cut), factor.dtype),
-            jax.ShapeDtypeStruct((rank, cut), factor.dtype),
             jax.ShapeDtypeStruct((8, count * rank), I32),
         ),
-        in_specs=[HBM] * 7,
-        out_specs=(VMEM,) * 4,
+        in_specs=[HBM] * 5,
+        out_specs=(VMEM,) * 2,
         scratch_shapes=[
             pltpu.SMEM(demand.shape, I32),
             pltpu.SMEM(lengths.shape, I32),
             pltpu.SMEM(holder_slot.shape, I32),
             pltpu.SMEM((1, 1, count), I32),
-            pltpu.SemaphoreType.DMA((7,)),
+            pltpu.SemaphoreType.DMA((4,)),
             pltpu.SemaphoreType.DMA((depth // 128,)),
         ],
         compiler_params=params(),
-    )(*map(in_hbm, (hidden, factor, factor_out, demand, lengths, holder_slot, slots)))
+        cost_estimate=LONG,
+    )(*map(in_hbm, (hidden, demand, lengths, holder_slot, slots)))
 
 
 def mark_kernel(bounds_ref, out_ref):
@@ -337,14 +351,10 @@
         [[order[(order.index(me) - distance) % owners] for distance in distances]]
         for me in range(owners)
     ]
-    to_other, first, second, bounds = prologue(
-        hidden,
-        factor_in[0].T,
-        factor_out[0],
-        demand,
-        lengths,
-        holder_slot,
-        jnp.asarray(table, I32),
+    first, second = shard_call(factor_in[0].T, factor_out[0], depth)
+    first, rows_here = lax.optimization_barrier((first, hidden))
+    to_other, bounds = rows_call(
+        rows_here, demand, lengths, holder_slot, jnp.asarray(table, I32), rank
     )
 
     bounds, first_later, second_later = lax.optimization_barrier((mark(bounds), first, second))

time: 39.2 us -> 40.7 us (1.038)
  waiting for transfers between devices: 12.7 us -> 14 us
  Pallas kernels: 6.75 us -> 7.58 us
  starting transfers between devices: 19.4 us -> 18.8 us
    ppermute x3, starting transfers between devices: 6.68 us -> 2.26 us  [per_device(): d = lax.ppermute(behind[1], 'batch', backward)]
    ppermute x3, starting transfers between devices: 0.74 us -> 4.93 us  [per_device(): a = lax.ppermute(ahead[0], 'batch', forward)]
    ppermute x3, waiting for transfers between devices: 0.36 us -> 3.55 us  [per_device(): d = lax.ppermute(behind[1], 'batch', backward)]
    ppermute x3, starting transfers between devices: 2.65 us -> 5.43 us  [per_device(): b = lax.ppermute(ahead[1], 'batch', forward)]
    ppermute x3, starting transfers between devices: 3.48 us -> 1.52 us  [per_device(): c = lax.ppermute(behind[0], 'batch', backward)]
    ppermute x3, waiting for transfers between devices: 3.91 us -> 2.25 us  [per_device(): b = lax.ppermute(ahead[1], 'batch', forward)]
    ppermute x1, waiting for transfers between devices: 0.32 us -> 1.63 us  [per_device(): seconds.append(lax.ppermute(behind[1], 'batch', backward))]
    ppermute x1, waiting for transfers between devices: 2.64 us -> 1.49 us  [per_device(): other = lax.ppermute(to_other, 'groups', swap)]
  transfers between devices with their start and end apart: 19 -> 19, of which waited for: 10 -> 8; matrix products, arithmetic and copies ran while one was open for 0% -> 0% of each run, Pallas kernels for 10% -> 13%
where the time goes in v12:
time: 40.7 us; the launch traced here: 40.5 us
  starting transfers between devices  18.8 us (46%)
  waiting for transfers between devices  14 us (34%)
  Pallas kernels  7.58 us (19%)
    ppermute x3, starting transfers between devices, per_device(): b = lax.ppermute(ahead[1], 'batch', forward)  5.43 us
    ppermute x3, starting transfers between devices, per_device(): a = lax.ppermute(ahead[0], 'batch', forward)  4.93 us
    ppermute x1, waiting for transfers between devices, per_device(): two = lax.ppermute(theirs, 'groups', swap)  3.75 us
    ppermute x3, waiting for transfers between devices, per_device(): d = lax.ppermute(behind[1], 'batch', backward)  3.55 us
    pallas_call x1, Pallas kernels, base_call(): pl.pallas_call(base_kernel, out_shape=(out, out), in_specs=[VMEM] * 2, ou...  2.36 us
    ppermute x3, starting transfers between devices, per_device(): d = lax.ppermute(behind[1], 'batch', backward)  2.26 us
    ppermute x3, waiting for transfers between devices, per_device(): b = lax.ppermute(ahead[1], 'batch', forward)  2.25 us
    ppermute x1, starting transfers between devices, per_device(): other = lax.ppermute(to_other, 'groups', swap)  1.97 us
  transfers between devices with their start and end apart: 19, of which 8 were waited for; matrix products, arithmetic and copies ran while one was open for 0% of the time, Pallas kernels for 13%

profile of v12, /device:TPU:0, one launch (start us, length us, event | category | flops | bytes accessed | tf_op | source)
XLA Modules:
  0.0 40.5 jit_solution(13460865544133239734)
XLA Ops:
  0.0 1.0 %shard_map.82 = (bf16[64,1280]{1,0:T(8,128)(2,1)S(1)}, bf16[64,1280]{1,0:T(8,128)(2,1)S(1)}) custom-call(bf16[64,4096]{1,0:T(8,128)(2,1)} %bitcast.6, bf16[64,512]{1,0:T(8,128)(2,1)} %bitcast.7), custom_call_target="tpu_custom_call" | custom-call | tf_op jit(solution)/shard_map/pallas_call | solution.py:67
  1.0 3.0 %collective-permute-start.3 = (bf16[64,1280]{1,0:T(8,128)(2,1)S(1)}, bf16[64,1280]{1,0:T(8,128)(2,1)S(1)}, u32[]{:S(2)}, u32[]{:S(2)}) collective-permute-start(bf16[64,1280]{1,0:T(8,128)(2,1)S(1)} %get-tuple-element.36.refs_3_), channel_id=1, source_target_pairs={{0,2},{2,6},{6,10},{10,14},{14,12},{12,8},{8,4},{4,0},{1,3},{3,7},... | collective-permute-start | bytes 491528 | tf_op jit(solution)/shard_map/ppermute | solution.py:365
  4.0 0.2 collective-permute-start.8
  4.2 1.4 %shard_map.83 = (bf16[4112,128]{1,0:T(8,128)(2,1)S(1)}, s32[8,512]{1,0:T(8,128)S(1)}) custom-call(bf16[256,4096]{1,0:T(8,128)(2,1)} %refs_0_.1, s32[1,4]{1,0:T(1,128)} %demand_ref.1, s32[1,4]{1,0:T(1,128)} %lengths_ref.1, s32[8]{0:T(128)} %holder_ref.1, s32[8,1,8]{2,1,0:T(1,128)} %constant.2.clone.slots_ref), custom_call_target="tpu_custom_call" | custom-call | flops 8589934592 | bytes 16777216 | tf_op jit(solution)/shard_map/pallas_call | solution.py:176
  5.6 2.0 %collective-permute-start = (bf16[4112,128]{1,0:T(8,128)(2,1)S(1)}, bf16[4112,128]{1,0:T(8,128)(2,1)S(1)}, u32[]{:S(2)}, u32[]{:S(2)}) collective-permute-start(bf16[4112,128]{1,0:T(8,128)(2,1)S(1)} %get-tuple-element.35), channel_id=1, source_target_pairs={{0,16},{16,0},{1,17},{17,1},{2,18},{18,2},{3,19},{19,3},{4,20},{20... | collective-permute-start | bytes 3158024 | tf_op jit(solution)/shard_map/ppermute | solution.py:376
  7.6 0.0 slice-start
  7.6 1.5 %collective-permute-start.10 = (bf16[64,1280]{1,0:T(8,128)(2,1)S(1)}, bf16[64,1280]{1,0:T(8,128)(2,1)S(1)}, u32[]{:S(2)}, u32[]{:S(2)}) collective-permute-start(bf16[64,1280]{1,0:T(8,128)(2,1)S(1)} %get-tuple-element.37.refs_7_.refs_0_), channel_id=1, source_target_pairs={{0,2},{2,6},{6,10},{10,14},{14,12},{12,8},{8,4},{4,0},{1,3},{3,7},... | collective-permute-start | bytes 491528 | tf_op jit(solution)/shard_map/ppermute | solution.py:367
  9.1 0.5 %collective-permute-start.1 = (bf16[64,1280]{1,0:T(8,128)(2,1)S(1)}, bf16[64,1280]{1,0:T(8,128)(2,1)S(1)}, u32[]{:S(2)}, u32[]{:S(2)}) collective-permute-start(bf16[64,1280]{1,0:T(8,128)(2,1)S(1)} %get-tuple-element.36.refs_3_), channel_id=1, source_target_pairs={{2,0},{6,2},{10,6},{14,10},{12,14},{8,12},{4,8},{0,4},{3,1},{7,3},... | collective-permute-start | bytes 491528 | tf_op jit(solution)/shard_map/ppermute | solution.py:368
  9.7 0.0 collective-permute-done.8.refs_9_.refs_2_
  9.7 1.6 %collective-permute-start.9 = (bf16[64,1280]{1,0:T(8,128)(2,1)S(1)}, bf16[64,1280]{1,0:T(8,128)(2,1)S(1)}, u32[]{:S(2)}, u32[]{:S(2)}) collective-permute-start(bf16[64,1280]{1,0:T(8,128)(2,1)S(1)} %collective-permute-done.8.refs_9_.refs_2_), channel_id=1, source_target_pairs={{2,0},{6,2},{10,6},{14,10},{12,14},{8,12},{4,8},{0,4},{3,1},{7,3},... | collective-permute-start | bytes 491528 | tf_op jit(solution)/shard_map/ppermute | solution.py:366
  11.2 0.0 collective-permute-done.3.refs_4_
  11.2 0.5 %collective-permute-start.4 = (bf16[64,1280]{1,0:T(8,128)(2,1)S(1)}, bf16[64,1280]{1,0:T(8,128)(2,1)S(1)}, u32[]{:S(2)}, u32[]{:S(2)}) collective-permute-start(bf16[64,1280]{1,0:T(8,128)(2,1)S(1)} %collective-permute-done.3.refs_4_), channel_id=1, source_target_pairs={{0,2},{2,6},{6,10},{10,14},{14,12},{12,8},{8,4},{4,0},{1,3},{3,7},... | collective-permute-start | bytes 491528 | tf_op jit(solution)/shard_map/ppermute | solution.py:365
  11.7 2.2 %collective-permute-done.10.refs_8_.refs_1_ = bf16[64,1280]{1,0:T(8,128)(2,1)S(1)} collective-permute-done((bf16[64,1280]{1,0:T(8,128)(2,1)S(1)}, bf16[64,1280]{1,0:T(8,128)(2,1)S(1)}, u32[]{:S(2)}, u32[]{:S(2)}) %collective-permute-start.10) | collective-permute-done | bytes 163872 | tf_op jit(solution)/shard_map/ppermute | solution.py:367
  13.9 2.3 %collective-permute-start.11 = (bf16[64,1280]{1,0:T(8,128)(2,1)S(1)}, bf16[64,1280]{1,0:T(8,128)(2,1)S(1)}, u32[]{:S(2)}, u32[]{:S(2)}) collective-permute-start(bf16[64,1280]{1,0:T(8,128)(2,1)S(1)} %collective-permute-done.10.refs_8_.refs_1_), channel_id=1, source_target_pairs={{0,2},{2,6},{6,10},{10,14},{14,12},{12,8},{8,4},{4,0},{1,3},{3,7},... | collective-permute-start | bytes 491528 | tf_op jit(solution)/shard_map/ppermute | solution.py:367
  16.2 0.1 collective-permute-done.1.refs_5_
  16.3 0.5 %collective-permute-start.2 = (bf16[64,1280]{1,0:T(8,128)(2,1)S(1)}, bf16[64,1280]{1,0:T(8,128)(2,1)S(1)}, u32[]{:S(2)}, u32[]{:S(2)}) collective-permute-start(bf16[64,1280]{1,0:T(8,128)(2,1)S(1)} %collective-permute-done.1.refs_5_), channel_id=1, source_target_pairs={{2,0},{6,2},{10,6},{14,10},{12,14},{8,12},{4,8},{0,4},{3,1},{7,3},... | collective-permute-start | bytes 491528 | tf_op jit(solution)/shard_map/ppermute | solution.py:368
  16.8 3.0 %collective-permute-done.9.refs_7_.refs_4_ = bf16[64,1280]{1,0:T(8,128)(2,1)S(1)} collective-permute-done((bf16[64,1280]{1,0:T(8,128)(2,1)S(1)}, bf16[64,1280]{1,0:T(8,128)(2,1)S(1)}, u32[]{:S(2)}, u32[]{:S(2)}) %collective-permute-start.9) | collective-permute-done | bytes 163872 | tf_op jit(solution)/shard_map/ppermute | solution.py:366
  19.8 0.5 %collective-permute-start.13 = (bf16[64,1280]{1,0:T(8,128)(2,1)S(1)}, bf16[64,1280]{1,0:T(8,128)(2,1)S(1)}, u32[]{:S(2)}, u32[]{:S(2)}) collective-permute-start(bf16[64,1280]{1,0:T(8,128)(2,1)S(1)} %collective-permute-done.9.refs_7_.refs_4_), channel_id=1, source_target_pairs={{2,0},{6,2},{10,6},{14,10},{12,14},{8,12},{4,8},{0,4},{3,1},{7,3},... | collective-permute-start | bytes 491528 | tf_op jit(solution)/shard_map/ppermute | solution.py:366
  20.3 0.0 collective-permute-done.4.refs_6_
  20.3 1.5 %collective-permute-start.5 = (bf16[64,1280]{1,0:T(8,128)(2,1)S(1)}, bf16[64,1280]{1,0:T(8,128)(2,1)S(1)}, u32[]{:S(2)}, u32[]{:S(2)}) collective-permute-start(bf16[64,1280]{1,0:T(8,128)(2,1)S(1)} %collective-permute-done.4.refs_6_), channel_id=1, source_target_pairs={{0,2},{2,6},{6,10},{10,14},{14,12},{12,8},{8,4},{4,0},{1,3},{3,7},... | collective-permute-start | bytes 491528 | tf_op jit(solution)/shard_map/ppermute | solution.py:365
  21.8 0.0 slice-done
  21.8 0.0 slice-done.1
  21.8 0.0 copy-done
  21.8 2.4 %shard_map.85 = (f32[256,512]{1,0:T(8,128)S(1)}, f32[256,512]{1,0:T(8,128)S(1)}) custom-call(bf16[256,4096]{1,0:T(8,128)(2,1)S(1)} %copy-done, bf16[4096,1024]{1,0:T(8,128)(2,1)S(1)} %bitcast.5), custom_call_target="tpu_custom_call" | custom-call | bytes 4194304 | tf_op jit(solution)/shard_map/pallas_call | solution.py:224
  24.2 0.0 collective-permute-done.11.refs_10_.refs_3_
  24.2 1.6 %collective-permute-start.12 = (bf16[64,1280]{1,0:T(8,128)(2,1)S(1)}, bf16[64,1280]{1,0:T(8,128)(2,1)S(1)}, u32[]{:S(2)}, u32[]{:S(2)}) collective-permute-start(bf16[64,1280]{1,0:T(8,128)(2,1)S(1)} %collective-permute-done.11.refs_10_.refs_3_), channel_id=1, source_target_pairs={{0,2},{2,6},{6,10},{10,14},{14,12},{12,8},{8,4},{4,0},{1,3},{3,7},... | collective-permute-start | bytes 491528 | tf_op jit(solution)/shard_map/ppermute | solution.py:367
  25.8 0.0 collective-permute-done.2.refs_3_
  25.8 0.5 %collective-permute-start.6 = (bf16[64,1280]{1,0:T(8,128)(2,1)S(1)}, bf16[64,1280]{1,0:T(8,128)(2,1)S(1)}, u32[]{:S(2)}, u32[]{:S(2)}) collective-permute-start(bf16[64,1280]{1,0:T(8,128)(2,1)S(1)} %collective-permute-done.2.refs_3_), channel_id=1, source_target_pairs={{2,0},{6,2},{10,6},{14,10},{12,14},{8,12},{4,8},{0,4},{3,1},{7,3},... | collective-permute-start | bytes 491528 | tf_op jit(solution)/shard_map/ppermute | solution.py:368
  26.3 0.6 %collective-permute-done.13.refs_9_.refs_6_ = bf16[64,1280]{1,0:T(8,128)(2,1)S(1)} collective-permute-done((bf16[64,1280]{1,0:T(8,128)(2,1)S(1)}, bf16[64,1280]{1,0:T(8,128)(2,1)S(1)}, u32[]{:S(2)}, u32[]{:S(2)}) %collective-permute-start.13) | collective-permute-done | bytes 163872 | tf_op jit(solution)/shard_map/ppermute | solution.py:366
  26.8 0.4 %collective-permute-start.14 = (bf16[64,1280]{1,0:T(8,128)(2,1)S(1)}, bf16[64,1280]{1,0:T(8,128)(2,1)S(1)}, u32[]{:S(2)}, u32[]{:S(2)}) collective-permute-start(bf16[64,1280]{1,0:T(8,128)(2,1)S(1)} %collective-permute-done.13.refs_9_.refs_6_), channel_id=1, source_target_pairs={{2,0},{6,2},{10,6},{14,10},{12,14},{8,12},{4,8},{0,4},{3,1},{7,3},... | collective-permute-start | bytes 491528 | tf_op jit(solution)/shard_map/ppermute | solution.py:373
  27.3 0.0 collective-permute-done.5.refs_4_
  27.3 1.6 %collective-permute-start.7 = (bf16[64,1280]{1,0:T(8,128)(2,1)S(1)}, bf16[64,1280]{1,0:T(8,128)(2,1)S(1)}, u32[]{:S(2)}, u32[]{:S(2)}) collective-permute-start(bf16[64,1280]{1,0:T(8,128)(2,1)S(1)} %collective-permute-done.5.refs_4_), channel_id=1, source_target_pairs={{0,2},{2,6},{6,10},{10,14},{14,12},{12,8},{8,4},{4,0},{1,3},{3,7},... | collective-permute-start | bytes 491528 | tf_op jit(solution)/shard_map/ppermute | solution.py:372
  28.9 1.5 %collective-permute-done.refs_1_ = bf16[4112,128]{1,0:T(8,128)(2,1)S(1)} collective-permute-done((bf16[4112,128]{1,0:T(8,128)(2,1)S(1)}, bf16[4112,128]{1,0:T(8,128)(2,1)S(1)}, u32[]{:S(2)}, u32[]{:S(2)}) %collective-permute-start) | collective-permute-done | bytes 1052704 | tf_op jit(solution)/shard_map/ppermute | solution.py:376
  30.4 0.8 %shard_map.86 = (f32[256,128]{1,0:T(8,128)S(1)}, f32[256,128]{1,0:T(8,128)S(1)}) custom-call(bf16[256,4096]{1,0:T(8,128)(2,1)S(1)} %copy-done, bf16[4112,128]{1,0:T(8,128)(2,1)S(1)} %collective-permute-done.refs_1_, s32[8,512]{1,0:T(8,128)S(1)} %shard_map.84.refs_2_.bounds_ref, bf16[64,1280]{1,0:T(8,128)(2,1)S(1)} %get-tuple-element.36.refs_3_, ...), custom_call_target="tpu_custom_call" | custom-call | flops 8589934592 | bytes 16777216 | tf_op jit(solution)/shard_map/pallas_call | solution.py:301
  31.2 0.1 collective-permute-start.18
  31.2 0.0 collective-permute-done.12.refs_8_.refs_5_
  31.3 0.0 collective-permute-done.6.refs_5_
  31.3 1.6 %collective-permute-done.14.refs_10_.refs_7_ = bf16[64,1280]{1,0:T(8,128)(2,1)S(1)} collective-permute-done((bf16[64,1280]{1,0:T(8,128)(2,1)S(1)}, bf16[64,1280]{1,0:T(8,128)(2,1)S(1)}, u32[]{:S(2)}, u32[]{:S(2)}) %collective-permute-start.14) | collective-permute-done | bytes 163872 | tf_op jit(solution)/shard_map/ppermute | solution.py:373
  32.9 0.0 collective-permute-done.7.refs_6_
  32.9 0.9 %shard_map.87 = (f32[128,128]{1,0:T(8,128)S(1)}, f32[128,128]{1,0:T(8,128)S(1)}) custom-call(bf16[256,4096]{1,0:T(8,128)(2,1)S(1)} %copy-done, bf16[4112,128]{1,0:T(8,128)(2,1)S(1)} %collective-permute-done.refs_1_, s32[8,512]{1,0:T(8,128)S(1)} %shard_map.84.refs_2_.bounds_ref, bf16[64,1280]{1,0:T(8,128)(2,1)S(1)} %collective-permute-done.2.refs_3_, ...), custom_call_target="tpu_custom_call" | custom-call | flops 8589934592 | bytes 16777216 | tf_op jit(solution)/shard_map/pallas_call | solution.py:301
  33.8 0.6 %collective-permute-start.16 = (f32[128,128]{1,0:T(8,128)S(1)}, f32[128,128]{1,0:T(8,128)S(1)}, u32[]{:S(2)}, u32[]{:S(2)}) collective-permute-start(f32[128,128]{1,0:T(8,128)S(1)} %get-tuple-element.44), channel_id=1, source_target_pairs={{0,16},{16,0},{1,17},{17,1},{2,18},{18,2},{3,19},{19,3},{4,20},{20... | collective-permute-start | bytes 196616 | tf_op jit(solution)/shard_map/ppermute | solution.py:391
  34.3 0.0 collective-permute-start.15
  34.3 3.8 %collective-permute-done.16.two = f32[128,128]{1,0:T(8,128)S(1)} collective-permute-done((f32[128,128]{1,0:T(8,128)S(1)}, f32[128,128]{1,0:T(8,128)S(1)}, u32[]{:S(2)}, u32[]{:S(2)}) %collective-permute-start.16) | collective-permute-done | bytes 65568 | tf_op jit(solution)/shard_map/ppermute | solution.py:391
  38.1 0.0 collective-permute-start.17
  38.1 0.0 collective-permute-done.15.one
  38.1 1.2 %collective-permute-done.17.three = f32[128,128]{1,0:T(8,128)S(1)} collective-permute-done((f32[128,128]{1,0:T(8,128)S(1)}, f32[128,128]{1,0:T(8,128)S(1)}, u32[]{:S(2)}, u32[]{:S(2)}) %collective-permute-start.17) | collective-permute-done | bytes 65568 | tf_op jit(solution)/shard_map/ppermute | solution.py:393
  39.4 0.0 collective-permute-done.18.far_ref
  39.4 1.1 %shard_map.88 = bf16[256,512]{1,0:T(8,128)(2,1)} custom-call(s32[8,512]{1,0:T(8,128)S(1)} %shard_map.84.refs_2_.bounds_ref, f32[128,128]{1,0:T(8,128)S(1)} %get-tuple-element.43.mine, f32[128,128]{1,0:T(8,128)S(1)} %collective-permute-done.15.one, f32[128,128]{1,0:T(8,128)S(1)} %collective-permute-done.16.two, f32[128,128]{1,0:T(8,128)S(1)} %collective-permute-done.17.three, ...), custom_call_target="tpu_custom_call" | custom-call | tf_op jit(solution)/shard_map/pallas_call | solution.py:396
  (4 shorter events, 0.0 us)
Async XLA Ops:
  1.0 10.2 %collective-permute-start.3 = (bf16[64,1280]{1,0:T(8,128)(2,1)S(1)}, bf16[64,1280]{1,0:T(8,128)(2,1)S(1)}, u32[]{:S(2)}, u32[]{:S(2)}) collective-permute-start(bf16[64,1280]{1,0:T(8,128)(2,1)S(1)} %get-tuple-element.36.refs_3_), channel_id=1, source_target_pairs={{0,2},{2,6},{6,10},{10,14},{14,12},{12,8},{8,4},{4,0},{1,3},{3,7},... | collective-permute-start | bytes 491528 | tf_op jit(solution)/shard_map/ppermute | solution.py:365
  4.0 5.7 %collective-permute-start.8 = (bf16[64,1280]{1,0:T(8,128)(2,1)S(1)}, bf16[64,1280]{1,0:T(8,128)(2,1)S(1)}, u32[]{:S(2)}, u32[]{:S(2)}) collective-permute-start(bf16[64,1280]{1,0:T(8,128)(2,1)S(1)} %get-tuple-element.37.refs_7_.refs_0_), channel_id=1, source_target_pairs={{2,0},{6,2},{10,6},{14,10},{12,14},{8,12},{4,8},{0,4},{3,1},{7,3},... | collective-permute-start | bytes 491528 | tf_op jit(solution)/shard_map/ppermute | solution.py:366
  5.6 24.8 %collective-permute-start = (bf16[4112,128]{1,0:T(8,128)(2,1)S(1)}, bf16[4112,128]{1,0:T(8,128)(2,1)S(1)}, u32[]{:S(2)}, u32[]{:S(2)}) collective-permute-start(bf16[4112,128]{1,0:T(8,128)(2,1)S(1)} %get-tuple-element.35), channel_id=1, source_target_pairs={{0,16},{16,0},{1,17},{17,1},{2,18},{18,2},{3,19},{19,3},{4,20},{20... | collective-permute-start | bytes 3158024 | tf_op jit(solution)/shard_map/ppermute | solution.py:376
  7.6 14.2 %slice-start = ((s8[8388608]{0:T(1024)(128)(4,1)}), s8[4194304]{0:T(1024)(128)(4,1)S(1)}, s32[]{:S(2)}) async-start(s8[8388608]{0:T(1024)(128)(4,1)} %bitcast.4), calls=%async_computation | async-start | bytes 8388608
  7.6 14.2 %slice-start.1 = ((s8[8388608]{0:T(1024)(128)(4,1)}), s8[4194304]{0:T(1024)(128)(4,1)S(1)}, s32[]{:S(2)}) async-start(s8[8388608]{0:T(1024)(128)(4,1)} %bitcast.4), calls=%async_computation.1 | async-start | bytes 8388608
  7.6 14.2 %copy-start = (bf16[256,4096]{1,0:T(8,128)(2,1)S(1)}, bf16[256,4096]{1,0:T(8,128)(2,1)}, u32[]{:S(2)}) copy-start(bf16[256,4096]{1,0:T(8,128)(2,1)} %refs_0_.1) | copy-start | bytes 6291460
  7.6 6.4 %collective-permute-start.10 = (bf16[64,1280]{1,0:T(8,128)(2,1)S(1)}, bf16[64,1280]{1,0:T(8,128)(2,1)S(1)}, u32[]{:S(2)}, u32[]{:S(2)}) collective-permute-start(bf16[64,1280]{1,0:T(8,128)(2,1)S(1)} %get-tuple-element.37.refs_7_.refs_0_), channel_id=1, source_target_pairs={{0,2},{2,6},{6,10},{10,14},{14,12},{12,8},{8,4},{4,0},{1,3},{3,7},... | collective-permute-start | bytes 491528 | tf_op jit(solution)/shard_map/ppermute | solution.py:367
  9.1 7.1 %collective-permute-start.1 = (bf16[64,1280]{1,0:T(8,128)(2,1)S(1)}, bf16[64,1280]{1,0:T(8,128)(2,1)S(1)}, u32[]{:S(2)}, u32[]{:S(2)}) collective-permute-start(bf16[64,1280]{1,0:T(8,128)(2,1)S(1)} %get-tuple-element.36.refs_3_), channel_id=1, source_target_pairs={{2,0},{6,2},{10,6},{14,10},{12,14},{8,12},{4,8},{0,4},{3,1},{7,3},... | collective-permute-start | bytes 491528 | tf_op jit(solution)/shard_map/ppermute | solution.py:368
  9.7 10.1 %collective-permute-start.9 = (bf16[64,1280]{1,0:T(8,128)(2,1)S(1)}, bf16[64,1280]{1,0:T(8,128)(2,1)S(1)}, u32[]{:S(2)}, u32[]{:S(2)}) collective-permute-start(bf16[64,1280]{1,0:T(8,128)(2,1)S(1)} %collective-permute-done.8.refs_9_.refs_2_), channel_id=1, source_target_pairs={{2,0},{6,2},{10,6},{14,10},{12,14},{8,12},{4,8},{0,4},{3,1},{7,3},... | collective-permute-start | bytes 491528 | tf_op jit(solution)/shard_map/ppermute | solution.py:366
  11.2 9.1 %collective-permute-start.4 = (bf16[64,1280]{1,0:T(8,128)(2,1)S(1)}, bf16[64,1280]{1,0:T(8,128)(2,1)S(1)}, u32[]{:S(2)}, u32[]{:S(2)}) collective-permute-start(bf16[64,1280]{1,0:T(8,128)(2,1)S(1)} %collective-permute-done.3.refs_4_), channel_id=1, source_target_pairs={{0,2},{2,6},{6,10},{10,14},{14,12},{12,8},{8,4},{4,0},{1,3},{3,7},... | collective-permute-start | bytes 491528 | tf_op jit(solution)/shard_map/ppermute | solution.py:365
  13.9 10.2 %collective-permute-start.11 = (bf16[64,1280]{1,0:T(8,128)(2,1)S(1)}, bf16[64,1280]{1,0:T(8,128)(2,1)S(1)}, u32[]{:S(2)}, u32[]{:S(2)}) collective-permute-start(bf16[64,1280]{1,0:T(8,128)(2,1)S(1)} %collective-permute-done.10.refs_8_.refs_1_), channel_id=1, source_target_pairs={{0,2},{2,6},{6,10},{10,14},{14,12},{12,8},{8,4},{4,0},{1,3},{3,7},... | collective-permute-start | bytes 491528 | tf_op jit(solution)/shard_map/ppermute | solution.py:367
  16.3 9.6 %collective-permute-start.2 = (bf16[64,1280]{1,0:T(8,128)(2,1)S(1)}, bf16[64,1280]{1,0:T(8,128)(2,1)S(1)}, u32[]{:S(2)}, u32[]{:S(2)}) collective-permute-start(bf16[64,1280]{1,0:T(8,128)(2,1)S(1)} %collective-permute-done.1.refs_5_), channel_id=1, source_target_pairs={{2,0},{6,2},{10,6},{14,10},{12,14},{8,12},{4,8},{0,4},{3,1},{7,3},... | collective-permute-start | bytes 491528 | tf_op jit(solution)/shard_map/ppermute | solution.py:368
  19.8 7.1 %collective-permute-start.13 = (bf16[64,1280]{1,0:T(8,128)(2,1)S(1)}, bf16[64,1280]{1,0:T(8,128)(2,1)S(1)}, u32[]{:S(2)}, u32[]{:S(2)}) collective-permute-start(bf16[64,1280]{1,0:T(8,128)(2,1)S(1)} %collective-permute-done.9.refs_7_.refs_4_), channel_id=1, source_target_pairs={{2,0},{6,2},{10,6},{14,10},{12,14},{8,12},{4,8},{0,4},{3,1},{7,3},... | collective-permute-start | bytes 491528 | tf_op jit(solution)/shard_map/ppermute | solution.py:366
  20.3 7.0 %collective-permute-start.5 = (bf16[64,1280]{1,0:T(8,128)(2,1)S(1)}, bf16[64,1280]{1,0:T(8,128)(2,1)S(1)}, u32[]{:S(2)}, u32[]{:S(2)}) collective-permute-start(bf16[64,1280]{1,0:T(8,128)(2,1)S(1)} %collective-permute-done.4.refs_6_), channel_id=1, source_target_pairs={{0,2},{2,6},{6,10},{10,14},{14,12},{12,8},{8,4},{4,0},{1,3},{3,7},... | collective-permute-start | bytes 491528 | tf_op jit(solution)/shard_map/ppermute | solution.py:365
  24.2 7.1 %collective-permute-start.12 = (bf16[64,1280]{1,0:T(8,128)(2,1)S(1)}, bf16[64,1280]{1,0:T(8,128)(2,1)S(1)}, u32[]{:S(2)}, u32[]{:S(2)}) collective-permute-start(bf16[64,1280]{1,0:T(8,128)(2,1)S(1)} %collective-permute-done.11.refs_10_.refs_3_), channel_id=1, source_target_pairs={{0,2},{2,6},{6,10},{10,14},{14,12},{12,8},{8,4},{4,0},{1,3},{3,7},... | collective-permute-start | bytes 491528 | tf_op jit(solution)/shard_map/ppermute | solution.py:367
  25.8 5.4 %collective-permute-start.6 = (bf16[64,1280]{1,0:T(8,128)(2,1)S(1)}, bf16[64,1280]{1,0:T(8,128)(2,1)S(1)}, u32[]{:S(2)}, u32[]{:S(2)}) collective-permute-start(bf16[64,1280]{1,0:T(8,128)(2,1)S(1)} %collective-permute-done.2.refs_3_), channel_id=1, source_target_pairs={{2,0},{6,2},{10,6},{14,10},{12,14},{8,12},{4,8},{0,4},{3,1},{7,3},... | collective-permute-start | bytes 491528 | tf_op jit(solution)/shard_map/ppermute | solution.py:368
  26.8 6.1 %collective-permute-start.14 = (bf16[64,1280]{1,0:T(8,128)(2,1)S(1)}, bf16[64,1280]{1,0:T(8,128)(2,1)S(1)}, u32[]{:S(2)}, u32[]{:S(2)}) collective-permute-start(bf16[64,1280]{1,0:T(8,128)(2,1)S(1)} %collective-permute-done.13.refs_9_.refs_6_), channel_id=1, source_target_pairs={{2,0},{6,2},{10,6},{14,10},{12,14},{8,12},{4,8},{0,4},{3,1},{7,3},... | collective-permute-start | bytes 491528 | tf_op jit(solution)/shard_map/ppermute | solution.py:373
  27.3 5.6 %collective-permute-start.7 = (bf16[64,1280]{1,0:T(8,128)(2,1)S(1)}, bf16[64,1280]{1,0:T(8,128)(2,1)S(1)}, u32[]{:S(2)}, u32[]{:S(2)}) collective-permute-start(bf16[64,1280]{1,0:T(8,128)(2,1)S(1)} %collective-permute-done.5.refs_4_), channel_id=1, source_target_pairs={{0,2},{2,6},{6,10},{10,14},{14,12},{12,8},{8,4},{4,0},{1,3},{3,7},... | collective-permute-start | bytes 491528 | tf_op jit(solution)/shard_map/ppermute | solution.py:372
  31.2 8.2 %collective-permute-start.18 = (f32[256,512]{1,0:T(8,128)S(1)}, f32[256,512]{1,0:T(8,128)S(1)}, u32[]{:S(2)}, u32[]{:S(2)}) collective-permute-start(f32[256,512]{1,0:T(8,128)S(1)} %get-tuple-element.46), channel_id=1, source_target_pairs={{0,1},{1,0},{2,3},{3,2},{4,5},{5,4},{6,7},{7,6},{8,9},{9,8},{10,11... | collective-permute-start | bytes 1572872 | tf_op jit(solution)/shard_map/ppermute | solution.py:387
  33.8 4.3 %collective-permute-start.16 = (f32[128,128]{1,0:T(8,128)S(1)}, f32[128,128]{1,0:T(8,128)S(1)}, u32[]{:S(2)}, u32[]{:S(2)}) collective-permute-start(f32[128,128]{1,0:T(8,128)S(1)} %get-tuple-element.44), channel_id=1, source_target_pairs={{0,16},{16,0},{1,17},{17,1},{2,18},{18,2},{3,19},{19,3},{4,20},{20... | collective-permute-start | bytes 196616 | tf_op jit(solution)/shard_map/ppermute | solution.py:391
  34.3 3.8 %collective-permute-start.15 = (f32[128,128]{1,0:T(8,128)S(1)}, f32[128,128]{1,0:T(8,128)S(1)}, u32[]{:S(2)}, u32[]{:S(2)}) collective-permute-start(f32[128,128]{1,0:T(8,128)S(1)} %get-tuple-element.43.mine), channel_id=1, source_target_pairs={{0,1},{1,0},{2,3},{3,2},{4,5},{5,4},{6,7},{7,6},{8,9},{9,8},{10,11... | collective-permute-start | bytes 196616 | tf_op jit(solution)/shard_map/ppermute | solution.py:392
  38.1 1.3 %collective-permute-start.17 = (f32[128,128]{1,0:T(8,128)S(1)}, f32[128,128]{1,0:T(8,128)S(1)}, u32[]{:S(2)}, u32[]{:S(2)}) collective-permute-start(f32[128,128]{1,0:T(8,128)S(1)} %collective-permute-done.16.two), channel_id=1, source_target_pairs={{0,1},{1,0},{2,3},{3,2},{4,5},{5,4},{6,7},{7,6},{8,9},{9,8},{10,11... | collective-permute-start | bytes 196616 | tf_op jit(solution)/shard_map/ppermute | solution.py:393

commit v13 on v11

--- a/solution.py
+++ b/solution.py
@@ -255,6 +255,7 @@
     other = jnp.concatenate(
         [other_ref[i * count : (i + 1) * count, :] for i in range(depth // 128)], axis=1
     )
+    rows = jnp.concatenate([own, other], axis=0)
     rank = pieces[0].shape[0]
     size = GROUP * rank
     extra = extra_rows(bounds_ref.shape[1])
@@ -264,9 +265,10 @@
         first = jnp.concatenate([ref[...] for ref in held[:GROUP]], axis=0)
         second = jnp.concatenate([ref[:, : depth - cut] for ref in held[GROUP:]], axis=0)
         ends = (own_ends(bounds_ref, group, size), other_ends(other_ref, extra, group, size))
-        for s, rows in enumerate((own, other)):
-            part = contract(rows[:, :cut], first) + contract(rows[:, cut:], second)
-            kept = fold(jnp.where(group_mask(*ends[s], part.shape), part, 0.0))
+        part = contract(rows, jnp.concatenate([first, second], axis=1))
+        for s in (0, 1):
+            mine = part[s * count : (s + 1) * count]
+            kept = fold(jnp.where(group_mask(*ends[s], mine.shape), mine, 0.0))
             totals[s] = kept if totals[s] is None else totals[s] + kept
     for total, out_ref in zip(totals, outs):
         if last:
@@ -274,7 +276,7 @@
             half = total.shape[0] // 2
             lane = lax.broadcasted_iota(I32, (half, 2 * rank), 1)
             total = jnp.where(lane < rank, total[:half], total[half:])
-        out_ref[...] = total
+        out_ref[...] = total.astype(out_ref.dtype)
 
 
 def rank_call(groups, depth, own, other, bounds, pieces, starts):
@@ -283,10 +285,11 @@
     last = starts is not None
     shape = (rows // 2, 2 * rank) if last else (rows, 2 * rank)
     out = jax.ShapeDtypeStruct(shape, F32)
+    other_out = jax.ShapeDtypeStruct(shape, BF16 if last else F32)
     operands = [own, other, bounds, *pieces, *(starts or ())]
     return pl.pallas_call(
         functools.partial(rank_kernel, groups, depth, last),
-        out_shape=(out, out),
+        out_shape=(out, other_out),
         in_specs=[VMEM] * len(operands),
         out_specs=(VMEM, VMEM),
         compiler_params=params(),
@@ -298,7 +301,7 @@
     factors, out_ref = refs[:-1], refs[-1]
     rank, width = factors[0].shape[0], out_ref.shape[1]
     begin = factors[0].shape[1] - width
-    packed = (mine[...] + one[...]) + (two[...] + three[...])
+    packed = (mine[...] + one[...]) + (two[...].astype(F32) + three[...].astype(F32))
     turned = pltpu.roll(packed, rank, 1)
     lane = lax.broadcasted_iota(I32, packed.shape, 1)
     values = jnp.concatenate(

time: 39.2 us -> 38.7 us (0.987)
  no operation moved by 1% of the time
where the time goes in v13:
time: 38.7 us; the launch traced here: 38.6 us
  starting transfers between devices  19.4 us (50%)
  waiting for transfers between devices  12.4 us (32%)
  Pallas kernels  6.66 us (17%)
    ppermute x3, starting transfers between devices, per_device(): d = lax.ppermute(behind[1], 'batch', backward)  6.68 us
    ppermute x3, waiting for transfers between devices, per_device(): b = lax.ppermute(ahead[1], 'batch', forward)  3.91 us
    ppermute x3, starting transfers between devices, per_device(): c = lax.ppermute(behind[0], 'batch', backward)  3.48 us
    ppermute x3, starting transfers between devices, per_device(): b = lax.ppermute(ahead[1], 'batch', forward)  2.65 us
    ppermute x1, waiting for transfers between devices, per_device(): other = lax.ppermute(to_other, 'groups', swap)  2.64 us
    ppermute x1, waiting for transfers between devices, per_device(): two = lax.ppermute(theirs, 'groups', swap)  2.39 us
    pallas_call x1, Pallas kernels, base_call(): pl.pallas_call(base_kernel, out_shape=(out, out), in_specs=[VMEM] * 2, ou...  2.35 us
    ppermute x1, starting transfers between devices, per_device(): other = lax.ppermute(to_other, 'groups', swap)  1.97 us
  transfers between devices with their start and end apart: 19, of which 10 were waited for; matrix products, arithmetic and copies ran while one was open for 0% of the time, Pallas kernels for 10%

profile of v13, /device:TPU:0, one launch (start us, length us, event | category | flops | bytes accessed | tf_op | source)
XLA Modules:
  0.0 38.6 jit_solution(15615673688523634223)
XLA Ops:
  0.0 1.6 %shard_map.82 = (bf16[4112,128]{1,0:T(8,128)(2,1)S(1)}, bf16[64,1280]{1,0:T(8,128)(2,1)S(1)}, bf16[64,1280]{1,0:T(8,128)(2,1)S(1)}, s32[8,512]{1,0:T(8,128)S(1)}) custom-call(bf16[256,4096]{1,0:T(8,128)(2,1)} %refs_0_.1, bf16[64,4096]{1,0:T(8,128)(2,1)} %bitcast.6, bf16[64,512]{1,0:T(8,128)(2,1)} %bitcast.7, s32[1,4]{1,0:T(1,128)} %demand_ref.1, ...), custom_call_target="tpu_custom_call" | custom-call | tf_op jit(solution)/shard_map/pallas_call | solution.py:161
  1.6 3.1 %collective-permute-start.8 = (bf16[64,1280]{1,0:T(8,128)(2,1)S(1)}, bf16[64,1280]{1,0:T(8,128)(2,1)S(1)}, u32[]{:S(2)}, u32[]{:S(2)}) collective-permute-start(bf16[64,1280]{1,0:T(8,128)(2,1)S(1)} %get-tuple-element.33.refs_7_.refs_0_), channel_id=1, source_target_pairs={{2,0},{6,2},{10,6},{14,10},{12,14},{8,12},{4,8},{0,4},{3,1},{7,3},... | collective-permute-start | bytes 491528 | tf_op jit(solution)/shard_map/ppermute | solution.py:359
  4.7 0.0 collective-permute-start.3
  4.7 2.0 %collective-permute-start = (bf16[4112,128]{1,0:T(8,128)(2,1)S(1)}, bf16[4112,128]{1,0:T(8,128)(2,1)S(1)}, u32[]{:S(2)}, u32[]{:S(2)}) collective-permute-start(bf16[4112,128]{1,0:T(8,128)(2,1)S(1)} %get-tuple-element.31), channel_id=1, source_target_pairs={{0,16},{16,0},{1,17},{17,1},{2,18},{18,2},{3,19},{19,3},{4,20},{20... | collective-permute-start | bytes 3158024 | tf_op jit(solution)/shard_map/ppermute | solution.py:369
  6.7 0.0 slice-start
  6.7 0.0 slice-start.1
  6.7 1.5 %collective-permute-start.10 = (bf16[64,1280]{1,0:T(8,128)(2,1)S(1)}, bf16[64,1280]{1,0:T(8,128)(2,1)S(1)}, u32[]{:S(2)}, u32[]{:S(2)}) collective-permute-start(bf16[64,1280]{1,0:T(8,128)(2,1)S(1)} %get-tuple-element.33.refs_7_.refs_0_), channel_id=1, source_target_pairs={{0,2},{2,6},{6,10},{10,14},{14,12},{12,8},{8,4},{4,0},{1,3},{3,7},... | collective-permute-start | bytes 491528 | tf_op jit(solution)/shard_map/ppermute | solution.py:360
  8.2 0.5 %collective-permute-start.1 = (bf16[64,1280]{1,0:T(8,128)(2,1)S(1)}, bf16[64,1280]{1,0:T(8,128)(2,1)S(1)}, u32[]{:S(2)}, u32[]{:S(2)}) collective-permute-start(bf16[64,1280]{1,0:T(8,128)(2,1)S(1)} %get-tuple-element.32.refs_3_), channel_id=1, source_target_pairs={{2,0},{6,2},{10,6},{14,10},{12,14},{8,12},{4,8},{0,4},{3,1},{7,3},... | collective-permute-start | bytes 491528 | tf_op jit(solution)/shard_map/ppermute | solution.py:361
  8.7 0.1 collective-permute-done.8.refs_9_.refs_2_
  8.8 2.3 %collective-permute-start.9 = (bf16[64,1280]{1,0:T(8,128)(2,1)S(1)}, bf16[64,1280]{1,0:T(8,128)(2,1)S(1)}, u32[]{:S(2)}, u32[]{:S(2)}) collective-permute-start(bf16[64,1280]{1,0:T(8,128)(2,1)S(1)} %collective-permute-done.8.refs_9_.refs_2_), channel_id=1, source_target_pairs={{2,0},{6,2},{10,6},{14,10},{12,14},{8,12},{4,8},{0,4},{3,1},{7,3},... | collective-permute-start | bytes 491528 | tf_op jit(solution)/shard_map/ppermute | solution.py:359
  11.1 0.7 %collective-permute-done.3.refs_4_ = bf16[64,1280]{1,0:T(8,128)(2,1)S(1)} collective-permute-done((bf16[64,1280]{1,0:T(8,128)(2,1)S(1)}, bf16[64,1280]{1,0:T(8,128)(2,1)S(1)}, u32[]{:S(2)}, u32[]{:S(2)}) %collective-permute-start.3) | collective-permute-done | bytes 163872 | tf_op jit(solution)/shard_map/ppermute | solution.py:358
  11.8 0.0 collective-permute-start.4
  11.8 3.5 %collective-permute-done.10.refs_8_.refs_1_ = bf16[64,1280]{1,0:T(8,128)(2,1)S(1)} collective-permute-done((bf16[64,1280]{1,0:T(8,128)(2,1)S(1)}, bf16[64,1280]{1,0:T(8,128)(2,1)S(1)}, u32[]{:S(2)}, u32[]{:S(2)}) %collective-permute-start.10) | collective-permute-done | bytes 163872 | tf_op jit(solution)/shard_map/ppermute | solution.py:360
  15.3 0.0 collective-permute-start.11
  15.3 0.0 collective-permute-done.1.refs_5_
  15.3 2.0 %collective-permute-start.2 = (bf16[64,1280]{1,0:T(8,128)(2,1)S(1)}, bf16[64,1280]{1,0:T(8,128)(2,1)S(1)}, u32[]{:S(2)}, u32[]{:S(2)}) collective-permute-start(bf16[64,1280]{1,0:T(8,128)(2,1)S(1)} %collective-permute-done.1.refs_5_), channel_id=1, source_target_pairs={{2,0},{6,2},{10,6},{14,10},{12,14},{8,12},{4,8},{0,4},{3,1},{7,3},... | collective-permute-start | bytes 491528 | tf_op jit(solution)/shard_map/ppermute | solution.py:361
  17.3 0.3 collective-permute-done.9.refs_7_.refs_4_
  17.6 1.3 %collective-permute-start.13 = (bf16[64,1280]{1,0:T(8,128)(2,1)S(1)}, bf16[64,1280]{1,0:T(8,128)(2,1)S(1)}, u32[]{:S(2)}, u32[]{:S(2)}) collective-permute-start(bf16[64,1280]{1,0:T(8,128)(2,1)S(1)} %collective-permute-done.9.refs_7_.refs_4_), channel_id=1, source_target_pairs={{2,0},{6,2},{10,6},{14,10},{12,14},{8,12},{4,8},{0,4},{3,1},{7,3},... | collective-permute-start | bytes 491528 | tf_op jit(solution)/shard_map/ppermute | solution.py:359
  18.9 0.0 collective-permute-done.4.refs_6_
  18.9 0.7 %collective-permute-start.5 = (bf16[64,1280]{1,0:T(8,128)(2,1)S(1)}, bf16[64,1280]{1,0:T(8,128)(2,1)S(1)}, u32[]{:S(2)}, u32[]{:S(2)}) collective-permute-start(bf16[64,1280]{1,0:T(8,128)(2,1)S(1)} %collective-permute-done.4.refs_6_), channel_id=1, source_target_pairs={{0,2},{2,6},{6,10},{10,14},{14,12},{12,8},{8,4},{4,0},{1,3},{3,7},... | collective-permute-start | bytes 491528 | tf_op jit(solution)/shard_map/ppermute | solution.py:358
  19.7 0.0 slice-done
  19.7 0.0 slice-done.1
  19.7 0.0 copy-done
  19.7 2.4 %shard_map.84 = (f32[256,512]{1,0:T(8,128)S(1)}, f32[256,512]{1,0:T(8,128)S(1)}) custom-call(bf16[256,4096]{1,0:T(8,128)(2,1)S(1)} %copy-done, bf16[4096,1024]{1,0:T(8,128)(2,1)S(1)} %bitcast.5), custom_call_target="tpu_custom_call" | custom-call | bytes 4194304 | tf_op jit(solution)/shard_map/pallas_call | solution.py:210
  22.1 0.4 %collective-permute-done.11.refs_10_.refs_3_ = bf16[64,1280]{1,0:T(8,128)(2,1)S(1)} collective-permute-done((bf16[64,1280]{1,0:T(8,128)(2,1)S(1)}, bf16[64,1280]{1,0:T(8,128)(2,1)S(1)}, u32[]{:S(2)}, u32[]{:S(2)}) %collective-permute-start.11) | collective-permute-done | bytes 163872 | tf_op jit(solution)/shard_map/ppermute | solution.py:360
  22.5 1.1 %collective-permute-start.12 = (bf16[64,1280]{1,0:T(8,128)(2,1)S(1)}, bf16[64,1280]{1,0:T(8,128)(2,1)S(1)}, u32[]{:S(2)}, u32[]{:S(2)}) collective-permute-start(bf16[64,1280]{1,0:T(8,128)(2,1)S(1)} %collective-permute-done.11.refs_10_.refs_3_), channel_id=1, source_target_pairs={{0,2},{2,6},{6,10},{10,14},{14,12},{12,8},{8,4},{4,0},{1,3},{3,7},... | collective-permute-start | bytes 491528 | tf_op jit(solution)/shard_map/ppermute | solution.py:360
  23.5 0.0 collective-permute-done.2.refs_3_
  23.5 0.9 %collective-permute-start.6 = (bf16[64,1280]{1,0:T(8,128)(2,1)S(1)}, bf16[64,1280]{1,0:T(8,128)(2,1)S(1)}, u32[]{:S(2)}, u32[]{:S(2)}) collective-permute-start(bf16[64,1280]{1,0:T(8,128)(2,1)S(1)} %collective-permute-done.2.refs_3_), channel_id=1, source_target_pairs={{2,0},{6,2},{10,6},{14,10},{12,14},{8,12},{4,8},{0,4},{3,1},{7,3},... | collective-permute-start | bytes 491528 | tf_op jit(solution)/shard_map/ppermute | solution.py:361
  24.5 0.0 collective-permute-done.13.refs_9_.refs_6_
  24.5 1.6 %collective-permute-start.14 = (bf16[64,1280]{1,0:T(8,128)(2,1)S(1)}, bf16[64,1280]{1,0:T(8,128)(2,1)S(1)}, u32[]{:S(2)}, u32[]{:S(2)}) collective-permute-start(bf16[64,1280]{1,0:T(8,128)(2,1)S(1)} %collective-permute-done.13.refs_9_.refs_6_), channel_id=1, source_target_pairs={{2,0},{6,2},{10,6},{14,10},{12,14},{8,12},{4,8},{0,4},{3,1},{7,3},... | collective-permute-start | bytes 491528 | tf_op jit(solution)/shard_map/ppermute | solution.py:366
  26.1 0.0 collective-permute-done.5.refs_4_
  26.1 0.7 %collective-permute-start.7 = (bf16[64,1280]{1,0:T(8,128)(2,1)S(1)}, bf16[64,1280]{1,0:T(8,128)(2,1)S(1)}, u32[]{:S(2)}, u32[]{:S(2)}) collective-permute-start(bf16[64,1280]{1,0:T(8,128)(2,1)S(1)} %collective-permute-done.5.refs_4_), channel_id=1, source_target_pairs={{0,2},{2,6},{6,10},{10,14},{14,12},{12,8},{8,4},{4,0},{1,3},{3,7},... | collective-permute-start | bytes 491528 | tf_op jit(solution)/shard_map/ppermute | solution.py:365
  26.8 2.6 %collective-permute-done.refs_1_ = bf16[4112,128]{1,0:T(8,128)(2,1)S(1)} collective-permute-done((bf16[4112,128]{1,0:T(8,128)(2,1)S(1)}, bf16[4112,128]{1,0:T(8,128)(2,1)S(1)}, u32[]{:S(2)}, u32[]{:S(2)}) %collective-permute-start) | collective-permute-done | bytes 1052704 | tf_op jit(solution)/shard_map/ppermute | solution.py:369
  29.4 0.7 %shard_map.85 = (f32[256,128]{1,0:T(8,128)S(1)}, f32[256,128]{1,0:T(8,128)S(1)}) custom-call(bf16[256,4096]{1,0:T(8,128)(2,1)S(1)} %copy-done, bf16[4112,128]{1,0:T(8,128)(2,1)S(1)} %collective-permute-done.refs_1_, s32[8,512]{1,0:T(8,128)S(1)} %shard_map.83.refs_2_.bounds_ref, bf16[64,1280]{1,0:T(8,128)(2,1)S(1)} %get-tuple-element.32.refs_3_, ...), custom_call_target="tpu_custom_call" | custom-call | flops 8589934592 | bytes 16777216 | tf_op jit(solution)/shard_map/pallas_call | solution.py:290
  30.1 0.1 collective-permute-start.18
  30.2 0.0 collective-permute-done.12.refs_8_.refs_5_
  30.2 0.0 collective-permute-done.6.refs_5_
  30.2 0.4 collective-permute-done.14.refs_10_.refs_7_
  30.6 0.8 %collective-permute-done.7.refs_6_ = bf16[64,1280]{1,0:T(8,128)(2,1)S(1)} collective-permute-done((bf16[64,1280]{1,0:T(8,128)(2,1)S(1)}, bf16[64,1280]{1,0:T(8,128)(2,1)S(1)}, u32[]{:S(2)}, u32[]{:S(2)}) %collective-permute-start.7) | collective-permute-done | bytes 163872 | tf_op jit(solution)/shard_map/ppermute | solution.py:365
  31.4 0.8 %shard_map.86 = (f32[128,128]{1,0:T(8,128)S(1)}, bf16[128,128]{1,0:T(8,128)(2,1)S(1)}) custom-call(bf16[256,4096]{1,0:T(8,128)(2,1)S(1)} %copy-done, bf16[4112,128]{1,0:T(8,128)(2,1)S(1)} %collective-permute-done.refs_1_, s32[8,512]{1,0:T(8,128)S(1)} %shard_map.83.refs_2_.bounds_ref, bf16[64,1280]{1,0:T(8,128)(2,1)S(1)} %collective-permute-done.2.refs_3_, ...), custom_call_target="tpu_custom_call" | custom-call | flops 8589934592 | bytes 16777216 | tf_op jit(solution)/shard_map/pallas_call | solution.py:290
  32.2 1.6 %collective-permute-start.16 = (bf16[128,128]{1,0:T(8,128)(2,1)S(1)}, bf16[128,128]{1,0:T(8,128)(2,1)S(1)}, u32[]{:S(2)}, u32[]{:S(2)}) collective-permute-start(bf16[128,128]{1,0:T(8,128)(2,1)S(1)} %get-tuple-element.40), channel_id=1, source_target_pairs={{0,16},{16,0},{1,17},{17,1},{2,18},{18,2},{3,19},{19,3},{4,20},{20... | collective-permute-start | bytes 98312 | tf_op jit(solution)/shard_map/ppermute | solution.py:384
  33.8 0.0 collective-permute-start.15
  33.8 2.4 %collective-permute-done.16.two = bf16[128,128]{1,0:T(8,128)(2,1)S(1)} collective-permute-done((bf16[128,128]{1,0:T(8,128)(2,1)S(1)}, bf16[128,128]{1,0:T(8,128)(2,1)S(1)}, u32[]{:S(2)}, u32[]{:S(2)}) %collective-permute-start.16) | collective-permute-done | bytes 32800 | tf_op jit(solution)/shard_map/ppermute | solution.py:384
  36.2 0.0 collective-permute-start.17
  36.2 1.2 %collective-permute-done.17.three = bf16[128,128]{1,0:T(8,128)(2,1)S(1)} collective-permute-done((bf16[128,128]{1,0:T(8,128)(2,1)S(1)}, bf16[128,128]{1,0:T(8,128)(2,1)S(1)}, u32[]{:S(2)}, u32[]{:S(2)}) %collective-permute-start.17) | collective-permute-done | bytes 32800 | tf_op jit(solution)/shard_map/ppermute | solution.py:386
  37.4 0.0 collective-permute-done.15.one
  37.4 0.0 collective-permute-done.18.far_ref
  37.4 1.1 %shard_map.87 = bf16[256,512]{1,0:T(8,128)(2,1)} custom-call(s32[8,512]{1,0:T(8,128)S(1)} %shard_map.83.refs_2_.bounds_ref, f32[128,128]{1,0:T(8,128)S(1)} %get-tuple-element.39.mine, f32[128,128]{1,0:T(8,128)S(1)} %collective-permute-done.15.one, bf16[128,128]{1,0:T(8,128)(2,1)S(1)} %collective-permute-done.16.two, ...), custom_call_target="tpu_custom_call" | custom-call | tf_op jit(solution)/shard_map/pallas_call | solution.py:389
  (3 shorter events, 0.0 us)
Async XLA Ops:
  1.6 7.2 %collective-permute-start.8 = (bf16[64,1280]{1,0:T(8,128)(2,1)S(1)}, bf16[64,1280]{1,0:T(8,128)(2,1)S(1)}, u32[]{:S(2)}, u32[]{:S(2)}) collective-permute-start(bf16[64,1280]{1,0:T(8,128)(2,1)S(1)} %get-tuple-element.33.refs_7_.refs_0_), channel_id=1, source_target_pairs={{2,0},{6,2},{10,6},{14,10},{12,14},{8,12},{4,8},{0,4},{3,1},{7,3},... | collective-permute-start | bytes 491528 | tf_op jit(solution)/shard_map/ppermute | solution.py:359
  4.7 7.1 %collective-permute-start.3 = (bf16[64,1280]{1,0:T(8,128)(2,1)S(1)}, bf16[64,1280]{1,0:T(8,128)(2,1)S(1)}, u32[]{:S(2)}, u32[]{:S(2)}) collective-permute-start(bf16[64,1280]{1,0:T(8,128)(2,1)S(1)} %get-tuple-element.32.refs_3_), channel_id=1, source_target_pairs={{0,2},{2,6},{6,10},{10,14},{14,12},{12,8},{8,4},{4,0},{1,3},{3,7},... | collective-permute-start | bytes 491528 | tf_op jit(solution)/shard_map/ppermute | solution.py:358
  4.7 24.7 %collective-permute-start = (bf16[4112,128]{1,0:T(8,128)(2,1)S(1)}, bf16[4112,128]{1,0:T(8,128)(2,1)S(1)}, u32[]{:S(2)}, u32[]{:S(2)}) collective-permute-start(bf16[4112,128]{1,0:T(8,128)(2,1)S(1)} %get-tuple-element.31), channel_id=1, source_target_pairs={{0,16},{16,0},{1,17},{17,1},{2,18},{18,2},{3,19},{19,3},{4,20},{20... | collective-permute-start | bytes 3158024 | tf_op jit(solution)/shard_map/ppermute | solution.py:369
  6.7 13.0 %slice-start = ((s8[8388608]{0:T(1024)(128)(4,1)}), s8[4194304]{0:T(1024)(128)(4,1)S(1)}, s32[]{:S(2)}) async-start(s8[8388608]{0:T(1024)(128)(4,1)} %bitcast.4), calls=%async_computation | async-start | bytes 8388608
  6.7 13.0 %slice-start.1 = ((s8[8388608]{0:T(1024)(128)(4,1)}), s8[4194304]{0:T(1024)(128)(4,1)S(1)}, s32[]{:S(2)}) async-start(s8[8388608]{0:T(1024)(128)(4,1)} %bitcast.4), calls=%async_computation.1 | async-start | bytes 8388608
  6.7 13.0 %copy-start = (bf16[256,4096]{1,0:T(8,128)(2,1)S(1)}, bf16[256,4096]{1,0:T(8,128)(2,1)}, u32[]{:S(2)}) copy-start(bf16[256,4096]{1,0:T(8,128)(2,1)} %refs_0_.1) | copy-start | bytes 6291460
  6.7 8.7 %collective-permute-start.10 = (bf16[64,1280]{1,0:T(8,128)(2,1)S(1)}, bf16[64,1280]{1,0:T(8,128)(2,1)S(1)}, u32[]{:S(2)}, u32[]{:S(2)}) collective-permute-start(bf16[64,1280]{1,0:T(8,128)(2,1)S(1)} %get-tuple-element.33.refs_7_.refs_0_), channel_id=1, source_target_pairs={{0,2},{2,6},{6,10},{10,14},{14,12},{12,8},{8,4},{4,0},{1,3},{3,7},... | collective-permute-start | bytes 491528 | tf_op jit(solution)/shard_map/ppermute | solution.py:360
  8.2 7.1 %collective-permute-start.1 = (bf16[64,1280]{1,0:T(8,128)(2,1)S(1)}, bf16[64,1280]{1,0:T(8,128)(2,1)S(1)}, u32[]{:S(2)}, u32[]{:S(2)}) collective-permute-start(bf16[64,1280]{1,0:T(8,128)(2,1)S(1)} %get-tuple-element.32.refs_3_), channel_id=1, source_target_pairs={{2,0},{6,2},{10,6},{14,10},{12,14},{8,12},{4,8},{0,4},{3,1},{7,3},... | collective-permute-start | bytes 491528 | tf_op jit(solution)/shard_map/ppermute | solution.py:361
  8.8 8.9 %collective-permute-start.9 = (bf16[64,1280]{1,0:T(8,128)(2,1)S(1)}, bf16[64,1280]{1,0:T(8,128)(2,1)S(1)}, u32[]{:S(2)}, u32[]{:S(2)}) collective-permute-start(bf16[64,1280]{1,0:T(8,128)(2,1)S(1)} %collective-permute-done.8.refs_9_.refs_2_), channel_id=1, source_target_pairs={{2,0},{6,2},{10,6},{14,10},{12,14},{8,12},{4,8},{0,4},{3,1},{7,3},... | collective-permute-start | bytes 491528 | tf_op jit(solution)/shard_map/ppermute | solution.py:359
  11.8 7.1 %collective-permute-start.4 = (bf16[64,1280]{1,0:T(8,128)(2,1)S(1)}, bf16[64,1280]{1,0:T(8,128)(2,1)S(1)}, u32[]{:S(2)}, u32[]{:S(2)}) collective-permute-start(bf16[64,1280]{1,0:T(8,128)(2,1)S(1)} %collective-permute-done.3.refs_4_), channel_id=1, source_target_pairs={{0,2},{2,6},{6,10},{10,14},{14,12},{12,8},{8,4},{4,0},{1,3},{3,7},... | collective-permute-start | bytes 491528 | tf_op jit(solution)/shard_map/ppermute | solution.py:358
  15.3 7.1 %collective-permute-start.11 = (bf16[64,1280]{1,0:T(8,128)(2,1)S(1)}, bf16[64,1280]{1,0:T(8,128)(2,1)S(1)}, u32[]{:S(2)}, u32[]{:S(2)}) collective-permute-start(bf16[64,1280]{1,0:T(8,128)(2,1)S(1)} %collective-permute-done.10.refs_8_.refs_1_), channel_id=1, source_target_pairs={{0,2},{2,6},{6,10},{10,14},{14,12},{12,8},{8,4},{4,0},{1,3},{3,7},... | collective-permute-start | bytes 491528 | tf_op jit(solution)/shard_map/ppermute | solution.py:360
  15.3 8.2 %collective-permute-start.2 = (bf16[64,1280]{1,0:T(8,128)(2,1)S(1)}, bf16[64,1280]{1,0:T(8,128)(2,1)S(1)}, u32[]{:S(2)}, u32[]{:S(2)}) collective-permute-start(bf16[64,1280]{1,0:T(8,128)(2,1)S(1)} %collective-permute-done.1.refs_5_), channel_id=1, source_target_pairs={{2,0},{6,2},{10,6},{14,10},{12,14},{8,12},{4,8},{0,4},{3,1},{7,3},... | collective-permute-start | bytes 491528 | tf_op jit(solution)/shard_map/ppermute | solution.py:361
  17.6 6.8 %collective-permute-start.13 = (bf16[64,1280]{1,0:T(8,128)(2,1)S(1)}, bf16[64,1280]{1,0:T(8,128)(2,1)S(1)}, u32[]{:S(2)}, u32[]{:S(2)}) collective-permute-start(bf16[64,1280]{1,0:T(8,128)(2,1)S(1)} %collective-permute-done.9.refs_7_.refs_4_), channel_id=1, source_target_pairs={{2,0},{6,2},{10,6},{14,10},{12,14},{8,12},{4,8},{0,4},{3,1},{7,3},... | collective-permute-start | bytes 491528 | tf_op jit(solution)/shard_map/ppermute | solution.py:359
  18.9 7.1 %collective-permute-start.5 = (bf16[64,1280]{1,0:T(8,128)(2,1)S(1)}, bf16[64,1280]{1,0:T(8,128)(2,1)S(1)}, u32[]{:S(2)}, u32[]{:S(2)}) collective-permute-start(bf16[64,1280]{1,0:T(8,128)(2,1)S(1)} %collective-permute-done.4.refs_6_), channel_id=1, source_target_pairs={{0,2},{2,6},{6,10},{10,14},{14,12},{12,8},{8,4},{4,0},{1,3},{3,7},... | collective-permute-start | bytes 491528 | tf_op jit(solution)/shard_map/ppermute | solution.py:358
  22.5 7.8 %collective-permute-start.12 = (bf16[64,1280]{1,0:T(8,128)(2,1)S(1)}, bf16[64,1280]{1,0:T(8,128)(2,1)S(1)}, u32[]{:S(2)}, u32[]{:S(2)}) collective-permute-start(bf16[64,1280]{1,0:T(8,128)(2,1)S(1)} %collective-permute-done.11.refs_10_.refs_3_), channel_id=1, source_target_pairs={{0,2},{2,6},{6,10},{10,14},{14,12},{12,8},{8,4},{4,0},{1,3},{3,7},... | collective-permute-start | bytes 491528 | tf_op jit(solution)/shard_map/ppermute | solution.py:360
  23.5 6.7 %collective-permute-start.6 = (bf16[64,1280]{1,0:T(8,128)(2,1)S(1)}, bf16[64,1280]{1,0:T(8,128)(2,1)S(1)}, u32[]{:S(2)}, u32[]{:S(2)}) collective-permute-start(bf16[64,1280]{1,0:T(8,128)(2,1)S(1)} %collective-permute-done.2.refs_3_), channel_id=1, source_target_pairs={{2,0},{6,2},{10,6},{14,10},{12,14},{8,12},{4,8},{0,4},{3,1},{7,3},... | collective-permute-start | bytes 491528 | tf_op jit(solution)/shard_map/ppermute | solution.py:361
  24.5 6.1 %collective-permute-start.14 = (bf16[64,1280]{1,0:T(8,128)(2,1)S(1)}, bf16[64,1280]{1,0:T(8,128)(2,1)S(1)}, u32[]{:S(2)}, u32[]{:S(2)}) collective-permute-start(bf16[64,1280]{1,0:T(8,128)(2,1)S(1)} %collective-permute-done.13.refs_9_.refs_6_), channel_id=1, source_target_pairs={{2,0},{6,2},{10,6},{14,10},{12,14},{8,12},{4,8},{0,4},{3,1},{7,3},... | collective-permute-start | bytes 491528 | tf_op jit(solution)/shard_map/ppermute | solution.py:366
  26.1 5.3 %collective-permute-start.7 = (bf16[64,1280]{1,0:T(8,128)(2,1)S(1)}, bf16[64,1280]{1,0:T(8,128)(2,1)S(1)}, u32[]{:S(2)}, u32[]{:S(2)}) collective-permute-start(bf16[64,1280]{1,0:T(8,128)(2,1)S(1)} %collective-permute-done.5.refs_4_), channel_id=1, source_target_pairs={{0,2},{2,6},{6,10},{10,14},{14,12},{12,8},{8,4},{4,0},{1,3},{3,7},... | collective-permute-start | bytes 491528 | tf_op jit(solution)/shard_map/ppermute | solution.py:365
  30.1 7.3 %collective-permute-start.18 = (f32[256,512]{1,0:T(8,128)S(1)}, f32[256,512]{1,0:T(8,128)S(1)}, u32[]{:S(2)}, u32[]{:S(2)}) collective-permute-start(f32[256,512]{1,0:T(8,128)S(1)} %get-tuple-element.42), channel_id=1, source_target_pairs={{0,1},{1,0},{2,3},{3,2},{4,5},{5,4},{6,7},{7,6},{8,9},{9,8},{10,11... | collective-permute-start | bytes 1572872 | tf_op jit(solution)/shard_map/ppermute | solution.py:380
  32.2 4.0 %collective-permute-start.16 = (bf16[128,128]{1,0:T(8,128)(2,1)S(1)}, bf16[128,128]{1,0:T(8,128)(2,1)S(1)}, u32[]{:S(2)}, u32[]{:S(2)}) collective-permute-start(bf16[128,128]{1,0:T(8,128)(2,1)S(1)} %get-tuple-element.40), channel_id=1, source_target_pairs={{0,16},{16,0},{1,17},{17,1},{2,18},{18,2},{3,19},{19,3},{4,20},{20... | collective-permute-start | bytes 98312 | tf_op jit(solution)/shard_map/ppermute | solution.py:384
  33.8 3.6 %collective-permute-start.15 = (f32[128,128]{1,0:T(8,128)S(1)}, f32[128,128]{1,0:T(8,128)S(1)}, u32[]{:S(2)}, u32[]{:S(2)}) collective-permute-start(f32[128,128]{1,0:T(8,128)S(1)} %get-tuple-element.39.mine), channel_id=1, source_target_pairs={{0,1},{1,0},{2,3},{3,2},{4,5},{5,4},{6,7},{7,6},{8,9},{9,8},{10,11... | collective-permute-start | bytes 196616 | tf_op jit(solution)/shard_map/ppermute | solution.py:385
  36.2 1.2 %collective-permute-start.17 = (bf16[128,128]{1,0:T(8,128)(2,1)S(1)}, bf16[128,128]{1,0:T(8,128)(2,1)S(1)}, u32[]{:S(2)}, u32[]{:S(2)}) collective-permute-start(bf16[128,128]{1,0:T(8,128)(2,1)S(1)} %collective-permute-done.16.two), channel_id=1, source_target_pairs={{0,1},{1,0},{2,3},{3,2},{4,5},{5,4},{6,7},{7,6},{8,9},{9,8},{10,11... | collective-permute-start | bytes 98312 | tf_op jit(solution)/shard_map/ppermute | solution.py:386

commit v14 on v11

--- a/solution.py
+++ b/solution.py
@@ -242,53 +242,62 @@
     return total
 
 
-def rank_kernel(groups, depth, last, *refs):
+def rank_kernel(sides, groups, depth, last, *refs):
     refs = list(refs)
-    own_ref, other_ref, bounds_ref = refs[:3]
-    pieces = refs[3:]
+    rows_refs, refs = refs[: len(sides)], refs[len(sides) :]
+    bounds_ref, pieces = refs[0], refs[1:]
     pieces, rest = pieces[: 2 * GROUP * len(groups)], pieces[2 * GROUP * len(groups) :]
-    starts, outs = (rest[:2], rest[2:]) if last else ((None, None), rest)
+    starts, outs = rest[: -len(sides)], rest[-len(sides) :]
     cut = pieces[0].shape[1]
-    offset = pl.multiple_of(lax.axis_index("groups") * depth, 128)
-    own = own_ref[:, pl.ds(offset, depth)]
-    count = own.shape[0]
-    other = jnp.concatenate(
-        [other_ref[i * count : (i + 1) * count, :] for i in range(depth // 128)], axis=1
-    )
     rank = pieces[0].shape[0]
     size = GROUP * rank
     extra = extra_rows(bounds_ref.shape[1])
-    totals = [start_ref[...] if last else None for start_ref in starts]
+    rows = []
+    for side, ref in zip(sides, rows_refs):
+        if side == 0:
+            offset = pl.multiple_of(lax.axis_index("groups") * depth, 128)
+            rows.append(ref[:, pl.ds(offset, depth)])
+        else:
+            blocks = depth // 128
+            tall = (ref.shape[0] - extra) // blocks
+            rows.append(
+                jnp.concatenate([ref[i * tall : (i + 1) * tall, :] for i in range(blocks)], axis=1)
+            )
+    count = rows[0].shape[0]
+    rows = jnp.concatenate(rows, axis=0)
+    totals = [ref[...] for ref in starts] if last else [None] * len(sides)
     for i, group in enumerate(groups):
         held = pieces[2 * GROUP * i : 2 * GROUP * (i + 1)]
         first = jnp.concatenate([ref[...] for ref in held[:GROUP]], axis=0)
         second = jnp.concatenate([ref[:, : depth - cut] for ref in held[GROUP:]], axis=0)
-        ends = (own_ends(bounds_ref, group, size), other_ends(other_ref, extra, group, size))
-        for s, rows in enumerate((own, other)):
-            part = contract(rows[:, :cut], first) + contract(rows[:, cut:], second)
-            kept = fold(jnp.where(group_mask(*ends[s], part.shape), part, 0.0))
+        part = contract(rows, jnp.concatenate([first, second], axis=1))
+        for s, side in enumerate(sides):
+            if side == 0:
+                ends = own_ends(bounds_ref, group, size)
+            else:
+                ends = other_ends(rows_refs[s], extra, group, size)
+            here = part[s * count : (s + 1) * count]
+            kept = fold(jnp.where(group_mask(*ends, here.shape), here, 0.0))
             totals[s] = kept if totals[s] is None else totals[s] + kept
     for total, out_ref in zip(totals, outs):
         if last:
             total = total + pltpu.roll(total, rank, 1)
-            half = total.shape[0] // 2
+            half = count // 2
             lane = lax.broadcasted_iota(I32, (half, 2 * rank), 1)
             total = jnp.where(lane < rank, total[:half], total[half:])
         out_ref[...] = total
 
 
-def rank_call(groups, depth, own, other, bounds, pieces, starts):
-    rows = own.shape[0]
+def rank_call(sides, groups, depth, count, rows, bounds, pieces, starts):
     rank = pieces[0].shape[0]
-    last = starts is not None
-    shape = (rows // 2, 2 * rank) if last else (rows, 2 * rank)
-    out = jax.ShapeDtypeStruct(shape, F32)
-    operands = [own, other, bounds, *pieces, *(starts or ())]
+    last = len(starts) > 0
+    shape = (count // 2, 2 * rank) if last else (count, 2 * rank)
+    operands = [*rows, bounds, *pieces, *starts]
     return pl.pallas_call(
-        functools.partial(rank_kernel, groups, depth, last),
-        out_shape=(out, out),
+        functools.partial(rank_kernel, sides, groups, depth, last),
+        out_shape=(jax.ShapeDtypeStruct(shape, F32),) * len(sides),
         in_specs=[VMEM] * len(operands),
-        out_specs=(VMEM, VMEM),
+        out_specs=(VMEM,) * len(sides),
         compiler_params=params(),
         cost_estimate=LONG,
     )(*operands)
@@ -371,12 +380,16 @@
     for group in early:
         pieces += firsts[group * GROUP : (group + 1) * GROUP]
         pieces += seconds[group * GROUP : (group + 1) * GROUP]
-    sides = (hidden, other, bounds)
-    starts = rank_call(tuple(early), depth, *sides, pieces, None)
-    *starts, far = lax.optimization_barrier((*starts, far))
+    both = (hidden, other)
+    start_mine, start_theirs = rank_call(
+        (0, 1), tuple(early), depth, rows, both, bounds, pieces, ()
+    )
+    start_theirs, far = lax.optimization_barrier((start_theirs, far))
     far = lax.ppermute(far, "tensor", swap)
     pieces = firsts[-GROUP:] + seconds[-GROUP:]
-    mine, theirs = rank_call((count - 1,), depth, *sides, pieces, starts)
+    late = (count - 1,)
+    (theirs,) = rank_call((1,), late, depth, rows, (other,), bounds, pieces, (start_theirs,))
+    (mine,) = rank_call((0,), late, depth, rows, (hidden,), bounds, pieces, (start_mine,))
 
     two = lax.ppermute(theirs, "groups", swap)
     one = lax.ppermute(mine, "tensor", swap)

time: 39.2 us -> 38.8 us (0.990)
  waiting for transfers between devices: 12.7 us -> 12.2 us
    ppermute x1, waiting for transfers between devices: 2.74 us -> 2.11 us  [per_device(): two = lax.ppermute(theirs, 'groups', swap)]
    pallas_call x2 -> x3, Pallas kernels: 1.66 us -> 1.83 us  [rank_call(): pl.pallas_call(functools.partial(rank_kernel, sides, groups, depth, last)...]
  transfers between devices with their start and end apart: 19 -> 19, of which waited for: 10 -> 10; matrix products, arithmetic and copies ran while one was open for 0% -> 0% of each run, Pallas kernels for 10% -> 11%
where the time goes in v14:
time: 38.8 us; the launch traced here: 38.7 us
  starting transfers between devices  19.5 us (50%)
  waiting for transfers between devices  12.2 us (31%)
  Pallas kernels  6.9 us (18%)
    ppermute x3, starting transfers between devices, per_device(): d = lax.ppermute(behind[1], 'batch', backward)  6.68 us
    ppermute x3, waiting for transfers between devices, per_device(): b = lax.ppermute(ahead[1], 'batch', forward)  3.91 us
    ppermute x3, starting transfers between devices, per_device(): c = lax.ppermute(behind[0], 'batch', backward)  3.48 us
    ppermute x3, starting transfers between devices, per_device(): b = lax.ppermute(ahead[1], 'batch', forward)  2.65 us
    ppermute x1, waiting for transfers between devices, per_device(): other = lax.ppermute(to_other, 'groups', swap)  2.64 us
    pallas_call x1, Pallas kernels, base_call(): pl.pallas_call(base_kernel, out_shape=(out, out), in_specs=[VMEM] * 2, ou...  2.35 us
    ppermute x1, waiting for transfers between devices, per_device(): two = lax.ppermute(theirs, 'groups', swap)  2.11 us
    ppermute x1, starting transfers between devices, per_device(): other = lax.ppermute(to_other, 'groups', swap)  1.97 us
  transfers between devices with their start and end apart: 19, of which 10 were waited for; matrix products, arithmetic and copies ran while one was open for 0% of the time, Pallas kernels for 11%

profile of v14, /device:TPU:0, one launch (start us, length us, event | category | flops | bytes accessed | tf_op | source)
XLA Modules:
  0.0 38.7 jit_solution(1691975038820246149)
XLA Ops:
  0.0 1.6 %shard_map.82 = (bf16[4112,128]{1,0:T(8,128)(2,1)S(1)}, bf16[64,1280]{1,0:T(8,128)(2,1)S(1)}, bf16[64,1280]{1,0:T(8,128)(2,1)S(1)}, s32[8,512]{1,0:T(8,128)S(1)}) custom-call(bf16[256,4096]{1,0:T(8,128)(2,1)} %refs_0_.1, bf16[64,4096]{1,0:T(8,128)(2,1)} %bitcast.6, bf16[64,512]{1,0:T(8,128)(2,1)} %bitcast.7, s32[1,4]{1,0:T(1,128)} %demand_ref.1, ...), custom_call_target="tpu_custom_call" | custom-call | tf_op jit(solution)/shard_map/pallas_call | solution.py:161
  1.6 3.1 %collective-permute-start.7 = (bf16[64,1280]{1,0:T(8,128)(2,1)S(1)}, bf16[64,1280]{1,0:T(8,128)(2,1)S(1)}, u32[]{:S(2)}, u32[]{:S(2)}) collective-permute-start(bf16[64,1280]{1,0:T(8,128)(2,1)S(1)} %get-tuple-element.29.refs_7_.refs_0_), channel_id=1, source_target_pairs={{2,0},{6,2},{10,6},{14,10},{12,14},{8,12},{4,8},{0,4},{3,1},{7,3},... | collective-permute-start | bytes 491528 | tf_op jit(solution)/shard_map/ppermute | solution.py:365
  4.7 0.0 collective-permute-start.2
  4.7 2.0 %collective-permute-start.14 = (bf16[4112,128]{1,0:T(8,128)(2,1)S(1)}, bf16[4112,128]{1,0:T(8,128)(2,1)S(1)}, u32[]{:S(2)}, u32[]{:S(2)}) collective-permute-start(bf16[4112,128]{1,0:T(8,128)(2,1)S(1)} %get-tuple-element.30), channel_id=1, source_target_pairs={{0,16},{16,0},{1,17},{17,1},{2,18},{18,2},{3,19},{19,3},{4,20},{20... | collective-permute-start | bytes 3158024 | tf_op jit(solution)/shard_map/ppermute | solution.py:375
  6.7 0.0 slice-start
  6.7 1.5 %collective-permute-start.9 = (bf16[64,1280]{1,0:T(8,128)(2,1)S(1)}, bf16[64,1280]{1,0:T(8,128)(2,1)S(1)}, u32[]{:S(2)}, u32[]{:S(2)}) collective-permute-start(bf16[64,1280]{1,0:T(8,128)(2,1)S(1)} %get-tuple-element.29.refs_7_.refs_0_), channel_id=1, source_target_pairs={{0,2},{2,6},{6,10},{10,14},{14,12},{12,8},{8,4},{4,0},{1,3},{3,7},... | collective-permute-start | bytes 491528 | tf_op jit(solution)/shard_map/ppermute | solution.py:366
  8.2 0.5 %collective-permute-start = (bf16[64,1280]{1,0:T(8,128)(2,1)S(1)}, bf16[64,1280]{1,0:T(8,128)(2,1)S(1)}, u32[]{:S(2)}, u32[]{:S(2)}) collective-permute-start(bf16[64,1280]{1,0:T(8,128)(2,1)S(1)} %get-tuple-element.28.refs_3_), channel_id=1, source_target_pairs={{2,0},{6,2},{10,6},{14,10},{12,14},{8,12},{4,8},{0,4},{3,1},{7,3},... | collective-permute-start | bytes 491528 | tf_op jit(solution)/shard_map/ppermute | solution.py:367
  8.7 0.1 collective-permute-done.7.refs_9_.refs_2_
  8.8 2.3 %collective-permute-start.8 = (bf16[64,1280]{1,0:T(8,128)(2,1)S(1)}, bf16[64,1280]{1,0:T(8,128)(2,1)S(1)}, u32[]{:S(2)}, u32[]{:S(2)}) collective-permute-start(bf16[64,1280]{1,0:T(8,128)(2,1)S(1)} %collective-permute-done.7.refs_9_.refs_2_), channel_id=1, source_target_pairs={{2,0},{6,2},{10,6},{14,10},{12,14},{8,12},{4,8},{0,4},{3,1},{7,3},... | collective-permute-start | bytes 491528 | tf_op jit(solution)/shard_map/ppermute | solution.py:365
  11.1 0.7 %collective-permute-done.2.refs_4_ = bf16[64,1280]{1,0:T(8,128)(2,1)S(1)} collective-permute-done((bf16[64,1280]{1,0:T(8,128)(2,1)S(1)}, bf16[64,1280]{1,0:T(8,128)(2,1)S(1)}, u32[]{:S(2)}, u32[]{:S(2)}) %collective-permute-start.2) | collective-permute-done | bytes 163872 | tf_op jit(solution)/shard_map/ppermute | solution.py:364
  11.8 0.0 collective-permute-start.3
  11.8 3.5 %collective-permute-done.9.refs_8_.refs_1_ = bf16[64,1280]{1,0:T(8,128)(2,1)S(1)} collective-permute-done((bf16[64,1280]{1,0:T(8,128)(2,1)S(1)}, bf16[64,1280]{1,0:T(8,128)(2,1)S(1)}, u32[]{:S(2)}, u32[]{:S(2)}) %collective-permute-start.9) | collective-permute-done | bytes 163872 | tf_op jit(solution)/shard_map/ppermute | solution.py:366
  15.3 0.0 collective-permute-start.10
  15.3 0.0 collective-permute-done.refs_5_
  15.3 2.0 %collective-permute-start.1 = (bf16[64,1280]{1,0:T(8,128)(2,1)S(1)}, bf16[64,1280]{1,0:T(8,128)(2,1)S(1)}, u32[]{:S(2)}, u32[]{:S(2)}) collective-permute-start(bf16[64,1280]{1,0:T(8,128)(2,1)S(1)} %collective-permute-done.refs_5_), channel_id=1, source_target_pairs={{2,0},{6,2},{10,6},{14,10},{12,14},{8,12},{4,8},{0,4},{3,1},{7,3},... | collective-permute-start | bytes 491528 | tf_op jit(solution)/shard_map/ppermute | solution.py:367
  17.3 0.3 collective-permute-done.8.refs_6_.refs_4_
  17.6 1.3 %collective-permute-start.12 = (bf16[64,1280]{1,0:T(8,128)(2,1)S(1)}, bf16[64,1280]{1,0:T(8,128)(2,1)S(1)}, u32[]{:S(2)}, u32[]{:S(2)}) collective-permute-start(bf16[64,1280]{1,0:T(8,128)(2,1)S(1)} %collective-permute-done.8.refs_6_.refs_4_), channel_id=1, source_target_pairs={{2,0},{6,2},{10,6},{14,10},{12,14},{8,12},{4,8},{0,4},{3,1},{7,3},... | collective-permute-start | bytes 491528 | tf_op jit(solution)/shard_map/ppermute | solution.py:365
  18.9 0.0 collective-permute-done.3.refs_6_
  18.9 0.7 %collective-permute-start.4 = (bf16[64,1280]{1,0:T(8,128)(2,1)S(1)}, bf16[64,1280]{1,0:T(8,128)(2,1)S(1)}, u32[]{:S(2)}, u32[]{:S(2)}) collective-permute-start(bf16[64,1280]{1,0:T(8,128)(2,1)S(1)} %collective-permute-done.3.refs_6_), channel_id=1, source_target_pairs={{0,2},{2,6},{6,10},{10,14},{14,12},{12,8},{8,4},{4,0},{1,3},{3,7},... | collective-permute-start | bytes 491528 | tf_op jit(solution)/shard_map/ppermute | solution.py:364
  19.7 0.0 slice-done
  19.7 0.0 slice-done.1
  19.7 0.0 copy-done
  19.7 2.4 %shard_map.84 = (f32[256,512]{1,0:T(8,128)S(1)}, f32[256,512]{1,0:T(8,128)S(1)}) custom-call(bf16[256,4096]{1,0:T(8,128)(2,1)S(1)} %copy-done, bf16[4096,1024]{1,0:T(8,128)(2,1)S(1)} %bitcast.5), custom_call_target="tpu_custom_call" | custom-call | bytes 4194304 | tf_op jit(solution)/shard_map/pallas_call | solution.py:210
  22.1 0.4 %collective-permute-done.10.refs_10_.refs_3_ = bf16[64,1280]{1,0:T(8,128)(2,1)S(1)} collective-permute-done((bf16[64,1280]{1,0:T(8,128)(2,1)S(1)}, bf16[64,1280]{1,0:T(8,128)(2,1)S(1)}, u32[]{:S(2)}, u32[]{:S(2)}) %collective-permute-start.10) | collective-permute-done | bytes 163872 | tf_op jit(solution)/shard_map/ppermute | solution.py:366
  22.5 1.1 %collective-permute-start.11 = (bf16[64,1280]{1,0:T(8,128)(2,1)S(1)}, bf16[64,1280]{1,0:T(8,128)(2,1)S(1)}, u32[]{:S(2)}, u32[]{:S(2)}) collective-permute-start(bf16[64,1280]{1,0:T(8,128)(2,1)S(1)} %collective-permute-done.10.refs_10_.refs_3_), channel_id=1, source_target_pairs={{0,2},{2,6},{6,10},{10,14},{14,12},{12,8},{8,4},{4,0},{1,3},{3,7},... | collective-permute-start | bytes 491528 | tf_op jit(solution)/shard_map/ppermute | solution.py:366
  23.5 0.0 collective-permute-done.1.refs_2_
  23.5 0.9 %collective-permute-start.5 = (bf16[64,1280]{1,0:T(8,128)(2,1)S(1)}, bf16[64,1280]{1,0:T(8,128)(2,1)S(1)}, u32[]{:S(2)}, u32[]{:S(2)}) collective-permute-start(bf16[64,1280]{1,0:T(8,128)(2,1)S(1)} %collective-permute-done.1.refs_2_), channel_id=1, source_target_pairs={{2,0},{6,2},{10,6},{14,10},{12,14},{8,12},{4,8},{0,4},{3,1},{7,3},... | collective-permute-start | bytes 491528 | tf_op jit(solution)/shard_map/ppermute | solution.py:367
  24.5 0.0 collective-permute-done.12.refs_8_.refs_6_
  24.5 1.6 %collective-permute-start.13 = (bf16[64,1280]{1,0:T(8,128)(2,1)S(1)}, bf16[64,1280]{1,0:T(8,128)(2,1)S(1)}, u32[]{:S(2)}, u32[]{:S(2)}) collective-permute-start(bf16[64,1280]{1,0:T(8,128)(2,1)S(1)} %collective-permute-done.12.refs_8_.refs_6_), channel_id=1, source_target_pairs={{2,0},{6,2},{10,6},{14,10},{12,14},{8,12},{4,8},{0,4},{3,1},{7,3},... | collective-permute-start | bytes 491528 | tf_op jit(solution)/shard_map/ppermute | solution.py:372
  26.1 0.0 collective-permute-done.4.refs_3_
  26.1 0.7 %collective-permute-start.6 = (bf16[64,1280]{1,0:T(8,128)(2,1)S(1)}, bf16[64,1280]{1,0:T(8,128)(2,1)S(1)}, u32[]{:S(2)}, u32[]{:S(2)}) collective-permute-start(bf16[64,1280]{1,0:T(8,128)(2,1)S(1)} %collective-permute-done.4.refs_3_), channel_id=1, source_target_pairs={{0,2},{2,6},{6,10},{10,14},{14,12},{12,8},{8,4},{4,0},{1,3},{3,7},... | collective-permute-start | bytes 491528 | tf_op jit(solution)/shard_map/ppermute | solution.py:371
  26.8 2.6 %collective-permute-done.14.refs_1_.refs_0_ = bf16[4112,128]{1,0:T(8,128)(2,1)S(1)} collective-permute-done((bf16[4112,128]{1,0:T(8,128)(2,1)S(1)}, bf16[4112,128]{1,0:T(8,128)(2,1)S(1)}, u32[]{:S(2)}, u32[]{:S(2)}) %collective-permute-start.14) | collective-permute-done | bytes 1052704 | tf_op jit(solution)/shard_map/ppermute | solution.py:375
  29.4 0.7 %shard_map.85 = (f32[256,128]{1,0:T(8,128)S(1)}, f32[256,128]{1,0:T(8,128)S(1)}) custom-call(bf16[256,4096]{1,0:T(8,128)(2,1)S(1)} %copy-done, bf16[4112,128]{1,0:T(8,128)(2,1)S(1)} %collective-permute-done.14.refs_1_.refs_0_, s32[8,512]{1,0:T(8,128)S(1)} %shard_map.83.refs_2_.refs_1_.bounds_ref, bf16[64,1280]{1,0:T(8,128)(2,1)S(1)} %get-tuple-element.28.refs_3_, ...), custom_call_target="tpu_custom_call" | custom-call | flops 8589934592 | bytes 16777216 | tf_op jit(solution)/shard_map/pallas_call | solution.py:296
  30.1 0.1 collective-permute-start.18
  30.2 0.0 collective-permute-done.11.refs_7_.refs_5_
  30.2 0.0 collective-permute-done.5.refs_4_
  30.2 0.4 collective-permute-done.13.refs_9_.refs_7_
  30.6 0.8 %collective-permute-done.6.refs_5_ = bf16[64,1280]{1,0:T(8,128)(2,1)S(1)} collective-permute-done((bf16[64,1280]{1,0:T(8,128)(2,1)S(1)}, bf16[64,1280]{1,0:T(8,128)(2,1)S(1)}, u32[]{:S(2)}, u32[]{:S(2)}) %collective-permute-start.6) | collective-permute-done | bytes 163872 | tf_op jit(solution)/shard_map/ppermute | solution.py:371
  31.4 0.5 %shard_map.87 = f32[128,128]{1,0:T(8,128)S(1)} custom-call(bf16[4112,128]{1,0:T(8,128)(2,1)S(1)} %collective-permute-done.14.refs_1_.refs_0_, s32[8,512]{1,0:T(8,128)S(1)} %shard_map.83.refs_2_.refs_1_.bounds_ref, bf16[64,1280]{1,0:T(8,128)(2,1)S(1)} %collective-permute-done.1.refs_2_, bf16[64,1280]{1,0:T(8,128)(2,1)S(1)} %collective-permute-done.4.refs_3_, ...), custom_call_target="tpu_custom_call" | custom-call | flops 8589934592 | bytes 16777216 | tf_op jit(solution)/shard_map/pallas_call | solution.py:296
  32.0 1.6 %collective-permute-start.16 = (f32[128,128]{1,0:T(8,128)S(1)}, f32[128,128]{1,0:T(8,128)S(1)}, u32[]{:S(2)}, u32[]{:S(2)}) collective-permute-start(f32[128,128]{1,0:T(8,128)S(1)} %shard_map.87), channel_id=1, source_target_pairs={{0,16},{16,0},{1,17},{17,1},{2,18},{18,2},{3,19},{19,3},{4,20},{20... | collective-permute-start | bytes 196616 | tf_op jit(solution)/shard_map/ppermute | solution.py:394
  33.5 0.5 %shard_map.86.mine = f32[128,128]{1,0:T(8,128)S(1)} custom-call(bf16[256,4096]{1,0:T(8,128)(2,1)S(1)} %copy-done, s32[8,512]{1,0:T(8,128)S(1)} %shard_map.83.refs_2_.refs_1_.bounds_ref, bf16[64,1280]{1,0:T(8,128)(2,1)S(1)} %collective-permute-done.1.refs_2_, bf16[64,1280]{1,0:T(8,128)(2,1)S(1)} %collective-permute-done.4.refs_3_, ...), custom_call_target="tpu_custom_call" | custom-call | flops 8589934592 | bytes 16777216 | tf_op jit(solution)/shard_map/pallas_call | solution.py:296
  34.1 0.1 collective-permute-start.15
  34.2 2.1 %collective-permute-done.16.two = f32[128,128]{1,0:T(8,128)S(1)} collective-permute-done((f32[128,128]{1,0:T(8,128)S(1)}, f32[128,128]{1,0:T(8,128)S(1)}, u32[]{:S(2)}, u32[]{:S(2)}) %collective-permute-start.16) | collective-permute-done | bytes 65568 | tf_op jit(solution)/shard_map/ppermute | solution.py:394
  36.3 0.0 collective-permute-start.17
  36.3 0.0 collective-permute-done.15.one
  36.3 1.2 %collective-permute-done.17.three = f32[128,128]{1,0:T(8,128)S(1)} collective-permute-done((f32[128,128]{1,0:T(8,128)S(1)}, f32[128,128]{1,0:T(8,128)S(1)}, u32[]{:S(2)}, u32[]{:S(2)}) %collective-permute-start.17) | collective-permute-done | bytes 65568 | tf_op jit(solution)/shard_map/ppermute | solution.py:396
  37.5 0.0 collective-permute-done.18.far_ref
  37.5 1.1 %shard_map.88 = bf16[256,512]{1,0:T(8,128)(2,1)} custom-call(s32[8,512]{1,0:T(8,128)S(1)} %shard_map.83.refs_2_.refs_1_.bounds_ref, f32[128,128]{1,0:T(8,128)S(1)} %shard_map.86.mine, f32[128,128]{1,0:T(8,128)S(1)} %collective-permute-done.15.one, f32[128,128]{1,0:T(8,128)S(1)} %collective-permute-done.16.two, f32[128,128]{1,0:T(8,128)S(1)} %collective-permute-done.17.three, ...), custom_call_target="tpu_custom_call" | custom-call | tf_op jit(solution)/shard_map/pallas_call | solution.py:399
  (4 shorter events, 0.0 us)
Async XLA Ops:
  1.6 7.2 %collective-permute-start.7 = (bf16[64,1280]{1,0:T(8,128)(2,1)S(1)}, bf16[64,1280]{1,0:T(8,128)(2,1)S(1)}, u32[]{:S(2)}, u32[]{:S(2)}) collective-permute-start(bf16[64,1280]{1,0:T(8,128)(2,1)S(1)} %get-tuple-element.29.refs_7_.refs_0_), channel_id=1, source_target_pairs={{2,0},{6,2},{10,6},{14,10},{12,14},{8,12},{4,8},{0,4},{3,1},{7,3},... | collective-permute-start | bytes 491528 | tf_op jit(solution)/shard_map/ppermute | solution.py:365
  4.7 7.1 %collective-permute-start.2 = (bf16[64,1280]{1,0:T(8,128)(2,1)S(1)}, bf16[64,1280]{1,0:T(8,128)(2,1)S(1)}, u32[]{:S(2)}, u32[]{:S(2)}) collective-permute-start(bf16[64,1280]{1,0:T(8,128)(2,1)S(1)} %get-tuple-element.28.refs_3_), channel_id=1, source_target_pairs={{0,2},{2,6},{6,10},{10,14},{14,12},{12,8},{8,4},{4,0},{1,3},{3,7},... | collective-permute-start | bytes 491528 | tf_op jit(solution)/shard_map/ppermute | solution.py:364
  4.7 24.7 %collective-permute-start.14 = (bf16[4112,128]{1,0:T(8,128)(2,1)S(1)}, bf16[4112,128]{1,0:T(8,128)(2,1)S(1)}, u32[]{:S(2)}, u32[]{:S(2)}) collective-permute-start(bf16[4112,128]{1,0:T(8,128)(2,1)S(1)} %get-tuple-element.30), channel_id=1, source_target_pairs={{0,16},{16,0},{1,17},{17,1},{2,18},{18,2},{3,19},{19,3},{4,20},{20... | collective-permute-start | bytes 3158024 | tf_op jit(solution)/shard_map/ppermute | solution.py:375
  6.7 13.0 %slice-start = ((s8[8388608]{0:T(1024)(128)(4,1)}), s8[4194304]{0:T(1024)(128)(4,1)S(1)}, s32[]{:S(2)}) async-start(s8[8388608]{0:T(1024)(128)(4,1)} %bitcast.4), calls=%async_computation | async-start | bytes 8388608
  6.7 13.0 %slice-start.1 = ((s8[8388608]{0:T(1024)(128)(4,1)}), s8[4194304]{0:T(1024)(128)(4,1)S(1)}, s32[]{:S(2)}) async-start(s8[8388608]{0:T(1024)(128)(4,1)} %bitcast.4), calls=%async_computation.1 | async-start | bytes 8388608
  6.7 13.0 %copy-start = (bf16[256,4096]{1,0:T(8,128)(2,1)S(1)}, bf16[256,4096]{1,0:T(8,128)(2,1)}, u32[]{:S(2)}) copy-start(bf16[256,4096]{1,0:T(8,128)(2,1)} %refs_0_.1) | copy-start | bytes 6291460
  6.7 8.7 %collective-permute-start.9 = (bf16[64,1280]{1,0:T(8,128)(2,1)S(1)}, bf16[64,1280]{1,0:T(8,128)(2,1)S(1)}, u32[]{:S(2)}, u32[]{:S(2)}) collective-permute-start(bf16[64,1280]{1,0:T(8,128)(2,1)S(1)} %get-tuple-element.29.refs_7_.refs_0_), channel_id=1, source_target_pairs={{0,2},{2,6},{6,10},{10,14},{14,12},{12,8},{8,4},{4,0},{1,3},{3,7},... | collective-permute-start | bytes 491528 | tf_op jit(solution)/shard_map/ppermute | solution.py:366
  8.2 7.1 %collective-permute-start = (bf16[64,1280]{1,0:T(8,128)(2,1)S(1)}, bf16[64,1280]{1,0:T(8,128)(2,1)S(1)}, u32[]{:S(2)}, u32[]{:S(2)}) collective-permute-start(bf16[64,1280]{1,0:T(8,128)(2,1)S(1)} %get-tuple-element.28.refs_3_), channel_id=1, source_target_pairs={{2,0},{6,2},{10,6},{14,10},{12,14},{8,12},{4,8},{0,4},{3,1},{7,3},... | collective-permute-start | bytes 491528 | tf_op jit(solution)/shard_map/ppermute | solution.py:367
  8.8 8.9 %collective-permute-start.8 = (bf16[64,1280]{1,0:T(8,128)(2,1)S(1)}, bf16[64,1280]{1,0:T(8,128)(2,1)S(1)}, u32[]{:S(2)}, u32[]{:S(2)}) collective-permute-start(bf16[64,1280]{1,0:T(8,128)(2,1)S(1)} %collective-permute-done.7.refs_9_.refs_2_), channel_id=1, source_target_pairs={{2,0},{6,2},{10,6},{14,10},{12,14},{8,12},{4,8},{0,4},{3,1},{7,3},... | collective-permute-start | bytes 491528 | tf_op jit(solution)/shard_map/ppermute | solution.py:365
  11.8 7.1 %collective-permute-start.3 = (bf16[64,1280]{1,0:T(8,128)(2,1)S(1)}, bf16[64,1280]{1,0:T(8,128)(2,1)S(1)}, u32[]{:S(2)}, u32[]{:S(2)}) collective-permute-start(bf16[64,1280]{1,0:T(8,128)(2,1)S(1)} %collective-permute-done.2.refs_4_), channel_id=1, source_target_pairs={{0,2},{2,6},{6,10},{10,14},{14,12},{12,8},{8,4},{4,0},{1,3},{3,7},... | collective-permute-start | bytes 491528 | tf_op jit(solution)/shard_map/ppermute | solution.py:364
  15.3 7.1 %collective-permute-start.10 = (bf16[64,1280]{1,0:T(8,128)(2,1)S(1)}, bf16[64,1280]{1,0:T(8,128)(2,1)S(1)}, u32[]{:S(2)}, u32[]{:S(2)}) collective-permute-start(bf16[64,1280]{1,0:T(8,128)(2,1)S(1)} %collective-permute-done.9.refs_8_.refs_1_), channel_id=1, source_target_pairs={{0,2},{2,6},{6,10},{10,14},{14,12},{12,8},{8,4},{4,0},{1,3},{3,7},... | collective-permute-start | bytes 491528 | tf_op jit(solution)/shard_map/ppermute | solution.py:366
  15.3 8.2 %collective-permute-start.1 = (bf16[64,1280]{1,0:T(8,128)(2,1)S(1)}, bf16[64,1280]{1,0:T(8,128)(2,1)S(1)}, u32[]{:S(2)}, u32[]{:S(2)}) collective-permute-start(bf16[64,1280]{1,0:T(8,128)(2,1)S(1)} %collective-permute-done.refs_5_), channel_id=1, source_target_pairs={{2,0},{6,2},{10,6},{14,10},{12,14},{8,12},{4,8},{0,4},{3,1},{7,3},... | collective-permute-start | bytes 491528 | tf_op jit(solution)/shard_map/ppermute | solution.py:367
  17.6 6.8 %collective-permute-start.12 = (bf16[64,1280]{1,0:T(8,128)(2,1)S(1)}, bf16[64,1280]{1,0:T(8,128)(2,1)S(1)}, u32[]{:S(2)}, u32[]{:S(2)}) collective-permute-start(bf16[64,1280]{1,0:T(8,128)(2,1)S(1)} %collective-permute-done.8.refs_6_.refs_4_), channel_id=1, source_target_pairs={{2,0},{6,2},{10,6},{14,10},{12,14},{8,12},{4,8},{0,4},{3,1},{7,3},... | collective-permute-start | bytes 491528 | tf_op jit(solution)/shard_map/ppermute | solution.py:365
  18.9 7.1 %collective-permute-start.4 = (bf16[64,1280]{1,0:T(8,128)(2,1)S(1)}, bf16[64,1280]{1,0:T(8,128)(2,1)S(1)}, u32[]{:S(2)}, u32[]{:S(2)}) collective-permute-start(bf16[64,1280]{1,0:T(8,128)(2,1)S(1)} %collective-permute-done.3.refs_6_), channel_id=1, source_target_pairs={{0,2},{2,6},{6,10},{10,14},{14,12},{12,8},{8,4},{4,0},{1,3},{3,7},... | collective-permute-start | bytes 491528 | tf_op jit(solution)/shard_map/ppermute | solution.py:364
  22.5 7.8 %collective-permute-start.11 = (bf16[64,1280]{1,0:T(8,128)(2,1)S(1)}, bf16[64,1280]{1,0:T(8,128)(2,1)S(1)}, u32[]{:S(2)}, u32[]{:S(2)}) collective-permute-start(bf16[64,1280]{1,0:T(8,128)(2,1)S(1)} %collective-permute-done.10.refs_10_.refs_3_), channel_id=1, source_target_pairs={{0,2},{2,6},{6,10},{10,14},{14,12},{12,8},{8,4},{4,0},{1,3},{3,7},... | collective-permute-start | bytes 491528 | tf_op jit(solution)/shard_map/ppermute | solution.py:366
  23.5 6.7 %collective-permute-start.5 = (bf16[64,1280]{1,0:T(8,128)(2,1)S(1)}, bf16[64,1280]{1,0:T(8,128)(2,1)S(1)}, u32[]{:S(2)}, u32[]{:S(2)}) collective-permute-start(bf16[64,1280]{1,0:T(8,128)(2,1)S(1)} %collective-permute-done.1.refs_2_), channel_id=1, source_target_pairs={{2,0},{6,2},{10,6},{14,10},{12,14},{8,12},{4,8},{0,4},{3,1},{7,3},... | collective-permute-start | bytes 491528 | tf_op jit(solution)/shard_map/ppermute | solution.py:367
  24.5 6.1 %collective-permute-start.13 = (bf16[64,1280]{1,0:T(8,128)(2,1)S(1)}, bf16[64,1280]{1,0:T(8,128)(2,1)S(1)}, u32[]{:S(2)}, u32[]{:S(2)}) collective-permute-start(bf16[64,1280]{1,0:T(8,128)(2,1)S(1)} %collective-permute-done.12.refs_8_.refs_6_), channel_id=1, source_target_pairs={{2,0},{6,2},{10,6},{14,10},{12,14},{8,12},{4,8},{0,4},{3,1},{7,3},... | collective-permute-start | bytes 491528 | tf_op jit(solution)/shard_map/ppermute | solution.py:372
  26.1 5.3 %collective-permute-start.6 = (bf16[64,1280]{1,0:T(8,128)(2,1)S(1)}, bf16[64,1280]{1,0:T(8,128)(2,1)S(1)}, u32[]{:S(2)}, u32[]{:S(2)}) collective-permute-start(bf16[64,1280]{1,0:T(8,128)(2,1)S(1)} %collective-permute-done.4.refs_3_), channel_id=1, source_target_pairs={{0,2},{2,6},{6,10},{10,14},{14,12},{12,8},{8,4},{4,0},{1,3},{3,7},... | collective-permute-start | bytes 491528 | tf_op jit(solution)/shard_map/ppermute | solution.py:371
  30.1 7.4 %collective-permute-start.18 = (f32[256,512]{1,0:T(8,128)S(1)}, f32[256,512]{1,0:T(8,128)S(1)}, u32[]{:S(2)}, u32[]{:S(2)}) collective-permute-start(f32[256,512]{1,0:T(8,128)S(1)} %get-tuple-element.36), channel_id=1, source_target_pairs={{0,1},{1,0},{2,3},{3,2},{4,5},{5,4},{6,7},{7,6},{8,9},{9,8},{10,11... | collective-permute-start | bytes 1572872 | tf_op jit(solution)/shard_map/ppermute | solution.py:388
  32.0 4.3 %collective-permute-start.16 = (f32[128,128]{1,0:T(8,128)S(1)}, f32[128,128]{1,0:T(8,128)S(1)}, u32[]{:S(2)}, u32[]{:S(2)}) collective-permute-start(f32[128,128]{1,0:T(8,128)S(1)} %shard_map.87), channel_id=1, source_target_pairs={{0,16},{16,0},{1,17},{17,1},{2,18},{18,2},{3,19},{19,3},{4,20},{20... | collective-permute-start | bytes 196616 | tf_op jit(solution)/shard_map/ppermute | solution.py:394
  34.1 2.2 %collective-permute-start.15 = (f32[128,128]{1,0:T(8,128)S(1)}, f32[128,128]{1,0:T(8,128)S(1)}, u32[]{:S(2)}, u32[]{:S(2)}) collective-permute-start(f32[128,128]{1,0:T(8,128)S(1)} %shard_map.86.mine), channel_id=1, source_target_pairs={{0,1},{1,0},{2,3},{3,2},{4,5},{5,4},{6,7},{7,6},{8,9},{9,8},{10,11... | collective-permute-start | bytes 196616 | tf_op jit(solution)/shard_map/ppermute | solution.py:395
  36.3 1.3 %collective-permute-start.17 = (f32[128,128]{1,0:T(8,128)S(1)}, f32[128,128]{1,0:T(8,128)S(1)}, u32[]{:S(2)}, u32[]{:S(2)}) collective-permute-start(f32[128,128]{1,0:T(8,128)S(1)} %collective-permute-done.16.two), channel_id=1, source_target_pairs={{0,1},{1,0},{2,3},{3,2},{4,5},{5,4},{6,7},{7,6},{8,9},{9,8},{10,11... | collective-permute-start | bytes 196616 | tf_op jit(solution)/shard_map/ppermute | solution.py:396

commit v15 on v14

--- a/solution.py
+++ b/solution.py
@@ -392,8 +392,8 @@
     (mine,) = rank_call((0,), late, depth, rows, (hidden,), bounds, pieces, (start_mine,))
 
     two = lax.ppermute(theirs, "groups", swap)
+    three = lax.ppermute(theirs, ("groups", "tensor"), [(0, 3), (1, 2), (2, 1), (3, 0)])
     one = lax.ppermute(mine, "tensor", swap)
-    three = lax.ppermute(two, "tensor", swap)
 
     operands = [bounds, mine, one, two, three, near, far, *seconds]
     return pl.pallas_call(

time: 38.8 us -> 39 us (level)
  starting transfers between devices: 19.5 us -> 20 us
  waiting for transfers between devices: 12.2 us -> 11.8 us
    ppermute x1, waiting for transfers between devices: 2.11 us -> 1.49 us  [per_device(): two = lax.ppermute(theirs, 'groups', swap)]
    ppermute x1, starting transfers between devices: 0.07 us -> 0.62 us  [per_device(): far = lax.ppermute(far, 'tensor', swap)]
  transfers between devices with their start and end apart: 19 -> 19, of which waited for: 10 -> 10; matrix products, arithmetic and copies ran while one was open for 0% -> 0% of each run, Pallas kernels for 11% -> 9%
where the time goes in v15:
time: 39 us; the launch traced here: 38.8 us
  starting transfers between devices  20 us (51%)
  waiting for transfers between devices  11.8 us (30%)
  Pallas kernels  6.9 us (18%)
    ppermute x3, starting transfers between devices, per_device(): d = lax.ppermute(behind[1], 'batch', backward)  6.68 us
    ppermute x3, waiting for transfers between devices, per_device(): b = lax.ppermute(ahead[1], 'batch', forward)  3.91 us
    ppermute x3, starting transfers between devices, per_device(): c = lax.ppermute(behind[0], 'batch', backward)  3.48 us
    ppermute x3, starting transfers between devices, per_device(): b = lax.ppermute(ahead[1], 'batch', forward)  2.65 us
    ppermute x1, waiting for transfers between devices, per_device(): other = lax.ppermute(to_other, 'groups', swap)  2.64 us
    pallas_call x1, Pallas kernels, base_call(): pl.pallas_call(base_kernel, out_shape=(out, out), in_specs=[VMEM] * 2, ou...  2.35 us
    ppermute x1, starting transfers between devices, per_device(): other = lax.ppermute(to_other, 'groups', swap)  1.97 us
    pallas_call x3, Pallas kernels, rank_call(): pl.pallas_call(functools.partial(rank_kernel, sides, groups, depth, last)...  1.83 us
  transfers between devices with their start and end apart: 19, of which 10 were waited for; matrix products, arithmetic and copies ran while one was open for 0% of the time, Pallas kernels for 9%

profile of v15, /device:TPU:0, one launch (start us, length us, event | category | flops | bytes accessed | tf_op | source)
XLA Modules:
  0.0 38.8 jit_solution(15387248999086082515)
XLA Ops:
  0.0 1.6 %shard_map.82 = (bf16[4112,128]{1,0:T(8,128)(2,1)S(1)}, bf16[64,1280]{1,0:T(8,128)(2,1)S(1)}, bf16[64,1280]{1,0:T(8,128)(2,1)S(1)}, s32[8,512]{1,0:T(8,128)S(1)}) custom-call(bf16[256,4096]{1,0:T(8,128)(2,1)} %refs_0_.1, bf16[64,4096]{1,0:T(8,128)(2,1)} %bitcast.6, bf16[64,512]{1,0:T(8,128)(2,1)} %bitcast.7, s32[1,4]{1,0:T(1,128)} %demand_ref.1, ...), custom_call_target="tpu_custom_call" | custom-call | tf_op jit(solution)/shard_map/pallas_call | solution.py:161
  1.6 3.1 %collective-permute-start.7 = (bf16[64,1280]{1,0:T(8,128)(2,1)S(1)}, bf16[64,1280]{1,0:T(8,128)(2,1)S(1)}, u32[]{:S(2)}, u32[]{:S(2)}) collective-permute-start(bf16[64,1280]{1,0:T(8,128)(2,1)S(1)} %get-tuple-element.29.refs_7_.refs_0_), channel_id=1, source_target_pairs={{2,0},{6,2},{10,6},{14,10},{12,14},{8,12},{4,8},{0,4},{3,1},{7,3},... | collective-permute-start | bytes 491528 | tf_op jit(solution)/shard_map/ppermute | solution.py:365
  4.7 0.0 collective-permute-start.2
  4.7 2.0 %collective-permute-start.14 = (bf16[4112,128]{1,0:T(8,128)(2,1)S(1)}, bf16[4112,128]{1,0:T(8,128)(2,1)S(1)}, u32[]{:S(2)}, u32[]{:S(2)}) collective-permute-start(bf16[4112,128]{1,0:T(8,128)(2,1)S(1)} %get-tuple-element.30), channel_id=1, source_target_pairs={{0,16},{16,0},{1,17},{17,1},{2,18},{18,2},{3,19},{19,3},{4,20},{20... | collective-permute-start | bytes 3158024 | tf_op jit(solution)/shard_map/ppermute | solution.py:375
  6.7 0.0 slice-start
  6.7 1.5 %collective-permute-start.9 = (bf16[64,1280]{1,0:T(8,128)(2,1)S(1)}, bf16[64,1280]{1,0:T(8,128)(2,1)S(1)}, u32[]{:S(2)}, u32[]{:S(2)}) collective-permute-start(bf16[64,1280]{1,0:T(8,128)(2,1)S(1)} %get-tuple-element.29.refs_7_.refs_0_), channel_id=1, source_target_pairs={{0,2},{2,6},{6,10},{10,14},{14,12},{12,8},{8,4},{4,0},{1,3},{3,7},... | collective-permute-start | bytes 491528 | tf_op jit(solution)/shard_map/ppermute | solution.py:366
  8.2 0.5 %collective-permute-start = (bf16[64,1280]{1,0:T(8,128)(2,1)S(1)}, bf16[64,1280]{1,0:T(8,128)(2,1)S(1)}, u32[]{:S(2)}, u32[]{:S(2)}) collective-permute-start(bf16[64,1280]{1,0:T(8,128)(2,1)S(1)} %get-tuple-element.28.refs_3_), channel_id=1, source_target_pairs={{2,0},{6,2},{10,6},{14,10},{12,14},{8,12},{4,8},{0,4},{3,1},{7,3},... | collective-permute-start | bytes 491528 | tf_op jit(solution)/shard_map/ppermute | solution.py:367
  8.7 0.1 collective-permute-done.7.refs_9_.refs_2_
  8.8 2.3 %collective-permute-start.8 = (bf16[64,1280]{1,0:T(8,128)(2,1)S(1)}, bf16[64,1280]{1,0:T(8,128)(2,1)S(1)}, u32[]{:S(2)}, u32[]{:S(2)}) collective-permute-start(bf16[64,1280]{1,0:T(8,128)(2,1)S(1)} %collective-permute-done.7.refs_9_.refs_2_), channel_id=1, source_target_pairs={{2,0},{6,2},{10,6},{14,10},{12,14},{8,12},{4,8},{0,4},{3,1},{7,3},... | collective-permute-start | bytes 491528 | tf_op jit(solution)/shard_map/ppermute | solution.py:365
  11.1 0.7 %collective-permute-done.2.refs_4_ = bf16[64,1280]{1,0:T(8,128)(2,1)S(1)} collective-permute-done((bf16[64,1280]{1,0:T(8,128)(2,1)S(1)}, bf16[64,1280]{1,0:T(8,128)(2,1)S(1)}, u32[]{:S(2)}, u32[]{:S(2)}) %collective-permute-start.2) | collective-permute-done | bytes 163872 | tf_op jit(solution)/shard_map/ppermute | solution.py:364
  11.8 0.0 collective-permute-start.3
  11.8 3.5 %collective-permute-done.9.refs_8_.refs_1_ = bf16[64,1280]{1,0:T(8,128)(2,1)S(1)} collective-permute-done((bf16[64,1280]{1,0:T(8,128)(2,1)S(1)}, bf16[64,1280]{1,0:T(8,128)(2,1)S(1)}, u32[]{:S(2)}, u32[]{:S(2)}) %collective-permute-start.9) | collective-permute-done | bytes 163872 | tf_op jit(solution)/shard_map/ppermute | solution.py:366
  15.3 0.0 collective-permute-start.10
  15.3 0.0 collective-permute-done.refs_5_
  15.3 2.0 %collective-permute-start.1 = (bf16[64,1280]{1,0:T(8,128)(2,1)S(1)}, bf16[64,1280]{1,0:T(8,128)(2,1)S(1)}, u32[]{:S(2)}, u32[]{:S(2)}) collective-permute-start(bf16[64,1280]{1,0:T(8,128)(2,1)S(1)} %collective-permute-done.refs_5_), channel_id=1, source_target_pairs={{2,0},{6,2},{10,6},{14,10},{12,14},{8,12},{4,8},{0,4},{3,1},{7,3},... | collective-permute-start | bytes 491528 | tf_op jit(solution)/shard_map/ppermute | solution.py:367
  17.3 0.3 collective-permute-done.8.refs_6_.refs_4_
  17.6 1.3 %collective-permute-start.12 = (bf16[64,1280]{1,0:T(8,128)(2,1)S(1)}, bf16[64,1280]{1,0:T(8,128)(2,1)S(1)}, u32[]{:S(2)}, u32[]{:S(2)}) collective-permute-start(bf16[64,1280]{1,0:T(8,128)(2,1)S(1)} %collective-permute-done.8.refs_6_.refs_4_), channel_id=1, source_target_pairs={{2,0},{6,2},{10,6},{14,10},{12,14},{8,12},{4,8},{0,4},{3,1},{7,3},... | collective-permute-start | bytes 491528 | tf_op jit(solution)/shard_map/ppermute | solution.py:365
  18.9 0.0 collective-permute-done.3.refs_6_
  18.9 0.7 %collective-permute-start.4 = (bf16[64,1280]{1,0:T(8,128)(2,1)S(1)}, bf16[64,1280]{1,0:T(8,128)(2,1)S(1)}, u32[]{:S(2)}, u32[]{:S(2)}) collective-permute-start(bf16[64,1280]{1,0:T(8,128)(2,1)S(1)} %collective-permute-done.3.refs_6_), channel_id=1, source_target_pairs={{0,2},{2,6},{6,10},{10,14},{14,12},{12,8},{8,4},{4,0},{1,3},{3,7},... | collective-permute-start | bytes 491528 | tf_op jit(solution)/shard_map/ppermute | solution.py:364
  19.7 0.0 slice-done
  19.7 0.0 slice-done.1
  19.7 0.0 copy-done
  19.7 2.4 %shard_map.84 = (f32[256,512]{1,0:T(8,128)S(1)}, f32[256,512]{1,0:T(8,128)S(1)}) custom-call(bf16[256,4096]{1,0:T(8,128)(2,1)S(1)} %copy-done, bf16[4096,1024]{1,0:T(8,128)(2,1)S(1)} %bitcast.5), custom_call_target="tpu_custom_call" | custom-call | bytes 4194304 | tf_op jit(solution)/shard_map/pallas_call | solution.py:210
  22.1 0.4 %collective-permute-done.10.refs_10_.refs_3_ = bf16[64,1280]{1,0:T(8,128)(2,1)S(1)} collective-permute-done((bf16[64,1280]{1,0:T(8,128)(2,1)S(1)}, bf16[64,1280]{1,0:T(8,128)(2,1)S(1)}, u32[]{:S(2)}, u32[]{:S(2)}) %collective-permute-start.10) | collective-permute-done | bytes 163872 | tf_op jit(solution)/shard_map/ppermute | solution.py:366
  22.5 1.1 %collective-permute-start.11 = (bf16[64,1280]{1,0:T(8,128)(2,1)S(1)}, bf16[64,1280]{1,0:T(8,128)(2,1)S(1)}, u32[]{:S(2)}, u32[]{:S(2)}) collective-permute-start(bf16[64,1280]{1,0:T(8,128)(2,1)S(1)} %collective-permute-done.10.refs_10_.refs_3_), channel_id=1, source_target_pairs={{0,2},{2,6},{6,10},{10,14},{14,12},{12,8},{8,4},{4,0},{1,3},{3,7},... | collective-permute-start | bytes 491528 | tf_op jit(solution)/shard_map/ppermute | solution.py:366
  23.5 0.0 collective-permute-done.1.refs_2_
  23.5 0.9 %collective-permute-start.5 = (bf16[64,1280]{1,0:T(8,128)(2,1)S(1)}, bf16[64,1280]{1,0:T(8,128)(2,1)S(1)}, u32[]{:S(2)}, u32[]{:S(2)}) collective-permute-start(bf16[64,1280]{1,0:T(8,128)(2,1)S(1)} %collective-permute-done.1.refs_2_), channel_id=1, source_target_pairs={{2,0},{6,2},{10,6},{14,10},{12,14},{8,12},{4,8},{0,4},{3,1},{7,3},... | collective-permute-start | bytes 491528 | tf_op jit(solution)/shard_map/ppermute | solution.py:367
  24.5 0.0 collective-permute-done.12.refs_8_.refs_6_
  24.5 1.6 %collective-permute-start.13 = (bf16[64,1280]{1,0:T(8,128)(2,1)S(1)}, bf16[64,1280]{1,0:T(8,128)(2,1)S(1)}, u32[]{:S(2)}, u32[]{:S(2)}) collective-permute-start(bf16[64,1280]{1,0:T(8,128)(2,1)S(1)} %collective-permute-done.12.refs_8_.refs_6_), channel_id=1, source_target_pairs={{2,0},{6,2},{10,6},{14,10},{12,14},{8,12},{4,8},{0,4},{3,1},{7,3},... | collective-permute-start | bytes 491528 | tf_op jit(solution)/shard_map/ppermute | solution.py:372
  26.1 0.0 collective-permute-done.4.refs_3_
  26.1 0.7 %collective-permute-start.6 = (bf16[64,1280]{1,0:T(8,128)(2,1)S(1)}, bf16[64,1280]{1,0:T(8,128)(2,1)S(1)}, u32[]{:S(2)}, u32[]{:S(2)}) collective-permute-start(bf16[64,1280]{1,0:T(8,128)(2,1)S(1)} %collective-permute-done.4.refs_3_), channel_id=1, source_target_pairs={{0,2},{2,6},{6,10},{10,14},{14,12},{12,8},{8,4},{4,0},{1,3},{3,7},... | collective-permute-start | bytes 491528 | tf_op jit(solution)/shard_map/ppermute | solution.py:371
  26.8 2.6 %collective-permute-done.14.refs_1_.refs_0_ = bf16[4112,128]{1,0:T(8,128)(2,1)S(1)} collective-permute-done((bf16[4112,128]{1,0:T(8,128)(2,1)S(1)}, bf16[4112,128]{1,0:T(8,128)(2,1)S(1)}, u32[]{:S(2)}, u32[]{:S(2)}) %collective-permute-start.14) | collective-permute-done | bytes 1052704 | tf_op jit(solution)/shard_map/ppermute | solution.py:375
  29.4 0.7 %shard_map.85 = (f32[256,128]{1,0:T(8,128)S(1)}, f32[256,128]{1,0:T(8,128)S(1)}) custom-call(bf16[256,4096]{1,0:T(8,128)(2,1)S(1)} %copy-done, bf16[4112,128]{1,0:T(8,128)(2,1)S(1)} %collective-permute-done.14.refs_1_.refs_0_, s32[8,512]{1,0:T(8,128)S(1)} %shard_map.83.refs_2_.refs_1_.bounds_ref, bf16[64,1280]{1,0:T(8,128)(2,1)S(1)} %get-tuple-element.28.refs_3_, ...), custom_call_target="tpu_custom_call" | custom-call | flops 8589934592 | bytes 16777216 | tf_op jit(solution)/shard_map/pallas_call | solution.py:296
  30.1 0.0 collective-permute-done.11.refs_7_.refs_5_
  30.2 0.0 collective-permute-done.5.refs_4_
  30.2 0.5 %collective-permute-done.13.refs_9_.refs_7_ = bf16[64,1280]{1,0:T(8,128)(2,1)S(1)} collective-permute-done((bf16[64,1280]{1,0:T(8,128)(2,1)S(1)}, bf16[64,1280]{1,0:T(8,128)(2,1)S(1)}, u32[]{:S(2)}, u32[]{:S(2)}) %collective-permute-start.13) | collective-permute-done | bytes 163872 | tf_op jit(solution)/shard_map/ppermute | solution.py:372
  30.6 0.8 %collective-permute-done.6.refs_5_ = bf16[64,1280]{1,0:T(8,128)(2,1)S(1)} collective-permute-done((bf16[64,1280]{1,0:T(8,128)(2,1)S(1)}, bf16[64,1280]{1,0:T(8,128)(2,1)S(1)}, u32[]{:S(2)}, u32[]{:S(2)}) %collective-permute-start.6) | collective-permute-done | bytes 163872 | tf_op jit(solution)/shard_map/ppermute | solution.py:371
  31.4 0.5 %shard_map.87 = f32[128,128]{1,0:T(8,128)S(1)} custom-call(bf16[4112,128]{1,0:T(8,128)(2,1)S(1)} %collective-permute-done.14.refs_1_.refs_0_, s32[8,512]{1,0:T(8,128)S(1)} %shard_map.83.refs_2_.refs_1_.bounds_ref, bf16[64,1280]{1,0:T(8,128)(2,1)S(1)} %collective-permute-done.1.refs_2_, bf16[64,1280]{1,0:T(8,128)(2,1)S(1)} %collective-permute-done.4.refs_3_, ...), custom_call_target="tpu_custom_call" | custom-call | flops 8589934592 | bytes 16777216 | tf_op jit(solution)/shard_map/pallas_call | solution.py:296
  32.0 1.6 %collective-permute-start.16 = (f32[128,128]{1,0:T(8,128)S(1)}, f32[128,128]{1,0:T(8,128)S(1)}, u32[]{:S(2)}, u32[]{:S(2)}) collective-permute-start(f32[128,128]{1,0:T(8,128)S(1)} %shard_map.87), channel_id=1, source_target_pairs={{0,16},{16,0},{1,17},{17,1},{2,18},{18,2},{3,19},{19,3},{4,20},{20... | collective-permute-start | bytes 196616 | tf_op jit(solution)/shard_map/ppermute | solution.py:394
  33.5 0.0 collective-permute-start.17
  33.5 0.6 %collective-permute-start.18 = (f32[256,512]{1,0:T(8,128)S(1)}, f32[256,512]{1,0:T(8,128)S(1)}, u32[]{:S(2)}, u32[]{:S(2)}) collective-permute-start(f32[256,512]{1,0:T(8,128)S(1)} %get-tuple-element.36), channel_id=1, source_target_pairs={{0,1},{1,0},{2,3},{3,2},{4,5},{5,4},{6,7},{7,6},{8,9},{9,8},{10,11... | collective-permute-start | bytes 1572872 | tf_op jit(solution)/shard_map/ppermute | solution.py:388
  34.2 0.5 %shard_map.86.mine = f32[128,128]{1,0:T(8,128)S(1)} custom-call(bf16[256,4096]{1,0:T(8,128)(2,1)S(1)} %copy-done, s32[8,512]{1,0:T(8,128)S(1)} %shard_map.83.refs_2_.refs_1_.bounds_ref, bf16[64,1280]{1,0:T(8,128)(2,1)S(1)} %collective-permute-done.1.refs_2_, bf16[64,1280]{1,0:T(8,128)(2,1)S(1)} %collective-permute-done.4.refs_3_, ...), custom_call_target="tpu_custom_call" | custom-call | flops 8589934592 | bytes 16777216 | tf_op jit(solution)/shard_map/pallas_call | solution.py:296
  34.7 0.1 collective-permute-start.15
  34.8 1.5 %collective-permute-done.16.two = f32[128,128]{1,0:T(8,128)S(1)} collective-permute-done((f32[128,128]{1,0:T(8,128)S(1)}, f32[128,128]{1,0:T(8,128)S(1)}, u32[]{:S(2)}, u32[]{:S(2)}) %collective-permute-start.16) | collective-permute-done | bytes 65568 | tf_op jit(solution)/shard_map/ppermute | solution.py:394
  36.3 1.4 %collective-permute-done.17.three = f32[128,128]{1,0:T(8,128)S(1)} collective-permute-done((f32[128,128]{1,0:T(8,128)S(1)}, f32[128,128]{1,0:T(8,128)S(1)}, u32[]{:S(2)}, u32[]{:S(2)}) %collective-permute-start.17) | collective-permute-done | bytes 65568 | tf_op jit(solution)/shard_map/ppermute | solution.py:395
  37.7 0.0 collective-permute-done.15.one
  37.7 0.0 collective-permute-done.18.far_ref
  37.7 1.1 %shard_map.88 = bf16[256,512]{1,0:T(8,128)(2,1)} custom-call(s32[8,512]{1,0:T(8,128)S(1)} %shard_map.83.refs_2_.refs_1_.bounds_ref, f32[128,128]{1,0:T(8,128)S(1)} %shard_map.86.mine, f32[128,128]{1,0:T(8,128)S(1)} %collective-permute-done.15.one, f32[128,128]{1,0:T(8,128)S(1)} %collective-permute-done.16.two, f32[128,128]{1,0:T(8,128)S(1)} %collective-permute-done.17.three, ...), custom_call_target="tpu_custom_call" | custom-call | tf_op jit(solution)/shard_map/pallas_call | solution.py:399
  (4 shorter events, 0.0 us)
Async XLA Ops:
  1.6 7.2 %collective-permute-start.7 = (bf16[64,1280]{1,0:T(8,128)(2,1)S(1)}, bf16[64,1280]{1,0:T(8,128)(2,1)S(1)}, u32[]{:S(2)}, u32[]{:S(2)}) collective-permute-start(bf16[64,1280]{1,0:T(8,128)(2,1)S(1)} %get-tuple-element.29.refs_7_.refs_0_), channel_id=1, source_target_pairs={{2,0},{6,2},{10,6},{14,10},{12,14},{8,12},{4,8},{0,4},{3,1},{7,3},... | collective-permute-start | bytes 491528 | tf_op jit(solution)/shard_map/ppermute | solution.py:365
  4.7 7.1 %collective-permute-start.2 = (bf16[64,1280]{1,0:T(8,128)(2,1)S(1)}, bf16[64,1280]{1,0:T(8,128)(2,1)S(1)}, u32[]{:S(2)}, u32[]{:S(2)}) collective-permute-start(bf16[64,1280]{1,0:T(8,128)(2,1)S(1)} %get-tuple-element.28.refs_3_), channel_id=1, source_target_pairs={{0,2},{2,6},{6,10},{10,14},{14,12},{12,8},{8,4},{4,0},{1,3},{3,7},... | collective-permute-start | bytes 491528 | tf_op jit(solution)/shard_map/ppermute | solution.py:364
  4.7 24.7 %collective-permute-start.14 = (bf16[4112,128]{1,0:T(8,128)(2,1)S(1)}, bf16[4112,128]{1,0:T(8,128)(2,1)S(1)}, u32[]{:S(2)}, u32[]{:S(2)}) collective-permute-start(bf16[4112,128]{1,0:T(8,128)(2,1)S(1)} %get-tuple-element.30), channel_id=1, source_target_pairs={{0,16},{16,0},{1,17},{17,1},{2,18},{18,2},{3,19},{19,3},{4,20},{20... | collective-permute-start | bytes 3158024 | tf_op jit(solution)/shard_map/ppermute | solution.py:375
  6.7 13.0 %slice-start = ((s8[8388608]{0:T(1024)(128)(4,1)}), s8[4194304]{0:T(1024)(128)(4,1)S(1)}, s32[]{:S(2)}) async-start(s8[8388608]{0:T(1024)(128)(4,1)} %bitcast.4), calls=%async_computation | async-start | bytes 8388608
  6.7 13.0 %slice-start.1 = ((s8[8388608]{0:T(1024)(128)(4,1)}), s8[4194304]{0:T(1024)(128)(4,1)S(1)}, s32[]{:S(2)}) async-start(s8[8388608]{0:T(1024)(128)(4,1)} %bitcast.4), calls=%async_computation.1 | async-start | bytes 8388608
  6.7 13.0 %copy-start = (bf16[256,4096]{1,0:T(8,128)(2,1)S(1)}, bf16[256,4096]{1,0:T(8,128)(2,1)}, u32[]{:S(2)}) copy-start(bf16[256,4096]{1,0:T(8,128)(2,1)} %refs_0_.1) | copy-start | bytes 6291460
  6.7 8.7 %collective-permute-start.9 = (bf16[64,1280]{1,0:T(8,128)(2,1)S(1)}, bf16[64,1280]{1,0:T(8,128)(2,1)S(1)}, u32[]{:S(2)}, u32[]{:S(2)}) collective-permute-start(bf16[64,1280]{1,0:T(8,128)(2,1)S(1)} %get-tuple-element.29.refs_7_.refs_0_), channel_id=1, source_target_pairs={{0,2},{2,6},{6,10},{10,14},{14,12},{12,8},{8,4},{4,0},{1,3},{3,7},... | collective-permute-start | bytes 491528 | tf_op jit(solution)/shard_map/ppermute | solution.py:366
  8.2 7.1 %collective-permute-start = (bf16[64,1280]{1,0:T(8,128)(2,1)S(1)}, bf16[64,1280]{1,0:T(8,128)(2,1)S(1)}, u32[]{:S(2)}, u32[]{:S(2)}) collective-permute-start(bf16[64,1280]{1,0:T(8,128)(2,1)S(1)} %get-tuple-element.28.refs_3_), channel_id=1, source_target_pairs={{2,0},{6,2},{10,6},{14,10},{12,14},{8,12},{4,8},{0,4},{3,1},{7,3},... | collective-permute-start | bytes 491528 | tf_op jit(solution)/shard_map/ppermute | solution.py:367
  8.8 8.9 %collective-permute-start.8 = (bf16[64,1280]{1,0:T(8,128)(2,1)S(1)}, bf16[64,1280]{1,0:T(8,128)(2,1)S(1)}, u32[]{:S(2)}, u32[]{:S(2)}) collective-permute-start(bf16[64,1280]{1,0:T(8,128)(2,1)S(1)} %collective-permute-done.7.refs_9_.refs_2_), channel_id=1, source_target_pairs={{2,0},{6,2},{10,6},{14,10},{12,14},{8,12},{4,8},{0,4},{3,1},{7,3},... | collective-permute-start | bytes 491528 | tf_op jit(solution)/shard_map/ppermute | solution.py:365
  11.8 7.1 %collective-permute-start.3 = (bf16[64,1280]{1,0:T(8,128)(2,1)S(1)}, bf16[64,1280]{1,0:T(8,128)(2,1)S(1)}, u32[]{:S(2)}, u32[]{:S(2)}) collective-permute-start(bf16[64,1280]{1,0:T(8,128)(2,1)S(1)} %collective-permute-done.2.refs_4_), channel_id=1, source_target_pairs={{0,2},{2,6},{6,10},{10,14},{14,12},{12,8},{8,4},{4,0},{1,3},{3,7},... | collective-permute-start | bytes 491528 | tf_op jit(solution)/shard_map/ppermute | solution.py:364
  15.3 7.1 %collective-permute-start.10 = (bf16[64,1280]{1,0:T(8,128)(2,1)S(1)}, bf16[64,1280]{1,0:T(8,128)(2,1)S(1)}, u32[]{:S(2)}, u32[]{:S(2)}) collective-permute-start(bf16[64,1280]{1,0:T(8,128)(2,1)S(1)} %collective-permute-done.9.refs_8_.refs_1_), channel_id=1, source_target_pairs={{0,2},{2,6},{6,10},{10,14},{14,12},{12,8},{8,4},{4,0},{1,3},{3,7},... | collective-permute-start | bytes 491528 | tf_op jit(solution)/shard_map/ppermute | solution.py:366
  15.3 8.2 %collective-permute-start.1 = (bf16[64,1280]{1,0:T(8,128)(2,1)S(1)}, bf16[64,1280]{1,0:T(8,128)(2,1)S(1)}, u32[]{:S(2)}, u32[]{:S(2)}) collective-permute-start(bf16[64,1280]{1,0:T(8,128)(2,1)S(1)} %collective-permute-done.refs_5_), channel_id=1, source_target_pairs={{2,0},{6,2},{10,6},{14,10},{12,14},{8,12},{4,8},{0,4},{3,1},{7,3},... | collective-permute-start | bytes 491528 | tf_op jit(solution)/shard_map/ppermute | solution.py:367
  17.6 6.8 %collective-permute-start.12 = (bf16[64,1280]{1,0:T(8,128)(2,1)S(1)}, bf16[64,1280]{1,0:T(8,128)(2,1)S(1)}, u32[]{:S(2)}, u32[]{:S(2)}) collective-permute-start(bf16[64,1280]{1,0:T(8,128)(2,1)S(1)} %collective-permute-done.8.refs_6_.refs_4_), channel_id=1, source_target_pairs={{2,0},{6,2},{10,6},{14,10},{12,14},{8,12},{4,8},{0,4},{3,1},{7,3},... | collective-permute-start | bytes 491528 | tf_op jit(solution)/shard_map/ppermute | solution.py:365
  18.9 7.1 %collective-permute-start.4 = (bf16[64,1280]{1,0:T(8,128)(2,1)S(1)}, bf16[64,1280]{1,0:T(8,128)(2,1)S(1)}, u32[]{:S(2)}, u32[]{:S(2)}) collective-permute-start(bf16[64,1280]{1,0:T(8,128)(2,1)S(1)} %collective-permute-done.3.refs_6_), channel_id=1, source_target_pairs={{0,2},{2,6},{6,10},{10,14},{14,12},{12,8},{8,4},{4,0},{1,3},{3,7},... | collective-permute-start | bytes 491528 | tf_op jit(solution)/shard_map/ppermute | solution.py:364
  22.5 7.7 %collective-permute-start.11 = (bf16[64,1280]{1,0:T(8,128)(2,1)S(1)}, bf16[64,1280]{1,0:T(8,128)(2,1)S(1)}, u32[]{:S(2)}, u32[]{:S(2)}) collective-permute-start(bf16[64,1280]{1,0:T(8,128)(2,1)S(1)} %collective-permute-done.10.refs_10_.refs_3_), channel_id=1, source_target_pairs={{0,2},{2,6},{6,10},{10,14},{14,12},{12,8},{8,4},{4,0},{1,3},{3,7},... | collective-permute-start | bytes 491528 | tf_op jit(solution)/shard_map/ppermute | solution.py:366
  23.5 6.6 %collective-permute-start.5 = (bf16[64,1280]{1,0:T(8,128)(2,1)S(1)}, bf16[64,1280]{1,0:T(8,128)(2,1)S(1)}, u32[]{:S(2)}, u32[]{:S(2)}) collective-permute-start(bf16[64,1280]{1,0:T(8,128)(2,1)S(1)} %collective-permute-done.1.refs_2_), channel_id=1, source_target_pairs={{2,0},{6,2},{10,6},{14,10},{12,14},{8,12},{4,8},{0,4},{3,1},{7,3},... | collective-permute-start | bytes 491528 | tf_op jit(solution)/shard_map/ppermute | solution.py:367
  24.5 6.1 %collective-permute-start.13 = (bf16[64,1280]{1,0:T(8,128)(2,1)S(1)}, bf16[64,1280]{1,0:T(8,128)(2,1)S(1)}, u32[]{:S(2)}, u32[]{:S(2)}) collective-permute-start(bf16[64,1280]{1,0:T(8,128)(2,1)S(1)} %collective-permute-done.12.refs_8_.refs_6_), channel_id=1, source_target_pairs={{2,0},{6,2},{10,6},{14,10},{12,14},{8,12},{4,8},{0,4},{3,1},{7,3},... | collective-permute-start | bytes 491528 | tf_op jit(solution)/shard_map/ppermute | solution.py:372
  26.1 5.3 %collective-permute-start.6 = (bf16[64,1280]{1,0:T(8,128)(2,1)S(1)}, bf16[64,1280]{1,0:T(8,128)(2,1)S(1)}, u32[]{:S(2)}, u32[]{:S(2)}) collective-permute-start(bf16[64,1280]{1,0:T(8,128)(2,1)S(1)} %collective-permute-done.4.refs_3_), channel_id=1, source_target_pairs={{0,2},{2,6},{6,10},{10,14},{14,12},{12,8},{8,4},{4,0},{1,3},{3,7},... | collective-permute-start | bytes 491528 | tf_op jit(solution)/shard_map/ppermute | solution.py:371
  32.0 4.3 %collective-permute-start.16 = (f32[128,128]{1,0:T(8,128)S(1)}, f32[128,128]{1,0:T(8,128)S(1)}, u32[]{:S(2)}, u32[]{:S(2)}) collective-permute-start(f32[128,128]{1,0:T(8,128)S(1)} %shard_map.87), channel_id=1, source_target_pairs={{0,16},{16,0},{1,17},{17,1},{2,18},{18,2},{3,19},{19,3},{4,20},{20... | collective-permute-start | bytes 196616 | tf_op jit(solution)/shard_map/ppermute | solution.py:394
  33.5 4.2 %collective-permute-start.17 = (f32[128,128]{1,0:T(8,128)S(1)}, f32[128,128]{1,0:T(8,128)S(1)}, u32[]{:S(2)}, u32[]{:S(2)}) collective-permute-start(f32[128,128]{1,0:T(8,128)S(1)} %shard_map.87), channel_id=1, source_target_pairs={{0,17},{1,16},{16,1},{17,0},{2,19},{3,18},{18,3},{19,2},{4,21},{5,... | collective-permute-start | bytes 196616 | tf_op jit(solution)/shard_map/ppermute | solution.py:395
  33.5 4.2 %collective-permute-start.18 = (f32[256,512]{1,0:T(8,128)S(1)}, f32[256,512]{1,0:T(8,128)S(1)}, u32[]{:S(2)}, u32[]{:S(2)}) collective-permute-start(f32[256,512]{1,0:T(8,128)S(1)} %get-tuple-element.36), channel_id=1, source_target_pairs={{0,1},{1,0},{2,3},{3,2},{4,5},{5,4},{6,7},{7,6},{8,9},{9,8},{10,11... | collective-permute-start | bytes 1572872 | tf_op jit(solution)/shard_map/ppermute | solution.py:388
  34.7 3.0 %collective-permute-start.15 = (f32[128,128]{1,0:T(8,128)S(1)}, f32[128,128]{1,0:T(8,128)S(1)}, u32[]{:S(2)}, u32[]{:S(2)}) collective-permute-start(f32[128,128]{1,0:T(8,128)S(1)} %shard_map.86.mine), channel_id=1, source_target_pairs={{0,1},{1,0},{2,3},{3,2},{4,5},{5,4},{6,7},{7,6},{8,9},{9,8},{10,11... | collective-permute-start | bytes 196616 | tf_op jit(solution)/shard_map/ppermute | solution.py:396

commit v16 on v15

--- a/solution.py
+++ b/solution.py
@@ -247,7 +247,7 @@
     rows_refs, refs = refs[: len(sides)], refs[len(sides) :]
     bounds_ref, pieces = refs[0], refs[1:]
     pieces, rest = pieces[: 2 * GROUP * len(groups)], pieces[2 * GROUP * len(groups) :]
-    starts, outs = rest[: -len(sides)], rest[-len(sides) :]
+    starts, outs = (rest[: len(sides)], rest[len(sides) :]) if last else ((), rest)
     cut = pieces[0].shape[1]
     rank = pieces[0].shape[0]
     size = GROUP * rank
@@ -279,35 +279,44 @@
             here = part[s * count : (s + 1) * count]
             kept = fold(jnp.where(group_mask(*ends, here.shape), here, 0.0))
             totals[s] = kept if totals[s] is None else totals[s] + kept
+    if last:
+        (total,) = totals
+        total = total + pltpu.roll(total, rank, 1)
+        half = count // 2
+        lane = lax.broadcasted_iota(I32, (half, 2 * rank), 1)
+        total = jnp.where(lane < rank, total[:half], total[half:])
+        size = outs[0].shape[0]
+        totals = [total[i * size : (i + 1) * size] for i in range(len(outs))]
     for total, out_ref in zip(totals, outs):
-        if last:
-            total = total + pltpu.roll(total, rank, 1)
-            half = count // 2
-            lane = lax.broadcasted_iota(I32, (half, 2 * rank), 1)
-            total = jnp.where(lane < rank, total[:half], total[half:])
-        out_ref[...] = total
+        out_ref[...] = total.astype(out_ref.dtype)
 
 
 def rank_call(sides, groups, depth, count, rows, bounds, pieces, starts):
     rank = pieces[0].shape[0]
     last = len(starts) > 0
-    shape = (count // 2, 2 * rank) if last else (count, 2 * rank)
+    if not last:
+        out = (jax.ShapeDtypeStruct((count, 2 * rank), F32),) * len(sides)
+    elif sides == (1,):
+        out = (jax.ShapeDtypeStruct((count // 2, 2 * rank), BF16),)
+    else:
+        out = (jax.ShapeDtypeStruct((count // 4, 2 * rank), F32),) * 2
     operands = [*rows, bounds, *pieces, *starts]
     return pl.pallas_call(
         functools.partial(rank_kernel, sides, groups, depth, last),
-        out_shape=(jax.ShapeDtypeStruct(shape, F32),) * len(sides),
+        out_shape=out,
         in_specs=[VMEM] * len(operands),
-        out_specs=(VMEM,) * len(sides),
+        out_specs=(VMEM,) * len(out),
         compiler_params=params(),
-        cost_estimate=LONG,
+        cost_estimate=HALF if last and sides == (0,) else LONG,
     )(*operands)
 
 
-def final_kernel(bounds_ref, mine, one, two, three, near_ref, far_ref, *refs):
+def final_kernel(bounds_ref, top, low, one_top, one_low, two, three, near_ref, far_ref, *refs):
     factors, out_ref = refs[:-1], refs[-1]
     rank, width = factors[0].shape[0], out_ref.shape[1]
     begin = factors[0].shape[1] - width
-    packed = (mine[...] + one[...]) + (two[...] + three[...])
+    here = jnp.concatenate([top[...] + one_top[...], low[...] + one_low[...]], axis=0)
+    packed = here + (two[...].astype(F32) + three[...].astype(F32))
     turned = pltpu.roll(packed, rank, 1)
     lane = lax.broadcasted_iota(I32, packed.shape, 1)
     values = jnp.concatenate(
@@ -389,13 +398,13 @@
     pieces = firsts[-GROUP:] + seconds[-GROUP:]
     late = (count - 1,)
     (theirs,) = rank_call((1,), late, depth, rows, (other,), bounds, pieces, (start_theirs,))
-    (mine,) = rank_call((0,), late, depth, rows, (hidden,), bounds, pieces, (start_mine,))
+    mine = rank_call((0,), late, depth, rows, (hidden,), bounds, pieces, (start_mine,))
 
     two = lax.ppermute(theirs, "groups", swap)
     three = lax.ppermute(theirs, ("groups", "tensor"), [(0, 3), (1, 2), (2, 1), (3, 0)])
-    one = lax.ppermute(mine, "tensor", swap)
-
-    operands = [bounds, mine, one, two, three, near, far, *seconds]
+    one = [lax.ppermute(part, "tensor", swap) for part in mine]
+
+    operands = [bounds, *mine, *one, two, three, near, far, *seconds]
     return pl.pallas_call(
         final_kernel,
         out_shape=jax.ShapeDtypeStruct((rows, width), BF16),

time: 39 us -> 38.2 us (0.979)
  waiting for transfers between devices: 11.8 us -> 10.8 us
    ppermute x1 -> x2, starting transfers between devices: 0.07 us -> 0.77 us  [per_device(): one = [lax.ppermute(part, 'tensor', swap) for part in mine]]
    ppermute x1, starting transfers between devices: 0.62 us -> 0.07 us  [per_device(): far = lax.ppermute(far, 'tensor', swap)]
    ppermute x1, waiting for transfers between devices: 1.4 us -> 0.94 us  [per_device(): lax.ppermute(theirs, ('groups', 'tensor'), [(0, 3), (1, 2), (2, 1), (3, 0)])]
    ppermute x1, waiting for transfers between devices: 1.49 us -> 1.07 us  [per_device(): two = lax.ppermute(theirs, 'groups', swap)]
  transfers between devices with their start and end apart: 19 -> 20, of which waited for: 10 -> 10; matrix products, arithmetic and copies ran while one was open for 0% -> 0% of each run, Pallas kernels for 9% -> 11%
where the time goes in v16:
time: 38.2 us; the launch traced here: 38 us
  starting transfers between devices  20.2 us (53%)
  waiting for transfers between devices  10.8 us (28%)
  Pallas kernels  6.91 us (18%)
    ppermute x3, starting transfers between devices, per_device(): d = lax.ppermute(behind[1], 'batch', backward)  6.68 us
    ppermute x3, waiting for transfers between devices, per_device(): b = lax.ppermute(ahead[1], 'batch', forward)  3.91 us
    ppermute x3, starting transfers between devices, per_device(): c = lax.ppermute(behind[0], 'batch', backward)  3.48 us
    ppermute x3, starting transfers between devices, per_device(): b = lax.ppermute(ahead[1], 'batch', forward)  2.65 us
    ppermute x1, waiting for transfers between devices, per_device(): other = lax.ppermute(to_other, 'groups', swap)  2.64 us
    pallas_call x1, Pallas kernels, base_call(): pl.pallas_call(base_kernel, out_shape=(out, out), in_specs=[VMEM] * 2, ou...  2.35 us
    ppermute x1, starting transfers between devices, per_device(): other = lax.ppermute(to_other, 'groups', swap)  1.97 us
    pallas_call x3, Pallas kernels, rank_call(): pl.pallas_call(functools.partial(rank_kernel, sides, groups, depth, last)...  1.84 us
  transfers between devices with their start and end apart: 20, of which 10 were waited for; matrix products, arithmetic and copies ran while one was open for 0% of the time, Pallas kernels for 11%

profile of v16, /device:TPU:0, one launch (start us, length us, event | category | flops | bytes accessed | tf_op | source)
XLA Modules:
  0.0 38.0 jit_solution(11663117851327618239)
XLA Ops:
  0.0 1.6 %shard_map.82 = (bf16[4112,128]{1,0:T(8,128)(2,1)S(1)}, bf16[64,1280]{1,0:T(8,128)(2,1)S(1)}, bf16[64,1280]{1,0:T(8,128)(2,1)S(1)}, s32[8,512]{1,0:T(8,128)S(1)}) custom-call(bf16[256,4096]{1,0:T(8,128)(2,1)} %refs_0_.1, bf16[64,4096]{1,0:T(8,128)(2,1)} %bitcast.6, bf16[64,512]{1,0:T(8,128)(2,1)} %bitcast.7, s32[1,4]{1,0:T(1,128)} %demand_ref.1, ...), custom_call_target="tpu_custom_call" | custom-call | tf_op jit(solution)/shard_map/pallas_call | solution.py:161
  1.6 3.1 %collective-permute-start.7 = (bf16[64,1280]{1,0:T(8,128)(2,1)S(1)}, bf16[64,1280]{1,0:T(8,128)(2,1)S(1)}, u32[]{:S(2)}, u32[]{:S(2)}) collective-permute-start(bf16[64,1280]{1,0:T(8,128)(2,1)S(1)} %get-tuple-element.31.refs_7_.refs_0_), channel_id=1, source_target_pairs={{2,0},{6,2},{10,6},{14,10},{12,14},{8,12},{4,8},{0,4},{3,1},{7,3},... | collective-permute-start | bytes 491528 | tf_op jit(solution)/shard_map/ppermute | solution.py:374
  4.7 0.0 collective-permute-start.2
  4.7 2.0 %collective-permute-start.14 = (bf16[4112,128]{1,0:T(8,128)(2,1)S(1)}, bf16[4112,128]{1,0:T(8,128)(2,1)S(1)}, u32[]{:S(2)}, u32[]{:S(2)}) collective-permute-start(bf16[4112,128]{1,0:T(8,128)(2,1)S(1)} %get-tuple-element.32), channel_id=1, source_target_pairs={{0,16},{16,0},{1,17},{17,1},{2,18},{18,2},{3,19},{19,3},{4,20},{20... | collective-permute-start | bytes 3158024 | tf_op jit(solution)/shard_map/ppermute | solution.py:384
  6.7 1.5 %collective-permute-start.9 = (bf16[64,1280]{1,0:T(8,128)(2,1)S(1)}, bf16[64,1280]{1,0:T(8,128)(2,1)S(1)}, u32[]{:S(2)}, u32[]{:S(2)}) collective-permute-start(bf16[64,1280]{1,0:T(8,128)(2,1)S(1)} %get-tuple-element.31.refs_7_.refs_0_), channel_id=1, source_target_pairs={{0,2},{2,6},{6,10},{10,14},{14,12},{12,8},{8,4},{4,0},{1,3},{3,7},... | collective-permute-start | bytes 491528 | tf_op jit(solution)/shard_map/ppermute | solution.py:375
  8.2 0.5 %collective-permute-start = (bf16[64,1280]{1,0:T(8,128)(2,1)S(1)}, bf16[64,1280]{1,0:T(8,128)(2,1)S(1)}, u32[]{:S(2)}, u32[]{:S(2)}) collective-permute-start(bf16[64,1280]{1,0:T(8,128)(2,1)S(1)} %get-tuple-element.30.refs_3_), channel_id=1, source_target_pairs={{2,0},{6,2},{10,6},{14,10},{12,14},{8,12},{4,8},{0,4},{3,1},{7,3},... | collective-permute-start | bytes 491528 | tf_op jit(solution)/shard_map/ppermute | solution.py:376
  8.7 0.1 collective-permute-done.7.refs_9_.refs_2_
  8.8 2.3 %collective-permute-start.8 = (bf16[64,1280]{1,0:T(8,128)(2,1)S(1)}, bf16[64,1280]{1,0:T(8,128)(2,1)S(1)}, u32[]{:S(2)}, u32[]{:S(2)}) collective-permute-start(bf16[64,1280]{1,0:T(8,128)(2,1)S(1)} %collective-permute-done.7.refs_9_.refs_2_), channel_id=1, source_target_pairs={{2,0},{6,2},{10,6},{14,10},{12,14},{8,12},{4,8},{0,4},{3,1},{7,3},... | collective-permute-start | bytes 491528 | tf_op jit(solution)/shard_map/ppermute | solution.py:374
  11.1 0.7 %collective-permute-done.2.refs_4_ = bf16[64,1280]{1,0:T(8,128)(2,1)S(1)} collective-permute-done((bf16[64,1280]{1,0:T(8,128)(2,1)S(1)}, bf16[64,1280]{1,0:T(8,128)(2,1)S(1)}, u32[]{:S(2)}, u32[]{:S(2)}) %collective-permute-start.2) | collective-permute-done | bytes 163872 | tf_op jit(solution)/shard_map/ppermute | solution.py:373
  11.8 0.0 collective-permute-start.3
  11.8 3.5 %collective-permute-done.9.refs_8_.refs_1_ = bf16[64,1280]{1,0:T(8,128)(2,1)S(1)} collective-permute-done((bf16[64,1280]{1,0:T(8,128)(2,1)S(1)}, bf16[64,1280]{1,0:T(8,128)(2,1)S(1)}, u32[]{:S(2)}, u32[]{:S(2)}) %collective-permute-start.9) | collective-permute-done | bytes 163872 | tf_op jit(solution)/shard_map/ppermute | solution.py:375
  15.3 0.0 collective-permute-start.10
  15.3 0.0 collective-permute-done.refs_5_
  15.3 2.0 %collective-permute-start.1 = (bf16[64,1280]{1,0:T(8,128)(2,1)S(1)}, bf16[64,1280]{1,0:T(8,128)(2,1)S(1)}, u32[]{:S(2)}, u32[]{:S(2)}) collective-permute-start(bf16[64,1280]{1,0:T(8,128)(2,1)S(1)} %collective-permute-done.refs_5_), channel_id=1, source_target_pairs={{2,0},{6,2},{10,6},{14,10},{12,14},{8,12},{4,8},{0,4},{3,1},{7,3},... | collective-permute-start | bytes 491528 | tf_op jit(solution)/shard_map/ppermute | solution.py:376
  17.3 0.3 collective-permute-done.8.refs_6_.refs_4_
  17.6 1.3 %collective-permute-start.12 = (bf16[64,1280]{1,0:T(8,128)(2,1)S(1)}, bf16[64,1280]{1,0:T(8,128)(2,1)S(1)}, u32[]{:S(2)}, u32[]{:S(2)}) collective-permute-start(bf16[64,1280]{1,0:T(8,128)(2,1)S(1)} %collective-permute-done.8.refs_6_.refs_4_), channel_id=1, source_target_pairs={{2,0},{6,2},{10,6},{14,10},{12,14},{8,12},{4,8},{0,4},{3,1},{7,3},... | collective-permute-start | bytes 491528 | tf_op jit(solution)/shard_map/ppermute | solution.py:374
  18.9 0.0 collective-permute-done.3.refs_6_
  18.9 0.7 %collective-permute-start.4 = (bf16[64,1280]{1,0:T(8,128)(2,1)S(1)}, bf16[64,1280]{1,0:T(8,128)(2,1)S(1)}, u32[]{:S(2)}, u32[]{:S(2)}) collective-permute-start(bf16[64,1280]{1,0:T(8,128)(2,1)S(1)} %collective-permute-done.3.refs_6_), channel_id=1, source_target_pairs={{0,2},{2,6},{6,10},{10,14},{14,12},{12,8},{8,4},{4,0},{1,3},{3,7},... | collective-permute-start | bytes 491528 | tf_op jit(solution)/shard_map/ppermute | solution.py:373
  19.7 0.0 slice-done
  19.7 0.0 copy-done
  19.7 2.4 %shard_map.84 = (f32[256,512]{1,0:T(8,128)S(1)}, f32[256,512]{1,0:T(8,128)S(1)}) custom-call(bf16[256,4096]{1,0:T(8,128)(2,1)S(1)} %copy-done, bf16[4096,1024]{1,0:T(8,128)(2,1)S(1)} %bitcast.5), custom_call_target="tpu_custom_call" | custom-call | bytes 4194304 | tf_op jit(solution)/shard_map/pallas_call | solution.py:210
  22.1 0.4 %collective-permute-done.10.refs_10_.refs_3_ = bf16[64,1280]{1,0:T(8,128)(2,1)S(1)} collective-permute-done((bf16[64,1280]{1,0:T(8,128)(2,1)S(1)}, bf16[64,1280]{1,0:T(8,128)(2,1)S(1)}, u32[]{:S(2)}, u32[]{:S(2)}) %collective-permute-start.10) | collective-permute-done | bytes 163872 | tf_op jit(solution)/shard_map/ppermute | solution.py:375
  22.5 1.1 %collective-permute-start.11 = (bf16[64,1280]{1,0:T(8,128)(2,1)S(1)}, bf16[64,1280]{1,0:T(8,128)(2,1)S(1)}, u32[]{:S(2)}, u32[]{:S(2)}) collective-permute-start(bf16[64,1280]{1,0:T(8,128)(2,1)S(1)} %collective-permute-done.10.refs_10_.refs_3_), channel_id=1, source_target_pairs={{0,2},{2,6},{6,10},{10,14},{14,12},{12,8},{8,4},{4,0},{1,3},{3,7},... | collective-permute-start | bytes 491528 | tf_op jit(solution)/shard_map/ppermute | solution.py:375
  23.5 0.0 collective-permute-done.1.refs_2_
  23.5 0.9 %collective-permute-start.5 = (bf16[64,1280]{1,0:T(8,128)(2,1)S(1)}, bf16[64,1280]{1,0:T(8,128)(2,1)S(1)}, u32[]{:S(2)}, u32[]{:S(2)}) collective-permute-start(bf16[64,1280]{1,0:T(8,128)(2,1)S(1)} %collective-permute-done.1.refs_2_), channel_id=1, source_target_pairs={{2,0},{6,2},{10,6},{14,10},{12,14},{8,12},{4,8},{0,4},{3,1},{7,3},... | collective-permute-start | bytes 491528 | tf_op jit(solution)/shard_map/ppermute | solution.py:376
  24.5 0.0 collective-permute-done.12.refs_8_.refs_6_
  24.5 1.6 %collective-permute-start.13 = (bf16[64,1280]{1,0:T(8,128)(2,1)S(1)}, bf16[64,1280]{1,0:T(8,128)(2,1)S(1)}, u32[]{:S(2)}, u32[]{:S(2)}) collective-permute-start(bf16[64,1280]{1,0:T(8,128)(2,1)S(1)} %collective-permute-done.12.refs_8_.refs_6_), channel_id=1, source_target_pairs={{2,0},{6,2},{10,6},{14,10},{12,14},{8,12},{4,8},{0,4},{3,1},{7,3},... | collective-permute-start | bytes 491528 | tf_op jit(solution)/shard_map/ppermute | solution.py:381
  26.1 0.0 collective-permute-done.4.refs_3_
  26.1 0.7 %collective-permute-start.6 = (bf16[64,1280]{1,0:T(8,128)(2,1)S(1)}, bf16[64,1280]{1,0:T(8,128)(2,1)S(1)}, u32[]{:S(2)}, u32[]{:S(2)}) collective-permute-start(bf16[64,1280]{1,0:T(8,128)(2,1)S(1)} %collective-permute-done.4.refs_3_), channel_id=1, source_target_pairs={{0,2},{2,6},{6,10},{10,14},{14,12},{12,8},{8,4},{4,0},{1,3},{3,7},... | collective-permute-start | bytes 491528 | tf_op jit(solution)/shard_map/ppermute | solution.py:380
  26.8 2.6 %collective-permute-done.14.refs_1_.refs_0_ = bf16[4112,128]{1,0:T(8,128)(2,1)S(1)} collective-permute-done((bf16[4112,128]{1,0:T(8,128)(2,1)S(1)}, bf16[4112,128]{1,0:T(8,128)(2,1)S(1)}, u32[]{:S(2)}, u32[]{:S(2)}) %collective-permute-start.14) | collective-permute-done | bytes 1052704 | tf_op jit(solution)/shard_map/ppermute | solution.py:384
  29.4 0.7 %shard_map.85 = (f32[256,128]{1,0:T(8,128)S(1)}, f32[256,128]{1,0:T(8,128)S(1)}) custom-call(bf16[256,4096]{1,0:T(8,128)(2,1)S(1)} %copy-done, bf16[4112,128]{1,0:T(8,128)(2,1)S(1)} %collective-permute-done.14.refs_1_.refs_0_, s32[8,512]{1,0:T(8,128)S(1)} %shard_map.83.refs_2_.refs_1_.bounds_ref, bf16[64,1280]{1,0:T(8,128)(2,1)S(1)} %get-tuple-element.30.refs_3_, ...), custom_call_target="tpu_custom_call" | custom-call | flops 8589934592 | bytes 16777216 | tf_op jit(solution)/shard_map/pallas_call | solution.py:304
  30.1 0.1 collective-permute-start.19
  30.2 0.0 collective-permute-done.11.refs_7_.refs_5_
  30.2 0.0 collective-permute-done.5.refs_4_
  30.2 0.4 collective-permute-done.13.refs_9_.refs_7_
  30.6 0.8 %collective-permute-done.6.refs_5_ = bf16[64,1280]{1,0:T(8,128)(2,1)S(1)} collective-permute-done((bf16[64,1280]{1,0:T(8,128)(2,1)S(1)}, bf16[64,1280]{1,0:T(8,128)(2,1)S(1)}, u32[]{:S(2)}, u32[]{:S(2)}) %collective-permute-start.6) | collective-permute-done | bytes 163872 | tf_op jit(solution)/shard_map/ppermute | solution.py:380
  31.4 0.5 %shard_map.87 = bf16[128,128]{1,0:T(8,128)(2,1)S(1)} custom-call(bf16[4112,128]{1,0:T(8,128)(2,1)S(1)} %collective-permute-done.14.refs_1_.refs_0_, s32[8,512]{1,0:T(8,128)S(1)} %shard_map.83.refs_2_.refs_1_.bounds_ref, bf16[64,1280]{1,0:T(8,128)(2,1)S(1)} %collective-permute-done.1.refs_2_, bf16[64,1280]{1,0:T(8,128)(2,1)S(1)} %collective-permute-done.4.refs_3_, ...), custom_call_target="tpu_custom_call" | custom-call | flops 8589934592 | bytes 16777216 | tf_op jit(solution)/shard_map/pallas_call | solution.py:304
  32.0 1.6 %collective-permute-start.17 = (bf16[128,128]{1,0:T(8,128)(2,1)S(1)}, bf16[128,128]{1,0:T(8,128)(2,1)S(1)}, u32[]{:S(2)}, u32[]{:S(2)}) collective-permute-start(bf16[128,128]{1,0:T(8,128)(2,1)S(1)} %shard_map.87), channel_id=1, source_target_pairs={{0,16},{16,0},{1,17},{17,1},{2,18},{18,2},{3,19},{19,3},{4,20},{20... | collective-permute-start | bytes 98312 | tf_op jit(solution)/shard_map/ppermute | solution.py:403
  33.5 0.0 collective-permute-start.18
  33.5 0.5 %shard_map.86 = (f32[64,128]{1,0:T(8,128)S(1)}, f32[64,128]{1,0:T(8,128)S(1)}) custom-call(bf16[256,4096]{1,0:T(8,128)(2,1)S(1)} %copy-done, s32[8,512]{1,0:T(8,128)S(1)} %shard_map.83.refs_2_.refs_1_.bounds_ref, bf16[64,1280]{1,0:T(8,128)(2,1)S(1)} %collective-permute-done.1.refs_2_, bf16[64,1280]{1,0:T(8,128)(2,1)S(1)} %collective-permute-done.4.refs_3_, ...), custom_call_target="tpu_custom_call" | custom-call | bytes 4194304 | tf_op jit(solution)/shard_map/pallas_call | solution.py:304
  34.1 0.7 %collective-permute-start.15 = (f32[64,128]{1,0:T(8,128)S(1)}, f32[64,128]{1,0:T(8,128)S(1)}, u32[]{:S(2)}, u32[]{:S(2)}) collective-permute-start(f32[64,128]{1,0:T(8,128)S(1)} %get-tuple-element.34.top), channel_id=1, source_target_pairs={{0,1},{1,0},{2,3},{3,2},{4,5},{5,4},{6,7},{7,6},{8,9},{9,8},{10,11... | collective-permute-start | bytes 98312 | tf_op jit(solution)/shard_map/ppermute | solution.py:405
  34.8 0.1 collective-permute-start.16
  34.9 1.1 %collective-permute-done.17.two = bf16[128,128]{1,0:T(8,128)(2,1)S(1)} collective-permute-done((bf16[128,128]{1,0:T(8,128)(2,1)S(1)}, bf16[128,128]{1,0:T(8,128)(2,1)S(1)}, u32[]{:S(2)}, u32[]{:S(2)}) %collective-permute-start.17) | collective-permute-done | bytes 32800 | tf_op jit(solution)/shard_map/ppermute | solution.py:403
  35.9 0.9 %collective-permute-done.18.three = bf16[128,128]{1,0:T(8,128)(2,1)S(1)} collective-permute-done((bf16[128,128]{1,0:T(8,128)(2,1)S(1)}, bf16[128,128]{1,0:T(8,128)(2,1)S(1)}, u32[]{:S(2)}, u32[]{:S(2)}) %collective-permute-start.18) | collective-permute-done | bytes 32800 | tf_op jit(solution)/shard_map/ppermute | solution.py:404
  36.9 0.0 collective-permute-done.15.one_top
  36.9 0.0 collective-permute-done.16.one_low
  36.9 0.0 collective-permute-done.19.far_ref
  36.9 1.1 %shard_map.88 = bf16[256,512]{1,0:T(8,128)(2,1)} custom-call(s32[8,512]{1,0:T(8,128)S(1)} %shard_map.83.refs_2_.refs_1_.bounds_ref, f32[64,128]{1,0:T(8,128)S(1)} %get-tuple-element.34.top, f32[64,128]{1,0:T(8,128)S(1)} %get-tuple-element.35.low, f32[64,128]{1,0:T(8,128)S(1)} %collective-permute-done.15.one_top, ...), custom_call_target="tpu_custom_call" | custom-call | tf_op jit(solution)/shard_map/pallas_call | solution.py:408
  (6 shorter events, 0.0 us)
Async XLA Ops:
  1.6 7.2 %collective-permute-start.7 = (bf16[64,1280]{1,0:T(8,128)(2,1)S(1)}, bf16[64,1280]{1,0:T(8,128)(2,1)S(1)}, u32[]{:S(2)}, u32[]{:S(2)}) collective-permute-start(bf16[64,1280]{1,0:T(8,128)(2,1)S(1)} %get-tuple-element.31.refs_7_.refs_0_), channel_id=1, source_target_pairs={{2,0},{6,2},{10,6},{14,10},{12,14},{8,12},{4,8},{0,4},{3,1},{7,3},... | collective-permute-start | bytes 491528 | tf_op jit(solution)/shard_map/ppermute | solution.py:374
  4.7 7.1 %collective-permute-start.2 = (bf16[64,1280]{1,0:T(8,128)(2,1)S(1)}, bf16[64,1280]{1,0:T(8,128)(2,1)S(1)}, u32[]{:S(2)}, u32[]{:S(2)}) collective-permute-start(bf16[64,1280]{1,0:T(8,128)(2,1)S(1)} %get-tuple-element.30.refs_3_), channel_id=1, source_target_pairs={{0,2},{2,6},{6,10},{10,14},{14,12},{12,8},{8,4},{4,0},{1,3},{3,7},... | collective-permute-start | bytes 491528 | tf_op jit(solution)/shard_map/ppermute | solution.py:373
  4.7 24.7 %collective-permute-start.14 = (bf16[4112,128]{1,0:T(8,128)(2,1)S(1)}, bf16[4112,128]{1,0:T(8,128)(2,1)S(1)}, u32[]{:S(2)}, u32[]{:S(2)}) collective-permute-start(bf16[4112,128]{1,0:T(8,128)(2,1)S(1)} %get-tuple-element.32), channel_id=1, source_target_pairs={{0,16},{16,0},{1,17},{17,1},{2,18},{18,2},{3,19},{19,3},{4,20},{20... | collective-permute-start | bytes 3158024 | tf_op jit(solution)/shard_map/ppermute | solution.py:384
  6.7 13.0 %slice-start = ((s8[8388608]{0:T(1024)(128)(4,1)}), s8[4194304]{0:T(1024)(128)(4,1)S(1)}, s32[]{:S(2)}) async-start(s8[8388608]{0:T(1024)(128)(4,1)} %bitcast.4), calls=%async_computation | async-start | bytes 8388608
  6.7 13.0 %copy-start = (bf16[256,4096]{1,0:T(8,128)(2,1)S(1)}, bf16[256,4096]{1,0:T(8,128)(2,1)}, u32[]{:S(2)}) copy-start(bf16[256,4096]{1,0:T(8,128)(2,1)} %refs_0_.1) | copy-start | bytes 6291460
  6.7 13.0 %slice-start.1 = ((s8[8388608]{0:T(1024)(128)(4,1)}), s8[4194304]{0:T(1024)(128)(4,1)S(1)}, s32[]{:S(2)}) async-start(s8[8388608]{0:T(1024)(128)(4,1)} %bitcast.4), calls=%async_computation.1 | async-start | bytes 8388608
  6.7 8.7 %collective-permute-start.9 = (bf16[64,1280]{1,0:T(8,128)(2,1)S(1)}, bf16[64,1280]{1,0:T(8,128)(2,1)S(1)}, u32[]{:S(2)}, u32[]{:S(2)}) collective-permute-start(bf16[64,1280]{1,0:T(8,128)(2,1)S(1)} %get-tuple-element.31.refs_7_.refs_0_), channel_id=1, source_target_pairs={{0,2},{2,6},{6,10},{10,14},{14,12},{12,8},{8,4},{4,0},{1,3},{3,7},... | collective-permute-start | bytes 491528 | tf_op jit(solution)/shard_map/ppermute | solution.py:375
  8.2 7.1 %collective-permute-start = (bf16[64,1280]{1,0:T(8,128)(2,1)S(1)}, bf16[64,1280]{1,0:T(8,128)(2,1)S(1)}, u32[]{:S(2)}, u32[]{:S(2)}) collective-permute-start(bf16[64,1280]{1,0:T(8,128)(2,1)S(1)} %get-tuple-element.30.refs_3_), channel_id=1, source_target_pairs={{2,0},{6,2},{10,6},{14,10},{12,14},{8,12},{4,8},{0,4},{3,1},{7,3},... | collective-permute-start | bytes 491528 | tf_op jit(solution)/shard_map/ppermute | solution.py:376
  8.8 8.9 %collective-permute-start.8 = (bf16[64,1280]{1,0:T(8,128)(2,1)S(1)}, bf16[64,1280]{1,0:T(8,128)(2,1)S(1)}, u32[]{:S(2)}, u32[]{:S(2)}) collective-permute-start(bf16[64,1280]{1,0:T(8,128)(2,1)S(1)} %collective-permute-done.7.refs_9_.refs_2_), channel_id=1, source_target_pairs={{2,0},{6,2},{10,6},{14,10},{12,14},{8,12},{4,8},{0,4},{3,1},{7,3},... | collective-permute-start | bytes 491528 | tf_op jit(solution)/shard_map/ppermute | solution.py:374
  11.8 7.1 %collective-permute-start.3 = (bf16[64,1280]{1,0:T(8,128)(2,1)S(1)}, bf16[64,1280]{1,0:T(8,128)(2,1)S(1)}, u32[]{:S(2)}, u32[]{:S(2)}) collective-permute-start(bf16[64,1280]{1,0:T(8,128)(2,1)S(1)} %collective-permute-done.2.refs_4_), channel_id=1, source_target_pairs={{0,2},{2,6},{6,10},{10,14},{14,12},{12,8},{8,4},{4,0},{1,3},{3,7},... | collective-permute-start | bytes 491528 | tf_op jit(solution)/shard_map/ppermute | solution.py:373
  15.3 7.1 %collective-permute-start.10 = (bf16[64,1280]{1,0:T(8,128)(2,1)S(1)}, bf16[64,1280]{1,0:T(8,128)(2,1)S(1)}, u32[]{:S(2)}, u32[]{:S(2)}) collective-permute-start(bf16[64,1280]{1,0:T(8,128)(2,1)S(1)} %collective-permute-done.9.refs_8_.refs_1_), channel_id=1, source_target_pairs={{0,2},{2,6},{6,10},{10,14},{14,12},{12,8},{8,4},{4,0},{1,3},{3,7},... | collective-permute-start | bytes 491528 | tf_op jit(solution)/shard_map/ppermute | solution.py:375
  15.3 8.2 %collective-permute-start.1 = (bf16[64,1280]{1,0:T(8,128)(2,1)S(1)}, bf16[64,1280]{1,0:T(8,128)(2,1)S(1)}, u32[]{:S(2)}, u32[]{:S(2)}) collective-permute-start(bf16[64,1280]{1,0:T(8,128)(2,1)S(1)} %collective-permute-done.refs_5_), channel_id=1, source_target_pairs={{2,0},{6,2},{10,6},{14,10},{12,14},{8,12},{4,8},{0,4},{3,1},{7,3},... | collective-permute-start | bytes 491528 | tf_op jit(solution)/shard_map/ppermute | solution.py:376
  17.6 6.8 %collective-permute-start.12 = (bf16[64,1280]{1,0:T(8,128)(2,1)S(1)}, bf16[64,1280]{1,0:T(8,128)(2,1)S(1)}, u32[]{:S(2)}, u32[]{:S(2)}) collective-permute-start(bf16[64,1280]{1,0:T(8,128)(2,1)S(1)} %collective-permute-done.8.refs_6_.refs_4_), channel_id=1, source_target_pairs={{2,0},{6,2},{10,6},{14,10},{12,14},{8,12},{4,8},{0,4},{3,1},{7,3},... | collective-permute-start | bytes 491528 | tf_op jit(solution)/shard_map/ppermute | solution.py:374
  18.9 7.1 %collective-permute-start.4 = (bf16[64,1280]{1,0:T(8,128)(2,1)S(1)}, bf16[64,1280]{1,0:T(8,128)(2,1)S(1)}, u32[]{:S(2)}, u32[]{:S(2)}) collective-permute-start(bf16[64,1280]{1,0:T(8,128)(2,1)S(1)} %collective-permute-done.3.refs_6_), channel_id=1, source_target_pairs={{0,2},{2,6},{6,10},{10,14},{14,12},{12,8},{8,4},{4,0},{1,3},{3,7},... | collective-permute-start | bytes 491528 | tf_op jit(solution)/shard_map/ppermute | solution.py:373
  22.5 7.8 %collective-permute-start.11 = (bf16[64,1280]{1,0:T(8,128)(2,1)S(1)}, bf16[64,1280]{1,0:T(8,128)(2,1)S(1)}, u32[]{:S(2)}, u32[]{:S(2)}) collective-permute-start(bf16[64,1280]{1,0:T(8,128)(2,1)S(1)} %collective-permute-done.10.refs_10_.refs_3_), channel_id=1, source_target_pairs={{0,2},{2,6},{6,10},{10,14},{14,12},{12,8},{8,4},{4,0},{1,3},{3,7},... | collective-permute-start | bytes 491528 | tf_op jit(solution)/shard_map/ppermute | solution.py:375
  23.5 6.7 %collective-permute-start.5 = (bf16[64,1280]{1,0:T(8,128)(2,1)S(1)}, bf16[64,1280]{1,0:T(8,128)(2,1)S(1)}, u32[]{:S(2)}, u32[]{:S(2)}) collective-permute-start(bf16[64,1280]{1,0:T(8,128)(2,1)S(1)} %collective-permute-done.1.refs_2_), channel_id=1, source_target_pairs={{2,0},{6,2},{10,6},{14,10},{12,14},{8,12},{4,8},{0,4},{3,1},{7,3},... | collective-permute-start | bytes 491528 | tf_op jit(solution)/shard_map/ppermute | solution.py:376
  24.5 6.1 %collective-permute-start.13 = (bf16[64,1280]{1,0:T(8,128)(2,1)S(1)}, bf16[64,1280]{1,0:T(8,128)(2,1)S(1)}, u32[]{:S(2)}, u32[]{:S(2)}) collective-permute-start(bf16[64,1280]{1,0:T(8,128)(2,1)S(1)} %collective-permute-done.12.refs_8_.refs_6_), channel_id=1, source_target_pairs={{2,0},{6,2},{10,6},{14,10},{12,14},{8,12},{4,8},{0,4},{3,1},{7,3},... | collective-permute-start | bytes 491528 | tf_op jit(solution)/shard_map/ppermute | solution.py:381
  26.1 5.3 %collective-permute-start.6 = (bf16[64,1280]{1,0:T(8,128)(2,1)S(1)}, bf16[64,1280]{1,0:T(8,128)(2,1)S(1)}, u32[]{:S(2)}, u32[]{:S(2)}) collective-permute-start(bf16[64,1280]{1,0:T(8,128)(2,1)S(1)} %collective-permute-done.4.refs_3_), channel_id=1, source_target_pairs={{0,2},{2,6},{6,10},{10,14},{14,12},{12,8},{8,4},{4,0},{1,3},{3,7},... | collective-permute-start | bytes 491528 | tf_op jit(solution)/shard_map/ppermute | solution.py:380
  30.1 6.7 %collective-permute-start.19 = (f32[256,512]{1,0:T(8,128)S(1)}, f32[256,512]{1,0:T(8,128)S(1)}, u32[]{:S(2)}, u32[]{:S(2)}) collective-permute-start(f32[256,512]{1,0:T(8,128)S(1)} %get-tuple-element.40), channel_id=1, source_target_pairs={{0,1},{1,0},{2,3},{3,2},{4,5},{5,4},{6,7},{7,6},{8,9},{9,8},{10,11... | collective-permute-start | bytes 1572872 | tf_op jit(solution)/shard_map/ppermute | solution.py:397
  32.0 4.0 %collective-permute-start.17 = (bf16[128,128]{1,0:T(8,128)(2,1)S(1)}, bf16[128,128]{1,0:T(8,128)(2,1)S(1)}, u32[]{:S(2)}, u32[]{:S(2)}) collective-permute-start(bf16[128,128]{1,0:T(8,128)(2,1)S(1)} %shard_map.87), channel_id=1, source_target_pairs={{0,16},{16,0},{1,17},{17,1},{2,18},{18,2},{3,19},{19,3},{4,20},{20... | collective-permute-start | bytes 98312 | tf_op jit(solution)/shard_map/ppermute | solution.py:403
  33.5 3.3 %collective-permute-start.18 = (bf16[128,128]{1,0:T(8,128)(2,1)S(1)}, bf16[128,128]{1,0:T(8,128)(2,1)S(1)}, u32[]{:S(2)}, u32[]{:S(2)}) collective-permute-start(bf16[128,128]{1,0:T(8,128)(2,1)S(1)} %shard_map.87), channel_id=1, source_target_pairs={{0,17},{1,16},{16,1},{17,0},{2,19},{3,18},{18,3},{19,2},{4,21},{5,... | collective-permute-start | bytes 98312 | tf_op jit(solution)/shard_map/ppermute | solution.py:404
  34.1 2.8 %collective-permute-start.15 = (f32[64,128]{1,0:T(8,128)S(1)}, f32[64,128]{1,0:T(8,128)S(1)}, u32[]{:S(2)}, u32[]{:S(2)}) collective-permute-start(f32[64,128]{1,0:T(8,128)S(1)} %get-tuple-element.34.top), channel_id=1, source_target_pairs={{0,1},{1,0},{2,3},{3,2},{4,5},{5,4},{6,7},{7,6},{8,9},{9,8},{10,11... | collective-permute-start | bytes 98312 | tf_op jit(solution)/shard_map/ppermute | solution.py:405
  34.8 2.1 %collective-permute-start.16 = (f32[64,128]{1,0:T(8,128)S(1)}, f32[64,128]{1,0:T(8,128)S(1)}, u32[]{:S(2)}, u32[]{:S(2)}) collective-permute-start(f32[64,128]{1,0:T(8,128)S(1)} %get-tuple-element.35.low), channel_id=1, source_target_pairs={{0,1},{1,0},{2,3},{3,2},{4,5},{5,4},{6,7},{7,6},{8,9},{9,8},{10,11... | collective-permute-start | bytes 98312 | tf_op jit(solution)/shard_map/ppermute | solution.py:405

commit v17 on v16

--- a/solution.py
+++ b/solution.py
@@ -43,17 +43,15 @@
     return 2 * -(-columns // 1024) * 8
 
 
-def prologue_kernel(
+def shard_kernel(
     depth,
     rank,
-    hidden_ref,
     factor_ref,
     factor_out_ref,
     demand_ref,
     lengths_ref,
     holder_ref,
     slots_ref,
-    to_other_ref,
     first_ref,
     second_ref,
     bounds_ref,
@@ -62,13 +60,10 @@
     holder,
     slots,
     sems,
-    hidden_sem,
 ):
     group, place = lax.axis_index("groups"), lax.axis_index("batch")
     cut = first_ref.shape[1]
-    rows = hidden_ref.shape[0]
     here = pl.multiple_of(group * depth, 128)
-    there = pl.multiple_of((1 - group) * depth, 128)
     after = pl.multiple_of(group * depth + cut, 128)
     small = [
         pltpu.make_async_copy(demand_ref, demand, sems.at[0]),
@@ -83,14 +78,6 @@
         ),
         pltpu.make_async_copy(factor_out_ref, second_ref.at[:, depth - cut :], sems.at[6]),
     ]
-    for i in range(depth // 128):
-        large.append(
-            pltpu.make_async_copy(
-                hidden_ref.at[:, pl.ds(there + i * 128, 128)],
-                to_other_ref.at[i * rows : (i + 1) * rows],
-                hidden_sem.at[i],
-            )
-        )
     for copy in small + large:
         copy.start()
     for copy in small:
@@ -139,45 +126,67 @@
     bounds_ref[0:1, :] = low
     bounds_ref[1:2, :] = high
     bounds_ref[2:8, :] = jnp.zeros((6, count * rank), I32)
-    extra = extra_rows(count * rank)
-    line = lax.broadcasted_iota(I32, (extra, 128), 0)
-    ends = jnp.zeros((extra, 128), I32)
-    for i in range(count * rank // 128):
-        columns = slice(i * 128, (i + 1) * 128)
-        ends = jnp.where(line == i, low[:, columns], ends)
-        ends = jnp.where(line == extra // 2 + i, high[:, columns], ends)
-    to_other_ref[-extra:, :] = ends.astype(F32).astype(BF16)
     for copy in large:
         copy.wait()
 
 
-def prologue(hidden, factor, factor_out, demand, lengths, holder_slot, slots):
-    rows, features = hidden.shape
+def shard_call(factor, factor_out, demand, lengths, holder_slot, slots, depth):
     rank, width = factor_out.shape
-    depth = features // 2
     cut = (depth + width) // 2
     count = slots.shape[2]
-    tall = depth // 128 * rows + extra_rows(count * rank)
-    return pl.pallas_call(
-        functools.partial(prologue_kernel, depth, rank),
+    return pl.pallas_call(
+        functools.partial(shard_kernel, depth, rank),
         out_shape=(
-            jax.ShapeDtypeStruct((tall, 128), hidden.dtype),
             jax.ShapeDtypeStruct((rank, cut), factor.dtype),
             jax.ShapeDtypeStruct((rank, cut), factor.dtype),
             jax.ShapeDtypeStruct((8, count * rank), I32),
         ),
-        in_specs=[HBM] * 7,
-        out_specs=(VMEM,) * 4,
+        in_specs=[HBM] * 6,
+        out_specs=(VMEM,) * 3,
         scratch_shapes=[
             pltpu.SMEM(demand.shape, I32),
             pltpu.SMEM(lengths.shape, I32),
             pltpu.SMEM(holder_slot.shape, I32),
             pltpu.SMEM((1, 1, count), I32),
             pltpu.SemaphoreType.DMA((7,)),
-            pltpu.SemaphoreType.DMA((depth // 128,)),
         ],
         compiler_params=params(),
-    )(*map(in_hbm, (hidden, factor, factor_out, demand, lengths, holder_slot, slots)))
+        cost_estimate=LONG,
+    )(*map(in_hbm, (factor, factor_out, demand, lengths, holder_slot, slots)))
+
+
+def rows_kernel(depth, hidden_ref, bounds_ref, to_other_ref, bounds_out_ref):
+    rows = hidden_ref.shape[0]
+    there = pl.multiple_of((1 - lax.axis_index("groups")) * depth, 128)
+    for i in range(depth // 128):
+        to_other_ref[i * rows : (i + 1) * rows, :] = hidden_ref[:, pl.ds(there + i * 128, 128)]
+    columns = bounds_ref.shape[1]
+    extra = extra_rows(columns)
+    line = lax.broadcasted_iota(I32, (extra, 128), 0)
+    ends = jnp.zeros((extra, 128), I32)
+    for i in range(columns // 128):
+        span = slice(i * 128, (i + 1) * 128)
+        ends = jnp.where(line == i, bounds_ref[0:1, span], ends)
+        ends = jnp.where(line == extra // 2 + i, bounds_ref[1:2, span], ends)
+    to_other_ref[-extra:, :] = ends.astype(F32).astype(BF16)
+    bounds_out_ref[...] = bounds_ref[...]
+
+
+def rows_call(hidden, bounds):
+    rows, features = hidden.shape
+    depth = features // 2
+    tall = depth // 128 * rows + extra_rows(bounds.shape[1])
+    return pl.pallas_call(
+        functools.partial(rows_kernel, depth),
+        out_shape=(
+            jax.ShapeDtypeStruct((tall, 128), hidden.dtype),
+            jax.ShapeDtypeStruct(bounds.shape, I32),
+        ),
+        in_specs=[VMEM] * 2,
+        out_specs=(VMEM,) * 2,
+        compiler_params=params(),
+        cost_estimate=LONG,
+    )(hidden, bounds)
 
 
 def mark_kernel(bounds_ref, out_ref):
@@ -355,16 +364,10 @@
         [[order[(order.index(me) - distance) % owners] for distance in distances]]
         for me in range(owners)
     ]
-    to_other, first, second, bounds = prologue(
-        hidden,
-        factor_in[0].T,
-        factor_out[0],
-        demand,
-        lengths,
-        holder_slot,
-        jnp.asarray(table, I32),
+    first, second, bounds = shard_call(
+        factor_in[0].T, factor_out[0], demand, lengths, holder_slot, jnp.asarray(table, I32), depth
     )
-
+    to_other, bounds = rows_call(hidden, bounds)
     bounds, first_later, second_later = lax.optimization_barrier((mark(bounds), first, second))
 
     firsts, seconds = [first], [second]

time: 38.2 us -> 37.9 us (level)
  starting transfers between devices: 20.2 us -> 19.5 us
  waiting for transfers between devices: 10.8 us -> 11.3 us
    ppermute x3, starting transfers between devices: 6.68 us -> 5.32 us  [per_device(): d = lax.ppermute(behind[1], 'batch', backward)]
    ppermute x3, waiting for transfers between devices: 0.36 us -> 1.35 us  [per_device(): d = lax.ppermute(behind[1], 'batch', backward)]
    ppermute x3, starting transfers between devices: 0.74 us -> 1.58 us  [per_device(): a = lax.ppermute(ahead[0], 'batch', forward)]
    ppermute x1, waiting for transfers between devices: 0.79 us -> 0.01 us  [per_device(): firsts.append(lax.ppermute(ahead[0], 'batch', forward))]
    ppermute x1, starting transfers between devices: 1.58 us -> 0.89 us  [per_device(): seconds.append(lax.ppermute(behind[1], 'batch', backward))]
    ppermute x3, starting transfers between devices: 3.48 us -> 2.84 us  [per_device(): c = lax.ppermute(behind[0], 'batch', backward)]
    ppermute x3, starting transfers between devices: 2.65 us -> 3.3 us  [per_device(): b = lax.ppermute(ahead[1], 'batch', forward)]
    ppermute x1, waiting for transfers between devices: 0.37 us -> 0.87 us  [per_device(): seconds.append(lax.ppermute(behind[1], 'batch', backward))]
  transfers between devices with their start and end apart: 20 -> 20, of which waited for: 10 -> 8; matrix products, arithmetic and copies ran while one was open for 0% -> 0% of each run, Pallas kernels for 11% -> 12%
where the time goes in v17:
time: 37.9 us; the launch traced here: 37.7 us
  starting transfers between devices  19.5 us (51%)
  waiting for transfers between devices  11.3 us (30%)
  Pallas kernels  6.77 us (18%)
    ppermute x3, starting transfers between devices, per_device(): d = lax.ppermute(behind[1], 'batch', backward)  5.32 us
    ppermute x3, waiting for transfers between devices, per_device(): b = lax.ppermute(ahead[1], 'batch', forward)  3.51 us
    ppermute x3, starting transfers between devices, per_device(): b = lax.ppermute(ahead[1], 'batch', forward)  3.3 us
    ppermute x3, starting transfers between devices, per_device(): c = lax.ppermute(behind[0], 'batch', backward)  2.84 us
    ppermute x1, waiting for transfers between devices, per_device(): other = lax.ppermute(to_other, 'groups', swap)  2.53 us
    pallas_call x1, Pallas kernels, base_call(): pl.pallas_call(base_kernel, out_shape=(out, out), in_specs=[VMEM] * 2, ou...  2.35 us
    ppermute x1, starting transfers between devices, per_device(): other = lax.ppermute(to_other, 'groups', swap)  2.03 us
    pallas_call x3, Pallas kernels, rank_call(): pl.pallas_call(functools.partial(rank_kernel, sides, groups, depth, last)...  1.84 us
  transfers between devices with their start and end apart: 20, of which 8 were waited for; matrix products, arithmetic and copies ran while one was open for 0% of the time, Pallas kernels for 12%

profile of v17, /device:TPU:0, one launch (start us, length us, event | category | flops | bytes accessed | tf_op | source)
XLA Modules:
  0.0 37.7 jit_solution(7539522081843755360)
XLA Ops:
  0.0 1.2 %shard_map.82 = (bf16[64,1280]{1,0:T(8,128)(2,1)S(1)}, bf16[64,1280]{1,0:T(8,128)(2,1)S(1)}, s32[8,512]{1,0:T(8,128)S(1)}) custom-call(bf16[64,4096]{1,0:T(8,128)(2,1)} %bitcast.6, bf16[64,512]{1,0:T(8,128)(2,1)} %bitcast.7, s32[1,4]{1,0:T(1,128)} %demand_ref.1, s32[1,4]{1,0:T(1,128)} %lengths_ref.1, s32[8]{0:T(128)} %holder_ref.1, ...), custom_call_target="tpu_custom_call" | custom-call | flops 8589934592 | bytes 16777216 | tf_op jit(solution)/shard_map/pallas_call | solution.py:137
  1.2 3.1 %collective-permute-start.7 = (bf16[64,1280]{1,0:T(8,128)(2,1)S(1)}, bf16[64,1280]{1,0:T(8,128)(2,1)S(1)}, u32[]{:S(2)}, u32[]{:S(2)}) collective-permute-start(bf16[64,1280]{1,0:T(8,128)(2,1)S(1)} %get-tuple-element.33.refs_7_.refs_0_), channel_id=1, source_target_pairs={{2,0},{6,2},{10,6},{14,10},{12,14},{8,12},{4,8},{0,4},{3,1},{7,3},... | collective-permute-start | bytes 491528 | tf_op jit(solution)/shard_map/ppermute | solution.py:377
  4.3 0.0 collective-permute-start.2
  4.3 0.3 shard_map.83
  4.6 2.0 %collective-permute-start.14 = (bf16[4112,128]{1,0:T(8,128)(2,1)S(1)}, bf16[4112,128]{1,0:T(8,128)(2,1)S(1)}, u32[]{:S(2)}, u32[]{:S(2)}) collective-permute-start(bf16[4112,128]{1,0:T(8,128)(2,1)S(1)} %get-tuple-element.34), channel_id=1, source_target_pairs={{0,16},{16,0},{1,17},{17,1},{2,18},{18,2},{3,19},{19,3},{4,20},{20... | collective-permute-start | bytes 3158024 | tf_op jit(solution)/shard_map/ppermute | solution.py:387
  6.6 1.5 %collective-permute-start.9 = (bf16[64,1280]{1,0:T(8,128)(2,1)S(1)}, bf16[64,1280]{1,0:T(8,128)(2,1)S(1)}, u32[]{:S(2)}, u32[]{:S(2)}) collective-permute-start(bf16[64,1280]{1,0:T(8,128)(2,1)S(1)} %get-tuple-element.33.refs_7_.refs_0_), channel_id=1, source_target_pairs={{0,2},{2,6},{6,10},{10,14},{14,12},{12,8},{8,4},{4,0},{1,3},{3,7},... | collective-permute-start | bytes 491528 | tf_op jit(solution)/shard_map/ppermute | solution.py:378
  8.1 0.5 %collective-permute-start = (bf16[64,1280]{1,0:T(8,128)(2,1)S(1)}, bf16[64,1280]{1,0:T(8,128)(2,1)S(1)}, u32[]{:S(2)}, u32[]{:S(2)}) collective-permute-start(bf16[64,1280]{1,0:T(8,128)(2,1)S(1)} %get-tuple-element.32.refs_3_), channel_id=1, source_target_pairs={{2,0},{6,2},{10,6},{14,10},{12,14},{8,12},{4,8},{0,4},{3,1},{7,3},... | collective-permute-start | bytes 491528 | tf_op jit(solution)/shard_map/ppermute | solution.py:379
  8.6 0.0 collective-permute-done.7.refs_9_.refs_2_
  8.6 1.8 %collective-permute-start.8 = (bf16[64,1280]{1,0:T(8,128)(2,1)S(1)}, bf16[64,1280]{1,0:T(8,128)(2,1)S(1)}, u32[]{:S(2)}, u32[]{:S(2)}) collective-permute-start(bf16[64,1280]{1,0:T(8,128)(2,1)S(1)} %collective-permute-done.7.refs_9_.refs_2_), channel_id=1, source_target_pairs={{2,0},{6,2},{10,6},{14,10},{12,14},{8,12},{4,8},{0,4},{3,1},{7,3},... | collective-permute-start | bytes 491528 | tf_op jit(solution)/shard_map/ppermute | solution.py:377
  10.4 1.0 %collective-permute-done.2.refs_4_ = bf16[64,1280]{1,0:T(8,128)(2,1)S(1)} collective-permute-done((bf16[64,1280]{1,0:T(8,128)(2,1)S(1)}, bf16[64,1280]{1,0:T(8,128)(2,1)S(1)}, u32[]{:S(2)}, u32[]{:S(2)}) %collective-permute-start.2) | collective-permute-done | bytes 163872 | tf_op jit(solution)/shard_map/ppermute | solution.py:376
  11.4 0.0 collective-permute-start.3
  11.4 3.5 %collective-permute-done.9.refs_8_.refs_1_ = bf16[64,1280]{1,0:T(8,128)(2,1)S(1)} collective-permute-done((bf16[64,1280]{1,0:T(8,128)(2,1)S(1)}, bf16[64,1280]{1,0:T(8,128)(2,1)S(1)}, u32[]{:S(2)}, u32[]{:S(2)}) %collective-permute-start.9) | collective-permute-done | bytes 163872 | tf_op jit(solution)/shard_map/ppermute | solution.py:378
  14.9 0.3 collective-permute-start.10
  15.2 0.0 collective-permute-done.refs_5_
  15.2 1.7 %collective-permute-start.1 = (bf16[64,1280]{1,0:T(8,128)(2,1)S(1)}, bf16[64,1280]{1,0:T(8,128)(2,1)S(1)}, u32[]{:S(2)}, u32[]{:S(2)}) collective-permute-start(bf16[64,1280]{1,0:T(8,128)(2,1)S(1)} %collective-permute-done.refs_5_), channel_id=1, source_target_pairs={{2,0},{6,2},{10,6},{14,10},{12,14},{8,12},{4,8},{0,4},{3,1},{7,3},... | collective-permute-start | bytes 491528 | tf_op jit(solution)/shard_map/ppermute | solution.py:379
  16.9 1.1 %collective-permute-done.8.refs_6_.refs_4_ = bf16[64,1280]{1,0:T(8,128)(2,1)S(1)} collective-permute-done((bf16[64,1280]{1,0:T(8,128)(2,1)S(1)}, bf16[64,1280]{1,0:T(8,128)(2,1)S(1)}, u32[]{:S(2)}, u32[]{:S(2)}) %collective-permute-start.8) | collective-permute-done | bytes 163872 | tf_op jit(solution)/shard_map/ppermute | solution.py:377
  18.1 0.4 %collective-permute-start.12 = (bf16[64,1280]{1,0:T(8,128)(2,1)S(1)}, bf16[64,1280]{1,0:T(8,128)(2,1)S(1)}, u32[]{:S(2)}, u32[]{:S(2)}) collective-permute-start(bf16[64,1280]{1,0:T(8,128)(2,1)S(1)} %collective-permute-done.8.refs_6_.refs_4_), channel_id=1, source_target_pairs={{2,0},{6,2},{10,6},{14,10},{12,14},{8,12},{4,8},{0,4},{3,1},{7,3},... | collective-permute-start | bytes 491528 | tf_op jit(solution)/shard_map/ppermute | solution.py:377
  18.5 0.0 collective-permute-done.3.refs_6_
  18.5 1.6 %collective-permute-start.4 = (bf16[64,1280]{1,0:T(8,128)(2,1)S(1)}, bf16[64,1280]{1,0:T(8,128)(2,1)S(1)}, u32[]{:S(2)}, u32[]{:S(2)}) collective-permute-start(bf16[64,1280]{1,0:T(8,128)(2,1)S(1)} %collective-permute-done.3.refs_6_), channel_id=1, source_target_pairs={{0,2},{2,6},{6,10},{10,14},{14,12},{12,8},{8,4},{4,0},{1,3},{3,7},... | collective-permute-start | bytes 491528 | tf_op jit(solution)/shard_map/ppermute | solution.py:376
  20.1 0.0 slice-done
  20.1 2.3 %shard_map.85 = (f32[256,512]{1,0:T(8,128)S(1)}, f32[256,512]{1,0:T(8,128)S(1)}) custom-call(bf16[256,4096]{1,0:T(8,128)(2,1)S(1)} %copy-done, bf16[4096,1024]{1,0:T(8,128)(2,1)S(1)} %bitcast.5), custom_call_target="tpu_custom_call" | custom-call | bytes 4194304 | tf_op jit(solution)/shard_map/pallas_call | solution.py:219
  22.5 0.0 collective-permute-done.10.refs_10_.refs_3_
  22.5 1.5 %collective-permute-start.11 = (bf16[64,1280]{1,0:T(8,128)(2,1)S(1)}, bf16[64,1280]{1,0:T(8,128)(2,1)S(1)}, u32[]{:S(2)}, u32[]{:S(2)}) collective-permute-start(bf16[64,1280]{1,0:T(8,128)(2,1)S(1)} %collective-permute-done.10.refs_10_.refs_3_), channel_id=1, source_target_pairs={{0,2},{2,6},{6,10},{10,14},{14,12},{12,8},{8,4},{4,0},{1,3},{3,7},... | collective-permute-start | bytes 491528 | tf_op jit(solution)/shard_map/ppermute | solution.py:378
  24.0 0.0 collective-permute-done.1.refs_2_
  24.0 0.6 %collective-permute-start.5 = (bf16[64,1280]{1,0:T(8,128)(2,1)S(1)}, bf16[64,1280]{1,0:T(8,128)(2,1)S(1)}, u32[]{:S(2)}, u32[]{:S(2)}) collective-permute-start(bf16[64,1280]{1,0:T(8,128)(2,1)S(1)} %collective-permute-done.1.refs_2_), channel_id=1, source_target_pairs={{2,0},{6,2},{10,6},{14,10},{12,14},{8,12},{4,8},{0,4},{3,1},{7,3},... | collective-permute-start | bytes 491528 | tf_op jit(solution)/shard_map/ppermute | solution.py:379
  24.6 0.2 collective-permute-done.12.refs_8_.refs_6_
  24.8 0.9 %collective-permute-start.13 = (bf16[64,1280]{1,0:T(8,128)(2,1)S(1)}, bf16[64,1280]{1,0:T(8,128)(2,1)S(1)}, u32[]{:S(2)}, u32[]{:S(2)}) collective-permute-start(bf16[64,1280]{1,0:T(8,128)(2,1)S(1)} %collective-permute-done.12.refs_8_.refs_6_), channel_id=1, source_target_pairs={{2,0},{6,2},{10,6},{14,10},{12,14},{8,12},{4,8},{0,4},{3,1},{7,3},... | collective-permute-start | bytes 491528 | tf_op jit(solution)/shard_map/ppermute | solution.py:384
  25.7 0.0 collective-permute-done.4.refs_3_
  25.7 1.1 %collective-permute-start.6 = (bf16[64,1280]{1,0:T(8,128)(2,1)S(1)}, bf16[64,1280]{1,0:T(8,128)(2,1)S(1)}, u32[]{:S(2)}, u32[]{:S(2)}) collective-permute-start(bf16[64,1280]{1,0:T(8,128)(2,1)S(1)} %collective-permute-done.4.refs_3_), channel_id=1, source_target_pairs={{0,2},{2,6},{6,10},{10,14},{14,12},{12,8},{8,4},{4,0},{1,3},{3,7},... | collective-permute-start | bytes 491528 | tf_op jit(solution)/shard_map/ppermute | solution.py:383
  26.8 2.5 %collective-permute-done.14.refs_1_.refs_0_ = bf16[4112,128]{1,0:T(8,128)(2,1)S(1)} collective-permute-done((bf16[4112,128]{1,0:T(8,128)(2,1)S(1)}, bf16[4112,128]{1,0:T(8,128)(2,1)S(1)}, u32[]{:S(2)}, u32[]{:S(2)}) %collective-permute-start.14) | collective-permute-done | bytes 1052704 | tf_op jit(solution)/shard_map/ppermute | solution.py:387
  29.3 0.7 %shard_map.86 = (f32[256,128]{1,0:T(8,128)S(1)}, f32[256,128]{1,0:T(8,128)S(1)}) custom-call(bf16[256,4096]{1,0:T(8,128)(2,1)S(1)} %copy-done, bf16[4112,128]{1,0:T(8,128)(2,1)S(1)} %collective-permute-done.14.refs_1_.refs_0_, s32[8,512]{1,0:T(8,128)S(1)} %shard_map.84.refs_2_.refs_1_.bounds_ref, bf16[64,1280]{1,0:T(8,128)(2,1)S(1)} %get-tuple-element.32.refs_3_, ...), custom_call_target="tpu_custom_call" | custom-call | flops 8589934592 | bytes 16777216 | tf_op jit(solution)/shard_map/pallas_call | solution.py:313
  30.1 0.1 collective-permute-start.19
  30.2 0.0 collective-permute-done.11.refs_7_.refs_5_
  30.2 0.0 collective-permute-done.5.refs_4_
  30.2 0.9 %collective-permute-done.13.refs_9_.refs_7_ = bf16[64,1280]{1,0:T(8,128)(2,1)S(1)} collective-permute-done((bf16[64,1280]{1,0:T(8,128)(2,1)S(1)}, bf16[64,1280]{1,0:T(8,128)(2,1)S(1)}, u32[]{:S(2)}, u32[]{:S(2)}) %collective-permute-start.13) | collective-permute-done | bytes 163872 | tf_op jit(solution)/shard_map/ppermute | solution.py:384
  31.1 0.0 collective-permute-done.6.refs_5_
  31.1 0.5 %shard_map.88 = bf16[128,128]{1,0:T(8,128)(2,1)S(1)} custom-call(bf16[4112,128]{1,0:T(8,128)(2,1)S(1)} %collective-permute-done.14.refs_1_.refs_0_, s32[8,512]{1,0:T(8,128)S(1)} %shard_map.84.refs_2_.refs_1_.bounds_ref, bf16[64,1280]{1,0:T(8,128)(2,1)S(1)} %collective-permute-done.1.refs_2_, bf16[64,1280]{1,0:T(8,128)(2,1)S(1)} %collective-permute-done.4.refs_3_, ...), custom_call_target="tpu_custom_call" | custom-call | flops 8589934592 | bytes 16777216 | tf_op jit(solution)/shard_map/pallas_call | solution.py:313
  31.6 1.5 %collective-permute-start.17 = (bf16[128,128]{1,0:T(8,128)(2,1)S(1)}, bf16[128,128]{1,0:T(8,128)(2,1)S(1)}, u32[]{:S(2)}, u32[]{:S(2)}) collective-permute-start(bf16[128,128]{1,0:T(8,128)(2,1)S(1)} %shard_map.88), channel_id=1, source_target_pairs={{0,16},{16,0},{1,17},{17,1},{2,18},{18,2},{3,19},{19,3},{4,20},{20... | collective-permute-start | bytes 98312 | tf_op jit(solution)/shard_map/ppermute | solution.py:406
  33.1 0.0 collective-permute-start.18
  33.1 0.5 %shard_map.87 = (f32[64,128]{1,0:T(8,128)S(1)}, f32[64,128]{1,0:T(8,128)S(1)}) custom-call(bf16[256,4096]{1,0:T(8,128)(2,1)S(1)} %copy-done, s32[8,512]{1,0:T(8,128)S(1)} %shard_map.84.refs_2_.refs_1_.bounds_ref, bf16[64,1280]{1,0:T(8,128)(2,1)S(1)} %collective-permute-done.1.refs_2_, bf16[64,1280]{1,0:T(8,128)(2,1)S(1)} %collective-permute-done.4.refs_3_, ...), custom_call_target="tpu_custom_call" | custom-call | bytes 4194304 | tf_op jit(solution)/shard_map/pallas_call | solution.py:313
  33.7 0.7 %collective-permute-start.15 = (f32[64,128]{1,0:T(8,128)S(1)}, f32[64,128]{1,0:T(8,128)S(1)}, u32[]{:S(2)}, u32[]{:S(2)}) collective-permute-start(f32[64,128]{1,0:T(8,128)S(1)} %get-tuple-element.36.top), channel_id=1, source_target_pairs={{0,1},{1,0},{2,3},{3,2},{4,5},{5,4},{6,7},{7,6},{8,9},{9,8},{10,11... | collective-permute-start | bytes 98312 | tf_op jit(solution)/shard_map/ppermute | solution.py:408
  34.4 0.1 collective-permute-start.16
  34.5 1.1 %collective-permute-done.17.two = bf16[128,128]{1,0:T(8,128)(2,1)S(1)} collective-permute-done((bf16[128,128]{1,0:T(8,128)(2,1)S(1)}, bf16[128,128]{1,0:T(8,128)(2,1)S(1)}, u32[]{:S(2)}, u32[]{:S(2)}) %collective-permute-start.17) | collective-permute-done | bytes 32800 | tf_op jit(solution)/shard_map/ppermute | solution.py:406
  35.6 1.0 %collective-permute-done.18.three = bf16[128,128]{1,0:T(8,128)(2,1)S(1)} collective-permute-done((bf16[128,128]{1,0:T(8,128)(2,1)S(1)}, bf16[128,128]{1,0:T(8,128)(2,1)S(1)}, u32[]{:S(2)}, u32[]{:S(2)}) %collective-permute-start.18) | collective-permute-done | bytes 32800 | tf_op jit(solution)/shard_map/ppermute | solution.py:407
  36.6 0.0 collective-permute-done.15.one_top
  36.6 0.0 collective-permute-done.16.one_low
  36.6 0.0 collective-permute-done.19.far_ref
  36.6 1.1 %shard_map.89 = bf16[256,512]{1,0:T(8,128)(2,1)} custom-call(s32[8,512]{1,0:T(8,128)S(1)} %shard_map.84.refs_2_.refs_1_.bounds_ref, f32[64,128]{1,0:T(8,128)S(1)} %get-tuple-element.36.top, f32[64,128]{1,0:T(8,128)S(1)} %get-tuple-element.37.low, f32[64,128]{1,0:T(8,128)S(1)} %collective-permute-done.15.one_top, ...), custom_call_target="tpu_custom_call" | custom-call | tf_op jit(solution)/shard_map/pallas_call | solution.py:411
  (7 shorter events, 0.0 us)
Async XLA Ops:
  0.0 4.3 %copy-start = (bf16[256,4096]{1,0:T(8,128)(2,1)S(1)}, bf16[256,4096]{1,0:T(8,128)(2,1)}, u32[]{:S(2)}) copy-start(bf16[256,4096]{1,0:T(8,128)(2,1)} %refs_0_.1) | copy-start | bytes 6291460
  1.2 7.4 %collective-permute-start.7 = (bf16[64,1280]{1,0:T(8,128)(2,1)S(1)}, bf16[64,1280]{1,0:T(8,128)(2,1)S(1)}, u32[]{:S(2)}, u32[]{:S(2)}) collective-permute-start(bf16[64,1280]{1,0:T(8,128)(2,1)S(1)} %get-tuple-element.33.refs_7_.refs_0_), channel_id=1, source_target_pairs={{2,0},{6,2},{10,6},{14,10},{12,14},{8,12},{4,8},{0,4},{3,1},{7,3},... | collective-permute-start | bytes 491528 | tf_op jit(solution)/shard_map/ppermute | solution.py:377
  4.3 7.1 %collective-permute-start.2 = (bf16[64,1280]{1,0:T(8,128)(2,1)S(1)}, bf16[64,1280]{1,0:T(8,128)(2,1)S(1)}, u32[]{:S(2)}, u32[]{:S(2)}) collective-permute-start(bf16[64,1280]{1,0:T(8,128)(2,1)S(1)} %get-tuple-element.32.refs_3_), channel_id=1, source_target_pairs={{0,2},{2,6},{6,10},{10,14},{14,12},{12,8},{8,4},{4,0},{1,3},{3,7},... | collective-permute-start | bytes 491528 | tf_op jit(solution)/shard_map/ppermute | solution.py:376
  4.6 24.8 %collective-permute-start.14 = (bf16[4112,128]{1,0:T(8,128)(2,1)S(1)}, bf16[4112,128]{1,0:T(8,128)(2,1)S(1)}, u32[]{:S(2)}, u32[]{:S(2)}) collective-permute-start(bf16[4112,128]{1,0:T(8,128)(2,1)S(1)} %get-tuple-element.34), channel_id=1, source_target_pairs={{0,16},{16,0},{1,17},{17,1},{2,18},{18,2},{3,19},{19,3},{4,20},{20... | collective-permute-start | bytes 3158024 | tf_op jit(solution)/shard_map/ppermute | solution.py:387
  6.6 13.5 %slice-start = ((s8[8388608]{0:T(1024)(128)(4,1)}), s8[4194304]{0:T(1024)(128)(4,1)S(1)}, s32[]{:S(2)}) async-start(s8[8388608]{0:T(1024)(128)(4,1)} %bitcast.4), calls=%async_computation | async-start | bytes 8388608
  6.6 13.5 %slice-start.1 = ((s8[8388608]{0:T(1024)(128)(4,1)}), s8[4194304]{0:T(1024)(128)(4,1)S(1)}, s32[]{:S(2)}) async-start(s8[8388608]{0:T(1024)(128)(4,1)} %bitcast.4), calls=%async_computation.1 | async-start | bytes 8388608
  6.6 8.3 %collective-permute-start.9 = (bf16[64,1280]{1,0:T(8,128)(2,1)S(1)}, bf16[64,1280]{1,0:T(8,128)(2,1)S(1)}, u32[]{:S(2)}, u32[]{:S(2)}) collective-permute-start(bf16[64,1280]{1,0:T(8,128)(2,1)S(1)} %get-tuple-element.33.refs_7_.refs_0_), channel_id=1, source_target_pairs={{0,2},{2,6},{6,10},{10,14},{14,12},{12,8},{8,4},{4,0},{1,3},{3,7},... | collective-permute-start | bytes 491528 | tf_op jit(solution)/shard_map/ppermute | solution.py:378
  8.1 7.1 %collective-permute-start = (bf16[64,1280]{1,0:T(8,128)(2,1)S(1)}, bf16[64,1280]{1,0:T(8,128)(2,1)S(1)}, u32[]{:S(2)}, u32[]{:S(2)}) collective-permute-start(bf16[64,1280]{1,0:T(8,128)(2,1)S(1)} %get-tuple-element.32.refs_3_), channel_id=1, source_target_pairs={{2,0},{6,2},{10,6},{14,10},{12,14},{8,12},{4,8},{0,4},{3,1},{7,3},... | collective-permute-start | bytes 491528 | tf_op jit(solution)/shard_map/ppermute | solution.py:379
  8.6 9.5 %collective-permute-start.8 = (bf16[64,1280]{1,0:T(8,128)(2,1)S(1)}, bf16[64,1280]{1,0:T(8,128)(2,1)S(1)}, u32[]{:S(2)}, u32[]{:S(2)}) collective-permute-start(bf16[64,1280]{1,0:T(8,128)(2,1)S(1)} %collective-permute-done.7.refs_9_.refs_2_), channel_id=1, source_target_pairs={{2,0},{6,2},{10,6},{14,10},{12,14},{8,12},{4,8},{0,4},{3,1},{7,3},... | collective-permute-start | bytes 491528 | tf_op jit(solution)/shard_map/ppermute | solution.py:377
  11.4 7.1 %collective-permute-start.3 = (bf16[64,1280]{1,0:T(8,128)(2,1)S(1)}, bf16[64,1280]{1,0:T(8,128)(2,1)S(1)}, u32[]{:S(2)}, u32[]{:S(2)}) collective-permute-start(bf16[64,1280]{1,0:T(8,128)(2,1)S(1)} %collective-permute-done.2.refs_4_), channel_id=1, source_target_pairs={{0,2},{2,6},{6,10},{10,14},{14,12},{12,8},{8,4},{4,0},{1,3},{3,7},... | collective-permute-start | bytes 491528 | tf_op jit(solution)/shard_map/ppermute | solution.py:376
  14.9 7.6 %collective-permute-start.10 = (bf16[64,1280]{1,0:T(8,128)(2,1)S(1)}, bf16[64,1280]{1,0:T(8,128)(2,1)S(1)}, u32[]{:S(2)}, u32[]{:S(2)}) collective-permute-start(bf16[64,1280]{1,0:T(8,128)(2,1)S(1)} %collective-permute-done.9.refs_8_.refs_1_), channel_id=1, source_target_pairs={{0,2},{2,6},{6,10},{10,14},{14,12},{12,8},{8,4},{4,0},{1,3},{3,7},... | collective-permute-start | bytes 491528 | tf_op jit(solution)/shard_map/ppermute | solution.py:378
  15.2 8.7 %collective-permute-start.1 = (bf16[64,1280]{1,0:T(8,128)(2,1)S(1)}, bf16[64,1280]{1,0:T(8,128)(2,1)S(1)}, u32[]{:S(2)}, u32[]{:S(2)}) collective-permute-start(bf16[64,1280]{1,0:T(8,128)(2,1)S(1)} %collective-permute-done.refs_5_), channel_id=1, source_target_pairs={{2,0},{6,2},{10,6},{14,10},{12,14},{8,12},{4,8},{0,4},{3,1},{7,3},... | collective-permute-start | bytes 491528 | tf_op jit(solution)/shard_map/ppermute | solution.py:379
  18.1 6.7 %collective-permute-start.12 = (bf16[64,1280]{1,0:T(8,128)(2,1)S(1)}, bf16[64,1280]{1,0:T(8,128)(2,1)S(1)}, u32[]{:S(2)}, u32[]{:S(2)}) collective-permute-start(bf16[64,1280]{1,0:T(8,128)(2,1)S(1)} %collective-permute-done.8.refs_6_.refs_4_), channel_id=1, source_target_pairs={{2,0},{6,2},{10,6},{14,10},{12,14},{8,12},{4,8},{0,4},{3,1},{7,3},... | collective-permute-start | bytes 491528 | tf_op jit(solution)/shard_map/ppermute | solution.py:377
  18.5 7.1 %collective-permute-start.4 = (bf16[64,1280]{1,0:T(8,128)(2,1)S(1)}, bf16[64,1280]{1,0:T(8,128)(2,1)S(1)}, u32[]{:S(2)}, u32[]{:S(2)}) collective-permute-start(bf16[64,1280]{1,0:T(8,128)(2,1)S(1)} %collective-permute-done.3.refs_6_), channel_id=1, source_target_pairs={{0,2},{2,6},{6,10},{10,14},{14,12},{12,8},{8,4},{4,0},{1,3},{3,7},... | collective-permute-start | bytes 491528 | tf_op jit(solution)/shard_map/ppermute | solution.py:376
  22.5 7.7 %collective-permute-start.11 = (bf16[64,1280]{1,0:T(8,128)(2,1)S(1)}, bf16[64,1280]{1,0:T(8,128)(2,1)S(1)}, u32[]{:S(2)}, u32[]{:S(2)}) collective-permute-start(bf16[64,1280]{1,0:T(8,128)(2,1)S(1)} %collective-permute-done.10.refs_10_.refs_3_), channel_id=1, source_target_pairs={{0,2},{2,6},{6,10},{10,14},{14,12},{12,8},{8,4},{4,0},{1,3},{3,7},... | collective-permute-start | bytes 491528 | tf_op jit(solution)/shard_map/ppermute | solution.py:378
  24.0 6.2 %collective-permute-start.5 = (bf16[64,1280]{1,0:T(8,128)(2,1)S(1)}, bf16[64,1280]{1,0:T(8,128)(2,1)S(1)}, u32[]{:S(2)}, u32[]{:S(2)}) collective-permute-start(bf16[64,1280]{1,0:T(8,128)(2,1)S(1)} %collective-permute-done.1.refs_2_), channel_id=1, source_target_pairs={{2,0},{6,2},{10,6},{14,10},{12,14},{8,12},{4,8},{0,4},{3,1},{7,3},... | collective-permute-start | bytes 491528 | tf_op jit(solution)/shard_map/ppermute | solution.py:379
  24.8 6.3 %collective-permute-start.13 = (bf16[64,1280]{1,0:T(8,128)(2,1)S(1)}, bf16[64,1280]{1,0:T(8,128)(2,1)S(1)}, u32[]{:S(2)}, u32[]{:S(2)}) collective-permute-start(bf16[64,1280]{1,0:T(8,128)(2,1)S(1)} %collective-permute-done.12.refs_8_.refs_6_), channel_id=1, source_target_pairs={{2,0},{6,2},{10,6},{14,10},{12,14},{8,12},{4,8},{0,4},{3,1},{7,3},... | collective-permute-start | bytes 491528 | tf_op jit(solution)/shard_map/ppermute | solution.py:384
  25.7 5.4 %collective-permute-start.6 = (bf16[64,1280]{1,0:T(8,128)(2,1)S(1)}, bf16[64,1280]{1,0:T(8,128)(2,1)S(1)}, u32[]{:S(2)}, u32[]{:S(2)}) collective-permute-start(bf16[64,1280]{1,0:T(8,128)(2,1)S(1)} %collective-permute-done.4.refs_3_), channel_id=1, source_target_pairs={{0,2},{2,6},{6,10},{10,14},{14,12},{12,8},{8,4},{4,0},{1,3},{3,7},... | collective-permute-start | bytes 491528 | tf_op jit(solution)/shard_map/ppermute | solution.py:383
  30.1 6.5 %collective-permute-start.19 = (f32[256,512]{1,0:T(8,128)S(1)}, f32[256,512]{1,0:T(8,128)S(1)}, u32[]{:S(2)}, u32[]{:S(2)}) collective-permute-start(f32[256,512]{1,0:T(8,128)S(1)} %get-tuple-element.42), channel_id=1, source_target_pairs={{0,1},{1,0},{2,3},{3,2},{4,5},{5,4},{6,7},{7,6},{8,9},{9,8},{10,11... | collective-permute-start | bytes 1572872 | tf_op jit(solution)/shard_map/ppermute | solution.py:400
  31.6 4.0 %collective-permute-start.17 = (bf16[128,128]{1,0:T(8,128)(2,1)S(1)}, bf16[128,128]{1,0:T(8,128)(2,1)S(1)}, u32[]{:S(2)}, u32[]{:S(2)}) collective-permute-start(bf16[128,128]{1,0:T(8,128)(2,1)S(1)} %shard_map.88), channel_id=1, source_target_pairs={{0,16},{16,0},{1,17},{17,1},{2,18},{18,2},{3,19},{19,3},{4,20},{20... | collective-permute-start | bytes 98312 | tf_op jit(solution)/shard_map/ppermute | solution.py:406
  33.1 3.4 %collective-permute-start.18 = (bf16[128,128]{1,0:T(8,128)(2,1)S(1)}, bf16[128,128]{1,0:T(8,128)(2,1)S(1)}, u32[]{:S(2)}, u32[]{:S(2)}) collective-permute-start(bf16[128,128]{1,0:T(8,128)(2,1)S(1)} %shard_map.88), channel_id=1, source_target_pairs={{0,17},{1,16},{16,1},{17,0},{2,19},{3,18},{18,3},{19,2},{4,21},{5,... | collective-permute-start | bytes 98312 | tf_op jit(solution)/shard_map/ppermute | solution.py:407
  33.7 2.9 %collective-permute-start.15 = (f32[64,128]{1,0:T(8,128)S(1)}, f32[64,128]{1,0:T(8,128)S(1)}, u32[]{:S(2)}, u32[]{:S(2)}) collective-permute-start(f32[64,128]{1,0:T(8,128)S(1)} %get-tuple-element.36.top), channel_id=1, source_target_pairs={{0,1},{1,0},{2,3},{3,2},{4,5},{5,4},{6,7},{7,6},{8,9},{9,8},{10,11... | collective-permute-start | bytes 98312 | tf_op jit(solution)/shard_map/ppermute | solution.py:408
  34.4 2.2 %collective-permute-start.16 = (f32[64,128]{1,0:T(8,128)S(1)}, f32[64,128]{1,0:T(8,128)S(1)}, u32[]{:S(2)}, u32[]{:S(2)}) collective-permute-start(f32[64,128]{1,0:T(8,128)S(1)} %get-tuple-element.37.low), channel_id=1, source_target_pairs={{0,1},{1,0},{2,3},{3,2},{4,5},{5,4},{6,7},{7,6},{8,9},{9,8},{10,11... | collective-permute-start | bytes 98312 | tf_op jit(solution)/shard_map/ppermute | solution.py:408

commit v18 on v17

--- a/solution.py
+++ b/solution.py
@@ -204,7 +204,7 @@
     )(bounds)
 
 
-def base_kernel(rows_ref, weight_ref, near_ref, far_ref):
+def base_kernel(size, rows_ref, weight_ref, bounds_ref, near_ref, far_ref, mask_ref):
     width = near_ref.shape[1]
     core = lax.axis_index("tensor")
     for out_ref, side in ((near_ref, core), (far_ref, 1 - core)):
@@ -212,18 +212,22 @@
         out_ref[...] = jnp.dot(
             rows_ref[...], weight_ref[:, columns], preferred_element_type=F32
         )
-
-
-def base_call(rows, weight):
+    for group in range(mask_ref.shape[1] // size):
+        mask = group_mask(*own_ends(bounds_ref, group, size), (rows_ref.shape[0], size))
+        mask_ref[:, group * size : (group + 1) * size] = jnp.where(mask, 1.0, 0.0).astype(BF16)
+
+
+def base_call(rows, weight, bounds, size):
+    mask = jax.ShapeDtypeStruct((rows.shape[0], bounds.shape[1]), BF16)
     out = jax.ShapeDtypeStruct((rows.shape[0], weight.shape[1] // 2), F32)
     return pl.pallas_call(
-        base_kernel,
-        out_shape=(out, out),
-        in_specs=[VMEM] * 2,
-        out_specs=(VMEM,) * 2,
+        functools.partial(base_kernel, size),
+        out_shape=(out, out, mask),
+        in_specs=[VMEM] * 3,
+        out_specs=(VMEM,) * 3,
         compiler_params=params(),
         cost_estimate=HALF,
-    )(rows, weight)
+    )(rows, weight, bounds)
 
 
 def group_mask(low, high, shape):
@@ -320,7 +324,7 @@
     )(*operands)
 
 
-def final_kernel(bounds_ref, top, low, one_top, one_low, two, three, near_ref, far_ref, *refs):
+def final_kernel(mask_ref, top, low, one_top, one_low, three, two, near_ref, far_ref, *refs):
     factors, out_ref = refs[:-1], refs[-1]
     rank, width = factors[0].shape[0], out_ref.shape[1]
     begin = factors[0].shape[1] - width
@@ -331,11 +335,10 @@
     values = jnp.concatenate(
         [jnp.where(lane < rank, packed, turned), jnp.where(lane < rank, turned, packed)], axis=0
     )
-    wide = jnp.concatenate([values] * (GROUP // 2), axis=1)
+    wide = jnp.concatenate([values.astype(BF16)] * (GROUP // 2), axis=1)
     total = None
     for group in range(len(factors) // GROUP):
-        mask = group_mask(*own_ends(bounds_ref, group, GROUP * rank), wide.shape)
-        chosen = jnp.where(mask, wide, 0.0).astype(BF16)
+        chosen = wide * mask_ref[:, group * GROUP * rank : (group + 1) * GROUP * rank]
         factor = jnp.concatenate(
             [ref[:, begin:] for ref in factors[group * GROUP : (group + 1) * GROUP]], axis=0
         )
@@ -382,7 +385,7 @@
         seconds += [b, d]
     firsts.append(lax.ppermute(ahead[0], "batch", forward))
     seconds.append(lax.ppermute(behind[1], "batch", backward))
-    near, far = base_call(hidden, value_weight)
+    near, far, mask = base_call(hidden, value_weight, bounds, GROUP * rank)
     hidden, near, far = lax.optimization_barrier((hidden, near, far))
     other = lax.ppermute(to_other, "groups", swap)
 
@@ -403,11 +406,11 @@
     (theirs,) = rank_call((1,), late, depth, rows, (other,), bounds, pieces, (start_theirs,))
     mine = rank_call((0,), late, depth, rows, (hidden,), bounds, pieces, (start_mine,))
 
+    three = lax.ppermute(theirs, ("groups", "tensor"), [(0, 3), (1, 2), (2, 1), (3, 0)])
     two = lax.ppermute(theirs, "groups", swap)
-    three = lax.ppermute(theirs, ("groups", "tensor"), [(0, 3), (1, 2), (2, 1), (3, 0)])
     one = [lax.ppermute(part, "tensor", swap) for part in mine]
 
-    operands = [bounds, *mine, *one, two, three, near, far, *seconds]
+    operands = [mask, *mine, *one, three, two, near, far, *seconds]
     return pl.pallas_call(
         final_kernel,
         out_shape=jax.ShapeDtypeStruct((rows, width), BF16),

time: 37.9 us -> 37.8 us (level)
    ppermute x1, starting transfers between devices: 1.53 us -> 0.63 us  [per_device(): two = lax.ppermute(theirs, 'groups', swap)]
    ppermute x1, starting transfers between devices: 0.01 us -> 0.86 us  [per_device(): lax.ppermute(theirs, ('groups', 'tensor'), [(0, 3), (1, 2), (2, 1), (3, 0)])]
  transfers between devices with their start and end apart: 20 -> 20, of which waited for: 8 -> 7; matrix products, arithmetic and copies ran while one was open for 0% -> 0% of each run, Pallas kernels for 12% -> 12%
where the time goes in v18:
time: 37.8 us; the launch traced here: 37.6 us
  starting transfers between devices  19.2 us (51%)
  waiting for transfers between devices  11.5 us (30%)
  Pallas kernels  6.83 us (18%)
    ppermute x3, starting transfers between devices, per_device(): d = lax.ppermute(behind[1], 'batch', backward)  5.32 us
    ppermute x3, waiting for transfers between devices, per_device(): b = lax.ppermute(ahead[1], 'batch', forward)  3.51 us
    ppermute x3, starting transfers between devices, per_device(): b = lax.ppermute(ahead[1], 'batch', forward)  3.3 us
    ppermute x3, starting transfers between devices, per_device(): c = lax.ppermute(behind[0], 'batch', backward)  2.83 us
    ppermute x1, waiting for transfers between devices, per_device(): other = lax.ppermute(to_other, 'groups', swap)  2.61 us
    pallas_call x1, Pallas kernels, base_call(): pl.pallas_call(functools.partial(base_kernel, size), out_shape=(out, out,...  2.47 us
    ppermute x1, starting transfers between devices, per_device(): other = lax.ppermute(to_other, 'groups', swap)  2.03 us
    pallas_call x3, Pallas kernels, rank_call(): pl.pallas_call(functools.partial(rank_kernel, sides, groups, depth, last)...  1.84 us
  transfers between devices with their start and end apart: 20, of which 7 were waited for; matrix products, arithmetic and copies ran while one was open for 0% of the time, Pallas kernels for 12%

profile of v18, /device:TPU:0, one launch (start us, length us, event | category | flops | bytes accessed | tf_op | source)
XLA Modules:
  0.0 37.6 jit_solution(7851604068194977545)
XLA Ops:
  0.0 1.2 %shard_map.82 = (bf16[64,1280]{1,0:T(8,128)(2,1)S(1)}, bf16[64,1280]{1,0:T(8,128)(2,1)S(1)}, s32[8,512]{1,0:T(8,128)S(1)}) custom-call(bf16[64,4096]{1,0:T(8,128)(2,1)} %bitcast.6, bf16[64,512]{1,0:T(8,128)(2,1)} %bitcast.7, s32[1,4]{1,0:T(1,128)} %demand_ref.1, s32[1,4]{1,0:T(1,128)} %lengths_ref.1, s32[8]{0:T(128)} %holder_ref.1, ...), custom_call_target="tpu_custom_call" | custom-call | flops 8589934592 | bytes 16777216 | tf_op jit(solution)/shard_map/pallas_call | solution.py:137
  1.2 3.1 %collective-permute-start.7 = (bf16[64,1280]{1,0:T(8,128)(2,1)S(1)}, bf16[64,1280]{1,0:T(8,128)(2,1)S(1)}, u32[]{:S(2)}, u32[]{:S(2)}) collective-permute-start(bf16[64,1280]{1,0:T(8,128)(2,1)S(1)} %get-tuple-element.35.refs_7_.refs_0_), channel_id=1, source_target_pairs={{2,0},{6,2},{10,6},{14,10},{12,14},{8,12},{4,8},{0,4},{3,1},{7,3},... | collective-permute-start | bytes 491528 | tf_op jit(solution)/shard_map/ppermute | solution.py:380
  4.3 0.0 collective-permute-start.2
  4.3 0.0 copy-done
  4.3 0.3 shard_map.83
  4.6 2.0 %collective-permute-start.14 = (bf16[4112,128]{1,0:T(8,128)(2,1)S(1)}, bf16[4112,128]{1,0:T(8,128)(2,1)S(1)}, u32[]{:S(2)}, u32[]{:S(2)}) collective-permute-start(bf16[4112,128]{1,0:T(8,128)(2,1)S(1)} %get-tuple-element.36), channel_id=1, source_target_pairs={{0,16},{16,0},{1,17},{17,1},{2,18},{18,2},{3,19},{19,3},{4,20},{20... | collective-permute-start | bytes 3158024 | tf_op jit(solution)/shard_map/ppermute | solution.py:390
  6.6 1.5 %collective-permute-start.9 = (bf16[64,1280]{1,0:T(8,128)(2,1)S(1)}, bf16[64,1280]{1,0:T(8,128)(2,1)S(1)}, u32[]{:S(2)}, u32[]{:S(2)}) collective-permute-start(bf16[64,1280]{1,0:T(8,128)(2,1)S(1)} %get-tuple-element.35.refs_7_.refs_0_), channel_id=1, source_target_pairs={{0,2},{2,6},{6,10},{10,14},{14,12},{12,8},{8,4},{4,0},{1,3},{3,7},... | collective-permute-start | bytes 491528 | tf_op jit(solution)/shard_map/ppermute | solution.py:381
  8.1 0.5 %collective-permute-start = (bf16[64,1280]{1,0:T(8,128)(2,1)S(1)}, bf16[64,1280]{1,0:T(8,128)(2,1)S(1)}, u32[]{:S(2)}, u32[]{:S(2)}) collective-permute-start(bf16[64,1280]{1,0:T(8,128)(2,1)S(1)} %get-tuple-element.34.refs_3_), channel_id=1, source_target_pairs={{2,0},{6,2},{10,6},{14,10},{12,14},{8,12},{4,8},{0,4},{3,1},{7,3},... | collective-permute-start | bytes 491528 | tf_op jit(solution)/shard_map/ppermute | solution.py:382
  8.6 0.0 collective-permute-done.7.refs_9_.refs_2_
  8.6 1.8 %collective-permute-start.8 = (bf16[64,1280]{1,0:T(8,128)(2,1)S(1)}, bf16[64,1280]{1,0:T(8,128)(2,1)S(1)}, u32[]{:S(2)}, u32[]{:S(2)}) collective-permute-start(bf16[64,1280]{1,0:T(8,128)(2,1)S(1)} %collective-permute-done.7.refs_9_.refs_2_), channel_id=1, source_target_pairs={{2,0},{6,2},{10,6},{14,10},{12,14},{8,12},{4,8},{0,4},{3,1},{7,3},... | collective-permute-start | bytes 491528 | tf_op jit(solution)/shard_map/ppermute | solution.py:380
  10.4 1.0 %collective-permute-done.2.refs_4_ = bf16[64,1280]{1,0:T(8,128)(2,1)S(1)} collective-permute-done((bf16[64,1280]{1,0:T(8,128)(2,1)S(1)}, bf16[64,1280]{1,0:T(8,128)(2,1)S(1)}, u32[]{:S(2)}, u32[]{:S(2)}) %collective-permute-start.2) | collective-permute-done | bytes 163872 | tf_op jit(solution)/shard_map/ppermute | solution.py:379
  11.4 0.0 collective-permute-start.3
  11.4 3.5 %collective-permute-done.9.refs_8_.refs_1_ = bf16[64,1280]{1,0:T(8,128)(2,1)S(1)} collective-permute-done((bf16[64,1280]{1,0:T(8,128)(2,1)S(1)}, bf16[64,1280]{1,0:T(8,128)(2,1)S(1)}, u32[]{:S(2)}, u32[]{:S(2)}) %collective-permute-start.9) | collective-permute-done | bytes 163872 | tf_op jit(solution)/shard_map/ppermute | solution.py:381
  14.9 0.3 collective-permute-start.10
  15.2 0.0 collective-permute-done.refs_5_
  15.2 1.7 %collective-permute-start.1 = (bf16[64,1280]{1,0:T(8,128)(2,1)S(1)}, bf16[64,1280]{1,0:T(8,128)(2,1)S(1)}, u32[]{:S(2)}, u32[]{:S(2)}) collective-permute-start(bf16[64,1280]{1,0:T(8,128)(2,1)S(1)} %collective-permute-done.refs_5_), channel_id=1, source_target_pairs={{2,0},{6,2},{10,6},{14,10},{12,14},{8,12},{4,8},{0,4},{3,1},{7,3},... | collective-permute-start | bytes 491528 | tf_op jit(solution)/shard_map/ppermute | solution.py:382
  16.9 1.1 %collective-permute-done.8.refs_6_.refs_4_ = bf16[64,1280]{1,0:T(8,128)(2,1)S(1)} collective-permute-done((bf16[64,1280]{1,0:T(8,128)(2,1)S(1)}, bf16[64,1280]{1,0:T(8,128)(2,1)S(1)}, u32[]{:S(2)}, u32[]{:S(2)}) %collective-permute-start.8) | collective-permute-done | bytes 163872 | tf_op jit(solution)/shard_map/ppermute | solution.py:380
  18.1 0.4 %collective-permute-start.12 = (bf16[64,1280]{1,0:T(8,128)(2,1)S(1)}, bf16[64,1280]{1,0:T(8,128)(2,1)S(1)}, u32[]{:S(2)}, u32[]{:S(2)}) collective-permute-start(bf16[64,1280]{1,0:T(8,128)(2,1)S(1)} %collective-permute-done.8.refs_6_.refs_4_), channel_id=1, source_target_pairs={{2,0},{6,2},{10,6},{14,10},{12,14},{8,12},{4,8},{0,4},{3,1},{7,3},... | collective-permute-start | bytes 491528 | tf_op jit(solution)/shard_map/ppermute | solution.py:380
  18.5 0.0 collective-permute-done.3.refs_6_
  18.5 1.6 %collective-permute-start.4 = (bf16[64,1280]{1,0:T(8,128)(2,1)S(1)}, bf16[64,1280]{1,0:T(8,128)(2,1)S(1)}, u32[]{:S(2)}, u32[]{:S(2)}) collective-permute-start(bf16[64,1280]{1,0:T(8,128)(2,1)S(1)} %collective-permute-done.3.refs_6_), channel_id=1, source_target_pairs={{0,2},{2,6},{6,10},{10,14},{14,12},{12,8},{8,4},{4,0},{1,3},{3,7},... | collective-permute-start | bytes 491528 | tf_op jit(solution)/shard_map/ppermute | solution.py:379
  20.1 2.5 %shard_map.85 = (f32[256,512]{1,0:T(8,128)S(1)}, f32[256,512]{1,0:T(8,128)S(1)}, bf16[256,512]{1,0:T(8,128)(2,1)S(1)}) custom-call(bf16[256,4096]{1,0:T(8,128)(2,1)S(1)} %copy-done, bf16[4096,1024]{1,0:T(8,128)(2,1)S(1)} %bitcast.5, s32[8,512]{1,0:T(8,128)S(1)} %shard_map.84.bounds_ref.refs_2_.refs_1_), custom_call_target="tpu_custom_call" | custom-call | bytes 4194304 | tf_op jit(solution)/shard_map/pallas_call | solution.py:223
  22.6 0.0 collective-permute-done.10.refs_10_.refs_3_
  22.6 1.5 %collective-permute-start.11 = (bf16[64,1280]{1,0:T(8,128)(2,1)S(1)}, bf16[64,1280]{1,0:T(8,128)(2,1)S(1)}, u32[]{:S(2)}, u32[]{:S(2)}) collective-permute-start(bf16[64,1280]{1,0:T(8,128)(2,1)S(1)} %collective-permute-done.10.refs_10_.refs_3_), channel_id=1, source_target_pairs={{0,2},{2,6},{6,10},{10,14},{14,12},{12,8},{8,4},{4,0},{1,3},{3,7},... | collective-permute-start | bytes 491528 | tf_op jit(solution)/shard_map/ppermute | solution.py:381
  24.1 0.0 collective-permute-done.1.refs_2_
  24.1 0.6 %collective-permute-start.5 = (bf16[64,1280]{1,0:T(8,128)(2,1)S(1)}, bf16[64,1280]{1,0:T(8,128)(2,1)S(1)}, u32[]{:S(2)}, u32[]{:S(2)}) collective-permute-start(bf16[64,1280]{1,0:T(8,128)(2,1)S(1)} %collective-permute-done.1.refs_2_), channel_id=1, source_target_pairs={{2,0},{6,2},{10,6},{14,10},{12,14},{8,12},{4,8},{0,4},{3,1},{7,3},... | collective-permute-start | bytes 491528 | tf_op jit(solution)/shard_map/ppermute | solution.py:382
  24.7 0.0 collective-permute-done.12.refs_8_.refs_6_
  24.7 1.0 %collective-permute-start.13 = (bf16[64,1280]{1,0:T(8,128)(2,1)S(1)}, bf16[64,1280]{1,0:T(8,128)(2,1)S(1)}, u32[]{:S(2)}, u32[]{:S(2)}) collective-permute-start(bf16[64,1280]{1,0:T(8,128)(2,1)S(1)} %collective-permute-done.12.refs_8_.refs_6_), channel_id=1, source_target_pairs={{2,0},{6,2},{10,6},{14,10},{12,14},{8,12},{4,8},{0,4},{3,1},{7,3},... | collective-permute-start | bytes 491528 | tf_op jit(solution)/shard_map/ppermute | solution.py:387
  25.7 0.0 collective-permute-done.4.refs_3_
  25.7 1.0 %collective-permute-start.6 = (bf16[64,1280]{1,0:T(8,128)(2,1)S(1)}, bf16[64,1280]{1,0:T(8,128)(2,1)S(1)}, u32[]{:S(2)}, u32[]{:S(2)}) collective-permute-start(bf16[64,1280]{1,0:T(8,128)(2,1)S(1)} %collective-permute-done.4.refs_3_), channel_id=1, source_target_pairs={{0,2},{2,6},{6,10},{10,14},{14,12},{12,8},{8,4},{4,0},{1,3},{3,7},... | collective-permute-start | bytes 491528 | tf_op jit(solution)/shard_map/ppermute | solution.py:386
  26.7 2.6 %collective-permute-done.14.refs_1_.refs_0_ = bf16[4112,128]{1,0:T(8,128)(2,1)S(1)} collective-permute-done((bf16[4112,128]{1,0:T(8,128)(2,1)S(1)}, bf16[4112,128]{1,0:T(8,128)(2,1)S(1)}, u32[]{:S(2)}, u32[]{:S(2)}) %collective-permute-start.14) | collective-permute-done | bytes 1052704 | tf_op jit(solution)/shard_map/ppermute | solution.py:390
  29.3 0.7 %shard_map.86 = (f32[256,128]{1,0:T(8,128)S(1)}, f32[256,128]{1,0:T(8,128)S(1)}) custom-call(bf16[256,4096]{1,0:T(8,128)(2,1)S(1)} %copy-done, bf16[4112,128]{1,0:T(8,128)(2,1)S(1)} %collective-permute-done.14.refs_1_.refs_0_, s32[8,512]{1,0:T(8,128)S(1)} %shard_map.84.bounds_ref.refs_2_.refs_1_, bf16[64,1280]{1,0:T(8,128)(2,1)S(1)} %get-tuple-element.34.refs_3_, ...), custom_call_target="tpu_custom_call" | custom-call | flops 8589934592 | bytes 16777216 | tf_op jit(solution)/shard_map/pallas_call | solution.py:317
  30.1 0.1 collective-permute-start.19
  30.2 0.0 collective-permute-done.11.refs_7_.refs_5_
  30.2 0.0 collective-permute-done.5.refs_4_
  30.2 1.0 %collective-permute-done.13.refs_9_.refs_7_ = bf16[64,1280]{1,0:T(8,128)(2,1)S(1)} collective-permute-done((bf16[64,1280]{1,0:T(8,128)(2,1)S(1)}, bf16[64,1280]{1,0:T(8,128)(2,1)S(1)}, u32[]{:S(2)}, u32[]{:S(2)}) %collective-permute-start.13) | collective-permute-done | bytes 163872 | tf_op jit(solution)/shard_map/ppermute | solution.py:387
  31.2 0.0 collective-permute-done.6.refs_5_
  31.2 0.5 %shard_map.88 = bf16[128,128]{1,0:T(8,128)(2,1)S(1)} custom-call(bf16[4112,128]{1,0:T(8,128)(2,1)S(1)} %collective-permute-done.14.refs_1_.refs_0_, s32[8,512]{1,0:T(8,128)S(1)} %shard_map.84.bounds_ref.refs_2_.refs_1_, bf16[64,1280]{1,0:T(8,128)(2,1)S(1)} %collective-permute-done.1.refs_2_, bf16[64,1280]{1,0:T(8,128)(2,1)S(1)} %collective-permute-done.4.refs_3_, ...), custom_call_target="tpu_custom_call" | custom-call | flops 8589934592 | bytes 16777216 | tf_op jit(solution)/shard_map/pallas_call | solution.py:317
  31.7 0.9 %collective-permute-start.17 = (bf16[128,128]{1,0:T(8,128)(2,1)S(1)}, bf16[128,128]{1,0:T(8,128)(2,1)S(1)}, u32[]{:S(2)}, u32[]{:S(2)}) collective-permute-start(bf16[128,128]{1,0:T(8,128)(2,1)S(1)} %shard_map.88), channel_id=1, source_target_pairs={{0,17},{1,16},{16,1},{17,0},{2,19},{3,18},{18,3},{19,2},{4,21},{5,... | collective-permute-start | bytes 98312 | tf_op jit(solution)/shard_map/ppermute | solution.py:409
  32.6 0.6 %collective-permute-start.18 = (bf16[128,128]{1,0:T(8,128)(2,1)S(1)}, bf16[128,128]{1,0:T(8,128)(2,1)S(1)}, u32[]{:S(2)}, u32[]{:S(2)}) collective-permute-start(bf16[128,128]{1,0:T(8,128)(2,1)S(1)} %shard_map.88), channel_id=1, source_target_pairs={{0,16},{16,0},{1,17},{17,1},{2,18},{18,2},{3,19},{19,3},{4,20},{20... | collective-permute-start | bytes 98312 | tf_op jit(solution)/shard_map/ppermute | solution.py:410
  33.2 0.5 %shard_map.87 = (f32[64,128]{1,0:T(8,128)S(1)}, f32[64,128]{1,0:T(8,128)S(1)}) custom-call(bf16[256,4096]{1,0:T(8,128)(2,1)S(1)} %copy-done, s32[8,512]{1,0:T(8,128)S(1)} %shard_map.84.bounds_ref.refs_2_.refs_1_, bf16[64,1280]{1,0:T(8,128)(2,1)S(1)} %collective-permute-done.1.refs_2_, bf16[64,1280]{1,0:T(8,128)(2,1)S(1)} %collective-permute-done.4.refs_3_, ...), custom_call_target="tpu_custom_call" | custom-call | bytes 4194304 | tf_op jit(solution)/shard_map/pallas_call | solution.py:317
  33.8 0.5 %collective-permute-start.15 = (f32[64,128]{1,0:T(8,128)S(1)}, f32[64,128]{1,0:T(8,128)S(1)}, u32[]{:S(2)}, u32[]{:S(2)}) collective-permute-start(f32[64,128]{1,0:T(8,128)S(1)} %get-tuple-element.38.top), channel_id=1, source_target_pairs={{0,1},{1,0},{2,3},{3,2},{4,5},{5,4},{6,7},{7,6},{8,9},{9,8},{10,11... | collective-permute-start | bytes 98312 | tf_op jit(solution)/shard_map/ppermute | solution.py:411
  34.3 0.1 collective-permute-start.16
  34.4 1.0 %collective-permute-done.17.three = bf16[128,128]{1,0:T(8,128)(2,1)S(1)} collective-permute-done((bf16[128,128]{1,0:T(8,128)(2,1)S(1)}, bf16[128,128]{1,0:T(8,128)(2,1)S(1)}, u32[]{:S(2)}, u32[]{:S(2)}) %collective-permute-start.17) | collective-permute-done | bytes 32800 | tf_op jit(solution)/shard_map/ppermute | solution.py:409
  35.4 1.2 %collective-permute-done.18.two = bf16[128,128]{1,0:T(8,128)(2,1)S(1)} collective-permute-done((bf16[128,128]{1,0:T(8,128)(2,1)S(1)}, bf16[128,128]{1,0:T(8,128)(2,1)S(1)}, u32[]{:S(2)}, u32[]{:S(2)}) %collective-permute-start.18) | collective-permute-done | bytes 32800 | tf_op jit(solution)/shard_map/ppermute | solution.py:410
  36.5 0.0 collective-permute-done.15.one_top
  36.6 0.0 collective-permute-done.16.one_low
  36.6 0.0 collective-permute-done.19.far_ref
  36.6 1.1 %shard_map.89 = bf16[256,512]{1,0:T(8,128)(2,1)} custom-call(bf16[256,512]{1,0:T(8,128)(2,1)S(1)} %get-tuple-element.30.mask_ref, f32[64,128]{1,0:T(8,128)S(1)} %get-tuple-element.38.top, f32[64,128]{1,0:T(8,128)S(1)} %get-tuple-element.39.low, f32[64,128]{1,0:T(8,128)S(1)} %collective-permute-done.15.one_top, ...), custom_call_target="tpu_custom_call" | custom-call | tf_op jit(solution)/shard_map/pallas_call | solution.py:414
  (7 shorter events, 0.0 us)
Async XLA Ops:
  0.0 4.3 %copy-start = (bf16[256,4096]{1,0:T(8,128)(2,1)S(1)}, bf16[256,4096]{1,0:T(8,128)(2,1)}, u32[]{:S(2)}) copy-start(bf16[256,4096]{1,0:T(8,128)(2,1)} %refs_0_.1) | copy-start | bytes 6291460
  1.2 7.4 %collective-permute-start.7 = (bf16[64,1280]{1,0:T(8,128)(2,1)S(1)}, bf16[64,1280]{1,0:T(8,128)(2,1)S(1)}, u32[]{:S(2)}, u32[]{:S(2)}) collective-permute-start(bf16[64,1280]{1,0:T(8,128)(2,1)S(1)} %get-tuple-element.35.refs_7_.refs_0_), channel_id=1, source_target_pairs={{2,0},{6,2},{10,6},{14,10},{12,14},{8,12},{4,8},{0,4},{3,1},{7,3},... | collective-permute-start | bytes 491528 | tf_op jit(solution)/shard_map/ppermute | solution.py:380
  4.3 7.1 %collective-permute-start.2 = (bf16[64,1280]{1,0:T(8,128)(2,1)S(1)}, bf16[64,1280]{1,0:T(8,128)(2,1)S(1)}, u32[]{:S(2)}, u32[]{:S(2)}) collective-permute-start(bf16[64,1280]{1,0:T(8,128)(2,1)S(1)} %get-tuple-element.34.refs_3_), channel_id=1, source_target_pairs={{0,2},{2,6},{6,10},{10,14},{14,12},{12,8},{8,4},{4,0},{1,3},{3,7},... | collective-permute-start | bytes 491528 | tf_op jit(solution)/shard_map/ppermute | solution.py:379
  4.6 24.8 %collective-permute-start.14 = (bf16[4112,128]{1,0:T(8,128)(2,1)S(1)}, bf16[4112,128]{1,0:T(8,128)(2,1)S(1)}, u32[]{:S(2)}, u32[]{:S(2)}) collective-permute-start(bf16[4112,128]{1,0:T(8,128)(2,1)S(1)} %get-tuple-element.36), channel_id=1, source_target_pairs={{0,16},{16,0},{1,17},{17,1},{2,18},{18,2},{3,19},{19,3},{4,20},{20... | collective-permute-start | bytes 3158024 | tf_op jit(solution)/shard_map/ppermute | solution.py:390
  6.6 13.5 %slice-start = ((s8[8388608]{0:T(1024)(128)(4,1)}), s8[4194304]{0:T(1024)(128)(4,1)S(1)}, s32[]{:S(2)}) async-start(s8[8388608]{0:T(1024)(128)(4,1)} %bitcast.4), calls=%async_computation | async-start | bytes 8388608
  6.6 13.5 %slice-start.1 = ((s8[8388608]{0:T(1024)(128)(4,1)}), s8[4194304]{0:T(1024)(128)(4,1)S(1)}, s32[]{:S(2)}) async-start(s8[8388608]{0:T(1024)(128)(4,1)} %bitcast.4), calls=%async_computation.1 | async-start | bytes 8388608
  6.6 8.3 %collective-permute-start.9 = (bf16[64,1280]{1,0:T(8,128)(2,1)S(1)}, bf16[64,1280]{1,0:T(8,128)(2,1)S(1)}, u32[]{:S(2)}, u32[]{:S(2)}) collective-permute-start(bf16[64,1280]{1,0:T(8,128)(2,1)S(1)} %get-tuple-element.35.refs_7_.refs_0_), channel_id=1, source_target_pairs={{0,2},{2,6},{6,10},{10,14},{14,12},{12,8},{8,4},{4,0},{1,3},{3,7},... | collective-permute-start | bytes 491528 | tf_op jit(solution)/shard_map/ppermute | solution.py:381
  8.1 7.1 %collective-permute-start = (bf16[64,1280]{1,0:T(8,128)(2,1)S(1)}, bf16[64,1280]{1,0:T(8,128)(2,1)S(1)}, u32[]{:S(2)}, u32[]{:S(2)}) collective-permute-start(bf16[64,1280]{1,0:T(8,128)(2,1)S(1)} %get-tuple-element.34.refs_3_), channel_id=1, source_target_pairs={{2,0},{6,2},{10,6},{14,10},{12,14},{8,12},{4,8},{0,4},{3,1},{7,3},... | collective-permute-start | bytes 491528 | tf_op jit(solution)/shard_map/ppermute | solution.py:382
  8.6 9.4 %collective-permute-start.8 = (bf16[64,1280]{1,0:T(8,128)(2,1)S(1)}, bf16[64,1280]{1,0:T(8,128)(2,1)S(1)}, u32[]{:S(2)}, u32[]{:S(2)}) collective-permute-start(bf16[64,1280]{1,0:T(8,128)(2,1)S(1)} %collective-permute-done.7.refs_9_.refs_2_), channel_id=1, source_target_pairs={{2,0},{6,2},{10,6},{14,10},{12,14},{8,12},{4,8},{0,4},{3,1},{7,3},... | collective-permute-start | bytes 491528 | tf_op jit(solution)/shard_map/ppermute | solution.py:380
  11.4 7.1 %collective-permute-start.3 = (bf16[64,1280]{1,0:T(8,128)(2,1)S(1)}, bf16[64,1280]{1,0:T(8,128)(2,1)S(1)}, u32[]{:S(2)}, u32[]{:S(2)}) collective-permute-start(bf16[64,1280]{1,0:T(8,128)(2,1)S(1)} %collective-permute-done.2.refs_4_), channel_id=1, source_target_pairs={{0,2},{2,6},{6,10},{10,14},{14,12},{12,8},{8,4},{4,0},{1,3},{3,7},... | collective-permute-start | bytes 491528 | tf_op jit(solution)/shard_map/ppermute | solution.py:379
  14.9 7.7 %collective-permute-start.10 = (bf16[64,1280]{1,0:T(8,128)(2,1)S(1)}, bf16[64,1280]{1,0:T(8,128)(2,1)S(1)}, u32[]{:S(2)}, u32[]{:S(2)}) collective-permute-start(bf16[64,1280]{1,0:T(8,128)(2,1)S(1)} %collective-permute-done.9.refs_8_.refs_1_), channel_id=1, source_target_pairs={{0,2},{2,6},{6,10},{10,14},{14,12},{12,8},{8,4},{4,0},{1,3},{3,7},... | collective-permute-start | bytes 491528 | tf_op jit(solution)/shard_map/ppermute | solution.py:381
  15.2 8.9 %collective-permute-start.1 = (bf16[64,1280]{1,0:T(8,128)(2,1)S(1)}, bf16[64,1280]{1,0:T(8,128)(2,1)S(1)}, u32[]{:S(2)}, u32[]{:S(2)}) collective-permute-start(bf16[64,1280]{1,0:T(8,128)(2,1)S(1)} %collective-permute-done.refs_5_), channel_id=1, source_target_pairs={{2,0},{6,2},{10,6},{14,10},{12,14},{8,12},{4,8},{0,4},{3,1},{7,3},... | collective-permute-start | bytes 491528 | tf_op jit(solution)/shard_map/ppermute | solution.py:382
  18.1 6.6 %collective-permute-start.12 = (bf16[64,1280]{1,0:T(8,128)(2,1)S(1)}, bf16[64,1280]{1,0:T(8,128)(2,1)S(1)}, u32[]{:S(2)}, u32[]{:S(2)}) collective-permute-start(bf16[64,1280]{1,0:T(8,128)(2,1)S(1)} %collective-permute-done.8.refs_6_.refs_4_), channel_id=1, source_target_pairs={{2,0},{6,2},{10,6},{14,10},{12,14},{8,12},{4,8},{0,4},{3,1},{7,3},... | collective-permute-start | bytes 491528 | tf_op jit(solution)/shard_map/ppermute | solution.py:380
  18.5 7.1 %collective-permute-start.4 = (bf16[64,1280]{1,0:T(8,128)(2,1)S(1)}, bf16[64,1280]{1,0:T(8,128)(2,1)S(1)}, u32[]{:S(2)}, u32[]{:S(2)}) collective-permute-start(bf16[64,1280]{1,0:T(8,128)(2,1)S(1)} %collective-permute-done.3.refs_6_), channel_id=1, source_target_pairs={{0,2},{2,6},{6,10},{10,14},{14,12},{12,8},{8,4},{4,0},{1,3},{3,7},... | collective-permute-start | bytes 491528 | tf_op jit(solution)/shard_map/ppermute | solution.py:379
  22.6 7.6 %collective-permute-start.11 = (bf16[64,1280]{1,0:T(8,128)(2,1)S(1)}, bf16[64,1280]{1,0:T(8,128)(2,1)S(1)}, u32[]{:S(2)}, u32[]{:S(2)}) collective-permute-start(bf16[64,1280]{1,0:T(8,128)(2,1)S(1)} %collective-permute-done.10.refs_10_.refs_3_), channel_id=1, source_target_pairs={{0,2},{2,6},{6,10},{10,14},{14,12},{12,8},{8,4},{4,0},{1,3},{3,7},... | collective-permute-start | bytes 491528 | tf_op jit(solution)/shard_map/ppermute | solution.py:381
  24.1 6.1 %collective-permute-start.5 = (bf16[64,1280]{1,0:T(8,128)(2,1)S(1)}, bf16[64,1280]{1,0:T(8,128)(2,1)S(1)}, u32[]{:S(2)}, u32[]{:S(2)}) collective-permute-start(bf16[64,1280]{1,0:T(8,128)(2,1)S(1)} %collective-permute-done.1.refs_2_), channel_id=1, source_target_pairs={{2,0},{6,2},{10,6},{14,10},{12,14},{8,12},{4,8},{0,4},{3,1},{7,3},... | collective-permute-start | bytes 491528 | tf_op jit(solution)/shard_map/ppermute | solution.py:382
  24.7 6.5 %collective-permute-start.13 = (bf16[64,1280]{1,0:T(8,128)(2,1)S(1)}, bf16[64,1280]{1,0:T(8,128)(2,1)S(1)}, u32[]{:S(2)}, u32[]{:S(2)}) collective-permute-start(bf16[64,1280]{1,0:T(8,128)(2,1)S(1)} %collective-permute-done.12.refs_8_.refs_6_), channel_id=1, source_target_pairs={{2,0},{6,2},{10,6},{14,10},{12,14},{8,12},{4,8},{0,4},{3,1},{7,3},... | collective-permute-start | bytes 491528 | tf_op jit(solution)/shard_map/ppermute | solution.py:387
  25.7 5.5 %collective-permute-start.6 = (bf16[64,1280]{1,0:T(8,128)(2,1)S(1)}, bf16[64,1280]{1,0:T(8,128)(2,1)S(1)}, u32[]{:S(2)}, u32[]{:S(2)}) collective-permute-start(bf16[64,1280]{1,0:T(8,128)(2,1)S(1)} %collective-permute-done.4.refs_3_), channel_id=1, source_target_pairs={{0,2},{2,6},{6,10},{10,14},{14,12},{12,8},{8,4},{4,0},{1,3},{3,7},... | collective-permute-start | bytes 491528 | tf_op jit(solution)/shard_map/ppermute | solution.py:386
  30.1 6.5 %collective-permute-start.19 = (f32[256,512]{1,0:T(8,128)S(1)}, f32[256,512]{1,0:T(8,128)S(1)}, u32[]{:S(2)}, u32[]{:S(2)}) collective-permute-start(f32[256,512]{1,0:T(8,128)S(1)} %get-tuple-element.44), channel_id=1, source_target_pairs={{0,1},{1,0},{2,3},{3,2},{4,5},{5,4},{6,7},{7,6},{8,9},{9,8},{10,11... | collective-permute-start | bytes 1572872 | tf_op jit(solution)/shard_map/ppermute | solution.py:403
  31.7 3.7 %collective-permute-start.17 = (bf16[128,128]{1,0:T(8,128)(2,1)S(1)}, bf16[128,128]{1,0:T(8,128)(2,1)S(1)}, u32[]{:S(2)}, u32[]{:S(2)}) collective-permute-start(bf16[128,128]{1,0:T(8,128)(2,1)S(1)} %shard_map.88), channel_id=1, source_target_pairs={{0,17},{1,16},{16,1},{17,0},{2,19},{3,18},{18,3},{19,2},{4,21},{5,... | collective-permute-start | bytes 98312 | tf_op jit(solution)/shard_map/ppermute | solution.py:409
  32.6 4.0 %collective-permute-start.18 = (bf16[128,128]{1,0:T(8,128)(2,1)S(1)}, bf16[128,128]{1,0:T(8,128)(2,1)S(1)}, u32[]{:S(2)}, u32[]{:S(2)}) collective-permute-start(bf16[128,128]{1,0:T(8,128)(2,1)S(1)} %shard_map.88), channel_id=1, source_target_pairs={{0,16},{16,0},{1,17},{17,1},{2,18},{18,2},{3,19},{19,3},{4,20},{20... | collective-permute-start | bytes 98312 | tf_op jit(solution)/shard_map/ppermute | solution.py:410
  33.8 2.8 %collective-permute-start.15 = (f32[64,128]{1,0:T(8,128)S(1)}, f32[64,128]{1,0:T(8,128)S(1)}, u32[]{:S(2)}, u32[]{:S(2)}) collective-permute-start(f32[64,128]{1,0:T(8,128)S(1)} %get-tuple-element.38.top), channel_id=1, source_target_pairs={{0,1},{1,0},{2,3},{3,2},{4,5},{5,4},{6,7},{7,6},{8,9},{9,8},{10,11... | collective-permute-start | bytes 98312 | tf_op jit(solution)/shard_map/ppermute | solution.py:411
  34.3 2.3 %collective-permute-start.16 = (f32[64,128]{1,0:T(8,128)S(1)}, f32[64,128]{1,0:T(8,128)S(1)}, u32[]{:S(2)}, u32[]{:S(2)}) collective-permute-start(f32[64,128]{1,0:T(8,128)S(1)} %get-tuple-element.39.low), channel_id=1, source_target_pairs={{0,1},{1,0},{2,3},{3,2},{4,5},{5,4},{6,7},{7,6},{8,9},{9,8},{10,11... | collective-permute-start | bytes 98312 | tf_op jit(solution)/shard_map/ppermute | solution.py:411

commit v19 on v18

--- a/solution.py
+++ b/solution.py
@@ -310,9 +310,9 @@
     if not last:
         out = (jax.ShapeDtypeStruct((count, 2 * rank), F32),) * len(sides)
     elif sides == (1,):
-        out = (jax.ShapeDtypeStruct((count // 2, 2 * rank), BF16),)
+        out = (jax.ShapeDtypeStruct((count // 2, 2 * rank), F32),)
     else:
-        out = (jax.ShapeDtypeStruct((count // 4, 2 * rank), F32),) * 2
+        out = (jax.ShapeDtypeStruct((count // 2, 2 * rank), F32),)
     operands = [*rows, bounds, *pieces, *starts]
     return pl.pallas_call(
         functools.partial(rank_kernel, sides, groups, depth, last),
@@ -324,12 +324,11 @@
     )(*operands)
 
 
-def final_kernel(mask_ref, top, low, one_top, one_low, three, two, near_ref, far_ref, *refs):
+def final_kernel(mask_ref, mine, one, three, two, near_ref, far_ref, *refs):
     factors, out_ref = refs[:-1], refs[-1]
     rank, width = factors[0].shape[0], out_ref.shape[1]
     begin = factors[0].shape[1] - width
-    here = jnp.concatenate([top[...] + one_top[...], low[...] + one_low[...]], axis=0)
-    packed = here + (two[...].astype(F32) + three[...].astype(F32))
+    packed = (mine[...] + one[...]) + (two[...] + three[...])
     turned = pltpu.roll(packed, rank, 1)
     lane = lax.broadcasted_iota(I32, packed.shape, 1)
     values = jnp.concatenate(

time: 37.8 us -> 38.7 us (1.024)
  waiting for transfers between devices: 11.5 us -> 12.5 us
    ppermute x1, waiting for transfers between devices: 1.02 us -> 1.8 us  [per_device(): lax.ppermute(theirs, ('groups', 'tensor'), [(0, 3), (1, 2), (2, 1), (3, 0)])]
  transfers between devices with their start and end apart: 20 -> 19, of which waited for: 7 -> 7; matrix products, arithmetic and copies ran while one was open for 0% -> 0% of each run, Pallas kernels for 12% -> 12%
where the time goes in v19:
time: 38.7 us; the launch traced here: 38.6 us
  starting transfers between devices  19.1 us (49%)
  waiting for transfers between devices  12.5 us (32%)
  Pallas kernels  6.83 us (18%)
    ppermute x3, starting transfers between devices, per_device(): d = lax.ppermute(behind[1], 'batch', backward)  5.32 us
    ppermute x3, waiting for transfers between devices, per_device(): b = lax.ppermute(ahead[1], 'batch', forward)  3.51 us
    ppermute x3, starting transfers between devices, per_device(): b = lax.ppermute(ahead[1], 'batch', forward)  3.3 us
    ppermute x3, starting transfers between devices, per_device(): c = lax.ppermute(behind[0], 'batch', backward)  2.83 us
    ppermute x1, waiting for transfers between devices, per_device(): other = lax.ppermute(to_other, 'groups', swap)  2.61 us
    pallas_call x1, Pallas kernels, base_call(): pl.pallas_call(functools.partial(base_kernel, size), out_shape=(out, out,...  2.47 us
    ppermute x1, starting transfers between devices, per_device(): other = lax.ppermute(to_other, 'groups', swap)  2.03 us
    pallas_call x3, Pallas kernels, rank_call(): pl.pallas_call(functools.partial(rank_kernel, sides, groups, depth, last)...  1.84 us
  transfers between devices with their start and end apart: 19, of which 7 were waited for; matrix products, arithmetic and copies ran while one was open for 0% of the time, Pallas kernels for 12%

profile of v19, /device:TPU:0, one launch (start us, length us, event | category | flops | bytes accessed | tf_op | source)
XLA Modules:
  0.0 38.6 jit_solution(1088764960338746154)
XLA Ops:
  0.0 1.2 %shard_map.82 = (bf16[64,1280]{1,0:T(8,128)(2,1)S(1)}, bf16[64,1280]{1,0:T(8,128)(2,1)S(1)}, s32[8,512]{1,0:T(8,128)S(1)}) custom-call(bf16[64,4096]{1,0:T(8,128)(2,1)} %bitcast.6, bf16[64,512]{1,0:T(8,128)(2,1)} %bitcast.7, s32[1,4]{1,0:T(1,128)} %demand_ref.1, s32[1,4]{1,0:T(1,128)} %lengths_ref.1, s32[8]{0:T(128)} %holder_ref.1, ...), custom_call_target="tpu_custom_call" | custom-call | flops 8589934592 | bytes 16777216 | tf_op jit(solution)/shard_map/pallas_call | solution.py:137
  1.2 3.1 %collective-permute-start.7 = (bf16[64,1280]{1,0:T(8,128)(2,1)S(1)}, bf16[64,1280]{1,0:T(8,128)(2,1)S(1)}, u32[]{:S(2)}, u32[]{:S(2)}) collective-permute-start(bf16[64,1280]{1,0:T(8,128)(2,1)S(1)} %get-tuple-element.33.refs_7_.refs_0_), channel_id=1, source_target_pairs={{2,0},{6,2},{10,6},{14,10},{12,14},{8,12},{4,8},{0,4},{3,1},{7,3},... | collective-permute-start | bytes 491528 | tf_op jit(solution)/shard_map/ppermute | solution.py:379
  4.3 0.0 collective-permute-start.2
  4.3 0.0 copy-done
  4.3 0.3 shard_map.83
  4.6 2.0 %collective-permute-start.14 = (bf16[4112,128]{1,0:T(8,128)(2,1)S(1)}, bf16[4112,128]{1,0:T(8,128)(2,1)S(1)}, u32[]{:S(2)}, u32[]{:S(2)}) collective-permute-start(bf16[4112,128]{1,0:T(8,128)(2,1)S(1)} %get-tuple-element.34), channel_id=1, source_target_pairs={{0,16},{16,0},{1,17},{17,1},{2,18},{18,2},{3,19},{19,3},{4,20},{20... | collective-permute-start | bytes 3158024 | tf_op jit(solution)/shard_map/ppermute | solution.py:389
  6.6 1.5 %collective-permute-start.9 = (bf16[64,1280]{1,0:T(8,128)(2,1)S(1)}, bf16[64,1280]{1,0:T(8,128)(2,1)S(1)}, u32[]{:S(2)}, u32[]{:S(2)}) collective-permute-start(bf16[64,1280]{1,0:T(8,128)(2,1)S(1)} %get-tuple-element.33.refs_7_.refs_0_), channel_id=1, source_target_pairs={{0,2},{2,6},{6,10},{10,14},{14,12},{12,8},{8,4},{4,0},{1,3},{3,7},... | collective-permute-start | bytes 491528 | tf_op jit(solution)/shard_map/ppermute | solution.py:380
  8.1 0.5 %collective-permute-start = (bf16[64,1280]{1,0:T(8,128)(2,1)S(1)}, bf16[64,1280]{1,0:T(8,128)(2,1)S(1)}, u32[]{:S(2)}, u32[]{:S(2)}) collective-permute-start(bf16[64,1280]{1,0:T(8,128)(2,1)S(1)} %get-tuple-element.32.refs_3_), channel_id=1, source_target_pairs={{2,0},{6,2},{10,6},{14,10},{12,14},{8,12},{4,8},{0,4},{3,1},{7,3},... | collective-permute-start | bytes 491528 | tf_op jit(solution)/shard_map/ppermute | solution.py:381
  8.6 0.0 collective-permute-done.7.refs_9_.refs_2_
  8.6 1.8 %collective-permute-start.8 = (bf16[64,1280]{1,0:T(8,128)(2,1)S(1)}, bf16[64,1280]{1,0:T(8,128)(2,1)S(1)}, u32[]{:S(2)}, u32[]{:S(2)}) collective-permute-start(bf16[64,1280]{1,0:T(8,128)(2,1)S(1)} %collective-permute-done.7.refs_9_.refs_2_), channel_id=1, source_target_pairs={{2,0},{6,2},{10,6},{14,10},{12,14},{8,12},{4,8},{0,4},{3,1},{7,3},... | collective-permute-start | bytes 491528 | tf_op jit(solution)/shard_map/ppermute | solution.py:379
  10.4 1.0 %collective-permute-done.2.refs_4_ = bf16[64,1280]{1,0:T(8,128)(2,1)S(1)} collective-permute-done((bf16[64,1280]{1,0:T(8,128)(2,1)S(1)}, bf16[64,1280]{1,0:T(8,128)(2,1)S(1)}, u32[]{:S(2)}, u32[]{:S(2)}) %collective-permute-start.2) | collective-permute-done | bytes 163872 | tf_op jit(solution)/shard_map/ppermute | solution.py:378
  11.4 0.0 collective-permute-start.3
  11.4 3.5 %collective-permute-done.9.refs_8_.refs_1_ = bf16[64,1280]{1,0:T(8,128)(2,1)S(1)} collective-permute-done((bf16[64,1280]{1,0:T(8,128)(2,1)S(1)}, bf16[64,1280]{1,0:T(8,128)(2,1)S(1)}, u32[]{:S(2)}, u32[]{:S(2)}) %collective-permute-start.9) | collective-permute-done | bytes 163872 | tf_op jit(solution)/shard_map/ppermute | solution.py:380
  14.9 0.3 collective-permute-start.10
  15.2 0.0 collective-permute-done.refs_5_
  15.2 1.7 %collective-permute-start.1 = (bf16[64,1280]{1,0:T(8,128)(2,1)S(1)}, bf16[64,1280]{1,0:T(8,128)(2,1)S(1)}, u32[]{:S(2)}, u32[]{:S(2)}) collective-permute-start(bf16[64,1280]{1,0:T(8,128)(2,1)S(1)} %collective-permute-done.refs_5_), channel_id=1, source_target_pairs={{2,0},{6,2},{10,6},{14,10},{12,14},{8,12},{4,8},{0,4},{3,1},{7,3},... | collective-permute-start | bytes 491528 | tf_op jit(solution)/shard_map/ppermute | solution.py:381
  16.9 1.1 %collective-permute-done.8.refs_6_.refs_4_ = bf16[64,1280]{1,0:T(8,128)(2,1)S(1)} collective-permute-done((bf16[64,1280]{1,0:T(8,128)(2,1)S(1)}, bf16[64,1280]{1,0:T(8,128)(2,1)S(1)}, u32[]{:S(2)}, u32[]{:S(2)}) %collective-permute-start.8) | collective-permute-done | bytes 163872 | tf_op jit(solution)/shard_map/ppermute | solution.py:379
  18.1 0.4 %collective-permute-start.12 = (bf16[64,1280]{1,0:T(8,128)(2,1)S(1)}, bf16[64,1280]{1,0:T(8,128)(2,1)S(1)}, u32[]{:S(2)}, u32[]{:S(2)}) collective-permute-start(bf16[64,1280]{1,0:T(8,128)(2,1)S(1)} %collective-permute-done.8.refs_6_.refs_4_), channel_id=1, source_target_pairs={{2,0},{6,2},{10,6},{14,10},{12,14},{8,12},{4,8},{0,4},{3,1},{7,3},... | collective-permute-start | bytes 491528 | tf_op jit(solution)/shard_map/ppermute | solution.py:379
  18.5 0.0 collective-permute-done.3.refs_6_
  18.5 1.6 %collective-permute-start.4 = (bf16[64,1280]{1,0:T(8,128)(2,1)S(1)}, bf16[64,1280]{1,0:T(8,128)(2,1)S(1)}, u32[]{:S(2)}, u32[]{:S(2)}) collective-permute-start(bf16[64,1280]{1,0:T(8,128)(2,1)S(1)} %collective-permute-done.3.refs_6_), channel_id=1, source_target_pairs={{0,2},{2,6},{6,10},{10,14},{14,12},{12,8},{8,4},{4,0},{1,3},{3,7},... | collective-permute-start | bytes 491528 | tf_op jit(solution)/shard_map/ppermute | solution.py:378
  20.1 0.0 slice-done
  20.1 0.0 slice-done.1
  20.1 2.5 %shard_map.85 = (f32[256,512]{1,0:T(8,128)S(1)}, f32[256,512]{1,0:T(8,128)S(1)}, bf16[256,512]{1,0:T(8,128)(2,1)S(1)}) custom-call(bf16[256,4096]{1,0:T(8,128)(2,1)S(1)} %copy-done, bf16[4096,1024]{1,0:T(8,128)(2,1)S(1)} %bitcast.5, s32[8,512]{1,0:T(8,128)S(1)} %shard_map.84.bounds_ref.refs_2_.refs_1_), custom_call_target="tpu_custom_call" | custom-call | bytes 4194304 | tf_op jit(solution)/shard_map/pallas_call | solution.py:223
  22.6 0.0 collective-permute-done.10.refs_10_.refs_3_
  22.6 1.5 %collective-permute-start.11 = (bf16[64,1280]{1,0:T(8,128)(2,1)S(1)}, bf16[64,1280]{1,0:T(8,128)(2,1)S(1)}, u32[]{:S(2)}, u32[]{:S(2)}) collective-permute-start(bf16[64,1280]{1,0:T(8,128)(2,1)S(1)} %collective-permute-done.10.refs_10_.refs_3_), channel_id=1, source_target_pairs={{0,2},{2,6},{6,10},{10,14},{14,12},{12,8},{8,4},{4,0},{1,3},{3,7},... | collective-permute-start | bytes 491528 | tf_op jit(solution)/shard_map/ppermute | solution.py:380
  24.1 0.0 collective-permute-done.1.refs_2_
  24.1 0.6 %collective-permute-start.5 = (bf16[64,1280]{1,0:T(8,128)(2,1)S(1)}, bf16[64,1280]{1,0:T(8,128)(2,1)S(1)}, u32[]{:S(2)}, u32[]{:S(2)}) collective-permute-start(bf16[64,1280]{1,0:T(8,128)(2,1)S(1)} %collective-permute-done.1.refs_2_), channel_id=1, source_target_pairs={{2,0},{6,2},{10,6},{14,10},{12,14},{8,12},{4,8},{0,4},{3,1},{7,3},... | collective-permute-start | bytes 491528 | tf_op jit(solution)/shard_map/ppermute | solution.py:381
  24.7 0.0 collective-permute-done.12.refs_8_.refs_6_
  24.7 1.0 %collective-permute-start.13 = (bf16[64,1280]{1,0:T(8,128)(2,1)S(1)}, bf16[64,1280]{1,0:T(8,128)(2,1)S(1)}, u32[]{:S(2)}, u32[]{:S(2)}) collective-permute-start(bf16[64,1280]{1,0:T(8,128)(2,1)S(1)} %collective-permute-done.12.refs_8_.refs_6_), channel_id=1, source_target_pairs={{2,0},{6,2},{10,6},{14,10},{12,14},{8,12},{4,8},{0,4},{3,1},{7,3},... | collective-permute-start | bytes 491528 | tf_op jit(solution)/shard_map/ppermute | solution.py:386
  25.7 0.0 collective-permute-done.4.refs_3_
  25.7 1.0 %collective-permute-start.6 = (bf16[64,1280]{1,0:T(8,128)(2,1)S(1)}, bf16[64,1280]{1,0:T(8,128)(2,1)S(1)}, u32[]{:S(2)}, u32[]{:S(2)}) collective-permute-start(bf16[64,1280]{1,0:T(8,128)(2,1)S(1)} %collective-permute-done.4.refs_3_), channel_id=1, source_target_pairs={{0,2},{2,6},{6,10},{10,14},{14,12},{12,8},{8,4},{4,0},{1,3},{3,7},... | collective-permute-start | bytes 491528 | tf_op jit(solution)/shard_map/ppermute | solution.py:385
  26.7 2.6 %collective-permute-done.14.refs_1_.refs_0_ = bf16[4112,128]{1,0:T(8,128)(2,1)S(1)} collective-permute-done((bf16[4112,128]{1,0:T(8,128)(2,1)S(1)}, bf16[4112,128]{1,0:T(8,128)(2,1)S(1)}, u32[]{:S(2)}, u32[]{:S(2)}) %collective-permute-start.14) | collective-permute-done | bytes 1052704 | tf_op jit(solution)/shard_map/ppermute | solution.py:389
  29.3 0.7 %shard_map.86 = (f32[256,128]{1,0:T(8,128)S(1)}, f32[256,128]{1,0:T(8,128)S(1)}) custom-call(bf16[256,4096]{1,0:T(8,128)(2,1)S(1)} %copy-done, bf16[4112,128]{1,0:T(8,128)(2,1)S(1)} %collective-permute-done.14.refs_1_.refs_0_, s32[8,512]{1,0:T(8,128)S(1)} %shard_map.84.bounds_ref.refs_2_.refs_1_, bf16[64,1280]{1,0:T(8,128)(2,1)S(1)} %get-tuple-element.32.refs_3_, ...), custom_call_target="tpu_custom_call" | custom-call | flops 8589934592 | bytes 16777216 | tf_op jit(solution)/shard_map/pallas_call | solution.py:317
  30.1 0.1 collective-permute-start.18
  30.2 0.0 collective-permute-done.11.refs_7_.refs_5_
  30.2 0.0 collective-permute-done.5.refs_4_
  30.2 1.0 %collective-permute-done.13.refs_9_.refs_7_ = bf16[64,1280]{1,0:T(8,128)(2,1)S(1)} collective-permute-done((bf16[64,1280]{1,0:T(8,128)(2,1)S(1)}, bf16[64,1280]{1,0:T(8,128)(2,1)S(1)}, u32[]{:S(2)}, u32[]{:S(2)}) %collective-permute-start.13) | collective-permute-done | bytes 163872 | tf_op jit(solution)/shard_map/ppermute | solution.py:386
  31.2 0.0 collective-permute-done.6.refs_5_
  31.2 0.5 %shard_map.88 = f32[128,128]{1,0:T(8,128)S(1)} custom-call(bf16[4112,128]{1,0:T(8,128)(2,1)S(1)} %collective-permute-done.14.refs_1_.refs_0_, s32[8,512]{1,0:T(8,128)S(1)} %shard_map.84.bounds_ref.refs_2_.refs_1_, bf16[64,1280]{1,0:T(8,128)(2,1)S(1)} %collective-permute-done.1.refs_2_, bf16[64,1280]{1,0:T(8,128)(2,1)S(1)} %collective-permute-done.4.refs_3_, ...), custom_call_target="tpu_custom_call" | custom-call | flops 8589934592 | bytes 16777216 | tf_op jit(solution)/shard_map/pallas_call | solution.py:317
  31.7 0.9 %collective-permute-start.16 = (f32[128,128]{1,0:T(8,128)S(1)}, f32[128,128]{1,0:T(8,128)S(1)}, u32[]{:S(2)}, u32[]{:S(2)}) collective-permute-start(f32[128,128]{1,0:T(8,128)S(1)} %shard_map.88), channel_id=1, source_target_pairs={{0,17},{1,16},{16,1},{17,0},{2,19},{3,18},{18,3},{19,2},{4,21},{5,... | collective-permute-start | bytes 196616 | tf_op jit(solution)/shard_map/ppermute | solution.py:408
  32.6 0.6 %collective-permute-start.17 = (f32[128,128]{1,0:T(8,128)S(1)}, f32[128,128]{1,0:T(8,128)S(1)}, u32[]{:S(2)}, u32[]{:S(2)}) collective-permute-start(f32[128,128]{1,0:T(8,128)S(1)} %shard_map.88), channel_id=1, source_target_pairs={{0,16},{16,0},{1,17},{17,1},{2,18},{18,2},{3,19},{19,3},{4,20},{20... | collective-permute-start | bytes 196616 | tf_op jit(solution)/shard_map/ppermute | solution.py:409
  33.2 0.5 %shard_map.87.mine = f32[128,128]{1,0:T(8,128)S(1)} custom-call(bf16[256,4096]{1,0:T(8,128)(2,1)S(1)} %copy-done, s32[8,512]{1,0:T(8,128)S(1)} %shard_map.84.bounds_ref.refs_2_.refs_1_, bf16[64,1280]{1,0:T(8,128)(2,1)S(1)} %collective-permute-done.1.refs_2_, bf16[64,1280]{1,0:T(8,128)(2,1)S(1)} %collective-permute-done.4.refs_3_, ...), custom_call_target="tpu_custom_call" | custom-call | bytes 4194304 | tf_op jit(solution)/shard_map/pallas_call | solution.py:317
  33.8 0.5 %collective-permute-start.15 = (f32[128,128]{1,0:T(8,128)S(1)}, f32[128,128]{1,0:T(8,128)S(1)}, u32[]{:S(2)}, u32[]{:S(2)}) collective-permute-start(f32[128,128]{1,0:T(8,128)S(1)} %shard_map.87.mine), channel_id=1, source_target_pairs={{0,1},{1,0},{2,3},{3,2},{4,5},{5,4},{6,7},{7,6},{8,9},{9,8},{10,11... | collective-permute-start | bytes 196616 | tf_op jit(solution)/shard_map/ppermute | solution.py:410
  34.3 1.8 %collective-permute-done.16.three = f32[128,128]{1,0:T(8,128)S(1)} collective-permute-done((f32[128,128]{1,0:T(8,128)S(1)}, f32[128,128]{1,0:T(8,128)S(1)}, u32[]{:S(2)}, u32[]{:S(2)}) %collective-permute-start.16) | collective-permute-done | bytes 65568 | tf_op jit(solution)/shard_map/ppermute | solution.py:408
  36.1 1.4 %collective-permute-done.17.two = f32[128,128]{1,0:T(8,128)S(1)} collective-permute-done((f32[128,128]{1,0:T(8,128)S(1)}, f32[128,128]{1,0:T(8,128)S(1)}, u32[]{:S(2)}, u32[]{:S(2)}) %collective-permute-start.17) | collective-permute-done | bytes 65568 | tf_op jit(solution)/shard_map/ppermute | solution.py:409
  37.5 0.0 collective-permute-done.15.one
  37.5 0.0 collective-permute-done.18.far_ref
  37.5 1.1 %shard_map.89 = bf16[256,512]{1,0:T(8,128)(2,1)} custom-call(bf16[256,512]{1,0:T(8,128)(2,1)S(1)} %get-tuple-element.28.mask_ref, f32[128,128]{1,0:T(8,128)S(1)} %shard_map.87.mine, f32[128,128]{1,0:T(8,128)S(1)} %collective-permute-done.15.one, f32[128,128]{1,0:T(8,128)S(1)} %collective-permute-done.16.three, f32[128,128]{1,0:T(8,128)S(1)} %collective-permute-done.17.two, ...), custom_call_target="tpu_custom_call" | custom-call | tf_op jit(solution)/shard_map/pallas_call | solution.py:413
  (5 shorter events, 0.0 us)
Async XLA Ops:
  0.0 4.3 %copy-start = (bf16[256,4096]{1,0:T(8,128)(2,1)S(1)}, bf16[256,4096]{1,0:T(8,128)(2,1)}, u32[]{:S(2)}) copy-start(bf16[256,4096]{1,0:T(8,128)(2,1)} %refs_0_.1) | copy-start | bytes 6291460
  1.2 7.4 %collective-permute-start.7 = (bf16[64,1280]{1,0:T(8,128)(2,1)S(1)}, bf16[64,1280]{1,0:T(8,128)(2,1)S(1)}, u32[]{:S(2)}, u32[]{:S(2)}) collective-permute-start(bf16[64,1280]{1,0:T(8,128)(2,1)S(1)} %get-tuple-element.33.refs_7_.refs_0_), channel_id=1, source_target_pairs={{2,0},{6,2},{10,6},{14,10},{12,14},{8,12},{4,8},{0,4},{3,1},{7,3},... | collective-permute-start | bytes 491528 | tf_op jit(solution)/shard_map/ppermute | solution.py:379
  4.3 7.1 %collective-permute-start.2 = (bf16[64,1280]{1,0:T(8,128)(2,1)S(1)}, bf16[64,1280]{1,0:T(8,128)(2,1)S(1)}, u32[]{:S(2)}, u32[]{:S(2)}) collective-permute-start(bf16[64,1280]{1,0:T(8,128)(2,1)S(1)} %get-tuple-element.32.refs_3_), channel_id=1, source_target_pairs={{0,2},{2,6},{6,10},{10,14},{14,12},{12,8},{8,4},{4,0},{1,3},{3,7},... | collective-permute-start | bytes 491528 | tf_op jit(solution)/shard_map/ppermute | solution.py:378
  4.6 24.8 %collective-permute-start.14 = (bf16[4112,128]{1,0:T(8,128)(2,1)S(1)}, bf16[4112,128]{1,0:T(8,128)(2,1)S(1)}, u32[]{:S(2)}, u32[]{:S(2)}) collective-permute-start(bf16[4112,128]{1,0:T(8,128)(2,1)S(1)} %get-tuple-element.34), channel_id=1, source_target_pairs={{0,16},{16,0},{1,17},{17,1},{2,18},{18,2},{3,19},{19,3},{4,20},{20... | collective-permute-start | bytes 3158024 | tf_op jit(solution)/shard_map/ppermute | solution.py:389
  6.6 13.5 %slice-start = ((s8[8388608]{0:T(1024)(128)(4,1)}), s8[4194304]{0:T(1024)(128)(4,1)S(1)}, s32[]{:S(2)}) async-start(s8[8388608]{0:T(1024)(128)(4,1)} %bitcast.4), calls=%async_computation | async-start | bytes 8388608
  6.6 13.5 %slice-start.1 = ((s8[8388608]{0:T(1024)(128)(4,1)}), s8[4194304]{0:T(1024)(128)(4,1)S(1)}, s32[]{:S(2)}) async-start(s8[8388608]{0:T(1024)(128)(4,1)} %bitcast.4), calls=%async_computation.1 | async-start | bytes 8388608
  6.6 8.3 %collective-permute-start.9 = (bf16[64,1280]{1,0:T(8,128)(2,1)S(1)}, bf16[64,1280]{1,0:T(8,128)(2,1)S(1)}, u32[]{:S(2)}, u32[]{:S(2)}) collective-permute-start(bf16[64,1280]{1,0:T(8,128)(2,1)S(1)} %get-tuple-element.33.refs_7_.refs_0_), channel_id=1, source_target_pairs={{0,2},{2,6},{6,10},{10,14},{14,12},{12,8},{8,4},{4,0},{1,3},{3,7},... | collective-permute-start | bytes 491528 | tf_op jit(solution)/shard_map/ppermute | solution.py:380
  8.1 7.1 %collective-permute-start = (bf16[64,1280]{1,0:T(8,128)(2,1)S(1)}, bf16[64,1280]{1,0:T(8,128)(2,1)S(1)}, u32[]{:S(2)}, u32[]{:S(2)}) collective-permute-start(bf16[64,1280]{1,0:T(8,128)(2,1)S(1)} %get-tuple-element.32.refs_3_), channel_id=1, source_target_pairs={{2,0},{6,2},{10,6},{14,10},{12,14},{8,12},{4,8},{0,4},{3,1},{7,3},... | collective-permute-start | bytes 491528 | tf_op jit(solution)/shard_map/ppermute | solution.py:381
  8.6 9.4 %collective-permute-start.8 = (bf16[64,1280]{1,0:T(8,128)(2,1)S(1)}, bf16[64,1280]{1,0:T(8,128)(2,1)S(1)}, u32[]{:S(2)}, u32[]{:S(2)}) collective-permute-start(bf16[64,1280]{1,0:T(8,128)(2,1)S(1)} %collective-permute-done.7.refs_9_.refs_2_), channel_id=1, source_target_pairs={{2,0},{6,2},{10,6},{14,10},{12,14},{8,12},{4,8},{0,4},{3,1},{7,3},... | collective-permute-start | bytes 491528 | tf_op jit(solution)/shard_map/ppermute | solution.py:379
  11.4 7.1 %collective-permute-start.3 = (bf16[64,1280]{1,0:T(8,128)(2,1)S(1)}, bf16[64,1280]{1,0:T(8,128)(2,1)S(1)}, u32[]{:S(2)}, u32[]{:S(2)}) collective-permute-start(bf16[64,1280]{1,0:T(8,128)(2,1)S(1)} %collective-permute-done.2.refs_4_), channel_id=1, source_target_pairs={{0,2},{2,6},{6,10},{10,14},{14,12},{12,8},{8,4},{4,0},{1,3},{3,7},... | collective-permute-start | bytes 491528 | tf_op jit(solution)/shard_map/ppermute | solution.py:378
  14.9 7.7 %collective-permute-start.10 = (bf16[64,1280]{1,0:T(8,128)(2,1)S(1)}, bf16[64,1280]{1,0:T(8,128)(2,1)S(1)}, u32[]{:S(2)}, u32[]{:S(2)}) collective-permute-start(bf16[64,1280]{1,0:T(8,128)(2,1)S(1)} %collective-permute-done.9.refs_8_.refs_1_), channel_id=1, source_target_pairs={{0,2},{2,6},{6,10},{10,14},{14,12},{12,8},{8,4},{4,0},{1,3},{3,7},... | collective-permute-start | bytes 491528 | tf_op jit(solution)/shard_map/ppermute | solution.py:380
  15.2 8.9 %collective-permute-start.1 = (bf16[64,1280]{1,0:T(8,128)(2,1)S(1)}, bf16[64,1280]{1,0:T(8,128)(2,1)S(1)}, u32[]{:S(2)}, u32[]{:S(2)}) collective-permute-start(bf16[64,1280]{1,0:T(8,128)(2,1)S(1)} %collective-permute-done.refs_5_), channel_id=1, source_target_pairs={{2,0},{6,2},{10,6},{14,10},{12,14},{8,12},{4,8},{0,4},{3,1},{7,3},... | collective-permute-start | bytes 491528 | tf_op jit(solution)/shard_map/ppermute | solution.py:381
  18.1 6.6 %collective-permute-start.12 = (bf16[64,1280]{1,0:T(8,128)(2,1)S(1)}, bf16[64,1280]{1,0:T(8,128)(2,1)S(1)}, u32[]{:S(2)}, u32[]{:S(2)}) collective-permute-start(bf16[64,1280]{1,0:T(8,128)(2,1)S(1)} %collective-permute-done.8.refs_6_.refs_4_), channel_id=1, source_target_pairs={{2,0},{6,2},{10,6},{14,10},{12,14},{8,12},{4,8},{0,4},{3,1},{7,3},... | collective-permute-start | bytes 491528 | tf_op jit(solution)/shard_map/ppermute | solution.py:379
  18.5 7.1 %collective-permute-start.4 = (bf16[64,1280]{1,0:T(8,128)(2,1)S(1)}, bf16[64,1280]{1,0:T(8,128)(2,1)S(1)}, u32[]{:S(2)}, u32[]{:S(2)}) collective-permute-start(bf16[64,1280]{1,0:T(8,128)(2,1)S(1)} %collective-permute-done.3.refs_6_), channel_id=1, source_target_pairs={{0,2},{2,6},{6,10},{10,14},{14,12},{12,8},{8,4},{4,0},{1,3},{3,7},... | collective-permute-start | bytes 491528 | tf_op jit(solution)/shard_map/ppermute | solution.py:378
  22.6 7.6 %collective-permute-start.11 = (bf16[64,1280]{1,0:T(8,128)(2,1)S(1)}, bf16[64,1280]{1,0:T(8,128)(2,1)S(1)}, u32[]{:S(2)}, u32[]{:S(2)}) collective-permute-start(bf16[64,1280]{1,0:T(8,128)(2,1)S(1)} %collective-permute-done.10.refs_10_.refs_3_), channel_id=1, source_target_pairs={{0,2},{2,6},{6,10},{10,14},{14,12},{12,8},{8,4},{4,0},{1,3},{3,7},... | collective-permute-start | bytes 491528 | tf_op jit(solution)/shard_map/ppermute | solution.py:380
  24.1 6.1 %collective-permute-start.5 = (bf16[64,1280]{1,0:T(8,128)(2,1)S(1)}, bf16[64,1280]{1,0:T(8,128)(2,1)S(1)}, u32[]{:S(2)}, u32[]{:S(2)}) collective-permute-start(bf16[64,1280]{1,0:T(8,128)(2,1)S(1)} %collective-permute-done.1.refs_2_), channel_id=1, source_target_pairs={{2,0},{6,2},{10,6},{14,10},{12,14},{8,12},{4,8},{0,4},{3,1},{7,3},... | collective-permute-start | bytes 491528 | tf_op jit(solution)/shard_map/ppermute | solution.py:381
  24.7 6.5 %collective-permute-start.13 = (bf16[64,1280]{1,0:T(8,128)(2,1)S(1)}, bf16[64,1280]{1,0:T(8,128)(2,1)S(1)}, u32[]{:S(2)}, u32[]{:S(2)}) collective-permute-start(bf16[64,1280]{1,0:T(8,128)(2,1)S(1)} %collective-permute-done.12.refs_8_.refs_6_), channel_id=1, source_target_pairs={{2,0},{6,2},{10,6},{14,10},{12,14},{8,12},{4,8},{0,4},{3,1},{7,3},... | collective-permute-start | bytes 491528 | tf_op jit(solution)/shard_map/ppermute | solution.py:386
  25.7 5.5 %collective-permute-start.6 = (bf16[64,1280]{1,0:T(8,128)(2,1)S(1)}, bf16[64,1280]{1,0:T(8,128)(2,1)S(1)}, u32[]{:S(2)}, u32[]{:S(2)}) collective-permute-start(bf16[64,1280]{1,0:T(8,128)(2,1)S(1)} %collective-permute-done.4.refs_3_), channel_id=1, source_target_pairs={{0,2},{2,6},{6,10},{10,14},{14,12},{12,8},{8,4},{4,0},{1,3},{3,7},... | collective-permute-start | bytes 491528 | tf_op jit(solution)/shard_map/ppermute | solution.py:385
  30.1 7.4 %collective-permute-start.18 = (f32[256,512]{1,0:T(8,128)S(1)}, f32[256,512]{1,0:T(8,128)S(1)}, u32[]{:S(2)}, u32[]{:S(2)}) collective-permute-start(f32[256,512]{1,0:T(8,128)S(1)} %get-tuple-element.40), channel_id=1, source_target_pairs={{0,1},{1,0},{2,3},{3,2},{4,5},{5,4},{6,7},{7,6},{8,9},{9,8},{10,11... | collective-permute-start | bytes 1572872 | tf_op jit(solution)/shard_map/ppermute | solution.py:402
  31.7 4.4 %collective-permute-start.16 = (f32[128,128]{1,0:T(8,128)S(1)}, f32[128,128]{1,0:T(8,128)S(1)}, u32[]{:S(2)}, u32[]{:S(2)}) collective-permute-start(f32[128,128]{1,0:T(8,128)S(1)} %shard_map.88), channel_id=1, source_target_pairs={{0,17},{1,16},{16,1},{17,0},{2,19},{3,18},{18,3},{19,2},{4,21},{5,... | collective-permute-start | bytes 196616 | tf_op jit(solution)/shard_map/ppermute | solution.py:408
  32.6 4.9 %collective-permute-start.17 = (f32[128,128]{1,0:T(8,128)S(1)}, f32[128,128]{1,0:T(8,128)S(1)}, u32[]{:S(2)}, u32[]{:S(2)}) collective-permute-start(f32[128,128]{1,0:T(8,128)S(1)} %shard_map.88), channel_id=1, source_target_pairs={{0,16},{16,0},{1,17},{17,1},{2,18},{18,2},{3,19},{19,3},{4,20},{20... | collective-permute-start | bytes 196616 | tf_op jit(solution)/shard_map/ppermute | solution.py:409
  33.8 3.7 %collective-permute-start.15 = (f32[128,128]{1,0:T(8,128)S(1)}, f32[128,128]{1,0:T(8,128)S(1)}, u32[]{:S(2)}, u32[]{:S(2)}) collective-permute-start(f32[128,128]{1,0:T(8,128)S(1)} %shard_map.87.mine), channel_id=1, source_target_pairs={{0,1},{1,0},{2,3},{3,2},{4,5},{5,4},{6,7},{7,6},{8,9},{9,8},{10,11... | collective-permute-start | bytes 196616 | tf_op jit(solution)/shard_map/ppermute | solution.py:410

commit v20 on v18

--- a/solution.py
+++ b/solution.py
@@ -354,19 +354,21 @@
     rank, width = factor_out.shape[1:]
     depth = features // 2
     order = ring_order(owners)
-    forward = [(order[i], order[(i + 1) % owners]) for i in range(owners)]
-    backward = [(b, a) for a, b in forward]
     swap = [(0, 1), (1, 0)]
+    edges = [[], []]
+    for i in range(owners):
+        a, b = order[i], order[(i + 1) % owners]
+        edges[i % 2] += [(a, b), (b, a)]
 
     full = (owners - 1) // 2
-    distances = [0]
-    for step in range(1, full + 1):
-        distances += [step, -step]
-    distances.append(owners // 2)
-    table = [
-        [[order[(order.index(me) - distance) % owners] for distance in distances]]
-        for me in range(owners)
-    ]
+    held = [list(range(owners)), list(range(owners))]
+    table = [[[me]] for me in range(owners)]
+    for step in range(1, owners // 2 + 1):
+        for chain in (0, 1):
+            came = dict((b, a) for a, b in edges[(step - 1 + chain) % 2])
+            held[chain] = [held[chain][came[me]] for me in range(owners)]
+        for me in range(owners):
+            table[me][0] += [held[0][me], held[1][me]] if step <= full else [held[0][me]]
     first, second, bounds = shard_call(
         factor_in[0].T, factor_out[0], demand, lengths, holder_slot, jnp.asarray(table, I32), depth
     )
@@ -376,15 +378,16 @@
     firsts, seconds = [first], [second]
     ahead, behind = (first, second_later), (first_later, second)
     for step in range(1, full + 1):
-        a = lax.ppermute(ahead[0], "batch", forward)
-        d = lax.ppermute(behind[1], "batch", backward)
-        b = lax.ppermute(ahead[1], "batch", forward)
-        c = lax.ppermute(behind[0], "batch", backward)
+        first_edges, second_edges = edges[(step - 1) % 2], edges[step % 2]
+        a = lax.ppermute(ahead[0], "batch", first_edges)
+        d = lax.ppermute(behind[1], "batch", second_edges)
+        b = lax.ppermute(ahead[1], "batch", first_edges)
+        c = lax.ppermute(behind[0], "batch", second_edges)
         ahead, behind = (a, b), (c, d)
         firsts += [a, c]
         seconds += [b, d]
-    firsts.append(lax.ppermute(ahead[0], "batch", forward))
-    seconds.append(lax.ppermute(behind[1], "batch", backward))
+    firsts.append(lax.ppermute(ahead[0], "batch", edges[full % 2]))
+    seconds.append(lax.ppermute(behind[1], "batch", edges[(full + 1) % 2]))
     near, far, mask = base_call(hidden, value_weight, bounds, GROUP * rank)
     hidden, near, far = lax.optimization_barrier((hidden, near, far))
     other = lax.ppermute(to_other, "groups", swap)

time: 37.8 us -> 38.8 us (1.026)
  starting transfers between devices: 19.2 us -> 22.9 us
  waiting for transfers between devices: 11.5 us -> 8.81 us
    ppermute x14, starting transfers between devices: 15 us -> 19.1 us  [the longest x3 6.38 us: per_device(): d = lax.ppermute(behind[1], 'batch', second_edges)]
    ppermute x14, waiting for transfers between devices: 6.65 us -> 4.38 us  [the longest x3 2.73 us: per_device(): b = lax.ppermute(ahead[1], 'batch', first_edges)]
    ppermute x1, starting transfers between devices: 2.03 us -> 1.61 us  [per_device(): other = lax.ppermute(to_other, 'groups', swap)]
  transfers between devices with their start and end apart: 20 -> 20, of which waited for: 7 -> 8; matrix products, arithmetic and copies ran while one was open for 0% -> 0% of each run, Pallas kernels for 12% -> 12%
where the time goes in v20:
time: 38.8 us; the launch traced here: 38.6 us
  starting transfers between devices  22.9 us (59%)
  waiting for transfers between devices  8.81 us (23%)
  Pallas kernels  6.83 us (18%)
    ppermute x3, starting transfers between devices, per_device(): d = lax.ppermute(behind[1], 'batch', second_edges)  6.38 us
    ppermute x3, starting transfers between devices, per_device(): a = lax.ppermute(ahead[0], 'batch', first_edges)  4.18 us
    ppermute x3, starting transfers between devices, per_device(): c = lax.ppermute(behind[0], 'batch', second_edges)  3.09 us
    ppermute x3, starting transfers between devices, per_device(): b = lax.ppermute(ahead[1], 'batch', first_edges)  2.74 us
    ppermute x3, waiting for transfers between devices, per_device(): b = lax.ppermute(ahead[1], 'batch', first_edges)  2.73 us
    pallas_call x1, Pallas kernels, base_call(): pl.pallas_call(functools.partial(base_kernel, size), out_shape=(out, out,...  2.47 us
    ppermute x1, waiting for transfers between devices, per_device(): other = lax.ppermute(to_other, 'groups', swap)  2.33 us
    pallas_call x3, Pallas kernels, rank_call(): pl.pallas_call(functools.partial(rank_kernel, sides, groups, depth, last)...  1.84 us
  transfers between devices with their start and end apart: 20, of which 8 were waited for; matrix products, arithmetic and copies ran while one was open for 0% of the time, Pallas kernels for 12%

profile of v20, /device:TPU:0, one launch (start us, length us, event | category | flops | bytes accessed | tf_op | source)
XLA Modules:
  0.0 38.6 jit_solution(1680184913047014119)
XLA Ops:
  0.0 1.2 %shard_map.82 = (bf16[64,1280]{1,0:T(8,128)(2,1)S(1)}, bf16[64,1280]{1,0:T(8,128)(2,1)S(1)}, s32[8,512]{1,0:T(8,128)S(1)}) custom-call(bf16[64,4096]{1,0:T(8,128)(2,1)} %bitcast.6, bf16[64,512]{1,0:T(8,128)(2,1)} %bitcast.7, s32[1,4]{1,0:T(1,128)} %demand_ref.1, s32[1,4]{1,0:T(1,128)} %lengths_ref.1, s32[8]{0:T(128)} %holder_ref.1, ...), custom_call_target="tpu_custom_call" | custom-call | flops 8589934592 | bytes 16777216 | tf_op jit(solution)/shard_map/pallas_call | solution.py:137
  1.2 3.1 %collective-permute-start.7 = (bf16[64,1280]{1,0:T(8,128)(2,1)S(1)}, bf16[64,1280]{1,0:T(8,128)(2,1)S(1)}, u32[]{:S(2)}, u32[]{:S(2)}) collective-permute-start(bf16[64,1280]{1,0:T(8,128)(2,1)S(1)} %get-tuple-element.35.refs_7_.refs_0_), channel_id=1, source_target_pairs={{2,6},{6,2},{10,14},{14,10},{12,8},{8,12},{4,0},{0,4},{3,7},{7,3},... | collective-permute-start | bytes 491528 | tf_op jit(solution)/shard_map/ppermute | solution.py:383
  4.3 1.5 %collective-permute-start.2 = (bf16[64,1280]{1,0:T(8,128)(2,1)S(1)}, bf16[64,1280]{1,0:T(8,128)(2,1)S(1)}, u32[]{:S(2)}, u32[]{:S(2)}) collective-permute-start(bf16[64,1280]{1,0:T(8,128)(2,1)S(1)} %get-tuple-element.34.refs_3_), channel_id=1, source_target_pairs={{0,2},{2,0},{6,10},{10,6},{14,12},{12,14},{8,4},{4,8},{1,3},{3,1},... | collective-permute-start | bytes 491528 | tf_op jit(solution)/shard_map/ppermute | solution.py:382
  5.8 0.0 copy-done
  5.8 0.3 shard_map.83
  6.1 1.6 %collective-permute-start.14 = (bf16[4112,128]{1,0:T(8,128)(2,1)S(1)}, bf16[4112,128]{1,0:T(8,128)(2,1)S(1)}, u32[]{:S(2)}, u32[]{:S(2)}) collective-permute-start(bf16[4112,128]{1,0:T(8,128)(2,1)S(1)} %get-tuple-element.36), channel_id=1, source_target_pairs={{0,16},{16,0},{1,17},{17,1},{2,18},{18,2},{3,19},{19,3},{4,20},{20... | collective-permute-start | bytes 3158024 | tf_op jit(solution)/shard_map/ppermute | solution.py:393
  7.7 0.5 %collective-permute-start.9 = (bf16[64,1280]{1,0:T(8,128)(2,1)S(1)}, bf16[64,1280]{1,0:T(8,128)(2,1)S(1)}, u32[]{:S(2)}, u32[]{:S(2)}) collective-permute-start(bf16[64,1280]{1,0:T(8,128)(2,1)S(1)} %get-tuple-element.35.refs_7_.refs_0_), channel_id=1, source_target_pairs={{0,2},{2,0},{6,10},{10,6},{14,12},{12,14},{8,4},{4,8},{1,3},{3,1},... | collective-permute-start | bytes 491528 | tf_op jit(solution)/shard_map/ppermute | solution.py:384
  8.2 1.2 %collective-permute-start = (bf16[64,1280]{1,0:T(8,128)(2,1)S(1)}, bf16[64,1280]{1,0:T(8,128)(2,1)S(1)}, u32[]{:S(2)}, u32[]{:S(2)}) collective-permute-start(bf16[64,1280]{1,0:T(8,128)(2,1)S(1)} %get-tuple-element.34.refs_3_), channel_id=1, source_target_pairs={{2,6},{6,2},{10,14},{14,10},{12,8},{8,12},{4,0},{0,4},{3,7},{7,3},... | collective-permute-start | bytes 491528 | tf_op jit(solution)/shard_map/ppermute | solution.py:385
  9.4 0.0 collective-permute-done.7.refs_9_.refs_2_
  9.4 1.5 %collective-permute-start.8 = (bf16[64,1280]{1,0:T(8,128)(2,1)S(1)}, bf16[64,1280]{1,0:T(8,128)(2,1)S(1)}, u32[]{:S(2)}, u32[]{:S(2)}) collective-permute-start(bf16[64,1280]{1,0:T(8,128)(2,1)S(1)} %collective-permute-done.7.refs_9_.refs_2_), channel_id=1, source_target_pairs={{0,2},{2,0},{6,10},{10,6},{14,12},{12,14},{8,4},{4,8},{1,3},{3,1},... | collective-permute-start | bytes 491528 | tf_op jit(solution)/shard_map/ppermute | solution.py:383
  10.9 0.0 collective-permute-done.2.refs_4_
  10.9 1.2 %collective-permute-start.3 = (bf16[64,1280]{1,0:T(8,128)(2,1)S(1)}, bf16[64,1280]{1,0:T(8,128)(2,1)S(1)}, u32[]{:S(2)}, u32[]{:S(2)}) collective-permute-start(bf16[64,1280]{1,0:T(8,128)(2,1)S(1)} %collective-permute-done.2.refs_4_), channel_id=1, source_target_pairs={{2,6},{6,2},{10,14},{14,10},{12,8},{8,12},{4,0},{0,4},{3,7},{7,3},... | collective-permute-start | bytes 491528 | tf_op jit(solution)/shard_map/ppermute | solution.py:382
  12.1 2.7 %collective-permute-done.9.refs_8_.refs_1_ = bf16[64,1280]{1,0:T(8,128)(2,1)S(1)} collective-permute-done((bf16[64,1280]{1,0:T(8,128)(2,1)S(1)}, bf16[64,1280]{1,0:T(8,128)(2,1)S(1)}, u32[]{:S(2)}, u32[]{:S(2)}) %collective-permute-start.9) | collective-permute-done | bytes 163872 | tf_op jit(solution)/shard_map/ppermute | solution.py:384
  14.8 1.6 %collective-permute-start.10 = (bf16[64,1280]{1,0:T(8,128)(2,1)S(1)}, bf16[64,1280]{1,0:T(8,128)(2,1)S(1)}, u32[]{:S(2)}, u32[]{:S(2)}) collective-permute-start(bf16[64,1280]{1,0:T(8,128)(2,1)S(1)} %collective-permute-done.9.refs_8_.refs_1_), channel_id=1, source_target_pairs={{2,6},{6,2},{10,14},{14,10},{12,8},{8,12},{4,0},{0,4},{3,7},{7,3},... | collective-permute-start | bytes 491528 | tf_op jit(solution)/shard_map/ppermute | solution.py:384
  16.4 0.0 collective-permute-done.refs_5_
  16.4 1.5 %collective-permute-start.1 = (bf16[64,1280]{1,0:T(8,128)(2,1)S(1)}, bf16[64,1280]{1,0:T(8,128)(2,1)S(1)}, u32[]{:S(2)}, u32[]{:S(2)}) collective-permute-start(bf16[64,1280]{1,0:T(8,128)(2,1)S(1)} %collective-permute-done.refs_5_), channel_id=1, source_target_pairs={{0,2},{2,0},{6,10},{10,6},{14,12},{12,14},{8,4},{4,8},{1,3},{3,1},... | collective-permute-start | bytes 491528 | tf_op jit(solution)/shard_map/ppermute | solution.py:385
  17.9 0.2 collective-permute-done.8.refs_6_.refs_4_
  18.2 1.8 %collective-permute-start.12 = (bf16[64,1280]{1,0:T(8,128)(2,1)S(1)}, bf16[64,1280]{1,0:T(8,128)(2,1)S(1)}, u32[]{:S(2)}, u32[]{:S(2)}) collective-permute-start(bf16[64,1280]{1,0:T(8,128)(2,1)S(1)} %collective-permute-done.8.refs_6_.refs_4_), channel_id=1, source_target_pairs={{2,6},{6,2},{10,14},{14,10},{12,8},{8,12},{4,0},{0,4},{3,7},{7,3},... | collective-permute-start | bytes 491528 | tf_op jit(solution)/shard_map/ppermute | solution.py:383
  20.0 0.0 collective-permute-done.3.refs_6_
  20.0 1.5 %collective-permute-start.4 = (bf16[64,1280]{1,0:T(8,128)(2,1)S(1)}, bf16[64,1280]{1,0:T(8,128)(2,1)S(1)}, u32[]{:S(2)}, u32[]{:S(2)}) collective-permute-start(bf16[64,1280]{1,0:T(8,128)(2,1)S(1)} %collective-permute-done.3.refs_6_), channel_id=1, source_target_pairs={{0,2},{2,0},{6,10},{10,6},{14,12},{12,14},{8,4},{4,8},{1,3},{3,1},... | collective-permute-start | bytes 491528 | tf_op jit(solution)/shard_map/ppermute | solution.py:382
  21.5 2.5 %shard_map.85 = (f32[256,512]{1,0:T(8,128)S(1)}, f32[256,512]{1,0:T(8,128)S(1)}, bf16[256,512]{1,0:T(8,128)(2,1)S(1)}) custom-call(bf16[256,4096]{1,0:T(8,128)(2,1)S(1)} %copy-done, bf16[4096,1024]{1,0:T(8,128)(2,1)S(1)} %bitcast.5, s32[8,512]{1,0:T(8,128)S(1)} %shard_map.84.bounds_ref.refs_2_.refs_1_), custom_call_target="tpu_custom_call" | custom-call | bytes 4194304 | tf_op jit(solution)/shard_map/pallas_call | solution.py:223
  23.9 0.0 collective-permute-done.10.refs_10_.refs_3_
  23.9 0.6 %collective-permute-start.11 = (bf16[64,1280]{1,0:T(8,128)(2,1)S(1)}, bf16[64,1280]{1,0:T(8,128)(2,1)S(1)}, u32[]{:S(2)}, u32[]{:S(2)}) collective-permute-start(bf16[64,1280]{1,0:T(8,128)(2,1)S(1)} %collective-permute-done.10.refs_10_.refs_3_), channel_id=1, source_target_pairs={{0,2},{2,0},{6,10},{10,6},{14,12},{12,14},{8,4},{4,8},{1,3},{3,1},... | collective-permute-start | bytes 491528 | tf_op jit(solution)/shard_map/ppermute | solution.py:384
  24.5 0.0 collective-permute-done.1.refs_2_
  24.6 0.4 %collective-permute-start.5 = (bf16[64,1280]{1,0:T(8,128)(2,1)S(1)}, bf16[64,1280]{1,0:T(8,128)(2,1)S(1)}, u32[]{:S(2)}, u32[]{:S(2)}) collective-permute-start(bf16[64,1280]{1,0:T(8,128)(2,1)S(1)} %collective-permute-done.1.refs_2_), channel_id=1, source_target_pairs={{2,6},{6,2},{10,14},{14,10},{12,8},{8,12},{4,0},{0,4},{3,7},{7,3},... | collective-permute-start | bytes 491528 | tf_op jit(solution)/shard_map/ppermute | solution.py:385
  24.9 0.0 collective-permute-done.12.refs_8_.refs_6_
  24.9 1.5 %collective-permute-start.13 = (bf16[64,1280]{1,0:T(8,128)(2,1)S(1)}, bf16[64,1280]{1,0:T(8,128)(2,1)S(1)}, u32[]{:S(2)}, u32[]{:S(2)}) collective-permute-start(bf16[64,1280]{1,0:T(8,128)(2,1)S(1)} %collective-permute-done.12.refs_8_.refs_6_), channel_id=1, source_target_pairs={{0,2},{2,0},{6,10},{10,6},{14,12},{12,14},{8,4},{4,8},{1,3},{3,1},... | collective-permute-start | bytes 491528 | tf_op jit(solution)/shard_map/ppermute | solution.py:390
  26.4 0.5 %collective-permute-done.4.refs_3_ = bf16[64,1280]{1,0:T(8,128)(2,1)S(1)} collective-permute-done((bf16[64,1280]{1,0:T(8,128)(2,1)S(1)}, bf16[64,1280]{1,0:T(8,128)(2,1)S(1)}, u32[]{:S(2)}, u32[]{:S(2)}) %collective-permute-start.4) | collective-permute-done | bytes 163872 | tf_op jit(solution)/shard_map/ppermute | solution.py:382
  27.0 1.2 %collective-permute-start.6 = (bf16[64,1280]{1,0:T(8,128)(2,1)S(1)}, bf16[64,1280]{1,0:T(8,128)(2,1)S(1)}, u32[]{:S(2)}, u32[]{:S(2)}) collective-permute-start(bf16[64,1280]{1,0:T(8,128)(2,1)S(1)} %collective-permute-done.4.refs_3_), channel_id=1, source_target_pairs={{2,6},{6,2},{10,14},{14,10},{12,8},{8,12},{4,0},{0,4},{3,7},{7,3},... | collective-permute-start | bytes 491528 | tf_op jit(solution)/shard_map/ppermute | solution.py:389
  28.2 2.3 %collective-permute-done.14.refs_1_.refs_0_ = bf16[4112,128]{1,0:T(8,128)(2,1)S(1)} collective-permute-done((bf16[4112,128]{1,0:T(8,128)(2,1)S(1)}, bf16[4112,128]{1,0:T(8,128)(2,1)S(1)}, u32[]{:S(2)}, u32[]{:S(2)}) %collective-permute-start.14) | collective-permute-done | bytes 1052704 | tf_op jit(solution)/shard_map/ppermute | solution.py:393
  30.5 0.7 %shard_map.86 = (f32[256,128]{1,0:T(8,128)S(1)}, f32[256,128]{1,0:T(8,128)S(1)}) custom-call(bf16[256,4096]{1,0:T(8,128)(2,1)S(1)} %copy-done, bf16[4112,128]{1,0:T(8,128)(2,1)S(1)} %collective-permute-done.14.refs_1_.refs_0_, s32[8,512]{1,0:T(8,128)S(1)} %shard_map.84.bounds_ref.refs_2_.refs_1_, bf16[64,1280]{1,0:T(8,128)(2,1)S(1)} %get-tuple-element.34.refs_3_, ...), custom_call_target="tpu_custom_call" | custom-call | flops 8589934592 | bytes 16777216 | tf_op jit(solution)/shard_map/pallas_call | solution.py:317
  31.3 0.1 collective-permute-start.19
  31.4 0.0 collective-permute-done.11.refs_7_.refs_5_
  31.4 0.0 collective-permute-done.5.refs_4_
  31.4 0.4 collective-permute-done.13.refs_9_.refs_7_
  31.8 0.5 %collective-permute-done.6.refs_5_ = bf16[64,1280]{1,0:T(8,128)(2,1)S(1)} collective-permute-done((bf16[64,1280]{1,0:T(8,128)(2,1)S(1)}, bf16[64,1280]{1,0:T(8,128)(2,1)S(1)}, u32[]{:S(2)}, u32[]{:S(2)}) %collective-permute-start.6) | collective-permute-done | bytes 163872 | tf_op jit(solution)/shard_map/ppermute | solution.py:389
  32.3 0.5 %shard_map.88 = bf16[128,128]{1,0:T(8,128)(2,1)S(1)} custom-call(bf16[4112,128]{1,0:T(8,128)(2,1)S(1)} %collective-permute-done.14.refs_1_.refs_0_, s32[8,512]{1,0:T(8,128)S(1)} %shard_map.84.bounds_ref.refs_2_.refs_1_, bf16[64,1280]{1,0:T(8,128)(2,1)S(1)} %collective-permute-done.1.refs_2_, bf16[64,1280]{1,0:T(8,128)(2,1)S(1)} %collective-permute-done.4.refs_3_, ...), custom_call_target="tpu_custom_call" | custom-call | flops 8589934592 | bytes 16777216 | tf_op jit(solution)/shard_map/pallas_call | solution.py:317
  32.8 0.8 %collective-permute-start.17 = (bf16[128,128]{1,0:T(8,128)(2,1)S(1)}, bf16[128,128]{1,0:T(8,128)(2,1)S(1)}, u32[]{:S(2)}, u32[]{:S(2)}) collective-permute-start(bf16[128,128]{1,0:T(8,128)(2,1)S(1)} %shard_map.88), channel_id=1, source_target_pairs={{0,17},{1,16},{16,1},{17,0},{2,19},{3,18},{18,3},{19,2},{4,21},{5,... | collective-permute-start | bytes 98312 | tf_op jit(solution)/shard_map/ppermute | solution.py:412
  33.6 0.5 %collective-permute-start.18 = (bf16[128,128]{1,0:T(8,128)(2,1)S(1)}, bf16[128,128]{1,0:T(8,128)(2,1)S(1)}, u32[]{:S(2)}, u32[]{:S(2)}) collective-permute-start(bf16[128,128]{1,0:T(8,128)(2,1)S(1)} %shard_map.88), channel_id=1, source_target_pairs={{0,16},{16,0},{1,17},{17,1},{2,18},{18,2},{3,19},{19,3},{4,20},{20... | collective-permute-start | bytes 98312 | tf_op jit(solution)/shard_map/ppermute | solution.py:413
  34.2 0.5 %shard_map.87 = (f32[64,128]{1,0:T(8,128)S(1)}, f32[64,128]{1,0:T(8,128)S(1)}) custom-call(bf16[256,4096]{1,0:T(8,128)(2,1)S(1)} %copy-done, s32[8,512]{1,0:T(8,128)S(1)} %shard_map.84.bounds_ref.refs_2_.refs_1_, bf16[64,1280]{1,0:T(8,128)(2,1)S(1)} %collective-permute-done.1.refs_2_, bf16[64,1280]{1,0:T(8,128)(2,1)S(1)} %collective-permute-done.4.refs_3_, ...), custom_call_target="tpu_custom_call" | custom-call | bytes 4194304 | tf_op jit(solution)/shard_map/pallas_call | solution.py:317
  34.7 0.7 %collective-permute-start.15 = (f32[64,128]{1,0:T(8,128)S(1)}, f32[64,128]{1,0:T(8,128)S(1)}, u32[]{:S(2)}, u32[]{:S(2)}) collective-permute-start(f32[64,128]{1,0:T(8,128)S(1)} %get-tuple-element.38.top), channel_id=1, source_target_pairs={{0,1},{1,0},{2,3},{3,2},{4,5},{5,4},{6,7},{7,6},{8,9},{9,8},{10,11... | collective-permute-start | bytes 98312 | tf_op jit(solution)/shard_map/ppermute | solution.py:414
  35.4 0.1 collective-permute-start.16
  35.5 0.9 %collective-permute-done.17.three = bf16[128,128]{1,0:T(8,128)(2,1)S(1)} collective-permute-done((bf16[128,128]{1,0:T(8,128)(2,1)S(1)}, bf16[128,128]{1,0:T(8,128)(2,1)S(1)}, u32[]{:S(2)}, u32[]{:S(2)}) %collective-permute-start.17) | collective-permute-done | bytes 32800 | tf_op jit(solution)/shard_map/ppermute | solution.py:412
  36.4 1.2 %collective-permute-done.18.two = bf16[128,128]{1,0:T(8,128)(2,1)S(1)} collective-permute-done((bf16[128,128]{1,0:T(8,128)(2,1)S(1)}, bf16[128,128]{1,0:T(8,128)(2,1)S(1)}, u32[]{:S(2)}, u32[]{:S(2)}) %collective-permute-start.18) | collective-permute-done | bytes 32800 | tf_op jit(solution)/shard_map/ppermute | solution.py:413
  37.6 0.0 collective-permute-done.15.one_top
  37.6 0.0 collective-permute-done.16.one_low
  37.6 0.0 collective-permute-done.19.far_ref
  37.6 1.1 %shard_map.89 = bf16[256,512]{1,0:T(8,128)(2,1)} custom-call(bf16[256,512]{1,0:T(8,128)(2,1)S(1)} %get-tuple-element.30.mask_ref, f32[64,128]{1,0:T(8,128)S(1)} %get-tuple-element.38.top, f32[64,128]{1,0:T(8,128)S(1)} %get-tuple-element.39.low, f32[64,128]{1,0:T(8,128)S(1)} %collective-permute-done.15.one_top, ...), custom_call_target="tpu_custom_call" | custom-call | tf_op jit(solution)/shard_map/pallas_call | solution.py:417
  (7 shorter events, 0.0 us)
Async XLA Ops:
  0.0 5.8 %copy-start = (bf16[256,4096]{1,0:T(8,128)(2,1)S(1)}, bf16[256,4096]{1,0:T(8,128)(2,1)}, u32[]{:S(2)}) copy-start(bf16[256,4096]{1,0:T(8,128)(2,1)} %refs_0_.1) | copy-start | bytes 6291460
  1.2 8.2 %collective-permute-start.7 = (bf16[64,1280]{1,0:T(8,128)(2,1)S(1)}, bf16[64,1280]{1,0:T(8,128)(2,1)S(1)}, u32[]{:S(2)}, u32[]{:S(2)}) collective-permute-start(bf16[64,1280]{1,0:T(8,128)(2,1)S(1)} %get-tuple-element.35.refs_7_.refs_0_), channel_id=1, source_target_pairs={{2,6},{6,2},{10,14},{14,10},{12,8},{8,12},{4,0},{0,4},{3,7},{7,3},... | collective-permute-start | bytes 491528 | tf_op jit(solution)/shard_map/ppermute | solution.py:383
  4.3 6.6 %collective-permute-start.2 = (bf16[64,1280]{1,0:T(8,128)(2,1)S(1)}, bf16[64,1280]{1,0:T(8,128)(2,1)S(1)}, u32[]{:S(2)}, u32[]{:S(2)}) collective-permute-start(bf16[64,1280]{1,0:T(8,128)(2,1)S(1)} %get-tuple-element.34.refs_3_), channel_id=1, source_target_pairs={{0,2},{2,0},{6,10},{10,6},{14,12},{12,14},{8,4},{4,8},{1,3},{3,1},... | collective-permute-start | bytes 491528 | tf_op jit(solution)/shard_map/ppermute | solution.py:382
  6.1 24.5 %collective-permute-start.14 = (bf16[4112,128]{1,0:T(8,128)(2,1)S(1)}, bf16[4112,128]{1,0:T(8,128)(2,1)S(1)}, u32[]{:S(2)}, u32[]{:S(2)}) collective-permute-start(bf16[4112,128]{1,0:T(8,128)(2,1)S(1)} %get-tuple-element.36), channel_id=1, source_target_pairs={{0,16},{16,0},{1,17},{17,1},{2,18},{18,2},{3,19},{19,3},{4,20},{20... | collective-permute-start | bytes 3158024 | tf_op jit(solution)/shard_map/ppermute | solution.py:393
  7.7 13.8 %slice-start = ((s8[8388608]{0:T(1024)(128)(4,1)}), s8[4194304]{0:T(1024)(128)(4,1)S(1)}, s32[]{:S(2)}) async-start(s8[8388608]{0:T(1024)(128)(4,1)} %bitcast.4), calls=%async_computation | async-start | bytes 8388608
  7.7 13.8 %slice-start.1 = ((s8[8388608]{0:T(1024)(128)(4,1)}), s8[4194304]{0:T(1024)(128)(4,1)S(1)}, s32[]{:S(2)}) async-start(s8[8388608]{0:T(1024)(128)(4,1)} %bitcast.4), calls=%async_computation.1 | async-start | bytes 8388608
  7.7 7.1 %collective-permute-start.9 = (bf16[64,1280]{1,0:T(8,128)(2,1)S(1)}, bf16[64,1280]{1,0:T(8,128)(2,1)S(1)}, u32[]{:S(2)}, u32[]{:S(2)}) collective-permute-start(bf16[64,1280]{1,0:T(8,128)(2,1)S(1)} %get-tuple-element.35.refs_7_.refs_0_), channel_id=1, source_target_pairs={{0,2},{2,0},{6,10},{10,6},{14,12},{12,14},{8,4},{4,8},{1,3},{3,1},... | collective-permute-start | bytes 491528 | tf_op jit(solution)/shard_map/ppermute | solution.py:384
  8.2 8.3 %collective-permute-start = (bf16[64,1280]{1,0:T(8,128)(2,1)S(1)}, bf16[64,1280]{1,0:T(8,128)(2,1)S(1)}, u32[]{:S(2)}, u32[]{:S(2)}) collective-permute-start(bf16[64,1280]{1,0:T(8,128)(2,1)S(1)} %get-tuple-element.34.refs_3_), channel_id=1, source_target_pairs={{2,6},{6,2},{10,14},{14,10},{12,8},{8,12},{4,0},{0,4},{3,7},{7,3},... | collective-permute-start | bytes 491528 | tf_op jit(solution)/shard_map/ppermute | solution.py:385
  9.4 8.8 %collective-permute-start.8 = (bf16[64,1280]{1,0:T(8,128)(2,1)S(1)}, bf16[64,1280]{1,0:T(8,128)(2,1)S(1)}, u32[]{:S(2)}, u32[]{:S(2)}) collective-permute-start(bf16[64,1280]{1,0:T(8,128)(2,1)S(1)} %collective-permute-done.7.refs_9_.refs_2_), channel_id=1, source_target_pairs={{0,2},{2,0},{6,10},{10,6},{14,12},{12,14},{8,4},{4,8},{1,3},{3,1},... | collective-permute-start | bytes 491528 | tf_op jit(solution)/shard_map/ppermute | solution.py:383
  10.9 9.1 %collective-permute-start.3 = (bf16[64,1280]{1,0:T(8,128)(2,1)S(1)}, bf16[64,1280]{1,0:T(8,128)(2,1)S(1)}, u32[]{:S(2)}, u32[]{:S(2)}) collective-permute-start(bf16[64,1280]{1,0:T(8,128)(2,1)S(1)} %collective-permute-done.2.refs_4_), channel_id=1, source_target_pairs={{2,6},{6,2},{10,14},{14,10},{12,8},{8,12},{4,0},{0,4},{3,7},{7,3},... | collective-permute-start | bytes 491528 | tf_op jit(solution)/shard_map/ppermute | solution.py:382
  14.8 9.1 %collective-permute-start.10 = (bf16[64,1280]{1,0:T(8,128)(2,1)S(1)}, bf16[64,1280]{1,0:T(8,128)(2,1)S(1)}, u32[]{:S(2)}, u32[]{:S(2)}) collective-permute-start(bf16[64,1280]{1,0:T(8,128)(2,1)S(1)} %collective-permute-done.9.refs_8_.refs_1_), channel_id=1, source_target_pairs={{2,6},{6,2},{10,14},{14,10},{12,8},{8,12},{4,0},{0,4},{3,7},{7,3},... | collective-permute-start | bytes 491528 | tf_op jit(solution)/shard_map/ppermute | solution.py:384
  16.4 8.1 %collective-permute-start.1 = (bf16[64,1280]{1,0:T(8,128)(2,1)S(1)}, bf16[64,1280]{1,0:T(8,128)(2,1)S(1)}, u32[]{:S(2)}, u32[]{:S(2)}) collective-permute-start(bf16[64,1280]{1,0:T(8,128)(2,1)S(1)} %collective-permute-done.refs_5_), channel_id=1, source_target_pairs={{0,2},{2,0},{6,10},{10,6},{14,12},{12,14},{8,4},{4,8},{1,3},{3,1},... | collective-permute-start | bytes 491528 | tf_op jit(solution)/shard_map/ppermute | solution.py:385
  18.2 6.8 %collective-permute-start.12 = (bf16[64,1280]{1,0:T(8,128)(2,1)S(1)}, bf16[64,1280]{1,0:T(8,128)(2,1)S(1)}, u32[]{:S(2)}, u32[]{:S(2)}) collective-permute-start(bf16[64,1280]{1,0:T(8,128)(2,1)S(1)} %collective-permute-done.8.refs_6_.refs_4_), channel_id=1, source_target_pairs={{2,6},{6,2},{10,14},{14,10},{12,8},{8,12},{4,0},{0,4},{3,7},{7,3},... | collective-permute-start | bytes 491528 | tf_op jit(solution)/shard_map/ppermute | solution.py:383
  20.0 7.0 %collective-permute-start.4 = (bf16[64,1280]{1,0:T(8,128)(2,1)S(1)}, bf16[64,1280]{1,0:T(8,128)(2,1)S(1)}, u32[]{:S(2)}, u32[]{:S(2)}) collective-permute-start(bf16[64,1280]{1,0:T(8,128)(2,1)S(1)} %collective-permute-done.3.refs_6_), channel_id=1, source_target_pairs={{0,2},{2,0},{6,10},{10,6},{14,12},{12,14},{8,4},{4,8},{1,3},{3,1},... | collective-permute-start | bytes 491528 | tf_op jit(solution)/shard_map/ppermute | solution.py:382
  23.9 7.4 %collective-permute-start.11 = (bf16[64,1280]{1,0:T(8,128)(2,1)S(1)}, bf16[64,1280]{1,0:T(8,128)(2,1)S(1)}, u32[]{:S(2)}, u32[]{:S(2)}) collective-permute-start(bf16[64,1280]{1,0:T(8,128)(2,1)S(1)} %collective-permute-done.10.refs_10_.refs_3_), channel_id=1, source_target_pairs={{0,2},{2,0},{6,10},{10,6},{14,12},{12,14},{8,4},{4,8},{1,3},{3,1},... | collective-permute-start | bytes 491528 | tf_op jit(solution)/shard_map/ppermute | solution.py:384
  24.6 6.8 %collective-permute-start.5 = (bf16[64,1280]{1,0:T(8,128)(2,1)S(1)}, bf16[64,1280]{1,0:T(8,128)(2,1)S(1)}, u32[]{:S(2)}, u32[]{:S(2)}) collective-permute-start(bf16[64,1280]{1,0:T(8,128)(2,1)S(1)} %collective-permute-done.1.refs_2_), channel_id=1, source_target_pairs={{2,6},{6,2},{10,14},{14,10},{12,8},{8,12},{4,0},{0,4},{3,7},{7,3},... | collective-permute-start | bytes 491528 | tf_op jit(solution)/shard_map/ppermute | solution.py:385
  24.9 6.8 %collective-permute-start.13 = (bf16[64,1280]{1,0:T(8,128)(2,1)S(1)}, bf16[64,1280]{1,0:T(8,128)(2,1)S(1)}, u32[]{:S(2)}, u32[]{:S(2)}) collective-permute-start(bf16[64,1280]{1,0:T(8,128)(2,1)S(1)} %collective-permute-done.12.refs_8_.refs_6_), channel_id=1, source_target_pairs={{0,2},{2,0},{6,10},{10,6},{14,12},{12,14},{8,4},{4,8},{1,3},{3,1},... | collective-permute-start | bytes 491528 | tf_op jit(solution)/shard_map/ppermute | solution.py:390
  27.0 5.3 %collective-permute-start.6 = (bf16[64,1280]{1,0:T(8,128)(2,1)S(1)}, bf16[64,1280]{1,0:T(8,128)(2,1)S(1)}, u32[]{:S(2)}, u32[]{:S(2)}) collective-permute-start(bf16[64,1280]{1,0:T(8,128)(2,1)S(1)} %collective-permute-done.4.refs_3_), channel_id=1, source_target_pairs={{2,6},{6,2},{10,14},{14,10},{12,8},{8,12},{4,0},{0,4},{3,7},{7,3},... | collective-permute-start | bytes 491528 | tf_op jit(solution)/shard_map/ppermute | solution.py:389
  31.3 6.3 %collective-permute-start.19 = (f32[256,512]{1,0:T(8,128)S(1)}, f32[256,512]{1,0:T(8,128)S(1)}, u32[]{:S(2)}, u32[]{:S(2)}) collective-permute-start(f32[256,512]{1,0:T(8,128)S(1)} %get-tuple-element.44), channel_id=1, source_target_pairs={{0,1},{1,0},{2,3},{3,2},{4,5},{5,4},{6,7},{7,6},{8,9},{9,8},{10,11... | collective-permute-start | bytes 1572872 | tf_op jit(solution)/shard_map/ppermute | solution.py:406
  32.8 3.5 %collective-permute-start.17 = (bf16[128,128]{1,0:T(8,128)(2,1)S(1)}, bf16[128,128]{1,0:T(8,128)(2,1)S(1)}, u32[]{:S(2)}, u32[]{:S(2)}) collective-permute-start(bf16[128,128]{1,0:T(8,128)(2,1)S(1)} %shard_map.88), channel_id=1, source_target_pairs={{0,17},{1,16},{16,1},{17,0},{2,19},{3,18},{18,3},{19,2},{4,21},{5,... | collective-permute-start | bytes 98312 | tf_op jit(solution)/shard_map/ppermute | solution.py:412
  33.6 3.9 %collective-permute-start.18 = (bf16[128,128]{1,0:T(8,128)(2,1)S(1)}, bf16[128,128]{1,0:T(8,128)(2,1)S(1)}, u32[]{:S(2)}, u32[]{:S(2)}) collective-permute-start(bf16[128,128]{1,0:T(8,128)(2,1)S(1)} %shard_map.88), channel_id=1, source_target_pairs={{0,16},{16,0},{1,17},{17,1},{2,18},{18,2},{3,19},{19,3},{4,20},{20... | collective-permute-start | bytes 98312 | tf_op jit(solution)/shard_map/ppermute | solution.py:413
  34.7 2.9 %collective-permute-start.15 = (f32[64,128]{1,0:T(8,128)S(1)}, f32[64,128]{1,0:T(8,128)S(1)}, u32[]{:S(2)}, u32[]{:S(2)}) collective-permute-start(f32[64,128]{1,0:T(8,128)S(1)} %get-tuple-element.38.top), channel_id=1, source_target_pairs={{0,1},{1,0},{2,3},{3,2},{4,5},{5,4},{6,7},{7,6},{8,9},{9,8},{10,11... | collective-permute-start | bytes 98312 | tf_op jit(solution)/shard_map/ppermute | solution.py:414
  35.4 2.2 %collective-permute-start.16 = (f32[64,128]{1,0:T(8,128)S(1)}, f32[64,128]{1,0:T(8,128)S(1)}, u32[]{:S(2)}, u32[]{:S(2)}) collective-permute-start(f32[64,128]{1,0:T(8,128)S(1)} %get-tuple-element.39.low), channel_id=1, source_target_pairs={{0,1},{1,0},{2,3},{3,2},{4,5},{5,4},{6,7},{7,6},{8,9},{9,8},{10,11... | collective-permute-start | bytes 98312 | tf_op jit(solution)/shard_map/ppermute | solution.py:414

commit v21 on v17

--- a/solution.py
+++ b/solution.py
@@ -308,7 +308,7 @@
     elif sides == (1,):
         out = (jax.ShapeDtypeStruct((count // 2, 2 * rank), BF16),)
     else:
-        out = (jax.ShapeDtypeStruct((count // 4, 2 * rank), F32),) * 2
+        out = (jax.ShapeDtypeStruct((count // 2, 2 * rank), F32),)
     operands = [*rows, bounds, *pieces, *starts]
     return pl.pallas_call(
         functools.partial(rank_kernel, sides, groups, depth, last),
@@ -320,12 +320,11 @@
     )(*operands)
 
 
-def final_kernel(bounds_ref, top, low, one_top, one_low, two, three, near_ref, far_ref, *refs):
+def final_kernel(bounds_ref, mine, one, two, three, near_ref, far_ref, *refs):
     factors, out_ref = refs[:-1], refs[-1]
     rank, width = factors[0].shape[0], out_ref.shape[1]
     begin = factors[0].shape[1] - width
-    here = jnp.concatenate([top[...] + one_top[...], low[...] + one_low[...]], axis=0)
-    packed = here + (two[...].astype(F32) + three[...].astype(F32))
+    packed = (mine[...] + one[...]) + (two[...].astype(F32) + three[...].astype(F32))
     turned = pltpu.roll(packed, rank, 1)
     lane = lax.broadcasted_iota(I32, packed.shape, 1)
     values = jnp.concatenate(
@@ -404,7 +403,7 @@
     mine = rank_call((0,), late, depth, rows, (hidden,), bounds, pieces, (start_mine,))
 
     two = lax.ppermute(theirs, "groups", swap)
-    three = lax.ppermute(theirs, ("groups", "tensor"), [(0, 3), (1, 2), (2, 1), (3, 0)])
+    three = lax.ppermute(two, "tensor", swap)
     one = [lax.ppermute(part, "tensor", swap) for part in mine]
 
     operands = [bounds, *mine, *one, two, three, near, far, *seconds]

time: 37.9 us -> 38.1 us (level)
  waiting for transfers between devices: 11.3 us -> 12.3 us
  starting transfers between devices: 19.5 us -> 18.8 us
    ppermute x2 -> x1, starting transfers between devices: 0.82 us -> 0.07 us  [per_device(): one = [lax.ppermute(part, 'tensor', swap) for part in mine]]
    ppermute x1, waiting for transfers between devices: 1.08 us -> 1.82 us  [per_device(): two = lax.ppermute(theirs, 'groups', swap)]
  transfers between devices with their start and end apart: 20 -> 19, of which waited for: 8 -> 8; matrix products, arithmetic and copies ran while one was open for 0% -> 0% of each run, Pallas kernels for 12% -> 12%
where the time goes in v21:
time: 38.1 us; the launch traced here: 37.9 us
  starting transfers between devices  18.8 us (49%)
  waiting for transfers between devices  12.3 us (32%)
  Pallas kernels  6.77 us (18%)
    ppermute x3, starting transfers between devices, per_device(): d = lax.ppermute(behind[1], 'batch', backward)  5.32 us
    ppermute x3, waiting for transfers between devices, per_device(): b = lax.ppermute(ahead[1], 'batch', forward)  3.51 us
    ppermute x3, starting transfers between devices, per_device(): b = lax.ppermute(ahead[1], 'batch', forward)  3.3 us
    ppermute x3, starting transfers between devices, per_device(): c = lax.ppermute(behind[0], 'batch', backward)  2.84 us
    ppermute x1, waiting for transfers between devices, per_device(): other = lax.ppermute(to_other, 'groups', swap)  2.53 us
    pallas_call x1, Pallas kernels, base_call(): pl.pallas_call(base_kernel, out_shape=(out, out), in_specs=[VMEM] * 2, ou...  2.35 us
    ppermute x1, starting transfers between devices, per_device(): other = lax.ppermute(to_other, 'groups', swap)  2.03 us
    pallas_call x3, Pallas kernels, rank_call(): pl.pallas_call(functools.partial(rank_kernel, sides, groups, depth, last)...  1.83 us
  transfers between devices with their start and end apart: 19, of which 8 were waited for; matrix products, arithmetic and copies ran while one was open for 0% of the time, Pallas kernels for 12%

profile of v21, /device:TPU:0, one launch (start us, length us, event | category | flops | bytes accessed | tf_op | source)
XLA Modules:
  0.0 37.9 jit_solution(18159179085906487796)
XLA Ops:
  0.0 1.2 %shard_map.82 = (bf16[64,1280]{1,0:T(8,128)(2,1)S(1)}, bf16[64,1280]{1,0:T(8,128)(2,1)S(1)}, s32[8,512]{1,0:T(8,128)S(1)}) custom-call(bf16[64,4096]{1,0:T(8,128)(2,1)} %bitcast.6, bf16[64,512]{1,0:T(8,128)(2,1)} %bitcast.7, s32[1,4]{1,0:T(1,128)} %demand_ref.1, s32[1,4]{1,0:T(1,128)} %lengths_ref.1, s32[8]{0:T(128)} %holder_ref.1, ...), custom_call_target="tpu_custom_call" | custom-call | flops 8589934592 | bytes 16777216 | tf_op jit(solution)/shard_map/pallas_call | solution.py:137
  1.2 3.1 %collective-permute-start.7 = (bf16[64,1280]{1,0:T(8,128)(2,1)S(1)}, bf16[64,1280]{1,0:T(8,128)(2,1)S(1)}, u32[]{:S(2)}, u32[]{:S(2)}) collective-permute-start(bf16[64,1280]{1,0:T(8,128)(2,1)S(1)} %get-tuple-element.31.refs_7_.refs_0_), channel_id=1, source_target_pairs={{2,0},{6,2},{10,6},{14,10},{12,14},{8,12},{4,8},{0,4},{3,1},{7,3},... | collective-permute-start | bytes 491528 | tf_op jit(solution)/shard_map/ppermute | solution.py:376
  4.3 0.0 collective-permute-start.2
  4.3 0.0 copy-done
  4.3 0.3 shard_map.83
  4.6 2.0 %collective-permute-start.14 = (bf16[4112,128]{1,0:T(8,128)(2,1)S(1)}, bf16[4112,128]{1,0:T(8,128)(2,1)S(1)}, u32[]{:S(2)}, u32[]{:S(2)}) collective-permute-start(bf16[4112,128]{1,0:T(8,128)(2,1)S(1)} %get-tuple-element.32), channel_id=1, source_target_pairs={{0,16},{16,0},{1,17},{17,1},{2,18},{18,2},{3,19},{19,3},{4,20},{20... | collective-permute-start | bytes 3158024 | tf_op jit(solution)/shard_map/ppermute | solution.py:386
  6.6 1.5 %collective-permute-start.9 = (bf16[64,1280]{1,0:T(8,128)(2,1)S(1)}, bf16[64,1280]{1,0:T(8,128)(2,1)S(1)}, u32[]{:S(2)}, u32[]{:S(2)}) collective-permute-start(bf16[64,1280]{1,0:T(8,128)(2,1)S(1)} %get-tuple-element.31.refs_7_.refs_0_), channel_id=1, source_target_pairs={{0,2},{2,6},{6,10},{10,14},{14,12},{12,8},{8,4},{4,0},{1,3},{3,7},... | collective-permute-start | bytes 491528 | tf_op jit(solution)/shard_map/ppermute | solution.py:377
  8.1 0.5 %collective-permute-start = (bf16[64,1280]{1,0:T(8,128)(2,1)S(1)}, bf16[64,1280]{1,0:T(8,128)(2,1)S(1)}, u32[]{:S(2)}, u32[]{:S(2)}) collective-permute-start(bf16[64,1280]{1,0:T(8,128)(2,1)S(1)} %get-tuple-element.30.refs_3_), channel_id=1, source_target_pairs={{2,0},{6,2},{10,6},{14,10},{12,14},{8,12},{4,8},{0,4},{3,1},{7,3},... | collective-permute-start | bytes 491528 | tf_op jit(solution)/shard_map/ppermute | solution.py:378
  8.6 0.0 collective-permute-done.7.refs_9_.refs_2_
  8.6 1.8 %collective-permute-start.8 = (bf16[64,1280]{1,0:T(8,128)(2,1)S(1)}, bf16[64,1280]{1,0:T(8,128)(2,1)S(1)}, u32[]{:S(2)}, u32[]{:S(2)}) collective-permute-start(bf16[64,1280]{1,0:T(8,128)(2,1)S(1)} %collective-permute-done.7.refs_9_.refs_2_), channel_id=1, source_target_pairs={{2,0},{6,2},{10,6},{14,10},{12,14},{8,12},{4,8},{0,4},{3,1},{7,3},... | collective-permute-start | bytes 491528 | tf_op jit(solution)/shard_map/ppermute | solution.py:376
  10.4 1.0 %collective-permute-done.2.refs_4_ = bf16[64,1280]{1,0:T(8,128)(2,1)S(1)} collective-permute-done((bf16[64,1280]{1,0:T(8,128)(2,1)S(1)}, bf16[64,1280]{1,0:T(8,128)(2,1)S(1)}, u32[]{:S(2)}, u32[]{:S(2)}) %collective-permute-start.2) | collective-permute-done | bytes 163872 | tf_op jit(solution)/shard_map/ppermute | solution.py:375
  11.4 0.0 collective-permute-start.3
  11.4 3.5 %collective-permute-done.9.refs_8_.refs_1_ = bf16[64,1280]{1,0:T(8,128)(2,1)S(1)} collective-permute-done((bf16[64,1280]{1,0:T(8,128)(2,1)S(1)}, bf16[64,1280]{1,0:T(8,128)(2,1)S(1)}, u32[]{:S(2)}, u32[]{:S(2)}) %collective-permute-start.9) | collective-permute-done | bytes 163872 | tf_op jit(solution)/shard_map/ppermute | solution.py:377
  14.9 0.3 collective-permute-start.10
  15.2 0.0 collective-permute-done.refs_5_
  15.2 1.7 %collective-permute-start.1 = (bf16[64,1280]{1,0:T(8,128)(2,1)S(1)}, bf16[64,1280]{1,0:T(8,128)(2,1)S(1)}, u32[]{:S(2)}, u32[]{:S(2)}) collective-permute-start(bf16[64,1280]{1,0:T(8,128)(2,1)S(1)} %collective-permute-done.refs_5_), channel_id=1, source_target_pairs={{2,0},{6,2},{10,6},{14,10},{12,14},{8,12},{4,8},{0,4},{3,1},{7,3},... | collective-permute-start | bytes 491528 | tf_op jit(solution)/shard_map/ppermute | solution.py:378
  16.9 1.1 %collective-permute-done.8.refs_6_.refs_4_ = bf16[64,1280]{1,0:T(8,128)(2,1)S(1)} collective-permute-done((bf16[64,1280]{1,0:T(8,128)(2,1)S(1)}, bf16[64,1280]{1,0:T(8,128)(2,1)S(1)}, u32[]{:S(2)}, u32[]{:S(2)}) %collective-permute-start.8) | collective-permute-done | bytes 163872 | tf_op jit(solution)/shard_map/ppermute | solution.py:376
  18.1 0.4 %collective-permute-start.12 = (bf16[64,1280]{1,0:T(8,128)(2,1)S(1)}, bf16[64,1280]{1,0:T(8,128)(2,1)S(1)}, u32[]{:S(2)}, u32[]{:S(2)}) collective-permute-start(bf16[64,1280]{1,0:T(8,128)(2,1)S(1)} %collective-permute-done.8.refs_6_.refs_4_), channel_id=1, source_target_pairs={{2,0},{6,2},{10,6},{14,10},{12,14},{8,12},{4,8},{0,4},{3,1},{7,3},... | collective-permute-start | bytes 491528 | tf_op jit(solution)/shard_map/ppermute | solution.py:376
  18.5 0.0 collective-permute-done.3.refs_6_
  18.5 1.6 %collective-permute-start.4 = (bf16[64,1280]{1,0:T(8,128)(2,1)S(1)}, bf16[64,1280]{1,0:T(8,128)(2,1)S(1)}, u32[]{:S(2)}, u32[]{:S(2)}) collective-permute-start(bf16[64,1280]{1,0:T(8,128)(2,1)S(1)} %collective-permute-done.3.refs_6_), channel_id=1, source_target_pairs={{0,2},{2,6},{6,10},{10,14},{14,12},{12,8},{8,4},{4,0},{1,3},{3,7},... | collective-permute-start | bytes 491528 | tf_op jit(solution)/shard_map/ppermute | solution.py:375
  20.1 0.0 slice-done
  20.1 0.0 slice-done.1
  20.1 2.3 %shard_map.85 = (f32[256,512]{1,0:T(8,128)S(1)}, f32[256,512]{1,0:T(8,128)S(1)}) custom-call(bf16[256,4096]{1,0:T(8,128)(2,1)S(1)} %copy-done, bf16[4096,1024]{1,0:T(8,128)(2,1)S(1)} %bitcast.5), custom_call_target="tpu_custom_call" | custom-call | bytes 4194304 | tf_op jit(solution)/shard_map/pallas_call | solution.py:219
  22.5 0.0 collective-permute-done.10.refs_10_.refs_3_
  22.5 1.5 %collective-permute-start.11 = (bf16[64,1280]{1,0:T(8,128)(2,1)S(1)}, bf16[64,1280]{1,0:T(8,128)(2,1)S(1)}, u32[]{:S(2)}, u32[]{:S(2)}) collective-permute-start(bf16[64,1280]{1,0:T(8,128)(2,1)S(1)} %collective-permute-done.10.refs_10_.refs_3_), channel_id=1, source_target_pairs={{0,2},{2,6},{6,10},{10,14},{14,12},{12,8},{8,4},{4,0},{1,3},{3,7},... | collective-permute-start | bytes 491528 | tf_op jit(solution)/shard_map/ppermute | solution.py:377
  24.0 0.0 collective-permute-done.1.refs_2_
  24.0 0.6 %collective-permute-start.5 = (bf16[64,1280]{1,0:T(8,128)(2,1)S(1)}, bf16[64,1280]{1,0:T(8,128)(2,1)S(1)}, u32[]{:S(2)}, u32[]{:S(2)}) collective-permute-start(bf16[64,1280]{1,0:T(8,128)(2,1)S(1)} %collective-permute-done.1.refs_2_), channel_id=1, source_target_pairs={{2,0},{6,2},{10,6},{14,10},{12,14},{8,12},{4,8},{0,4},{3,1},{7,3},... | collective-permute-start | bytes 491528 | tf_op jit(solution)/shard_map/ppermute | solution.py:378
  24.6 0.2 collective-permute-done.12.refs_8_.refs_6_
  24.8 0.9 %collective-permute-start.13 = (bf16[64,1280]{1,0:T(8,128)(2,1)S(1)}, bf16[64,1280]{1,0:T(8,128)(2,1)S(1)}, u32[]{:S(2)}, u32[]{:S(2)}) collective-permute-start(bf16[64,1280]{1,0:T(8,128)(2,1)S(1)} %collective-permute-done.12.refs_8_.refs_6_), channel_id=1, source_target_pairs={{2,0},{6,2},{10,6},{14,10},{12,14},{8,12},{4,8},{0,4},{3,1},{7,3},... | collective-permute-start | bytes 491528 | tf_op jit(solution)/shard_map/ppermute | solution.py:383
  25.7 0.0 collective-permute-done.4.refs_3_
  25.7 1.1 %collective-permute-start.6 = (bf16[64,1280]{1,0:T(8,128)(2,1)S(1)}, bf16[64,1280]{1,0:T(8,128)(2,1)S(1)}, u32[]{:S(2)}, u32[]{:S(2)}) collective-permute-start(bf16[64,1280]{1,0:T(8,128)(2,1)S(1)} %collective-permute-done.4.refs_3_), channel_id=1, source_target_pairs={{0,2},{2,6},{6,10},{10,14},{14,12},{12,8},{8,4},{4,0},{1,3},{3,7},... | collective-permute-start | bytes 491528 | tf_op jit(solution)/shard_map/ppermute | solution.py:382
  26.8 2.5 %collective-permute-done.14.refs_1_.refs_0_ = bf16[4112,128]{1,0:T(8,128)(2,1)S(1)} collective-permute-done((bf16[4112,128]{1,0:T(8,128)(2,1)S(1)}, bf16[4112,128]{1,0:T(8,128)(2,1)S(1)}, u32[]{:S(2)}, u32[]{:S(2)}) %collective-permute-start.14) | collective-permute-done | bytes 1052704 | tf_op jit(solution)/shard_map/ppermute | solution.py:386
  29.3 0.7 %shard_map.86 = (f32[256,128]{1,0:T(8,128)S(1)}, f32[256,128]{1,0:T(8,128)S(1)}) custom-call(bf16[256,4096]{1,0:T(8,128)(2,1)S(1)} %copy-done, bf16[4112,128]{1,0:T(8,128)(2,1)S(1)} %collective-permute-done.14.refs_1_.refs_0_, s32[8,512]{1,0:T(8,128)S(1)} %shard_map.84.refs_2_.refs_1_.bounds_ref, bf16[64,1280]{1,0:T(8,128)(2,1)S(1)} %get-tuple-element.30.refs_3_, ...), custom_call_target="tpu_custom_call" | custom-call | flops 8589934592 | bytes 16777216 | tf_op jit(solution)/shard_map/pallas_call | solution.py:313
  30.1 0.1 collective-permute-start.18
  30.2 0.0 collective-permute-done.11.refs_7_.refs_5_
  30.2 0.0 collective-permute-done.5.refs_4_
  30.2 0.9 %collective-permute-done.13.refs_9_.refs_7_ = bf16[64,1280]{1,0:T(8,128)(2,1)S(1)} collective-permute-done((bf16[64,1280]{1,0:T(8,128)(2,1)S(1)}, bf16[64,1280]{1,0:T(8,128)(2,1)S(1)}, u32[]{:S(2)}, u32[]{:S(2)}) %collective-permute-start.13) | collective-permute-done | bytes 163872 | tf_op jit(solution)/shard_map/ppermute | solution.py:383
  31.1 0.0 collective-permute-done.6.refs_5_
  31.1 0.5 %shard_map.88 = bf16[128,128]{1,0:T(8,128)(2,1)S(1)} custom-call(bf16[4112,128]{1,0:T(8,128)(2,1)S(1)} %collective-permute-done.14.refs_1_.refs_0_, s32[8,512]{1,0:T(8,128)S(1)} %shard_map.84.refs_2_.refs_1_.bounds_ref, bf16[64,1280]{1,0:T(8,128)(2,1)S(1)} %collective-permute-done.1.refs_2_, bf16[64,1280]{1,0:T(8,128)(2,1)S(1)} %collective-permute-done.4.refs_3_, ...), custom_call_target="tpu_custom_call" | custom-call | flops 8589934592 | bytes 16777216 | tf_op jit(solution)/shard_map/pallas_call | solution.py:313
  31.6 1.5 %collective-permute-start.16 = (bf16[128,128]{1,0:T(8,128)(2,1)S(1)}, bf16[128,128]{1,0:T(8,128)(2,1)S(1)}, u32[]{:S(2)}, u32[]{:S(2)}) collective-permute-start(bf16[128,128]{1,0:T(8,128)(2,1)S(1)} %shard_map.88), channel_id=1, source_target_pairs={{0,16},{16,0},{1,17},{17,1},{2,18},{18,2},{3,19},{19,3},{4,20},{20... | collective-permute-start | bytes 98312 | tf_op jit(solution)/shard_map/ppermute | solution.py:405
  33.1 0.5 %shard_map.87.mine = f32[128,128]{1,0:T(8,128)S(1)} custom-call(bf16[256,4096]{1,0:T(8,128)(2,1)S(1)} %copy-done, s32[8,512]{1,0:T(8,128)S(1)} %shard_map.84.refs_2_.refs_1_.bounds_ref, bf16[64,1280]{1,0:T(8,128)(2,1)S(1)} %collective-permute-done.1.refs_2_, bf16[64,1280]{1,0:T(8,128)(2,1)S(1)} %collective-permute-done.4.refs_3_, ...), custom_call_target="tpu_custom_call" | custom-call | bytes 4194304 | tf_op jit(solution)/shard_map/pallas_call | solution.py:313
  33.7 0.1 collective-permute-start.15
  33.8 1.8 %collective-permute-done.16.two = bf16[128,128]{1,0:T(8,128)(2,1)S(1)} collective-permute-done((bf16[128,128]{1,0:T(8,128)(2,1)S(1)}, bf16[128,128]{1,0:T(8,128)(2,1)S(1)}, u32[]{:S(2)}, u32[]{:S(2)}) %collective-permute-start.16) | collective-permute-done | bytes 32800 | tf_op jit(solution)/shard_map/ppermute | solution.py:405
  35.6 0.0 collective-permute-start.17
  35.6 1.2 %collective-permute-done.17.three = bf16[128,128]{1,0:T(8,128)(2,1)S(1)} collective-permute-done((bf16[128,128]{1,0:T(8,128)(2,1)S(1)}, bf16[128,128]{1,0:T(8,128)(2,1)S(1)}, u32[]{:S(2)}, u32[]{:S(2)}) %collective-permute-start.17) | collective-permute-done | bytes 32800 | tf_op jit(solution)/shard_map/ppermute | solution.py:406
  36.8 0.0 collective-permute-done.15.one
  36.8 0.0 collective-permute-done.18.far_ref
  36.8 1.1 %shard_map.89 = bf16[256,512]{1,0:T(8,128)(2,1)} custom-call(s32[8,512]{1,0:T(8,128)S(1)} %shard_map.84.refs_2_.refs_1_.bounds_ref, f32[128,128]{1,0:T(8,128)S(1)} %shard_map.87.mine, f32[128,128]{1,0:T(8,128)S(1)} %collective-permute-done.15.one, bf16[128,128]{1,0:T(8,128)(2,1)S(1)} %collective-permute-done.16.two, ...), custom_call_target="tpu_custom_call" | custom-call | tf_op jit(solution)/shard_map/pallas_call | solution.py:410
  (5 shorter events, 0.0 us)
Async XLA Ops:
  0.0 4.3 %copy-start = (bf16[256,4096]{1,0:T(8,128)(2,1)S(1)}, bf16[256,4096]{1,0:T(8,128)(2,1)}, u32[]{:S(2)}) copy-start(bf16[256,4096]{1,0:T(8,128)(2,1)} %refs_0_.1) | copy-start | bytes 6291460
  1.2 7.4 %collective-permute-start.7 = (bf16[64,1280]{1,0:T(8,128)(2,1)S(1)}, bf16[64,1280]{1,0:T(8,128)(2,1)S(1)}, u32[]{:S(2)}, u32[]{:S(2)}) collective-permute-start(bf16[64,1280]{1,0:T(8,128)(2,1)S(1)} %get-tuple-element.31.refs_7_.refs_0_), channel_id=1, source_target_pairs={{2,0},{6,2},{10,6},{14,10},{12,14},{8,12},{4,8},{0,4},{3,1},{7,3},... | collective-permute-start | bytes 491528 | tf_op jit(solution)/shard_map/ppermute | solution.py:376
  4.3 7.1 %collective-permute-start.2 = (bf16[64,1280]{1,0:T(8,128)(2,1)S(1)}, bf16[64,1280]{1,0:T(8,128)(2,1)S(1)}, u32[]{:S(2)}, u32[]{:S(2)}) collective-permute-start(bf16[64,1280]{1,0:T(8,128)(2,1)S(1)} %get-tuple-element.30.refs_3_), channel_id=1, source_target_pairs={{0,2},{2,6},{6,10},{10,14},{14,12},{12,8},{8,4},{4,0},{1,3},{3,7},... | collective-permute-start | bytes 491528 | tf_op jit(solution)/shard_map/ppermute | solution.py:375
  4.6 24.8 %collective-permute-start.14 = (bf16[4112,128]{1,0:T(8,128)(2,1)S(1)}, bf16[4112,128]{1,0:T(8,128)(2,1)S(1)}, u32[]{:S(2)}, u32[]{:S(2)}) collective-permute-start(bf16[4112,128]{1,0:T(8,128)(2,1)S(1)} %get-tuple-element.32), channel_id=1, source_target_pairs={{0,16},{16,0},{1,17},{17,1},{2,18},{18,2},{3,19},{19,3},{4,20},{20... | collective-permute-start | bytes 3158024 | tf_op jit(solution)/shard_map/ppermute | solution.py:386
  6.6 13.5 %slice-start = ((s8[8388608]{0:T(1024)(128)(4,1)}), s8[4194304]{0:T(1024)(128)(4,1)S(1)}, s32[]{:S(2)}) async-start(s8[8388608]{0:T(1024)(128)(4,1)} %bitcast.4), calls=%async_computation | async-start | bytes 8388608
  6.6 13.5 %slice-start.1 = ((s8[8388608]{0:T(1024)(128)(4,1)}), s8[4194304]{0:T(1024)(128)(4,1)S(1)}, s32[]{:S(2)}) async-start(s8[8388608]{0:T(1024)(128)(4,1)} %bitcast.4), calls=%async_computation.1 | async-start | bytes 8388608
  6.6 8.3 %collective-permute-start.9 = (bf16[64,1280]{1,0:T(8,128)(2,1)S(1)}, bf16[64,1280]{1,0:T(8,128)(2,1)S(1)}, u32[]{:S(2)}, u32[]{:S(2)}) collective-permute-start(bf16[64,1280]{1,0:T(8,128)(2,1)S(1)} %get-tuple-element.31.refs_7_.refs_0_), channel_id=1, source_target_pairs={{0,2},{2,6},{6,10},{10,14},{14,12},{12,8},{8,4},{4,0},{1,3},{3,7},... | collective-permute-start | bytes 491528 | tf_op jit(solution)/shard_map/ppermute | solution.py:377
  8.1 7.1 %collective-permute-start = (bf16[64,1280]{1,0:T(8,128)(2,1)S(1)}, bf16[64,1280]{1,0:T(8,128)(2,1)S(1)}, u32[]{:S(2)}, u32[]{:S(2)}) collective-permute-start(bf16[64,1280]{1,0:T(8,128)(2,1)S(1)} %get-tuple-element.30.refs_3_), channel_id=1, source_target_pairs={{2,0},{6,2},{10,6},{14,10},{12,14},{8,12},{4,8},{0,4},{3,1},{7,3},... | collective-permute-start | bytes 491528 | tf_op jit(solution)/shard_map/ppermute | solution.py:378
  8.6 9.5 %collective-permute-start.8 = (bf16[64,1280]{1,0:T(8,128)(2,1)S(1)}, bf16[64,1280]{1,0:T(8,128)(2,1)S(1)}, u32[]{:S(2)}, u32[]{:S(2)}) collective-permute-start(bf16[64,1280]{1,0:T(8,128)(2,1)S(1)} %collective-permute-done.7.refs_9_.refs_2_), channel_id=1, source_target_pairs={{2,0},{6,2},{10,6},{14,10},{12,14},{8,12},{4,8},{0,4},{3,1},{7,3},... | collective-permute-start | bytes 491528 | tf_op jit(solution)/shard_map/ppermute | solution.py:376
  11.4 7.1 %collective-permute-start.3 = (bf16[64,1280]{1,0:T(8,128)(2,1)S(1)}, bf16[64,1280]{1,0:T(8,128)(2,1)S(1)}, u32[]{:S(2)}, u32[]{:S(2)}) collective-permute-start(bf16[64,1280]{1,0:T(8,128)(2,1)S(1)} %collective-permute-done.2.refs_4_), channel_id=1, source_target_pairs={{0,2},{2,6},{6,10},{10,14},{14,12},{12,8},{8,4},{4,0},{1,3},{3,7},... | collective-permute-start | bytes 491528 | tf_op jit(solution)/shard_map/ppermute | solution.py:375
  14.9 7.6 %collective-permute-start.10 = (bf16[64,1280]{1,0:T(8,128)(2,1)S(1)}, bf16[64,1280]{1,0:T(8,128)(2,1)S(1)}, u32[]{:S(2)}, u32[]{:S(2)}) collective-permute-start(bf16[64,1280]{1,0:T(8,128)(2,1)S(1)} %collective-permute-done.9.refs_8_.refs_1_), channel_id=1, source_target_pairs={{0,2},{2,6},{6,10},{10,14},{14,12},{12,8},{8,4},{4,0},{1,3},{3,7},... | collective-permute-start | bytes 491528 | tf_op jit(solution)/shard_map/ppermute | solution.py:377
  15.2 8.7 %collective-permute-start.1 = (bf16[64,1280]{1,0:T(8,128)(2,1)S(1)}, bf16[64,1280]{1,0:T(8,128)(2,1)S(1)}, u32[]{:S(2)}, u32[]{:S(2)}) collective-permute-start(bf16[64,1280]{1,0:T(8,128)(2,1)S(1)} %collective-permute-done.refs_5_), channel_id=1, source_target_pairs={{2,0},{6,2},{10,6},{14,10},{12,14},{8,12},{4,8},{0,4},{3,1},{7,3},... | collective-permute-start | bytes 491528 | tf_op jit(solution)/shard_map/ppermute | solution.py:378
  18.1 6.7 %collective-permute-start.12 = (bf16[64,1280]{1,0:T(8,128)(2,1)S(1)}, bf16[64,1280]{1,0:T(8,128)(2,1)S(1)}, u32[]{:S(2)}, u32[]{:S(2)}) collective-permute-start(bf16[64,1280]{1,0:T(8,128)(2,1)S(1)} %collective-permute-done.8.refs_6_.refs_4_), channel_id=1, source_target_pairs={{2,0},{6,2},{10,6},{14,10},{12,14},{8,12},{4,8},{0,4},{3,1},{7,3},... | collective-permute-start | bytes 491528 | tf_op jit(solution)/shard_map/ppermute | solution.py:376
  18.5 7.1 %collective-permute-start.4 = (bf16[64,1280]{1,0:T(8,128)(2,1)S(1)}, bf16[64,1280]{1,0:T(8,128)(2,1)S(1)}, u32[]{:S(2)}, u32[]{:S(2)}) collective-permute-start(bf16[64,1280]{1,0:T(8,128)(2,1)S(1)} %collective-permute-done.3.refs_6_), channel_id=1, source_target_pairs={{0,2},{2,6},{6,10},{10,14},{14,12},{12,8},{8,4},{4,0},{1,3},{3,7},... | collective-permute-start | bytes 491528 | tf_op jit(solution)/shard_map/ppermute | solution.py:375
  22.5 7.7 %collective-permute-start.11 = (bf16[64,1280]{1,0:T(8,128)(2,1)S(1)}, bf16[64,1280]{1,0:T(8,128)(2,1)S(1)}, u32[]{:S(2)}, u32[]{:S(2)}) collective-permute-start(bf16[64,1280]{1,0:T(8,128)(2,1)S(1)} %collective-permute-done.10.refs_10_.refs_3_), channel_id=1, source_target_pairs={{0,2},{2,6},{6,10},{10,14},{14,12},{12,8},{8,4},{4,0},{1,3},{3,7},... | collective-permute-start | bytes 491528 | tf_op jit(solution)/shard_map/ppermute | solution.py:377
  24.0 6.2 %collective-permute-start.5 = (bf16[64,1280]{1,0:T(8,128)(2,1)S(1)}, bf16[64,1280]{1,0:T(8,128)(2,1)S(1)}, u32[]{:S(2)}, u32[]{:S(2)}) collective-permute-start(bf16[64,1280]{1,0:T(8,128)(2,1)S(1)} %collective-permute-done.1.refs_2_), channel_id=1, source_target_pairs={{2,0},{6,2},{10,6},{14,10},{12,14},{8,12},{4,8},{0,4},{3,1},{7,3},... | collective-permute-start | bytes 491528 | tf_op jit(solution)/shard_map/ppermute | solution.py:378
  24.8 6.3 %collective-permute-start.13 = (bf16[64,1280]{1,0:T(8,128)(2,1)S(1)}, bf16[64,1280]{1,0:T(8,128)(2,1)S(1)}, u32[]{:S(2)}, u32[]{:S(2)}) collective-permute-start(bf16[64,1280]{1,0:T(8,128)(2,1)S(1)} %collective-permute-done.12.refs_8_.refs_6_), channel_id=1, source_target_pairs={{2,0},{6,2},{10,6},{14,10},{12,14},{8,12},{4,8},{0,4},{3,1},{7,3},... | collective-permute-start | bytes 491528 | tf_op jit(solution)/shard_map/ppermute | solution.py:383
  25.7 5.4 %collective-permute-start.6 = (bf16[64,1280]{1,0:T(8,128)(2,1)S(1)}, bf16[64,1280]{1,0:T(8,128)(2,1)S(1)}, u32[]{:S(2)}, u32[]{:S(2)}) collective-permute-start(bf16[64,1280]{1,0:T(8,128)(2,1)S(1)} %collective-permute-done.4.refs_3_), channel_id=1, source_target_pairs={{0,2},{2,6},{6,10},{10,14},{14,12},{12,8},{8,4},{4,0},{1,3},{3,7},... | collective-permute-start | bytes 491528 | tf_op jit(solution)/shard_map/ppermute | solution.py:382
  30.1 6.7 %collective-permute-start.18 = (f32[256,512]{1,0:T(8,128)S(1)}, f32[256,512]{1,0:T(8,128)S(1)}, u32[]{:S(2)}, u32[]{:S(2)}) collective-permute-start(f32[256,512]{1,0:T(8,128)S(1)} %get-tuple-element.38), channel_id=1, source_target_pairs={{0,1},{1,0},{2,3},{3,2},{4,5},{5,4},{6,7},{7,6},{8,9},{9,8},{10,11... | collective-permute-start | bytes 1572872 | tf_op jit(solution)/shard_map/ppermute | solution.py:399
  31.6 4.0 %collective-permute-start.16 = (bf16[128,128]{1,0:T(8,128)(2,1)S(1)}, bf16[128,128]{1,0:T(8,128)(2,1)S(1)}, u32[]{:S(2)}, u32[]{:S(2)}) collective-permute-start(bf16[128,128]{1,0:T(8,128)(2,1)S(1)} %shard_map.88), channel_id=1, source_target_pairs={{0,16},{16,0},{1,17},{17,1},{2,18},{18,2},{3,19},{19,3},{4,20},{20... | collective-permute-start | bytes 98312 | tf_op jit(solution)/shard_map/ppermute | solution.py:405
  33.7 3.1 %collective-permute-start.15 = (f32[128,128]{1,0:T(8,128)S(1)}, f32[128,128]{1,0:T(8,128)S(1)}, u32[]{:S(2)}, u32[]{:S(2)}) collective-permute-start(f32[128,128]{1,0:T(8,128)S(1)} %shard_map.87.mine), channel_id=1, source_target_pairs={{0,1},{1,0},{2,3},{3,2},{4,5},{5,4},{6,7},{7,6},{8,9},{9,8},{10,11... | collective-permute-start | bytes 196616 | tf_op jit(solution)/shard_map/ppermute | solution.py:407
  35.6 1.2 %collective-permute-start.17 = (bf16[128,128]{1,0:T(8,128)(2,1)S(1)}, bf16[128,128]{1,0:T(8,128)(2,1)S(1)}, u32[]{:S(2)}, u32[]{:S(2)}) collective-permute-start(bf16[128,128]{1,0:T(8,128)(2,1)S(1)} %collective-permute-done.16.two), channel_id=1, source_target_pairs={{0,1},{1,0},{2,3},{3,2},{4,5},{5,4},{6,7},{7,6},{8,9},{9,8},{10,11... | collective-permute-start | bytes 98312 | tf_op jit(solution)/shard_map/ppermute | solution.py:406

commit v22 on v17

--- a/solution.py
+++ b/solution.py
@@ -368,10 +368,10 @@
         factor_in[0].T, factor_out[0], demand, lengths, holder_slot, jnp.asarray(table, I32), depth
     )
     to_other, bounds = rows_call(hidden, bounds)
-    bounds, first_later, second_later = lax.optimization_barrier((mark(bounds), first, second))
+    bounds, first_later = lax.optimization_barrier((mark(bounds), first))
 
     firsts, seconds = [first], [second]
-    ahead, behind = (first, second_later), (first_later, second)
+    ahead, behind = (first, second), (first_later, second)
     for step in range(1, full + 1):
         a = lax.ppermute(ahead[0], "batch", forward)
         d = lax.ppermute(behind[1], "batch", backward)

time: 37.9 us -> 37.9 us (level)
  starting transfers between devices: 19.5 us -> 20 us
  waiting for transfers between devices: 11.3 us -> 10.9 us
    ppermute x3, waiting for transfers between devices: 3.51 us -> 0.01 us  [per_device(): b = lax.ppermute(ahead[1], 'batch', forward)]
    ppermute x3, waiting for transfers between devices: 0.01 us -> 2.91 us  [per_device(): c = lax.ppermute(behind[0], 'batch', backward)]
    ppermute x3, starting transfers between devices: 2.84 us -> 5.02 us  [per_device(): c = lax.ppermute(behind[0], 'batch', backward)]
    ppermute x3, starting transfers between devices: 3.3 us -> 1.21 us  [per_device(): b = lax.ppermute(ahead[1], 'batch', forward)]
    ppermute x3, starting transfers between devices: 5.32 us -> 6.79 us  [per_device(): d = lax.ppermute(behind[1], 'batch', backward)]
    ppermute x3, starting transfers between devices: 1.58 us -> 0.44 us  [per_device(): a = lax.ppermute(ahead[0], 'batch', forward)]
    ppermute x1, waiting for transfers between devices: 0.01 us -> 1.09 us  [per_device(): firsts.append(lax.ppermute(ahead[0], 'batch', forward))]
    ppermute x3, waiting for transfers between devices: 1 us -> 0.01 us  [per_device(): a = lax.ppermute(ahead[0], 'batch', forward)]
  transfers between devices with their start and end apart: 20 -> 20, of which waited for: 8 -> 7; matrix products, arithmetic and copies ran while one was open for 0% -> 0% of each run, Pallas kernels for 12% -> 12%
where the time goes in v22:
time: 37.9 us; the launch traced here: 37.7 us
  starting transfers between devices  20 us (53%)
  waiting for transfers between devices  10.9 us (29%)
  Pallas kernels  6.77 us (18%)
    ppermute x3, starting transfers between devices, per_device(): d = lax.ppermute(behind[1], 'batch', backward)  6.79 us
    ppermute x3, starting transfers between devices, per_device(): c = lax.ppermute(behind[0], 'batch', backward)  5.02 us
    ppermute x1, waiting for transfers between devices, per_device(): other = lax.ppermute(to_other, 'groups', swap)  3.05 us
    ppermute x3, waiting for transfers between devices, per_device(): c = lax.ppermute(behind[0], 'batch', backward)  2.91 us
    pallas_call x1, Pallas kernels, base_call(): pl.pallas_call(base_kernel, out_shape=(out, out), in_specs=[VMEM] * 2, ou...  2.35 us
    ppermute x1, starting transfers between devices, per_device(): other = lax.ppermute(to_other, 'groups', swap)  2.03 us
    ppermute x3, waiting for transfers between devices, per_device(): d = lax.ppermute(behind[1], 'batch', backward)  1.94 us
    pallas_call x3, Pallas kernels, rank_call(): pl.pallas_call(functools.partial(rank_kernel, sides, groups, depth, last)...  1.83 us
  transfers between devices with their start and end apart: 20, of which 7 were waited for; matrix products, arithmetic and copies ran while one was open for 0% of the time, Pallas kernels for 12%

profile of v22, /device:TPU:0, one launch (start us, length us, event | category | flops | bytes accessed | tf_op | source)
XLA Modules:
  0.0 37.7 jit_solution(14218338008125322402)
XLA Ops:
  0.0 1.2 %shard_map.82 = (bf16[64,1280]{1,0:T(8,128)(2,1)S(1)}, bf16[64,1280]{1,0:T(8,128)(2,1)S(1)}, s32[8,512]{1,0:T(8,128)S(1)}) custom-call(bf16[64,4096]{1,0:T(8,128)(2,1)} %bitcast.6, bf16[64,512]{1,0:T(8,128)(2,1)} %bitcast.7, s32[1,4]{1,0:T(1,128)} %demand_ref.1, s32[1,4]{1,0:T(1,128)} %lengths_ref.1, s32[8]{0:T(128)} %holder_ref.1, ...), custom_call_target="tpu_custom_call" | custom-call | flops 8589934592 | bytes 16777216 | tf_op jit(solution)/shard_map/pallas_call | solution.py:137
  1.2 3.1 %collective-permute-start.7 = (bf16[64,1280]{1,0:T(8,128)(2,1)S(1)}, bf16[64,1280]{1,0:T(8,128)(2,1)S(1)}, u32[]{:S(2)}, u32[]{:S(2)}) collective-permute-start(bf16[64,1280]{1,0:T(8,128)(2,1)S(1)} %get-tuple-element.31.refs_7_.refs_0_), channel_id=1, source_target_pairs={{2,0},{6,2},{10,6},{14,10},{12,14},{8,12},{4,8},{0,4},{3,1},{7,3},... | collective-permute-start | bytes 491528 | tf_op jit(solution)/shard_map/ppermute | solution.py:377
  4.3 0.0 collective-permute-start.2
  4.3 0.3 shard_map.83
  4.6 2.0 %collective-permute-start.14 = (bf16[4112,128]{1,0:T(8,128)(2,1)S(1)}, bf16[4112,128]{1,0:T(8,128)(2,1)S(1)}, u32[]{:S(2)}, u32[]{:S(2)}) collective-permute-start(bf16[4112,128]{1,0:T(8,128)(2,1)S(1)} %get-tuple-element.32), channel_id=1, source_target_pairs={{0,16},{16,0},{1,17},{17,1},{2,18},{18,2},{3,19},{19,3},{4,20},{20... | collective-permute-start | bytes 3158024 | tf_op jit(solution)/shard_map/ppermute | solution.py:387
  6.6 1.6 %collective-permute-start = (bf16[64,1280]{1,0:T(8,128)(2,1)S(1)}, bf16[64,1280]{1,0:T(8,128)(2,1)S(1)}, u32[]{:S(2)}, u32[]{:S(2)}) collective-permute-start(bf16[64,1280]{1,0:T(8,128)(2,1)S(1)} %get-tuple-element.30.refs_3_), channel_id=1, source_target_pairs={{2,0},{6,2},{10,6},{14,10},{12,14},{8,12},{4,8},{0,4},{3,1},{7,3},... | collective-permute-start | bytes 491528 | tf_op jit(solution)/shard_map/ppermute | solution.py:379
  8.2 0.4 %collective-permute-start.9 = (bf16[64,1280]{1,0:T(8,128)(2,1)S(1)}, bf16[64,1280]{1,0:T(8,128)(2,1)S(1)}, u32[]{:S(2)}, u32[]{:S(2)}) collective-permute-start(bf16[64,1280]{1,0:T(8,128)(2,1)S(1)} %get-tuple-element.31.refs_7_.refs_0_), channel_id=1, source_target_pairs={{0,2},{2,6},{6,10},{10,14},{14,12},{12,8},{8,4},{4,0},{1,3},{3,7},... | collective-permute-start | bytes 491528 | tf_op jit(solution)/shard_map/ppermute | solution.py:378
  8.6 0.0 collective-permute-done.7.refs_9_.refs_2_
  8.6 2.0 %collective-permute-start.8 = (bf16[64,1280]{1,0:T(8,128)(2,1)S(1)}, bf16[64,1280]{1,0:T(8,128)(2,1)S(1)}, u32[]{:S(2)}, u32[]{:S(2)}) collective-permute-start(bf16[64,1280]{1,0:T(8,128)(2,1)S(1)} %collective-permute-done.7.refs_9_.refs_2_), channel_id=1, source_target_pairs={{2,0},{6,2},{10,6},{14,10},{12,14},{8,12},{4,8},{0,4},{3,1},{7,3},... | collective-permute-start | bytes 491528 | tf_op jit(solution)/shard_map/ppermute | solution.py:377
  10.6 0.0 collective-permute-done.2.refs_4_
  10.6 0.1 collective-permute-start.3
  10.7 2.9 %collective-permute-done.refs_5_ = bf16[64,1280]{1,0:T(8,128)(2,1)S(1)} collective-permute-done((bf16[64,1280]{1,0:T(8,128)(2,1)S(1)}, bf16[64,1280]{1,0:T(8,128)(2,1)S(1)}, u32[]{:S(2)}, u32[]{:S(2)}) %collective-permute-start) | collective-permute-done | bytes 163872 | tf_op jit(solution)/shard_map/ppermute | solution.py:379
  13.6 1.7 %collective-permute-start.1 = (bf16[64,1280]{1,0:T(8,128)(2,1)S(1)}, bf16[64,1280]{1,0:T(8,128)(2,1)S(1)}, u32[]{:S(2)}, u32[]{:S(2)}) collective-permute-start(bf16[64,1280]{1,0:T(8,128)(2,1)S(1)} %collective-permute-done.refs_5_), channel_id=1, source_target_pairs={{2,0},{6,2},{10,6},{14,10},{12,14},{8,12},{4,8},{0,4},{3,1},{7,3},... | collective-permute-start | bytes 491528 | tf_op jit(solution)/shard_map/ppermute | solution.py:379
  15.3 0.0 collective-permute-done.9.refs_8_.refs_1_
  15.3 0.4 %collective-permute-start.10 = (bf16[64,1280]{1,0:T(8,128)(2,1)S(1)}, bf16[64,1280]{1,0:T(8,128)(2,1)S(1)}, u32[]{:S(2)}, u32[]{:S(2)}) collective-permute-start(bf16[64,1280]{1,0:T(8,128)(2,1)S(1)} %collective-permute-done.9.refs_8_.refs_1_), channel_id=1, source_target_pairs={{0,2},{2,6},{6,10},{10,14},{14,12},{12,8},{8,4},{4,0},{1,3},{3,7},... | collective-permute-start | bytes 491528 | tf_op jit(solution)/shard_map/ppermute | solution.py:378
  15.7 1.4 %collective-permute-done.8.refs_6_.refs_4_ = bf16[64,1280]{1,0:T(8,128)(2,1)S(1)} collective-permute-done((bf16[64,1280]{1,0:T(8,128)(2,1)S(1)}, bf16[64,1280]{1,0:T(8,128)(2,1)S(1)}, u32[]{:S(2)}, u32[]{:S(2)}) %collective-permute-start.8) | collective-permute-done | bytes 163872 | tf_op jit(solution)/shard_map/ppermute | solution.py:377
  17.1 1.7 %collective-permute-start.12 = (bf16[64,1280]{1,0:T(8,128)(2,1)S(1)}, bf16[64,1280]{1,0:T(8,128)(2,1)S(1)}, u32[]{:S(2)}, u32[]{:S(2)}) collective-permute-start(bf16[64,1280]{1,0:T(8,128)(2,1)S(1)} %collective-permute-done.8.refs_6_.refs_4_), channel_id=1, source_target_pairs={{2,0},{6,2},{10,6},{14,10},{12,14},{8,12},{4,8},{0,4},{3,1},{7,3},... | collective-permute-start | bytes 491528 | tf_op jit(solution)/shard_map/ppermute | solution.py:377
  18.8 0.0 collective-permute-done.3.refs_6_
  18.8 0.4 %collective-permute-start.4 = (bf16[64,1280]{1,0:T(8,128)(2,1)S(1)}, bf16[64,1280]{1,0:T(8,128)(2,1)S(1)}, u32[]{:S(2)}, u32[]{:S(2)}) collective-permute-start(bf16[64,1280]{1,0:T(8,128)(2,1)S(1)} %collective-permute-done.3.refs_6_), channel_id=1, source_target_pairs={{0,2},{2,6},{6,10},{10,14},{14,12},{12,8},{8,4},{4,0},{1,3},{3,7},... | collective-permute-start | bytes 491528 | tf_op jit(solution)/shard_map/ppermute | solution.py:376
  19.2 0.0 slice-done
  19.2 2.3 %shard_map.85 = (f32[256,512]{1,0:T(8,128)S(1)}, f32[256,512]{1,0:T(8,128)S(1)}) custom-call(bf16[256,4096]{1,0:T(8,128)(2,1)S(1)} %copy-done, bf16[4096,1024]{1,0:T(8,128)(2,1)S(1)} %bitcast.5), custom_call_target="tpu_custom_call" | custom-call | bytes 4194304 | tf_op jit(solution)/shard_map/pallas_call | solution.py:219
  21.6 0.0 collective-permute-done.1.refs_2_
  21.6 1.7 %collective-permute-start.5 = (bf16[64,1280]{1,0:T(8,128)(2,1)S(1)}, bf16[64,1280]{1,0:T(8,128)(2,1)S(1)}, u32[]{:S(2)}, u32[]{:S(2)}) collective-permute-start(bf16[64,1280]{1,0:T(8,128)(2,1)S(1)} %collective-permute-done.1.refs_2_), channel_id=1, source_target_pairs={{2,0},{6,2},{10,6},{14,10},{12,14},{8,12},{4,8},{0,4},{3,1},{7,3},... | collective-permute-start | bytes 491528 | tf_op jit(solution)/shard_map/ppermute | solution.py:379
  23.3 0.0 collective-permute-done.10.refs_10_.refs_3_
  23.3 0.4 %collective-permute-start.11 = (bf16[64,1280]{1,0:T(8,128)(2,1)S(1)}, bf16[64,1280]{1,0:T(8,128)(2,1)S(1)}, u32[]{:S(2)}, u32[]{:S(2)}) collective-permute-start(bf16[64,1280]{1,0:T(8,128)(2,1)S(1)} %collective-permute-done.10.refs_10_.refs_3_), channel_id=1, source_target_pairs={{0,2},{2,6},{6,10},{10,14},{14,12},{12,8},{8,4},{4,0},{1,3},{3,7},... | collective-permute-start | bytes 491528 | tf_op jit(solution)/shard_map/ppermute | solution.py:378
  23.7 0.6 %collective-permute-done.12.refs_8_.refs_6_ = bf16[64,1280]{1,0:T(8,128)(2,1)S(1)} collective-permute-done((bf16[64,1280]{1,0:T(8,128)(2,1)S(1)}, bf16[64,1280]{1,0:T(8,128)(2,1)S(1)}, u32[]{:S(2)}, u32[]{:S(2)}) %collective-permute-start.12) | collective-permute-done | bytes 163872 | tf_op jit(solution)/shard_map/ppermute | solution.py:377
  24.2 1.7 %collective-permute-start.13 = (bf16[64,1280]{1,0:T(8,128)(2,1)S(1)}, bf16[64,1280]{1,0:T(8,128)(2,1)S(1)}, u32[]{:S(2)}, u32[]{:S(2)}) collective-permute-start(bf16[64,1280]{1,0:T(8,128)(2,1)S(1)} %collective-permute-done.12.refs_8_.refs_6_), channel_id=1, source_target_pairs={{2,0},{6,2},{10,6},{14,10},{12,14},{8,12},{4,8},{0,4},{3,1},{7,3},... | collective-permute-start | bytes 491528 | tf_op jit(solution)/shard_map/ppermute | solution.py:384
  26.0 0.0 collective-permute-done.4.refs_3_
  26.0 0.3 collective-permute-start.6
  26.3 3.1 %collective-permute-done.14.refs_1_.refs_0_ = bf16[4112,128]{1,0:T(8,128)(2,1)S(1)} collective-permute-done((bf16[4112,128]{1,0:T(8,128)(2,1)S(1)}, bf16[4112,128]{1,0:T(8,128)(2,1)S(1)}, u32[]{:S(2)}, u32[]{:S(2)}) %collective-permute-start.14) | collective-permute-done | bytes 1052704 | tf_op jit(solution)/shard_map/ppermute | solution.py:387
  29.3 0.7 %shard_map.86 = (f32[256,128]{1,0:T(8,128)S(1)}, f32[256,128]{1,0:T(8,128)S(1)}) custom-call(bf16[256,4096]{1,0:T(8,128)(2,1)S(1)} %copy-done, bf16[4112,128]{1,0:T(8,128)(2,1)S(1)} %collective-permute-done.14.refs_1_.refs_0_, s32[8,512]{1,0:T(8,128)S(1)} %shard_map.84.refs_2_.refs_1_.bounds_ref, bf16[64,1280]{1,0:T(8,128)(2,1)S(1)} %get-tuple-element.30.refs_3_, ...), custom_call_target="tpu_custom_call" | custom-call | flops 8589934592 | bytes 16777216 | tf_op jit(solution)/shard_map/pallas_call | solution.py:313
  30.1 0.1 collective-permute-start.19
  30.2 0.0 collective-permute-done.5.refs_4_
  30.2 0.0 collective-permute-done.11.refs_7_.refs_5_
  30.2 0.0 collective-permute-done.13.refs_9_.refs_7_
  30.2 1.1 %collective-permute-done.6.refs_5_ = bf16[64,1280]{1,0:T(8,128)(2,1)S(1)} collective-permute-done((bf16[64,1280]{1,0:T(8,128)(2,1)S(1)}, bf16[64,1280]{1,0:T(8,128)(2,1)S(1)}, u32[]{:S(2)}, u32[]{:S(2)}) %collective-permute-start.6) | collective-permute-done | bytes 163872 | tf_op jit(solution)/shard_map/ppermute | solution.py:383
  31.3 0.5 %shard_map.88 = bf16[128,128]{1,0:T(8,128)(2,1)S(1)} custom-call(bf16[4112,128]{1,0:T(8,128)(2,1)S(1)} %collective-permute-done.14.refs_1_.refs_0_, s32[8,512]{1,0:T(8,128)S(1)} %shard_map.84.refs_2_.refs_1_.bounds_ref, bf16[64,1280]{1,0:T(8,128)(2,1)S(1)} %collective-permute-done.1.refs_2_, bf16[64,1280]{1,0:T(8,128)(2,1)S(1)} %collective-permute-done.4.refs_3_, ...), custom_call_target="tpu_custom_call" | custom-call | flops 8589934592 | bytes 16777216 | tf_op jit(solution)/shard_map/pallas_call | solution.py:313
  31.8 1.3 %collective-permute-start.17 = (bf16[128,128]{1,0:T(8,128)(2,1)S(1)}, bf16[128,128]{1,0:T(8,128)(2,1)S(1)}, u32[]{:S(2)}, u32[]{:S(2)}) collective-permute-start(bf16[128,128]{1,0:T(8,128)(2,1)S(1)} %shard_map.88), channel_id=1, source_target_pairs={{0,16},{16,0},{1,17},{17,1},{2,18},{18,2},{3,19},{19,3},{4,20},{20... | collective-permute-start | bytes 98312 | tf_op jit(solution)/shard_map/ppermute | solution.py:406
  33.1 0.0 collective-permute-start.18
  33.1 0.5 %shard_map.87 = (f32[64,128]{1,0:T(8,128)S(1)}, f32[64,128]{1,0:T(8,128)S(1)}) custom-call(bf16[256,4096]{1,0:T(8,128)(2,1)S(1)} %copy-done, s32[8,512]{1,0:T(8,128)S(1)} %shard_map.84.refs_2_.refs_1_.bounds_ref, bf16[64,1280]{1,0:T(8,128)(2,1)S(1)} %collective-permute-done.1.refs_2_, bf16[64,1280]{1,0:T(8,128)(2,1)S(1)} %collective-permute-done.4.refs_3_, ...), custom_call_target="tpu_custom_call" | custom-call | bytes 4194304 | tf_op jit(solution)/shard_map/pallas_call | solution.py:313
  33.7 1.0 %collective-permute-start.15 = (f32[64,128]{1,0:T(8,128)S(1)}, f32[64,128]{1,0:T(8,128)S(1)}, u32[]{:S(2)}, u32[]{:S(2)}) collective-permute-start(f32[64,128]{1,0:T(8,128)S(1)} %get-tuple-element.34.top), channel_id=1, source_target_pairs={{0,1},{1,0},{2,3},{3,2},{4,5},{5,4},{6,7},{7,6},{8,9},{9,8},{10,11... | collective-permute-start | bytes 98312 | tf_op jit(solution)/shard_map/ppermute | solution.py:408
  34.7 0.1 collective-permute-start.16
  34.7 1.1 %collective-permute-done.17.two = bf16[128,128]{1,0:T(8,128)(2,1)S(1)} collective-permute-done((bf16[128,128]{1,0:T(8,128)(2,1)S(1)}, bf16[128,128]{1,0:T(8,128)(2,1)S(1)}, u32[]{:S(2)}, u32[]{:S(2)}) %collective-permute-start.17) | collective-permute-done | bytes 32800 | tf_op jit(solution)/shard_map/ppermute | solution.py:406
  35.8 0.8 %collective-permute-done.18.three = bf16[128,128]{1,0:T(8,128)(2,1)S(1)} collective-permute-done((bf16[128,128]{1,0:T(8,128)(2,1)S(1)}, bf16[128,128]{1,0:T(8,128)(2,1)S(1)}, u32[]{:S(2)}, u32[]{:S(2)}) %collective-permute-start.18) | collective-permute-done | bytes 32800 | tf_op jit(solution)/shard_map/ppermute | solution.py:407
  36.6 0.0 collective-permute-done.15.one_top
  36.6 0.0 collective-permute-done.16.one_low
  36.6 0.0 collective-permute-done.19.far_ref
  36.6 1.1 %shard_map.89 = bf16[256,512]{1,0:T(8,128)(2,1)} custom-call(s32[8,512]{1,0:T(8,128)S(1)} %shard_map.84.refs_2_.refs_1_.bounds_ref, f32[64,128]{1,0:T(8,128)S(1)} %get-tuple-element.34.top, f32[64,128]{1,0:T(8,128)S(1)} %get-tuple-element.35.low, f32[64,128]{1,0:T(8,128)S(1)} %collective-permute-done.15.one_top, ...), custom_call_target="tpu_custom_call" | custom-call | tf_op jit(solution)/shard_map/pallas_call | solution.py:411
  (7 shorter events, 0.0 us)
Async XLA Ops:
  0.0 4.3 %copy-start = (bf16[256,4096]{1,0:T(8,128)(2,1)S(1)}, bf16[256,4096]{1,0:T(8,128)(2,1)}, u32[]{:S(2)}) copy-start(bf16[256,4096]{1,0:T(8,128)(2,1)} %refs_0_.1) | copy-start | bytes 6291460
  1.2 7.4 %collective-permute-start.7 = (bf16[64,1280]{1,0:T(8,128)(2,1)S(1)}, bf16[64,1280]{1,0:T(8,128)(2,1)S(1)}, u32[]{:S(2)}, u32[]{:S(2)}) collective-permute-start(bf16[64,1280]{1,0:T(8,128)(2,1)S(1)} %get-tuple-element.31.refs_7_.refs_0_), channel_id=1, source_target_pairs={{2,0},{6,2},{10,6},{14,10},{12,14},{8,12},{4,8},{0,4},{3,1},{7,3},... | collective-permute-start | bytes 491528 | tf_op jit(solution)/shard_map/ppermute | solution.py:377
  4.3 6.3 %collective-permute-start.2 = (bf16[64,1280]{1,0:T(8,128)(2,1)S(1)}, bf16[64,1280]{1,0:T(8,128)(2,1)S(1)}, u32[]{:S(2)}, u32[]{:S(2)}) collective-permute-start(bf16[64,1280]{1,0:T(8,128)(2,1)S(1)} %get-tuple-element.30.refs_3_), channel_id=1, source_target_pairs={{0,2},{2,6},{6,10},{10,14},{14,12},{12,8},{8,4},{4,0},{1,3},{3,7},... | collective-permute-start | bytes 491528 | tf_op jit(solution)/shard_map/ppermute | solution.py:376
  4.6 24.8 %collective-permute-start.14 = (bf16[4112,128]{1,0:T(8,128)(2,1)S(1)}, bf16[4112,128]{1,0:T(8,128)(2,1)S(1)}, u32[]{:S(2)}, u32[]{:S(2)}) collective-permute-start(bf16[4112,128]{1,0:T(8,128)(2,1)S(1)} %get-tuple-element.32), channel_id=1, source_target_pairs={{0,16},{16,0},{1,17},{17,1},{2,18},{18,2},{3,19},{19,3},{4,20},{20... | collective-permute-start | bytes 3158024 | tf_op jit(solution)/shard_map/ppermute | solution.py:387
  6.6 12.6 %slice-start = ((s8[8388608]{0:T(1024)(128)(4,1)}), s8[4194304]{0:T(1024)(128)(4,1)S(1)}, s32[]{:S(2)}) async-start(s8[8388608]{0:T(1024)(128)(4,1)} %bitcast.4), calls=%async_computation | async-start | bytes 8388608
  6.6 12.6 %slice-start.1 = ((s8[8388608]{0:T(1024)(128)(4,1)}), s8[4194304]{0:T(1024)(128)(4,1)S(1)}, s32[]{:S(2)}) async-start(s8[8388608]{0:T(1024)(128)(4,1)} %bitcast.4), calls=%async_computation.1 | async-start | bytes 8388608
  6.6 7.0 %collective-permute-start = (bf16[64,1280]{1,0:T(8,128)(2,1)S(1)}, bf16[64,1280]{1,0:T(8,128)(2,1)S(1)}, u32[]{:S(2)}, u32[]{:S(2)}) collective-permute-start(bf16[64,1280]{1,0:T(8,128)(2,1)S(1)} %get-tuple-element.30.refs_3_), channel_id=1, source_target_pairs={{2,0},{6,2},{10,6},{14,10},{12,14},{8,12},{4,8},{0,4},{3,1},{7,3},... | collective-permute-start | bytes 491528 | tf_op jit(solution)/shard_map/ppermute | solution.py:379
  8.2 7.1 %collective-permute-start.9 = (bf16[64,1280]{1,0:T(8,128)(2,1)S(1)}, bf16[64,1280]{1,0:T(8,128)(2,1)S(1)}, u32[]{:S(2)}, u32[]{:S(2)}) collective-permute-start(bf16[64,1280]{1,0:T(8,128)(2,1)S(1)} %get-tuple-element.31.refs_7_.refs_0_), channel_id=1, source_target_pairs={{0,2},{2,6},{6,10},{10,14},{14,12},{12,8},{8,4},{4,0},{1,3},{3,7},... | collective-permute-start | bytes 491528 | tf_op jit(solution)/shard_map/ppermute | solution.py:378
  8.6 8.5 %collective-permute-start.8 = (bf16[64,1280]{1,0:T(8,128)(2,1)S(1)}, bf16[64,1280]{1,0:T(8,128)(2,1)S(1)}, u32[]{:S(2)}, u32[]{:S(2)}) collective-permute-start(bf16[64,1280]{1,0:T(8,128)(2,1)S(1)} %collective-permute-done.7.refs_9_.refs_2_), channel_id=1, source_target_pairs={{2,0},{6,2},{10,6},{14,10},{12,14},{8,12},{4,8},{0,4},{3,1},{7,3},... | collective-permute-start | bytes 491528 | tf_op jit(solution)/shard_map/ppermute | solution.py:377
  10.6 8.2 %collective-permute-start.3 = (bf16[64,1280]{1,0:T(8,128)(2,1)S(1)}, bf16[64,1280]{1,0:T(8,128)(2,1)S(1)}, u32[]{:S(2)}, u32[]{:S(2)}) collective-permute-start(bf16[64,1280]{1,0:T(8,128)(2,1)S(1)} %collective-permute-done.2.refs_4_), channel_id=1, source_target_pairs={{0,2},{2,6},{6,10},{10,14},{14,12},{12,8},{8,4},{4,0},{1,3},{3,7},... | collective-permute-start | bytes 491528 | tf_op jit(solution)/shard_map/ppermute | solution.py:376
  13.6 8.0 %collective-permute-start.1 = (bf16[64,1280]{1,0:T(8,128)(2,1)S(1)}, bf16[64,1280]{1,0:T(8,128)(2,1)S(1)}, u32[]{:S(2)}, u32[]{:S(2)}) collective-permute-start(bf16[64,1280]{1,0:T(8,128)(2,1)S(1)} %collective-permute-done.refs_5_), channel_id=1, source_target_pairs={{2,0},{6,2},{10,6},{14,10},{12,14},{8,12},{4,8},{0,4},{3,1},{7,3},... | collective-permute-start | bytes 491528 | tf_op jit(solution)/shard_map/ppermute | solution.py:379
  15.3 8.0 %collective-permute-start.10 = (bf16[64,1280]{1,0:T(8,128)(2,1)S(1)}, bf16[64,1280]{1,0:T(8,128)(2,1)S(1)}, u32[]{:S(2)}, u32[]{:S(2)}) collective-permute-start(bf16[64,1280]{1,0:T(8,128)(2,1)S(1)} %collective-permute-done.9.refs_8_.refs_1_), channel_id=1, source_target_pairs={{0,2},{2,6},{6,10},{10,14},{14,12},{12,8},{8,4},{4,0},{1,3},{3,7},... | collective-permute-start | bytes 491528 | tf_op jit(solution)/shard_map/ppermute | solution.py:378
  17.1 7.1 %collective-permute-start.12 = (bf16[64,1280]{1,0:T(8,128)(2,1)S(1)}, bf16[64,1280]{1,0:T(8,128)(2,1)S(1)}, u32[]{:S(2)}, u32[]{:S(2)}) collective-permute-start(bf16[64,1280]{1,0:T(8,128)(2,1)S(1)} %collective-permute-done.8.refs_6_.refs_4_), channel_id=1, source_target_pairs={{2,0},{6,2},{10,6},{14,10},{12,14},{8,12},{4,8},{0,4},{3,1},{7,3},... | collective-permute-start | bytes 491528 | tf_op jit(solution)/shard_map/ppermute | solution.py:377
  18.8 7.1 %collective-permute-start.4 = (bf16[64,1280]{1,0:T(8,128)(2,1)S(1)}, bf16[64,1280]{1,0:T(8,128)(2,1)S(1)}, u32[]{:S(2)}, u32[]{:S(2)}) collective-permute-start(bf16[64,1280]{1,0:T(8,128)(2,1)S(1)} %collective-permute-done.3.refs_6_), channel_id=1, source_target_pairs={{0,2},{2,6},{6,10},{10,14},{14,12},{12,8},{8,4},{4,0},{1,3},{3,7},... | collective-permute-start | bytes 491528 | tf_op jit(solution)/shard_map/ppermute | solution.py:376
  21.6 8.6 %collective-permute-start.5 = (bf16[64,1280]{1,0:T(8,128)(2,1)S(1)}, bf16[64,1280]{1,0:T(8,128)(2,1)S(1)}, u32[]{:S(2)}, u32[]{:S(2)}) collective-permute-start(bf16[64,1280]{1,0:T(8,128)(2,1)S(1)} %collective-permute-done.1.refs_2_), channel_id=1, source_target_pairs={{2,0},{6,2},{10,6},{14,10},{12,14},{8,12},{4,8},{0,4},{3,1},{7,3},... | collective-permute-start | bytes 491528 | tf_op jit(solution)/shard_map/ppermute | solution.py:379
  23.3 6.9 %collective-permute-start.11 = (bf16[64,1280]{1,0:T(8,128)(2,1)S(1)}, bf16[64,1280]{1,0:T(8,128)(2,1)S(1)}, u32[]{:S(2)}, u32[]{:S(2)}) collective-permute-start(bf16[64,1280]{1,0:T(8,128)(2,1)S(1)} %collective-permute-done.10.refs_10_.refs_3_), channel_id=1, source_target_pairs={{0,2},{2,6},{6,10},{10,14},{14,12},{12,8},{8,4},{4,0},{1,3},{3,7},... | collective-permute-start | bytes 491528 | tf_op jit(solution)/shard_map/ppermute | solution.py:378
  24.2 6.0 %collective-permute-start.13 = (bf16[64,1280]{1,0:T(8,128)(2,1)S(1)}, bf16[64,1280]{1,0:T(8,128)(2,1)S(1)}, u32[]{:S(2)}, u32[]{:S(2)}) collective-permute-start(bf16[64,1280]{1,0:T(8,128)(2,1)S(1)} %collective-permute-done.12.refs_8_.refs_6_), channel_id=1, source_target_pairs={{2,0},{6,2},{10,6},{14,10},{12,14},{8,12},{4,8},{0,4},{3,1},{7,3},... | collective-permute-start | bytes 491528 | tf_op jit(solution)/shard_map/ppermute | solution.py:384
  26.0 5.3 %collective-permute-start.6 = (bf16[64,1280]{1,0:T(8,128)(2,1)S(1)}, bf16[64,1280]{1,0:T(8,128)(2,1)S(1)}, u32[]{:S(2)}, u32[]{:S(2)}) collective-permute-start(bf16[64,1280]{1,0:T(8,128)(2,1)S(1)} %collective-permute-done.4.refs_3_), channel_id=1, source_target_pairs={{0,2},{2,6},{6,10},{10,14},{14,12},{12,8},{8,4},{4,0},{1,3},{3,7},... | collective-permute-start | bytes 491528 | tf_op jit(solution)/shard_map/ppermute | solution.py:383
  30.1 6.5 %collective-permute-start.19 = (f32[256,512]{1,0:T(8,128)S(1)}, f32[256,512]{1,0:T(8,128)S(1)}, u32[]{:S(2)}, u32[]{:S(2)}) collective-permute-start(f32[256,512]{1,0:T(8,128)S(1)} %get-tuple-element.40), channel_id=1, source_target_pairs={{0,1},{1,0},{2,3},{3,2},{4,5},{5,4},{6,7},{7,6},{8,9},{9,8},{10,11... | collective-permute-start | bytes 1572872 | tf_op jit(solution)/shard_map/ppermute | solution.py:400
  31.8 4.0 %collective-permute-start.17 = (bf16[128,128]{1,0:T(8,128)(2,1)S(1)}, bf16[128,128]{1,0:T(8,128)(2,1)S(1)}, u32[]{:S(2)}, u32[]{:S(2)}) collective-permute-start(bf16[128,128]{1,0:T(8,128)(2,1)S(1)} %shard_map.88), channel_id=1, source_target_pairs={{0,16},{16,0},{1,17},{17,1},{2,18},{18,2},{3,19},{19,3},{4,20},{20... | collective-permute-start | bytes 98312 | tf_op jit(solution)/shard_map/ppermute | solution.py:406
  33.1 3.4 %collective-permute-start.18 = (bf16[128,128]{1,0:T(8,128)(2,1)S(1)}, bf16[128,128]{1,0:T(8,128)(2,1)S(1)}, u32[]{:S(2)}, u32[]{:S(2)}) collective-permute-start(bf16[128,128]{1,0:T(8,128)(2,1)S(1)} %shard_map.88), channel_id=1, source_target_pairs={{0,17},{1,16},{16,1},{17,0},{2,19},{3,18},{18,3},{19,2},{4,21},{5,... | collective-permute-start | bytes 98312 | tf_op jit(solution)/shard_map/ppermute | solution.py:407
  33.7 2.9 %collective-permute-start.15 = (f32[64,128]{1,0:T(8,128)S(1)}, f32[64,128]{1,0:T(8,128)S(1)}, u32[]{:S(2)}, u32[]{:S(2)}) collective-permute-start(f32[64,128]{1,0:T(8,128)S(1)} %get-tuple-element.34.top), channel_id=1, source_target_pairs={{0,1},{1,0},{2,3},{3,2},{4,5},{5,4},{6,7},{7,6},{8,9},{9,8},{10,11... | collective-permute-start | bytes 98312 | tf_op jit(solution)/shard_map/ppermute | solution.py:408
  34.7 1.9 %collective-permute-start.16 = (f32[64,128]{1,0:T(8,128)S(1)}, f32[64,128]{1,0:T(8,128)S(1)}, u32[]{:S(2)}, u32[]{:S(2)}) collective-permute-start(f32[64,128]{1,0:T(8,128)S(1)} %get-tuple-element.35.low), channel_id=1, source_target_pairs={{0,1},{1,0},{2,3},{3,2},{4,5},{5,4},{6,7},{7,6},{8,9},{9,8},{10,11... | collective-permute-start | bytes 98312 | tf_op jit(solution)/shard_map/ppermute | solution.py:408

commit v23 on v22

--- a/solution.py
+++ b/solution.py
@@ -231,14 +231,13 @@
     return (row >= low) & (row < high)
 
 
-def own_ends(bounds_ref, group, size):
-    columns = slice(group * size, (group + 1) * size)
-    return bounds_ref[0:1, columns], bounds_ref[1:2, columns]
-
-
-def other_ends(other_ref, extra, group, size):
+def own_ends(bounds_ref, begin, end):
+    return bounds_ref[0:1, begin:end], bounds_ref[1:2, begin:end]
+
+
+def other_ends(other_ref, extra, begin, end):
     ends = other_ref[-extra:, :].astype(F32).astype(I32)
-    lines = range(group * size // 128, (group + 1) * size // 128)
+    lines = range(begin // 128, end // 128)
     low = jnp.concatenate([ends[i : i + 1] for i in lines], axis=1)
     high = jnp.concatenate([ends[extra // 2 + i : extra // 2 + i + 1] for i in lines], axis=1)
     return low, high
@@ -251,43 +250,51 @@
     return total
 
 
-def rank_kernel(sides, groups, depth, last, *refs):
+def rank_kernel(sides, plan, chunks, depth, last, started, *refs):
     refs = list(refs)
     rows_refs, refs = refs[: len(sides)], refs[len(sides) :]
     bounds_ref, pieces = refs[0], refs[1:]
-    pieces, rest = pieces[: 2 * GROUP * len(groups)], pieces[2 * GROUP * len(groups) :]
-    starts, outs = (rest[: len(sides)], rest[len(sides) :]) if last else ((), rest)
-    cut = pieces[0].shape[1]
-    rank = pieces[0].shape[0]
-    size = GROUP * rank
+    firsts = dict(zip(chunks, pieces))
+    seconds = dict(zip(chunks, pieces[len(chunks) :]))
+    rest = pieces[2 * len(chunks) :]
+    outs = rest[started:]
+    starts = rest[:started]
+    rank, cut = pieces[0].shape
     extra = extra_rows(bounds_ref.shape[1])
-    rows = []
+    rows = {}
     for side, ref in zip(sides, rows_refs):
         if side == 0:
             offset = pl.multiple_of(lax.axis_index("groups") * depth, 128)
-            rows.append(ref[:, pl.ds(offset, depth)])
+            rows[side] = ref[:, pl.ds(offset, depth)]
         else:
             blocks = depth // 128
             tall = (ref.shape[0] - extra) // blocks
-            rows.append(
-                jnp.concatenate([ref[i * tall : (i + 1) * tall, :] for i in range(blocks)], axis=1)
+            rows[side] = jnp.concatenate(
+                [ref[i * tall : (i + 1) * tall, :] for i in range(blocks)], axis=1
             )
-    count = rows[0].shape[0]
-    rows = jnp.concatenate(rows, axis=0)
-    totals = [ref[...] for ref in starts] if last else [None] * len(sides)
-    for i, group in enumerate(groups):
-        held = pieces[2 * GROUP * i : 2 * GROUP * (i + 1)]
-        first = jnp.concatenate([ref[...] for ref in held[:GROUP]], axis=0)
-        second = jnp.concatenate([ref[:, : depth - cut] for ref in held[GROUP:]], axis=0)
-        part = contract(rows, jnp.concatenate([first, second], axis=1))
-        for s, side in enumerate(sides):
+    count = rows[sides[0]].shape[0]
+    totals = {side: ref[...] for side, ref in zip(sides, starts)}
+    for begin, end, from_chunk, to_chunk, meant in plan:
+        held = [chunk if from_chunk <= chunk < to_chunk else from_chunk for chunk in range(begin, end)]
+        first = jnp.concatenate([firsts[chunk][...] for chunk in held], axis=0)
+        second = jnp.concatenate([seconds[chunk][:, : depth - cut] for chunk in held], axis=0)
+        tall = jnp.concatenate([rows[side] for side in meant], axis=0)
+        part = contract(tall, jnp.concatenate([first, second], axis=1))
+        for i, side in enumerate(meant):
+            columns = (begin * rank, end * rank)
             if side == 0:
-                ends = own_ends(bounds_ref, group, size)
+                ends = own_ends(bounds_ref, *columns)
             else:
-                ends = other_ends(rows_refs[s], extra, group, size)
-            here = part[s * count : (s + 1) * count]
-            kept = fold(jnp.where(group_mask(*ends, here.shape), here, 0.0))
-            totals[s] = kept if totals[s] is None else totals[s] + kept
+                ends = other_ends(rows_refs[sides.index(1)], extra, *columns)
+            here = part[i * count : (i + 1) * count]
+            mask = group_mask(*ends, here.shape)
+            if (from_chunk, to_chunk) != (begin, end):
+                lane = lax.broadcasted_iota(I32, here.shape, 1)
+                mask = mask & (lane >= (from_chunk - begin) * rank)
+                mask = mask & (lane < (to_chunk - begin) * rank)
+            kept = fold(jnp.where(mask, here, 0.0))
+            totals[side] = totals[side] + kept if side in totals else kept
+    totals = [totals[side] for side in sides]
     if last:
         (total,) = totals
         total = total + pltpu.roll(total, rank, 1)
@@ -300,9 +307,10 @@
         out_ref[...] = total.astype(out_ref.dtype)
 
 
-def rank_call(sides, groups, depth, count, rows, bounds, pieces, starts):
+def rank_call(sides, plan, chunks, depth, count, rows, bounds, firsts, seconds, starts, last=True):
+    pieces = [firsts[chunk] for chunk in chunks] + [seconds[chunk] for chunk in chunks]
     rank = pieces[0].shape[0]
-    last = len(starts) > 0
+    last = last and len(starts) > 0
     if not last:
         out = (jax.ShapeDtypeStruct((count, 2 * rank), F32),) * len(sides)
     elif sides == (1,):
@@ -311,7 +319,7 @@
         out = (jax.ShapeDtypeStruct((count // 4, 2 * rank), F32),) * 2
     operands = [*rows, bounds, *pieces, *starts]
     return pl.pallas_call(
-        functools.partial(rank_kernel, sides, groups, depth, last),
+        functools.partial(rank_kernel, sides, plan, chunks, depth, last, len(starts)),
         out_shape=out,
         in_specs=[VMEM] * len(operands),
         out_specs=(VMEM,) * len(out),
@@ -334,7 +342,8 @@
     wide = jnp.concatenate([values] * (GROUP // 2), axis=1)
     total = None
     for group in range(len(factors) // GROUP):
-        mask = group_mask(*own_ends(bounds_ref, group, GROUP * rank), wide.shape)
+        columns = (group * GROUP * rank, (group + 1) * GROUP * rank)
+        mask = group_mask(*own_ends(bounds_ref, *columns), wide.shape)
         chosen = jnp.where(mask, wide, 0.0).astype(BF16)
         factor = jnp.concatenate(
             [ref[:, begin:] for ref in factors[group * GROUP : (group + 1) * GROUP]], axis=0
@@ -386,22 +395,26 @@
     hidden, near, far = lax.optimization_barrier((hidden, near, far))
     other = lax.ppermute(to_other, "groups", swap)
 
-    count = owners // GROUP
-    early = range(count - 1)
-    pieces = []
-    for group in early:
-        pieces += firsts[group * GROUP : (group + 1) * GROUP]
-        pieces += seconds[group * GROUP : (group + 1) * GROUP]
-    both = (hidden, other)
+    before = owners - GROUP
+    held = (depth, rows)
+    plan = [(i, i + GROUP, i, i + GROUP, (0, 1)) for i in range(0, before, GROUP)]
     start_mine, start_theirs = rank_call(
-        (0, 1), tuple(early), depth, rows, both, bounds, pieces, ()
-    )
-    start_theirs, far = lax.optimization_barrier((start_theirs, far))
+        (0, 1), plan, range(before), *held, (hidden, other), bounds, firsts, seconds, ()
+    )
+    plan = [(before, owners, before, owners - 1, (1,))]
+    (start_theirs,) = rank_call(
+        (1,), plan, range(before, owners - 1), *held, (other,), bounds, firsts, seconds, (start_theirs,), False
+    )
+    plan = [(owners - 2, owners, owners - 1, owners, (1,))]
+    (theirs,) = rank_call(
+        (1,), plan, [owners - 1], *held, (other,), bounds, firsts, seconds, (start_theirs,)
+    )
+    theirs, far = lax.optimization_barrier((theirs, far))
     far = lax.ppermute(far, "tensor", swap)
-    pieces = firsts[-GROUP:] + seconds[-GROUP:]
-    late = (count - 1,)
-    (theirs,) = rank_call((1,), late, depth, rows, (other,), bounds, pieces, (start_theirs,))
-    mine = rank_call((0,), late, depth, rows, (hidden,), bounds, pieces, (start_mine,))
+    plan = [(before, owners, before, owners, (0,))]
+    mine = rank_call(
+        (0,), plan, range(before, owners), *held, (hidden,), bounds, firsts, seconds, (start_mine,)
+    )
 
     two = lax.ppermute(theirs, "groups", swap)
     three = lax.ppermute(theirs, ("groups", "tensor"), [(0, 3), (1, 2), (2, 1), (3, 0)])

time: 37.9 us -> 37.8 us (level)
  waiting for transfers between devices: 10.9 us -> 10.3 us
  Pallas kernels: 6.77 us -> 7.2 us
    ppermute x1, starting transfers between devices: 0.01 us -> 0.56 us  [per_device(): lax.ppermute(theirs, ('groups', 'tensor'), [(0, 3), (1, 2), (2, 1), (3, 0)])]
    ppermute x2, starting transfers between devices: 1.04 us -> 0.58 us  [per_device(): one = [lax.ppermute(part, 'tensor', swap) for part in mine]]
    pallas_call x3 -> x4, Pallas kernels: 1.83 us -> 2.27 us  [rank_call(): pl.pallas_call(functools.partial(rank_kernel, sides, plan, chunks, depth,...]
    ppermute x1, waiting for transfers between devices: 1.09 us -> 0.69 us  [per_device(): firsts.append(lax.ppermute(ahead[0], 'batch', forward))]
where the time goes in v23:
time: 37.8 us; the launch traced here: 37.7 us
  starting transfers between devices  20.1 us (53%)
  waiting for transfers between devices  10.3 us (27%)
  Pallas kernels  7.2 us (19%)
    ppermute x3, starting transfers between devices, per_device(): d = lax.ppermute(behind[1], 'batch', backward)  6.79 us
    ppermute x3, starting transfers between devices, per_device(): c = lax.ppermute(behind[0], 'batch', backward)  5.02 us
    ppermute x1, waiting for transfers between devices, per_device(): other = lax.ppermute(to_other, 'groups', swap)  3.05 us
    ppermute x3, waiting for transfers between devices, per_device(): c = lax.ppermute(behind[0], 'batch', backward)  2.91 us
    pallas_call x1, Pallas kernels, base_call(): pl.pallas_call(base_kernel, out_shape=(out, out), in_specs=[VMEM] * 2, ou...  2.35 us
    pallas_call x4, Pallas kernels, rank_call(): pl.pallas_call(functools.partial(rank_kernel, sides, plan, chunks, depth,...  2.27 us
    ppermute x1, starting transfers between devices, per_device(): other = lax.ppermute(to_other, 'groups', swap)  2.03 us
    ppermute x3, waiting for transfers between devices, per_device(): d = lax.ppermute(behind[1], 'batch', backward)  1.94 us
  transfers between devices with their start and end apart: 20, of which 7 were waited for; matrix products, arithmetic and copies ran while one was open for 0% of the time, Pallas kernels for 12%

profile of v23, /device:TPU:0, one launch (start us, length us, event | category | flops | bytes accessed | tf_op | source)
XLA Modules:
  0.0 37.7 jit_solution(6001018219242647386)
XLA Ops:
  0.0 1.2 %shard_map.82 = (bf16[64,1280]{1,0:T(8,128)(2,1)S(1)}, bf16[64,1280]{1,0:T(8,128)(2,1)S(1)}, s32[8,512]{1,0:T(8,128)S(1)}) custom-call(bf16[64,4096]{1,0:T(8,128)(2,1)} %bitcast.6, bf16[64,512]{1,0:T(8,128)(2,1)} %bitcast.7, s32[1,4]{1,0:T(1,128)} %demand_ref.1, s32[1,4]{1,0:T(1,128)} %lengths_ref.1, s32[8]{0:T(128)} %holder_ref.1, ...), custom_call_target="tpu_custom_call" | custom-call | flops 8589934592 | bytes 16777216 | tf_op jit(solution)/shard_map/pallas_call | solution.py:137
  1.2 3.1 %collective-permute-start.7 = (bf16[64,1280]{1,0:T(8,128)(2,1)S(1)}, bf16[64,1280]{1,0:T(8,128)(2,1)S(1)}, u32[]{:S(2)}, u32[]{:S(2)}) collective-permute-start(bf16[64,1280]{1,0:T(8,128)(2,1)S(1)} %get-tuple-element.31.refs_7_.refs_0_), channel_id=1, source_target_pairs={{2,0},{6,2},{10,6},{14,10},{12,14},{8,12},{4,8},{0,4},{3,1},{7,3},... | collective-permute-start | bytes 491528 | tf_op jit(solution)/shard_map/ppermute | solution.py:386
  4.3 0.0 collective-permute-start.2
  4.3 0.3 shard_map.83
  4.6 2.0 %collective-permute-start.14 = (bf16[4112,128]{1,0:T(8,128)(2,1)S(1)}, bf16[4112,128]{1,0:T(8,128)(2,1)S(1)}, u32[]{:S(2)}, u32[]{:S(2)}) collective-permute-start(bf16[4112,128]{1,0:T(8,128)(2,1)S(1)} %get-tuple-element.32), channel_id=1, source_target_pairs={{0,16},{16,0},{1,17},{17,1},{2,18},{18,2},{3,19},{19,3},{4,20},{20... | collective-permute-start | bytes 3158024 | tf_op jit(solution)/shard_map/ppermute | solution.py:396
  6.6 1.6 %collective-permute-start = (bf16[64,1280]{1,0:T(8,128)(2,1)S(1)}, bf16[64,1280]{1,0:T(8,128)(2,1)S(1)}, u32[]{:S(2)}, u32[]{:S(2)}) collective-permute-start(bf16[64,1280]{1,0:T(8,128)(2,1)S(1)} %get-tuple-element.30.refs_3_), channel_id=1, source_target_pairs={{2,0},{6,2},{10,6},{14,10},{12,14},{8,12},{4,8},{0,4},{3,1},{7,3},... | collective-permute-start | bytes 491528 | tf_op jit(solution)/shard_map/ppermute | solution.py:388
  8.2 0.4 %collective-permute-start.9 = (bf16[64,1280]{1,0:T(8,128)(2,1)S(1)}, bf16[64,1280]{1,0:T(8,128)(2,1)S(1)}, u32[]{:S(2)}, u32[]{:S(2)}) collective-permute-start(bf16[64,1280]{1,0:T(8,128)(2,1)S(1)} %get-tuple-element.31.refs_7_.refs_0_), channel_id=1, source_target_pairs={{0,2},{2,6},{6,10},{10,14},{14,12},{12,8},{8,4},{4,0},{1,3},{3,7},... | collective-permute-start | bytes 491528 | tf_op jit(solution)/shard_map/ppermute | solution.py:387
  8.6 0.0 collective-permute-done.7.refs_9_.refs_2_
  8.6 2.0 %collective-permute-start.8 = (bf16[64,1280]{1,0:T(8,128)(2,1)S(1)}, bf16[64,1280]{1,0:T(8,128)(2,1)S(1)}, u32[]{:S(2)}, u32[]{:S(2)}) collective-permute-start(bf16[64,1280]{1,0:T(8,128)(2,1)S(1)} %collective-permute-done.7.refs_9_.refs_2_), channel_id=1, source_target_pairs={{2,0},{6,2},{10,6},{14,10},{12,14},{8,12},{4,8},{0,4},{3,1},{7,3},... | collective-permute-start | bytes 491528 | tf_op jit(solution)/shard_map/ppermute | solution.py:386
  10.6 0.0 collective-permute-done.2.refs_4_
  10.6 0.1 collective-permute-start.3
  10.7 2.9 %collective-permute-done.refs_5_ = bf16[64,1280]{1,0:T(8,128)(2,1)S(1)} collective-permute-done((bf16[64,1280]{1,0:T(8,128)(2,1)S(1)}, bf16[64,1280]{1,0:T(8,128)(2,1)S(1)}, u32[]{:S(2)}, u32[]{:S(2)}) %collective-permute-start) | collective-permute-done | bytes 163872 | tf_op jit(solution)/shard_map/ppermute | solution.py:388
  13.6 1.7 %collective-permute-start.1 = (bf16[64,1280]{1,0:T(8,128)(2,1)S(1)}, bf16[64,1280]{1,0:T(8,128)(2,1)S(1)}, u32[]{:S(2)}, u32[]{:S(2)}) collective-permute-start(bf16[64,1280]{1,0:T(8,128)(2,1)S(1)} %collective-permute-done.refs_5_), channel_id=1, source_target_pairs={{2,0},{6,2},{10,6},{14,10},{12,14},{8,12},{4,8},{0,4},{3,1},{7,3},... | collective-permute-start | bytes 491528 | tf_op jit(solution)/shard_map/ppermute | solution.py:388
  15.3 0.0 collective-permute-done.9.refs_8_.refs_1_
  15.3 0.4 %collective-permute-start.10 = (bf16[64,1280]{1,0:T(8,128)(2,1)S(1)}, bf16[64,1280]{1,0:T(8,128)(2,1)S(1)}, u32[]{:S(2)}, u32[]{:S(2)}) collective-permute-start(bf16[64,1280]{1,0:T(8,128)(2,1)S(1)} %collective-permute-done.9.refs_8_.refs_1_), channel_id=1, source_target_pairs={{0,2},{2,6},{6,10},{10,14},{14,12},{12,8},{8,4},{4,0},{1,3},{3,7},... | collective-permute-start | bytes 491528 | tf_op jit(solution)/shard_map/ppermute | solution.py:387
  15.7 1.4 %collective-permute-done.8.refs_6_.refs_5_.refs_4_ = bf16[64,1280]{1,0:T(8,128)(2,1)S(1)} collective-permute-done((bf16[64,1280]{1,0:T(8,128)(2,1)S(1)}, bf16[64,1280]{1,0:T(8,128)(2,1)S(1)}, u32[]{:S(2)}, u32[]{:S(2)}) %collective-permute-start.8) | collective-permute-done | bytes 163872 | tf_op jit(solution)/shard_map/ppermute | solution.py:386
  17.1 1.7 %collective-permute-start.12 = (bf16[64,1280]{1,0:T(8,128)(2,1)S(1)}, bf16[64,1280]{1,0:T(8,128)(2,1)S(1)}, u32[]{:S(2)}, u32[]{:S(2)}) collective-permute-start(bf16[64,1280]{1,0:T(8,128)(2,1)S(1)} %collective-permute-done.8.refs_6_.refs_5_.refs_4_), channel_id=1, source_target_pairs={{2,0},{6,2},{10,6},{14,10},{12,14},{8,12},{4,8},{0,4},{3,1},{7,3},... | collective-permute-start | bytes 491528 | tf_op jit(solution)/shard_map/ppermute | solution.py:386
  18.8 0.0 collective-permute-done.3.refs_6_
  18.8 0.4 %collective-permute-start.4 = (bf16[64,1280]{1,0:T(8,128)(2,1)S(1)}, bf16[64,1280]{1,0:T(8,128)(2,1)S(1)}, u32[]{:S(2)}, u32[]{:S(2)}) collective-permute-start(bf16[64,1280]{1,0:T(8,128)(2,1)S(1)} %collective-permute-done.3.refs_6_), channel_id=1, source_target_pairs={{0,2},{2,6},{6,10},{10,14},{14,12},{12,8},{8,4},{4,0},{1,3},{3,7},... | collective-permute-start | bytes 491528 | tf_op jit(solution)/shard_map/ppermute | solution.py:385
  19.2 2.3 %shard_map.85 = (f32[256,512]{1,0:T(8,128)S(1)}, f32[256,512]{1,0:T(8,128)S(1)}) custom-call(bf16[256,4096]{1,0:T(8,128)(2,1)S(1)} %copy-done, bf16[4096,1024]{1,0:T(8,128)(2,1)S(1)} %bitcast.5), custom_call_target="tpu_custom_call" | custom-call | bytes 4194304 | tf_op jit(solution)/shard_map/pallas_call | solution.py:219
  21.6 0.0 collective-permute-done.1.refs_2_
  21.6 1.7 %collective-permute-start.5 = (bf16[64,1280]{1,0:T(8,128)(2,1)S(1)}, bf16[64,1280]{1,0:T(8,128)(2,1)S(1)}, u32[]{:S(2)}, u32[]{:S(2)}) collective-permute-start(bf16[64,1280]{1,0:T(8,128)(2,1)S(1)} %collective-permute-done.1.refs_2_), channel_id=1, source_target_pairs={{2,0},{6,2},{10,6},{14,10},{12,14},{8,12},{4,8},{0,4},{3,1},{7,3},... | collective-permute-start | bytes 491528 | tf_op jit(solution)/shard_map/ppermute | solution.py:388
  23.3 0.0 collective-permute-done.10.refs_10_.refs_3_
  23.3 0.4 %collective-permute-start.11 = (bf16[64,1280]{1,0:T(8,128)(2,1)S(1)}, bf16[64,1280]{1,0:T(8,128)(2,1)S(1)}, u32[]{:S(2)}, u32[]{:S(2)}) collective-permute-start(bf16[64,1280]{1,0:T(8,128)(2,1)S(1)} %collective-permute-done.10.refs_10_.refs_3_), channel_id=1, source_target_pairs={{0,2},{2,6},{6,10},{10,14},{14,12},{12,8},{8,4},{4,0},{1,3},{3,7},... | collective-permute-start | bytes 491528 | tf_op jit(solution)/shard_map/ppermute | solution.py:387
  23.7 0.6 %collective-permute-done.12.refs_8_.refs_7_.refs_6_ = bf16[64,1280]{1,0:T(8,128)(2,1)S(1)} collective-permute-done((bf16[64,1280]{1,0:T(8,128)(2,1)S(1)}, bf16[64,1280]{1,0:T(8,128)(2,1)S(1)}, u32[]{:S(2)}, u32[]{:S(2)}) %collective-permute-start.12) | collective-permute-done | bytes 163872 | tf_op jit(solution)/shard_map/ppermute | solution.py:386
  24.2 1.7 %collective-permute-start.13 = (bf16[64,1280]{1,0:T(8,128)(2,1)S(1)}, bf16[64,1280]{1,0:T(8,128)(2,1)S(1)}, u32[]{:S(2)}, u32[]{:S(2)}) collective-permute-start(bf16[64,1280]{1,0:T(8,128)(2,1)S(1)} %collective-permute-done.12.refs_8_.refs_7_.refs_6_), channel_id=1, source_target_pairs={{2,0},{6,2},{10,6},{14,10},{12,14},{8,12},{4,8},{0,4},{3,1},{7,3},... | collective-permute-start | bytes 491528 | tf_op jit(solution)/shard_map/ppermute | solution.py:393
  26.0 0.0 collective-permute-done.4.refs_3_
  26.0 0.3 collective-permute-start.6
  26.3 3.1 %collective-permute-done.14.refs_1_.refs_0_ = bf16[4112,128]{1,0:T(8,128)(2,1)S(1)} collective-permute-done((bf16[4112,128]{1,0:T(8,128)(2,1)S(1)}, bf16[4112,128]{1,0:T(8,128)(2,1)S(1)}, u32[]{:S(2)}, u32[]{:S(2)}) %collective-permute-start.14) | collective-permute-done | bytes 1052704 | tf_op jit(solution)/shard_map/ppermute | solution.py:396
  29.3 0.7 %shard_map.86 = (f32[256,128]{1,0:T(8,128)S(1)}, f32[256,128]{1,0:T(8,128)S(1)}) custom-call(bf16[256,4096]{1,0:T(8,128)(2,1)S(1)} %copy-done, bf16[4112,128]{1,0:T(8,128)(2,1)S(1)} %collective-permute-done.14.refs_1_.refs_0_, s32[8,512]{1,0:T(8,128)S(1)} %shard_map.84.refs_2_.refs_1_.bounds_ref, bf16[64,1280]{1,0:T(8,128)(2,1)S(1)} %get-tuple-element.30.refs_3_, ...), custom_call_target="tpu_custom_call" | custom-call | flops 8589934592 | bytes 16777216 | tf_op jit(solution)/shard_map/pallas_call | solution.py:321
  30.1 0.0 collective-permute-done.5.refs_4_
  30.1 0.0 collective-permute-done.11.refs_7_.refs_6_.refs_5_
  30.1 0.5 %shard_map.88.refs_4_ = f32[256,128]{1,0:T(8,128)S(1)} custom-call(bf16[4112,128]{1,0:T(8,128)(2,1)S(1)} %collective-permute-done.14.refs_1_.refs_0_, s32[8,512]{1,0:T(8,128)S(1)} %shard_map.84.refs_2_.refs_1_.bounds_ref, bf16[64,1280]{1,0:T(8,128)(2,1)S(1)} %collective-permute-done.1.refs_2_, bf16[64,1280]{1,0:T(8,128)(2,1)S(1)} %collective-permute-done.4.refs_3_, ...), custom_call_target="tpu_custom_call" | custom-call | flops 8589934592 | bytes 16777216 | tf_op jit(solution)/shard_map/pallas_call | solution.py:321
  30.6 0.0 collective-permute-done.13.refs_9_.refs_3_.refs_7_
  30.6 0.7 %collective-permute-done.6.refs_5_.refs_2_ = bf16[64,1280]{1,0:T(8,128)(2,1)S(1)} collective-permute-done((bf16[64,1280]{1,0:T(8,128)(2,1)S(1)}, bf16[64,1280]{1,0:T(8,128)(2,1)S(1)}, u32[]{:S(2)}, u32[]{:S(2)}) %collective-permute-start.6) | collective-permute-done | bytes 163872 | tf_op jit(solution)/shard_map/ppermute | solution.py:392
  31.3 0.5 %shard_map.89 = bf16[128,128]{1,0:T(8,128)(2,1)S(1)} custom-call(bf16[4112,128]{1,0:T(8,128)(2,1)S(1)} %collective-permute-done.14.refs_1_.refs_0_, s32[8,512]{1,0:T(8,128)S(1)} %shard_map.84.refs_2_.refs_1_.bounds_ref, bf16[64,1280]{1,0:T(8,128)(2,1)S(1)} %collective-permute-done.6.refs_5_.refs_2_, ...), custom_call_target="tpu_custom_call" | custom-call | flops 8589934592 | bytes 16777216 | tf_op jit(solution)/shard_map/pallas_call | solution.py:321
  31.8 0.1 collective-permute-start.19
  31.9 1.3 %collective-permute-start.17 = (bf16[128,128]{1,0:T(8,128)(2,1)S(1)}, bf16[128,128]{1,0:T(8,128)(2,1)S(1)}, u32[]{:S(2)}, u32[]{:S(2)}) collective-permute-start(bf16[128,128]{1,0:T(8,128)(2,1)S(1)} %shard_map.89), channel_id=1, source_target_pairs={{0,16},{16,0},{1,17},{17,1},{2,18},{18,2},{3,19},{19,3},{4,20},{20... | collective-permute-start | bytes 98312 | tf_op jit(solution)/shard_map/ppermute | solution.py:419
  33.2 0.6 %collective-permute-start.18 = (bf16[128,128]{1,0:T(8,128)(2,1)S(1)}, bf16[128,128]{1,0:T(8,128)(2,1)S(1)}, u32[]{:S(2)}, u32[]{:S(2)}) collective-permute-start(bf16[128,128]{1,0:T(8,128)(2,1)S(1)} %shard_map.89), channel_id=1, source_target_pairs={{0,17},{1,16},{16,1},{17,0},{2,19},{3,18},{18,3},{19,2},{4,21},{5,... | collective-permute-start | bytes 98312 | tf_op jit(solution)/shard_map/ppermute | solution.py:420
  33.7 0.5 %shard_map.87 = (f32[64,128]{1,0:T(8,128)S(1)}, f32[64,128]{1,0:T(8,128)S(1)}) custom-call(bf16[256,4096]{1,0:T(8,128)(2,1)S(1)} %copy-done, s32[8,512]{1,0:T(8,128)S(1)} %shard_map.84.refs_2_.refs_1_.bounds_ref, bf16[64,1280]{1,0:T(8,128)(2,1)S(1)} %collective-permute-done.1.refs_2_, bf16[64,1280]{1,0:T(8,128)(2,1)S(1)} %collective-permute-done.4.refs_3_, ...), custom_call_target="tpu_custom_call" | custom-call | bytes 4194304 | tf_op jit(solution)/shard_map/pallas_call | solution.py:321
  34.3 0.4 %collective-permute-start.15 = (f32[64,128]{1,0:T(8,128)S(1)}, f32[64,128]{1,0:T(8,128)S(1)}, u32[]{:S(2)}, u32[]{:S(2)}) collective-permute-start(f32[64,128]{1,0:T(8,128)S(1)} %get-tuple-element.34.top), channel_id=1, source_target_pairs={{0,1},{1,0},{2,3},{3,2},{4,5},{5,4},{6,7},{7,6},{8,9},{9,8},{10,11... | collective-permute-start | bytes 98312 | tf_op jit(solution)/shard_map/ppermute | solution.py:421
  34.7 0.2 collective-permute-start.16
  34.9 1.0 %collective-permute-done.17.two = bf16[128,128]{1,0:T(8,128)(2,1)S(1)} collective-permute-done((bf16[128,128]{1,0:T(8,128)(2,1)S(1)}, bf16[128,128]{1,0:T(8,128)(2,1)S(1)}, u32[]{:S(2)}, u32[]{:S(2)}) %collective-permute-start.17) | collective-permute-done | bytes 32800 | tf_op jit(solution)/shard_map/ppermute | solution.py:419
  35.9 0.7 %collective-permute-done.18.three = bf16[128,128]{1,0:T(8,128)(2,1)S(1)} collective-permute-done((bf16[128,128]{1,0:T(8,128)(2,1)S(1)}, bf16[128,128]{1,0:T(8,128)(2,1)S(1)}, u32[]{:S(2)}, u32[]{:S(2)}) %collective-permute-start.18) | collective-permute-done | bytes 32800 | tf_op jit(solution)/shard_map/ppermute | solution.py:420
  36.5 0.0 collective-permute-done.15.one_top
  36.5 0.0 collective-permute-done.16.one_low
  36.5 0.0 collective-permute-done.19.far_ref
  36.5 1.1 %shard_map.90 = bf16[256,512]{1,0:T(8,128)(2,1)} custom-call(s32[8,512]{1,0:T(8,128)S(1)} %shard_map.84.refs_2_.refs_1_.bounds_ref, f32[64,128]{1,0:T(8,128)S(1)} %get-tuple-element.34.top, f32[64,128]{1,0:T(8,128)S(1)} %get-tuple-element.35.low, f32[64,128]{1,0:T(8,128)S(1)} %collective-permute-done.15.one_top, ...), custom_call_target="tpu_custom_call" | custom-call | tf_op jit(solution)/shard_map/pallas_call | solution.py:424
  (8 shorter events, 0.0 us)
Async XLA Ops:
  0.0 4.3 %copy-start = (bf16[256,4096]{1,0:T(8,128)(2,1)S(1)}, bf16[256,4096]{1,0:T(8,128)(2,1)}, u32[]{:S(2)}) copy-start(bf16[256,4096]{1,0:T(8,128)(2,1)} %refs_0_.1) | copy-start | bytes 6291460
  1.2 7.4 %collective-permute-start.7 = (bf16[64,1280]{1,0:T(8,128)(2,1)S(1)}, bf16[64,1280]{1,0:T(8,128)(2,1)S(1)}, u32[]{:S(2)}, u32[]{:S(2)}) collective-permute-start(bf16[64,1280]{1,0:T(8,128)(2,1)S(1)} %get-tuple-element.31.refs_7_.refs_0_), channel_id=1, source_target_pairs={{2,0},{6,2},{10,6},{14,10},{12,14},{8,12},{4,8},{0,4},{3,1},{7,3},... | collective-permute-start | bytes 491528 | tf_op jit(solution)/shard_map/ppermute | solution.py:386
  4.3 6.3 %collective-permute-start.2 = (bf16[64,1280]{1,0:T(8,128)(2,1)S(1)}, bf16[64,1280]{1,0:T(8,128)(2,1)S(1)}, u32[]{:S(2)}, u32[]{:S(2)}) collective-permute-start(bf16[64,1280]{1,0:T(8,128)(2,1)S(1)} %get-tuple-element.30.refs_3_), channel_id=1, source_target_pairs={{0,2},{2,6},{6,10},{10,14},{14,12},{12,8},{8,4},{4,0},{1,3},{3,7},... | collective-permute-start | bytes 491528 | tf_op jit(solution)/shard_map/ppermute | solution.py:385
  4.6 24.8 %collective-permute-start.14 = (bf16[4112,128]{1,0:T(8,128)(2,1)S(1)}, bf16[4112,128]{1,0:T(8,128)(2,1)S(1)}, u32[]{:S(2)}, u32[]{:S(2)}) collective-permute-start(bf16[4112,128]{1,0:T(8,128)(2,1)S(1)} %get-tuple-element.32), channel_id=1, source_target_pairs={{0,16},{16,0},{1,17},{17,1},{2,18},{18,2},{3,19},{19,3},{4,20},{20... | collective-permute-start | bytes 3158024 | tf_op jit(solution)/shard_map/ppermute | solution.py:396
  6.6 12.6 %slice-start = ((s8[8388608]{0:T(1024)(128)(4,1)}), s8[4194304]{0:T(1024)(128)(4,1)S(1)}, s32[]{:S(2)}) async-start(s8[8388608]{0:T(1024)(128)(4,1)} %bitcast.4), calls=%async_computation | async-start | bytes 8388608
  6.6 12.6 %slice-start.1 = ((s8[8388608]{0:T(1024)(128)(4,1)}), s8[4194304]{0:T(1024)(128)(4,1)S(1)}, s32[]{:S(2)}) async-start(s8[8388608]{0:T(1024)(128)(4,1)} %bitcast.4), calls=%async_computation.1 | async-start | bytes 8388608
  6.6 7.0 %collective-permute-start = (bf16[64,1280]{1,0:T(8,128)(2,1)S(1)}, bf16[64,1280]{1,0:T(8,128)(2,1)S(1)}, u32[]{:S(2)}, u32[]{:S(2)}) collective-permute-start(bf16[64,1280]{1,0:T(8,128)(2,1)S(1)} %get-tuple-element.30.refs_3_), channel_id=1, source_target_pairs={{2,0},{6,2},{10,6},{14,10},{12,14},{8,12},{4,8},{0,4},{3,1},{7,3},... | collective-permute-start | bytes 491528 | tf_op jit(solution)/shard_map/ppermute | solution.py:388
  8.2 7.1 %collective-permute-start.9 = (bf16[64,1280]{1,0:T(8,128)(2,1)S(1)}, bf16[64,1280]{1,0:T(8,128)(2,1)S(1)}, u32[]{:S(2)}, u32[]{:S(2)}) collective-permute-start(bf16[64,1280]{1,0:T(8,128)(2,1)S(1)} %get-tuple-element.31.refs_7_.refs_0_), channel_id=1, source_target_pairs={{0,2},{2,6},{6,10},{10,14},{14,12},{12,8},{8,4},{4,0},{1,3},{3,7},... | collective-permute-start | bytes 491528 | tf_op jit(solution)/shard_map/ppermute | solution.py:387
  8.6 8.5 %collective-permute-start.8 = (bf16[64,1280]{1,0:T(8,128)(2,1)S(1)}, bf16[64,1280]{1,0:T(8,128)(2,1)S(1)}, u32[]{:S(2)}, u32[]{:S(2)}) collective-permute-start(bf16[64,1280]{1,0:T(8,128)(2,1)S(1)} %collective-permute-done.7.refs_9_.refs_2_), channel_id=1, source_target_pairs={{2,0},{6,2},{10,6},{14,10},{12,14},{8,12},{4,8},{0,4},{3,1},{7,3},... | collective-permute-start | bytes 491528 | tf_op jit(solution)/shard_map/ppermute | solution.py:386
  10.6 8.2 %collective-permute-start.3 = (bf16[64,1280]{1,0:T(8,128)(2,1)S(1)}, bf16[64,1280]{1,0:T(8,128)(2,1)S(1)}, u32[]{:S(2)}, u32[]{:S(2)}) collective-permute-start(bf16[64,1280]{1,0:T(8,128)(2,1)S(1)} %collective-permute-done.2.refs_4_), channel_id=1, source_target_pairs={{0,2},{2,6},{6,10},{10,14},{14,12},{12,8},{8,4},{4,0},{1,3},{3,7},... | collective-permute-start | bytes 491528 | tf_op jit(solution)/shard_map/ppermute | solution.py:385
  13.6 8.0 %collective-permute-start.1 = (bf16[64,1280]{1,0:T(8,128)(2,1)S(1)}, bf16[64,1280]{1,0:T(8,128)(2,1)S(1)}, u32[]{:S(2)}, u32[]{:S(2)}) collective-permute-start(bf16[64,1280]{1,0:T(8,128)(2,1)S(1)} %collective-permute-done.refs_5_), channel_id=1, source_target_pairs={{2,0},{6,2},{10,6},{14,10},{12,14},{8,12},{4,8},{0,4},{3,1},{7,3},... | collective-permute-start | bytes 491528 | tf_op jit(solution)/shard_map/ppermute | solution.py:388
  15.3 8.0 %collective-permute-start.10 = (bf16[64,1280]{1,0:T(8,128)(2,1)S(1)}, bf16[64,1280]{1,0:T(8,128)(2,1)S(1)}, u32[]{:S(2)}, u32[]{:S(2)}) collective-permute-start(bf16[64,1280]{1,0:T(8,128)(2,1)S(1)} %collective-permute-done.9.refs_8_.refs_1_), channel_id=1, source_target_pairs={{0,2},{2,6},{6,10},{10,14},{14,12},{12,8},{8,4},{4,0},{1,3},{3,7},... | collective-permute-start | bytes 491528 | tf_op jit(solution)/shard_map/ppermute | solution.py:387
  17.1 7.1 %collective-permute-start.12 = (bf16[64,1280]{1,0:T(8,128)(2,1)S(1)}, bf16[64,1280]{1,0:T(8,128)(2,1)S(1)}, u32[]{:S(2)}, u32[]{:S(2)}) collective-permute-start(bf16[64,1280]{1,0:T(8,128)(2,1)S(1)} %collective-permute-done.8.refs_6_.refs_5_.refs_4_), channel_id=1, source_target_pairs={{2,0},{6,2},{10,6},{14,10},{12,14},{8,12},{4,8},{0,4},{3,1},{7,3},... | collective-permute-start | bytes 491528 | tf_op jit(solution)/shard_map/ppermute | solution.py:386
  18.8 7.1 %collective-permute-start.4 = (bf16[64,1280]{1,0:T(8,128)(2,1)S(1)}, bf16[64,1280]{1,0:T(8,128)(2,1)S(1)}, u32[]{:S(2)}, u32[]{:S(2)}) collective-permute-start(bf16[64,1280]{1,0:T(8,128)(2,1)S(1)} %collective-permute-done.3.refs_6_), channel_id=1, source_target_pairs={{0,2},{2,6},{6,10},{10,14},{14,12},{12,8},{8,4},{4,0},{1,3},{3,7},... | collective-permute-start | bytes 491528 | tf_op jit(solution)/shard_map/ppermute | solution.py:385
  21.6 8.5 %collective-permute-start.5 = (bf16[64,1280]{1,0:T(8,128)(2,1)S(1)}, bf16[64,1280]{1,0:T(8,128)(2,1)S(1)}, u32[]{:S(2)}, u32[]{:S(2)}) collective-permute-start(bf16[64,1280]{1,0:T(8,128)(2,1)S(1)} %collective-permute-done.1.refs_2_), channel_id=1, source_target_pairs={{2,0},{6,2},{10,6},{14,10},{12,14},{8,12},{4,8},{0,4},{3,1},{7,3},... | collective-permute-start | bytes 491528 | tf_op jit(solution)/shard_map/ppermute | solution.py:388
  23.3 6.8 %collective-permute-start.11 = (bf16[64,1280]{1,0:T(8,128)(2,1)S(1)}, bf16[64,1280]{1,0:T(8,128)(2,1)S(1)}, u32[]{:S(2)}, u32[]{:S(2)}) collective-permute-start(bf16[64,1280]{1,0:T(8,128)(2,1)S(1)} %collective-permute-done.10.refs_10_.refs_3_), channel_id=1, source_target_pairs={{0,2},{2,6},{6,10},{10,14},{14,12},{12,8},{8,4},{4,0},{1,3},{3,7},... | collective-permute-start | bytes 491528 | tf_op jit(solution)/shard_map/ppermute | solution.py:387
  24.2 6.4 %collective-permute-start.13 = (bf16[64,1280]{1,0:T(8,128)(2,1)S(1)}, bf16[64,1280]{1,0:T(8,128)(2,1)S(1)}, u32[]{:S(2)}, u32[]{:S(2)}) collective-permute-start(bf16[64,1280]{1,0:T(8,128)(2,1)S(1)} %collective-permute-done.12.refs_8_.refs_7_.refs_6_), channel_id=1, source_target_pairs={{2,0},{6,2},{10,6},{14,10},{12,14},{8,12},{4,8},{0,4},{3,1},{7,3},... | collective-permute-start | bytes 491528 | tf_op jit(solution)/shard_map/ppermute | solution.py:393
  26.0 5.3 %collective-permute-start.6 = (bf16[64,1280]{1,0:T(8,128)(2,1)S(1)}, bf16[64,1280]{1,0:T(8,128)(2,1)S(1)}, u32[]{:S(2)}, u32[]{:S(2)}) collective-permute-start(bf16[64,1280]{1,0:T(8,128)(2,1)S(1)} %collective-permute-done.4.refs_3_), channel_id=1, source_target_pairs={{0,2},{2,6},{6,10},{10,14},{14,12},{12,8},{8,4},{4,0},{1,3},{3,7},... | collective-permute-start | bytes 491528 | tf_op jit(solution)/shard_map/ppermute | solution.py:392
  31.8 4.7 %collective-permute-start.19 = (f32[256,512]{1,0:T(8,128)S(1)}, f32[256,512]{1,0:T(8,128)S(1)}, u32[]{:S(2)}, u32[]{:S(2)}) collective-permute-start(f32[256,512]{1,0:T(8,128)S(1)} %get-tuple-element.40), channel_id=1, source_target_pairs={{0,1},{1,0},{2,3},{3,2},{4,5},{5,4},{6,7},{7,6},{8,9},{9,8},{10,11... | collective-permute-start | bytes 1572872 | tf_op jit(solution)/shard_map/ppermute | solution.py:413
  31.9 4.0 %collective-permute-start.17 = (bf16[128,128]{1,0:T(8,128)(2,1)S(1)}, bf16[128,128]{1,0:T(8,128)(2,1)S(1)}, u32[]{:S(2)}, u32[]{:S(2)}) collective-permute-start(bf16[128,128]{1,0:T(8,128)(2,1)S(1)} %shard_map.89), channel_id=1, source_target_pairs={{0,16},{16,0},{1,17},{17,1},{2,18},{18,2},{3,19},{19,3},{4,20},{20... | collective-permute-start | bytes 98312 | tf_op jit(solution)/shard_map/ppermute | solution.py:419
  33.2 3.3 %collective-permute-start.18 = (bf16[128,128]{1,0:T(8,128)(2,1)S(1)}, bf16[128,128]{1,0:T(8,128)(2,1)S(1)}, u32[]{:S(2)}, u32[]{:S(2)}) collective-permute-start(bf16[128,128]{1,0:T(8,128)(2,1)S(1)} %shard_map.89), channel_id=1, source_target_pairs={{0,17},{1,16},{16,1},{17,0},{2,19},{3,18},{18,3},{19,2},{4,21},{5,... | collective-permute-start | bytes 98312 | tf_op jit(solution)/shard_map/ppermute | solution.py:420
  34.3 2.2 %collective-permute-start.15 = (f32[64,128]{1,0:T(8,128)S(1)}, f32[64,128]{1,0:T(8,128)S(1)}, u32[]{:S(2)}, u32[]{:S(2)}) collective-permute-start(f32[64,128]{1,0:T(8,128)S(1)} %get-tuple-element.34.top), channel_id=1, source_target_pairs={{0,1},{1,0},{2,3},{3,2},{4,5},{5,4},{6,7},{7,6},{8,9},{9,8},{10,11... | collective-permute-start | bytes 98312 | tf_op jit(solution)/shard_map/ppermute | solution.py:421
  34.7 1.8 %collective-permute-start.16 = (f32[64,128]{1,0:T(8,128)S(1)}, f32[64,128]{1,0:T(8,128)S(1)}, u32[]{:S(2)}, u32[]{:S(2)}) collective-permute-start(f32[64,128]{1,0:T(8,128)S(1)} %get-tuple-element.35.low), channel_id=1, source_target_pairs={{0,1},{1,0},{2,3},{3,2},{4,5},{5,4},{6,7},{7,6},{8,9},{9,8},{10,11... | collective-permute-start | bytes 98312 | tf_op jit(solution)/shard_map/ppermute | solution.py:421

commit v24 on v23

--- a/solution.py
+++ b/solution.py
@@ -274,8 +274,20 @@
             )
     count = rows[sides[0]].shape[0]
     totals = {side: ref[...] for side, ref in zip(sides, starts)}
+    single = None
     for begin, end, from_chunk, to_chunk, meant in plan:
         held = [chunk if from_chunk <= chunk < to_chunk else from_chunk for chunk in range(begin, end)]
+        if last and to_chunk - from_chunk == 1:
+            factor = jnp.concatenate(
+                [firsts[from_chunk][...], seconds[from_chunk][:, : depth - cut]], axis=1
+            )
+            (side,) = meant
+            columns = (begin * rank, end * rank)
+            low, high = other_ends(rows_refs[0], extra, *columns)
+            low, high = low[:, -rank:], high[:, -rank:]
+            here = jnp.transpose(contract(factor, rows[side]))
+            single = jnp.where(group_mask(low, high, here.shape), here, 0.0)
+            continue
         first = jnp.concatenate([firsts[chunk][...] for chunk in held], axis=0)
         second = jnp.concatenate([seconds[chunk][:, : depth - cut] for chunk in held], axis=0)
         tall = jnp.concatenate([rows[side] for side in meant], axis=0)
@@ -298,6 +310,8 @@
     if last:
         (total,) = totals
         total = total + pltpu.roll(total, rank, 1)
+        if single is not None:
+            total = total + jnp.concatenate([single, single], axis=1)
         half = count // 2
         lane = lax.broadcasted_iota(I32, (half, 2 * rank), 1)
         total = jnp.where(lane < rank, total[:half], total[half:])
@@ -401,6 +415,8 @@
     start_mine, start_theirs = rank_call(
         (0, 1), plan, range(before), *held, (hidden, other), bounds, firsts, seconds, ()
     )
+    start_theirs, far = lax.optimization_barrier((start_theirs, far))
+    far = lax.ppermute(far, "tensor", swap)
     plan = [(before, owners, before, owners - 1, (1,))]
     (start_theirs,) = rank_call(
         (1,), plan, range(before, owners - 1), *held, (other,), bounds, firsts, seconds, (start_theirs,), False
@@ -409,8 +425,6 @@
     (theirs,) = rank_call(
         (1,), plan, [owners - 1], *held, (other,), bounds, firsts, seconds, (start_theirs,)
     )
-    theirs, far = lax.optimization_barrier((theirs, far))
-    far = lax.ppermute(far, "tensor", swap)
     plan = [(before, owners, before, owners, (0,))]
     mine = rank_call(
         (0,), plan, range(before, owners), *held, (hidden,), bounds, firsts, seconds, (start_mine,)

time: 37.8 us -> 38 us (level)
    ppermute x1, starting transfers between devices: 0.56 us -> 0.03 us  [per_device(): lax.ppermute(theirs, ('groups', 'tensor'), [(0, 3), (1, 2), (2, 1), (3, 0)])]
    ppermute x2, starting transfers between devices: 0.58 us -> 1.02 us  [per_device(): one = [lax.ppermute(part, 'tensor', swap) for part in mine]]
  transfers between devices with their start and end apart: 20 -> 20, of which waited for: 7 -> 7; matrix products, arithmetic and copies ran while one was open for 0% -> 0% of each run, Pallas kernels for 12% -> 13%
where the time goes in v24:
time: 38 us; the launch traced here: 37.9 us
  starting transfers between devices  20 us (53%)
  waiting for transfers between devices  10.4 us (27%)
  Pallas kernels  7.37 us (19%)
    ppermute x3, starting transfers between devices, per_device(): d = lax.ppermute(behind[1], 'batch', backward)  6.79 us
    ppermute x3, starting transfers between devices, per_device(): c = lax.ppermute(behind[0], 'batch', backward)  5.02 us
    ppermute x1, waiting for transfers between devices, per_device(): other = lax.ppermute(to_other, 'groups', swap)  3.05 us
    ppermute x3, waiting for transfers between devices, per_device(): c = lax.ppermute(behind[0], 'batch', backward)  2.91 us
    pallas_call x4, Pallas kernels, rank_call(): pl.pallas_call(functools.partial(rank_kernel, sides, plan, chunks, depth,...  2.44 us
    pallas_call x1, Pallas kernels, base_call(): pl.pallas_call(base_kernel, out_shape=(out, out), in_specs=[VMEM] * 2, ou...  2.35 us
    ppermute x1, starting transfers between devices, per_device(): other = lax.ppermute(to_other, 'groups', swap)  2.03 us
    ppermute x3, waiting for transfers between devices, per_device(): d = lax.ppermute(behind[1], 'batch', backward)  1.94 us
  transfers between devices with their start and end apart: 20, of which 7 were waited for; matrix products, arithmetic and copies ran while one was open for 0% of the time, Pallas kernels for 13%

profile of v24, /device:TPU:0, one launch (start us, length us, event | category | flops | bytes accessed | tf_op | source)
XLA Modules:
  0.0 37.9 jit_solution(14781942501314494836)
XLA Ops:
  0.0 1.2 %shard_map.82 = (bf16[64,1280]{1,0:T(8,128)(2,1)S(1)}, bf16[64,1280]{1,0:T(8,128)(2,1)S(1)}, s32[8,512]{1,0:T(8,128)S(1)}) custom-call(bf16[64,4096]{1,0:T(8,128)(2,1)} %bitcast.6, bf16[64,512]{1,0:T(8,128)(2,1)} %bitcast.7, s32[1,4]{1,0:T(1,128)} %demand_ref.1, s32[1,4]{1,0:T(1,128)} %lengths_ref.1, s32[8]{0:T(128)} %holder_ref.1, ...), custom_call_target="tpu_custom_call" | custom-call | flops 8589934592 | bytes 16777216 | tf_op jit(solution)/shard_map/pallas_call | solution.py:137
  1.2 3.1 %collective-permute-start.7 = (bf16[64,1280]{1,0:T(8,128)(2,1)S(1)}, bf16[64,1280]{1,0:T(8,128)(2,1)S(1)}, u32[]{:S(2)}, u32[]{:S(2)}) collective-permute-start(bf16[64,1280]{1,0:T(8,128)(2,1)S(1)} %get-tuple-element.31.refs_7_.refs_0_), channel_id=1, source_target_pairs={{2,0},{6,2},{10,6},{14,10},{12,14},{8,12},{4,8},{0,4},{3,1},{7,3},... | collective-permute-start | bytes 491528 | tf_op jit(solution)/shard_map/ppermute | solution.py:400
  4.3 0.0 collective-permute-start.2
  4.3 0.3 shard_map.83
  4.6 2.0 %collective-permute-start.14 = (bf16[4112,128]{1,0:T(8,128)(2,1)S(1)}, bf16[4112,128]{1,0:T(8,128)(2,1)S(1)}, u32[]{:S(2)}, u32[]{:S(2)}) collective-permute-start(bf16[4112,128]{1,0:T(8,128)(2,1)S(1)} %get-tuple-element.32), channel_id=1, source_target_pairs={{0,16},{16,0},{1,17},{17,1},{2,18},{18,2},{3,19},{19,3},{4,20},{20... | collective-permute-start | bytes 3158024 | tf_op jit(solution)/shard_map/ppermute | solution.py:410
  6.6 1.6 %collective-permute-start = (bf16[64,1280]{1,0:T(8,128)(2,1)S(1)}, bf16[64,1280]{1,0:T(8,128)(2,1)S(1)}, u32[]{:S(2)}, u32[]{:S(2)}) collective-permute-start(bf16[64,1280]{1,0:T(8,128)(2,1)S(1)} %get-tuple-element.30.refs_3_), channel_id=1, source_target_pairs={{2,0},{6,2},{10,6},{14,10},{12,14},{8,12},{4,8},{0,4},{3,1},{7,3},... | collective-permute-start | bytes 491528 | tf_op jit(solution)/shard_map/ppermute | solution.py:402
  8.2 0.4 %collective-permute-start.9 = (bf16[64,1280]{1,0:T(8,128)(2,1)S(1)}, bf16[64,1280]{1,0:T(8,128)(2,1)S(1)}, u32[]{:S(2)}, u32[]{:S(2)}) collective-permute-start(bf16[64,1280]{1,0:T(8,128)(2,1)S(1)} %get-tuple-element.31.refs_7_.refs_0_), channel_id=1, source_target_pairs={{0,2},{2,6},{6,10},{10,14},{14,12},{12,8},{8,4},{4,0},{1,3},{3,7},... | collective-permute-start | bytes 491528 | tf_op jit(solution)/shard_map/ppermute | solution.py:401
  8.6 0.0 collective-permute-done.7.refs_9_.refs_2_
  8.6 2.0 %collective-permute-start.8 = (bf16[64,1280]{1,0:T(8,128)(2,1)S(1)}, bf16[64,1280]{1,0:T(8,128)(2,1)S(1)}, u32[]{:S(2)}, u32[]{:S(2)}) collective-permute-start(bf16[64,1280]{1,0:T(8,128)(2,1)S(1)} %collective-permute-done.7.refs_9_.refs_2_), channel_id=1, source_target_pairs={{2,0},{6,2},{10,6},{14,10},{12,14},{8,12},{4,8},{0,4},{3,1},{7,3},... | collective-permute-start | bytes 491528 | tf_op jit(solution)/shard_map/ppermute | solution.py:400
  10.6 0.0 collective-permute-done.2.refs_4_
  10.6 0.1 collective-permute-start.3
  10.7 2.9 %collective-permute-done.refs_5_ = bf16[64,1280]{1,0:T(8,128)(2,1)S(1)} collective-permute-done((bf16[64,1280]{1,0:T(8,128)(2,1)S(1)}, bf16[64,1280]{1,0:T(8,128)(2,1)S(1)}, u32[]{:S(2)}, u32[]{:S(2)}) %collective-permute-start) | collective-permute-done | bytes 163872 | tf_op jit(solution)/shard_map/ppermute | solution.py:402
  13.6 1.7 %collective-permute-start.1 = (bf16[64,1280]{1,0:T(8,128)(2,1)S(1)}, bf16[64,1280]{1,0:T(8,128)(2,1)S(1)}, u32[]{:S(2)}, u32[]{:S(2)}) collective-permute-start(bf16[64,1280]{1,0:T(8,128)(2,1)S(1)} %collective-permute-done.refs_5_), channel_id=1, source_target_pairs={{2,0},{6,2},{10,6},{14,10},{12,14},{8,12},{4,8},{0,4},{3,1},{7,3},... | collective-permute-start | bytes 491528 | tf_op jit(solution)/shard_map/ppermute | solution.py:402
  15.3 0.0 collective-permute-done.9.refs_8_.refs_1_
  15.3 0.4 %collective-permute-start.10 = (bf16[64,1280]{1,0:T(8,128)(2,1)S(1)}, bf16[64,1280]{1,0:T(8,128)(2,1)S(1)}, u32[]{:S(2)}, u32[]{:S(2)}) collective-permute-start(bf16[64,1280]{1,0:T(8,128)(2,1)S(1)} %collective-permute-done.9.refs_8_.refs_1_), channel_id=1, source_target_pairs={{0,2},{2,6},{6,10},{10,14},{14,12},{12,8},{8,4},{4,0},{1,3},{3,7},... | collective-permute-start | bytes 491528 | tf_op jit(solution)/shard_map/ppermute | solution.py:401
  15.7 1.4 %collective-permute-done.8.refs_6_.refs_5_.refs_4_ = bf16[64,1280]{1,0:T(8,128)(2,1)S(1)} collective-permute-done((bf16[64,1280]{1,0:T(8,128)(2,1)S(1)}, bf16[64,1280]{1,0:T(8,128)(2,1)S(1)}, u32[]{:S(2)}, u32[]{:S(2)}) %collective-permute-start.8) | collective-permute-done | bytes 163872 | tf_op jit(solution)/shard_map/ppermute | solution.py:400
  17.1 1.7 %collective-permute-start.12 = (bf16[64,1280]{1,0:T(8,128)(2,1)S(1)}, bf16[64,1280]{1,0:T(8,128)(2,1)S(1)}, u32[]{:S(2)}, u32[]{:S(2)}) collective-permute-start(bf16[64,1280]{1,0:T(8,128)(2,1)S(1)} %collective-permute-done.8.refs_6_.refs_5_.refs_4_), channel_id=1, source_target_pairs={{2,0},{6,2},{10,6},{14,10},{12,14},{8,12},{4,8},{0,4},{3,1},{7,3},... | collective-permute-start | bytes 491528 | tf_op jit(solution)/shard_map/ppermute | solution.py:400
  18.8 0.0 collective-permute-done.3.refs_6_
  18.8 0.4 %collective-permute-start.4 = (bf16[64,1280]{1,0:T(8,128)(2,1)S(1)}, bf16[64,1280]{1,0:T(8,128)(2,1)S(1)}, u32[]{:S(2)}, u32[]{:S(2)}) collective-permute-start(bf16[64,1280]{1,0:T(8,128)(2,1)S(1)} %collective-permute-done.3.refs_6_), channel_id=1, source_target_pairs={{0,2},{2,6},{6,10},{10,14},{14,12},{12,8},{8,4},{4,0},{1,3},{3,7},... | collective-permute-start | bytes 491528 | tf_op jit(solution)/shard_map/ppermute | solution.py:399
  19.2 2.3 %shard_map.85 = (f32[256,512]{1,0:T(8,128)S(1)}, f32[256,512]{1,0:T(8,128)S(1)}) custom-call(bf16[256,4096]{1,0:T(8,128)(2,1)S(1)} %copy-done, bf16[4096,1024]{1,0:T(8,128)(2,1)S(1)} %bitcast.5), custom_call_target="tpu_custom_call" | custom-call | bytes 4194304 | tf_op jit(solution)/shard_map/pallas_call | solution.py:219
  21.6 0.0 collective-permute-done.1.refs_2_
  21.6 1.7 %collective-permute-start.5 = (bf16[64,1280]{1,0:T(8,128)(2,1)S(1)}, bf16[64,1280]{1,0:T(8,128)(2,1)S(1)}, u32[]{:S(2)}, u32[]{:S(2)}) collective-permute-start(bf16[64,1280]{1,0:T(8,128)(2,1)S(1)} %collective-permute-done.1.refs_2_), channel_id=1, source_target_pairs={{2,0},{6,2},{10,6},{14,10},{12,14},{8,12},{4,8},{0,4},{3,1},{7,3},... | collective-permute-start | bytes 491528 | tf_op jit(solution)/shard_map/ppermute | solution.py:402
  23.3 0.0 collective-permute-done.10.refs_10_.refs_3_
  23.3 0.4 %collective-permute-start.11 = (bf16[64,1280]{1,0:T(8,128)(2,1)S(1)}, bf16[64,1280]{1,0:T(8,128)(2,1)S(1)}, u32[]{:S(2)}, u32[]{:S(2)}) collective-permute-start(bf16[64,1280]{1,0:T(8,128)(2,1)S(1)} %collective-permute-done.10.refs_10_.refs_3_), channel_id=1, source_target_pairs={{0,2},{2,6},{6,10},{10,14},{14,12},{12,8},{8,4},{4,0},{1,3},{3,7},... | collective-permute-start | bytes 491528 | tf_op jit(solution)/shard_map/ppermute | solution.py:401
  23.7 0.6 %collective-permute-done.12.refs_8_.refs_7_.refs_6_ = bf16[64,1280]{1,0:T(8,128)(2,1)S(1)} collective-permute-done((bf16[64,1280]{1,0:T(8,128)(2,1)S(1)}, bf16[64,1280]{1,0:T(8,128)(2,1)S(1)}, u32[]{:S(2)}, u32[]{:S(2)}) %collective-permute-start.12) | collective-permute-done | bytes 163872 | tf_op jit(solution)/shard_map/ppermute | solution.py:400
  24.2 1.7 %collective-permute-start.13 = (bf16[64,1280]{1,0:T(8,128)(2,1)S(1)}, bf16[64,1280]{1,0:T(8,128)(2,1)S(1)}, u32[]{:S(2)}, u32[]{:S(2)}) collective-permute-start(bf16[64,1280]{1,0:T(8,128)(2,1)S(1)} %collective-permute-done.12.refs_8_.refs_7_.refs_6_), channel_id=1, source_target_pairs={{2,0},{6,2},{10,6},{14,10},{12,14},{8,12},{4,8},{0,4},{3,1},{7,3},... | collective-permute-start | bytes 491528 | tf_op jit(solution)/shard_map/ppermute | solution.py:407
  26.0 0.0 collective-permute-done.4.refs_3_
  26.0 0.3 collective-permute-start.6
  26.3 3.1 %collective-permute-done.14.refs_1_.refs_0_ = bf16[4112,128]{1,0:T(8,128)(2,1)S(1)} collective-permute-done((bf16[4112,128]{1,0:T(8,128)(2,1)S(1)}, bf16[4112,128]{1,0:T(8,128)(2,1)S(1)}, u32[]{:S(2)}, u32[]{:S(2)}) %collective-permute-start.14) | collective-permute-done | bytes 1052704 | tf_op jit(solution)/shard_map/ppermute | solution.py:410
  29.3 0.7 %shard_map.86 = (f32[256,128]{1,0:T(8,128)S(1)}, f32[256,128]{1,0:T(8,128)S(1)}) custom-call(bf16[256,4096]{1,0:T(8,128)(2,1)S(1)} %copy-done, bf16[4112,128]{1,0:T(8,128)(2,1)S(1)} %collective-permute-done.14.refs_1_.refs_0_, s32[8,512]{1,0:T(8,128)S(1)} %shard_map.84.refs_2_.refs_1_.bounds_ref, bf16[64,1280]{1,0:T(8,128)(2,1)S(1)} %get-tuple-element.30.refs_3_, ...), custom_call_target="tpu_custom_call" | custom-call | flops 8589934592 | bytes 16777216 | tf_op jit(solution)/shard_map/pallas_call | solution.py:335
  30.1 0.1 collective-permute-start.19
  30.2 0.0 collective-permute-done.5.refs_4_
  30.2 0.0 collective-permute-done.11.refs_7_.refs_6_.refs_5_
  30.2 0.5 %shard_map.88.refs_4_ = f32[256,128]{1,0:T(8,128)S(1)} custom-call(bf16[4112,128]{1,0:T(8,128)(2,1)S(1)} %collective-permute-done.14.refs_1_.refs_0_, s32[8,512]{1,0:T(8,128)S(1)} %shard_map.84.refs_2_.refs_1_.bounds_ref, bf16[64,1280]{1,0:T(8,128)(2,1)S(1)} %collective-permute-done.1.refs_2_, bf16[64,1280]{1,0:T(8,128)(2,1)S(1)} %collective-permute-done.4.refs_3_, ...), custom_call_target="tpu_custom_call" | custom-call | flops 8589934592 | bytes 16777216 | tf_op jit(solution)/shard_map/pallas_call | solution.py:335
  30.7 0.0 collective-permute-done.13.refs_9_.refs_3_.refs_7_
  30.7 0.6 %collective-permute-done.6.refs_5_.refs_2_ = bf16[64,1280]{1,0:T(8,128)(2,1)S(1)} collective-permute-done((bf16[64,1280]{1,0:T(8,128)(2,1)S(1)}, bf16[64,1280]{1,0:T(8,128)(2,1)S(1)}, u32[]{:S(2)}, u32[]{:S(2)}) %collective-permute-start.6) | collective-permute-done | bytes 163872 | tf_op jit(solution)/shard_map/ppermute | solution.py:406
  31.3 0.7 %shard_map.89 = bf16[128,128]{1,0:T(8,128)(2,1)S(1)} custom-call(bf16[4112,128]{1,0:T(8,128)(2,1)S(1)} %collective-permute-done.14.refs_1_.refs_0_, s32[8,512]{1,0:T(8,128)S(1)} %shard_map.84.refs_2_.refs_1_.bounds_ref, bf16[64,1280]{1,0:T(8,128)(2,1)S(1)} %collective-permute-done.6.refs_5_.refs_2_, ...), custom_call_target="tpu_custom_call" | custom-call | flops 8589934592 | bytes 16777216 | tf_op jit(solution)/shard_map/pallas_call | solution.py:335
  32.0 1.3 %collective-permute-start.17 = (bf16[128,128]{1,0:T(8,128)(2,1)S(1)}, bf16[128,128]{1,0:T(8,128)(2,1)S(1)}, u32[]{:S(2)}, u32[]{:S(2)}) collective-permute-start(bf16[128,128]{1,0:T(8,128)(2,1)S(1)} %shard_map.89), channel_id=1, source_target_pairs={{0,16},{16,0},{1,17},{17,1},{2,18},{18,2},{3,19},{19,3},{4,20},{20... | collective-permute-start | bytes 98312 | tf_op jit(solution)/shard_map/ppermute | solution.py:433
  33.3 0.0 collective-permute-start.18
  33.3 0.5 %shard_map.87 = (f32[64,128]{1,0:T(8,128)S(1)}, f32[64,128]{1,0:T(8,128)S(1)}) custom-call(bf16[256,4096]{1,0:T(8,128)(2,1)S(1)} %copy-done, s32[8,512]{1,0:T(8,128)S(1)} %shard_map.84.refs_2_.refs_1_.bounds_ref, bf16[64,1280]{1,0:T(8,128)(2,1)S(1)} %collective-permute-done.1.refs_2_, bf16[64,1280]{1,0:T(8,128)(2,1)S(1)} %collective-permute-done.4.refs_3_, ...), custom_call_target="tpu_custom_call" | custom-call | bytes 4194304 | tf_op jit(solution)/shard_map/pallas_call | solution.py:335
  33.8 0.9 %collective-permute-start.15 = (f32[64,128]{1,0:T(8,128)S(1)}, f32[64,128]{1,0:T(8,128)S(1)}, u32[]{:S(2)}, u32[]{:S(2)}) collective-permute-start(f32[64,128]{1,0:T(8,128)S(1)} %get-tuple-element.34.top), channel_id=1, source_target_pairs={{0,1},{1,0},{2,3},{3,2},{4,5},{5,4},{6,7},{7,6},{8,9},{9,8},{10,11... | collective-permute-start | bytes 98312 | tf_op jit(solution)/shard_map/ppermute | solution.py:435
  34.8 0.1 collective-permute-start.16
  34.9 1.1 %collective-permute-done.17.two = bf16[128,128]{1,0:T(8,128)(2,1)S(1)} collective-permute-done((bf16[128,128]{1,0:T(8,128)(2,1)S(1)}, bf16[128,128]{1,0:T(8,128)(2,1)S(1)}, u32[]{:S(2)}, u32[]{:S(2)}) %collective-permute-start.17) | collective-permute-done | bytes 32800 | tf_op jit(solution)/shard_map/ppermute | solution.py:433
  35.9 0.8 %collective-permute-done.18.three = bf16[128,128]{1,0:T(8,128)(2,1)S(1)} collective-permute-done((bf16[128,128]{1,0:T(8,128)(2,1)S(1)}, bf16[128,128]{1,0:T(8,128)(2,1)S(1)}, u32[]{:S(2)}, u32[]{:S(2)}) %collective-permute-start.18) | collective-permute-done | bytes 32800 | tf_op jit(solution)/shard_map/ppermute | solution.py:434
  36.7 0.0 collective-permute-done.15.one_top
  36.7 0.0 collective-permute-done.16.one_low
  36.7 0.0 collective-permute-done.19.far_ref
  36.7 1.1 %shard_map.90 = bf16[256,512]{1,0:T(8,128)(2,1)} custom-call(s32[8,512]{1,0:T(8,128)S(1)} %shard_map.84.refs_2_.refs_1_.bounds_ref, f32[64,128]{1,0:T(8,128)S(1)} %get-tuple-element.34.top, f32[64,128]{1,0:T(8,128)S(1)} %get-tuple-element.35.low, f32[64,128]{1,0:T(8,128)S(1)} %collective-permute-done.15.one_top, ...), custom_call_target="tpu_custom_call" | custom-call | tf_op jit(solution)/shard_map/pallas_call | solution.py:438
  (8 shorter events, 0.0 us)
Async XLA Ops:
  0.0 4.3 %copy-start = (bf16[256,4096]{1,0:T(8,128)(2,1)S(1)}, bf16[256,4096]{1,0:T(8,128)(2,1)}, u32[]{:S(2)}) copy-start(bf16[256,4096]{1,0:T(8,128)(2,1)} %refs_0_.1) | copy-start | bytes 6291460
  1.2 7.4 %collective-permute-start.7 = (bf16[64,1280]{1,0:T(8,128)(2,1)S(1)}, bf16[64,1280]{1,0:T(8,128)(2,1)S(1)}, u32[]{:S(2)}, u32[]{:S(2)}) collective-permute-start(bf16[64,1280]{1,0:T(8,128)(2,1)S(1)} %get-tuple-element.31.refs_7_.refs_0_), channel_id=1, source_target_pairs={{2,0},{6,2},{10,6},{14,10},{12,14},{8,12},{4,8},{0,4},{3,1},{7,3},... | collective-permute-start | bytes 491528 | tf_op jit(solution)/shard_map/ppermute | solution.py:400
  4.3 6.3 %collective-permute-start.2 = (bf16[64,1280]{1,0:T(8,128)(2,1)S(1)}, bf16[64,1280]{1,0:T(8,128)(2,1)S(1)}, u32[]{:S(2)}, u32[]{:S(2)}) collective-permute-start(bf16[64,1280]{1,0:T(8,128)(2,1)S(1)} %get-tuple-element.30.refs_3_), channel_id=1, source_target_pairs={{0,2},{2,6},{6,10},{10,14},{14,12},{12,8},{8,4},{4,0},{1,3},{3,7},... | collective-permute-start | bytes 491528 | tf_op jit(solution)/shard_map/ppermute | solution.py:399
  4.6 24.8 %collective-permute-start.14 = (bf16[4112,128]{1,0:T(8,128)(2,1)S(1)}, bf16[4112,128]{1,0:T(8,128)(2,1)S(1)}, u32[]{:S(2)}, u32[]{:S(2)}) collective-permute-start(bf16[4112,128]{1,0:T(8,128)(2,1)S(1)} %get-tuple-element.32), channel_id=1, source_target_pairs={{0,16},{16,0},{1,17},{17,1},{2,18},{18,2},{3,19},{19,3},{4,20},{20... | collective-permute-start | bytes 3158024 | tf_op jit(solution)/shard_map/ppermute | solution.py:410
  6.6 12.6 %slice-start = ((s8[8388608]{0:T(1024)(128)(4,1)}), s8[4194304]{0:T(1024)(128)(4,1)S(1)}, s32[]{:S(2)}) async-start(s8[8388608]{0:T(1024)(128)(4,1)} %bitcast.4), calls=%async_computation | async-start | bytes 8388608
  6.6 12.6 %slice-start.1 = ((s8[8388608]{0:T(1024)(128)(4,1)}), s8[4194304]{0:T(1024)(128)(4,1)S(1)}, s32[]{:S(2)}) async-start(s8[8388608]{0:T(1024)(128)(4,1)} %bitcast.4), calls=%async_computation.1 | async-start | bytes 8388608
  6.6 7.0 %collective-permute-start = (bf16[64,1280]{1,0:T(8,128)(2,1)S(1)}, bf16[64,1280]{1,0:T(8,128)(2,1)S(1)}, u32[]{:S(2)}, u32[]{:S(2)}) collective-permute-start(bf16[64,1280]{1,0:T(8,128)(2,1)S(1)} %get-tuple-element.30.refs_3_), channel_id=1, source_target_pairs={{2,0},{6,2},{10,6},{14,10},{12,14},{8,12},{4,8},{0,4},{3,1},{7,3},... | collective-permute-start | bytes 491528 | tf_op jit(solution)/shard_map/ppermute | solution.py:402
  8.2 7.1 %collective-permute-start.9 = (bf16[64,1280]{1,0:T(8,128)(2,1)S(1)}, bf16[64,1280]{1,0:T(8,128)(2,1)S(1)}, u32[]{:S(2)}, u32[]{:S(2)}) collective-permute-start(bf16[64,1280]{1,0:T(8,128)(2,1)S(1)} %get-tuple-element.31.refs_7_.refs_0_), channel_id=1, source_target_pairs={{0,2},{2,6},{6,10},{10,14},{14,12},{12,8},{8,4},{4,0},{1,3},{3,7},... | collective-permute-start | bytes 491528 | tf_op jit(solution)/shard_map/ppermute | solution.py:401
  8.6 8.5 %collective-permute-start.8 = (bf16[64,1280]{1,0:T(8,128)(2,1)S(1)}, bf16[64,1280]{1,0:T(8,128)(2,1)S(1)}, u32[]{:S(2)}, u32[]{:S(2)}) collective-permute-start(bf16[64,1280]{1,0:T(8,128)(2,1)S(1)} %collective-permute-done.7.refs_9_.refs_2_), channel_id=1, source_target_pairs={{2,0},{6,2},{10,6},{14,10},{12,14},{8,12},{4,8},{0,4},{3,1},{7,3},... | collective-permute-start | bytes 491528 | tf_op jit(solution)/shard_map/ppermute | solution.py:400
  10.6 8.2 %collective-permute-start.3 = (bf16[64,1280]{1,0:T(8,128)(2,1)S(1)}, bf16[64,1280]{1,0:T(8,128)(2,1)S(1)}, u32[]{:S(2)}, u32[]{:S(2)}) collective-permute-start(bf16[64,1280]{1,0:T(8,128)(2,1)S(1)} %collective-permute-done.2.refs_4_), channel_id=1, source_target_pairs={{0,2},{2,6},{6,10},{10,14},{14,12},{12,8},{8,4},{4,0},{1,3},{3,7},... | collective-permute-start | bytes 491528 | tf_op jit(solution)/shard_map/ppermute | solution.py:399
  13.6 8.0 %collective-permute-start.1 = (bf16[64,1280]{1,0:T(8,128)(2,1)S(1)}, bf16[64,1280]{1,0:T(8,128)(2,1)S(1)}, u32[]{:S(2)}, u32[]{:S(2)}) collective-permute-start(bf16[64,1280]{1,0:T(8,128)(2,1)S(1)} %collective-permute-done.refs_5_), channel_id=1, source_target_pairs={{2,0},{6,2},{10,6},{14,10},{12,14},{8,12},{4,8},{0,4},{3,1},{7,3},... | collective-permute-start | bytes 491528 | tf_op jit(solution)/shard_map/ppermute | solution.py:402
  15.3 8.0 %collective-permute-start.10 = (bf16[64,1280]{1,0:T(8,128)(2,1)S(1)}, bf16[64,1280]{1,0:T(8,128)(2,1)S(1)}, u32[]{:S(2)}, u32[]{:S(2)}) collective-permute-start(bf16[64,1280]{1,0:T(8,128)(2,1)S(1)} %collective-permute-done.9.refs_8_.refs_1_), channel_id=1, source_target_pairs={{0,2},{2,6},{6,10},{10,14},{14,12},{12,8},{8,4},{4,0},{1,3},{3,7},... | collective-permute-start | bytes 491528 | tf_op jit(solution)/shard_map/ppermute | solution.py:401
  17.1 7.1 %collective-permute-start.12 = (bf16[64,1280]{1,0:T(8,128)(2,1)S(1)}, bf16[64,1280]{1,0:T(8,128)(2,1)S(1)}, u32[]{:S(2)}, u32[]{:S(2)}) collective-permute-start(bf16[64,1280]{1,0:T(8,128)(2,1)S(1)} %collective-permute-done.8.refs_6_.refs_5_.refs_4_), channel_id=1, source_target_pairs={{2,0},{6,2},{10,6},{14,10},{12,14},{8,12},{4,8},{0,4},{3,1},{7,3},... | collective-permute-start | bytes 491528 | tf_op jit(solution)/shard_map/ppermute | solution.py:400
  18.8 7.1 %collective-permute-start.4 = (bf16[64,1280]{1,0:T(8,128)(2,1)S(1)}, bf16[64,1280]{1,0:T(8,128)(2,1)S(1)}, u32[]{:S(2)}, u32[]{:S(2)}) collective-permute-start(bf16[64,1280]{1,0:T(8,128)(2,1)S(1)} %collective-permute-done.3.refs_6_), channel_id=1, source_target_pairs={{0,2},{2,6},{6,10},{10,14},{14,12},{12,8},{8,4},{4,0},{1,3},{3,7},... | collective-permute-start | bytes 491528 | tf_op jit(solution)/shard_map/ppermute | solution.py:399
  21.6 8.6 %collective-permute-start.5 = (bf16[64,1280]{1,0:T(8,128)(2,1)S(1)}, bf16[64,1280]{1,0:T(8,128)(2,1)S(1)}, u32[]{:S(2)}, u32[]{:S(2)}) collective-permute-start(bf16[64,1280]{1,0:T(8,128)(2,1)S(1)} %collective-permute-done.1.refs_2_), channel_id=1, source_target_pairs={{2,0},{6,2},{10,6},{14,10},{12,14},{8,12},{4,8},{0,4},{3,1},{7,3},... | collective-permute-start | bytes 491528 | tf_op jit(solution)/shard_map/ppermute | solution.py:402
  23.3 6.9 %collective-permute-start.11 = (bf16[64,1280]{1,0:T(8,128)(2,1)S(1)}, bf16[64,1280]{1,0:T(8,128)(2,1)S(1)}, u32[]{:S(2)}, u32[]{:S(2)}) collective-permute-start(bf16[64,1280]{1,0:T(8,128)(2,1)S(1)} %collective-permute-done.10.refs_10_.refs_3_), channel_id=1, source_target_pairs={{0,2},{2,6},{6,10},{10,14},{14,12},{12,8},{8,4},{4,0},{1,3},{3,7},... | collective-permute-start | bytes 491528 | tf_op jit(solution)/shard_map/ppermute | solution.py:401
  24.2 6.5 %collective-permute-start.13 = (bf16[64,1280]{1,0:T(8,128)(2,1)S(1)}, bf16[64,1280]{1,0:T(8,128)(2,1)S(1)}, u32[]{:S(2)}, u32[]{:S(2)}) collective-permute-start(bf16[64,1280]{1,0:T(8,128)(2,1)S(1)} %collective-permute-done.12.refs_8_.refs_7_.refs_6_), channel_id=1, source_target_pairs={{2,0},{6,2},{10,6},{14,10},{12,14},{8,12},{4,8},{0,4},{3,1},{7,3},... | collective-permute-start | bytes 491528 | tf_op jit(solution)/shard_map/ppermute | solution.py:407
  26.0 5.3 %collective-permute-start.6 = (bf16[64,1280]{1,0:T(8,128)(2,1)S(1)}, bf16[64,1280]{1,0:T(8,128)(2,1)S(1)}, u32[]{:S(2)}, u32[]{:S(2)}) collective-permute-start(bf16[64,1280]{1,0:T(8,128)(2,1)S(1)} %collective-permute-done.4.refs_3_), channel_id=1, source_target_pairs={{0,2},{2,6},{6,10},{10,14},{14,12},{12,8},{8,4},{4,0},{1,3},{3,7},... | collective-permute-start | bytes 491528 | tf_op jit(solution)/shard_map/ppermute | solution.py:406
  30.1 6.6 %collective-permute-start.19 = (f32[256,512]{1,0:T(8,128)S(1)}, f32[256,512]{1,0:T(8,128)S(1)}, u32[]{:S(2)}, u32[]{:S(2)}) collective-permute-start(f32[256,512]{1,0:T(8,128)S(1)} %get-tuple-element.40), channel_id=1, source_target_pairs={{0,1},{1,0},{2,3},{3,2},{4,5},{5,4},{6,7},{7,6},{8,9},{9,8},{10,11... | collective-permute-start | bytes 1572872 | tf_op jit(solution)/shard_map/ppermute | solution.py:419
  32.0 4.0 %collective-permute-start.17 = (bf16[128,128]{1,0:T(8,128)(2,1)S(1)}, bf16[128,128]{1,0:T(8,128)(2,1)S(1)}, u32[]{:S(2)}, u32[]{:S(2)}) collective-permute-start(bf16[128,128]{1,0:T(8,128)(2,1)S(1)} %shard_map.89), channel_id=1, source_target_pairs={{0,16},{16,0},{1,17},{17,1},{2,18},{18,2},{3,19},{19,3},{4,20},{20... | collective-permute-start | bytes 98312 | tf_op jit(solution)/shard_map/ppermute | solution.py:433
  33.3 3.5 %collective-permute-start.18 = (bf16[128,128]{1,0:T(8,128)(2,1)S(1)}, bf16[128,128]{1,0:T(8,128)(2,1)S(1)}, u32[]{:S(2)}, u32[]{:S(2)}) collective-permute-start(bf16[128,128]{1,0:T(8,128)(2,1)S(1)} %shard_map.89), channel_id=1, source_target_pairs={{0,17},{1,16},{16,1},{17,0},{2,19},{3,18},{18,3},{19,2},{4,21},{5,... | collective-permute-start | bytes 98312 | tf_op jit(solution)/shard_map/ppermute | solution.py:434
  33.8 2.9 %collective-permute-start.15 = (f32[64,128]{1,0:T(8,128)S(1)}, f32[64,128]{1,0:T(8,128)S(1)}, u32[]{:S(2)}, u32[]{:S(2)}) collective-permute-start(f32[64,128]{1,0:T(8,128)S(1)} %get-tuple-element.34.top), channel_id=1, source_target_pairs={{0,1},{1,0},{2,3},{3,2},{4,5},{5,4},{6,7},{7,6},{8,9},{9,8},{10,11... | collective-permute-start | bytes 98312 | tf_op jit(solution)/shard_map/ppermute | solution.py:435
  34.8 1.9 %collective-permute-start.16 = (f32[64,128]{1,0:T(8,128)S(1)}, f32[64,128]{1,0:T(8,128)S(1)}, u32[]{:S(2)}, u32[]{:S(2)}) collective-permute-start(f32[64,128]{1,0:T(8,128)S(1)} %get-tuple-element.35.low), channel_id=1, source_target_pairs={{0,1},{1,0},{2,3},{3,2},{4,5},{5,4},{6,7},{7,6},{8,9},{9,8},{10,11... | collective-permute-start | bytes 98312 | tf_op jit(solution)/shard_map/ppermute | solution.py:435

commit v25 on v22

--- a/solution.py
+++ b/solution.py
@@ -14,6 +14,7 @@
 GROUP = 4
 VMEM = pl.BlockSpec(memory_space=pltpu.VMEM)
 HBM = pl.BlockSpec(memory_space=pltpu.HBM)
+SMEM = pl.BlockSpec(memory_space=pltpu.SMEM)
 
 
 def in_hbm(array):
@@ -43,45 +44,40 @@
     return 2 * -(-columns // 1024) * 8
 
 
-def shard_kernel(
-    depth,
-    rank,
-    factor_ref,
-    factor_out_ref,
-    demand_ref,
-    lengths_ref,
-    holder_ref,
-    slots_ref,
-    first_ref,
-    second_ref,
-    bounds_ref,
-    demand,
-    lengths,
-    holder,
-    slots,
-    sems,
-):
-    group, place = lax.axis_index("groups"), lax.axis_index("batch")
+def shard_kernel(depth, factor_ref, factor_out_ref, first_ref, second_ref, sems):
+    group = lax.axis_index("groups")
     cut = first_ref.shape[1]
     here = pl.multiple_of(group * depth, 128)
     after = pl.multiple_of(group * depth + cut, 128)
-    small = [
-        pltpu.make_async_copy(demand_ref, demand, sems.at[0]),
-        pltpu.make_async_copy(lengths_ref, lengths, sems.at[1]),
-        pltpu.make_async_copy(holder_ref, holder, sems.at[2]),
-        pltpu.make_async_copy(slots_ref.at[pl.ds(place, 1)], slots, sems.at[3]),
-    ]
-    large = [
-        pltpu.make_async_copy(factor_ref.at[:, pl.ds(here, cut)], first_ref, sems.at[4]),
+    copies = (
+        pltpu.make_async_copy(factor_ref.at[:, pl.ds(here, cut)], first_ref, sems.at[0]),
         pltpu.make_async_copy(
-            factor_ref.at[:, pl.ds(after, depth - cut)], second_ref.at[:, : depth - cut], sems.at[5]
+            factor_ref.at[:, pl.ds(after, depth - cut)], second_ref.at[:, : depth - cut], sems.at[1]
         ),
-        pltpu.make_async_copy(factor_out_ref, second_ref.at[:, depth - cut :], sems.at[6]),
-    ]
-    for copy in small + large:
+        pltpu.make_async_copy(factor_out_ref, second_ref.at[:, depth - cut :], sems.at[2]),
+    )
+    for copy in copies:
         copy.start()
-    for copy in small:
+    for copy in copies:
         copy.wait()
+
+
+def shard_call(factor, factor_out, depth):
+    rank, width = factor_out.shape
+    out = jax.ShapeDtypeStruct((rank, (depth + width) // 2), factor.dtype)
+    return pl.pallas_call(
+        functools.partial(shard_kernel, depth),
+        out_shape=(out, out),
+        in_specs=[HBM] * 2,
+        out_specs=(VMEM,) * 2,
+        scratch_shapes=[pltpu.SemaphoreType.DMA((3,))],
+        compiler_params=params(),
+        cost_estimate=LONG,
+    )(in_hbm(factor), in_hbm(factor_out))
+
+
+def row_ends(demand, lengths, holder, slots, rank):
+    place = lax.axis_index("batch")
     count = slots.shape[2]
     items = demand.shape[1]
     column = lax.broadcasted_iota(I32, (1, count * rank), 1)
@@ -99,7 +95,7 @@
             spans.append((holder[demand[0, item]], start, end))
             start = end
         for chunk in range(count):
-            slot = slots[0, 0, chunk]
+            slot = slots[place, 0, chunk]
             begin = end = zero
             for owner, first, last in spans:
                 begin = jnp.where(owner == slot, first, begin)
@@ -110,7 +106,7 @@
 
         def chunk_ends(chunk, carry):
             low, high = carry
-            slot = slots[0, 0, chunk]
+            slot = slots[place, 0, chunk]
 
             def item_ends(item, state):
                 start, begin, end = state
@@ -123,70 +119,45 @@
             return jnp.where(mask, begin, low), jnp.where(mask, end, high)
 
         low, high = lax.fori_loop(0, count, chunk_ends, (low, high))
-    bounds_ref[0:1, :] = low
-    bounds_ref[1:2, :] = high
-    bounds_ref[2:8, :] = jnp.zeros((6, count * rank), I32)
-    for copy in large:
-        copy.wait()
-
-
-def shard_call(factor, factor_out, demand, lengths, holder_slot, slots, depth):
-    rank, width = factor_out.shape
-    cut = (depth + width) // 2
-    count = slots.shape[2]
-    return pl.pallas_call(
-        functools.partial(shard_kernel, depth, rank),
-        out_shape=(
-            jax.ShapeDtypeStruct((rank, cut), factor.dtype),
-            jax.ShapeDtypeStruct((rank, cut), factor.dtype),
-            jax.ShapeDtypeStruct((8, count * rank), I32),
-        ),
-        in_specs=[HBM] * 6,
-        out_specs=(VMEM,) * 3,
-        scratch_shapes=[
-            pltpu.SMEM(demand.shape, I32),
-            pltpu.SMEM(lengths.shape, I32),
-            pltpu.SMEM(holder_slot.shape, I32),
-            pltpu.SMEM((1, 1, count), I32),
-            pltpu.SemaphoreType.DMA((7,)),
-        ],
-        compiler_params=params(),
-        cost_estimate=LONG,
-    )(*map(in_hbm, (factor, factor_out, demand, lengths, holder_slot, slots)))
-
-
-def rows_kernel(depth, hidden_ref, bounds_ref, to_other_ref, bounds_out_ref):
+    return low, high
+
+
+def rows_kernel(depth, rank, hidden_ref, demand, lengths, holder, slots, to_other_ref, bounds_ref):
     rows = hidden_ref.shape[0]
     there = pl.multiple_of((1 - lax.axis_index("groups")) * depth, 128)
     for i in range(depth // 128):
         to_other_ref[i * rows : (i + 1) * rows, :] = hidden_ref[:, pl.ds(there + i * 128, 128)]
     columns = bounds_ref.shape[1]
+    low, high = row_ends(demand, lengths, holder, slots, rank)
     extra = extra_rows(columns)
     line = lax.broadcasted_iota(I32, (extra, 128), 0)
     ends = jnp.zeros((extra, 128), I32)
     for i in range(columns // 128):
         span = slice(i * 128, (i + 1) * 128)
-        ends = jnp.where(line == i, bounds_ref[0:1, span], ends)
-        ends = jnp.where(line == extra // 2 + i, bounds_ref[1:2, span], ends)
+        ends = jnp.where(line == i, low[:, span], ends)
+        ends = jnp.where(line == extra // 2 + i, high[:, span], ends)
     to_other_ref[-extra:, :] = ends.astype(F32).astype(BF16)
-    bounds_out_ref[...] = bounds_ref[...]
-
-
-def rows_call(hidden, bounds):
+    bounds_ref[0:1, :] = low
+    bounds_ref[1:2, :] = high
+    bounds_ref[2:8, :] = jnp.zeros((6, columns), I32)
+
+
+def rows_call(hidden, demand, lengths, holder_slot, slots, rank):
     rows, features = hidden.shape
     depth = features // 2
-    tall = depth // 128 * rows + extra_rows(bounds.shape[1])
-    return pl.pallas_call(
-        functools.partial(rows_kernel, depth),
+    columns = slots.shape[2] * rank
+    tall = depth // 128 * rows + extra_rows(columns)
+    return pl.pallas_call(
+        functools.partial(rows_kernel, depth, rank),
         out_shape=(
             jax.ShapeDtypeStruct((tall, 128), hidden.dtype),
-            jax.ShapeDtypeStruct(bounds.shape, I32),
+            jax.ShapeDtypeStruct((8, columns), I32),
         ),
-        in_specs=[VMEM] * 2,
+        in_specs=[VMEM] + [SMEM] * 4,
         out_specs=(VMEM,) * 2,
         compiler_params=params(),
         cost_estimate=LONG,
-    )(hidden, bounds)
+    )(hidden, demand, lengths, holder_slot, slots)
 
 
 def mark_kernel(bounds_ref, out_ref):
@@ -364,10 +335,11 @@
         [[order[(order.index(me) - distance) % owners] for distance in distances]]
         for me in range(owners)
     ]
-    first, second, bounds = shard_call(
-        factor_in[0].T, factor_out[0], demand, lengths, holder_slot, jnp.asarray(table, I32), depth
+    first, second = shard_call(factor_in[0].T, factor_out[0], depth)
+    first, rows_here = lax.optimization_barrier((first, hidden))
+    to_other, bounds = rows_call(
+        rows_here, demand, lengths, holder_slot, jnp.asarray(table, I32), rank
     )
-    to_other, bounds = rows_call(hidden, bounds)
     bounds, first_later = lax.optimization_barrier((mark(bounds), first))
 
     firsts, seconds = [first], [second]

time: 37.9 us -> 38.2 us (level)
  Pallas kernels: 6.77 us -> 7.41 us
    ppermute x3, starting transfers between devices: 6.79 us -> 1.83 us  [per_device(): d = lax.ppermute(behind[1], 'batch', backward)]
    ppermute x3, starting transfers between devices: 0.44 us -> 5.38 us  [per_device(): a = lax.ppermute(ahead[0], 'batch', forward)]
    ppermute x3, waiting for transfers between devices: 1.94 us -> 3.61 us  [per_device(): d = lax.ppermute(behind[1], 'batch', backward)]
    ppermute x3, waiting for transfers between devices: 2.91 us -> 1.61 us  [per_device(): c = lax.ppermute(behind[0], 'batch', backward)]
    pallas_call x2, Pallas kernels: 1.46 us -> 2.1 us  [the longest x1 1.16 us: shard_call(): pl.pallas_call(functools.partial(shard_kernel, depth), out_shape=(out, ou...]
    ppermute x1, waiting for transfers between devices: 0.77 us -> 0.2 us  [per_device(): lax.ppermute(theirs, ('groups', 'tensor'), [(0, 3), (1, 2), (2, 1), (3, 0)])]
    ppermute x1, starting transfers between devices: 1.3 us -> 0.74 us  [per_device(): two = lax.ppermute(theirs, 'groups', swap)]
  transfers between devices with their start and end apart: 20 -> 20, of which waited for: 7 -> 8; matrix products, arithmetic and copies ran while one was open for 0% -> 0% of each run, Pallas kernels for 12% -> 13%
where the time goes in v25:
time: 38.2 us; the launch traced here: 38 us
  starting transfers between devices  19.8 us (52%)
  waiting for transfers between devices  10.7 us (28%)
  Pallas kernels  7.41 us (19%)
    ppermute x3, starting transfers between devices, per_device(): a = lax.ppermute(ahead[0], 'batch', forward)  5.38 us
    ppermute x3, starting transfers between devices, per_device(): c = lax.ppermute(behind[0], 'batch', backward)  4.78 us
    ppermute x3, waiting for transfers between devices, per_device(): d = lax.ppermute(behind[1], 'batch', backward)  3.61 us
    ppermute x1, waiting for transfers between devices, per_device(): other = lax.ppermute(to_other, 'groups', swap)  2.98 us
    pallas_call x1, Pallas kernels, base_call(): pl.pallas_call(base_kernel, out_shape=(out, out), in_specs=[VMEM] * 2, ou...  2.35 us
    ppermute x1, starting transfers between devices, per_device(): other = lax.ppermute(to_other, 'groups', swap)  1.97 us
    pallas_call x3, Pallas kernels, rank_call(): pl.pallas_call(functools.partial(rank_kernel, sides, groups, depth, last)...  1.83 us
    ppermute x3, starting transfers between devices, per_device(): d = lax.ppermute(behind[1], 'batch', backward)  1.83 us
  transfers between devices with their start and end apart: 20, of which 8 were waited for; matrix products, arithmetic and copies ran while one was open for 0% of the time, Pallas kernels for 13%

profile of v25, /device:TPU:0, one launch (start us, length us, event | category | flops | bytes accessed | tf_op | source)
XLA Modules:
  0.0 38.0 jit_solution(9192163440607799881)
XLA Ops:
  0.0 1.2 %shard_map.82 = (bf16[64,1280]{1,0:T(8,128)(2,1)S(1)}, bf16[64,1280]{1,0:T(8,128)(2,1)S(1)}) custom-call(bf16[64,4096]{1,0:T(8,128)(2,1)} %bitcast.6, bf16[64,512]{1,0:T(8,128)(2,1)} %bitcast.7), custom_call_target="tpu_custom_call" | custom-call | flops 8589934592 | bytes 16777216 | tf_op jit(solution)/shard_map/pallas_call | solution.py:68
  1.2 3.0 %collective-permute-start.2 = (bf16[64,1280]{1,0:T(8,128)(2,1)S(1)}, bf16[64,1280]{1,0:T(8,128)(2,1)S(1)}, u32[]{:S(2)}, u32[]{:S(2)}) collective-permute-start(bf16[64,1280]{1,0:T(8,128)(2,1)S(1)} %get-tuple-element.32.refs_3_), channel_id=1, source_target_pairs={{0,2},{2,6},{6,10},{10,14},{14,12},{12,8},{8,4},{4,0},{1,3},{3,7},... | collective-permute-start | bytes 491528 | tf_op jit(solution)/shard_map/ppermute | solution.py:348
  4.2 0.2 collective-permute-start.7
  4.3 0.0 copy-done.1
  4.4 0.9 %shard_map.83 = (bf16[4112,128]{1,0:T(8,128)(2,1)S(1)}, s32[8,512]{1,0:T(8,128)S(1)}) custom-call(bf16[256,4096]{1,0:T(8,128)(2,1)S(1)} %copy-done, s32[1,4]{1,0:T(1,128)S(1)} %copy-done.1, s32[1,4]{1,0:T(1,128)S(1)} %copy-done.2, s32[8]{0:T(128)S(1)} %copy-done.3, s32[8,1,8]{2,1,0:T(1,128)S(1)} %copy-done.4), custom_call_target="tpu_custom_call" | custom-call | flops 8589934592 | bytes 16777216 | tf_op jit(solution)/shard_map/pallas_call | solution.py:150
  5.3 2.0 %collective-permute-start.14 = (bf16[4112,128]{1,0:T(8,128)(2,1)S(1)}, bf16[4112,128]{1,0:T(8,128)(2,1)S(1)}, u32[]{:S(2)}, u32[]{:S(2)}) collective-permute-start(bf16[4112,128]{1,0:T(8,128)(2,1)S(1)} %get-tuple-element.34), channel_id=1, source_target_pairs={{0,16},{16,0},{1,17},{17,1},{2,18},{18,2},{3,19},{19,3},{4,20},{20... | collective-permute-start | bytes 3158024 | tf_op jit(solution)/shard_map/ppermute | solution.py:359
  7.3 1.6 %collective-permute-start = (bf16[64,1280]{1,0:T(8,128)(2,1)S(1)}, bf16[64,1280]{1,0:T(8,128)(2,1)S(1)}, u32[]{:S(2)}, u32[]{:S(2)}) collective-permute-start(bf16[64,1280]{1,0:T(8,128)(2,1)S(1)} %get-tuple-element.32.refs_3_), channel_id=1, source_target_pairs={{2,0},{6,2},{10,6},{14,10},{12,14},{8,12},{4,8},{0,4},{3,1},{7,3},... | collective-permute-start | bytes 491528 | tf_op jit(solution)/shard_map/ppermute | solution.py:351
  8.9 0.4 %collective-permute-start.9 = (bf16[64,1280]{1,0:T(8,128)(2,1)S(1)}, bf16[64,1280]{1,0:T(8,128)(2,1)S(1)}, u32[]{:S(2)}, u32[]{:S(2)}) collective-permute-start(bf16[64,1280]{1,0:T(8,128)(2,1)S(1)} %get-tuple-element.33.refs_7_.refs_0_), channel_id=1, source_target_pairs={{0,2},{2,6},{6,10},{10,14},{14,12},{12,8},{8,4},{4,0},{1,3},{3,7},... | collective-permute-start | bytes 491528 | tf_op jit(solution)/shard_map/ppermute | solution.py:350
  9.3 1.5 %collective-permute-done.7.refs_9_.refs_2_ = bf16[64,1280]{1,0:T(8,128)(2,1)S(1)} collective-permute-done((bf16[64,1280]{1,0:T(8,128)(2,1)S(1)}, bf16[64,1280]{1,0:T(8,128)(2,1)S(1)}, u32[]{:S(2)}, u32[]{:S(2)}) %collective-permute-start.7) | collective-permute-done | bytes 163872 | tf_op jit(solution)/shard_map/ppermute | solution.py:349
  10.8 0.1 collective-permute-start.8
  10.9 0.0 collective-permute-done.2.refs_4_
  10.9 1.9 %collective-permute-start.3 = (bf16[64,1280]{1,0:T(8,128)(2,1)S(1)}, bf16[64,1280]{1,0:T(8,128)(2,1)S(1)}, u32[]{:S(2)}, u32[]{:S(2)}) collective-permute-start(bf16[64,1280]{1,0:T(8,128)(2,1)S(1)} %collective-permute-done.2.refs_4_), channel_id=1, source_target_pairs={{0,2},{2,6},{6,10},{10,14},{14,12},{12,8},{8,4},{4,0},{1,3},{3,7},... | collective-permute-start | bytes 491528 | tf_op jit(solution)/shard_map/ppermute | solution.py:348
  12.8 1.6 %collective-permute-done.refs_5_ = bf16[64,1280]{1,0:T(8,128)(2,1)S(1)} collective-permute-done((bf16[64,1280]{1,0:T(8,128)(2,1)S(1)}, bf16[64,1280]{1,0:T(8,128)(2,1)S(1)}, u32[]{:S(2)}, u32[]{:S(2)}) %collective-permute-start) | collective-permute-done | bytes 163872 | tf_op jit(solution)/shard_map/ppermute | solution.py:351
  14.4 1.6 %collective-permute-start.1 = (bf16[64,1280]{1,0:T(8,128)(2,1)S(1)}, bf16[64,1280]{1,0:T(8,128)(2,1)S(1)}, u32[]{:S(2)}, u32[]{:S(2)}) collective-permute-start(bf16[64,1280]{1,0:T(8,128)(2,1)S(1)} %collective-permute-done.refs_5_), channel_id=1, source_target_pairs={{2,0},{6,2},{10,6},{14,10},{12,14},{8,12},{4,8},{0,4},{3,1},{7,3},... | collective-permute-start | bytes 491528 | tf_op jit(solution)/shard_map/ppermute | solution.py:351
  16.0 0.0 collective-permute-done.9.refs_8_.refs_1_
  16.0 0.5 %collective-permute-start.10 = (bf16[64,1280]{1,0:T(8,128)(2,1)S(1)}, bf16[64,1280]{1,0:T(8,128)(2,1)S(1)}, u32[]{:S(2)}, u32[]{:S(2)}) collective-permute-start(bf16[64,1280]{1,0:T(8,128)(2,1)S(1)} %collective-permute-done.9.refs_8_.refs_1_), channel_id=1, source_target_pairs={{0,2},{2,6},{6,10},{10,14},{14,12},{12,8},{8,4},{4,0},{1,3},{3,7},... | collective-permute-start | bytes 491528 | tf_op jit(solution)/shard_map/ppermute | solution.py:350
  16.5 1.5 %collective-permute-done.8.refs_6_.refs_4_ = bf16[64,1280]{1,0:T(8,128)(2,1)S(1)} collective-permute-done((bf16[64,1280]{1,0:T(8,128)(2,1)S(1)}, bf16[64,1280]{1,0:T(8,128)(2,1)S(1)}, u32[]{:S(2)}, u32[]{:S(2)}) %collective-permute-start.8) | collective-permute-done | bytes 163872 | tf_op jit(solution)/shard_map/ppermute | solution.py:349
  17.9 1.6 %collective-permute-start.12 = (bf16[64,1280]{1,0:T(8,128)(2,1)S(1)}, bf16[64,1280]{1,0:T(8,128)(2,1)S(1)}, u32[]{:S(2)}, u32[]{:S(2)}) collective-permute-start(bf16[64,1280]{1,0:T(8,128)(2,1)S(1)} %collective-permute-done.8.refs_6_.refs_4_), channel_id=1, source_target_pairs={{2,0},{6,2},{10,6},{14,10},{12,14},{8,12},{4,8},{0,4},{3,1},{7,3},... | collective-permute-start | bytes 491528 | tf_op jit(solution)/shard_map/ppermute | solution.py:349
  19.5 0.0 collective-permute-done.3.refs_6_
  19.5 0.5 %collective-permute-start.4 = (bf16[64,1280]{1,0:T(8,128)(2,1)S(1)}, bf16[64,1280]{1,0:T(8,128)(2,1)S(1)}, u32[]{:S(2)}, u32[]{:S(2)}) collective-permute-start(bf16[64,1280]{1,0:T(8,128)(2,1)S(1)} %collective-permute-done.3.refs_6_), channel_id=1, source_target_pairs={{0,2},{2,6},{6,10},{10,14},{14,12},{12,8},{8,4},{4,0},{1,3},{3,7},... | collective-permute-start | bytes 491528 | tf_op jit(solution)/shard_map/ppermute | solution.py:348
  20.0 2.3 %shard_map.85 = (f32[256,512]{1,0:T(8,128)S(1)}, f32[256,512]{1,0:T(8,128)S(1)}) custom-call(bf16[256,4096]{1,0:T(8,128)(2,1)S(1)} %copy-done, bf16[4096,1024]{1,0:T(8,128)(2,1)S(1)} %bitcast.5), custom_call_target="tpu_custom_call" | custom-call | bytes 4194304 | tf_op jit(solution)/shard_map/pallas_call | solution.py:190
  22.3 0.0 collective-permute-done.1.refs_2_
  22.3 1.6 %collective-permute-start.5 = (bf16[64,1280]{1,0:T(8,128)(2,1)S(1)}, bf16[64,1280]{1,0:T(8,128)(2,1)S(1)}, u32[]{:S(2)}, u32[]{:S(2)}) collective-permute-start(bf16[64,1280]{1,0:T(8,128)(2,1)S(1)} %collective-permute-done.1.refs_2_), channel_id=1, source_target_pairs={{2,0},{6,2},{10,6},{14,10},{12,14},{8,12},{4,8},{0,4},{3,1},{7,3},... | collective-permute-start | bytes 491528 | tf_op jit(solution)/shard_map/ppermute | solution.py:351
  24.0 0.0 collective-permute-done.10.refs_10_.refs_3_
  24.0 0.5 %collective-permute-start.11 = (bf16[64,1280]{1,0:T(8,128)(2,1)S(1)}, bf16[64,1280]{1,0:T(8,128)(2,1)S(1)}, u32[]{:S(2)}, u32[]{:S(2)}) collective-permute-start(bf16[64,1280]{1,0:T(8,128)(2,1)S(1)} %collective-permute-done.10.refs_10_.refs_3_), channel_id=1, source_target_pairs={{0,2},{2,6},{6,10},{10,14},{14,12},{12,8},{8,4},{4,0},{1,3},{3,7},... | collective-permute-start | bytes 491528 | tf_op jit(solution)/shard_map/ppermute | solution.py:350
  24.4 0.7 %collective-permute-done.12.refs_8_.refs_6_ = bf16[64,1280]{1,0:T(8,128)(2,1)S(1)} collective-permute-done((bf16[64,1280]{1,0:T(8,128)(2,1)S(1)}, bf16[64,1280]{1,0:T(8,128)(2,1)S(1)}, u32[]{:S(2)}, u32[]{:S(2)}) %collective-permute-start.12) | collective-permute-done | bytes 163872 | tf_op jit(solution)/shard_map/ppermute | solution.py:349
  25.1 1.5 %collective-permute-start.13 = (bf16[64,1280]{1,0:T(8,128)(2,1)S(1)}, bf16[64,1280]{1,0:T(8,128)(2,1)S(1)}, u32[]{:S(2)}, u32[]{:S(2)}) collective-permute-start(bf16[64,1280]{1,0:T(8,128)(2,1)S(1)} %collective-permute-done.12.refs_8_.refs_6_), channel_id=1, source_target_pairs={{2,0},{6,2},{10,6},{14,10},{12,14},{8,12},{4,8},{0,4},{3,1},{7,3},... | collective-permute-start | bytes 491528 | tf_op jit(solution)/shard_map/ppermute | solution.py:356
  26.6 0.0 collective-permute-done.4.refs_3_
  26.6 0.5 %collective-permute-start.6 = (bf16[64,1280]{1,0:T(8,128)(2,1)S(1)}, bf16[64,1280]{1,0:T(8,128)(2,1)S(1)}, u32[]{:S(2)}, u32[]{:S(2)}) collective-permute-start(bf16[64,1280]{1,0:T(8,128)(2,1)S(1)} %collective-permute-done.4.refs_3_), channel_id=1, source_target_pairs={{0,2},{2,6},{6,10},{10,14},{14,12},{12,8},{8,4},{4,0},{1,3},{3,7},... | collective-permute-start | bytes 491528 | tf_op jit(solution)/shard_map/ppermute | solution.py:355
  27.1 3.0 %collective-permute-done.14.refs_1_.refs_0_ = bf16[4112,128]{1,0:T(8,128)(2,1)S(1)} collective-permute-done((bf16[4112,128]{1,0:T(8,128)(2,1)S(1)}, bf16[4112,128]{1,0:T(8,128)(2,1)S(1)}, u32[]{:S(2)}, u32[]{:S(2)}) %collective-permute-start.14) | collective-permute-done | bytes 1052704 | tf_op jit(solution)/shard_map/ppermute | solution.py:359
  30.1 0.7 %shard_map.86 = (f32[256,128]{1,0:T(8,128)S(1)}, f32[256,128]{1,0:T(8,128)S(1)}) custom-call(bf16[256,4096]{1,0:T(8,128)(2,1)S(1)} %copy-done, bf16[4112,128]{1,0:T(8,128)(2,1)S(1)} %collective-permute-done.14.refs_1_.refs_0_, s32[8,512]{1,0:T(8,128)S(1)} %shard_map.84.refs_2_.refs_1_.bounds_ref, bf16[64,1280]{1,0:T(8,128)(2,1)S(1)} %get-tuple-element.32.refs_3_, ...), custom_call_target="tpu_custom_call" | custom-call | flops 8589934592 | bytes 16777216 | tf_op jit(solution)/shard_map/pallas_call | solution.py:284
  30.8 0.1 collective-permute-start.19
  30.9 0.0 collective-permute-done.5.refs_4_
  30.9 0.0 collective-permute-done.11.refs_7_.refs_5_
  30.9 0.0 collective-permute-done.13.refs_9_.refs_7_
  31.0 1.0 %collective-permute-done.6.refs_5_ = bf16[64,1280]{1,0:T(8,128)(2,1)S(1)} collective-permute-done((bf16[64,1280]{1,0:T(8,128)(2,1)S(1)}, bf16[64,1280]{1,0:T(8,128)(2,1)S(1)}, u32[]{:S(2)}, u32[]{:S(2)}) %collective-permute-start.6) | collective-permute-done | bytes 163872 | tf_op jit(solution)/shard_map/ppermute | solution.py:355
  31.9 0.5 %shard_map.88 = bf16[128,128]{1,0:T(8,128)(2,1)S(1)} custom-call(bf16[4112,128]{1,0:T(8,128)(2,1)S(1)} %collective-permute-done.14.refs_1_.refs_0_, s32[8,512]{1,0:T(8,128)S(1)} %shard_map.84.refs_2_.refs_1_.bounds_ref, bf16[64,1280]{1,0:T(8,128)(2,1)S(1)} %collective-permute-done.1.refs_2_, bf16[64,1280]{1,0:T(8,128)(2,1)S(1)} %collective-permute-done.4.refs_3_, ...), custom_call_target="tpu_custom_call" | custom-call | flops 8589934592 | bytes 16777216 | tf_op jit(solution)/shard_map/pallas_call | solution.py:284
  32.5 0.7 %collective-permute-start.17 = (bf16[128,128]{1,0:T(8,128)(2,1)S(1)}, bf16[128,128]{1,0:T(8,128)(2,1)S(1)}, u32[]{:S(2)}, u32[]{:S(2)}) collective-permute-start(bf16[128,128]{1,0:T(8,128)(2,1)S(1)} %shard_map.88), channel_id=1, source_target_pairs={{0,16},{16,0},{1,17},{17,1},{2,18},{18,2},{3,19},{19,3},{4,20},{20... | collective-permute-start | bytes 98312 | tf_op jit(solution)/shard_map/ppermute | solution.py:378
  33.2 0.2 collective-permute-start.18
  33.4 0.5 %shard_map.87 = (f32[64,128]{1,0:T(8,128)S(1)}, f32[64,128]{1,0:T(8,128)S(1)}) custom-call(bf16[256,4096]{1,0:T(8,128)(2,1)S(1)} %copy-done, s32[8,512]{1,0:T(8,128)S(1)} %shard_map.84.refs_2_.refs_1_.bounds_ref, bf16[64,1280]{1,0:T(8,128)(2,1)S(1)} %collective-permute-done.1.refs_2_, bf16[64,1280]{1,0:T(8,128)(2,1)S(1)} %collective-permute-done.4.refs_3_, ...), custom_call_target="tpu_custom_call" | custom-call | bytes 4194304 | tf_op jit(solution)/shard_map/pallas_call | solution.py:284
  34.0 1.3 %collective-permute-start.15 = (f32[64,128]{1,0:T(8,128)S(1)}, f32[64,128]{1,0:T(8,128)S(1)}, u32[]{:S(2)}, u32[]{:S(2)}) collective-permute-start(f32[64,128]{1,0:T(8,128)S(1)} %get-tuple-element.36.top), channel_id=1, source_target_pairs={{0,1},{1,0},{2,3},{3,2},{4,5},{5,4},{6,7},{7,6},{8,9},{9,8},{10,11... | collective-permute-start | bytes 98312 | tf_op jit(solution)/shard_map/ppermute | solution.py:380
  35.3 0.1 collective-permute-start.16
  35.4 1.3 %collective-permute-done.17.two = bf16[128,128]{1,0:T(8,128)(2,1)S(1)} collective-permute-done((bf16[128,128]{1,0:T(8,128)(2,1)S(1)}, bf16[128,128]{1,0:T(8,128)(2,1)S(1)}, u32[]{:S(2)}, u32[]{:S(2)}) %collective-permute-start.17) | collective-permute-done | bytes 32800 | tf_op jit(solution)/shard_map/ppermute | solution.py:378
  36.7 0.2 collective-permute-done.18.three
  36.9 0.0 collective-permute-done.15.one_top
  36.9 0.0 collective-permute-done.16.one_low
  36.9 0.0 collective-permute-done.19.far_ref
  36.9 1.1 %shard_map.89 = bf16[256,512]{1,0:T(8,128)(2,1)} custom-call(s32[8,512]{1,0:T(8,128)S(1)} %shard_map.84.refs_2_.refs_1_.bounds_ref, f32[64,128]{1,0:T(8,128)S(1)} %get-tuple-element.36.top, f32[64,128]{1,0:T(8,128)S(1)} %get-tuple-element.37.low, f32[64,128]{1,0:T(8,128)S(1)} %collective-permute-done.15.one_top, ...), custom_call_target="tpu_custom_call" | custom-call | tf_op jit(solution)/shard_map/pallas_call | solution.py:383
  (15 shorter events, 0.0 us)
Async XLA Ops:
  0.0 4.3 %copy-start = (bf16[256,4096]{1,0:T(8,128)(2,1)S(1)}, bf16[256,4096]{1,0:T(8,128)(2,1)}, u32[]{:S(2)}) copy-start(bf16[256,4096]{1,0:T(8,128)(2,1)} %refs_0_.1) | copy-start | bytes 6291460
  0.0 4.3 %copy-start.1 = (s32[1,4]{1,0:T(1,128)S(1)}, s32[1,4]{1,0:T(1,128)}, u32[]{:S(2)}) copy-start(s32[1,4]{1,0:T(1,128)} %demand.1) | copy-start | bytes 52
  0.0 4.3 %copy-start.2 = (s32[1,4]{1,0:T(1,128)S(1)}, s32[1,4]{1,0:T(1,128)}, u32[]{:S(2)}) copy-start(s32[1,4]{1,0:T(1,128)} %lengths.1) | copy-start | bytes 52
  0.0 4.3 %copy-start.3 = (s32[8]{0:T(128)S(1)}, s32[8]{0:T(128)}, u32[]{:S(2)}) copy-start(s32[8]{0:T(128)} %holder.1) | copy-start | bytes 100
  0.0 4.3 %copy-start.4 = (s32[8,1,8]{2,1,0:T(1,128)S(1)}, s32[8,1,8]{2,1,0:T(1,128)}, u32[]{:S(2)}) copy-start(s32[8,1,8]{2,1,0:T(1,128)} %constant.2.clone.slots) | copy-start | bytes 772
  1.2 9.7 %collective-permute-start.2 = (bf16[64,1280]{1,0:T(8,128)(2,1)S(1)}, bf16[64,1280]{1,0:T(8,128)(2,1)S(1)}, u32[]{:S(2)}, u32[]{:S(2)}) collective-permute-start(bf16[64,1280]{1,0:T(8,128)(2,1)S(1)} %get-tuple-element.32.refs_3_), channel_id=1, source_target_pairs={{0,2},{2,6},{6,10},{10,14},{14,12},{12,8},{8,4},{4,0},{1,3},{3,7},... | collective-permute-start | bytes 491528 | tf_op jit(solution)/shard_map/ppermute | solution.py:348
  4.2 6.6 %collective-permute-start.7 = (bf16[64,1280]{1,0:T(8,128)(2,1)S(1)}, bf16[64,1280]{1,0:T(8,128)(2,1)S(1)}, u32[]{:S(2)}, u32[]{:S(2)}) collective-permute-start(bf16[64,1280]{1,0:T(8,128)(2,1)S(1)} %get-tuple-element.33.refs_7_.refs_0_), channel_id=1, source_target_pairs={{2,0},{6,2},{10,6},{14,10},{12,14},{8,12},{4,8},{0,4},{3,1},{7,3},... | collective-permute-start | bytes 491528 | tf_op jit(solution)/shard_map/ppermute | solution.py:349
  5.3 24.8 %collective-permute-start.14 = (bf16[4112,128]{1,0:T(8,128)(2,1)S(1)}, bf16[4112,128]{1,0:T(8,128)(2,1)S(1)}, u32[]{:S(2)}, u32[]{:S(2)}) collective-permute-start(bf16[4112,128]{1,0:T(8,128)(2,1)S(1)} %get-tuple-element.34), channel_id=1, source_target_pairs={{0,16},{16,0},{1,17},{17,1},{2,18},{18,2},{3,19},{19,3},{4,20},{20... | collective-permute-start | bytes 3158024 | tf_op jit(solution)/shard_map/ppermute | solution.py:359
  7.3 12.7 %slice-start = ((s8[8388608]{0:T(1024)(128)(4,1)}), s8[4194304]{0:T(1024)(128)(4,1)S(1)}, s32[]{:S(2)}) async-start(s8[8388608]{0:T(1024)(128)(4,1)} %bitcast.4), calls=%async_computation | async-start | bytes 8388608
  7.3 12.7 %slice-start.1 = ((s8[8388608]{0:T(1024)(128)(4,1)}), s8[4194304]{0:T(1024)(128)(4,1)S(1)}, s32[]{:S(2)}) async-start(s8[8388608]{0:T(1024)(128)(4,1)} %bitcast.4), calls=%async_computation.1 | async-start | bytes 8388608
  7.3 7.1 %collective-permute-start = (bf16[64,1280]{1,0:T(8,128)(2,1)S(1)}, bf16[64,1280]{1,0:T(8,128)(2,1)S(1)}, u32[]{:S(2)}, u32[]{:S(2)}) collective-permute-start(bf16[64,1280]{1,0:T(8,128)(2,1)S(1)} %get-tuple-element.32.refs_3_), channel_id=1, source_target_pairs={{2,0},{6,2},{10,6},{14,10},{12,14},{8,12},{4,8},{0,4},{3,1},{7,3},... | collective-permute-start | bytes 491528 | tf_op jit(solution)/shard_map/ppermute | solution.py:351
  8.9 7.1 %collective-permute-start.9 = (bf16[64,1280]{1,0:T(8,128)(2,1)S(1)}, bf16[64,1280]{1,0:T(8,128)(2,1)S(1)}, u32[]{:S(2)}, u32[]{:S(2)}) collective-permute-start(bf16[64,1280]{1,0:T(8,128)(2,1)S(1)} %get-tuple-element.33.refs_7_.refs_0_), channel_id=1, source_target_pairs={{0,2},{2,6},{6,10},{10,14},{14,12},{12,8},{8,4},{4,0},{1,3},{3,7},... | collective-permute-start | bytes 491528 | tf_op jit(solution)/shard_map/ppermute | solution.py:350
  10.8 7.1 %collective-permute-start.8 = (bf16[64,1280]{1,0:T(8,128)(2,1)S(1)}, bf16[64,1280]{1,0:T(8,128)(2,1)S(1)}, u32[]{:S(2)}, u32[]{:S(2)}) collective-permute-start(bf16[64,1280]{1,0:T(8,128)(2,1)S(1)} %collective-permute-done.7.refs_9_.refs_2_), channel_id=1, source_target_pairs={{2,0},{6,2},{10,6},{14,10},{12,14},{8,12},{4,8},{0,4},{3,1},{7,3},... | collective-permute-start | bytes 491528 | tf_op jit(solution)/shard_map/ppermute | solution.py:349
  10.9 8.6 %collective-permute-start.3 = (bf16[64,1280]{1,0:T(8,128)(2,1)S(1)}, bf16[64,1280]{1,0:T(8,128)(2,1)S(1)}, u32[]{:S(2)}, u32[]{:S(2)}) collective-permute-start(bf16[64,1280]{1,0:T(8,128)(2,1)S(1)} %collective-permute-done.2.refs_4_), channel_id=1, source_target_pairs={{0,2},{2,6},{6,10},{10,14},{14,12},{12,8},{8,4},{4,0},{1,3},{3,7},... | collective-permute-start | bytes 491528 | tf_op jit(solution)/shard_map/ppermute | solution.py:348
  14.4 7.9 %collective-permute-start.1 = (bf16[64,1280]{1,0:T(8,128)(2,1)S(1)}, bf16[64,1280]{1,0:T(8,128)(2,1)S(1)}, u32[]{:S(2)}, u32[]{:S(2)}) collective-permute-start(bf16[64,1280]{1,0:T(8,128)(2,1)S(1)} %collective-permute-done.refs_5_), channel_id=1, source_target_pairs={{2,0},{6,2},{10,6},{14,10},{12,14},{8,12},{4,8},{0,4},{3,1},{7,3},... | collective-permute-start | bytes 491528 | tf_op jit(solution)/shard_map/ppermute | solution.py:351
  16.0 8.0 %collective-permute-start.10 = (bf16[64,1280]{1,0:T(8,128)(2,1)S(1)}, bf16[64,1280]{1,0:T(8,128)(2,1)S(1)}, u32[]{:S(2)}, u32[]{:S(2)}) collective-permute-start(bf16[64,1280]{1,0:T(8,128)(2,1)S(1)} %collective-permute-done.9.refs_8_.refs_1_), channel_id=1, source_target_pairs={{0,2},{2,6},{6,10},{10,14},{14,12},{12,8},{8,4},{4,0},{1,3},{3,7},... | collective-permute-start | bytes 491528 | tf_op jit(solution)/shard_map/ppermute | solution.py:350
  17.9 7.1 %collective-permute-start.12 = (bf16[64,1280]{1,0:T(8,128)(2,1)S(1)}, bf16[64,1280]{1,0:T(8,128)(2,1)S(1)}, u32[]{:S(2)}, u32[]{:S(2)}) collective-permute-start(bf16[64,1280]{1,0:T(8,128)(2,1)S(1)} %collective-permute-done.8.refs_6_.refs_4_), channel_id=1, source_target_pairs={{2,0},{6,2},{10,6},{14,10},{12,14},{8,12},{4,8},{0,4},{3,1},{7,3},... | collective-permute-start | bytes 491528 | tf_op jit(solution)/shard_map/ppermute | solution.py:349
  19.5 7.1 %collective-permute-start.4 = (bf16[64,1280]{1,0:T(8,128)(2,1)S(1)}, bf16[64,1280]{1,0:T(8,128)(2,1)S(1)}, u32[]{:S(2)}, u32[]{:S(2)}) collective-permute-start(bf16[64,1280]{1,0:T(8,128)(2,1)S(1)} %collective-permute-done.3.refs_6_), channel_id=1, source_target_pairs={{0,2},{2,6},{6,10},{10,14},{14,12},{12,8},{8,4},{4,0},{1,3},{3,7},... | collective-permute-start | bytes 491528 | tf_op jit(solution)/shard_map/ppermute | solution.py:348
  22.3 8.6 %collective-permute-start.5 = (bf16[64,1280]{1,0:T(8,128)(2,1)S(1)}, bf16[64,1280]{1,0:T(8,128)(2,1)S(1)}, u32[]{:S(2)}, u32[]{:S(2)}) collective-permute-start(bf16[64,1280]{1,0:T(8,128)(2,1)S(1)} %collective-permute-done.1.refs_2_), channel_id=1, source_target_pairs={{2,0},{6,2},{10,6},{14,10},{12,14},{8,12},{4,8},{0,4},{3,1},{7,3},... | collective-permute-start | bytes 491528 | tf_op jit(solution)/shard_map/ppermute | solution.py:351
  24.0 7.0 %collective-permute-start.11 = (bf16[64,1280]{1,0:T(8,128)(2,1)S(1)}, bf16[64,1280]{1,0:T(8,128)(2,1)S(1)}, u32[]{:S(2)}, u32[]{:S(2)}) collective-permute-start(bf16[64,1280]{1,0:T(8,128)(2,1)S(1)} %collective-permute-done.10.refs_10_.refs_3_), channel_id=1, source_target_pairs={{0,2},{2,6},{6,10},{10,14},{14,12},{12,8},{8,4},{4,0},{1,3},{3,7},... | collective-permute-start | bytes 491528 | tf_op jit(solution)/shard_map/ppermute | solution.py:350
  25.1 5.9 %collective-permute-start.13 = (bf16[64,1280]{1,0:T(8,128)(2,1)S(1)}, bf16[64,1280]{1,0:T(8,128)(2,1)S(1)}, u32[]{:S(2)}, u32[]{:S(2)}) collective-permute-start(bf16[64,1280]{1,0:T(8,128)(2,1)S(1)} %collective-permute-done.12.refs_8_.refs_6_), channel_id=1, source_target_pairs={{2,0},{6,2},{10,6},{14,10},{12,14},{8,12},{4,8},{0,4},{3,1},{7,3},... | collective-permute-start | bytes 491528 | tf_op jit(solution)/shard_map/ppermute | solution.py:356
  26.6 5.3 %collective-permute-start.6 = (bf16[64,1280]{1,0:T(8,128)(2,1)S(1)}, bf16[64,1280]{1,0:T(8,128)(2,1)S(1)}, u32[]{:S(2)}, u32[]{:S(2)}) collective-permute-start(bf16[64,1280]{1,0:T(8,128)(2,1)S(1)} %collective-permute-done.4.refs_3_), channel_id=1, source_target_pairs={{0,2},{2,6},{6,10},{10,14},{14,12},{12,8},{8,4},{4,0},{1,3},{3,7},... | collective-permute-start | bytes 491528 | tf_op jit(solution)/shard_map/ppermute | solution.py:355
  30.8 6.1 %collective-permute-start.19 = (f32[256,512]{1,0:T(8,128)S(1)}, f32[256,512]{1,0:T(8,128)S(1)}, u32[]{:S(2)}, u32[]{:S(2)}) collective-permute-start(f32[256,512]{1,0:T(8,128)S(1)} %get-tuple-element.42), channel_id=1, source_target_pairs={{0,1},{1,0},{2,3},{3,2},{4,5},{5,4},{6,7},{7,6},{8,9},{9,8},{10,11... | collective-permute-start | bytes 1572872 | tf_op jit(solution)/shard_map/ppermute | solution.py:372
  32.5 4.2 %collective-permute-start.17 = (bf16[128,128]{1,0:T(8,128)(2,1)S(1)}, bf16[128,128]{1,0:T(8,128)(2,1)S(1)}, u32[]{:S(2)}, u32[]{:S(2)}) collective-permute-start(bf16[128,128]{1,0:T(8,128)(2,1)S(1)} %shard_map.88), channel_id=1, source_target_pairs={{0,16},{16,0},{1,17},{17,1},{2,18},{18,2},{3,19},{19,3},{4,20},{20... | collective-permute-start | bytes 98312 | tf_op jit(solution)/shard_map/ppermute | solution.py:378
  33.2 3.7 %collective-permute-start.18 = (bf16[128,128]{1,0:T(8,128)(2,1)S(1)}, bf16[128,128]{1,0:T(8,128)(2,1)S(1)}, u32[]{:S(2)}, u32[]{:S(2)}) collective-permute-start(bf16[128,128]{1,0:T(8,128)(2,1)S(1)} %shard_map.88), channel_id=1, source_target_pairs={{0,17},{1,16},{16,1},{17,0},{2,19},{3,18},{18,3},{19,2},{4,21},{5,... | collective-permute-start | bytes 98312 | tf_op jit(solution)/shard_map/ppermute | solution.py:379
  34.0 2.9 %collective-permute-start.15 = (f32[64,128]{1,0:T(8,128)S(1)}, f32[64,128]{1,0:T(8,128)S(1)}, u32[]{:S(2)}, u32[]{:S(2)}) collective-permute-start(f32[64,128]{1,0:T(8,128)S(1)} %get-tuple-element.36.top), channel_id=1, source_target_pairs={{0,1},{1,0},{2,3},{3,2},{4,5},{5,4},{6,7},{7,6},{8,9},{9,8},{10,11... | collective-permute-start | bytes 98312 | tf_op jit(solution)/shard_map/ppermute | solution.py:380
  35.3 1.6 %collective-permute-start.16 = (f32[64,128]{1,0:T(8,128)S(1)}, f32[64,128]{1,0:T(8,128)S(1)}, u32[]{:S(2)}, u32[]{:S(2)}) collective-permute-start(f32[64,128]{1,0:T(8,128)S(1)} %get-tuple-element.37.low), channel_id=1, source_target_pairs={{0,1},{1,0},{2,3},{3,2},{4,5},{5,4},{6,7},{7,6},{8,9},{9,8},{10,11... | collective-permute-start | bytes 98312 | tf_op jit(solution)/shard_map/ppermute | solution.py:380

commit v26 on v22

--- a/solution.py
+++ b/solution.py
@@ -368,6 +368,7 @@
         factor_in[0].T, factor_out[0], demand, lengths, holder_slot, jnp.asarray(table, I32), depth
     )
     to_other, bounds = rows_call(hidden, bounds)
+    to_other, first = lax.optimization_barrier((to_other, first))
     bounds, first_later = lax.optimization_barrier((mark(bounds), first))
 
     firsts, seconds = [first], [second]

time: 37.9 us -> 39.7 us (1.047)
  waiting for transfers between devices: 10.9 us -> 12.4 us
  local copies, waits for them, and re-layouts: 0.01 us -> 0.56 us
    ppermute x3, starting transfers between devices: 0.44 us -> 5.97 us  [per_device(): a = lax.ppermute(ahead[0], 'batch', forward)]
    ppermute x3, starting transfers between devices: 6.79 us -> 1.62 us  [per_device(): d = lax.ppermute(behind[1], 'batch', backward)]
    ppermute x3, waiting for transfers between devices: 1.94 us -> 6.82 us  [per_device(): d = lax.ppermute(behind[1], 'batch', backward)]
    ppermute x1, waiting for transfers between devices: 3.05 us -> 0.01 us  [per_device(): other = lax.ppermute(to_other, 'groups', swap)]
    ppermute x3, starting transfers between devices: 5.02 us -> 2.7 us  [per_device(): c = lax.ppermute(behind[0], 'batch', backward)]
    ppermute x3, starting transfers between devices: 1.21 us -> 3.43 us  [per_device(): b = lax.ppermute(ahead[1], 'batch', forward)]
    ppermute x1, waiting for transfers between devices: 0.01 us -> 2.06 us  [per_device(): seconds.append(lax.ppermute(behind[1], 'batch', backward))]
    ppermute x1, starting transfers between devices: 1.74 us -> 0.53 us  [per_device(): seconds.append(lax.ppermute(behind[1], 'batch', backward))]
  transfers between devices with their start and end apart: 20 -> 20, of which waited for: 7 -> 8; matrix products, arithmetic and copies ran while one was open for 0% -> 0% of each run, Pallas kernels for 12% -> 11%
where the time goes in v26:
time: 39.7 us; the launch traced here: 39.5 us
  starting transfers between devices  19.7 us (50%)
  waiting for transfers between devices  12.4 us (31%)
  Pallas kernels  6.76 us (17%)
  local copies, waits for them, and re-layouts  0.56 us (1%)
    ppermute x3, waiting for transfers between devices, per_device(): d = lax.ppermute(behind[1], 'batch', backward)  6.82 us
    ppermute x3, starting transfers between devices, per_device(): a = lax.ppermute(ahead[0], 'batch', forward)  5.97 us
    ppermute x3, starting transfers between devices, per_device(): b = lax.ppermute(ahead[1], 'batch', forward)  3.43 us
    ppermute x3, starting transfers between devices, per_device(): c = lax.ppermute(behind[0], 'batch', backward)  2.7 us
    pallas_call x1, Pallas kernels, base_call(): pl.pallas_call(base_kernel, out_shape=(out, out), in_specs=[VMEM] * 2, ou...  2.35 us
    ppermute x2, starting transfers between devices, per_device(): one = [lax.ppermute(part, 'tensor', swap) for part in mine]  2.18 us
    ppermute x1, waiting for transfers between devices, per_device(): seconds.append(lax.ppermute(behind[1], 'batch', backward))  2.06 us
    ppermute x3, waiting for transfers between devices, per_device(): c = lax.ppermute(behind[0], 'batch', backward)  1.87 us
  transfers between devices with their start and end apart: 20, of which 8 were waited for; matrix products, arithmetic and copies ran while one was open for 0% of the time, Pallas kernels for 11%

profile of v26, /device:TPU:0, one launch (start us, length us, event | category | flops | bytes accessed | tf_op | source)
XLA Modules:
  0.0 39.5 jit_solution(634044490843006577)
XLA Ops:
  0.0 1.2 %shard_map.82 = (bf16[64,1280]{1,0:T(8,128)(2,1)S(1)}, bf16[64,1280]{1,0:T(8,128)(2,1)S(1)}, s32[8,512]{1,0:T(8,128)S(1)}) custom-call(bf16[64,4096]{1,0:T(8,128)(2,1)} %bitcast.6, bf16[64,512]{1,0:T(8,128)(2,1)} %bitcast.7, s32[1,4]{1,0:T(1,128)} %demand_ref.1, s32[1,4]{1,0:T(1,128)} %lengths_ref.1, s32[8]{0:T(128)} %holder_ref.1, ...), custom_call_target="tpu_custom_call" | custom-call | flops 8589934592 | bytes 16777216 | tf_op jit(solution)/shard_map/pallas_call | solution.py:137
  1.2 0.6 %copy-done = bf16[256,4096]{1,0:T(8,128)(2,1)S(1)} copy-done((bf16[256,4096]{1,0:T(8,128)(2,1)S(1)}, bf16[256,4096]{1,0:T(8,128)(2,1)}, u32[]{:S(2)}) %copy-start) | copy-done | bytes 2097176
  1.7 0.3 shard_map.83
  2.0 3.0 %collective-permute-start.2 = (bf16[64,1280]{1,0:T(8,128)(2,1)S(1)}, bf16[64,1280]{1,0:T(8,128)(2,1)S(1)}, u32[]{:S(2)}, u32[]{:S(2)}) collective-permute-start(bf16[64,1280]{1,0:T(8,128)(2,1)S(1)} %get-tuple-element.34.refs_3_), channel_id=1, source_target_pairs={{0,2},{2,6},{6,10},{10,14},{14,12},{12,8},{8,4},{4,0},{1,3},{3,7},... | collective-permute-start | bytes 491528 | tf_op jit(solution)/shard_map/ppermute | solution.py:377
  5.0 1.5 %collective-permute-start.14 = (bf16[4112,128]{1,0:T(8,128)(2,1)S(1)}, bf16[4112,128]{1,0:T(8,128)(2,1)S(1)}, u32[]{:S(2)}, u32[]{:S(2)}) collective-permute-start(bf16[4112,128]{1,0:T(8,128)(2,1)S(1)} %get-tuple-element.36), channel_id=1, source_target_pairs={{0,16},{16,0},{1,17},{17,1},{2,18},{18,2},{3,19},{19,3},{4,20},{20... | collective-permute-start | bytes 3158024 | tf_op jit(solution)/shard_map/ppermute | solution.py:388
  6.5 0.5 %collective-permute-start.7 = (bf16[64,1280]{1,0:T(8,128)(2,1)S(1)}, bf16[64,1280]{1,0:T(8,128)(2,1)S(1)}, u32[]{:S(2)}, u32[]{:S(2)}) collective-permute-start(bf16[64,1280]{1,0:T(8,128)(2,1)S(1)} %get-tuple-element.35.refs_7_.refs_0_), channel_id=1, source_target_pairs={{2,0},{6,2},{10,6},{14,10},{12,14},{8,12},{4,8},{0,4},{3,1},{7,3},... | collective-permute-start | bytes 491528 | tf_op jit(solution)/shard_map/ppermute | solution.py:378
  7.1 1.6 %collective-permute-start = (bf16[64,1280]{1,0:T(8,128)(2,1)S(1)}, bf16[64,1280]{1,0:T(8,128)(2,1)S(1)}, u32[]{:S(2)}, u32[]{:S(2)}) collective-permute-start(bf16[64,1280]{1,0:T(8,128)(2,1)S(1)} %get-tuple-element.34.refs_3_), channel_id=1, source_target_pairs={{2,0},{6,2},{10,6},{14,10},{12,14},{8,12},{4,8},{0,4},{3,1},{7,3},... | collective-permute-start | bytes 491528 | tf_op jit(solution)/shard_map/ppermute | solution.py:380
  8.7 0.4 %collective-permute-start.9 = (bf16[64,1280]{1,0:T(8,128)(2,1)S(1)}, bf16[64,1280]{1,0:T(8,128)(2,1)S(1)}, u32[]{:S(2)}, u32[]{:S(2)}) collective-permute-start(bf16[64,1280]{1,0:T(8,128)(2,1)S(1)} %get-tuple-element.35.refs_7_.refs_0_), channel_id=1, source_target_pairs={{0,2},{2,6},{6,10},{10,14},{14,12},{12,8},{8,4},{4,0},{1,3},{3,7},... | collective-permute-start | bytes 491528 | tf_op jit(solution)/shard_map/ppermute | solution.py:379
  9.1 4.6 %collective-permute-done.7.refs_9_.refs_2_ = bf16[64,1280]{1,0:T(8,128)(2,1)S(1)} collective-permute-done((bf16[64,1280]{1,0:T(8,128)(2,1)S(1)}, bf16[64,1280]{1,0:T(8,128)(2,1)S(1)}, u32[]{:S(2)}, u32[]{:S(2)}) %collective-permute-start.7) | collective-permute-done | bytes 163872 | tf_op jit(solution)/shard_map/ppermute | solution.py:378
  13.7 0.5 %collective-permute-start.8 = (bf16[64,1280]{1,0:T(8,128)(2,1)S(1)}, bf16[64,1280]{1,0:T(8,128)(2,1)S(1)}, u32[]{:S(2)}, u32[]{:S(2)}) collective-permute-start(bf16[64,1280]{1,0:T(8,128)(2,1)S(1)} %collective-permute-done.7.refs_9_.refs_2_), channel_id=1, source_target_pairs={{2,0},{6,2},{10,6},{14,10},{12,14},{8,12},{4,8},{0,4},{3,1},{7,3},... | collective-permute-start | bytes 491528 | tf_op jit(solution)/shard_map/ppermute | solution.py:378
  14.2 0.0 collective-permute-done.2.refs_4_
  14.2 1.5 %collective-permute-start.3 = (bf16[64,1280]{1,0:T(8,128)(2,1)S(1)}, bf16[64,1280]{1,0:T(8,128)(2,1)S(1)}, u32[]{:S(2)}, u32[]{:S(2)}) collective-permute-start(bf16[64,1280]{1,0:T(8,128)(2,1)S(1)} %collective-permute-done.2.refs_4_), channel_id=1, source_target_pairs={{0,2},{2,6},{6,10},{10,14},{14,12},{12,8},{8,4},{4,0},{1,3},{3,7},... | collective-permute-start | bytes 491528 | tf_op jit(solution)/shard_map/ppermute | solution.py:377
  15.7 1.5 %collective-permute-done.refs_5_ = bf16[64,1280]{1,0:T(8,128)(2,1)S(1)} collective-permute-done((bf16[64,1280]{1,0:T(8,128)(2,1)S(1)}, bf16[64,1280]{1,0:T(8,128)(2,1)S(1)}, u32[]{:S(2)}, u32[]{:S(2)}) %collective-permute-start) | collective-permute-done | bytes 163872 | tf_op jit(solution)/shard_map/ppermute | solution.py:380
  17.2 0.5 %collective-permute-start.1 = (bf16[64,1280]{1,0:T(8,128)(2,1)S(1)}, bf16[64,1280]{1,0:T(8,128)(2,1)S(1)}, u32[]{:S(2)}, u32[]{:S(2)}) collective-permute-start(bf16[64,1280]{1,0:T(8,128)(2,1)S(1)} %collective-permute-done.refs_5_), channel_id=1, source_target_pairs={{2,0},{6,2},{10,6},{14,10},{12,14},{8,12},{4,8},{0,4},{3,1},{7,3},... | collective-permute-start | bytes 491528 | tf_op jit(solution)/shard_map/ppermute | solution.py:380
  17.7 0.0 collective-permute-done.9.refs_8_.refs_1_
  17.7 1.5 %collective-permute-start.10 = (bf16[64,1280]{1,0:T(8,128)(2,1)S(1)}, bf16[64,1280]{1,0:T(8,128)(2,1)S(1)}, u32[]{:S(2)}, u32[]{:S(2)}) collective-permute-start(bf16[64,1280]{1,0:T(8,128)(2,1)S(1)} %collective-permute-done.9.refs_8_.refs_1_), channel_id=1, source_target_pairs={{0,2},{2,6},{6,10},{10,14},{14,12},{12,8},{8,4},{4,0},{1,3},{3,7},... | collective-permute-start | bytes 491528 | tf_op jit(solution)/shard_map/ppermute | solution.py:379
  19.2 1.6 %collective-permute-done.8.refs_6_.refs_4_ = bf16[64,1280]{1,0:T(8,128)(2,1)S(1)} collective-permute-done((bf16[64,1280]{1,0:T(8,128)(2,1)S(1)}, bf16[64,1280]{1,0:T(8,128)(2,1)S(1)}, u32[]{:S(2)}, u32[]{:S(2)}) %collective-permute-start.8) | collective-permute-done | bytes 163872 | tf_op jit(solution)/shard_map/ppermute | solution.py:378
  20.8 0.5 %collective-permute-start.12 = (bf16[64,1280]{1,0:T(8,128)(2,1)S(1)}, bf16[64,1280]{1,0:T(8,128)(2,1)S(1)}, u32[]{:S(2)}, u32[]{:S(2)}) collective-permute-start(bf16[64,1280]{1,0:T(8,128)(2,1)S(1)} %collective-permute-done.8.refs_6_.refs_4_), channel_id=1, source_target_pairs={{2,0},{6,2},{10,6},{14,10},{12,14},{8,12},{4,8},{0,4},{3,1},{7,3},... | collective-permute-start | bytes 491528 | tf_op jit(solution)/shard_map/ppermute | solution.py:378
  21.4 0.0 collective-permute-done.3.refs_6_
  21.4 1.5 %collective-permute-start.4 = (bf16[64,1280]{1,0:T(8,128)(2,1)S(1)}, bf16[64,1280]{1,0:T(8,128)(2,1)S(1)}, u32[]{:S(2)}, u32[]{:S(2)}) collective-permute-start(bf16[64,1280]{1,0:T(8,128)(2,1)S(1)} %collective-permute-done.3.refs_6_), channel_id=1, source_target_pairs={{0,2},{2,6},{6,10},{10,14},{14,12},{12,8},{8,4},{4,0},{1,3},{3,7},... | collective-permute-start | bytes 491528 | tf_op jit(solution)/shard_map/ppermute | solution.py:377
  22.9 2.3 %shard_map.85 = (f32[256,512]{1,0:T(8,128)S(1)}, f32[256,512]{1,0:T(8,128)S(1)}) custom-call(bf16[256,4096]{1,0:T(8,128)(2,1)S(1)} %copy-done, bf16[4096,1024]{1,0:T(8,128)(2,1)S(1)} %bitcast.5), custom_call_target="tpu_custom_call" | custom-call | bytes 4194304 | tf_op jit(solution)/shard_map/pallas_call | solution.py:219
  25.2 0.0 collective-permute-done.1.refs_2_
  25.2 0.6 %collective-permute-start.5 = (bf16[64,1280]{1,0:T(8,128)(2,1)S(1)}, bf16[64,1280]{1,0:T(8,128)(2,1)S(1)}, u32[]{:S(2)}, u32[]{:S(2)}) collective-permute-start(bf16[64,1280]{1,0:T(8,128)(2,1)S(1)} %collective-permute-done.1.refs_2_), channel_id=1, source_target_pairs={{2,0},{6,2},{10,6},{14,10},{12,14},{8,12},{4,8},{0,4},{3,1},{7,3},... | collective-permute-start | bytes 491528 | tf_op jit(solution)/shard_map/ppermute | solution.py:380
  25.8 0.0 collective-permute-done.10.refs_10_.refs_3_
  25.8 1.5 %collective-permute-start.11 = (bf16[64,1280]{1,0:T(8,128)(2,1)S(1)}, bf16[64,1280]{1,0:T(8,128)(2,1)S(1)}, u32[]{:S(2)}, u32[]{:S(2)}) collective-permute-start(bf16[64,1280]{1,0:T(8,128)(2,1)S(1)} %collective-permute-done.10.refs_10_.refs_3_), channel_id=1, source_target_pairs={{0,2},{2,6},{6,10},{10,14},{14,12},{12,8},{8,4},{4,0},{1,3},{3,7},... | collective-permute-start | bytes 491528 | tf_op jit(solution)/shard_map/ppermute | solution.py:379
  27.3 0.7 %collective-permute-done.12.refs_8_.refs_6_ = bf16[64,1280]{1,0:T(8,128)(2,1)S(1)} collective-permute-done((bf16[64,1280]{1,0:T(8,128)(2,1)S(1)}, bf16[64,1280]{1,0:T(8,128)(2,1)S(1)}, u32[]{:S(2)}, u32[]{:S(2)}) %collective-permute-start.12) | collective-permute-done | bytes 163872 | tf_op jit(solution)/shard_map/ppermute | solution.py:378
  28.0 0.5 %collective-permute-start.13 = (bf16[64,1280]{1,0:T(8,128)(2,1)S(1)}, bf16[64,1280]{1,0:T(8,128)(2,1)S(1)}, u32[]{:S(2)}, u32[]{:S(2)}) collective-permute-start(bf16[64,1280]{1,0:T(8,128)(2,1)S(1)} %collective-permute-done.12.refs_8_.refs_6_), channel_id=1, source_target_pairs={{2,0},{6,2},{10,6},{14,10},{12,14},{8,12},{4,8},{0,4},{3,1},{7,3},... | collective-permute-start | bytes 491528 | tf_op jit(solution)/shard_map/ppermute | solution.py:385
  28.5 0.0 collective-permute-done.4.refs_3_
  28.5 1.5 %collective-permute-start.6 = (bf16[64,1280]{1,0:T(8,128)(2,1)S(1)}, bf16[64,1280]{1,0:T(8,128)(2,1)S(1)}, u32[]{:S(2)}, u32[]{:S(2)}) collective-permute-start(bf16[64,1280]{1,0:T(8,128)(2,1)S(1)} %collective-permute-done.4.refs_3_), channel_id=1, source_target_pairs={{0,2},{2,6},{6,10},{10,14},{14,12},{12,8},{8,4},{4,0},{1,3},{3,7},... | collective-permute-start | bytes 491528 | tf_op jit(solution)/shard_map/ppermute | solution.py:384
  30.0 0.0 collective-permute-done.14.refs_1_.refs_0_
  30.0 0.7 %shard_map.86 = (f32[256,128]{1,0:T(8,128)S(1)}, f32[256,128]{1,0:T(8,128)S(1)}) custom-call(bf16[256,4096]{1,0:T(8,128)(2,1)S(1)} %copy-done, bf16[4112,128]{1,0:T(8,128)(2,1)S(1)} %collective-permute-done.14.refs_1_.refs_0_, s32[8,512]{1,0:T(8,128)S(1)} %shard_map.84.refs_2_.refs_1_.bounds_ref, bf16[64,1280]{1,0:T(8,128)(2,1)S(1)} %get-tuple-element.34.refs_3_, ...), custom_call_target="tpu_custom_call" | custom-call | flops 8589934592 | bytes 16777216 | tf_op jit(solution)/shard_map/pallas_call | solution.py:313
  30.8 0.1 collective-permute-start.19
  30.8 0.4 collective-permute-done.5.refs_4_
  31.2 0.0 collective-permute-done.11.refs_7_.refs_5_
  31.2 2.1 %collective-permute-done.13.refs_9_.refs_7_ = bf16[64,1280]{1,0:T(8,128)(2,1)S(1)} collective-permute-done((bf16[64,1280]{1,0:T(8,128)(2,1)S(1)}, bf16[64,1280]{1,0:T(8,128)(2,1)S(1)}, u32[]{:S(2)}, u32[]{:S(2)}) %collective-permute-start.13) | collective-permute-done | bytes 163872 | tf_op jit(solution)/shard_map/ppermute | solution.py:385
  33.3 0.5 %collective-permute-done.6.refs_5_ = bf16[64,1280]{1,0:T(8,128)(2,1)S(1)} collective-permute-done((bf16[64,1280]{1,0:T(8,128)(2,1)S(1)}, bf16[64,1280]{1,0:T(8,128)(2,1)S(1)}, u32[]{:S(2)}, u32[]{:S(2)}) %collective-permute-start.6) | collective-permute-done | bytes 163872 | tf_op jit(solution)/shard_map/ppermute | solution.py:384
  33.8 0.5 %shard_map.88 = bf16[128,128]{1,0:T(8,128)(2,1)S(1)} custom-call(bf16[4112,128]{1,0:T(8,128)(2,1)S(1)} %collective-permute-done.14.refs_1_.refs_0_, s32[8,512]{1,0:T(8,128)S(1)} %shard_map.84.refs_2_.refs_1_.bounds_ref, bf16[64,1280]{1,0:T(8,128)(2,1)S(1)} %collective-permute-done.1.refs_2_, bf16[64,1280]{1,0:T(8,128)(2,1)S(1)} %collective-permute-done.4.refs_3_, ...), custom_call_target="tpu_custom_call" | custom-call | flops 8589934592 | bytes 16777216 | tf_op jit(solution)/shard_map/pallas_call | solution.py:313
  34.4 0.2 collective-permute-start.17
  34.5 0.0 collective-permute-start.18
  34.5 0.5 %shard_map.87 = (f32[64,128]{1,0:T(8,128)S(1)}, f32[64,128]{1,0:T(8,128)S(1)}) custom-call(bf16[256,4096]{1,0:T(8,128)(2,1)S(1)} %copy-done, s32[8,512]{1,0:T(8,128)S(1)} %shard_map.84.refs_2_.refs_1_.bounds_ref, bf16[64,1280]{1,0:T(8,128)(2,1)S(1)} %collective-permute-done.1.refs_2_, bf16[64,1280]{1,0:T(8,128)(2,1)S(1)} %collective-permute-done.4.refs_3_, ...), custom_call_target="tpu_custom_call" | custom-call | bytes 4194304 | tf_op jit(solution)/shard_map/pallas_call | solution.py:313
  35.1 2.1 %collective-permute-start.15 = (f32[64,128]{1,0:T(8,128)S(1)}, f32[64,128]{1,0:T(8,128)S(1)}, u32[]{:S(2)}, u32[]{:S(2)}) collective-permute-start(f32[64,128]{1,0:T(8,128)S(1)} %get-tuple-element.38.top), channel_id=1, source_target_pairs={{0,1},{1,0},{2,3},{3,2},{4,5},{5,4},{6,7},{7,6},{8,9},{9,8},{10,11... | collective-permute-start | bytes 98312 | tf_op jit(solution)/shard_map/ppermute | solution.py:409
  37.2 0.1 collective-permute-start.16
  37.3 1.1 %collective-permute-done.17.two = bf16[128,128]{1,0:T(8,128)(2,1)S(1)} collective-permute-done((bf16[128,128]{1,0:T(8,128)(2,1)S(1)}, bf16[128,128]{1,0:T(8,128)(2,1)S(1)}, u32[]{:S(2)}, u32[]{:S(2)}) %collective-permute-start.17) | collective-permute-done | bytes 32800 | tf_op jit(solution)/shard_map/ppermute | solution.py:407
  38.4 0.0 collective-permute-done.18.three
  38.4 0.0 collective-permute-done.15.one_top
  38.4 0.0 collective-permute-done.16.one_low
  38.4 0.0 collective-permute-done.19.far_ref
  38.4 1.1 %shard_map.89 = bf16[256,512]{1,0:T(8,128)(2,1)} custom-call(s32[8,512]{1,0:T(8,128)S(1)} %shard_map.84.refs_2_.refs_1_.bounds_ref, f32[64,128]{1,0:T(8,128)S(1)} %get-tuple-element.38.top, f32[64,128]{1,0:T(8,128)S(1)} %get-tuple-element.39.low, f32[64,128]{1,0:T(8,128)S(1)} %collective-permute-done.15.one_top, ...), custom_call_target="tpu_custom_call" | custom-call | tf_op jit(solution)/shard_map/pallas_call | solution.py:412
  (7 shorter events, 0.0 us)
Async XLA Ops:
  0.0 1.7 %copy-start = (bf16[256,4096]{1,0:T(8,128)(2,1)S(1)}, bf16[256,4096]{1,0:T(8,128)(2,1)}, u32[]{:S(2)}) copy-start(bf16[256,4096]{1,0:T(8,128)(2,1)} %refs_0_.1) | copy-start | bytes 6291460
  2.0 12.2 %collective-permute-start.2 = (bf16[64,1280]{1,0:T(8,128)(2,1)S(1)}, bf16[64,1280]{1,0:T(8,128)(2,1)S(1)}, u32[]{:S(2)}, u32[]{:S(2)}) collective-permute-start(bf16[64,1280]{1,0:T(8,128)(2,1)S(1)} %get-tuple-element.34.refs_3_), channel_id=1, source_target_pairs={{0,2},{2,6},{6,10},{10,14},{14,12},{12,8},{8,4},{4,0},{1,3},{3,7},... | collective-permute-start | bytes 491528 | tf_op jit(solution)/shard_map/ppermute | solution.py:377
  5.0 25.0 %collective-permute-start.14 = (bf16[4112,128]{1,0:T(8,128)(2,1)S(1)}, bf16[4112,128]{1,0:T(8,128)(2,1)S(1)}, u32[]{:S(2)}, u32[]{:S(2)}) collective-permute-start(bf16[4112,128]{1,0:T(8,128)(2,1)S(1)} %get-tuple-element.36), channel_id=1, source_target_pairs={{0,16},{16,0},{1,17},{17,1},{2,18},{18,2},{3,19},{19,3},{4,20},{20... | collective-permute-start | bytes 3158024 | tf_op jit(solution)/shard_map/ppermute | solution.py:388
  6.5 7.1 %collective-permute-start.7 = (bf16[64,1280]{1,0:T(8,128)(2,1)S(1)}, bf16[64,1280]{1,0:T(8,128)(2,1)S(1)}, u32[]{:S(2)}, u32[]{:S(2)}) collective-permute-start(bf16[64,1280]{1,0:T(8,128)(2,1)S(1)} %get-tuple-element.35.refs_7_.refs_0_), channel_id=1, source_target_pairs={{2,0},{6,2},{10,6},{14,10},{12,14},{8,12},{4,8},{0,4},{3,1},{7,3},... | collective-permute-start | bytes 491528 | tf_op jit(solution)/shard_map/ppermute | solution.py:378
  7.1 15.8 %slice-start = ((s8[8388608]{0:T(1024)(128)(4,1)}), s8[4194304]{0:T(1024)(128)(4,1)S(1)}, s32[]{:S(2)}) async-start(s8[8388608]{0:T(1024)(128)(4,1)} %bitcast.4), calls=%async_computation | async-start | bytes 8388608
  7.1 15.8 %slice-start.1 = ((s8[8388608]{0:T(1024)(128)(4,1)}), s8[4194304]{0:T(1024)(128)(4,1)S(1)}, s32[]{:S(2)}) async-start(s8[8388608]{0:T(1024)(128)(4,1)} %bitcast.4), calls=%async_computation.1 | async-start | bytes 8388608
  7.1 10.1 %collective-permute-start = (bf16[64,1280]{1,0:T(8,128)(2,1)S(1)}, bf16[64,1280]{1,0:T(8,128)(2,1)S(1)}, u32[]{:S(2)}, u32[]{:S(2)}) collective-permute-start(bf16[64,1280]{1,0:T(8,128)(2,1)S(1)} %get-tuple-element.34.refs_3_), channel_id=1, source_target_pairs={{2,0},{6,2},{10,6},{14,10},{12,14},{8,12},{4,8},{0,4},{3,1},{7,3},... | collective-permute-start | bytes 491528 | tf_op jit(solution)/shard_map/ppermute | solution.py:380
  8.7 9.1 %collective-permute-start.9 = (bf16[64,1280]{1,0:T(8,128)(2,1)S(1)}, bf16[64,1280]{1,0:T(8,128)(2,1)S(1)}, u32[]{:S(2)}, u32[]{:S(2)}) collective-permute-start(bf16[64,1280]{1,0:T(8,128)(2,1)S(1)} %get-tuple-element.35.refs_7_.refs_0_), channel_id=1, source_target_pairs={{0,2},{2,6},{6,10},{10,14},{14,12},{12,8},{8,4},{4,0},{1,3},{3,7},... | collective-permute-start | bytes 491528 | tf_op jit(solution)/shard_map/ppermute | solution.py:379
  13.7 7.1 %collective-permute-start.8 = (bf16[64,1280]{1,0:T(8,128)(2,1)S(1)}, bf16[64,1280]{1,0:T(8,128)(2,1)S(1)}, u32[]{:S(2)}, u32[]{:S(2)}) collective-permute-start(bf16[64,1280]{1,0:T(8,128)(2,1)S(1)} %collective-permute-done.7.refs_9_.refs_2_), channel_id=1, source_target_pairs={{2,0},{6,2},{10,6},{14,10},{12,14},{8,12},{4,8},{0,4},{3,1},{7,3},... | collective-permute-start | bytes 491528 | tf_op jit(solution)/shard_map/ppermute | solution.py:378
  14.2 7.2 %collective-permute-start.3 = (bf16[64,1280]{1,0:T(8,128)(2,1)S(1)}, bf16[64,1280]{1,0:T(8,128)(2,1)S(1)}, u32[]{:S(2)}, u32[]{:S(2)}) collective-permute-start(bf16[64,1280]{1,0:T(8,128)(2,1)S(1)} %collective-permute-done.2.refs_4_), channel_id=1, source_target_pairs={{0,2},{2,6},{6,10},{10,14},{14,12},{12,8},{8,4},{4,0},{1,3},{3,7},... | collective-permute-start | bytes 491528 | tf_op jit(solution)/shard_map/ppermute | solution.py:377
  17.2 8.0 %collective-permute-start.1 = (bf16[64,1280]{1,0:T(8,128)(2,1)S(1)}, bf16[64,1280]{1,0:T(8,128)(2,1)S(1)}, u32[]{:S(2)}, u32[]{:S(2)}) collective-permute-start(bf16[64,1280]{1,0:T(8,128)(2,1)S(1)} %collective-permute-done.refs_5_), channel_id=1, source_target_pairs={{2,0},{6,2},{10,6},{14,10},{12,14},{8,12},{4,8},{0,4},{3,1},{7,3},... | collective-permute-start | bytes 491528 | tf_op jit(solution)/shard_map/ppermute | solution.py:380
  17.7 8.1 %collective-permute-start.10 = (bf16[64,1280]{1,0:T(8,128)(2,1)S(1)}, bf16[64,1280]{1,0:T(8,128)(2,1)S(1)}, u32[]{:S(2)}, u32[]{:S(2)}) collective-permute-start(bf16[64,1280]{1,0:T(8,128)(2,1)S(1)} %collective-permute-done.9.refs_8_.refs_1_), channel_id=1, source_target_pairs={{0,2},{2,6},{6,10},{10,14},{14,12},{12,8},{8,4},{4,0},{1,3},{3,7},... | collective-permute-start | bytes 491528 | tf_op jit(solution)/shard_map/ppermute | solution.py:379
  20.8 7.2 %collective-permute-start.12 = (bf16[64,1280]{1,0:T(8,128)(2,1)S(1)}, bf16[64,1280]{1,0:T(8,128)(2,1)S(1)}, u32[]{:S(2)}, u32[]{:S(2)}) collective-permute-start(bf16[64,1280]{1,0:T(8,128)(2,1)S(1)} %collective-permute-done.8.refs_6_.refs_4_), channel_id=1, source_target_pairs={{2,0},{6,2},{10,6},{14,10},{12,14},{8,12},{4,8},{0,4},{3,1},{7,3},... | collective-permute-start | bytes 491528 | tf_op jit(solution)/shard_map/ppermute | solution.py:378
  21.4 7.1 %collective-permute-start.4 = (bf16[64,1280]{1,0:T(8,128)(2,1)S(1)}, bf16[64,1280]{1,0:T(8,128)(2,1)S(1)}, u32[]{:S(2)}, u32[]{:S(2)}) collective-permute-start(bf16[64,1280]{1,0:T(8,128)(2,1)S(1)} %collective-permute-done.3.refs_6_), channel_id=1, source_target_pairs={{0,2},{2,6},{6,10},{10,14},{14,12},{12,8},{8,4},{4,0},{1,3},{3,7},... | collective-permute-start | bytes 491528 | tf_op jit(solution)/shard_map/ppermute | solution.py:377
  25.2 6.0 %collective-permute-start.5 = (bf16[64,1280]{1,0:T(8,128)(2,1)S(1)}, bf16[64,1280]{1,0:T(8,128)(2,1)S(1)}, u32[]{:S(2)}, u32[]{:S(2)}) collective-permute-start(bf16[64,1280]{1,0:T(8,128)(2,1)S(1)} %collective-permute-done.1.refs_2_), channel_id=1, source_target_pairs={{2,0},{6,2},{10,6},{14,10},{12,14},{8,12},{4,8},{0,4},{3,1},{7,3},... | collective-permute-start | bytes 491528 | tf_op jit(solution)/shard_map/ppermute | solution.py:380
  25.8 5.4 %collective-permute-start.11 = (bf16[64,1280]{1,0:T(8,128)(2,1)S(1)}, bf16[64,1280]{1,0:T(8,128)(2,1)S(1)}, u32[]{:S(2)}, u32[]{:S(2)}) collective-permute-start(bf16[64,1280]{1,0:T(8,128)(2,1)S(1)} %collective-permute-done.10.refs_10_.refs_3_), channel_id=1, source_target_pairs={{0,2},{2,6},{6,10},{10,14},{14,12},{12,8},{8,4},{4,0},{1,3},{3,7},... | collective-permute-start | bytes 491528 | tf_op jit(solution)/shard_map/ppermute | solution.py:379
  28.0 5.3 %collective-permute-start.13 = (bf16[64,1280]{1,0:T(8,128)(2,1)S(1)}, bf16[64,1280]{1,0:T(8,128)(2,1)S(1)}, u32[]{:S(2)}, u32[]{:S(2)}) collective-permute-start(bf16[64,1280]{1,0:T(8,128)(2,1)S(1)} %collective-permute-done.12.refs_8_.refs_6_), channel_id=1, source_target_pairs={{2,0},{6,2},{10,6},{14,10},{12,14},{8,12},{4,8},{0,4},{3,1},{7,3},... | collective-permute-start | bytes 491528 | tf_op jit(solution)/shard_map/ppermute | solution.py:385
  28.5 5.3 %collective-permute-start.6 = (bf16[64,1280]{1,0:T(8,128)(2,1)S(1)}, bf16[64,1280]{1,0:T(8,128)(2,1)S(1)}, u32[]{:S(2)}, u32[]{:S(2)}) collective-permute-start(bf16[64,1280]{1,0:T(8,128)(2,1)S(1)} %collective-permute-done.4.refs_3_), channel_id=1, source_target_pairs={{0,2},{2,6},{6,10},{10,14},{14,12},{12,8},{8,4},{4,0},{1,3},{3,7},... | collective-permute-start | bytes 491528 | tf_op jit(solution)/shard_map/ppermute | solution.py:384
  30.8 7.7 %collective-permute-start.19 = (f32[256,512]{1,0:T(8,128)S(1)}, f32[256,512]{1,0:T(8,128)S(1)}, u32[]{:S(2)}, u32[]{:S(2)}) collective-permute-start(f32[256,512]{1,0:T(8,128)S(1)} %get-tuple-element.44), channel_id=1, source_target_pairs={{0,1},{1,0},{2,3},{3,2},{4,5},{5,4},{6,7},{7,6},{8,9},{9,8},{10,11... | collective-permute-start | bytes 1572872 | tf_op jit(solution)/shard_map/ppermute | solution.py:401
  34.4 4.0 %collective-permute-start.17 = (bf16[128,128]{1,0:T(8,128)(2,1)S(1)}, bf16[128,128]{1,0:T(8,128)(2,1)S(1)}, u32[]{:S(2)}, u32[]{:S(2)}) collective-permute-start(bf16[128,128]{1,0:T(8,128)(2,1)S(1)} %shard_map.88), channel_id=1, source_target_pairs={{0,16},{16,0},{1,17},{17,1},{2,18},{18,2},{3,19},{19,3},{4,20},{20... | collective-permute-start | bytes 98312 | tf_op jit(solution)/shard_map/ppermute | solution.py:407
  34.5 3.8 %collective-permute-start.18 = (bf16[128,128]{1,0:T(8,128)(2,1)S(1)}, bf16[128,128]{1,0:T(8,128)(2,1)S(1)}, u32[]{:S(2)}, u32[]{:S(2)}) collective-permute-start(bf16[128,128]{1,0:T(8,128)(2,1)S(1)} %shard_map.88), channel_id=1, source_target_pairs={{0,17},{1,16},{16,1},{17,0},{2,19},{3,18},{18,3},{19,2},{4,21},{5,... | collective-permute-start | bytes 98312 | tf_op jit(solution)/shard_map/ppermute | solution.py:408
  35.1 3.3 %collective-permute-start.15 = (f32[64,128]{1,0:T(8,128)S(1)}, f32[64,128]{1,0:T(8,128)S(1)}, u32[]{:S(2)}, u32[]{:S(2)}) collective-permute-start(f32[64,128]{1,0:T(8,128)S(1)} %get-tuple-element.38.top), channel_id=1, source_target_pairs={{0,1},{1,0},{2,3},{3,2},{4,5},{5,4},{6,7},{7,6},{8,9},{9,8},{10,11... | collective-permute-start | bytes 98312 | tf_op jit(solution)/shard_map/ppermute | solution.py:409
  37.2 1.2 %collective-permute-start.16 = (f32[64,128]{1,0:T(8,128)S(1)}, f32[64,128]{1,0:T(8,128)S(1)}, u32[]{:S(2)}, u32[]{:S(2)}) collective-permute-start(f32[64,128]{1,0:T(8,128)S(1)} %get-tuple-element.39.low), channel_id=1, source_target_pairs={{0,1},{1,0},{2,3},{3,2},{4,5},{5,4},{6,7},{7,6},{8,9},{9,8},{10,11... | collective-permute-start | bytes 98312 | tf_op jit(solution)/shard_map/ppermute | solution.py:409

commit v27 on v18

--- a/solution.py
+++ b/solution.py
@@ -371,10 +371,10 @@
         factor_in[0].T, factor_out[0], demand, lengths, holder_slot, jnp.asarray(table, I32), depth
     )
     to_other, bounds = rows_call(hidden, bounds)
-    bounds, first_later, second_later = lax.optimization_barrier((mark(bounds), first, second))
+    bounds, first_later = lax.optimization_barrier((mark(bounds), first))
 
     firsts, seconds = [first], [second]
-    ahead, behind = (first, second_later), (first_later, second)
+    ahead, behind = (first, second), (first_later, second)
     for step in range(1, full + 1):
         a = lax.ppermute(ahead[0], "batch", forward)
         d = lax.ppermute(behind[1], "batch", backward)

time: 37.8 us -> 37.8 us (level)
  starting transfers between devices: 19.2 us -> 19.7 us
  waiting for transfers between devices: 11.5 us -> 11 us
    ppermute x3, waiting for transfers between devices: 3.51 us -> 0.01 us  [per_device(): b = lax.ppermute(ahead[1], 'batch', forward)]
    ppermute x3, waiting for transfers between devices: 0.01 us -> 2.91 us  [per_device(): c = lax.ppermute(behind[0], 'batch', backward)]
    ppermute x3, starting transfers between devices: 2.83 us -> 5.02 us  [per_device(): c = lax.ppermute(behind[0], 'batch', backward)]
    ppermute x3, starting transfers between devices: 3.3 us -> 1.21 us  [per_device(): b = lax.ppermute(ahead[1], 'batch', forward)]
    ppermute x3, starting transfers between devices: 5.32 us -> 6.79 us  [per_device(): d = lax.ppermute(behind[1], 'batch', backward)]
    ppermute x3, starting transfers between devices: 1.57 us -> 0.44 us  [per_device(): a = lax.ppermute(ahead[0], 'batch', forward)]
    ppermute x1, waiting for transfers between devices: 0.01 us -> 1.09 us  [per_device(): firsts.append(lax.ppermute(ahead[0], 'batch', forward))]
    ppermute x1, waiting for transfers between devices: 0.99 us -> 0.01 us  [per_device(): seconds.append(lax.ppermute(behind[1], 'batch', backward))]
where the time goes in v27:
time: 37.8 us; the launch traced here: 37.6 us
  starting transfers between devices  19.7 us (52%)
  waiting for transfers between devices  11 us (29%)
  Pallas kernels  6.83 us (18%)
    ppermute x3, starting transfers between devices, per_device(): d = lax.ppermute(behind[1], 'batch', backward)  6.79 us
    ppermute x3, starting transfers between devices, per_device(): c = lax.ppermute(behind[0], 'batch', backward)  5.02 us
    ppermute x1, waiting for transfers between devices, per_device(): other = lax.ppermute(to_other, 'groups', swap)  3.05 us
    ppermute x3, waiting for transfers between devices, per_device(): c = lax.ppermute(behind[0], 'batch', backward)  2.91 us
    pallas_call x1, Pallas kernels, base_call(): pl.pallas_call(functools.partial(base_kernel, size), out_shape=(out, out,...  2.47 us
    ppermute x1, starting transfers between devices, per_device(): other = lax.ppermute(to_other, 'groups', swap)  2.03 us
    pallas_call x3, Pallas kernels, rank_call(): pl.pallas_call(functools.partial(rank_kernel, sides, groups, depth, last)...  1.84 us
    ppermute x3, waiting for transfers between devices, per_device(): d = lax.ppermute(behind[1], 'batch', backward)  1.81 us
  transfers between devices with their start and end apart: 20, of which 7 were waited for; matrix products, arithmetic and copies ran while one was open for 0% of the time, Pallas kernels for 12%

profile of v27, /device:TPU:0, one launch (start us, length us, event | category | flops | bytes accessed | tf_op | source)
XLA Modules:
  0.0 37.6 jit_solution(7674626021773258841)
XLA Ops:
  0.0 1.2 %shard_map.82 = (bf16[64,1280]{1,0:T(8,128)(2,1)S(1)}, bf16[64,1280]{1,0:T(8,128)(2,1)S(1)}, s32[8,512]{1,0:T(8,128)S(1)}) custom-call(bf16[64,4096]{1,0:T(8,128)(2,1)} %bitcast.6, bf16[64,512]{1,0:T(8,128)(2,1)} %bitcast.7, s32[1,4]{1,0:T(1,128)} %demand_ref.1, s32[1,4]{1,0:T(1,128)} %lengths_ref.1, s32[8]{0:T(128)} %holder_ref.1, ...), custom_call_target="tpu_custom_call" | custom-call | flops 8589934592 | bytes 16777216 | tf_op jit(solution)/shard_map/pallas_call | solution.py:137
  1.2 3.1 %collective-permute-start.7 = (bf16[64,1280]{1,0:T(8,128)(2,1)S(1)}, bf16[64,1280]{1,0:T(8,128)(2,1)S(1)}, u32[]{:S(2)}, u32[]{:S(2)}) collective-permute-start(bf16[64,1280]{1,0:T(8,128)(2,1)S(1)} %get-tuple-element.33.refs_7_.refs_0_), channel_id=1, source_target_pairs={{2,0},{6,2},{10,6},{14,10},{12,14},{8,12},{4,8},{0,4},{3,1},{7,3},... | collective-permute-start | bytes 491528 | tf_op jit(solution)/shard_map/ppermute | solution.py:380
  4.3 0.0 collective-permute-start.2
  4.3 0.3 shard_map.83
  4.6 2.0 %collective-permute-start.14 = (bf16[4112,128]{1,0:T(8,128)(2,1)S(1)}, bf16[4112,128]{1,0:T(8,128)(2,1)S(1)}, u32[]{:S(2)}, u32[]{:S(2)}) collective-permute-start(bf16[4112,128]{1,0:T(8,128)(2,1)S(1)} %get-tuple-element.34), channel_id=1, source_target_pairs={{0,16},{16,0},{1,17},{17,1},{2,18},{18,2},{3,19},{19,3},{4,20},{20... | collective-permute-start | bytes 3158024 | tf_op jit(solution)/shard_map/ppermute | solution.py:390
  6.6 1.6 %collective-permute-start = (bf16[64,1280]{1,0:T(8,128)(2,1)S(1)}, bf16[64,1280]{1,0:T(8,128)(2,1)S(1)}, u32[]{:S(2)}, u32[]{:S(2)}) collective-permute-start(bf16[64,1280]{1,0:T(8,128)(2,1)S(1)} %get-tuple-element.32.refs_3_), channel_id=1, source_target_pairs={{2,0},{6,2},{10,6},{14,10},{12,14},{8,12},{4,8},{0,4},{3,1},{7,3},... | collective-permute-start | bytes 491528 | tf_op jit(solution)/shard_map/ppermute | solution.py:382
  8.2 0.4 %collective-permute-start.9 = (bf16[64,1280]{1,0:T(8,128)(2,1)S(1)}, bf16[64,1280]{1,0:T(8,128)(2,1)S(1)}, u32[]{:S(2)}, u32[]{:S(2)}) collective-permute-start(bf16[64,1280]{1,0:T(8,128)(2,1)S(1)} %get-tuple-element.33.refs_7_.refs_0_), channel_id=1, source_target_pairs={{0,2},{2,6},{6,10},{10,14},{14,12},{12,8},{8,4},{4,0},{1,3},{3,7},... | collective-permute-start | bytes 491528 | tf_op jit(solution)/shard_map/ppermute | solution.py:381
  8.6 0.0 collective-permute-done.7.refs_9_.refs_2_
  8.6 2.0 %collective-permute-start.8 = (bf16[64,1280]{1,0:T(8,128)(2,1)S(1)}, bf16[64,1280]{1,0:T(8,128)(2,1)S(1)}, u32[]{:S(2)}, u32[]{:S(2)}) collective-permute-start(bf16[64,1280]{1,0:T(8,128)(2,1)S(1)} %collective-permute-done.7.refs_9_.refs_2_), channel_id=1, source_target_pairs={{2,0},{6,2},{10,6},{14,10},{12,14},{8,12},{4,8},{0,4},{3,1},{7,3},... | collective-permute-start | bytes 491528 | tf_op jit(solution)/shard_map/ppermute | solution.py:380
  10.6 0.0 collective-permute-done.2.refs_4_
  10.6 0.1 collective-permute-start.3
  10.7 2.9 %collective-permute-done.refs_5_ = bf16[64,1280]{1,0:T(8,128)(2,1)S(1)} collective-permute-done((bf16[64,1280]{1,0:T(8,128)(2,1)S(1)}, bf16[64,1280]{1,0:T(8,128)(2,1)S(1)}, u32[]{:S(2)}, u32[]{:S(2)}) %collective-permute-start) | collective-permute-done | bytes 163872 | tf_op jit(solution)/shard_map/ppermute | solution.py:382
  13.6 1.7 %collective-permute-start.1 = (bf16[64,1280]{1,0:T(8,128)(2,1)S(1)}, bf16[64,1280]{1,0:T(8,128)(2,1)S(1)}, u32[]{:S(2)}, u32[]{:S(2)}) collective-permute-start(bf16[64,1280]{1,0:T(8,128)(2,1)S(1)} %collective-permute-done.refs_5_), channel_id=1, source_target_pairs={{2,0},{6,2},{10,6},{14,10},{12,14},{8,12},{4,8},{0,4},{3,1},{7,3},... | collective-permute-start | bytes 491528 | tf_op jit(solution)/shard_map/ppermute | solution.py:382
  15.3 0.0 collective-permute-done.9.refs_8_.refs_1_
  15.3 0.4 %collective-permute-start.10 = (bf16[64,1280]{1,0:T(8,128)(2,1)S(1)}, bf16[64,1280]{1,0:T(8,128)(2,1)S(1)}, u32[]{:S(2)}, u32[]{:S(2)}) collective-permute-start(bf16[64,1280]{1,0:T(8,128)(2,1)S(1)} %collective-permute-done.9.refs_8_.refs_1_), channel_id=1, source_target_pairs={{0,2},{2,6},{6,10},{10,14},{14,12},{12,8},{8,4},{4,0},{1,3},{3,7},... | collective-permute-start | bytes 491528 | tf_op jit(solution)/shard_map/ppermute | solution.py:381
  15.7 1.4 %collective-permute-done.8.refs_6_.refs_4_ = bf16[64,1280]{1,0:T(8,128)(2,1)S(1)} collective-permute-done((bf16[64,1280]{1,0:T(8,128)(2,1)S(1)}, bf16[64,1280]{1,0:T(8,128)(2,1)S(1)}, u32[]{:S(2)}, u32[]{:S(2)}) %collective-permute-start.8) | collective-permute-done | bytes 163872 | tf_op jit(solution)/shard_map/ppermute | solution.py:380
  17.1 1.7 %collective-permute-start.12 = (bf16[64,1280]{1,0:T(8,128)(2,1)S(1)}, bf16[64,1280]{1,0:T(8,128)(2,1)S(1)}, u32[]{:S(2)}, u32[]{:S(2)}) collective-permute-start(bf16[64,1280]{1,0:T(8,128)(2,1)S(1)} %collective-permute-done.8.refs_6_.refs_4_), channel_id=1, source_target_pairs={{2,0},{6,2},{10,6},{14,10},{12,14},{8,12},{4,8},{0,4},{3,1},{7,3},... | collective-permute-start | bytes 491528 | tf_op jit(solution)/shard_map/ppermute | solution.py:380
  18.8 0.0 collective-permute-done.3.refs_6_
  18.8 0.4 %collective-permute-start.4 = (bf16[64,1280]{1,0:T(8,128)(2,1)S(1)}, bf16[64,1280]{1,0:T(8,128)(2,1)S(1)}, u32[]{:S(2)}, u32[]{:S(2)}) collective-permute-start(bf16[64,1280]{1,0:T(8,128)(2,1)S(1)} %collective-permute-done.3.refs_6_), channel_id=1, source_target_pairs={{0,2},{2,6},{6,10},{10,14},{14,12},{12,8},{8,4},{4,0},{1,3},{3,7},... | collective-permute-start | bytes 491528 | tf_op jit(solution)/shard_map/ppermute | solution.py:379
  19.2 0.0 slice-done
  19.2 2.5 %shard_map.85 = (f32[256,512]{1,0:T(8,128)S(1)}, f32[256,512]{1,0:T(8,128)S(1)}, bf16[256,512]{1,0:T(8,128)(2,1)S(1)}) custom-call(bf16[256,4096]{1,0:T(8,128)(2,1)S(1)} %copy-done, bf16[4096,1024]{1,0:T(8,128)(2,1)S(1)} %bitcast.5, s32[8,512]{1,0:T(8,128)S(1)} %shard_map.84.bounds_ref.refs_2_.refs_1_), custom_call_target="tpu_custom_call" | custom-call | bytes 4194304 | tf_op jit(solution)/shard_map/pallas_call | solution.py:223
  21.7 0.0 collective-permute-done.1.refs_2_
  21.7 1.7 %collective-permute-start.5 = (bf16[64,1280]{1,0:T(8,128)(2,1)S(1)}, bf16[64,1280]{1,0:T(8,128)(2,1)S(1)}, u32[]{:S(2)}, u32[]{:S(2)}) collective-permute-start(bf16[64,1280]{1,0:T(8,128)(2,1)S(1)} %collective-permute-done.1.refs_2_), channel_id=1, source_target_pairs={{2,0},{6,2},{10,6},{14,10},{12,14},{8,12},{4,8},{0,4},{3,1},{7,3},... | collective-permute-start | bytes 491528 | tf_op jit(solution)/shard_map/ppermute | solution.py:382
  23.4 0.0 collective-permute-done.10.refs_10_.refs_3_
  23.4 0.4 %collective-permute-start.11 = (bf16[64,1280]{1,0:T(8,128)(2,1)S(1)}, bf16[64,1280]{1,0:T(8,128)(2,1)S(1)}, u32[]{:S(2)}, u32[]{:S(2)}) collective-permute-start(bf16[64,1280]{1,0:T(8,128)(2,1)S(1)} %collective-permute-done.10.refs_10_.refs_3_), channel_id=1, source_target_pairs={{0,2},{2,6},{6,10},{10,14},{14,12},{12,8},{8,4},{4,0},{1,3},{3,7},... | collective-permute-start | bytes 491528 | tf_op jit(solution)/shard_map/ppermute | solution.py:381
  23.8 0.4 %collective-permute-done.12.refs_8_.refs_6_ = bf16[64,1280]{1,0:T(8,128)(2,1)S(1)} collective-permute-done((bf16[64,1280]{1,0:T(8,128)(2,1)S(1)}, bf16[64,1280]{1,0:T(8,128)(2,1)S(1)}, u32[]{:S(2)}, u32[]{:S(2)}) %collective-permute-start.12) | collective-permute-done | bytes 163872 | tf_op jit(solution)/shard_map/ppermute | solution.py:380
  24.2 1.7 %collective-permute-start.13 = (bf16[64,1280]{1,0:T(8,128)(2,1)S(1)}, bf16[64,1280]{1,0:T(8,128)(2,1)S(1)}, u32[]{:S(2)}, u32[]{:S(2)}) collective-permute-start(bf16[64,1280]{1,0:T(8,128)(2,1)S(1)} %collective-permute-done.12.refs_8_.refs_6_), channel_id=1, source_target_pairs={{2,0},{6,2},{10,6},{14,10},{12,14},{8,12},{4,8},{0,4},{3,1},{7,3},... | collective-permute-start | bytes 491528 | tf_op jit(solution)/shard_map/ppermute | solution.py:387
  26.0 0.0 collective-permute-done.4.refs_3_
  26.0 0.3 collective-permute-start.6
  26.3 3.1 %collective-permute-done.14.refs_1_.refs_0_ = bf16[4112,128]{1,0:T(8,128)(2,1)S(1)} collective-permute-done((bf16[4112,128]{1,0:T(8,128)(2,1)S(1)}, bf16[4112,128]{1,0:T(8,128)(2,1)S(1)}, u32[]{:S(2)}, u32[]{:S(2)}) %collective-permute-start.14) | collective-permute-done | bytes 1052704 | tf_op jit(solution)/shard_map/ppermute | solution.py:390
  29.3 0.7 %shard_map.86 = (f32[256,128]{1,0:T(8,128)S(1)}, f32[256,128]{1,0:T(8,128)S(1)}) custom-call(bf16[256,4096]{1,0:T(8,128)(2,1)S(1)} %copy-done, bf16[4112,128]{1,0:T(8,128)(2,1)S(1)} %collective-permute-done.14.refs_1_.refs_0_, s32[8,512]{1,0:T(8,128)S(1)} %shard_map.84.bounds_ref.refs_2_.refs_1_, bf16[64,1280]{1,0:T(8,128)(2,1)S(1)} %get-tuple-element.32.refs_3_, ...), custom_call_target="tpu_custom_call" | custom-call | flops 8589934592 | bytes 16777216 | tf_op jit(solution)/shard_map/pallas_call | solution.py:317
  30.1 0.1 collective-permute-start.19
  30.2 0.0 collective-permute-done.5.refs_4_
  30.2 0.0 collective-permute-done.11.refs_7_.refs_5_
  30.2 0.0 collective-permute-done.13.refs_9_.refs_7_
  30.2 1.1 %collective-permute-done.6.refs_5_ = bf16[64,1280]{1,0:T(8,128)(2,1)S(1)} collective-permute-done((bf16[64,1280]{1,0:T(8,128)(2,1)S(1)}, bf16[64,1280]{1,0:T(8,128)(2,1)S(1)}, u32[]{:S(2)}, u32[]{:S(2)}) %collective-permute-start.6) | collective-permute-done | bytes 163872 | tf_op jit(solution)/shard_map/ppermute | solution.py:386
  31.3 0.5 %shard_map.88 = bf16[128,128]{1,0:T(8,128)(2,1)S(1)} custom-call(bf16[4112,128]{1,0:T(8,128)(2,1)S(1)} %collective-permute-done.14.refs_1_.refs_0_, s32[8,512]{1,0:T(8,128)S(1)} %shard_map.84.bounds_ref.refs_2_.refs_1_, bf16[64,1280]{1,0:T(8,128)(2,1)S(1)} %collective-permute-done.1.refs_2_, bf16[64,1280]{1,0:T(8,128)(2,1)S(1)} %collective-permute-done.4.refs_3_, ...), custom_call_target="tpu_custom_call" | custom-call | flops 8589934592 | bytes 16777216 | tf_op jit(solution)/shard_map/pallas_call | solution.py:317
  31.8 0.8 %collective-permute-start.17 = (bf16[128,128]{1,0:T(8,128)(2,1)S(1)}, bf16[128,128]{1,0:T(8,128)(2,1)S(1)}, u32[]{:S(2)}, u32[]{:S(2)}) collective-permute-start(bf16[128,128]{1,0:T(8,128)(2,1)S(1)} %shard_map.88), channel_id=1, source_target_pairs={{0,17},{1,16},{16,1},{17,0},{2,19},{3,18},{18,3},{19,2},{4,21},{5,... | collective-permute-start | bytes 98312 | tf_op jit(solution)/shard_map/ppermute | solution.py:409
  32.6 0.6 %collective-permute-start.18 = (bf16[128,128]{1,0:T(8,128)(2,1)S(1)}, bf16[128,128]{1,0:T(8,128)(2,1)S(1)}, u32[]{:S(2)}, u32[]{:S(2)}) collective-permute-start(bf16[128,128]{1,0:T(8,128)(2,1)S(1)} %shard_map.88), channel_id=1, source_target_pairs={{0,16},{16,0},{1,17},{17,1},{2,18},{18,2},{3,19},{19,3},{4,20},{20... | collective-permute-start | bytes 98312 | tf_op jit(solution)/shard_map/ppermute | solution.py:410
  33.2 0.5 %shard_map.87 = (f32[64,128]{1,0:T(8,128)S(1)}, f32[64,128]{1,0:T(8,128)S(1)}) custom-call(bf16[256,4096]{1,0:T(8,128)(2,1)S(1)} %copy-done, s32[8,512]{1,0:T(8,128)S(1)} %shard_map.84.bounds_ref.refs_2_.refs_1_, bf16[64,1280]{1,0:T(8,128)(2,1)S(1)} %collective-permute-done.1.refs_2_, bf16[64,1280]{1,0:T(8,128)(2,1)S(1)} %collective-permute-done.4.refs_3_, ...), custom_call_target="tpu_custom_call" | custom-call | bytes 4194304 | tf_op jit(solution)/shard_map/pallas_call | solution.py:317
  33.8 0.6 %collective-permute-start.15 = (f32[64,128]{1,0:T(8,128)S(1)}, f32[64,128]{1,0:T(8,128)S(1)}, u32[]{:S(2)}, u32[]{:S(2)}) collective-permute-start(f32[64,128]{1,0:T(8,128)S(1)} %get-tuple-element.36.top), channel_id=1, source_target_pairs={{0,1},{1,0},{2,3},{3,2},{4,5},{5,4},{6,7},{7,6},{8,9},{9,8},{10,11... | collective-permute-start | bytes 98312 | tf_op jit(solution)/shard_map/ppermute | solution.py:411
  34.4 0.1 collective-permute-start.16
  34.5 0.9 %collective-permute-done.17.three = bf16[128,128]{1,0:T(8,128)(2,1)S(1)} collective-permute-done((bf16[128,128]{1,0:T(8,128)(2,1)S(1)}, bf16[128,128]{1,0:T(8,128)(2,1)S(1)}, u32[]{:S(2)}, u32[]{:S(2)}) %collective-permute-start.17) | collective-permute-done | bytes 32800 | tf_op jit(solution)/shard_map/ppermute | solution.py:409
  35.4 1.2 %collective-permute-done.18.two = bf16[128,128]{1,0:T(8,128)(2,1)S(1)} collective-permute-done((bf16[128,128]{1,0:T(8,128)(2,1)S(1)}, bf16[128,128]{1,0:T(8,128)(2,1)S(1)}, u32[]{:S(2)}, u32[]{:S(2)}) %collective-permute-start.18) | collective-permute-done | bytes 32800 | tf_op jit(solution)/shard_map/ppermute | solution.py:410
  36.5 0.0 collective-permute-done.15.one_top
  36.6 0.0 collective-permute-done.16.one_low
  36.6 0.0 collective-permute-done.19.far_ref
  36.6 1.1 %shard_map.89 = bf16[256,512]{1,0:T(8,128)(2,1)} custom-call(bf16[256,512]{1,0:T(8,128)(2,1)S(1)} %get-tuple-element.28.mask_ref, f32[64,128]{1,0:T(8,128)S(1)} %get-tuple-element.36.top, f32[64,128]{1,0:T(8,128)S(1)} %get-tuple-element.37.low, f32[64,128]{1,0:T(8,128)S(1)} %collective-permute-done.15.one_top, ...), custom_call_target="tpu_custom_call" | custom-call | tf_op jit(solution)/shard_map/pallas_call | solution.py:414
  (7 shorter events, 0.0 us)
Async XLA Ops:
  0.0 4.3 %copy-start = (bf16[256,4096]{1,0:T(8,128)(2,1)S(1)}, bf16[256,4096]{1,0:T(8,128)(2,1)}, u32[]{:S(2)}) copy-start(bf16[256,4096]{1,0:T(8,128)(2,1)} %refs_0_.1) | copy-start | bytes 6291460
  1.2 7.4 %collective-permute-start.7 = (bf16[64,1280]{1,0:T(8,128)(2,1)S(1)}, bf16[64,1280]{1,0:T(8,128)(2,1)S(1)}, u32[]{:S(2)}, u32[]{:S(2)}) collective-permute-start(bf16[64,1280]{1,0:T(8,128)(2,1)S(1)} %get-tuple-element.33.refs_7_.refs_0_), channel_id=1, source_target_pairs={{2,0},{6,2},{10,6},{14,10},{12,14},{8,12},{4,8},{0,4},{3,1},{7,3},... | collective-permute-start | bytes 491528 | tf_op jit(solution)/shard_map/ppermute | solution.py:380
  4.3 6.3 %collective-permute-start.2 = (bf16[64,1280]{1,0:T(8,128)(2,1)S(1)}, bf16[64,1280]{1,0:T(8,128)(2,1)S(1)}, u32[]{:S(2)}, u32[]{:S(2)}) collective-permute-start(bf16[64,1280]{1,0:T(8,128)(2,1)S(1)} %get-tuple-element.32.refs_3_), channel_id=1, source_target_pairs={{0,2},{2,6},{6,10},{10,14},{14,12},{12,8},{8,4},{4,0},{1,3},{3,7},... | collective-permute-start | bytes 491528 | tf_op jit(solution)/shard_map/ppermute | solution.py:379
  4.6 24.8 %collective-permute-start.14 = (bf16[4112,128]{1,0:T(8,128)(2,1)S(1)}, bf16[4112,128]{1,0:T(8,128)(2,1)S(1)}, u32[]{:S(2)}, u32[]{:S(2)}) collective-permute-start(bf16[4112,128]{1,0:T(8,128)(2,1)S(1)} %get-tuple-element.34), channel_id=1, source_target_pairs={{0,16},{16,0},{1,17},{17,1},{2,18},{18,2},{3,19},{19,3},{4,20},{20... | collective-permute-start | bytes 3158024 | tf_op jit(solution)/shard_map/ppermute | solution.py:390
  6.6 12.6 %slice-start = ((s8[8388608]{0:T(1024)(128)(4,1)}), s8[4194304]{0:T(1024)(128)(4,1)S(1)}, s32[]{:S(2)}) async-start(s8[8388608]{0:T(1024)(128)(4,1)} %bitcast.4), calls=%async_computation | async-start | bytes 8388608
  6.6 12.6 %slice-start.1 = ((s8[8388608]{0:T(1024)(128)(4,1)}), s8[4194304]{0:T(1024)(128)(4,1)S(1)}, s32[]{:S(2)}) async-start(s8[8388608]{0:T(1024)(128)(4,1)} %bitcast.4), calls=%async_computation.1 | async-start | bytes 8388608
  6.6 7.0 %collective-permute-start = (bf16[64,1280]{1,0:T(8,128)(2,1)S(1)}, bf16[64,1280]{1,0:T(8,128)(2,1)S(1)}, u32[]{:S(2)}, u32[]{:S(2)}) collective-permute-start(bf16[64,1280]{1,0:T(8,128)(2,1)S(1)} %get-tuple-element.32.refs_3_), channel_id=1, source_target_pairs={{2,0},{6,2},{10,6},{14,10},{12,14},{8,12},{4,8},{0,4},{3,1},{7,3},... | collective-permute-start | bytes 491528 | tf_op jit(solution)/shard_map/ppermute | solution.py:382
  8.2 7.1 %collective-permute-start.9 = (bf16[64,1280]{1,0:T(8,128)(2,1)S(1)}, bf16[64,1280]{1,0:T(8,128)(2,1)S(1)}, u32[]{:S(2)}, u32[]{:S(2)}) collective-permute-start(bf16[64,1280]{1,0:T(8,128)(2,1)S(1)} %get-tuple-element.33.refs_7_.refs_0_), channel_id=1, source_target_pairs={{0,2},{2,6},{6,10},{10,14},{14,12},{12,8},{8,4},{4,0},{1,3},{3,7},... | collective-permute-start | bytes 491528 | tf_op jit(solution)/shard_map/ppermute | solution.py:381
  8.6 8.5 %collective-permute-start.8 = (bf16[64,1280]{1,0:T(8,128)(2,1)S(1)}, bf16[64,1280]{1,0:T(8,128)(2,1)S(1)}, u32[]{:S(2)}, u32[]{:S(2)}) collective-permute-start(bf16[64,1280]{1,0:T(8,128)(2,1)S(1)} %collective-permute-done.7.refs_9_.refs_2_), channel_id=1, source_target_pairs={{2,0},{6,2},{10,6},{14,10},{12,14},{8,12},{4,8},{0,4},{3,1},{7,3},... | collective-permute-start | bytes 491528 | tf_op jit(solution)/shard_map/ppermute | solution.py:380
  10.6 8.2 %collective-permute-start.3 = (bf16[64,1280]{1,0:T(8,128)(2,1)S(1)}, bf16[64,1280]{1,0:T(8,128)(2,1)S(1)}, u32[]{:S(2)}, u32[]{:S(2)}) collective-permute-start(bf16[64,1280]{1,0:T(8,128)(2,1)S(1)} %collective-permute-done.2.refs_4_), channel_id=1, source_target_pairs={{0,2},{2,6},{6,10},{10,14},{14,12},{12,8},{8,4},{4,0},{1,3},{3,7},... | collective-permute-start | bytes 491528 | tf_op jit(solution)/shard_map/ppermute | solution.py:379
  13.6 8.1 %collective-permute-start.1 = (bf16[64,1280]{1,0:T(8,128)(2,1)S(1)}, bf16[64,1280]{1,0:T(8,128)(2,1)S(1)}, u32[]{:S(2)}, u32[]{:S(2)}) collective-permute-start(bf16[64,1280]{1,0:T(8,128)(2,1)S(1)} %collective-permute-done.refs_5_), channel_id=1, source_target_pairs={{2,0},{6,2},{10,6},{14,10},{12,14},{8,12},{4,8},{0,4},{3,1},{7,3},... | collective-permute-start | bytes 491528 | tf_op jit(solution)/shard_map/ppermute | solution.py:382
  15.3 8.1 %collective-permute-start.10 = (bf16[64,1280]{1,0:T(8,128)(2,1)S(1)}, bf16[64,1280]{1,0:T(8,128)(2,1)S(1)}, u32[]{:S(2)}, u32[]{:S(2)}) collective-permute-start(bf16[64,1280]{1,0:T(8,128)(2,1)S(1)} %collective-permute-done.9.refs_8_.refs_1_), channel_id=1, source_target_pairs={{0,2},{2,6},{6,10},{10,14},{14,12},{12,8},{8,4},{4,0},{1,3},{3,7},... | collective-permute-start | bytes 491528 | tf_op jit(solution)/shard_map/ppermute | solution.py:381
  17.1 7.1 %collective-permute-start.12 = (bf16[64,1280]{1,0:T(8,128)(2,1)S(1)}, bf16[64,1280]{1,0:T(8,128)(2,1)S(1)}, u32[]{:S(2)}, u32[]{:S(2)}) collective-permute-start(bf16[64,1280]{1,0:T(8,128)(2,1)S(1)} %collective-permute-done.8.refs_6_.refs_4_), channel_id=1, source_target_pairs={{2,0},{6,2},{10,6},{14,10},{12,14},{8,12},{4,8},{0,4},{3,1},{7,3},... | collective-permute-start | bytes 491528 | tf_op jit(solution)/shard_map/ppermute | solution.py:380
  18.8 7.1 %collective-permute-start.4 = (bf16[64,1280]{1,0:T(8,128)(2,1)S(1)}, bf16[64,1280]{1,0:T(8,128)(2,1)S(1)}, u32[]{:S(2)}, u32[]{:S(2)}) collective-permute-start(bf16[64,1280]{1,0:T(8,128)(2,1)S(1)} %collective-permute-done.3.refs_6_), channel_id=1, source_target_pairs={{0,2},{2,6},{6,10},{10,14},{14,12},{12,8},{8,4},{4,0},{1,3},{3,7},... | collective-permute-start | bytes 491528 | tf_op jit(solution)/shard_map/ppermute | solution.py:379
  21.7 8.5 %collective-permute-start.5 = (bf16[64,1280]{1,0:T(8,128)(2,1)S(1)}, bf16[64,1280]{1,0:T(8,128)(2,1)S(1)}, u32[]{:S(2)}, u32[]{:S(2)}) collective-permute-start(bf16[64,1280]{1,0:T(8,128)(2,1)S(1)} %collective-permute-done.1.refs_2_), channel_id=1, source_target_pairs={{2,0},{6,2},{10,6},{14,10},{12,14},{8,12},{4,8},{0,4},{3,1},{7,3},... | collective-permute-start | bytes 491528 | tf_op jit(solution)/shard_map/ppermute | solution.py:382
  23.4 6.8 %collective-permute-start.11 = (bf16[64,1280]{1,0:T(8,128)(2,1)S(1)}, bf16[64,1280]{1,0:T(8,128)(2,1)S(1)}, u32[]{:S(2)}, u32[]{:S(2)}) collective-permute-start(bf16[64,1280]{1,0:T(8,128)(2,1)S(1)} %collective-permute-done.10.refs_10_.refs_3_), channel_id=1, source_target_pairs={{0,2},{2,6},{6,10},{10,14},{14,12},{12,8},{8,4},{4,0},{1,3},{3,7},... | collective-permute-start | bytes 491528 | tf_op jit(solution)/shard_map/ppermute | solution.py:381
  24.2 6.0 %collective-permute-start.13 = (bf16[64,1280]{1,0:T(8,128)(2,1)S(1)}, bf16[64,1280]{1,0:T(8,128)(2,1)S(1)}, u32[]{:S(2)}, u32[]{:S(2)}) collective-permute-start(bf16[64,1280]{1,0:T(8,128)(2,1)S(1)} %collective-permute-done.12.refs_8_.refs_6_), channel_id=1, source_target_pairs={{2,0},{6,2},{10,6},{14,10},{12,14},{8,12},{4,8},{0,4},{3,1},{7,3},... | collective-permute-start | bytes 491528 | tf_op jit(solution)/shard_map/ppermute | solution.py:387
  26.0 5.3 %collective-permute-start.6 = (bf16[64,1280]{1,0:T(8,128)(2,1)S(1)}, bf16[64,1280]{1,0:T(8,128)(2,1)S(1)}, u32[]{:S(2)}, u32[]{:S(2)}) collective-permute-start(bf16[64,1280]{1,0:T(8,128)(2,1)S(1)} %collective-permute-done.4.refs_3_), channel_id=1, source_target_pairs={{0,2},{2,6},{6,10},{10,14},{14,12},{12,8},{8,4},{4,0},{1,3},{3,7},... | collective-permute-start | bytes 491528 | tf_op jit(solution)/shard_map/ppermute | solution.py:386
  30.1 6.5 %collective-permute-start.19 = (f32[256,512]{1,0:T(8,128)S(1)}, f32[256,512]{1,0:T(8,128)S(1)}, u32[]{:S(2)}, u32[]{:S(2)}) collective-permute-start(f32[256,512]{1,0:T(8,128)S(1)} %get-tuple-element.42), channel_id=1, source_target_pairs={{0,1},{1,0},{2,3},{3,2},{4,5},{5,4},{6,7},{7,6},{8,9},{9,8},{10,11... | collective-permute-start | bytes 1572872 | tf_op jit(solution)/shard_map/ppermute | solution.py:403
  31.8 3.6 %collective-permute-start.17 = (bf16[128,128]{1,0:T(8,128)(2,1)S(1)}, bf16[128,128]{1,0:T(8,128)(2,1)S(1)}, u32[]{:S(2)}, u32[]{:S(2)}) collective-permute-start(bf16[128,128]{1,0:T(8,128)(2,1)S(1)} %shard_map.88), channel_id=1, source_target_pairs={{0,17},{1,16},{16,1},{17,0},{2,19},{3,18},{18,3},{19,2},{4,21},{5,... | collective-permute-start | bytes 98312 | tf_op jit(solution)/shard_map/ppermute | solution.py:409
  32.6 4.0 %collective-permute-start.18 = (bf16[128,128]{1,0:T(8,128)(2,1)S(1)}, bf16[128,128]{1,0:T(8,128)(2,1)S(1)}, u32[]{:S(2)}, u32[]{:S(2)}) collective-permute-start(bf16[128,128]{1,0:T(8,128)(2,1)S(1)} %shard_map.88), channel_id=1, source_target_pairs={{0,16},{16,0},{1,17},{17,1},{2,18},{18,2},{3,19},{19,3},{4,20},{20... | collective-permute-start | bytes 98312 | tf_op jit(solution)/shard_map/ppermute | solution.py:410
  33.8 2.8 %collective-permute-start.15 = (f32[64,128]{1,0:T(8,128)S(1)}, f32[64,128]{1,0:T(8,128)S(1)}, u32[]{:S(2)}, u32[]{:S(2)}) collective-permute-start(f32[64,128]{1,0:T(8,128)S(1)} %get-tuple-element.36.top), channel_id=1, source_target_pairs={{0,1},{1,0},{2,3},{3,2},{4,5},{5,4},{6,7},{7,6},{8,9},{9,8},{10,11... | collective-permute-start | bytes 98312 | tf_op jit(solution)/shard_map/ppermute | solution.py:411
  34.4 2.2 %collective-permute-start.16 = (f32[64,128]{1,0:T(8,128)S(1)}, f32[64,128]{1,0:T(8,128)S(1)}, u32[]{:S(2)}, u32[]{:S(2)}) collective-permute-start(f32[64,128]{1,0:T(8,128)S(1)} %get-tuple-element.37.low), channel_id=1, source_target_pairs={{0,1},{1,0},{2,3},{3,2},{4,5},{5,4},{6,7},{7,6},{8,9},{9,8},{10,11... | collective-permute-start | bytes 98312 | tf_op jit(solution)/shard_map/ppermute | solution.py:411

commit v28 on v27

--- a/solution.py
+++ b/solution.py
@@ -325,27 +325,27 @@
 
 
 def final_kernel(mask_ref, top, low, one_top, one_low, three, two, near_ref, far_ref, *refs):
-    factors, out_ref = refs[:-1], refs[-1]
+    factors, (out_ref, done, sems) = refs[:-3], refs[-3:]
     rank, width = factors[0].shape[0], out_ref.shape[1]
     begin = factors[0].shape[1] - width
     here = jnp.concatenate([top[...] + one_top[...], low[...] + one_low[...]], axis=0)
     packed = here + (two[...].astype(F32) + three[...].astype(F32))
     turned = pltpu.roll(packed, rank, 1)
     lane = lax.broadcasted_iota(I32, packed.shape, 1)
-    values = jnp.concatenate(
-        [jnp.where(lane < rank, packed, turned), jnp.where(lane < rank, turned, packed)], axis=0
-    )
-    wide = jnp.concatenate([values.astype(BF16)] * (GROUP // 2), axis=1)
-    total = None
-    for group in range(len(factors) // GROUP):
-        chosen = wide * mask_ref[:, group * GROUP * rank : (group + 1) * GROUP * rank]
-        factor = jnp.concatenate(
-            [ref[:, begin:] for ref in factors[group * GROUP : (group + 1) * GROUP]], axis=0
-        )
-        part = jnp.dot(chosen, factor, preferred_element_type=F32)
-        total = part if total is None else total + part
-    adapted = total.astype(BF16).astype(F32)
-    out_ref[...] = ((near_ref[...] + far_ref[...]) + adapted).astype(BF16)
+    factor = jnp.concatenate([ref[:, begin:] for ref in factors], axis=0)
+    half = packed.shape[0]
+    copies = []
+    for i in (0, 1):
+        values = jnp.where((lane < rank) == (i == 0), packed, turned).astype(BF16)
+        span = slice(i * half, (i + 1) * half)
+        chosen = jnp.concatenate([values] * (len(factors) // 2), axis=1) * mask_ref[span, :]
+        total = jnp.dot(chosen, factor, preferred_element_type=F32)
+        adapted = total.astype(BF16).astype(F32)
+        done[span, :] = ((near_ref[span, :] + far_ref[span, :]) + adapted).astype(BF16)
+        copies.append(pltpu.make_async_copy(done.at[span], out_ref.at[span], sems.at[i]))
+        copies[-1].start()
+    for copy in copies:
+        copy.wait()
 
 
 def per_device(hidden, demand, lengths, holder_slot, value_weight, factor_in, factor_out):
@@ -415,7 +415,8 @@
         final_kernel,
         out_shape=jax.ShapeDtypeStruct((rows, width), BF16),
         in_specs=[VMEM] * len(operands),
-        out_specs=VMEM,
+        out_specs=HBM,
+        scratch_shapes=[pltpu.VMEM((rows, width), BF16), pltpu.SemaphoreType.DMA((2,))],
         compiler_params=params(),
     )(*operands)
 

time: 37.8 us -> 37.7 us (level)
  no operation moved by 1% of the time
where the time goes in v28:
time: 37.7 us; the launch traced here: 37.6 us
  starting transfers between devices  19.7 us (52%)
  waiting for transfers between devices  11 us (29%)
  Pallas kernels  6.81 us (18%)
    ppermute x3, starting transfers between devices, per_device(): d = lax.ppermute(behind[1], 'batch', backward)  6.79 us
    ppermute x3, starting transfers between devices, per_device(): c = lax.ppermute(behind[0], 'batch', backward)  5.02 us
    ppermute x1, waiting for transfers between devices, per_device(): other = lax.ppermute(to_other, 'groups', swap)  3.05 us
    ppermute x3, waiting for transfers between devices, per_device(): c = lax.ppermute(behind[0], 'batch', backward)  2.91 us
    pallas_call x1, Pallas kernels, base_call(): pl.pallas_call(functools.partial(base_kernel, size), out_shape=(out, out,...  2.47 us
    ppermute x1, starting transfers between devices, per_device(): other = lax.ppermute(to_other, 'groups', swap)  2.03 us
    pallas_call x3, Pallas kernels, rank_call(): pl.pallas_call(functools.partial(rank_kernel, sides, groups, depth, last)...  1.84 us
    ppermute x3, waiting for transfers between devices, per_device(): d = lax.ppermute(behind[1], 'batch', backward)  1.81 us
  transfers between devices with their start and end apart: 20, of which 7 were waited for; matrix products, arithmetic and copies ran while one was open for 0% of the time, Pallas kernels for 12%

profile of v28, /device:TPU:0, one launch (start us, length us, event | category | flops | bytes accessed | tf_op | source)
XLA Modules:
  0.0 37.6 jit_solution(478624928138876831)
XLA Ops:
  0.0 1.2 %shard_map.82 = (bf16[64,1280]{1,0:T(8,128)(2,1)S(1)}, bf16[64,1280]{1,0:T(8,128)(2,1)S(1)}, s32[8,512]{1,0:T(8,128)S(1)}) custom-call(bf16[64,4096]{1,0:T(8,128)(2,1)} %bitcast.6, bf16[64,512]{1,0:T(8,128)(2,1)} %bitcast.7, s32[1,4]{1,0:T(1,128)} %demand_ref.1, s32[1,4]{1,0:T(1,128)} %lengths_ref.1, s32[8]{0:T(128)} %holder_ref.1, ...), custom_call_target="tpu_custom_call" | custom-call | flops 8589934592 | bytes 16777216 | tf_op jit(solution)/shard_map/pallas_call | solution.py:137
  1.2 3.1 %collective-permute-start.7 = (bf16[64,1280]{1,0:T(8,128)(2,1)S(1)}, bf16[64,1280]{1,0:T(8,128)(2,1)S(1)}, u32[]{:S(2)}, u32[]{:S(2)}) collective-permute-start(bf16[64,1280]{1,0:T(8,128)(2,1)S(1)} %get-tuple-element.33.refs_7_.refs_0_), channel_id=1, source_target_pairs={{2,0},{6,2},{10,6},{14,10},{12,14},{8,12},{4,8},{0,4},{3,1},{7,3},... | collective-permute-start | bytes 491528 | tf_op jit(solution)/shard_map/ppermute | solution.py:380
  4.3 0.0 collective-permute-start.2
  4.3 0.3 shard_map.83
  4.6 2.0 %collective-permute-start.14 = (bf16[4112,128]{1,0:T(8,128)(2,1)S(1)}, bf16[4112,128]{1,0:T(8,128)(2,1)S(1)}, u32[]{:S(2)}, u32[]{:S(2)}) collective-permute-start(bf16[4112,128]{1,0:T(8,128)(2,1)S(1)} %get-tuple-element.34), channel_id=1, source_target_pairs={{0,16},{16,0},{1,17},{17,1},{2,18},{18,2},{3,19},{19,3},{4,20},{20... | collective-permute-start | bytes 3158024 | tf_op jit(solution)/shard_map/ppermute | solution.py:390
  6.6 1.6 %collective-permute-start = (bf16[64,1280]{1,0:T(8,128)(2,1)S(1)}, bf16[64,1280]{1,0:T(8,128)(2,1)S(1)}, u32[]{:S(2)}, u32[]{:S(2)}) collective-permute-start(bf16[64,1280]{1,0:T(8,128)(2,1)S(1)} %get-tuple-element.32.refs_3_), channel_id=1, source_target_pairs={{2,0},{6,2},{10,6},{14,10},{12,14},{8,12},{4,8},{0,4},{3,1},{7,3},... | collective-permute-start | bytes 491528 | tf_op jit(solution)/shard_map/ppermute | solution.py:382
  8.2 0.4 %collective-permute-start.9 = (bf16[64,1280]{1,0:T(8,128)(2,1)S(1)}, bf16[64,1280]{1,0:T(8,128)(2,1)S(1)}, u32[]{:S(2)}, u32[]{:S(2)}) collective-permute-start(bf16[64,1280]{1,0:T(8,128)(2,1)S(1)} %get-tuple-element.33.refs_7_.refs_0_), channel_id=1, source_target_pairs={{0,2},{2,6},{6,10},{10,14},{14,12},{12,8},{8,4},{4,0},{1,3},{3,7},... | collective-permute-start | bytes 491528 | tf_op jit(solution)/shard_map/ppermute | solution.py:381
  8.6 0.0 collective-permute-done.7.refs_9_.refs_2_
  8.6 2.0 %collective-permute-start.8 = (bf16[64,1280]{1,0:T(8,128)(2,1)S(1)}, bf16[64,1280]{1,0:T(8,128)(2,1)S(1)}, u32[]{:S(2)}, u32[]{:S(2)}) collective-permute-start(bf16[64,1280]{1,0:T(8,128)(2,1)S(1)} %collective-permute-done.7.refs_9_.refs_2_), channel_id=1, source_target_pairs={{2,0},{6,2},{10,6},{14,10},{12,14},{8,12},{4,8},{0,4},{3,1},{7,3},... | collective-permute-start | bytes 491528 | tf_op jit(solution)/shard_map/ppermute | solution.py:380
  10.6 0.0 collective-permute-done.2.refs_4_
  10.6 0.1 collective-permute-start.3
  10.7 2.9 %collective-permute-done.refs_5_ = bf16[64,1280]{1,0:T(8,128)(2,1)S(1)} collective-permute-done((bf16[64,1280]{1,0:T(8,128)(2,1)S(1)}, bf16[64,1280]{1,0:T(8,128)(2,1)S(1)}, u32[]{:S(2)}, u32[]{:S(2)}) %collective-permute-start) | collective-permute-done | bytes 163872 | tf_op jit(solution)/shard_map/ppermute | solution.py:382
  13.6 1.7 %collective-permute-start.1 = (bf16[64,1280]{1,0:T(8,128)(2,1)S(1)}, bf16[64,1280]{1,0:T(8,128)(2,1)S(1)}, u32[]{:S(2)}, u32[]{:S(2)}) collective-permute-start(bf16[64,1280]{1,0:T(8,128)(2,1)S(1)} %collective-permute-done.refs_5_), channel_id=1, source_target_pairs={{2,0},{6,2},{10,6},{14,10},{12,14},{8,12},{4,8},{0,4},{3,1},{7,3},... | collective-permute-start | bytes 491528 | tf_op jit(solution)/shard_map/ppermute | solution.py:382
  15.3 0.0 collective-permute-done.9.refs_8_.refs_1_
  15.3 0.4 %collective-permute-start.10 = (bf16[64,1280]{1,0:T(8,128)(2,1)S(1)}, bf16[64,1280]{1,0:T(8,128)(2,1)S(1)}, u32[]{:S(2)}, u32[]{:S(2)}) collective-permute-start(bf16[64,1280]{1,0:T(8,128)(2,1)S(1)} %collective-permute-done.9.refs_8_.refs_1_), channel_id=1, source_target_pairs={{0,2},{2,6},{6,10},{10,14},{14,12},{12,8},{8,4},{4,0},{1,3},{3,7},... | collective-permute-start | bytes 491528 | tf_op jit(solution)/shard_map/ppermute | solution.py:381
  15.7 1.4 %collective-permute-done.8.refs_6_.refs_4_ = bf16[64,1280]{1,0:T(8,128)(2,1)S(1)} collective-permute-done((bf16[64,1280]{1,0:T(8,128)(2,1)S(1)}, bf16[64,1280]{1,0:T(8,128)(2,1)S(1)}, u32[]{:S(2)}, u32[]{:S(2)}) %collective-permute-start.8) | collective-permute-done | bytes 163872 | tf_op jit(solution)/shard_map/ppermute | solution.py:380
  17.1 1.7 %collective-permute-start.12 = (bf16[64,1280]{1,0:T(8,128)(2,1)S(1)}, bf16[64,1280]{1,0:T(8,128)(2,1)S(1)}, u32[]{:S(2)}, u32[]{:S(2)}) collective-permute-start(bf16[64,1280]{1,0:T(8,128)(2,1)S(1)} %collective-permute-done.8.refs_6_.refs_4_), channel_id=1, source_target_pairs={{2,0},{6,2},{10,6},{14,10},{12,14},{8,12},{4,8},{0,4},{3,1},{7,3},... | collective-permute-start | bytes 491528 | tf_op jit(solution)/shard_map/ppermute | solution.py:380
  18.8 0.0 collective-permute-done.3.refs_6_
  18.8 0.4 %collective-permute-start.4 = (bf16[64,1280]{1,0:T(8,128)(2,1)S(1)}, bf16[64,1280]{1,0:T(8,128)(2,1)S(1)}, u32[]{:S(2)}, u32[]{:S(2)}) collective-permute-start(bf16[64,1280]{1,0:T(8,128)(2,1)S(1)} %collective-permute-done.3.refs_6_), channel_id=1, source_target_pairs={{0,2},{2,6},{6,10},{10,14},{14,12},{12,8},{8,4},{4,0},{1,3},{3,7},... | collective-permute-start | bytes 491528 | tf_op jit(solution)/shard_map/ppermute | solution.py:379
  19.2 0.0 slice-done
  19.2 2.5 %shard_map.85 = (f32[256,512]{1,0:T(8,128)S(1)}, f32[256,512]{1,0:T(8,128)S(1)}, bf16[256,512]{1,0:T(8,128)(2,1)S(1)}) custom-call(bf16[256,4096]{1,0:T(8,128)(2,1)S(1)} %copy-done, bf16[4096,1024]{1,0:T(8,128)(2,1)S(1)} %bitcast.5, s32[8,512]{1,0:T(8,128)S(1)} %shard_map.84.bounds_ref.refs_2_.refs_1_), custom_call_target="tpu_custom_call" | custom-call | bytes 4194304 | tf_op jit(solution)/shard_map/pallas_call | solution.py:223
  21.7 0.0 collective-permute-done.1.refs_2_
  21.7 1.7 %collective-permute-start.5 = (bf16[64,1280]{1,0:T(8,128)(2,1)S(1)}, bf16[64,1280]{1,0:T(8,128)(2,1)S(1)}, u32[]{:S(2)}, u32[]{:S(2)}) collective-permute-start(bf16[64,1280]{1,0:T(8,128)(2,1)S(1)} %collective-permute-done.1.refs_2_), channel_id=1, source_target_pairs={{2,0},{6,2},{10,6},{14,10},{12,14},{8,12},{4,8},{0,4},{3,1},{7,3},... | collective-permute-start | bytes 491528 | tf_op jit(solution)/shard_map/ppermute | solution.py:382
  23.4 0.0 collective-permute-done.10.refs_10_.refs_3_
  23.4 0.4 %collective-permute-start.11 = (bf16[64,1280]{1,0:T(8,128)(2,1)S(1)}, bf16[64,1280]{1,0:T(8,128)(2,1)S(1)}, u32[]{:S(2)}, u32[]{:S(2)}) collective-permute-start(bf16[64,1280]{1,0:T(8,128)(2,1)S(1)} %collective-permute-done.10.refs_10_.refs_3_), channel_id=1, source_target_pairs={{0,2},{2,6},{6,10},{10,14},{14,12},{12,8},{8,4},{4,0},{1,3},{3,7},... | collective-permute-start | bytes 491528 | tf_op jit(solution)/shard_map/ppermute | solution.py:381
  23.8 0.4 %collective-permute-done.12.refs_8_.refs_6_ = bf16[64,1280]{1,0:T(8,128)(2,1)S(1)} collective-permute-done((bf16[64,1280]{1,0:T(8,128)(2,1)S(1)}, bf16[64,1280]{1,0:T(8,128)(2,1)S(1)}, u32[]{:S(2)}, u32[]{:S(2)}) %collective-permute-start.12) | collective-permute-done | bytes 163872 | tf_op jit(solution)/shard_map/ppermute | solution.py:380
  24.2 1.7 %collective-permute-start.13 = (bf16[64,1280]{1,0:T(8,128)(2,1)S(1)}, bf16[64,1280]{1,0:T(8,128)(2,1)S(1)}, u32[]{:S(2)}, u32[]{:S(2)}) collective-permute-start(bf16[64,1280]{1,0:T(8,128)(2,1)S(1)} %collective-permute-done.12.refs_8_.refs_6_), channel_id=1, source_target_pairs={{2,0},{6,2},{10,6},{14,10},{12,14},{8,12},{4,8},{0,4},{3,1},{7,3},... | collective-permute-start | bytes 491528 | tf_op jit(solution)/shard_map/ppermute | solution.py:387
  26.0 0.0 collective-permute-done.4.refs_3_
  26.0 0.3 collective-permute-start.6
  26.3 3.1 %collective-permute-done.14.refs_1_.refs_0_ = bf16[4112,128]{1,0:T(8,128)(2,1)S(1)} collective-permute-done((bf16[4112,128]{1,0:T(8,128)(2,1)S(1)}, bf16[4112,128]{1,0:T(8,128)(2,1)S(1)}, u32[]{:S(2)}, u32[]{:S(2)}) %collective-permute-start.14) | collective-permute-done | bytes 1052704 | tf_op jit(solution)/shard_map/ppermute | solution.py:390
  29.3 0.7 %shard_map.86 = (f32[256,128]{1,0:T(8,128)S(1)}, f32[256,128]{1,0:T(8,128)S(1)}) custom-call(bf16[256,4096]{1,0:T(8,128)(2,1)S(1)} %copy-done, bf16[4112,128]{1,0:T(8,128)(2,1)S(1)} %collective-permute-done.14.refs_1_.refs_0_, s32[8,512]{1,0:T(8,128)S(1)} %shard_map.84.bounds_ref.refs_2_.refs_1_, bf16[64,1280]{1,0:T(8,128)(2,1)S(1)} %get-tuple-element.32.refs_3_, ...), custom_call_target="tpu_custom_call" | custom-call | flops 8589934592 | bytes 16777216 | tf_op jit(solution)/shard_map/pallas_call | solution.py:317
  30.1 0.1 collective-permute-start.19
  30.2 0.0 collective-permute-done.5.refs_4_
  30.2 0.0 collective-permute-done.11.refs_7_.refs_5_
  30.2 0.0 collective-permute-done.13.refs_9_.refs_7_
  30.2 1.1 %collective-permute-done.6.refs_5_ = bf16[64,1280]{1,0:T(8,128)(2,1)S(1)} collective-permute-done((bf16[64,1280]{1,0:T(8,128)(2,1)S(1)}, bf16[64,1280]{1,0:T(8,128)(2,1)S(1)}, u32[]{:S(2)}, u32[]{:S(2)}) %collective-permute-start.6) | collective-permute-done | bytes 163872 | tf_op jit(solution)/shard_map/ppermute | solution.py:386
  31.3 0.5 %shard_map.88 = bf16[128,128]{1,0:T(8,128)(2,1)S(1)} custom-call(bf16[4112,128]{1,0:T(8,128)(2,1)S(1)} %collective-permute-done.14.refs_1_.refs_0_, s32[8,512]{1,0:T(8,128)S(1)} %shard_map.84.bounds_ref.refs_2_.refs_1_, bf16[64,1280]{1,0:T(8,128)(2,1)S(1)} %collective-permute-done.1.refs_2_, bf16[64,1280]{1,0:T(8,128)(2,1)S(1)} %collective-permute-done.4.refs_3_, ...), custom_call_target="tpu_custom_call" | custom-call | flops 8589934592 | bytes 16777216 | tf_op jit(solution)/shard_map/pallas_call | solution.py:317
  31.8 0.8 %collective-permute-start.17 = (bf16[128,128]{1,0:T(8,128)(2,1)S(1)}, bf16[128,128]{1,0:T(8,128)(2,1)S(1)}, u32[]{:S(2)}, u32[]{:S(2)}) collective-permute-start(bf16[128,128]{1,0:T(8,128)(2,1)S(1)} %shard_map.88), channel_id=1, source_target_pairs={{0,17},{1,16},{16,1},{17,0},{2,19},{3,18},{18,3},{19,2},{4,21},{5,... | collective-permute-start | bytes 98312 | tf_op jit(solution)/shard_map/ppermute | solution.py:409
  32.6 0.6 %collective-permute-start.18 = (bf16[128,128]{1,0:T(8,128)(2,1)S(1)}, bf16[128,128]{1,0:T(8,128)(2,1)S(1)}, u32[]{:S(2)}, u32[]{:S(2)}) collective-permute-start(bf16[128,128]{1,0:T(8,128)(2,1)S(1)} %shard_map.88), channel_id=1, source_target_pairs={{0,16},{16,0},{1,17},{17,1},{2,18},{18,2},{3,19},{19,3},{4,20},{20... | collective-permute-start | bytes 98312 | tf_op jit(solution)/shard_map/ppermute | solution.py:410
  33.2 0.5 %shard_map.87 = (f32[64,128]{1,0:T(8,128)S(1)}, f32[64,128]{1,0:T(8,128)S(1)}) custom-call(bf16[256,4096]{1,0:T(8,128)(2,1)S(1)} %copy-done, s32[8,512]{1,0:T(8,128)S(1)} %shard_map.84.bounds_ref.refs_2_.refs_1_, bf16[64,1280]{1,0:T(8,128)(2,1)S(1)} %collective-permute-done.1.refs_2_, bf16[64,1280]{1,0:T(8,128)(2,1)S(1)} %collective-permute-done.4.refs_3_, ...), custom_call_target="tpu_custom_call" | custom-call | bytes 4194304 | tf_op jit(solution)/shard_map/pallas_call | solution.py:317
  33.8 0.6 %collective-permute-start.15 = (f32[64,128]{1,0:T(8,128)S(1)}, f32[64,128]{1,0:T(8,128)S(1)}, u32[]{:S(2)}, u32[]{:S(2)}) collective-permute-start(f32[64,128]{1,0:T(8,128)S(1)} %get-tuple-element.36.top), channel_id=1, source_target_pairs={{0,1},{1,0},{2,3},{3,2},{4,5},{5,4},{6,7},{7,6},{8,9},{9,8},{10,11... | collective-permute-start | bytes 98312 | tf_op jit(solution)/shard_map/ppermute | solution.py:411
  34.4 0.1 collective-permute-start.16
  34.5 0.9 %collective-permute-done.17.three = bf16[128,128]{1,0:T(8,128)(2,1)S(1)} collective-permute-done((bf16[128,128]{1,0:T(8,128)(2,1)S(1)}, bf16[128,128]{1,0:T(8,128)(2,1)S(1)}, u32[]{:S(2)}, u32[]{:S(2)}) %collective-permute-start.17) | collective-permute-done | bytes 32800 | tf_op jit(solution)/shard_map/ppermute | solution.py:409
  35.4 1.2 %collective-permute-done.18.two = bf16[128,128]{1,0:T(8,128)(2,1)S(1)} collective-permute-done((bf16[128,128]{1,0:T(8,128)(2,1)S(1)}, bf16[128,128]{1,0:T(8,128)(2,1)S(1)}, u32[]{:S(2)}, u32[]{:S(2)}) %collective-permute-start.18) | collective-permute-done | bytes 32800 | tf_op jit(solution)/shard_map/ppermute | solution.py:410
  36.5 0.0 collective-permute-done.15.one_top
  36.6 0.0 collective-permute-done.16.one_low
  36.6 0.0 collective-permute-done.19.far_ref
  36.6 1.0 %shard_map.89 = bf16[256,512]{1,0:T(8,128)(2,1)} custom-call(bf16[256,512]{1,0:T(8,128)(2,1)S(1)} %get-tuple-element.28.mask_ref, f32[64,128]{1,0:T(8,128)S(1)} %get-tuple-element.36.top, f32[64,128]{1,0:T(8,128)S(1)} %get-tuple-element.37.low, f32[64,128]{1,0:T(8,128)S(1)} %collective-permute-done.15.one_top, ...), custom_call_target="tpu_custom_call" | custom-call | tf_op jit(solution)/shard_map/pallas_call | solution.py:414
  (7 shorter events, 0.0 us)
Async XLA Ops:
  0.0 4.3 %copy-start = (bf16[256,4096]{1,0:T(8,128)(2,1)S(1)}, bf16[256,4096]{1,0:T(8,128)(2,1)}, u32[]{:S(2)}) copy-start(bf16[256,4096]{1,0:T(8,128)(2,1)} %refs_0_.1) | copy-start | bytes 6291460
  1.2 7.4 %collective-permute-start.7 = (bf16[64,1280]{1,0:T(8,128)(2,1)S(1)}, bf16[64,1280]{1,0:T(8,128)(2,1)S(1)}, u32[]{:S(2)}, u32[]{:S(2)}) collective-permute-start(bf16[64,1280]{1,0:T(8,128)(2,1)S(1)} %get-tuple-element.33.refs_7_.refs_0_), channel_id=1, source_target_pairs={{2,0},{6,2},{10,6},{14,10},{12,14},{8,12},{4,8},{0,4},{3,1},{7,3},... | collective-permute-start | bytes 491528 | tf_op jit(solution)/shard_map/ppermute | solution.py:380
  4.3 6.3 %collective-permute-start.2 = (bf16[64,1280]{1,0:T(8,128)(2,1)S(1)}, bf16[64,1280]{1,0:T(8,128)(2,1)S(1)}, u32[]{:S(2)}, u32[]{:S(2)}) collective-permute-start(bf16[64,1280]{1,0:T(8,128)(2,1)S(1)} %get-tuple-element.32.refs_3_), channel_id=1, source_target_pairs={{0,2},{2,6},{6,10},{10,14},{14,12},{12,8},{8,4},{4,0},{1,3},{3,7},... | collective-permute-start | bytes 491528 | tf_op jit(solution)/shard_map/ppermute | solution.py:379
  4.6 24.8 %collective-permute-start.14 = (bf16[4112,128]{1,0:T(8,128)(2,1)S(1)}, bf16[4112,128]{1,0:T(8,128)(2,1)S(1)}, u32[]{:S(2)}, u32[]{:S(2)}) collective-permute-start(bf16[4112,128]{1,0:T(8,128)(2,1)S(1)} %get-tuple-element.34), channel_id=1, source_target_pairs={{0,16},{16,0},{1,17},{17,1},{2,18},{18,2},{3,19},{19,3},{4,20},{20... | collective-permute-start | bytes 3158024 | tf_op jit(solution)/shard_map/ppermute | solution.py:390
  6.6 12.6 %slice-start = ((s8[8388608]{0:T(1024)(128)(4,1)}), s8[4194304]{0:T(1024)(128)(4,1)S(1)}, s32[]{:S(2)}) async-start(s8[8388608]{0:T(1024)(128)(4,1)} %bitcast.4), calls=%async_computation | async-start | bytes 8388608
  6.6 12.6 %slice-start.1 = ((s8[8388608]{0:T(1024)(128)(4,1)}), s8[4194304]{0:T(1024)(128)(4,1)S(1)}, s32[]{:S(2)}) async-start(s8[8388608]{0:T(1024)(128)(4,1)} %bitcast.4), calls=%async_computation.1 | async-start | bytes 8388608
  6.6 7.0 %collective-permute-start = (bf16[64,1280]{1,0:T(8,128)(2,1)S(1)}, bf16[64,1280]{1,0:T(8,128)(2,1)S(1)}, u32[]{:S(2)}, u32[]{:S(2)}) collective-permute-start(bf16[64,1280]{1,0:T(8,128)(2,1)S(1)} %get-tuple-element.32.refs_3_), channel_id=1, source_target_pairs={{2,0},{6,2},{10,6},{14,10},{12,14},{8,12},{4,8},{0,4},{3,1},{7,3},... | collective-permute-start | bytes 491528 | tf_op jit(solution)/shard_map/ppermute | solution.py:382
  8.2 7.1 %collective-permute-start.9 = (bf16[64,1280]{1,0:T(8,128)(2,1)S(1)}, bf16[64,1280]{1,0:T(8,128)(2,1)S(1)}, u32[]{:S(2)}, u32[]{:S(2)}) collective-permute-start(bf16[64,1280]{1,0:T(8,128)(2,1)S(1)} %get-tuple-element.33.refs_7_.refs_0_), channel_id=1, source_target_pairs={{0,2},{2,6},{6,10},{10,14},{14,12},{12,8},{8,4},{4,0},{1,3},{3,7},... | collective-permute-start | bytes 491528 | tf_op jit(solution)/shard_map/ppermute | solution.py:381
  8.6 8.5 %collective-permute-start.8 = (bf16[64,1280]{1,0:T(8,128)(2,1)S(1)}, bf16[64,1280]{1,0:T(8,128)(2,1)S(1)}, u32[]{:S(2)}, u32[]{:S(2)}) collective-permute-start(bf16[64,1280]{1,0:T(8,128)(2,1)S(1)} %collective-permute-done.7.refs_9_.refs_2_), channel_id=1, source_target_pairs={{2,0},{6,2},{10,6},{14,10},{12,14},{8,12},{4,8},{0,4},{3,1},{7,3},... | collective-permute-start | bytes 491528 | tf_op jit(solution)/shard_map/ppermute | solution.py:380
  10.6 8.2 %collective-permute-start.3 = (bf16[64,1280]{1,0:T(8,128)(2,1)S(1)}, bf16[64,1280]{1,0:T(8,128)(2,1)S(1)}, u32[]{:S(2)}, u32[]{:S(2)}) collective-permute-start(bf16[64,1280]{1,0:T(8,128)(2,1)S(1)} %collective-permute-done.2.refs_4_), channel_id=1, source_target_pairs={{0,2},{2,6},{6,10},{10,14},{14,12},{12,8},{8,4},{4,0},{1,3},{3,7},... | collective-permute-start | bytes 491528 | tf_op jit(solution)/shard_map/ppermute | solution.py:379
  13.6 8.1 %collective-permute-start.1 = (bf16[64,1280]{1,0:T(8,128)(2,1)S(1)}, bf16[64,1280]{1,0:T(8,128)(2,1)S(1)}, u32[]{:S(2)}, u32[]{:S(2)}) collective-permute-start(bf16[64,1280]{1,0:T(8,128)(2,1)S(1)} %collective-permute-done.refs_5_), channel_id=1, source_target_pairs={{2,0},{6,2},{10,6},{14,10},{12,14},{8,12},{4,8},{0,4},{3,1},{7,3},... | collective-permute-start | bytes 491528 | tf_op jit(solution)/shard_map/ppermute | solution.py:382
  15.3 8.1 %collective-permute-start.10 = (bf16[64,1280]{1,0:T(8,128)(2,1)S(1)}, bf16[64,1280]{1,0:T(8,128)(2,1)S(1)}, u32[]{:S(2)}, u32[]{:S(2)}) collective-permute-start(bf16[64,1280]{1,0:T(8,128)(2,1)S(1)} %collective-permute-done.9.refs_8_.refs_1_), channel_id=1, source_target_pairs={{0,2},{2,6},{6,10},{10,14},{14,12},{12,8},{8,4},{4,0},{1,3},{3,7},... | collective-permute-start | bytes 491528 | tf_op jit(solution)/shard_map/ppermute | solution.py:381
  17.1 7.1 %collective-permute-start.12 = (bf16[64,1280]{1,0:T(8,128)(2,1)S(1)}, bf16[64,1280]{1,0:T(8,128)(2,1)S(1)}, u32[]{:S(2)}, u32[]{:S(2)}) collective-permute-start(bf16[64,1280]{1,0:T(8,128)(2,1)S(1)} %collective-permute-done.8.refs_6_.refs_4_), channel_id=1, source_target_pairs={{2,0},{6,2},{10,6},{14,10},{12,14},{8,12},{4,8},{0,4},{3,1},{7,3},... | collective-permute-start | bytes 491528 | tf_op jit(solution)/shard_map/ppermute | solution.py:380
  18.8 7.1 %collective-permute-start.4 = (bf16[64,1280]{1,0:T(8,128)(2,1)S(1)}, bf16[64,1280]{1,0:T(8,128)(2,1)S(1)}, u32[]{:S(2)}, u32[]{:S(2)}) collective-permute-start(bf16[64,1280]{1,0:T(8,128)(2,1)S(1)} %collective-permute-done.3.refs_6_), channel_id=1, source_target_pairs={{0,2},{2,6},{6,10},{10,14},{14,12},{12,8},{8,4},{4,0},{1,3},{3,7},... | collective-permute-start | bytes 491528 | tf_op jit(solution)/shard_map/ppermute | solution.py:379
  21.7 8.5 %collective-permute-start.5 = (bf16[64,1280]{1,0:T(8,128)(2,1)S(1)}, bf16[64,1280]{1,0:T(8,128)(2,1)S(1)}, u32[]{:S(2)}, u32[]{:S(2)}) collective-permute-start(bf16[64,1280]{1,0:T(8,128)(2,1)S(1)} %collective-permute-done.1.refs_2_), channel_id=1, source_target_pairs={{2,0},{6,2},{10,6},{14,10},{12,14},{8,12},{4,8},{0,4},{3,1},{7,3},... | collective-permute-start | bytes 491528 | tf_op jit(solution)/shard_map/ppermute | solution.py:382
  23.4 6.8 %collective-permute-start.11 = (bf16[64,1280]{1,0:T(8,128)(2,1)S(1)}, bf16[64,1280]{1,0:T(8,128)(2,1)S(1)}, u32[]{:S(2)}, u32[]{:S(2)}) collective-permute-start(bf16[64,1280]{1,0:T(8,128)(2,1)S(1)} %collective-permute-done.10.refs_10_.refs_3_), channel_id=1, source_target_pairs={{0,2},{2,6},{6,10},{10,14},{14,12},{12,8},{8,4},{4,0},{1,3},{3,7},... | collective-permute-start | bytes 491528 | tf_op jit(solution)/shard_map/ppermute | solution.py:381
  24.2 6.0 %collective-permute-start.13 = (bf16[64,1280]{1,0:T(8,128)(2,1)S(1)}, bf16[64,1280]{1,0:T(8,128)(2,1)S(1)}, u32[]{:S(2)}, u32[]{:S(2)}) collective-permute-start(bf16[64,1280]{1,0:T(8,128)(2,1)S(1)} %collective-permute-done.12.refs_8_.refs_6_), channel_id=1, source_target_pairs={{2,0},{6,2},{10,6},{14,10},{12,14},{8,12},{4,8},{0,4},{3,1},{7,3},... | collective-permute-start | bytes 491528 | tf_op jit(solution)/shard_map/ppermute | solution.py:387
  26.0 5.3 %collective-permute-start.6 = (bf16[64,1280]{1,0:T(8,128)(2,1)S(1)}, bf16[64,1280]{1,0:T(8,128)(2,1)S(1)}, u32[]{:S(2)}, u32[]{:S(2)}) collective-permute-start(bf16[64,1280]{1,0:T(8,128)(2,1)S(1)} %collective-permute-done.4.refs_3_), channel_id=1, source_target_pairs={{0,2},{2,6},{6,10},{10,14},{14,12},{12,8},{8,4},{4,0},{1,3},{3,7},... | collective-permute-start | bytes 491528 | tf_op jit(solution)/shard_map/ppermute | solution.py:386
  30.1 6.5 %collective-permute-start.19 = (f32[256,512]{1,0:T(8,128)S(1)}, f32[256,512]{1,0:T(8,128)S(1)}, u32[]{:S(2)}, u32[]{:S(2)}) collective-permute-start(f32[256,512]{1,0:T(8,128)S(1)} %get-tuple-element.42), channel_id=1, source_target_pairs={{0,1},{1,0},{2,3},{3,2},{4,5},{5,4},{6,7},{7,6},{8,9},{9,8},{10,11... | collective-permute-start | bytes 1572872 | tf_op jit(solution)/shard_map/ppermute | solution.py:403
  31.8 3.6 %collective-permute-start.17 = (bf16[128,128]{1,0:T(8,128)(2,1)S(1)}, bf16[128,128]{1,0:T(8,128)(2,1)S(1)}, u32[]{:S(2)}, u32[]{:S(2)}) collective-permute-start(bf16[128,128]{1,0:T(8,128)(2,1)S(1)} %shard_map.88), channel_id=1, source_target_pairs={{0,17},{1,16},{16,1},{17,0},{2,19},{3,18},{18,3},{19,2},{4,21},{5,... | collective-permute-start | bytes 98312 | tf_op jit(solution)/shard_map/ppermute | solution.py:409
  32.6 4.0 %collective-permute-start.18 = (bf16[128,128]{1,0:T(8,128)(2,1)S(1)}, bf16[128,128]{1,0:T(8,128)(2,1)S(1)}, u32[]{:S(2)}, u32[]{:S(2)}) collective-permute-start(bf16[128,128]{1,0:T(8,128)(2,1)S(1)} %shard_map.88), channel_id=1, source_target_pairs={{0,16},{16,0},{1,17},{17,1},{2,18},{18,2},{3,19},{19,3},{4,20},{20... | collective-permute-start | bytes 98312 | tf_op jit(solution)/shard_map/ppermute | solution.py:410
  33.8 2.8 %collective-permute-start.15 = (f32[64,128]{1,0:T(8,128)S(1)}, f32[64,128]{1,0:T(8,128)S(1)}, u32[]{:S(2)}, u32[]{:S(2)}) collective-permute-start(f32[64,128]{1,0:T(8,128)S(1)} %get-tuple-element.36.top), channel_id=1, source_target_pairs={{0,1},{1,0},{2,3},{3,2},{4,5},{5,4},{6,7},{7,6},{8,9},{9,8},{10,11... | collective-permute-start | bytes 98312 | tf_op jit(solution)/shard_map/ppermute | solution.py:411
  34.4 2.2 %collective-permute-start.16 = (f32[64,128]{1,0:T(8,128)S(1)}, f32[64,128]{1,0:T(8,128)S(1)}, u32[]{:S(2)}, u32[]{:S(2)}) collective-permute-start(f32[64,128]{1,0:T(8,128)S(1)} %get-tuple-element.37.low), channel_id=1, source_target_pairs={{0,1},{1,0},{2,3},{3,2},{4,5},{5,4},{6,7},{7,6},{8,9},{9,8},{10,11... | collective-permute-start | bytes 98312 | tf_op jit(solution)/shard_map/ppermute | solution.py:411

commit v29 on v28

--- a/solution.py
+++ b/solution.py
@@ -324,7 +324,7 @@
     )(*operands)
 
 
-def final_kernel(mask_ref, top, low, one_top, one_low, three, two, near_ref, far_ref, *refs):
+def final_kernel(mask_ref, top, low, one_top, one_low, two, three, near_ref, far_ref, *refs):
     factors, (out_ref, done, sems) = refs[:-3], refs[-3:]
     rank, width = factors[0].shape[0], out_ref.shape[1]
     begin = factors[0].shape[1] - width
@@ -410,7 +410,7 @@
     two = lax.ppermute(theirs, "groups", swap)
     one = [lax.ppermute(part, "tensor", swap) for part in mine]
 
-    operands = [mask, *mine, *one, three, two, near, far, *seconds]
+    operands = [mask, *mine, *one, two, three, near, far, *seconds]
     return pl.pallas_call(
         final_kernel,
         out_shape=jax.ShapeDtypeStruct((rows, width), BF16),

time: 37.7 us -> 37.8 us (level)
    ppermute x1, starting transfers between devices: 0.76 us -> 0.01 us  [per_device(): lax.ppermute(theirs, ('groups', 'tensor'), [(0, 3), (1, 2), (2, 1), (3, 0)])]
    ppermute x1, starting transfers between devices: 0.63 us -> 1.31 us  [per_device(): two = lax.ppermute(theirs, 'groups', swap)]
where the time goes in v29:
time: 37.8 us; the launch traced here: 37.6 us
  starting transfers between devices  20 us (53%)
  waiting for transfers between devices  10.7 us (28%)
  Pallas kernels  6.81 us (18%)
    ppermute x3, starting transfers between devices, per_device(): d = lax.ppermute(behind[1], 'batch', backward)  6.79 us
    ppermute x3, starting transfers between devices, per_device(): c = lax.ppermute(behind[0], 'batch', backward)  5.02 us
    ppermute x1, waiting for transfers between devices, per_device(): other = lax.ppermute(to_other, 'groups', swap)  3.05 us
    ppermute x3, waiting for transfers between devices, per_device(): c = lax.ppermute(behind[0], 'batch', backward)  2.91 us
    pallas_call x1, Pallas kernels, base_call(): pl.pallas_call(functools.partial(base_kernel, size), out_shape=(out, out,...  2.47 us
    ppermute x1, starting transfers between devices, per_device(): other = lax.ppermute(to_other, 'groups', swap)  2.03 us
    pallas_call x3, Pallas kernels, rank_call(): pl.pallas_call(functools.partial(rank_kernel, sides, groups, depth, last)...  1.84 us
    ppermute x3, waiting for transfers between devices, per_device(): d = lax.ppermute(behind[1], 'batch', backward)  1.81 us
  transfers between devices with their start and end apart: 20, of which 7 were waited for; matrix products, arithmetic and copies ran while one was open for 0% of the time, Pallas kernels for 12%

profile of v29, /device:TPU:0, one launch (start us, length us, event | category | flops | bytes accessed | tf_op | source)
XLA Modules:
  0.0 37.6 jit_solution(6963052186088139812)
XLA Ops:
  0.0 1.2 %shard_map.82 = (bf16[64,1280]{1,0:T(8,128)(2,1)S(1)}, bf16[64,1280]{1,0:T(8,128)(2,1)S(1)}, s32[8,512]{1,0:T(8,128)S(1)}) custom-call(bf16[64,4096]{1,0:T(8,128)(2,1)} %bitcast.6, bf16[64,512]{1,0:T(8,128)(2,1)} %bitcast.7, s32[1,4]{1,0:T(1,128)} %demand_ref.1, s32[1,4]{1,0:T(1,128)} %lengths_ref.1, s32[8]{0:T(128)} %holder_ref.1, ...), custom_call_target="tpu_custom_call" | custom-call | flops 8589934592 | bytes 16777216 | tf_op jit(solution)/shard_map/pallas_call | solution.py:137
  1.2 3.1 %collective-permute-start.7 = (bf16[64,1280]{1,0:T(8,128)(2,1)S(1)}, bf16[64,1280]{1,0:T(8,128)(2,1)S(1)}, u32[]{:S(2)}, u32[]{:S(2)}) collective-permute-start(bf16[64,1280]{1,0:T(8,128)(2,1)S(1)} %get-tuple-element.33.refs_7_.refs_0_), channel_id=1, source_target_pairs={{2,0},{6,2},{10,6},{14,10},{12,14},{8,12},{4,8},{0,4},{3,1},{7,3},... | collective-permute-start | bytes 491528 | tf_op jit(solution)/shard_map/ppermute | solution.py:380
  4.3 0.0 collective-permute-start.2
  4.3 0.0 copy-done
  4.3 0.3 shard_map.83
  4.6 2.0 %collective-permute-start.14 = (bf16[4112,128]{1,0:T(8,128)(2,1)S(1)}, bf16[4112,128]{1,0:T(8,128)(2,1)S(1)}, u32[]{:S(2)}, u32[]{:S(2)}) collective-permute-start(bf16[4112,128]{1,0:T(8,128)(2,1)S(1)} %get-tuple-element.34), channel_id=1, source_target_pairs={{0,16},{16,0},{1,17},{17,1},{2,18},{18,2},{3,19},{19,3},{4,20},{20... | collective-permute-start | bytes 3158024 | tf_op jit(solution)/shard_map/ppermute | solution.py:390
  6.6 1.6 %collective-permute-start = (bf16[64,1280]{1,0:T(8,128)(2,1)S(1)}, bf16[64,1280]{1,0:T(8,128)(2,1)S(1)}, u32[]{:S(2)}, u32[]{:S(2)}) collective-permute-start(bf16[64,1280]{1,0:T(8,128)(2,1)S(1)} %get-tuple-element.32.refs_3_), channel_id=1, source_target_pairs={{2,0},{6,2},{10,6},{14,10},{12,14},{8,12},{4,8},{0,4},{3,1},{7,3},... | collective-permute-start | bytes 491528 | tf_op jit(solution)/shard_map/ppermute | solution.py:382
  8.2 0.4 %collective-permute-start.9 = (bf16[64,1280]{1,0:T(8,128)(2,1)S(1)}, bf16[64,1280]{1,0:T(8,128)(2,1)S(1)}, u32[]{:S(2)}, u32[]{:S(2)}) collective-permute-start(bf16[64,1280]{1,0:T(8,128)(2,1)S(1)} %get-tuple-element.33.refs_7_.refs_0_), channel_id=1, source_target_pairs={{0,2},{2,6},{6,10},{10,14},{14,12},{12,8},{8,4},{4,0},{1,3},{3,7},... | collective-permute-start | bytes 491528 | tf_op jit(solution)/shard_map/ppermute | solution.py:381
  8.6 0.0 collective-permute-done.7.refs_9_.refs_2_
  8.6 2.0 %collective-permute-start.8 = (bf16[64,1280]{1,0:T(8,128)(2,1)S(1)}, bf16[64,1280]{1,0:T(8,128)(2,1)S(1)}, u32[]{:S(2)}, u32[]{:S(2)}) collective-permute-start(bf16[64,1280]{1,0:T(8,128)(2,1)S(1)} %collective-permute-done.7.refs_9_.refs_2_), channel_id=1, source_target_pairs={{2,0},{6,2},{10,6},{14,10},{12,14},{8,12},{4,8},{0,4},{3,1},{7,3},... | collective-permute-start | bytes 491528 | tf_op jit(solution)/shard_map/ppermute | solution.py:380
  10.6 0.0 collective-permute-done.2.refs_4_
  10.6 0.1 collective-permute-start.3
  10.7 2.9 %collective-permute-done.refs_5_ = bf16[64,1280]{1,0:T(8,128)(2,1)S(1)} collective-permute-done((bf16[64,1280]{1,0:T(8,128)(2,1)S(1)}, bf16[64,1280]{1,0:T(8,128)(2,1)S(1)}, u32[]{:S(2)}, u32[]{:S(2)}) %collective-permute-start) | collective-permute-done | bytes 163872 | tf_op jit(solution)/shard_map/ppermute | solution.py:382
  13.6 1.7 %collective-permute-start.1 = (bf16[64,1280]{1,0:T(8,128)(2,1)S(1)}, bf16[64,1280]{1,0:T(8,128)(2,1)S(1)}, u32[]{:S(2)}, u32[]{:S(2)}) collective-permute-start(bf16[64,1280]{1,0:T(8,128)(2,1)S(1)} %collective-permute-done.refs_5_), channel_id=1, source_target_pairs={{2,0},{6,2},{10,6},{14,10},{12,14},{8,12},{4,8},{0,4},{3,1},{7,3},... | collective-permute-start | bytes 491528 | tf_op jit(solution)/shard_map/ppermute | solution.py:382
  15.3 0.0 collective-permute-done.9.refs_8_.refs_1_
  15.3 0.4 %collective-permute-start.10 = (bf16[64,1280]{1,0:T(8,128)(2,1)S(1)}, bf16[64,1280]{1,0:T(8,128)(2,1)S(1)}, u32[]{:S(2)}, u32[]{:S(2)}) collective-permute-start(bf16[64,1280]{1,0:T(8,128)(2,1)S(1)} %collective-permute-done.9.refs_8_.refs_1_), channel_id=1, source_target_pairs={{0,2},{2,6},{6,10},{10,14},{14,12},{12,8},{8,4},{4,0},{1,3},{3,7},... | collective-permute-start | bytes 491528 | tf_op jit(solution)/shard_map/ppermute | solution.py:381
  15.7 1.4 %collective-permute-done.8.refs_6_.refs_4_ = bf16[64,1280]{1,0:T(8,128)(2,1)S(1)} collective-permute-done((bf16[64,1280]{1,0:T(8,128)(2,1)S(1)}, bf16[64,1280]{1,0:T(8,128)(2,1)S(1)}, u32[]{:S(2)}, u32[]{:S(2)}) %collective-permute-start.8) | collective-permute-done | bytes 163872 | tf_op jit(solution)/shard_map/ppermute | solution.py:380
  17.1 1.7 %collective-permute-start.12 = (bf16[64,1280]{1,0:T(8,128)(2,1)S(1)}, bf16[64,1280]{1,0:T(8,128)(2,1)S(1)}, u32[]{:S(2)}, u32[]{:S(2)}) collective-permute-start(bf16[64,1280]{1,0:T(8,128)(2,1)S(1)} %collective-permute-done.8.refs_6_.refs_4_), channel_id=1, source_target_pairs={{2,0},{6,2},{10,6},{14,10},{12,14},{8,12},{4,8},{0,4},{3,1},{7,3},... | collective-permute-start | bytes 491528 | tf_op jit(solution)/shard_map/ppermute | solution.py:380
  18.8 0.0 collective-permute-done.3.refs_6_
  18.8 0.4 %collective-permute-start.4 = (bf16[64,1280]{1,0:T(8,128)(2,1)S(1)}, bf16[64,1280]{1,0:T(8,128)(2,1)S(1)}, u32[]{:S(2)}, u32[]{:S(2)}) collective-permute-start(bf16[64,1280]{1,0:T(8,128)(2,1)S(1)} %collective-permute-done.3.refs_6_), channel_id=1, source_target_pairs={{0,2},{2,6},{6,10},{10,14},{14,12},{12,8},{8,4},{4,0},{1,3},{3,7},... | collective-permute-start | bytes 491528 | tf_op jit(solution)/shard_map/ppermute | solution.py:379
  19.2 2.5 %shard_map.85 = (f32[256,512]{1,0:T(8,128)S(1)}, f32[256,512]{1,0:T(8,128)S(1)}, bf16[256,512]{1,0:T(8,128)(2,1)S(1)}) custom-call(bf16[256,4096]{1,0:T(8,128)(2,1)S(1)} %copy-done, bf16[4096,1024]{1,0:T(8,128)(2,1)S(1)} %bitcast.5, s32[8,512]{1,0:T(8,128)S(1)} %shard_map.84.bounds_ref.refs_2_.refs_1_), custom_call_target="tpu_custom_call" | custom-call | bytes 4194304 | tf_op jit(solution)/shard_map/pallas_call | solution.py:223
  21.7 0.0 collective-permute-done.1.refs_2_
  21.7 1.7 %collective-permute-start.5 = (bf16[64,1280]{1,0:T(8,128)(2,1)S(1)}, bf16[64,1280]{1,0:T(8,128)(2,1)S(1)}, u32[]{:S(2)}, u32[]{:S(2)}) collective-permute-start(bf16[64,1280]{1,0:T(8,128)(2,1)S(1)} %collective-permute-done.1.refs_2_), channel_id=1, source_target_pairs={{2,0},{6,2},{10,6},{14,10},{12,14},{8,12},{4,8},{0,4},{3,1},{7,3},... | collective-permute-start | bytes 491528 | tf_op jit(solution)/shard_map/ppermute | solution.py:382
  23.4 0.0 collective-permute-done.10.refs_10_.refs_3_
  23.4 0.4 %collective-permute-start.11 = (bf16[64,1280]{1,0:T(8,128)(2,1)S(1)}, bf16[64,1280]{1,0:T(8,128)(2,1)S(1)}, u32[]{:S(2)}, u32[]{:S(2)}) collective-permute-start(bf16[64,1280]{1,0:T(8,128)(2,1)S(1)} %collective-permute-done.10.refs_10_.refs_3_), channel_id=1, source_target_pairs={{0,2},{2,6},{6,10},{10,14},{14,12},{12,8},{8,4},{4,0},{1,3},{3,7},... | collective-permute-start | bytes 491528 | tf_op jit(solution)/shard_map/ppermute | solution.py:381
  23.8 0.4 %collective-permute-done.12.refs_8_.refs_6_ = bf16[64,1280]{1,0:T(8,128)(2,1)S(1)} collective-permute-done((bf16[64,1280]{1,0:T(8,128)(2,1)S(1)}, bf16[64,1280]{1,0:T(8,128)(2,1)S(1)}, u32[]{:S(2)}, u32[]{:S(2)}) %collective-permute-start.12) | collective-permute-done | bytes 163872 | tf_op jit(solution)/shard_map/ppermute | solution.py:380
  24.2 1.7 %collective-permute-start.13 = (bf16[64,1280]{1,0:T(8,128)(2,1)S(1)}, bf16[64,1280]{1,0:T(8,128)(2,1)S(1)}, u32[]{:S(2)}, u32[]{:S(2)}) collective-permute-start(bf16[64,1280]{1,0:T(8,128)(2,1)S(1)} %collective-permute-done.12.refs_8_.refs_6_), channel_id=1, source_target_pairs={{2,0},{6,2},{10,6},{14,10},{12,14},{8,12},{4,8},{0,4},{3,1},{7,3},... | collective-permute-start | bytes 491528 | tf_op jit(solution)/shard_map/ppermute | solution.py:387
  26.0 0.0 collective-permute-done.4.refs_3_
  26.0 0.3 collective-permute-start.6
  26.3 3.1 %collective-permute-done.14.refs_1_.refs_0_ = bf16[4112,128]{1,0:T(8,128)(2,1)S(1)} collective-permute-done((bf16[4112,128]{1,0:T(8,128)(2,1)S(1)}, bf16[4112,128]{1,0:T(8,128)(2,1)S(1)}, u32[]{:S(2)}, u32[]{:S(2)}) %collective-permute-start.14) | collective-permute-done | bytes 1052704 | tf_op jit(solution)/shard_map/ppermute | solution.py:390
  29.3 0.7 %shard_map.86 = (f32[256,128]{1,0:T(8,128)S(1)}, f32[256,128]{1,0:T(8,128)S(1)}) custom-call(bf16[256,4096]{1,0:T(8,128)(2,1)S(1)} %copy-done, bf16[4112,128]{1,0:T(8,128)(2,1)S(1)} %collective-permute-done.14.refs_1_.refs_0_, s32[8,512]{1,0:T(8,128)S(1)} %shard_map.84.bounds_ref.refs_2_.refs_1_, bf16[64,1280]{1,0:T(8,128)(2,1)S(1)} %get-tuple-element.32.refs_3_, ...), custom_call_target="tpu_custom_call" | custom-call | flops 8589934592 | bytes 16777216 | tf_op jit(solution)/shard_map/pallas_call | solution.py:317
  30.1 0.1 collective-permute-start.19
  30.2 0.0 collective-permute-done.5.refs_4_
  30.2 0.0 collective-permute-done.11.refs_7_.refs_5_
  30.2 0.0 collective-permute-done.13.refs_9_.refs_7_
  30.2 1.1 %collective-permute-done.6.refs_5_ = bf16[64,1280]{1,0:T(8,128)(2,1)S(1)} collective-permute-done((bf16[64,1280]{1,0:T(8,128)(2,1)S(1)}, bf16[64,1280]{1,0:T(8,128)(2,1)S(1)}, u32[]{:S(2)}, u32[]{:S(2)}) %collective-permute-start.6) | collective-permute-done | bytes 163872 | tf_op jit(solution)/shard_map/ppermute | solution.py:386
  31.3 0.5 %shard_map.88 = bf16[128,128]{1,0:T(8,128)(2,1)S(1)} custom-call(bf16[4112,128]{1,0:T(8,128)(2,1)S(1)} %collective-permute-done.14.refs_1_.refs_0_, s32[8,512]{1,0:T(8,128)S(1)} %shard_map.84.bounds_ref.refs_2_.refs_1_, bf16[64,1280]{1,0:T(8,128)(2,1)S(1)} %collective-permute-done.1.refs_2_, bf16[64,1280]{1,0:T(8,128)(2,1)S(1)} %collective-permute-done.4.refs_3_, ...), custom_call_target="tpu_custom_call" | custom-call | flops 8589934592 | bytes 16777216 | tf_op jit(solution)/shard_map/pallas_call | solution.py:317
  31.8 1.3 %collective-permute-start.17 = (bf16[128,128]{1,0:T(8,128)(2,1)S(1)}, bf16[128,128]{1,0:T(8,128)(2,1)S(1)}, u32[]{:S(2)}, u32[]{:S(2)}) collective-permute-start(bf16[128,128]{1,0:T(8,128)(2,1)S(1)} %shard_map.88), channel_id=1, source_target_pairs={{0,16},{16,0},{1,17},{17,1},{2,18},{18,2},{3,19},{19,3},{4,20},{20... | collective-permute-start | bytes 98312 | tf_op jit(solution)/shard_map/ppermute | solution.py:410
  33.1 0.0 collective-permute-start.18
  33.1 0.5 %shard_map.87 = (f32[64,128]{1,0:T(8,128)S(1)}, f32[64,128]{1,0:T(8,128)S(1)}) custom-call(bf16[256,4096]{1,0:T(8,128)(2,1)S(1)} %copy-done, s32[8,512]{1,0:T(8,128)S(1)} %shard_map.84.bounds_ref.refs_2_.refs_1_, bf16[64,1280]{1,0:T(8,128)(2,1)S(1)} %collective-permute-done.1.refs_2_, bf16[64,1280]{1,0:T(8,128)(2,1)S(1)} %collective-permute-done.4.refs_3_, ...), custom_call_target="tpu_custom_call" | custom-call | bytes 4194304 | tf_op jit(solution)/shard_map/pallas_call | solution.py:317
  33.7 1.0 %collective-permute-start.15 = (f32[64,128]{1,0:T(8,128)S(1)}, f32[64,128]{1,0:T(8,128)S(1)}, u32[]{:S(2)}, u32[]{:S(2)}) collective-permute-start(f32[64,128]{1,0:T(8,128)S(1)} %get-tuple-element.36.top), channel_id=1, source_target_pairs={{0,1},{1,0},{2,3},{3,2},{4,5},{5,4},{6,7},{7,6},{8,9},{9,8},{10,11... | collective-permute-start | bytes 98312 | tf_op jit(solution)/shard_map/ppermute | solution.py:411
  34.7 0.1 collective-permute-start.16
  34.7 1.1 %collective-permute-done.17.two = bf16[128,128]{1,0:T(8,128)(2,1)S(1)} collective-permute-done((bf16[128,128]{1,0:T(8,128)(2,1)S(1)}, bf16[128,128]{1,0:T(8,128)(2,1)S(1)}, u32[]{:S(2)}, u32[]{:S(2)}) %collective-permute-start.17) | collective-permute-done | bytes 32800 | tf_op jit(solution)/shard_map/ppermute | solution.py:410
  35.8 0.8 %collective-permute-done.18.three = bf16[128,128]{1,0:T(8,128)(2,1)S(1)} collective-permute-done((bf16[128,128]{1,0:T(8,128)(2,1)S(1)}, bf16[128,128]{1,0:T(8,128)(2,1)S(1)}, u32[]{:S(2)}, u32[]{:S(2)}) %collective-permute-start.18) | collective-permute-done | bytes 32800 | tf_op jit(solution)/shard_map/ppermute | solution.py:409
  36.6 0.0 collective-permute-done.15.one_top
  36.6 0.0 collective-permute-done.16.one_low
  36.6 0.0 collective-permute-done.19.far_ref
  36.6 1.0 %shard_map.89 = bf16[256,512]{1,0:T(8,128)(2,1)} custom-call(bf16[256,512]{1,0:T(8,128)(2,1)S(1)} %get-tuple-element.28.mask_ref, f32[64,128]{1,0:T(8,128)S(1)} %get-tuple-element.36.top, f32[64,128]{1,0:T(8,128)S(1)} %get-tuple-element.37.low, f32[64,128]{1,0:T(8,128)S(1)} %collective-permute-done.15.one_top, ...), custom_call_target="tpu_custom_call" | custom-call | tf_op jit(solution)/shard_map/pallas_call | solution.py:414
  (7 shorter events, 0.0 us)
Async XLA Ops:
  0.0 4.3 %copy-start = (bf16[256,4096]{1,0:T(8,128)(2,1)S(1)}, bf16[256,4096]{1,0:T(8,128)(2,1)}, u32[]{:S(2)}) copy-start(bf16[256,4096]{1,0:T(8,128)(2,1)} %refs_0_.1) | copy-start | bytes 6291460
  1.2 7.4 %collective-permute-start.7 = (bf16[64,1280]{1,0:T(8,128)(2,1)S(1)}, bf16[64,1280]{1,0:T(8,128)(2,1)S(1)}, u32[]{:S(2)}, u32[]{:S(2)}) collective-permute-start(bf16[64,1280]{1,0:T(8,128)(2,1)S(1)} %get-tuple-element.33.refs_7_.refs_0_), channel_id=1, source_target_pairs={{2,0},{6,2},{10,6},{14,10},{12,14},{8,12},{4,8},{0,4},{3,1},{7,3},... | collective-permute-start | bytes 491528 | tf_op jit(solution)/shard_map/ppermute | solution.py:380
  4.3 6.3 %collective-permute-start.2 = (bf16[64,1280]{1,0:T(8,128)(2,1)S(1)}, bf16[64,1280]{1,0:T(8,128)(2,1)S(1)}, u32[]{:S(2)}, u32[]{:S(2)}) collective-permute-start(bf16[64,1280]{1,0:T(8,128)(2,1)S(1)} %get-tuple-element.32.refs_3_), channel_id=1, source_target_pairs={{0,2},{2,6},{6,10},{10,14},{14,12},{12,8},{8,4},{4,0},{1,3},{3,7},... | collective-permute-start | bytes 491528 | tf_op jit(solution)/shard_map/ppermute | solution.py:379
  4.6 24.8 %collective-permute-start.14 = (bf16[4112,128]{1,0:T(8,128)(2,1)S(1)}, bf16[4112,128]{1,0:T(8,128)(2,1)S(1)}, u32[]{:S(2)}, u32[]{:S(2)}) collective-permute-start(bf16[4112,128]{1,0:T(8,128)(2,1)S(1)} %get-tuple-element.34), channel_id=1, source_target_pairs={{0,16},{16,0},{1,17},{17,1},{2,18},{18,2},{3,19},{19,3},{4,20},{20... | collective-permute-start | bytes 3158024 | tf_op jit(solution)/shard_map/ppermute | solution.py:390
  6.6 12.6 %slice-start = ((s8[8388608]{0:T(1024)(128)(4,1)}), s8[4194304]{0:T(1024)(128)(4,1)S(1)}, s32[]{:S(2)}) async-start(s8[8388608]{0:T(1024)(128)(4,1)} %bitcast.4), calls=%async_computation | async-start | bytes 8388608
  6.6 12.6 %slice-start.1 = ((s8[8388608]{0:T(1024)(128)(4,1)}), s8[4194304]{0:T(1024)(128)(4,1)S(1)}, s32[]{:S(2)}) async-start(s8[8388608]{0:T(1024)(128)(4,1)} %bitcast.4), calls=%async_computation.1 | async-start | bytes 8388608
  6.6 7.0 %collective-permute-start = (bf16[64,1280]{1,0:T(8,128)(2,1)S(1)}, bf16[64,1280]{1,0:T(8,128)(2,1)S(1)}, u32[]{:S(2)}, u32[]{:S(2)}) collective-permute-start(bf16[64,1280]{1,0:T(8,128)(2,1)S(1)} %get-tuple-element.32.refs_3_), channel_id=1, source_target_pairs={{2,0},{6,2},{10,6},{14,10},{12,14},{8,12},{4,8},{0,4},{3,1},{7,3},... | collective-permute-start | bytes 491528 | tf_op jit(solution)/shard_map/ppermute | solution.py:382
  8.2 7.1 %collective-permute-start.9 = (bf16[64,1280]{1,0:T(8,128)(2,1)S(1)}, bf16[64,1280]{1,0:T(8,128)(2,1)S(1)}, u32[]{:S(2)}, u32[]{:S(2)}) collective-permute-start(bf16[64,1280]{1,0:T(8,128)(2,1)S(1)} %get-tuple-element.33.refs_7_.refs_0_), channel_id=1, source_target_pairs={{0,2},{2,6},{6,10},{10,14},{14,12},{12,8},{8,4},{4,0},{1,3},{3,7},... | collective-permute-start | bytes 491528 | tf_op jit(solution)/shard_map/ppermute | solution.py:381
  8.6 8.5 %collective-permute-start.8 = (bf16[64,1280]{1,0:T(8,128)(2,1)S(1)}, bf16[64,1280]{1,0:T(8,128)(2,1)S(1)}, u32[]{:S(2)}, u32[]{:S(2)}) collective-permute-start(bf16[64,1280]{1,0:T(8,128)(2,1)S(1)} %collective-permute-done.7.refs_9_.refs_2_), channel_id=1, source_target_pairs={{2,0},{6,2},{10,6},{14,10},{12,14},{8,12},{4,8},{0,4},{3,1},{7,3},... | collective-permute-start | bytes 491528 | tf_op jit(solution)/shard_map/ppermute | solution.py:380
  10.6 8.2 %collective-permute-start.3 = (bf16[64,1280]{1,0:T(8,128)(2,1)S(1)}, bf16[64,1280]{1,0:T(8,128)(2,1)S(1)}, u32[]{:S(2)}, u32[]{:S(2)}) collective-permute-start(bf16[64,1280]{1,0:T(8,128)(2,1)S(1)} %collective-permute-done.2.refs_4_), channel_id=1, source_target_pairs={{0,2},{2,6},{6,10},{10,14},{14,12},{12,8},{8,4},{4,0},{1,3},{3,7},... | collective-permute-start | bytes 491528 | tf_op jit(solution)/shard_map/ppermute | solution.py:379
  13.6 8.1 %collective-permute-start.1 = (bf16[64,1280]{1,0:T(8,128)(2,1)S(1)}, bf16[64,1280]{1,0:T(8,128)(2,1)S(1)}, u32[]{:S(2)}, u32[]{:S(2)}) collective-permute-start(bf16[64,1280]{1,0:T(8,128)(2,1)S(1)} %collective-permute-done.refs_5_), channel_id=1, source_target_pairs={{2,0},{6,2},{10,6},{14,10},{12,14},{8,12},{4,8},{0,4},{3,1},{7,3},... | collective-permute-start | bytes 491528 | tf_op jit(solution)/shard_map/ppermute | solution.py:382
  15.3 8.1 %collective-permute-start.10 = (bf16[64,1280]{1,0:T(8,128)(2,1)S(1)}, bf16[64,1280]{1,0:T(8,128)(2,1)S(1)}, u32[]{:S(2)}, u32[]{:S(2)}) collective-permute-start(bf16[64,1280]{1,0:T(8,128)(2,1)S(1)} %collective-permute-done.9.refs_8_.refs_1_), channel_id=1, source_target_pairs={{0,2},{2,6},{6,10},{10,14},{14,12},{12,8},{8,4},{4,0},{1,3},{3,7},... | collective-permute-start | bytes 491528 | tf_op jit(solution)/shard_map/ppermute | solution.py:381
  17.1 7.1 %collective-permute-start.12 = (bf16[64,1280]{1,0:T(8,128)(2,1)S(1)}, bf16[64,1280]{1,0:T(8,128)(2,1)S(1)}, u32[]{:S(2)}, u32[]{:S(2)}) collective-permute-start(bf16[64,1280]{1,0:T(8,128)(2,1)S(1)} %collective-permute-done.8.refs_6_.refs_4_), channel_id=1, source_target_pairs={{2,0},{6,2},{10,6},{14,10},{12,14},{8,12},{4,8},{0,4},{3,1},{7,3},... | collective-permute-start | bytes 491528 | tf_op jit(solution)/shard_map/ppermute | solution.py:380
  18.8 7.1 %collective-permute-start.4 = (bf16[64,1280]{1,0:T(8,128)(2,1)S(1)}, bf16[64,1280]{1,0:T(8,128)(2,1)S(1)}, u32[]{:S(2)}, u32[]{:S(2)}) collective-permute-start(bf16[64,1280]{1,0:T(8,128)(2,1)S(1)} %collective-permute-done.3.refs_6_), channel_id=1, source_target_pairs={{0,2},{2,6},{6,10},{10,14},{14,12},{12,8},{8,4},{4,0},{1,3},{3,7},... | collective-permute-start | bytes 491528 | tf_op jit(solution)/shard_map/ppermute | solution.py:379
  21.7 8.5 %collective-permute-start.5 = (bf16[64,1280]{1,0:T(8,128)(2,1)S(1)}, bf16[64,1280]{1,0:T(8,128)(2,1)S(1)}, u32[]{:S(2)}, u32[]{:S(2)}) collective-permute-start(bf16[64,1280]{1,0:T(8,128)(2,1)S(1)} %collective-permute-done.1.refs_2_), channel_id=1, source_target_pairs={{2,0},{6,2},{10,6},{14,10},{12,14},{8,12},{4,8},{0,4},{3,1},{7,3},... | collective-permute-start | bytes 491528 | tf_op jit(solution)/shard_map/ppermute | solution.py:382
  23.4 6.8 %collective-permute-start.11 = (bf16[64,1280]{1,0:T(8,128)(2,1)S(1)}, bf16[64,1280]{1,0:T(8,128)(2,1)S(1)}, u32[]{:S(2)}, u32[]{:S(2)}) collective-permute-start(bf16[64,1280]{1,0:T(8,128)(2,1)S(1)} %collective-permute-done.10.refs_10_.refs_3_), channel_id=1, source_target_pairs={{0,2},{2,6},{6,10},{10,14},{14,12},{12,8},{8,4},{4,0},{1,3},{3,7},... | collective-permute-start | bytes 491528 | tf_op jit(solution)/shard_map/ppermute | solution.py:381
  24.2 6.0 %collective-permute-start.13 = (bf16[64,1280]{1,0:T(8,128)(2,1)S(1)}, bf16[64,1280]{1,0:T(8,128)(2,1)S(1)}, u32[]{:S(2)}, u32[]{:S(2)}) collective-permute-start(bf16[64,1280]{1,0:T(8,128)(2,1)S(1)} %collective-permute-done.12.refs_8_.refs_6_), channel_id=1, source_target_pairs={{2,0},{6,2},{10,6},{14,10},{12,14},{8,12},{4,8},{0,4},{3,1},{7,3},... | collective-permute-start | bytes 491528 | tf_op jit(solution)/shard_map/ppermute | solution.py:387
  26.0 5.3 %collective-permute-start.6 = (bf16[64,1280]{1,0:T(8,128)(2,1)S(1)}, bf16[64,1280]{1,0:T(8,128)(2,1)S(1)}, u32[]{:S(2)}, u32[]{:S(2)}) collective-permute-start(bf16[64,1280]{1,0:T(8,128)(2,1)S(1)} %collective-permute-done.4.refs_3_), channel_id=1, source_target_pairs={{0,2},{2,6},{6,10},{10,14},{14,12},{12,8},{8,4},{4,0},{1,3},{3,7},... | collective-permute-start | bytes 491528 | tf_op jit(solution)/shard_map/ppermute | solution.py:386
  30.1 6.5 %collective-permute-start.19 = (f32[256,512]{1,0:T(8,128)S(1)}, f32[256,512]{1,0:T(8,128)S(1)}, u32[]{:S(2)}, u32[]{:S(2)}) collective-permute-start(f32[256,512]{1,0:T(8,128)S(1)} %get-tuple-element.42), channel_id=1, source_target_pairs={{0,1},{1,0},{2,3},{3,2},{4,5},{5,4},{6,7},{7,6},{8,9},{9,8},{10,11... | collective-permute-start | bytes 1572872 | tf_op jit(solution)/shard_map/ppermute | solution.py:403
  31.8 4.0 %collective-permute-start.17 = (bf16[128,128]{1,0:T(8,128)(2,1)S(1)}, bf16[128,128]{1,0:T(8,128)(2,1)S(1)}, u32[]{:S(2)}, u32[]{:S(2)}) collective-permute-start(bf16[128,128]{1,0:T(8,128)(2,1)S(1)} %shard_map.88), channel_id=1, source_target_pairs={{0,16},{16,0},{1,17},{17,1},{2,18},{18,2},{3,19},{19,3},{4,20},{20... | collective-permute-start | bytes 98312 | tf_op jit(solution)/shard_map/ppermute | solution.py:410
  33.1 3.4 %collective-permute-start.18 = (bf16[128,128]{1,0:T(8,128)(2,1)S(1)}, bf16[128,128]{1,0:T(8,128)(2,1)S(1)}, u32[]{:S(2)}, u32[]{:S(2)}) collective-permute-start(bf16[128,128]{1,0:T(8,128)(2,1)S(1)} %shard_map.88), channel_id=1, source_target_pairs={{0,17},{1,16},{16,1},{17,0},{2,19},{3,18},{18,3},{19,2},{4,21},{5,... | collective-permute-start | bytes 98312 | tf_op jit(solution)/shard_map/ppermute | solution.py:409
  33.7 2.9 %collective-permute-start.15 = (f32[64,128]{1,0:T(8,128)S(1)}, f32[64,128]{1,0:T(8,128)S(1)}, u32[]{:S(2)}, u32[]{:S(2)}) collective-permute-start(f32[64,128]{1,0:T(8,128)S(1)} %get-tuple-element.36.top), channel_id=1, source_target_pairs={{0,1},{1,0},{2,3},{3,2},{4,5},{5,4},{6,7},{7,6},{8,9},{9,8},{10,11... | collective-permute-start | bytes 98312 | tf_op jit(solution)/shard_map/ppermute | solution.py:411
  34.7 1.9 %collective-permute-start.16 = (f32[64,128]{1,0:T(8,128)S(1)}, f32[64,128]{1,0:T(8,128)S(1)}, u32[]{:S(2)}, u32[]{:S(2)}) collective-permute-start(f32[64,128]{1,0:T(8,128)S(1)} %get-tuple-element.37.low), channel_id=1, source_target_pairs={{0,1},{1,0},{2,3},{3,2},{4,5},{5,4},{6,7},{7,6},{8,9},{9,8},{10,11... | collective-permute-start | bytes 98312 | tf_op jit(solution)/shard_map/ppermute | solution.py:411
